TPU v7x, 32 devices: a whole 2x2x4 slice. The times are simulated.
32 devices in a mesh: dp: 8 (over z, x), etp: 4 (over y, core).
Axes of the slice: x: 2, y: 2, z: 4, core: 2. Of those that a mesh axis runs over, the one named last changes fastest.
Arguments:
- tokens: bfloat16 [16384, 5120], P(('dp', 'etp')), may hold values from -6 to 6
- slots: int32 [2048], P(('dp', 'etp')), may hold values from 0 to 511, as said below
- gate_probs: bfloat16 [2048], P(('dp', 'etp')), may hold values from 0.099609375 to 1
- w_gate: bfloat16 [5120, 1536], P('dp', 'etp'), may hold values from -0.078125 to 0.078125
- w_up: bfloat16 [5120, 1536], P('dp', 'etp'), may hold values from -0.078125 to 0.078125
- d_hidden: bfloat16 [2048, 1536], P('dp', 'etp'), may hold values from -6 to 6
Outputs:
- hidden: bfloat16 [2048, 1536], P('dp', 'etp')
- grad_tokens: bfloat16 [16384, 5120], P(('dp', 'etp'))
- grad_gate: float32 [5120, 1536], P('dp', 'etp')
- grad_up: float32 [5120, 1536], P('dp', 'etp')
Inputs may be any that keep to these rules, and one draw needn't show every extreme that they name: `slots`: within each aligned block of 64 entries (one device's) the values are distinct; every block holds 0 and 511.
All inputs are finite; a program needn't handle non-finite values.
Results may differ from a plain program's by a relative error of at most 0.0049.
Values may be sent and summed in bfloat16 or wider, within the bound.
No kernel may reach another device: no remote copies, remote signals or barrier semaphores. Data moves between devices by JAX's collectives and lax.ppermute only.
A program may use at most 128 MiB of HBM per device.

v0:
```python
import jax
import jax.numpy as jnp
from jax import lax
from jax.sharding import PartitionSpec as P


def shards(tokens, slots, gate_probs, w_gate, w_up, d_hidden):
    local_rows = jnp.take(tokens, slots, axis=0)
    gathered_rows, gathered_probs = (
        lax.all_gather(local_rows, "etp", axis=0, tiled=True),
        lax.all_gather(gate_probs, "etp", axis=0, tiled=True),
    )
    gate_full, up_full = (
        lax.all_gather(w_gate, "dp", axis=0, tiled=True),
        lax.all_gather(w_up, "dp", axis=0, tiled=True),
    )
    gate_pre = jnp.dot(gathered_rows, gate_full, preferred_element_type=jnp.float32)
    up_pre = jnp.dot(gathered_rows, up_full, preferred_element_type=jnp.float32)
    slot_scale = gathered_probs.astype(jnp.float32)[:, None]
    sig_gate = jax.nn.sigmoid(gate_pre)
    activated = gate_pre * sig_gate
    hidden = (slot_scale * activated * up_pre).astype(jnp.bfloat16)
    scaled_grad = d_hidden.astype(jnp.float32) * slot_scale
    gate_grad = (scaled_grad * up_pre * sig_gate * (1.0 + gate_pre * (1.0 - sig_gate))).astype(
        jnp.bfloat16
    )
    up_grad = (scaled_grad * activated).astype(jnp.bfloat16)
    paired = jnp.concatenate([gate_grad, up_grad], axis=1)
    width = gate_grad.shape[1]
    contract_rows = (((0,), (0,)), ((), ()))
    summed = lax.psum_scatter(
        lax.dot_general(gathered_rows, paired, contract_rows, preferred_element_type=jnp.float32),
        "dp",
        scatter_dimension=0,
        tiled=True,
    )
    grad_gate = summed[:, :width]
    grad_up = summed[:, width:]
    weights_wide = jnp.concatenate([gate_full, up_full], axis=1)
    input_grad = lax.psum_scatter(
        lax.dot_general(
            paired, weights_wide, (((1,), (1,)), ((), ())), preferred_element_type=jnp.float32
        ),
        "etp",
        scatter_dimension=0,
        tiled=True,
    ).astype(jnp.bfloat16)
    grad_tokens = jnp.zeros_like(tokens).at[slots].set(input_grad)
    return (hidden, grad_tokens, grad_gate, grad_up)


def solution(mesh):
    in_specs = (
        P(("dp", "etp"), None),
        P(("dp", "etp")),
        P(("dp", "etp")),
        P("dp", "etp"),
        P("dp", "etp"),
        P("dp", "etp"),
    )
    out_specs = (P("dp", "etp"), P(("dp", "etp"), None), P("dp", "etp"), P("dp", "etp"))
    return jax.shard_map(shards, mesh=mesh, in_specs=in_specs, out_specs=out_specs, check_vma=False)
```

profile of v0, /device:TPU:0, one launch (start us, length us, event | category | flops | bytes accessed | tf_op | source)
XLA Modules:
  0.0 508.9 jit_solution(8389999218196087229)
XLA Ops:
  7.2 0.0 all-gather.4.cloned.1.call-start
  7.2 0.7 compare_select_fusion
  7.9 0.7 compare_and_fusion
  8.5 0.0 copy-start.5
  8.6 0.0 copy-start.4
  8.6 4.7 gather_fusion
  13.3 1.0 broadcast_select_fusion
  14.3 0.0 all-gather.4.cloned.1.call-update
  14.3 0.0 all-gather.8.cloned.1.call-start
  14.4 0.7 all-gather.8.cloned.1.call-update
  15.1 0.0 copy-start.3
  15.1 0.0 all-gather.6.cloned.1.call-start
  15.1 0.7 all-gather.6.cloned.1.call-update
  15.8 0.0 reduce-scatter.3.cloned.1.call-start
  15.9 0.6 dynamic-slice
  17.1 0.2 dynamic-update-slice
  17.4 8.3 %all-reduce = bf16[256]{0:T(256)(128)(2,1)S(1)} all-reduce(bf16[256]{0:T(256)(128)(2,1)S(1)} %dynamic-update-slice), channel_id=1, replica_groups=mesh['dp'=8,'etp'=4] {'etp'}, use_global_device_ids=true, to_apply=%add | all-reduce | flops 256 | bytes 1024
  25.7 17.0 %all-gather.4.cloned.1.call-done = bf16[256,5120]{1,0:T(8,128)(2,1)} async-done(((bf16[64,5120]{1,0:T(8,128)(2,1)}), bf16[256,5120]{1,0:T(8,128)(2,1)}) %all-gather.4.cloned.1.call-update) | async-done | bytes 2621456 | tf_op jit(solution)/shard_map/all_gather | solution.py:10
  42.7 72.3 %all-gather.8.cloned.1.call-done = bf16[5120,384]{1,0:T(8,128)(2,1)} async-done(((bf16[640,384]{1,0:T(8,128)(2,1)}), bf16[5120,384]{1,0:T(8,128)(2,1)}) %all-gather.8.cloned.1.call-update) | async-done | bytes 3932176 | tf_op jit(solution)/shard_map/all_gather | solution.py:15
  115.0 5.2 %fusion.12 = f32[256,384]{1,0:T(8,128)} fusion(bf16[256,5120]{1,0:T(8,128)(2,1)} %all-gather.4.cloned.1.call-done, bf16[5120,384]{1,0:T(8,128)(2,1)} %all-gather.8.cloned.1.call-done), kind=kOutput, calls=%fused_computation.24 | convolution fusion | flops 1006632960 | bytes 6946816 | tf_op jit(solution)/shard_map/dot_general | solution.py:18
  120.2 65.5 %all-gather.6.cloned.1.call-done = bf16[5120,384]{1,0:T(8,128)(2,1)} async-done(((bf16[640,384]{1,0:T(8,128)(2,1)}), bf16[5120,384]{1,0:T(8,128)(2,1)}) %all-gather.6.cloned.1.call-update) | async-done | bytes 3932176 | tf_op jit(solution)/shard_map/all_gather | solution.py:14
  185.7 0.0 copy-done.3
  185.7 4.8 multiply_convert_fusion.1
  190.5 4.0 fusion
  194.5 0.0 reduce-scatter.3.cloned.1.call-update
  194.5 0.0 reduce-scatter.5.cloned.1.call-start
  194.5 9.9 %fusion.8 = f32[5120,768]{1,0:T(8,128)} fusion(bf16[256,5120]{1,0:T(8,128)(2,1)S(1)} %copy-done, bf16[256,384]{1,0:T(8,128)(2,1)S(1)} %get-tuple-element.8, bf16[256,384]{1,0:T(8,128)(2,1)S(1)} %get-tuple-element.6), kind=kOutput, calls=%fused_computation.17 | convolution fusion | flops 2014052352 | bytes 18743296 | tf_op jit(solution)/shard_map/dot_general | solution.py:32
  204.5 0.0 reduce-scatter.5.cloned.1.call-update
  204.5 39.9 %reduce-scatter.3.cloned.1.call-done = f32[64,5120]{1,0:T(8,128)} async-done(((f32[256,5120]{1,0:T(8,128)}), f32[64,5120]{1,0:T(8,128)}) %reduce-scatter.3.cloned.1.call-update) | async-done | bytes 1310736 | tf_op jit(solution)/shard_map/reduce_scatter | solution.py:40
  244.4 5.7 %scatter_custom_fusion = bf16[512,5120]{1,0:T(8,128)(2,1)} fusion(s32[64]{0:T(128)S(1)} %compare_select_fusion, bf16[]{:T(256)} %constant.21.clone.1, f32[64,5120]{1,0:T(8,128)} %reduce-scatter.3.cloned.1.call-done), kind=kCustom, calls=%fused_computation.6 | custom fusion | flops 327680 | bytes 6553602 | tf_op jit(solution)/shard_map/scatter | solution.py:48
  250.0 249.4 %reduce-scatter.5.cloned.1.call-done = f32[640,768]{1,0:T(8,128)} async-done(((f32[5120,768]{1,0:T(8,128)}), f32[640,768]{1,0:T(8,128)}) %reduce-scatter.5.cloned.1.call-update) | async-done | bytes 1966096 | tf_op jit(solution)/shard_map/reduce_scatter | solution.py:31
  499.5 2.9 fusion.11
  (11 shorter events, 0.0 us)
Async XLA Ops:
  7.2 35.6 %all-gather.4.cloned.1.call-start = ((), (), s32[]{:S(2)}) async-start(), calls=%async_computation.2 | async-start | bytes 3276800 | tf_op jit(solution)/shard_map/all_gather | solution.py:10
  8.5 7.3 %copy-start.5 = (u32[32]{0:T(128)S(1)}, u32[32]{0:T(128)}, u32[]{:S(2)}) copy-start(u32[32]{0:T(128)} %constant.24) | copy-start | bytes 388
  8.6 8.6 %copy-start.4 = (bf16[64]{0:T(256)(128)(2,1)S(1)}, bf16[64]{0:T(256)(128)(2,1)}, u32[]{:S(2)}) copy-start(bf16[64]{0:T(256)(128)(2,1)} %param.8) | copy-start | bytes 388
  14.3 100.7 %all-gather.8.cloned.1.call-start = ((), (), s32[]{:S(2)}) async-start(), calls=%async_computation.4 | async-start | bytes 4423680 | tf_op jit(solution)/shard_map/all_gather | solution.py:15
  15.1 170.7 %copy-start.3 = (bf16[256,384]{1,0:T(8,128)(2,1)S(1)}, bf16[256,384]{1,0:T(8,128)(2,1)}, u32[]{:S(2)}) copy-start(bf16[256,384]{1,0:T(8,128)(2,1)} %param.11) | copy-start | bytes 589828
  15.1 170.6 %all-gather.6.cloned.1.call-start = ((), (), s32[]{:S(2)}) async-start(), calls=%async_computation.3 | async-start | bytes 4423680 | tf_op jit(solution)/shard_map/all_gather | solution.py:14
  15.8 228.6 %reduce-scatter.3.cloned.1.call-start = ((), (), s32[]{:S(2)}) async-start(), calls=%async_computation.5 | async-start | bytes 6553600 | tf_op jit(solution)/shard_map/reduce_scatter | solution.py:40
  42.7 143.0 %copy-start = (bf16[256,5120]{1,0:T(8,128)(2,1)S(1)}, bf16[256,5120]{1,0:T(8,128)(2,1)}, u32[]{:S(2)}) copy-start(bf16[256,5120]{1,0:T(8,128)(2,1)} %all-gather.4.cloned.1.call-done) | copy-start | bytes 7864324
  185.7 4.8 copy-start.1
  185.7 4.8 copy-start.2
  194.5 305.0 %reduce-scatter.5.cloned.1.call-start = ((), (), s32[]{:S(2)}) async-start(), calls=%async_computation.6 | async-start | bytes 17694720 | tf_op jit(solution)/shard_map/reduce_scatter | solution.py:31
Sparse Core Ops, SparseCore 0:
  14.4 28.2 all-gather.3
  44.9 70.0 all-gather.7
  117.2 68.4 all-gather.5
  194.6 49.7 reduce-scatter.2
  248.2 251.1 reduce-scatter.4
where the time goes:
time: 509 us
  waiting for transfers between devices  446 us (88%)
  matrix products  23.9 us (5%)
  between operations  14.5 us (3%)
  local copies, waits for them, and re-layouts  8.5 us (2%)
  blocking collectives  8.34 us (2%)
  other arithmetic  7.96 us (2%)
    reduce_scatter x1, waiting for transfers between devices, shards(): lax.psum_scatter(lax.dot_general(gathered_rows, paired, contract_rows, pr...  249 us
    all_gather x1, waiting for transfers between devices, shards(): lax.all_gather(w_up, 'dp', axis=0, tiled=True)  72.3 us
    all_gather x1, waiting for transfers between devices, shards(): lax.all_gather(w_gate, 'dp', axis=0, tiled=True)  65.5 us
    reduce_scatter x1, waiting for transfers between devices, shards(): lax.psum_scatter(lax.dot_general(paired, weights_wide, (((1,), (1,)), (()...  39.9 us
    all_gather x1, waiting for transfers between devices, shards(): lax.all_gather(local_rows, 'etp', axis=0, tiled=True)  17 us
  transfers between devices with their start and end apart: 5, of which 5 were waited for; matrix products, arithmetic and copies ran while one was open for 4% of the time, Pallas kernels for 0%

commit v1 on v0

v1 whole, which is shorter than its diff:
```python
import jax
import jax.numpy as jnp
from jax import lax
from jax.sharding import PartitionSpec as P

F32 = jnp.float32
BF16 = jnp.bfloat16


def split_dp(dp):
    outer = 1
    while 4 * outer * outer <= 2 * dp:
        outer *= 2
    return outer, dp // outer


def make_shards(dp_size, etp_size):
    outer, inner = split_dp(dp_size)

    def over_outer(value, k):
        pairs = [(i, i ^ (k * inner)) for i in range(dp_size)]
        return lax.ppermute(value, "dp", pairs)

    def over_inner(value, j):
        pairs = [(i, i ^ j) for i in range(dp_size)]
        return lax.ppermute(value, "dp", pairs)

    def over_etp(value, e):
        pairs = [(i, i ^ e) for i in range(etp_size)]
        return lax.ppermute(value, "etp", pairs)

    chunk_order = [0]
    bit = etp_size // 2
    bits = []
    while bit:
        bits.append(bit)
        chunk_order = chunk_order + [c ^ bit for c in chunk_order]
        bit //= 2

    def gather_etp(value):
        for b in bits:
            value = jnp.concatenate([value, over_etp(value, b)], axis=0)
        return value

    def reduce_etp(value):
        for b in reversed(bits):
            half = value.shape[0] // 2
            sent = over_etp(value[half:].astype(BF16), b)
            value = value[:half] + sent.astype(F32)
        return value

    far_first = sorted(range(1, outer), key=lambda k: -k)

    def shards(tokens, slots, gate_probs, w_gate, w_up, d_hidden):
        dp = lax.axis_index("dp")
        etp = lax.axis_index("etp")
        a, b = dp // inner, dp % inner
        depth, width = w_gate.shape
        cap = slots.shape[0]
        tok = tokens.shape[0]
        span = depth * inner

        weights = jnp.zeros((inner, depth, 2 * width), BF16)
        for j in range(inner):
            gate_j = over_inner(w_gate, j) if j else w_gate
            up_j = over_inner(w_up, j) if j else w_up
            both = jnp.concatenate([gate_j, up_j], axis=1)[None]
            weights = lax.dynamic_update_slice(weights, both, (b ^ j, 0, 0))
        weights = weights.reshape(span, 2 * width)

        onehot = (slots[:, None] == jnp.arange(tok, dtype=slots.dtype)[None, :]).astype(BF16)
        rows = jnp.dot(onehot, tokens, preferred_element_type=F32).astype(BF16)
        x_chunks = [None] * outer
        for k in far_first + [0]:
            piece = lax.dynamic_slice(rows, (0, (a ^ k) * span), (cap, span))
            x_chunks[k] = over_outer(piece, k) if k else piece
        x_chunks = [gather_etp(c) for c in x_chunks]
        probs = gather_etp(gate_probs)

        pre = jnp.dot(x_chunks[0], weights, preferred_element_type=F32)
        parts = {
            k: over_outer(jnp.dot(x_chunks[k], weights, preferred_element_type=F32).astype(BF16), k)
            for k in far_first
        }
        for k in far_first:
            pre = pre + parts[k].astype(F32)
        gate_pre, up_pre = pre[:, :width], pre[:, width:]

        order = etp ^ jnp.array(chunk_order, jnp.int32)
        d_own = jnp.take(d_hidden.reshape(etp_size, cap, width), order, axis=0).reshape(-1, width)
        prob = probs.astype(F32)[:, None]
        sig = jax.nn.sigmoid(gate_pre)
        act = gate_pre * sig
        hidden = (prob * act * up_pre).astype(BF16)
        scaled = d_own.astype(F32) * prob
        gate_grad = (scaled * up_pre * sig * (1.0 + gate_pre * (1.0 - sig))).astype(BF16)
        up_grad = (scaled * act).astype(BF16)
        paired = jnp.concatenate([gate_grad, up_grad], axis=1)
        inverse = jnp.zeros((etp_size,), jnp.int32).at[order].set(jnp.arange(etp_size, dtype=jnp.int32))
        hidden = jnp.take(hidden.reshape(etp_size, cap, width), inverse, axis=0).reshape(-1, width)

        grads = [over_outer(paired, k) if k else paired for k in range(outer)]

        dx = jnp.zeros((cap, outer * span), BF16)
        for k in range(outer):
            partial = lax.dot_general(
                grads[k], weights, (((1,), (1,)), ((), ())), preferred_element_type=F32
            )
            own = reduce_etp(partial).astype(BF16)
            own = over_outer(own, k) if k else own
            dx = lax.dynamic_update_slice(dx, own, (0, (a ^ k) * span))
        grad_tokens = lax.dot_general(
            onehot, dx, (((0,), (0,)), ((), ())), preferred_element_type=F32
        ).astype(BF16)

        summed = lax.dot_general(
            jnp.concatenate(x_chunks, axis=0),
            jnp.concatenate(grads, axis=0),
            (((0,), (0,)), ((), ())),
            preferred_element_type=F32,
        )
        total = lax.dynamic_slice(summed, (b * depth, 0), (depth, 2 * width))
        for j in range(1, inner):
            part = lax.dynamic_slice(summed, ((b ^ j) * depth, 0), (depth, 2 * width))
            total = total + over_inner(part.astype(BF16), j).astype(F32)
        return (hidden, grad_tokens, total[:, :width], total[:, width:])

    return shards


def solution(mesh):
    in_specs = (
        P(("dp", "etp"), None),
        P(("dp", "etp")),
        P(("dp", "etp")),
        P("dp", "etp"),
        P("dp", "etp"),
        P("dp", "etp"),
    )
    out_specs = (P("dp", "etp"), P(("dp", "etp"), None), P("dp", "etp"), P("dp", "etp"))
    shards = make_shards(mesh.shape["dp"], mesh.shape["etp"])
    return jax.shard_map(shards, mesh=mesh, in_specs=in_specs, out_specs=out_specs, check_vma=False)
```

time: 509 us -> 170 us (0.33)
  waiting for transfers between devices: 446 us -> 81.7 us
  starting transfers between devices: 0.2 us -> 42.5 us
  between operations: 14.5 us -> 1.15 us
  blocking collectives: 8.34 us -> 0 us
  local copies, waits for them, and re-layouts: 8.5 us -> 14.7 us
    reduce_scatter x2 -> x0, waiting for transfers between devices: 289 us -> none  [the longest x1 249 us: shards(): lax.psum_scatter(lax.dot_general(gathered_rows, paired, contract_rows, pr...]
    all_gather x3 -> x0, waiting for transfers between devices: 155 us -> none  [the longest x1 72.3 us: shards(): lax.all_gather(w_up, 'dp', axis=0, tiled=True)]
    ppermute x0 -> x33, waiting for transfers between devices: none -> 81.7 us  [the longest x12 64.7 us: over_outer(): return lax.ppermute(value, 'dp', pairs)]
    ppermute x0 -> x33, starting transfers between devices: none -> 42.5 us  [the longest x12 26 us: over_outer(): return lax.ppermute(value, 'dp', pairs)]
    unnamed x1 -> x0, blocking collectives: 8.34 us -> none
    unnamed x15 -> x29, local copies, waits for them, and re-layouts: 0.86 us -> 7.88 us
    scatter x1 -> x0, other arithmetic: 5.66 us -> none  [shards(): grad_tokens = jnp.zeros_like(tokens).at[slots].set(input_grad)]
    dot_general x4 -> x11, matrix products: 23.9 us -> 20.5 us  [the longest x4 5.84 us: shards(): lax.dot_general(grads[k], weights, (((1,), (1,)), ((), ())), preferred_el...]
  transfers between devices with their start and end apart: 5 -> 33, of which waited for: 5 -> 13; matrix products, arithmetic and copies ran while one was open for 4% -> 21% of each run, Pallas kernels for 0% -> 0%
where the time goes in v1:
time: 170 us
  waiting for transfers between devices  81.7 us (48%)
  starting transfers between devices  42.5 us (25%)
  matrix products  20.5 us (12%)
  local copies, waits for them, and re-layouts  14.7 us (9%)
  other arithmetic  9.2 us (5%)
    ppermute x12, waiting for transfers between devices, over_outer(): return lax.ppermute(value, 'dp', pairs)  64.7 us
    ppermute x12, starting transfers between devices, over_outer(): return lax.ppermute(value, 'dp', pairs)  26 us
    ppermute x18, waiting for transfers between devices, over_etp(): return lax.ppermute(value, 'etp', pairs)  17 us
    ppermute x18, starting transfers between devices, over_etp(): return lax.ppermute(value, 'etp', pairs)  12.9 us
    unnamed x29, local copies, waits for them, and re-layouts  7.88 us
    dot_general x4, matrix products, shards(): lax.dot_general(grads[k], weights, (((1,), (1,)), ((), ())), preferred_el...  5.84 us
    dot_general x1, matrix products, shards(): lax.dot_general(jnp.concatenate(x_chunks, axis=0), jnp.concatenate(grads,...  4.29 us
    dot_general x1, matrix products, shards(): lax.dot_general(onehot, dx, (((0,), (0,)), ((), ())), preferred_element_t...  4 us
  transfers between devices with their start and end apart: 33, of which 13 were waited for; matrix products, arithmetic and copies ran while one was open for 21% of the time, Pallas kernels for 0%

profile of v1, /device:TPU:0, one launch (start us, length us, event | category | flops | bytes accessed | tf_op | source)
XLA Modules:
  0.0 169.7 jit_solution(13962105919524394698)
XLA Ops:
  0.7 3.6 %convolution_convert_fusion.1 = bf16[64,5120]{1,0:T(8,128)(2,1)S(1)} fusion(bf16[512,5120]{1,0:T(8,128)(2,1)} %param.9, s32[64]{0:T(128)} %param.10), kind=kOutput, calls=%fused_computation.4 | convolution fusion | flops 335904768 | bytes 5898496 | tf_op jit(solution)/shard_map/dot_general | solution.py:72
  5.2 3.0 %collective-permute-start.2 = (bf16[64,1280]{1,0:T(8,128)(2,1)S(1)}, bf16[64,1280]{1,0:T(8,128)(2,1)S(1)}, u32[]{:S(2)}, u32[]{:S(2)}) collective-permute-start(bf16[64,1280]{1,0:T(8,128)(2,1)S(1)} %get-tuple-element.6), channel_id=1, source_target_pairs={{0,2},{1,3},{2,0},{3,1},{4,6},{5,7},{6,4},{7,5},{8,10},{9,11},{10,... | collective-permute-start | bytes 491528 | tf_op jit(solution)/shard_map/ppermute | solution.py:30
  8.2 1.6 collective-permute-start.14
  9.8 1.5 collective-permute-start.4
  17.1 2.6 %collective-permute-start.10 = (bf16[64,1280]{1,0:T(8,128)(2,1)}, bf16[64,1280]{1,0:T(8,128)(2,1)S(1)}, u32[]{:S(2)}, u32[]{:S(2)}) collective-permute-start(bf16[64,1280]{1,0:T(8,128)(2,1)} %get-tuple-element.15), channel_id=1, source_target_pairs={{0,16},{4,20},{8,24},{12,28},{16,0},{20,4},{24,8},{28,12},{1,17},{... | collective-permute-start | bytes 491528 | tf_op jit(solution)/shard_map/ppermute | solution.py:22
  20.7 1.3 collective-permute-start.15
  22.7 8.8 %collective-permute-done.10 = bf16[64,1280]{1,0:T(8,128)(2,1)S(1)} collective-permute-done((bf16[64,1280]{1,0:T(8,128)(2,1)}, bf16[64,1280]{1,0:T(8,128)(2,1)S(1)}, u32[]{:S(2)}, u32[]{:S(2)}) %collective-permute-start.10) | collective-permute-done | bytes 163872 | tf_op jit(solution)/shard_map/ppermute | solution.py:22
  33.6 4.9 %collective-permute-done.11 = bf16[64,1280]{1,0:T(8,128)(2,1)S(1)} collective-permute-done((bf16[64,1280]{1,0:T(8,128)(2,1)S(1)}, bf16[64,1280]{1,0:T(8,128)(2,1)S(1)}, u32[]{:S(2)}, u32[]{:S(2)}) %collective-permute-start.11) | collective-permute-done | bytes 163872 | tf_op jit(solution)/shard_map/ppermute | solution.py:30
  38.6 3.1 %collective-permute-done.7 = bf16[64,1280]{1,0:T(8,128)(2,1)S(1)} collective-permute-done((bf16[64,1280]{1,0:T(8,128)(2,1)S(1)}, bf16[64,1280]{1,0:T(8,128)(2,1)S(1)}, u32[]{:S(2)}, u32[]{:S(2)}) %collective-permute-start.7) | collective-permute-done | bytes 163872 | tf_op jit(solution)/shard_map/ppermute | solution.py:30
  46.4 3.3 %collective-permute-start.9 = (bf16[256,768]{1,0:T(8,128)(2,1)S(1)}, bf16[256,768]{1,0:T(8,128)(2,1)S(1)}, u32[]{:S(2)}, u32[]{:S(2)}) collective-permute-start(bf16[256,768]{1,0:T(8,128)(2,1)S(1)} %convolution_convert_fusion.4), channel_id=1, source_target_pairs={{0,24},{4,28},{8,16},{12,20},{16,8},{20,12},{24,0},{28,4},{1,25},{... | collective-permute-start | bytes 1179656 | tf_op jit(solution)/shard_map/ppermute | solution.py:22
  50.4 1.8 %collective-permute-start.13 = (bf16[256,768]{1,0:T(8,128)(2,1)S(1)}, bf16[256,768]{1,0:T(8,128)(2,1)S(1)}, u32[]{:S(2)}, u32[]{:S(2)}) collective-permute-start(bf16[256,768]{1,0:T(8,128)(2,1)S(1)} %convolution_convert_fusion.3), channel_id=1, source_target_pairs={{0,16},{4,20},{8,24},{12,28},{16,0},{20,4},{24,8},{28,12},{1,17},{... | collective-permute-start | bytes 1179656 | tf_op jit(solution)/shard_map/ppermute | solution.py:22
  57.9 2.4 %collective-permute-done.9 = bf16[256,768]{1,0:T(8,128)(2,1)S(1)} collective-permute-done((bf16[256,768]{1,0:T(8,128)(2,1)S(1)}, bf16[256,768]{1,0:T(8,128)(2,1)S(1)}, u32[]{:S(2)}, u32[]{:S(2)}) %collective-permute-start.9) | collective-permute-done | bytes 393248 | tf_op jit(solution)/shard_map/ppermute | solution.py:22
  60.4 24.2 %collective-permute-done.13 = bf16[256,768]{1,0:T(8,128)(2,1)S(1)} collective-permute-done((bf16[256,768]{1,0:T(8,128)(2,1)S(1)}, bf16[256,768]{1,0:T(8,128)(2,1)S(1)}, u32[]{:S(2)}, u32[]{:S(2)}) %collective-permute-start.13) | collective-permute-done | bytes 393248 | tf_op jit(solution)/shard_map/ppermute | solution.py:22
  88.9 3.4 %collective-permute-start.24 = (bf16[256,768]{1,0:T(8,128)(2,1)}, bf16[256,768]{1,0:T(8,128)(2,1)}, u32[]{:S(2)}, u32[]{:S(2)}) collective-permute-start(bf16[256,768]{1,0:T(8,128)(2,1)} %pad_maximum_fusion), channel_id=1, source_target_pairs={{0,16},{4,20},{8,24},{12,28},{16,0},{20,4},{24,8},{28,12},{1,17},{... | collective-permute-start | bytes 1179656 | tf_op jit(solution)/shard_map/ppermute | solution.py:22
  93.0 2.2 %gather_fusion = bf16[4,64,384]{2,1,0:T(8,128)(2,1)} fusion(bf16[4,64,384]{2,1,0:T(8,128)(2,1)} %bitcast.39, s32[1024]{0:T(1024)S(1)} %pad_clamp_fusion.1), kind=kCustom, calls=%fused_computation.clone | custom fusion | bytes 393232 | tf_op jit(solution)/shard_map/jit(_take)/gather | solution.py:100
  95.1 1.7 %broadcast_select_fusion.1 = bf16[4,64,384]{2,1,0:T(8,128)(2,1)} fusion(bf16[4,64,384]{2,1,0:T(8,128)(2,1)} %gather_fusion, pred[4]{0:T(512)(128)(4,1)S(1)} %compare_and_fusion.1), kind=kLoop, calls=%fused_computation.83 | loop fusion | flops 98304 | bytes 393220 | tf_op jit(solution)/shard_map/jit(_take)/select_n | solution.py:100
  98.0 1.3 collective-permute-start.19
  99.3 9.2 %collective-permute-done.20 = bf16[256,768]{1,0:T(8,128)(2,1)} collective-permute-done((bf16[256,768]{1,0:T(8,128)(2,1)}, bf16[256,768]{1,0:T(8,128)(2,1)}, u32[]{:S(2)}, u32[]{:S(2)}) %collective-permute-start.20) | collective-permute-done | bytes 393248 | tf_op jit(solution)/shard_map/ppermute | solution.py:22
  108.5 10.9 %collective-permute-done.24 = bf16[256,768]{1,0:T(8,128)(2,1)} collective-permute-done((bf16[256,768]{1,0:T(8,128)(2,1)}, bf16[256,768]{1,0:T(8,128)(2,1)}, u32[]{:S(2)}, u32[]{:S(2)}) %collective-permute-start.24) | collective-permute-done | bytes 393248 | tf_op jit(solution)/shard_map/ppermute | solution.py:22
  119.4 4.3 %fusion = f32[1280,768]{1,0:T(8,128)S(1)} fusion(bf16[1024,1280]{1,0:T(8,128)(2,1)} %constant_dynamic-update-slice_fusion, bf16[256,768]{1,0:T(8,128)(2,1)} %collective-permute-done.28, bf16[256,768]{1,0:T(8,128)(2,1)} %collective-permute-done.24, bf16[256,768]{1,0:T(8,128)(2,1)} %collective-permute-done.20, bf16[256,384]{1,0:T(8,128)(2,1)S(1)} %copy-done.4, ...), kind=kOutput, calls=%fused_computation.7 | convolution fusion | flops 2021130240 | bytes 8126464 | tf_op jit(solution)/shard_map/dot_general | solution.py:116
  123.8 1.6 collective-permute-start.32
  125.3 1.7 %fusion.59 = f32[256,1280]{1,0:T(8,128)S(1)} fusion(bf16[256,768]{1,0:T(8,128)(2,1)} %collective-permute-done.28, bf16[1280,768]{1,0:T(8,128)(2,1)S(1)} %bitcast.36), kind=kOutput, calls=%fused_computation.126 | convolution fusion | flops 503316480 | bytes 3670016 | tf_op jit(solution)/shard_map/dot_general | solution.py:106
  127.2 1.7 %fusion.58 = f32[256,1280]{1,0:T(8,128)S(1)} fusion(bf16[256,768]{1,0:T(8,128)(2,1)} %collective-permute-done.24, bf16[1280,768]{1,0:T(8,128)(2,1)S(1)} %bitcast.37), kind=kOutput, calls=%fused_computation.125 | convolution fusion | flops 503316480 | bytes 3670016 | tf_op jit(solution)/shard_map/dot_general | solution.py:106
  129.5 1.7 %fusion.57 = f32[256,1280]{1,0:T(8,128)S(1)} fusion(bf16[256,768]{1,0:T(8,128)(2,1)} %collective-permute-done.20, bf16[1280,768]{1,0:T(8,128)(2,1)S(1)} %bitcast.38), kind=kOutput, calls=%fused_computation.124 | convolution fusion | flops 503316480 | bytes 3670016 | tf_op jit(solution)/shard_map/dot_general | solution.py:106
  135.2 3.4 %collective-permute-done.30 = bf16[64,1280]{1,0:T(8,128)(2,1)S(1)} collective-permute-done((bf16[64,1280]{1,0:T(8,128)(2,1)S(1)}, bf16[64,1280]{1,0:T(8,128)(2,1)S(1)}, u32[]{:S(2)}, u32[]{:S(2)}) %collective-permute-start.30) | collective-permute-done | bytes 163872 | tf_op jit(solution)/shard_map/ppermute | solution.py:30
  138.6 2.4 %collective-permute-start.31 = (bf16[64,1280]{1,0:T(8,128)(2,1)S(1)}, bf16[64,1280]{1,0:T(8,128)(2,1)S(1)}, u32[]{:S(2)}, u32[]{:S(2)}) collective-permute-start(bf16[64,1280]{1,0:T(8,128)(2,1)S(1)} %fusion.41), channel_id=1, source_target_pairs={{0,24},{4,28},{8,16},{12,20},{16,8},{20,12},{24,0},{28,4},{1,25},{... | collective-permute-start | bytes 491528 | tf_op jit(solution)/shard_map/ppermute | solution.py:22
  141.0 4.2 %collective-permute-done.22 = bf16[64,1280]{1,0:T(8,128)(2,1)S(1)} collective-permute-done((bf16[64,1280]{1,0:T(8,128)(2,1)S(1)}, bf16[64,1280]{1,0:T(8,128)(2,1)S(1)}, u32[]{:S(2)}, u32[]{:S(2)}) %collective-permute-start.22) | collective-permute-done | bytes 163872 | tf_op jit(solution)/shard_map/ppermute | solution.py:30
  145.3 8.7 %collective-permute-start.23 = (bf16[64,1280]{1,0:T(8,128)(2,1)S(1)}, bf16[64,1280]{1,0:T(8,128)(2,1)S(1)}, u32[]{:S(2)}, u32[]{:S(2)}) collective-permute-start(bf16[64,1280]{1,0:T(8,128)(2,1)S(1)} %fusion.43), channel_id=1, source_target_pairs={{0,8},{4,12},{8,0},{12,4},{16,24},{20,28},{24,16},{28,20},{1,9},{5... | collective-permute-start | bytes 491528 | tf_op jit(solution)/shard_map/ppermute | solution.py:22
  154.9 5.8 %collective-permute-done.23 = bf16[64,1280]{1,0:T(8,128)(2,1)S(1)} collective-permute-done((bf16[64,1280]{1,0:T(8,128)(2,1)S(1)}, bf16[64,1280]{1,0:T(8,128)(2,1)S(1)}, u32[]{:S(2)}, u32[]{:S(2)}) %collective-permute-start.23) | collective-permute-done | bytes 163872 | tf_op jit(solution)/shard_map/ppermute | solution.py:22
  160.7 3.3 %collective-permute-done.27 = bf16[64,1280]{1,0:T(8,128)(2,1)S(1)} collective-permute-done((bf16[64,1280]{1,0:T(8,128)(2,1)S(1)}, bf16[64,1280]{1,0:T(8,128)(2,1)S(1)}, u32[]{:S(2)}, u32[]{:S(2)}) %collective-permute-start.27) | collective-permute-done | bytes 163872 | tf_op jit(solution)/shard_map/ppermute | solution.py:22
  164.1 4.0 %convolution_convert_fusion = bf16[512,5120]{1,0:T(8,128)(2,1)} fusion(bf16[64,5120]{1,0:T(8,128)(2,1)S(1)} %constant_dynamic-update-slice_fusion.12, s32[64]{0:T(128)S(1)} %copy-done.6), kind=kOutput, calls=%fused_computation.3 | convolution fusion | flops 338198528 | bytes 5898496 | tf_op jit(solution)/shard_map/dot_general | solution.py:112
  168.3 1.4 fusion.56
  (120 shorter events, 33.6 us)
Async XLA Ops:
  5.2 15.3 %collective-permute-start.2 = (bf16[64,1280]{1,0:T(8,128)(2,1)S(1)}, bf16[64,1280]{1,0:T(8,128)(2,1)S(1)}, u32[]{:S(2)}, u32[]{:S(2)}) collective-permute-start(bf16[64,1280]{1,0:T(8,128)(2,1)S(1)} %get-tuple-element.6), channel_id=1, source_target_pairs={{0,2},{1,3},{2,0},{3,1},{4,6},{5,7},{6,4},{7,5},{8,10},{9,11},{10,... | collective-permute-start | bytes 491528 | tf_op jit(solution)/shard_map/ppermute | solution.py:30
  8.2 12.6 %collective-permute-start.14 = (bf16[64,1280]{1,0:T(8,128)(2,1)}, bf16[64,1280]{1,0:T(8,128)(2,1)S(1)}, u32[]{:S(2)}, u32[]{:S(2)}) collective-permute-start(bf16[64,1280]{1,0:T(8,128)(2,1)} %get-tuple-element.14), channel_id=1, source_target_pairs={{0,8},{4,12},{8,0},{12,4},{16,24},{20,28},{24,16},{28,20},{1,9},{5... | collective-permute-start | bytes 491528 | tf_op jit(solution)/shard_map/ppermute | solution.py:22
  9.8 34.6 %collective-permute-start.4 = (bf16[640,384]{1,0:T(8,128)(2,1)S(1)}, bf16[640,384]{1,0:T(8,128)(2,1)}, u32[]{:S(2)}, u32[]{:S(2)}) collective-permute-start(bf16[640,384]{1,0:T(8,128)(2,1)S(1)} %copy-done.5), channel_id=1, source_target_pairs={{0,4},{4,0},{8,12},{12,8},{16,20},{20,16},{24,28},{28,24},{1,5},{5... | collective-permute-start | bytes 1474568 | tf_op jit(solution)/shard_map/ppermute | solution.py:26
  11.3 33.1 %collective-permute-start.5 = (bf16[640,384]{1,0:T(8,128)(2,1)}, bf16[640,384]{1,0:T(8,128)(2,1)}, u32[]{:S(2)}, u32[]{:S(2)}) collective-permute-start(bf16[640,384]{1,0:T(8,128)(2,1)} %param.13), channel_id=1, source_target_pairs={{0,4},{4,0},{8,12},{12,8},{16,20},{20,16},{24,28},{28,24},{1,5},{5... | collective-permute-start | bytes 1474568 | tf_op jit(solution)/shard_map/ppermute | solution.py:26
  11.8 3.5 %collective-permute-start = (bf16[64]{0:T(256)(128)(2,1)S(1)}, bf16[64]{0:T(256)(128)(2,1)}, u32[]{:S(2)}, u32[]{:S(2)}) collective-permute-start(bf16[64]{0:T(256)(128)(2,1)S(1)} %copy-done.7), channel_id=1, source_target_pairs={{0,2},{1,3},{2,0},{3,1},{4,6},{5,7},{6,4},{7,5},{8,10},{9,11},{10,... | collective-permute-start | bytes 392 | tf_op jit(solution)/shard_map/ppermute | solution.py:30
  17.1 14.4 %collective-permute-start.10 = (bf16[64,1280]{1,0:T(8,128)(2,1)}, bf16[64,1280]{1,0:T(8,128)(2,1)S(1)}, u32[]{:S(2)}, u32[]{:S(2)}) collective-permute-start(bf16[64,1280]{1,0:T(8,128)(2,1)} %get-tuple-element.15), channel_id=1, source_target_pairs={{0,16},{4,20},{8,24},{12,28},{16,0},{20,4},{24,8},{28,12},{1,17},{... | collective-permute-start | bytes 491528 | tf_op jit(solution)/shard_map/ppermute | solution.py:22
  20.5 11.1 %collective-permute-start.6 = (bf16[64,1280]{1,0:T(8,128)(2,1)}, bf16[64,1280]{1,0:T(8,128)(2,1)S(1)}, u32[]{:S(2)}, u32[]{:S(2)}) collective-permute-start(bf16[64,1280]{1,0:T(8,128)(2,1)} %get-tuple-element.16), channel_id=1, source_target_pairs={{0,24},{4,28},{8,16},{12,20},{16,8},{20,12},{24,0},{28,4},{1,25},{... | collective-permute-start | bytes 491528 | tf_op jit(solution)/shard_map/ppermute | solution.py:22
  20.7 12.1 %collective-permute-start.15 = (bf16[64,1280]{1,0:T(8,128)(2,1)S(1)}, bf16[64,1280]{1,0:T(8,128)(2,1)S(1)}, u32[]{:S(2)}, u32[]{:S(2)}) collective-permute-start(bf16[64,1280]{1,0:T(8,128)(2,1)S(1)} %collective-permute-done.14), channel_id=1, source_target_pairs={{0,2},{1,3},{2,0},{3,1},{4,6},{5,7},{6,4},{7,5},{8,10},{9,11},{10,... | collective-permute-start | bytes 491528 | tf_op jit(solution)/shard_map/ppermute | solution.py:30
  31.5 10.2 %collective-permute-start.3 = (bf16[128,1280]{1,0:T(8,128)(2,1)S(1)}, bf16[128,1280]{1,0:T(8,128)(2,1)S(1)}, u32[]{:S(2)}, u32[]{:S(2)}) collective-permute-start(bf16[128,1280]{1,0:T(8,128)(2,1)S(1)} %pad_maximum_fusion.1), channel_id=1, source_target_pairs={{0,1},{1,0},{2,3},{3,2},{4,5},{5,4},{6,7},{7,6},{8,9},{9,8},{10,11... | collective-permute-start | bytes 983048 | tf_op jit(solution)/shard_map/ppermute | solution.py:30
  31.6 7.0 %collective-permute-start.11 = (bf16[64,1280]{1,0:T(8,128)(2,1)S(1)}, bf16[64,1280]{1,0:T(8,128)(2,1)S(1)}, u32[]{:S(2)}, u32[]{:S(2)}) collective-permute-start(bf16[64,1280]{1,0:T(8,128)(2,1)S(1)} %collective-permute-done.10), channel_id=1, source_target_pairs={{0,2},{1,3},{2,0},{3,1},{4,6},{5,7},{6,4},{7,5},{8,10},{9,11},{10,... | collective-permute-start | bytes 491528 | tf_op jit(solution)/shard_map/ppermute | solution.py:30
  32.8 8.9 %collective-permute-start.7 = (bf16[64,1280]{1,0:T(8,128)(2,1)S(1)}, bf16[64,1280]{1,0:T(8,128)(2,1)S(1)}, u32[]{:S(2)}, u32[]{:S(2)}) collective-permute-start(bf16[64,1280]{1,0:T(8,128)(2,1)S(1)} %collective-permute-done.6), channel_id=1, source_target_pairs={{0,2},{1,3},{2,0},{3,1},{4,6},{5,7},{6,4},{7,5},{8,10},{9,11},{10,... | collective-permute-start | bytes 491528 | tf_op jit(solution)/shard_map/ppermute | solution.py:30
  38.5 13.7 %collective-permute-start.16 = (bf16[128,1280]{1,0:T(8,128)(2,1)S(1)}, bf16[128,1280]{1,0:T(8,128)(2,1)S(1)}, u32[]{:S(2)}, u32[]{:S(2)}) collective-permute-start(bf16[128,1280]{1,0:T(8,128)(2,1)S(1)} %pad_maximum_fusion.4), channel_id=1, source_target_pairs={{0,1},{1,0},{2,3},{3,2},{4,5},{5,4},{6,7},{7,6},{8,9},{9,8},{10,11... | collective-permute-start | bytes 983048 | tf_op jit(solution)/shard_map/ppermute | solution.py:30
  41.7 8.0 %collective-permute-start.12 = (bf16[128,1280]{1,0:T(8,128)(2,1)S(1)}, bf16[128,1280]{1,0:T(8,128)(2,1)S(1)}, u32[]{:S(2)}, u32[]{:S(2)}) collective-permute-start(bf16[128,1280]{1,0:T(8,128)(2,1)S(1)} %pad_maximum_fusion.3), channel_id=1, source_target_pairs={{0,1},{1,0},{2,3},{3,2},{4,5},{5,4},{6,7},{7,6},{8,9},{9,8},{10,11... | collective-permute-start | bytes 983048 | tf_op jit(solution)/shard_map/ppermute | solution.py:30
  41.7 4.0 %collective-permute-start.8 = (bf16[128,1280]{1,0:T(8,128)(2,1)S(1)}, bf16[128,1280]{1,0:T(8,128)(2,1)S(1)}, u32[]{:S(2)}, u32[]{:S(2)}) collective-permute-start(bf16[128,1280]{1,0:T(8,128)(2,1)S(1)} %pad_maximum_fusion.2), channel_id=1, source_target_pairs={{0,1},{1,0},{2,3},{3,2},{4,5},{5,4},{6,7},{7,6},{8,9},{9,8},{10,11... | collective-permute-start | bytes 983048 | tf_op jit(solution)/shard_map/ppermute | solution.py:30
  46.4 14.0 %collective-permute-start.9 = (bf16[256,768]{1,0:T(8,128)(2,1)S(1)}, bf16[256,768]{1,0:T(8,128)(2,1)S(1)}, u32[]{:S(2)}, u32[]{:S(2)}) collective-permute-start(bf16[256,768]{1,0:T(8,128)(2,1)S(1)} %convolution_convert_fusion.4), channel_id=1, source_target_pairs={{0,24},{4,28},{8,16},{12,20},{16,8},{20,12},{24,0},{28,4},{1,25},{... | collective-permute-start | bytes 1179656 | tf_op jit(solution)/shard_map/ppermute | solution.py:22
  50.4 34.2 %collective-permute-start.13 = (bf16[256,768]{1,0:T(8,128)(2,1)S(1)}, bf16[256,768]{1,0:T(8,128)(2,1)S(1)}, u32[]{:S(2)}, u32[]{:S(2)}) collective-permute-start(bf16[256,768]{1,0:T(8,128)(2,1)S(1)} %convolution_convert_fusion.3), channel_id=1, source_target_pairs={{0,16},{4,20},{8,24},{12,28},{16,0},{20,4},{24,8},{28,12},{1,17},{... | collective-permute-start | bytes 1179656 | tf_op jit(solution)/shard_map/ppermute | solution.py:22
  52.9 31.7 %collective-permute-start.17 = (bf16[256,768]{1,0:T(8,128)(2,1)S(1)}, bf16[256,768]{1,0:T(8,128)(2,1)S(1)}, u32[]{:S(2)}, u32[]{:S(2)}) collective-permute-start(bf16[256,768]{1,0:T(8,128)(2,1)S(1)} %convolution_convert_fusion.2), channel_id=1, source_target_pairs={{0,8},{4,12},{8,0},{12,4},{16,24},{20,28},{24,16},{28,20},{1,9},{5... | collective-permute-start | bytes 1179656 | tf_op jit(solution)/shard_map/ppermute | solution.py:22
  87.8 9.1 %collective-permute-start.18 = (bf16[128,1280]{1,0:T(8,128)(2,1)}, bf16[128,1280]{1,0:T(8,128)(2,1)}, u32[]{:S(2)}, u32[]{:S(2)}) collective-permute-start(bf16[128,1280]{1,0:T(8,128)(2,1)} %slice.149), channel_id=1, source_target_pairs={{0,1},{1,0},{2,3},{3,2},{4,5},{5,4},{6,7},{7,6},{8,9},{9,8},{10,11... | collective-permute-start | bytes 983048 | tf_op jit(solution)/shard_map/ppermute | solution.py:30
  88.6 19.9 %collective-permute-start.20 = (bf16[256,768]{1,0:T(8,128)(2,1)}, bf16[256,768]{1,0:T(8,128)(2,1)}, u32[]{:S(2)}, u32[]{:S(2)}) collective-permute-start(bf16[256,768]{1,0:T(8,128)(2,1)} %pad_maximum_fusion), channel_id=1, source_target_pairs={{0,8},{4,12},{8,0},{12,4},{16,24},{20,28},{24,16},{28,20},{1,9},{5... | collective-permute-start | bytes 1179656 | tf_op jit(solution)/shard_map/ppermute | solution.py:22
  88.9 30.5 %collective-permute-start.24 = (bf16[256,768]{1,0:T(8,128)(2,1)}, bf16[256,768]{1,0:T(8,128)(2,1)}, u32[]{:S(2)}, u32[]{:S(2)}) collective-permute-start(bf16[256,768]{1,0:T(8,128)(2,1)} %pad_maximum_fusion), channel_id=1, source_target_pairs={{0,16},{4,20},{8,24},{12,28},{16,0},{20,4},{24,8},{28,12},{1,17},{... | collective-permute-start | bytes 1179656 | tf_op jit(solution)/shard_map/ppermute | solution.py:22
  92.2 27.1 %collective-permute-start.28 = (bf16[256,768]{1,0:T(8,128)(2,1)}, bf16[256,768]{1,0:T(8,128)(2,1)}, u32[]{:S(2)}, u32[]{:S(2)}) collective-permute-start(bf16[256,768]{1,0:T(8,128)(2,1)} %pad_maximum_fusion), channel_id=1, source_target_pairs={{0,24},{4,28},{8,16},{12,20},{16,8},{20,12},{24,0},{28,4},{1,25},{... | collective-permute-start | bytes 1179656 | tf_op jit(solution)/shard_map/ppermute | solution.py:22
  98.0 33.4 %collective-permute-start.19 = (bf16[64,1280]{1,0:T(8,128)(2,1)S(1)}, bf16[64,1280]{1,0:T(8,128)(2,1)S(1)}, u32[]{:S(2)}, u32[]{:S(2)}) collective-permute-start(bf16[64,1280]{1,0:T(8,128)(2,1)S(1)} %slice.153), channel_id=1, source_target_pairs={{0,2},{1,3},{2,0},{3,1},{4,6},{5,7},{6,4},{7,5},{8,10},{9,11},{10,... | collective-permute-start | bytes 491528 | tf_op jit(solution)/shard_map/ppermute | solution.py:30
  123.8 44.3 %collective-permute-start.32 = (bf16[640,768]{1,0:T(8,128)(2,1)S(1)}, bf16[640,768]{1,0:T(8,128)(2,1)S(1)}, u32[]{:S(2)}, u32[]{:S(2)}) collective-permute-start(bf16[640,768]{1,0:T(8,128)(2,1)S(1)} %dynamic-slice_convert_fusion), channel_id=1, source_target_pairs={{0,4},{4,0},{8,12},{12,8},{16,20},{20,16},{24,28},{28,24},{1,5},{5... | collective-permute-start | bytes 2949128 | tf_op jit(solution)/shard_map/ppermute | solution.py:26
  127.1 4.3 %collective-permute-start.29 = (bf16[128,1280]{1,0:T(8,128)(2,1)S(1)}, bf16[128,1280]{1,0:T(8,128)(2,1)S(1)}, u32[]{:S(2)}, u32[]{:S(2)}) collective-permute-start(bf16[128,1280]{1,0:T(8,128)(2,1)S(1)} %slice.146), channel_id=1, source_target_pairs={{0,1},{1,0},{2,3},{3,2},{4,5},{5,4},{6,7},{7,6},{8,9},{9,8},{10,11... | collective-permute-start | bytes 983048 | tf_op jit(solution)/shard_map/ppermute | solution.py:30
  128.9 3.9 %collective-permute-start.25 = (bf16[128,1280]{1,0:T(8,128)(2,1)S(1)}, bf16[128,1280]{1,0:T(8,128)(2,1)S(1)}, u32[]{:S(2)}, u32[]{:S(2)}) collective-permute-start(bf16[128,1280]{1,0:T(8,128)(2,1)S(1)} %slice.147), channel_id=1, source_target_pairs={{0,1},{1,0},{2,3},{3,2},{4,5},{5,4},{6,7},{7,6},{8,9},{9,8},{10,11... | collective-permute-start | bytes 983048 | tf_op jit(solution)/shard_map/ppermute | solution.py:30
  131.2 2.5 %collective-permute-start.21 = (bf16[128,1280]{1,0:T(8,128)(2,1)S(1)}, bf16[128,1280]{1,0:T(8,128)(2,1)S(1)}, u32[]{:S(2)}, u32[]{:S(2)}) collective-permute-start(bf16[128,1280]{1,0:T(8,128)(2,1)S(1)} %slice.148), channel_id=1, source_target_pairs={{0,1},{1,0},{2,3},{3,2},{4,5},{5,4},{6,7},{7,6},{8,9},{9,8},{10,11... | collective-permute-start | bytes 983048 | tf_op jit(solution)/shard_map/ppermute | solution.py:30
  131.5 7.1 %collective-permute-start.30 = (bf16[64,1280]{1,0:T(8,128)(2,1)S(1)}, bf16[64,1280]{1,0:T(8,128)(2,1)S(1)}, u32[]{:S(2)}, u32[]{:S(2)}) collective-permute-start(bf16[64,1280]{1,0:T(8,128)(2,1)S(1)} %slice.150), channel_id=1, source_target_pairs={{0,2},{1,3},{2,0},{3,1},{4,6},{5,7},{6,4},{7,5},{8,10},{9,11},{10,... | collective-permute-start | bytes 491528 | tf_op jit(solution)/shard_map/ppermute | solution.py:30
  132.9 21.0 %collective-permute-start.26 = (bf16[64,1280]{1,0:T(8,128)(2,1)S(1)}, bf16[64,1280]{1,0:T(8,128)(2,1)S(1)}, u32[]{:S(2)}, u32[]{:S(2)}) collective-permute-start(bf16[64,1280]{1,0:T(8,128)(2,1)S(1)} %slice.151), channel_id=1, source_target_pairs={{0,2},{1,3},{2,0},{3,1},{4,6},{5,7},{6,4},{7,5},{8,10},{9,11},{10,... | collective-permute-start | bytes 491528 | tf_op jit(solution)/shard_map/ppermute | solution.py:30
  133.9 11.3 %collective-permute-start.22 = (bf16[64,1280]{1,0:T(8,128)(2,1)S(1)}, bf16[64,1280]{1,0:T(8,128)(2,1)S(1)}, u32[]{:S(2)}, u32[]{:S(2)}) collective-permute-start(bf16[64,1280]{1,0:T(8,128)(2,1)S(1)} %slice.152), channel_id=1, source_target_pairs={{0,2},{1,3},{2,0},{3,1},{4,6},{5,7},{6,4},{7,5},{8,10},{9,11},{10,... | collective-permute-start | bytes 491528 | tf_op jit(solution)/shard_map/ppermute | solution.py:30
  138.6 25.4 %collective-permute-start.31 = (bf16[64,1280]{1,0:T(8,128)(2,1)S(1)}, bf16[64,1280]{1,0:T(8,128)(2,1)S(1)}, u32[]{:S(2)}, u32[]{:S(2)}) collective-permute-start(bf16[64,1280]{1,0:T(8,128)(2,1)S(1)} %fusion.41), channel_id=1, source_target_pairs={{0,24},{4,28},{8,16},{12,20},{16,8},{20,12},{24,0},{28,4},{1,25},{... | collective-permute-start | bytes 491528 | tf_op jit(solution)/shard_map/ppermute | solution.py:22
  145.3 15.5 %collective-permute-start.23 = (bf16[64,1280]{1,0:T(8,128)(2,1)S(1)}, bf16[64,1280]{1,0:T(8,128)(2,1)S(1)}, u32[]{:S(2)}, u32[]{:S(2)}) collective-permute-start(bf16[64,1280]{1,0:T(8,128)(2,1)S(1)} %fusion.43), channel_id=1, source_target_pairs={{0,8},{4,12},{8,0},{12,4},{16,24},{20,28},{24,16},{28,20},{1,9},{5... | collective-permute-start | bytes 491528 | tf_op jit(solution)/shard_map/ppermute | solution.py:22
  154.0 10.1 %collective-permute-start.27 = (bf16[64,1280]{1,0:T(8,128)(2,1)S(1)}, bf16[64,1280]{1,0:T(8,128)(2,1)S(1)}, u32[]{:S(2)}, u32[]{:S(2)}) collective-permute-start(bf16[64,1280]{1,0:T(8,128)(2,1)S(1)} %fusion.42), channel_id=1, source_target_pairs={{0,16},{4,20},{8,24},{12,28},{16,0},{20,4},{24,8},{28,12},{1,17},{... | collective-permute-start | bytes 491528 | tf_op jit(solution)/shard_map/ppermute | solution.py:22
  (10 other events, 128.3 us)

commit v2 on v1

v2 whole, which is shorter than its diff:
```python
import functools

import jax
import jax.numpy as jnp
from jax import lax
from jax.experimental import pallas as pl
from jax.experimental.pallas import tpu as pltpu
from jax.sharding import PartitionSpec as P

F32 = jnp.float32
BF16 = jnp.bfloat16


def split_dp(dp):
    outer = 1
    while 4 * outer * outer <= 2 * dp:
        outer *= 2
    return outer, dp // outer


def after(value, *others):
    return lax.optimization_barrier((value,) + others)[0]


def gate_kernel(steps, order_ref, pre_ref, prob_ref, cot_ref, *refs):
    part_refs, (hidden_ref, grad_ref) = refs[:-2], refs[-2:]
    rows, width = cot_ref.shape
    cap = rows // steps
    for i in range(steps):
        here = pl.ds(i * cap, cap)
        there = pl.ds(pl.multiple_of(order_ref[i] * cap, cap), cap)
        total = pre_ref[here, :]
        for part_ref in part_refs:
            total = total + part_ref[here, :].astype(F32)
        gate, up = total[:, :width], total[:, width:]
        prob = prob_ref[here, :].astype(F32)
        sig = jax.nn.sigmoid(gate)
        act = gate * sig
        hidden_ref[there, :] = (prob * act * up).astype(BF16)
        scaled = cot_ref[there, :].astype(F32) * prob
        grad_ref[here, :width] = (scaled * up * sig * (1.0 + gate * (1.0 - sig))).astype(BF16)
        grad_ref[here, width:] = (scaled * act).astype(BF16)


def gate_call(order, pre, prob, cotangent, parts):
    rows, width = cotangent.shape
    steps = order.shape[0]
    vmem = pl.BlockSpec(memory_space=pltpu.VMEM)
    return pl.pallas_call(
        functools.partial(gate_kernel, steps),
        out_shape=(
            jax.ShapeDtypeStruct((rows, width), BF16),
            jax.ShapeDtypeStruct((rows, 2 * width), BF16),
        ),
        in_specs=[pl.BlockSpec(memory_space=pltpu.SMEM)] + [vmem] * (3 + len(parts)),
        out_specs=(vmem, vmem),
        compiler_params=pltpu.CompilerParams(vmem_limit_bytes=24 * 2**20),
        cost_estimate=pl.CostEstimate(
            flops=20 * rows * width, bytes_accessed=rows * width * 30, transcendentals=rows * width
        ),
    )(order, pre, prob, cotangent, *parts)


def make_shards(dp_size, etp_size):
    outer, inner = split_dp(dp_size)

    def over_outer(value, k):
        pairs = [(i, i ^ (k * inner)) for i in range(dp_size)]
        return lax.ppermute(value, "dp", pairs)

    def over_inner(value, j):
        pairs = [(i, i ^ j) for i in range(dp_size)]
        return lax.ppermute(value, "dp", pairs)

    def over_etp(value, e):
        pairs = [(i, i ^ e) for i in range(etp_size)]
        return lax.ppermute(value, "etp", pairs)

    chunk_order = [0]
    bit = etp_size // 2
    bits = []
    while bit:
        bits.append(bit)
        chunk_order = chunk_order + [c ^ bit for c in chunk_order]
        bit //= 2

    def gather_etp(value):
        for b in bits:
            value = jnp.concatenate([value, over_etp(value, b)], axis=0)
        return value

    def reduce_etp(value):
        for b in reversed(bits):
            half = value.shape[0] // 2
            sent = over_etp(value[half:].astype(BF16), b)
            value = value[:half] + sent.astype(F32)
        return value

    far_first = sorted(range(1, outer), key=lambda k: -k)
    near_first = sorted(range(1, outer))

    def shards(tokens, slots, gate_probs, w_gate, w_up, d_hidden):
        dp = lax.axis_index("dp")
        etp = lax.axis_index("etp")
        a, b = dp // inner, dp % inner
        depth, width = w_gate.shape
        cap = slots.shape[0]
        tok = tokens.shape[0]
        span = depth * inner

        weights = [jnp.concatenate([w_gate, w_up], axis=1)]
        for j in range(1, inner):
            weights.append(jnp.concatenate([over_inner(w_gate, j), over_inner(w_up, j)], axis=1))
        weights = jnp.concatenate(weights, axis=0)

        onehot = (slots[:, None] == jnp.arange(tok, dtype=slots.dtype)[None, :]).astype(BF16)
        rows = jnp.dot(onehot, tokens, preferred_element_type=F32).astype(BF16)
        pieces = {}
        for k in far_first + [0]:
            pieces[k] = jnp.concatenate(
                [
                    lax.dynamic_slice(rows, (0, (a ^ k) * span + (b ^ j) * depth), (cap, depth))
                    for j in range(inner)
                ],
                axis=1,
            )
        got = {k: over_outer(pieces[k], k) for k in far_first}
        x_chunks = {k: gather_etp(got[k]) for k in far_first}
        x_chunks[0] = gather_etp(after(pieces[0], got[near_first[0]]))
        probs = gather_etp(after(gate_probs, x_chunks[0]))

        parts = {
            k: over_outer(jnp.dot(x_chunks[k], weights, preferred_element_type=F32).astype(BF16), k)
            for k in far_first
        }
        pre = jnp.dot(x_chunks[0], weights, preferred_element_type=F32)
        order = etp ^ jnp.array(chunk_order, jnp.int32)
        hidden, paired = gate_call(
            order, pre, probs[:, None], d_hidden, [parts[k] for k in near_first]
        )

        grads = {k: over_outer(paired, k) for k in far_first}
        grads[0] = paired

        dx = jnp.zeros((cap, outer * span), BF16)
        last = paired
        for k in [0] + near_first:
            partial = lax.dot_general(
                after(grads[k], last), weights, (((1,), (1,)), ((), ())), preferred_element_type=F32
            )
            last = partial
            own = reduce_etp(partial).astype(BF16)
            own = over_outer(own, k) if k else own
            for j in range(inner):
                block = own[:, j * depth : (j + 1) * depth]
                dx = lax.dynamic_update_slice(dx, block, (0, (a ^ k) * span + (b ^ j) * depth))
        grad_tokens = lax.dot_general(
            onehot, dx, (((0,), (0,)), ((), ())), preferred_element_type=F32
        ).astype(BF16)

        keys = [0] + near_first
        summed = lax.dot_general(
            jnp.concatenate([x_chunks[k] for k in keys], axis=0),
            after(jnp.concatenate([grads[k] for k in keys], axis=0), last),
            (((0,), (0,)), ((), ())),
            preferred_element_type=F32,
        )
        total = summed[:depth]
        for j in range(1, inner):
            part = summed[j * depth : (j + 1) * depth]
            total = total + over_inner(part.astype(BF16), j).astype(F32)
        return (hidden, grad_tokens, total[:, :width], total[:, width:])

    return shards


def solution(mesh):
    in_specs = (
        P(("dp", "etp"), None),
        P(("dp", "etp")),
        P(("dp", "etp")),
        P("dp", "etp"),
        P("dp", "etp"),
        P("dp", "etp"),
    )
    out_specs = (P("dp", "etp"), P(("dp", "etp"), None), P("dp", "etp"), P("dp", "etp"))
    shards = make_shards(mesh.shape["dp"], mesh.shape["etp"])
    return jax.shard_map(shards, mesh=mesh, in_specs=in_specs, out_specs=out_specs, check_vma=False)
```

time: 170 us -> 146 us (0.86)
  local copies, waits for them, and re-layouts: 14.7 us -> 2.38 us
  other arithmetic: 9.2 us -> 1.13 us
  matrix products: 20.5 us -> 15.4 us
  starting transfers between devices: 42.5 us -> 39.6 us
    unnamed x29 -> x23, local copies, waits for them, and re-layouts: 7.88 us -> 0.25 us
    dot_general x5, matrix products: 10.1 us -> 5.16 us  [the longest x4 2.83 us: shards(): lax.dot_general(after(grads[k], last), weights, (((1,), (1,)), ((), ())),...]
    ppermute x12, starting transfers between devices: 26 us -> 21.5 us  [over_outer(): return lax.ppermute(value, 'dp', pairs)]
    gather x2 -> x0, local copies, waits for them, and re-layouts: 2.76 us -> none  [the longest x1 2.17 us: shards(): jnp.take(hidden.reshape(etp_size, cap, width), inverse, axis=0)]
    dynamic_update_slice x3 -> x0, other arithmetic: 2.5 us -> none  [the longest x2 2.47 us: shards(): weights = lax.dynamic_update_slice(weights, both, (b ^ j, 0, 0))]
    select_n x3 -> x0, other arithmetic: 1.85 us -> none  [the longest x2 1.75 us: shards(): jnp.take(hidden.reshape(etp_size, cap, width), inverse, axis=0)]
  transfers between devices with their start and end apart: 33 -> 33, of which waited for: 13 -> 15; matrix products, arithmetic and copies ran while one was open for 21% -> 11% of each run, Pallas kernels for 0% -> 0%
where the time goes in v2:
time: 146 us; the launch traced here: 144 us
  waiting for transfers between devices  83.1 us (57%)
  starting transfers between devices  39.6 us (27%)
  matrix products  15.4 us (11%)
  local copies, waits for them, and re-layouts  2.38 us (2%)
  Pallas kernels  1.65 us (1%)
    ppermute x12, waiting for transfers between devices, over_outer(): return lax.ppermute(value, 'dp', pairs)  65.7 us
    ppermute x12, starting transfers between devices, over_outer(): return lax.ppermute(value, 'dp', pairs)  21.5 us
    ppermute x18, waiting for transfers between devices, over_etp(): return lax.ppermute(value, 'etp', pairs)  17.4 us
    ppermute x18, starting transfers between devices, over_etp(): return lax.ppermute(value, 'etp', pairs)  13.5 us
    ppermute x3, starting transfers between devices, over_inner(): return lax.ppermute(value, 'dp', pairs)  4.66 us
    dot_general x1, matrix products, shards(): lax.dot_general(onehot, dx, (((0,), (0,)), ((), ())), preferred_element_t...  4 us
    dot_general x1, matrix products, shards(): rows = jnp.dot(onehot, tokens, preferred_element_type=F32).astype(BF16)  3.57 us
  transfers between devices with their start and end apart: 33, of which 15 were waited for; matrix products, arithmetic and copies ran while one was open for 11% of the time, Pallas kernels for 0%

profile of v2, /device:TPU:0, one launch (start us, length us, event | category | flops | bytes accessed | tf_op | source)
XLA Modules:
  0.0 144.4 jit_solution(3309220833023226712)
XLA Ops:
  0.6 3.0 %collective-permute-start.3 = (bf16[640,384]{1,0:T(8,128)(2,1)}, bf16[640,384]{1,0:T(8,128)(2,1)S(1)}, u32[]{:S(2)}, u32[]{:S(2)}) collective-permute-start(bf16[640,384]{1,0:T(8,128)(2,1)} %param.10), channel_id=1, source_target_pairs={{0,4},{4,0},{8,12},{12,8},{16,20},{20,16},{24,28},{28,24},{1,5},{5... | collective-permute-start | bytes 1474568 | tf_op jit(solution)/shard_map/ppermute | solution.py:73
  3.7 3.6 %convolution_convert_fusion.1 = bf16[64,5120]{1,0:T(8,128)(2,1)S(1)} fusion(bf16[512,5120]{1,0:T(8,128)(2,1)} %param.7, s32[64]{0:T(128)} %param.8), kind=kOutput, calls=%fused_computation.1 | convolution fusion | flops 335904768 | bytes 5898496 | tf_op jit(solution)/shard_map/dot_general | solution.py:117
  7.4 2.1 %collective-permute-start = (bf16[64,1280]{1,0:T(8,128)(2,1)S(1)}, bf16[64,1280]{1,0:T(8,128)(2,1)S(1)}, u32[]{:S(2)}, u32[]{:S(2)}) collective-permute-start(bf16[64,1280]{1,0:T(8,128)(2,1)S(1)} %pad_maximum_fusion.6), channel_id=1, source_target_pairs={{0,8},{4,12},{8,0},{12,4},{16,24},{20,28},{24,16},{28,20},{1,9},{5... | collective-permute-start | bytes 491528 | tf_op jit(solution)/shard_map/ppermute | solution.py:69
  9.5 2.7 %collective-permute-start.10 = (bf16[64,1280]{1,0:T(8,128)(2,1)S(1)}, bf16[64,1280]{1,0:T(8,128)(2,1)S(1)}, u32[]{:S(2)}, u32[]{:S(2)}) collective-permute-start(bf16[64,1280]{1,0:T(8,128)(2,1)S(1)} %pad_maximum_fusion.7), channel_id=1, source_target_pairs={{0,16},{4,20},{8,24},{12,28},{16,0},{20,4},{24,8},{28,12},{1,17},{... | collective-permute-start | bytes 491528 | tf_op jit(solution)/shard_map/ppermute | solution.py:69
  12.4 2.8 %collective-permute-done = bf16[64,1280]{1,0:T(8,128)(2,1)S(1)} collective-permute-done((bf16[64,1280]{1,0:T(8,128)(2,1)S(1)}, bf16[64,1280]{1,0:T(8,128)(2,1)S(1)}, u32[]{:S(2)}, u32[]{:S(2)}) %collective-permute-start) | collective-permute-done | bytes 163872 | tf_op jit(solution)/shard_map/ppermute | solution.py:69
  15.2 1.7 %collective-permute-start.1 = (bf16[64,1280]{1,0:T(8,128)(2,1)S(1)}, bf16[64,1280]{1,0:T(8,128)(2,1)S(1)}, u32[]{:S(2)}, u32[]{:S(2)}) collective-permute-start(bf16[64,1280]{1,0:T(8,128)(2,1)S(1)} %pad_maximum_fusion.5), channel_id=1, source_target_pairs={{0,2},{1,3},{2,0},{3,1},{4,6},{5,7},{6,4},{7,5},{8,10},{9,11},{10,... | collective-permute-start | bytes 491528 | tf_op jit(solution)/shard_map/ppermute | solution.py:77
  16.9 7.5 %collective-permute-done.10 = bf16[64,1280]{1,0:T(8,128)(2,1)S(1)} collective-permute-done((bf16[64,1280]{1,0:T(8,128)(2,1)S(1)}, bf16[64,1280]{1,0:T(8,128)(2,1)S(1)}, u32[]{:S(2)}, u32[]{:S(2)}) %collective-permute-start.10) | collective-permute-done | bytes 163872 | tf_op jit(solution)/shard_map/ppermute | solution.py:69
  28.0 1.7 %collective-permute-done.7 = bf16[64,1280]{1,0:T(8,128)(2,1)S(1)} collective-permute-done((bf16[64,1280]{1,0:T(8,128)(2,1)S(1)}, bf16[64,1280]{1,0:T(8,128)(2,1)S(1)}, u32[]{:S(2)}, u32[]{:S(2)}) %collective-permute-start.7) | collective-permute-done | bytes 163872 | tf_op jit(solution)/shard_map/ppermute | solution.py:77
  29.8 1.7 %collective-permute-done.11 = bf16[64,1280]{1,0:T(8,128)(2,1)S(1)} collective-permute-done((bf16[64,1280]{1,0:T(8,128)(2,1)S(1)}, bf16[64,1280]{1,0:T(8,128)(2,1)S(1)}, u32[]{:S(2)}, u32[]{:S(2)}) %collective-permute-start.11) | collective-permute-done | bytes 163872 | tf_op jit(solution)/shard_map/ppermute | solution.py:77
  31.5 1.7 %collective-permute-done.15 = bf16[64,1280]{1,0:T(8,128)(2,1)S(1)} collective-permute-done((bf16[64,1280]{1,0:T(8,128)(2,1)S(1)}, bf16[64,1280]{1,0:T(8,128)(2,1)S(1)}, u32[]{:S(2)}, u32[]{:S(2)}) %collective-permute-start.15) | collective-permute-done | bytes 163872 | tf_op jit(solution)/shard_map/ppermute | solution.py:77
  34.8 3.0 %collective-permute-start.9 = (bf16[256,768]{1,0:T(8,128)(2,1)S(1)}, bf16[256,768]{1,0:T(8,128)(2,1)S(1)}, u32[]{:S(2)}, u32[]{:S(2)}) collective-permute-start(bf16[256,768]{1,0:T(8,128)(2,1)S(1)} %convolution_convert_fusion.4), channel_id=1, source_target_pairs={{0,8},{4,12},{8,0},{12,4},{16,24},{20,28},{24,16},{28,20},{1,9},{5... | collective-permute-start | bytes 1179656 | tf_op jit(solution)/shard_map/ppermute | solution.py:69
  39.4 2.3 %collective-permute-start.17 = (bf16[256,768]{1,0:T(8,128)(2,1)S(1)}, bf16[256,768]{1,0:T(8,128)(2,1)S(1)}, u32[]{:S(2)}, u32[]{:S(2)}) collective-permute-start(bf16[256,768]{1,0:T(8,128)(2,1)S(1)} %convolution_convert_fusion.2), channel_id=1, source_target_pairs={{0,24},{4,28},{8,16},{12,20},{16,8},{20,12},{24,0},{28,4},{1,25},{... | collective-permute-start | bytes 1179656 | tf_op jit(solution)/shard_map/ppermute | solution.py:69
  42.4 1.6 %collective-permute-start.5 = (bf16[64]{0:T(256)(128)(2,1)S(1)}, bf16[64]{0:T(256)(128)(2,1)S(1)}, u32[]{:S(2)}, u32[]{:S(2)}) collective-permute-start(bf16[64]{0:T(256)(128)(2,1)S(1)} %copy-done.4), channel_id=1, source_target_pairs={{0,2},{1,3},{2,0},{3,1},{4,6},{5,7},{6,4},{7,5},{8,10},{9,11},{10,... | collective-permute-start | bytes 392 | tf_op jit(solution)/shard_map/ppermute | solution.py:77
  44.1 1.9 %collective-permute-done.5 = bf16[64]{0:T(256)(128)(2,1)S(1)} collective-permute-done((bf16[64]{0:T(256)(128)(2,1)S(1)}, bf16[64]{0:T(256)(128)(2,1)S(1)}, u32[]{:S(2)}, u32[]{:S(2)}) %collective-permute-start.5) | collective-permute-done | bytes 160 | tf_op jit(solution)/shard_map/ppermute | solution.py:77
  47.4 6.4 %collective-permute-done.9.refs_0_ = bf16[256,768]{1,0:T(8,128)(2,1)S(1)} collective-permute-done((bf16[256,768]{1,0:T(8,128)(2,1)S(1)}, bf16[256,768]{1,0:T(8,128)(2,1)S(1)}, u32[]{:S(2)}, u32[]{:S(2)}) %collective-permute-start.9) | collective-permute-done | bytes 393248 | tf_op jit(solution)/shard_map/ppermute | solution.py:69
  53.8 14.5 %collective-permute-done.13.refs_1_ = bf16[256,768]{1,0:T(8,128)(2,1)S(1)} collective-permute-done((bf16[256,768]{1,0:T(8,128)(2,1)S(1)}, bf16[256,768]{1,0:T(8,128)(2,1)S(1)}, u32[]{:S(2)}, u32[]{:S(2)}) %collective-permute-start.13) | collective-permute-done | bytes 393248 | tf_op jit(solution)/shard_map/ppermute | solution.py:69
  68.3 1.6 %shard_map.102 = (bf16[256,384]{1,0:T(8,128)(2,1)}, bf16[256,768]{1,0:T(8,128)(2,1)S(1)}) custom-call(s32[4]{0:T(128)S(1)} %broadcast_xor_fusion.order_ref, f32[256,768]{1,0:T(8,128)S(1)} %fusion.25.pre_ref, bf16[256,1]{1,0:T(8,128)(2,1)S(1)} %broadcast_in_dim.10.prob_ref, bf16[256,384]{1,0:T(8,128)(2,1)S(1)} %copy-done, ...), custom_call_target="tpu_custom_call" | custom-call | flops 1966080 | bytes 2949120 | tf_op jit(solution)/shard_map/pallas_call | solution.py:49
  70.8 1.7 %collective-permute-start.28 = (bf16[256,768]{1,0:T(8,128)(2,1)S(1)}, bf16[256,768]{1,0:T(8,128)(2,1)S(1)}, u32[]{:S(2)}, u32[]{:S(2)}) collective-permute-start(bf16[256,768]{1,0:T(8,128)(2,1)S(1)} %get-tuple-element.17), channel_id=1, source_target_pairs={{0,24},{4,28},{8,16},{12,20},{16,8},{20,12},{24,0},{28,4},{1,25},{... | collective-permute-start | bytes 1179656 | tf_op jit(solution)/shard_map/ppermute | solution.py:69
  72.5 7.6 %collective-permute-start.24 = (bf16[256,768]{1,0:T(8,128)(2,1)S(1)}, bf16[256,768]{1,0:T(8,128)(2,1)S(1)}, u32[]{:S(2)}, u32[]{:S(2)}) collective-permute-start(bf16[256,768]{1,0:T(8,128)(2,1)S(1)} %get-tuple-element.17), channel_id=1, source_target_pairs={{0,16},{4,20},{8,24},{12,28},{16,0},{20,4},{24,8},{28,12},{1,17},{... | collective-permute-start | bytes 1179656 | tf_op jit(solution)/shard_map/ppermute | solution.py:69
  80.2 1.6 %collective-permute-start.19 = (bf16[64,1280]{1,0:T(8,128)(2,1)S(1)}, bf16[64,1280]{1,0:T(8,128)(2,1)S(1)}, u32[]{:S(2)}, u32[]{:S(2)}) collective-permute-start(bf16[64,1280]{1,0:T(8,128)(2,1)S(1)} %slice.191), channel_id=1, source_target_pairs={{0,2},{1,3},{2,0},{3,1},{4,6},{5,7},{6,4},{7,5},{8,10},{9,11},{10,... | collective-permute-start | bytes 491528 | tf_op jit(solution)/shard_map/ppermute | solution.py:77
  81.8 16.6 %collective-permute-done.20 = bf16[256,768]{1,0:T(8,128)(2,1)S(1)} collective-permute-done((bf16[256,768]{1,0:T(8,128)(2,1)S(1)}, bf16[256,768]{1,0:T(8,128)(2,1)S(1)}, u32[]{:S(2)}, u32[]{:S(2)}) %collective-permute-start.20) | collective-permute-done | bytes 393248 | tf_op jit(solution)/shard_map/ppermute | solution.py:69
  99.2 10.3 %collective-permute-done.24 = bf16[256,768]{1,0:T(8,128)(2,1)S(1)} collective-permute-done((bf16[256,768]{1,0:T(8,128)(2,1)S(1)}, bf16[256,768]{1,0:T(8,128)(2,1)S(1)}, u32[]{:S(2)}, u32[]{:S(2)}) %collective-permute-start.24) | collective-permute-done | bytes 393248 | tf_op jit(solution)/shard_map/ppermute | solution.py:69
  111.8 2.3 %fusion.30 = f32[1280,768]{1,0:T(8,128)S(1)} fusion(bf16[1024,1280]{1,0:T(8,128)(2,1)S(1)} %constant_dynamic-update-slice_fusion.3, bf16[1024,768]{1,0:T(8,128)(2,1)S(1)} %pad_maximum_fusion), kind=kOutput, calls=%fused_computation.98 | convolution fusion | flops 2013265920 | bytes 8126464 | tf_op jit(solution)/shard_map/dot_general | solution.py:162
  114.2 1.6 %collective-permute-start.32 = (bf16[640,768]{1,0:T(8,128)(2,1)S(1)}, bf16[640,768]{1,0:T(8,128)(2,1)S(1)}, u32[]{:S(2)}, u32[]{:S(2)}) collective-permute-start(bf16[640,768]{1,0:T(8,128)(2,1)S(1)} %slice.183), channel_id=1, source_target_pairs={{0,4},{4,0},{8,12},{12,8},{16,20},{20,16},{24,28},{28,24},{1,5},{5... | collective-permute-start | bytes 2949128 | tf_op jit(solution)/shard_map/ppermute | solution.py:73
  116.0 1.6 %collective-permute-start.22 = (bf16[64,1280]{1,0:T(8,128)(2,1)S(1)}, bf16[64,1280]{1,0:T(8,128)(2,1)S(1)}, u32[]{:S(2)}, u32[]{:S(2)}) collective-permute-start(bf16[64,1280]{1,0:T(8,128)(2,1)S(1)} %slice.190), channel_id=1, source_target_pairs={{0,2},{1,3},{2,0},{3,1},{4,6},{5,7},{6,4},{7,5},{8,10},{9,11},{10,... | collective-permute-start | bytes 491528 | tf_op jit(solution)/shard_map/ppermute | solution.py:77
  118.4 1.6 %collective-permute-start.30 = (bf16[64,1280]{1,0:T(8,128)(2,1)S(1)}, bf16[64,1280]{1,0:T(8,128)(2,1)S(1)}, u32[]{:S(2)}, u32[]{:S(2)}) collective-permute-start(bf16[64,1280]{1,0:T(8,128)(2,1)S(1)} %slice.188), channel_id=1, source_target_pairs={{0,2},{1,3},{2,0},{3,1},{4,6},{5,7},{6,4},{7,5},{8,10},{9,11},{10,... | collective-permute-start | bytes 491528 | tf_op jit(solution)/shard_map/ppermute | solution.py:77
  119.9 3.2 %collective-permute-done.22 = bf16[64,1280]{1,0:T(8,128)(2,1)S(1)} collective-permute-done((bf16[64,1280]{1,0:T(8,128)(2,1)S(1)}, bf16[64,1280]{1,0:T(8,128)(2,1)S(1)}, u32[]{:S(2)}, u32[]{:S(2)}) %collective-permute-start.22) | collective-permute-done | bytes 163872 | tf_op jit(solution)/shard_map/ppermute | solution.py:77
  123.2 3.4 %collective-permute-done.26 = bf16[64,1280]{1,0:T(8,128)(2,1)S(1)} collective-permute-done((bf16[64,1280]{1,0:T(8,128)(2,1)S(1)}, bf16[64,1280]{1,0:T(8,128)(2,1)S(1)}, u32[]{:S(2)}, u32[]{:S(2)}) %collective-permute-start.26) | collective-permute-done | bytes 163872 | tf_op jit(solution)/shard_map/ppermute | solution.py:77
  126.7 2.6 %collective-permute-done.30 = bf16[64,1280]{1,0:T(8,128)(2,1)S(1)} collective-permute-done((bf16[64,1280]{1,0:T(8,128)(2,1)S(1)}, bf16[64,1280]{1,0:T(8,128)(2,1)S(1)}, u32[]{:S(2)}, u32[]{:S(2)}) %collective-permute-start.30) | collective-permute-done | bytes 163872 | tf_op jit(solution)/shard_map/ppermute | solution.py:77
  129.4 1.7 %collective-permute-start.31 = (bf16[64,1280]{1,0:T(8,128)(2,1)S(1)}, bf16[64,1280]{1,0:T(8,128)(2,1)S(1)}, u32[]{:S(2)}, u32[]{:S(2)}) collective-permute-start(bf16[64,1280]{1,0:T(8,128)(2,1)S(1)} %fusion.15), channel_id=1, source_target_pairs={{0,24},{4,28},{8,16},{12,20},{16,8},{20,12},{24,0},{28,4},{1,25},{... | collective-permute-start | bytes 491528 | tf_op jit(solution)/shard_map/ppermute | solution.py:69
  131.1 7.6 %collective-permute-done.27 = bf16[64,1280]{1,0:T(8,128)(2,1)S(1)} collective-permute-done((bf16[64,1280]{1,0:T(8,128)(2,1)S(1)}, bf16[64,1280]{1,0:T(8,128)(2,1)S(1)}, u32[]{:S(2)}, u32[]{:S(2)}) %collective-permute-start.27) | collective-permute-done | bytes 163872 | tf_op jit(solution)/shard_map/ppermute | solution.py:69
  138.9 4.0 %convolution_convert_fusion = bf16[512,5120]{1,0:T(8,128)(2,1)} fusion(bf16[64,5120]{1,0:T(8,128)(2,1)S(1)} %slice_dynamic-update-slice_fusion, s32[64]{0:T(128)S(1)} %copy-done.3), kind=kOutput, calls=%fused_computation | convolution fusion | flops 338198528 | bytes 5898496 | tf_op jit(solution)/shard_map/dot_general | solution.py:157
  (113 shorter events, 16.2 us)
Async XLA Ops:
  0.6 32.7 %collective-permute-start.3 = (bf16[640,384]{1,0:T(8,128)(2,1)}, bf16[640,384]{1,0:T(8,128)(2,1)S(1)}, u32[]{:S(2)}, u32[]{:S(2)}) collective-permute-start(bf16[640,384]{1,0:T(8,128)(2,1)} %param.10), channel_id=1, source_target_pairs={{0,4},{4,0},{8,12},{12,8},{16,20},{20,16},{24,28},{28,24},{1,5},{5... | collective-permute-start | bytes 1474568 | tf_op jit(solution)/shard_map/ppermute | solution.py:73
  3.6 30.3 %collective-permute-start.4 = (bf16[640,384]{1,0:T(8,128)(2,1)}, bf16[640,384]{1,0:T(8,128)(2,1)S(1)}, u32[]{:S(2)}, u32[]{:S(2)}) collective-permute-start(bf16[640,384]{1,0:T(8,128)(2,1)} %param.11), channel_id=1, source_target_pairs={{0,4},{4,0},{8,12},{12,8},{16,20},{20,16},{24,28},{28,24},{1,5},{5... | collective-permute-start | bytes 1474568 | tf_op jit(solution)/shard_map/ppermute | solution.py:73
  7.4 7.7 %collective-permute-start = (bf16[64,1280]{1,0:T(8,128)(2,1)S(1)}, bf16[64,1280]{1,0:T(8,128)(2,1)S(1)}, u32[]{:S(2)}, u32[]{:S(2)}) collective-permute-start(bf16[64,1280]{1,0:T(8,128)(2,1)S(1)} %pad_maximum_fusion.6), channel_id=1, source_target_pairs={{0,8},{4,12},{8,0},{12,4},{16,24},{20,28},{24,16},{28,20},{1,9},{5... | collective-permute-start | bytes 491528 | tf_op jit(solution)/shard_map/ppermute | solution.py:69
  9.5 14.9 %collective-permute-start.10 = (bf16[64,1280]{1,0:T(8,128)(2,1)S(1)}, bf16[64,1280]{1,0:T(8,128)(2,1)S(1)}, u32[]{:S(2)}, u32[]{:S(2)}) collective-permute-start(bf16[64,1280]{1,0:T(8,128)(2,1)S(1)} %pad_maximum_fusion.7), channel_id=1, source_target_pairs={{0,16},{4,20},{8,24},{12,28},{16,0},{20,4},{24,8},{28,12},{1,17},{... | collective-permute-start | bytes 491528 | tf_op jit(solution)/shard_map/ppermute | solution.py:69
  12.2 13.7 %collective-permute-start.14 = (bf16[64,1280]{1,0:T(8,128)(2,1)S(1)}, bf16[64,1280]{1,0:T(8,128)(2,1)S(1)}, u32[]{:S(2)}, u32[]{:S(2)}) collective-permute-start(bf16[64,1280]{1,0:T(8,128)(2,1)S(1)} %pad_maximum_fusion.8), channel_id=1, source_target_pairs={{0,24},{4,28},{8,16},{12,20},{16,8},{20,12},{24,0},{28,4},{1,25},{... | collective-permute-start | bytes 491528 | tf_op jit(solution)/shard_map/ppermute | solution.py:69
  15.2 11.3 %collective-permute-start.1 = (bf16[64,1280]{1,0:T(8,128)(2,1)S(1)}, bf16[64,1280]{1,0:T(8,128)(2,1)S(1)}, u32[]{:S(2)}, u32[]{:S(2)}) collective-permute-start(bf16[64,1280]{1,0:T(8,128)(2,1)S(1)} %pad_maximum_fusion.5), channel_id=1, source_target_pairs={{0,2},{1,3},{2,0},{3,1},{4,6},{5,7},{6,4},{7,5},{8,10},{9,11},{10,... | collective-permute-start | bytes 491528 | tf_op jit(solution)/shard_map/ppermute | solution.py:77
  24.4 5.3 %collective-permute-start.7 = (bf16[64,1280]{1,0:T(8,128)(2,1)S(1)}, bf16[64,1280]{1,0:T(8,128)(2,1)S(1)}, u32[]{:S(2)}, u32[]{:S(2)}) collective-permute-start(bf16[64,1280]{1,0:T(8,128)(2,1)S(1)} %collective-permute-done), channel_id=1, source_target_pairs={{0,2},{1,3},{2,0},{3,1},{4,6},{5,7},{6,4},{7,5},{8,10},{9,11},{10,... | collective-permute-start | bytes 491528 | tf_op jit(solution)/shard_map/ppermute | solution.py:77
  26.0 5.6 %collective-permute-start.11 = (bf16[64,1280]{1,0:T(8,128)(2,1)S(1)}, bf16[64,1280]{1,0:T(8,128)(2,1)S(1)}, u32[]{:S(2)}, u32[]{:S(2)}) collective-permute-start(bf16[64,1280]{1,0:T(8,128)(2,1)S(1)} %collective-permute-done.10), channel_id=1, source_target_pairs={{0,2},{1,3},{2,0},{3,1},{4,6},{5,7},{6,4},{7,5},{8,10},{9,11},{10,... | collective-permute-start | bytes 491528 | tf_op jit(solution)/shard_map/ppermute | solution.py:77
  26.5 6.8 %collective-permute-start.15 = (bf16[64,1280]{1,0:T(8,128)(2,1)S(1)}, bf16[64,1280]{1,0:T(8,128)(2,1)S(1)}, u32[]{:S(2)}, u32[]{:S(2)}) collective-permute-start(bf16[64,1280]{1,0:T(8,128)(2,1)S(1)} %collective-permute-done.14), channel_id=1, source_target_pairs={{0,2},{1,3},{2,0},{3,1},{4,6},{5,7},{6,4},{7,5},{8,10},{9,11},{10,... | collective-permute-start | bytes 491528 | tf_op jit(solution)/shard_map/ppermute | solution.py:77
  29.7 11.9 %collective-permute-start.2 = (bf16[128,1280]{1,0:T(8,128)(2,1)S(1)}, bf16[128,1280]{1,0:T(8,128)(2,1)S(1)}, u32[]{:S(2)}, u32[]{:S(2)}) collective-permute-start(bf16[128,1280]{1,0:T(8,128)(2,1)S(1)} %pad_maximum_fusion.1), channel_id=1, source_target_pairs={{0,1},{1,0},{2,3},{3,2},{4,5},{5,4},{6,7},{7,6},{8,9},{9,8},{10,11... | collective-permute-start | bytes 983048 | tf_op jit(solution)/shard_map/ppermute | solution.py:77
  31.5 2.6 %collective-permute-start.8 = (bf16[128,1280]{1,0:T(8,128)(2,1)S(1)}, bf16[128,1280]{1,0:T(8,128)(2,1)S(1)}, u32[]{:S(2)}, u32[]{:S(2)}) collective-permute-start(bf16[128,1280]{1,0:T(8,128)(2,1)S(1)} %pad_maximum_fusion.2), channel_id=1, source_target_pairs={{0,1},{1,0},{2,3},{3,2},{4,5},{5,4},{6,7},{7,6},{8,9},{9,8},{10,11... | collective-permute-start | bytes 983048 | tf_op jit(solution)/shard_map/ppermute | solution.py:77
  33.3 4.5 %collective-permute-start.12 = (bf16[128,1280]{1,0:T(8,128)(2,1)S(1)}, bf16[128,1280]{1,0:T(8,128)(2,1)S(1)}, u32[]{:S(2)}, u32[]{:S(2)}) collective-permute-start(bf16[128,1280]{1,0:T(8,128)(2,1)S(1)} %pad_maximum_fusion.3), channel_id=1, source_target_pairs={{0,1},{1,0},{2,3},{3,2},{4,5},{5,4},{6,7},{7,6},{8,9},{9,8},{10,11... | collective-permute-start | bytes 983048 | tf_op jit(solution)/shard_map/ppermute | solution.py:77
  33.3 5.4 %collective-permute-start.16 = (bf16[128,1280]{1,0:T(8,128)(2,1)S(1)}, bf16[128,1280]{1,0:T(8,128)(2,1)S(1)}, u32[]{:S(2)}, u32[]{:S(2)}) collective-permute-start(bf16[128,1280]{1,0:T(8,128)(2,1)S(1)} %pad_maximum_fusion.4), channel_id=1, source_target_pairs={{0,1},{1,0},{2,3},{3,2},{4,5},{5,4},{6,7},{7,6},{8,9},{9,8},{10,11... | collective-permute-start | bytes 983048 | tf_op jit(solution)/shard_map/ppermute | solution.py:77
  34.8 19.0 %collective-permute-start.9 = (bf16[256,768]{1,0:T(8,128)(2,1)S(1)}, bf16[256,768]{1,0:T(8,128)(2,1)S(1)}, u32[]{:S(2)}, u32[]{:S(2)}) collective-permute-start(bf16[256,768]{1,0:T(8,128)(2,1)S(1)} %convolution_convert_fusion.4), channel_id=1, source_target_pairs={{0,8},{4,12},{8,0},{12,4},{16,24},{20,28},{24,16},{28,20},{1,9},{5... | collective-permute-start | bytes 1179656 | tf_op jit(solution)/shard_map/ppermute | solution.py:69
  38.4 29.8 %collective-permute-start.13 = (bf16[256,768]{1,0:T(8,128)(2,1)S(1)}, bf16[256,768]{1,0:T(8,128)(2,1)S(1)}, u32[]{:S(2)}, u32[]{:S(2)}) collective-permute-start(bf16[256,768]{1,0:T(8,128)(2,1)S(1)} %convolution_convert_fusion.3), channel_id=1, source_target_pairs={{0,16},{4,20},{8,24},{12,28},{16,0},{20,4},{24,8},{28,12},{1,17},{... | collective-permute-start | bytes 1179656 | tf_op jit(solution)/shard_map/ppermute | solution.py:69
  39.4 28.9 %collective-permute-start.17 = (bf16[256,768]{1,0:T(8,128)(2,1)S(1)}, bf16[256,768]{1,0:T(8,128)(2,1)S(1)}, u32[]{:S(2)}, u32[]{:S(2)}) collective-permute-start(bf16[256,768]{1,0:T(8,128)(2,1)S(1)} %convolution_convert_fusion.2), channel_id=1, source_target_pairs={{0,24},{4,28},{8,16},{12,20},{16,8},{20,12},{24,0},{28,4},{1,25},{... | collective-permute-start | bytes 1179656 | tf_op jit(solution)/shard_map/ppermute | solution.py:69
  42.4 3.6 %collective-permute-start.5 = (bf16[64]{0:T(256)(128)(2,1)S(1)}, bf16[64]{0:T(256)(128)(2,1)S(1)}, u32[]{:S(2)}, u32[]{:S(2)}) collective-permute-start(bf16[64]{0:T(256)(128)(2,1)S(1)} %copy-done.4), channel_id=1, source_target_pairs={{0,2},{1,3},{2,0},{3,1},{4,6},{5,7},{6,4},{7,5},{8,10},{9,11},{10,... | collective-permute-start | bytes 392 | tf_op jit(solution)/shard_map/ppermute | solution.py:77
  70.7 9.5 %collective-permute-start.18 = (bf16[128,1280]{1,0:T(8,128)(2,1)S(1)}, bf16[128,1280]{1,0:T(8,128)(2,1)S(1)}, u32[]{:S(2)}, u32[]{:S(2)}) collective-permute-start(bf16[128,1280]{1,0:T(8,128)(2,1)S(1)} %slice.187), channel_id=1, source_target_pairs={{0,1},{1,0},{2,3},{3,2},{4,5},{5,4},{6,7},{7,6},{8,9},{9,8},{10,11... | collective-permute-start | bytes 983048 | tf_op jit(solution)/shard_map/ppermute | solution.py:77
  70.8 39.5 %collective-permute-start.28 = (bf16[256,768]{1,0:T(8,128)(2,1)S(1)}, bf16[256,768]{1,0:T(8,128)(2,1)S(1)}, u32[]{:S(2)}, u32[]{:S(2)}) collective-permute-start(bf16[256,768]{1,0:T(8,128)(2,1)S(1)} %get-tuple-element.17), channel_id=1, source_target_pairs={{0,24},{4,28},{8,16},{12,20},{16,8},{20,12},{24,0},{28,4},{1,25},{... | collective-permute-start | bytes 1179656 | tf_op jit(solution)/shard_map/ppermute | solution.py:69
  72.5 37.0 %collective-permute-start.24 = (bf16[256,768]{1,0:T(8,128)(2,1)S(1)}, bf16[256,768]{1,0:T(8,128)(2,1)S(1)}, u32[]{:S(2)}, u32[]{:S(2)}) collective-permute-start(bf16[256,768]{1,0:T(8,128)(2,1)S(1)} %get-tuple-element.17), channel_id=1, source_target_pairs={{0,16},{4,20},{8,24},{12,28},{16,0},{20,4},{24,8},{28,12},{1,17},{... | collective-permute-start | bytes 1179656 | tf_op jit(solution)/shard_map/ppermute | solution.py:69
  80.1 18.3 %collective-permute-start.20 = (bf16[256,768]{1,0:T(8,128)(2,1)S(1)}, bf16[256,768]{1,0:T(8,128)(2,1)S(1)}, u32[]{:S(2)}, u32[]{:S(2)}) collective-permute-start(bf16[256,768]{1,0:T(8,128)(2,1)S(1)} %get-tuple-element.17), channel_id=1, source_target_pairs={{0,8},{4,12},{8,0},{12,4},{16,24},{20,28},{24,16},{28,20},{1,9},{5... | collective-permute-start | bytes 1179656 | tf_op jit(solution)/shard_map/ppermute | solution.py:69
  80.2 35.5 %collective-permute-start.19 = (bf16[64,1280]{1,0:T(8,128)(2,1)S(1)}, bf16[64,1280]{1,0:T(8,128)(2,1)S(1)}, u32[]{:S(2)}, u32[]{:S(2)}) collective-permute-start(bf16[64,1280]{1,0:T(8,128)(2,1)S(1)} %slice.191), channel_id=1, source_target_pairs={{0,2},{1,3},{2,0},{3,1},{4,6},{5,7},{6,4},{7,5},{8,10},{9,11},{10,... | collective-permute-start | bytes 491528 | tf_op jit(solution)/shard_map/ppermute | solution.py:77
  109.5 6.4 %collective-permute-start.21 = (bf16[128,1280]{1,0:T(8,128)(2,1)S(1)}, bf16[128,1280]{1,0:T(8,128)(2,1)S(1)}, u32[]{:S(2)}, u32[]{:S(2)}) collective-permute-start(bf16[128,1280]{1,0:T(8,128)(2,1)S(1)} %slice.186), channel_id=1, source_target_pairs={{0,1},{1,0},{2,3},{3,2},{4,5},{5,4},{6,7},{7,6},{8,9},{9,8},{10,11... | collective-permute-start | bytes 983048 | tf_op jit(solution)/shard_map/ppermute | solution.py:77
  111.1 6.5 %collective-permute-start.25 = (bf16[128,1280]{1,0:T(8,128)(2,1)S(1)}, bf16[128,1280]{1,0:T(8,128)(2,1)S(1)}, u32[]{:S(2)}, u32[]{:S(2)}) collective-permute-start(bf16[128,1280]{1,0:T(8,128)(2,1)S(1)} %slice.185), channel_id=1, source_target_pairs={{0,1},{1,0},{2,3},{3,2},{4,5},{5,4},{6,7},{7,6},{8,9},{9,8},{10,11... | collective-permute-start | bytes 983048 | tf_op jit(solution)/shard_map/ppermute | solution.py:77
  111.6 6.7 %collective-permute-start.29 = (bf16[128,1280]{1,0:T(8,128)(2,1)S(1)}, bf16[128,1280]{1,0:T(8,128)(2,1)S(1)}, u32[]{:S(2)}, u32[]{:S(2)}) collective-permute-start(bf16[128,1280]{1,0:T(8,128)(2,1)S(1)} %slice.184), channel_id=1, source_target_pairs={{0,1},{1,0},{2,3},{3,2},{4,5},{5,4},{6,7},{7,6},{8,9},{9,8},{10,11... | collective-permute-start | bytes 983048 | tf_op jit(solution)/shard_map/ppermute | solution.py:77
  114.2 28.7 %collective-permute-start.32 = (bf16[640,768]{1,0:T(8,128)(2,1)S(1)}, bf16[640,768]{1,0:T(8,128)(2,1)S(1)}, u32[]{:S(2)}, u32[]{:S(2)}) collective-permute-start(bf16[640,768]{1,0:T(8,128)(2,1)S(1)} %slice.183), channel_id=1, source_target_pairs={{0,4},{4,0},{8,12},{12,8},{16,20},{20,16},{24,28},{28,24},{1,5},{5... | collective-permute-start | bytes 2949128 | tf_op jit(solution)/shard_map/ppermute | solution.py:73
  116.0 7.1 %collective-permute-start.22 = (bf16[64,1280]{1,0:T(8,128)(2,1)S(1)}, bf16[64,1280]{1,0:T(8,128)(2,1)S(1)}, u32[]{:S(2)}, u32[]{:S(2)}) collective-permute-start(bf16[64,1280]{1,0:T(8,128)(2,1)S(1)} %slice.190), channel_id=1, source_target_pairs={{0,2},{1,3},{2,0},{3,1},{4,6},{5,7},{6,4},{7,5},{8,10},{9,11},{10,... | collective-permute-start | bytes 491528 | tf_op jit(solution)/shard_map/ppermute | solution.py:77
  117.7 8.9 %collective-permute-start.26 = (bf16[64,1280]{1,0:T(8,128)(2,1)S(1)}, bf16[64,1280]{1,0:T(8,128)(2,1)S(1)}, u32[]{:S(2)}, u32[]{:S(2)}) collective-permute-start(bf16[64,1280]{1,0:T(8,128)(2,1)S(1)} %slice.189), channel_id=1, source_target_pairs={{0,2},{1,3},{2,0},{3,1},{4,6},{5,7},{6,4},{7,5},{8,10},{9,11},{10,... | collective-permute-start | bytes 491528 | tf_op jit(solution)/shard_map/ppermute | solution.py:77
  118.4 11.0 %collective-permute-start.30 = (bf16[64,1280]{1,0:T(8,128)(2,1)S(1)}, bf16[64,1280]{1,0:T(8,128)(2,1)S(1)}, u32[]{:S(2)}, u32[]{:S(2)}) collective-permute-start(bf16[64,1280]{1,0:T(8,128)(2,1)S(1)} %slice.188), channel_id=1, source_target_pairs={{0,2},{1,3},{2,0},{3,1},{4,6},{5,7},{6,4},{7,5},{8,10},{9,11},{10,... | collective-permute-start | bytes 491528 | tf_op jit(solution)/shard_map/ppermute | solution.py:77
  123.2 7.9 %collective-permute-start.23 = (bf16[64,1280]{1,0:T(8,128)(2,1)S(1)}, bf16[64,1280]{1,0:T(8,128)(2,1)S(1)}, u32[]{:S(2)}, u32[]{:S(2)}) collective-permute-start(bf16[64,1280]{1,0:T(8,128)(2,1)S(1)} %fusion.17), channel_id=1, source_target_pairs={{0,8},{4,12},{8,0},{12,4},{16,24},{20,28},{24,16},{28,20},{1,9},{5... | collective-permute-start | bytes 491528 | tf_op jit(solution)/shard_map/ppermute | solution.py:69
  126.7 12.1 %collective-permute-start.27 = (bf16[64,1280]{1,0:T(8,128)(2,1)S(1)}, bf16[64,1280]{1,0:T(8,128)(2,1)S(1)}, u32[]{:S(2)}, u32[]{:S(2)}) collective-permute-start(bf16[64,1280]{1,0:T(8,128)(2,1)S(1)} %fusion.16), channel_id=1, source_target_pairs={{0,16},{4,20},{8,24},{12,28},{16,0},{20,4},{24,8},{28,12},{1,17},{... | collective-permute-start | bytes 491528 | tf_op jit(solution)/shard_map/ppermute | solution.py:69
  129.4 9.4 %collective-permute-start.31 = (bf16[64,1280]{1,0:T(8,128)(2,1)S(1)}, bf16[64,1280]{1,0:T(8,128)(2,1)S(1)}, u32[]{:S(2)}, u32[]{:S(2)}) collective-permute-start(bf16[64,1280]{1,0:T(8,128)(2,1)S(1)} %fusion.15), channel_id=1, source_target_pairs={{0,24},{4,28},{8,16},{12,20},{16,8},{20,12},{24,0},{28,4},{1,25},{... | collective-permute-start | bytes 491528 | tf_op jit(solution)/shard_map/ppermute | solution.py:69
  (7 other events, 96.5 us)

commit v3 on v2

--- a/solution.py
+++ b/solution.py
@@ -61,11 +61,54 @@
     )(order, pre, prob, cotangent, *parts)
 
 
+def place_kernel(place_ref, slots_ref, chunk_ref, *refs):
+    out_ref = refs[-1]
+    rows = lax.broadcasted_iota(jnp.int32, (out_ref.shape[0], slots_ref.shape[1]), 0)
+    onehot = (rows == slots_ref[...]).astype(BF16)
+    out_ref[...] = jnp.dot(onehot, chunk_ref[...], preferred_element_type=F32).astype(BF16)
+
+
+def place_call(place, slots, chunk, tok, columns, buffer):
+    cap = chunk.shape[0]
+    blocks = place.shape[0]
+    depth = chunk.shape[1] // blocks
+    in_specs = [
+        pl.BlockSpec((1, cap), lambda i, place: (0, 0)),
+        pl.BlockSpec((cap, depth), lambda i, place: (0, i)),
+    ]
+    operands = [place, slots[None, :], chunk]
+    aliases = {}
+    if buffer is not None:
+        in_specs.append(pl.BlockSpec(memory_space=pl.ANY))
+        operands.append(buffer)
+        aliases = {3: 0}
+    return pl.pallas_call(
+        place_kernel,
+        out_shape=jax.ShapeDtypeStruct((tok, columns), BF16),
+        grid_spec=pltpu.PrefetchScalarGridSpec(
+            num_scalar_prefetch=1,
+            grid=(blocks,),
+            in_specs=in_specs,
+            out_specs=pl.BlockSpec((tok, depth), lambda i, place: (0, place[i])),
+        ),
+        input_output_aliases=aliases,
+        compiler_params=pltpu.CompilerParams(vmem_limit_bytes=16 * 2**20),
+        cost_estimate=pl.CostEstimate(
+            flops=2 * tok * cap * chunk.shape[1], bytes_accessed=2 * tok * chunk.shape[1], transcendentals=0
+        ),
+    )(*operands)
+
+
 def make_shards(dp_size, etp_size):
     outer, inner = split_dp(dp_size)
+    relay = outer == 4
 
     def over_outer(value, k):
         pairs = [(i, i ^ (k * inner)) for i in range(dp_size)]
+        return lax.ppermute(value, "dp", pairs)
+
+    def outer_pairs(value, pairs):
+        pairs = [(s * inner + i, t * inner + i) for s, t in pairs for i in range(inner)]
         return lax.ppermute(value, "dp", pairs)
 
     def over_inner(value, j):
@@ -96,8 +139,18 @@
             value = value[:half] + sent.astype(F32)
         return value
 
-    far_first = sorted(range(1, outer), key=lambda k: -k)
     near_first = sorted(range(1, outer))
+    far_first = near_first[::-1]
+
+    def sum_outer(products):
+        if not relay:
+            return [over_outer(products[k].astype(BF16), k) for k in far_first]
+        far = products[3].astype(BF16)
+        carried = outer_pairs(far, [(0, 1), (3, 2)])
+        middle = outer_pairs(far, [(1, 2), (2, 1)])
+        two = over_outer((products[2] + carried.astype(F32)).astype(BF16), 2)
+        one = over_outer(after(products[1].astype(BF16), carried), 1)
+        return [middle, one, two]
 
     def shards(tokens, slots, gate_probs, w_gate, w_up, d_hidden):
         dp = lax.axis_index("dp")
@@ -107,11 +160,6 @@
         cap = slots.shape[0]
         tok = tokens.shape[0]
         span = depth * inner
-
-        weights = [jnp.concatenate([w_gate, w_up], axis=1)]
-        for j in range(1, inner):
-            weights.append(jnp.concatenate([over_inner(w_gate, j), over_inner(w_up, j)], axis=1))
-        weights = jnp.concatenate(weights, axis=0)
 
         onehot = (slots[:, None] == jnp.arange(tok, dtype=slots.dtype)[None, :]).astype(BF16)
         rows = jnp.dot(onehot, tokens, preferred_element_type=F32).astype(BF16)
@@ -125,51 +173,93 @@
                 axis=1,
             )
         got = {k: over_outer(pieces[k], k) for k in far_first}
-        x_chunks = {k: gather_etp(got[k]) for k in far_first}
-        x_chunks[0] = gather_etp(after(pieces[0], got[near_first[0]]))
+
+        weights = [jnp.concatenate([w_gate, w_up], axis=1)]
+        for j in range(1, inner):
+            sent = [over_inner(after(w, rows), j) for w in (w_gate, w_up)]
+            weights.append(jnp.concatenate(sent, axis=1))
+        weights = jnp.concatenate(weights, axis=0)
+
+        x_chunks = {}
+        last = got[far_first[0]]
+        for k in far_first:
+            x_chunks[k] = gather_etp(after(got[k], last))
+            last = got[k]
+        x_chunks[0] = gather_etp(after(pieces[0], got[1] if outer > 1 else pieces[0]))
         probs = gather_etp(after(gate_probs, x_chunks[0]))
 
-        parts = {
-            k: over_outer(jnp.dot(x_chunks[k], weights, preferred_element_type=F32).astype(BF16), k)
-            for k in far_first
+        products = {
+            k: jnp.dot(x_chunks[k], weights, preferred_element_type=F32) for k in far_first + [0]
         }
-        pre = jnp.dot(x_chunks[0], weights, preferred_element_type=F32)
+        parts = sum_outer(products)
+
+        x_other = {
+            (k, j): over_inner(x_chunks[k][:, j * depth : (j + 1) * depth], j)
+            for k in far_first + [0]
+            for j in range(1, inner)
+        }
+        probs = after(probs, *x_other.values())
         order = etp ^ jnp.array(chunk_order, jnp.int32)
-        hidden, paired = gate_call(
-            order, pre, probs[:, None], d_hidden, [parts[k] for k in near_first]
-        )
-
-        grads = {k: over_outer(paired, k) for k in far_first}
-        grads[0] = paired
-
-        dx = jnp.zeros((cap, outer * span), BF16)
-        last = paired
-        for k in [0] + near_first:
-            partial = lax.dot_general(
+        hidden, paired = gate_call(order, products[0], probs[:, None], d_hidden, parts)
+
+        keys = [0] + near_first
+        grads = {0: paired}
+        if relay:
+            grads[2] = over_outer(paired, 2)
+            grads[1] = over_outer(paired, 1)
+        else:
+            for k in near_first:
+                grads[k] = over_outer(paired, k)
+        grads_other = {}
+        partials = {}
+
+        def advance(k, last):
+            for j in range(1, inner):
+                grads_other[k, j] = over_inner(grads[k], j)
+            partials[k] = lax.dot_general(
                 after(grads[k], last), weights, (((1,), (1,)), ((), ())), preferred_element_type=F32
             )
-            last = partial
-            own = reduce_etp(partial).astype(BF16)
+            return partials[k]
+
+        last = grads[near_first[0]] if outer > 1 else paired
+        for k in keys:
+            if relay and k == 2:
+                turn = after(grads[2], last)
+                ends = outer_pairs(turn, [(2, 3), (1, 0)])
+                middle = outer_pairs(after(paired, turn), [(1, 2), (2, 1)])
+                last = grads_other[1, 1] if inner > 1 else last
+                grads[3] = middle + ends
+            last = advance(k, last)
+
+        wide = depth % 128 == 0
+        grad_tokens = None
+        dx = jnp.zeros((cap, outer * span), BF16)
+        for k in keys:
+            own = reduce_etp(partials[k]).astype(BF16)
             own = over_outer(own, k) if k else own
+            if wide:
+                place = dp ^ (k * inner + jnp.arange(inner, dtype=jnp.int32))
+                grad_tokens = place_call(place, slots, own, tok, outer * span, grad_tokens)
+            else:
+                for j in range(inner):
+                    block = own[:, j * depth : (j + 1) * depth]
+                    dx = lax.dynamic_update_slice(dx, block, (0, (a ^ k) * span + (b ^ j) * depth))
+        if not wide:
+            grad_tokens = lax.dot_general(
+                onehot, dx, (((0,), (0,)), ((), ())), preferred_element_type=F32
+            ).astype(BF16)
+
+        gate_total = up_total = jnp.zeros((), F32)
+        for k in keys:
             for j in range(inner):
-                block = own[:, j * depth : (j + 1) * depth]
-                dx = lax.dynamic_update_slice(dx, block, (0, (a ^ k) * span + (b ^ j) * depth))
-        grad_tokens = lax.dot_general(
-            onehot, dx, (((0,), (0,)), ((), ())), preferred_element_type=F32
-        ).astype(BF16)
-
-        keys = [0] + near_first
-        summed = lax.dot_general(
-            jnp.concatenate([x_chunks[k] for k in keys], axis=0),
-            after(jnp.concatenate([grads[k] for k in keys], axis=0), last),
-            (((0,), (0,)), ((), ())),
-            preferred_element_type=F32,
-        )
-        total = summed[:depth]
-        for j in range(1, inner):
-            part = summed[j * depth : (j + 1) * depth]
-            total = total + over_inner(part.astype(BF16), j).astype(F32)
-        return (hidden, grad_tokens, total[:, :width], total[:, width:])
+                x_part = x_other[k, j] if j else x_chunks[k][:, :depth]
+                grad_part = grads_other[k, j] if j else grads[k]
+                product = lax.dot_general(
+                    x_part, grad_part, (((0,), (0,)), ((), ())), preferred_element_type=F32
+                )
+                gate_total = gate_total + product[:, :width]
+                up_total = up_total + product[:, width:]
+        return (hidden, grad_tokens, gate_total, up_total)
 
     return shards
 

time: 146 us -> 159 us (1.089)
  starting transfers between devices: 39.6 us -> 50.8 us
  Pallas kernels: 1.65 us -> 9.89 us
  waiting for transfers between devices: 83.1 us -> 79.8 us
  matrix products: 15.4 us -> 13 us
  other arithmetic: 1.13 us -> 2.93 us
  local copies, waits for them, and re-layouts: 2.38 us -> 0.75 us
    ppermute x12 -> x10, waiting for transfers between devices: 65.7 us -> 35.6 us  [over_outer(): return lax.ppermute(value, 'dp', pairs)]
    ppermute x3 -> x10, waiting for transfers between devices: 0.01 us -> 30 us  [over_inner(): return lax.ppermute(value, 'dp', pairs)]
    ppermute x3 -> x10, starting transfers between devices: 4.66 us -> 13 us  [over_inner(): return lax.ppermute(value, 'dp', pairs)]
    pallas_call x0 -> x4, Pallas kernels: none -> 8.24 us  [place_call(): pl.pallas_call(place_kernel, out_shape=jax.ShapeDtypeStruct((tok, columns...]
    ppermute x0 -> x4, starting transfers between devices: none -> 6.48 us  [outer_pairs(): return lax.ppermute(value, 'dp', pairs)]
    ppermute x18, waiting for transfers between devices: 17.4 us -> 11.6 us  [over_etp(): return lax.ppermute(value, 'etp', pairs)]
    ppermute x0 -> x4, waiting for transfers between devices: none -> 2.57 us  [outer_pairs(): return lax.ppermute(value, 'dp', pairs)]
    dot_general x10 -> x16, matrix products: 11.9 us -> 9.31 us  [the longest x8 3.76 us: shards(): lax.dot_general(x_part, grad_part, (((0,), (0,)), ((), ())), preferred_el...]
  transfers between devices with their start and end apart: 33 -> 42, of which waited for: 15 -> 21; matrix products, arithmetic and copies ran while one was open for 11% -> 8% of each run, Pallas kernels for 0% -> 4%
where the time goes in v3:
time: 159 us; the launch traced here: 158 us
  waiting for transfers between devices  79.8 us (50%)
  starting transfers between devices  50.8 us (32%)
  matrix products  13 us (8%)
  Pallas kernels  9.89 us (6%)
  other arithmetic  2.93 us (2%)
    ppermute x10, waiting for transfers between devices, over_outer(): return lax.ppermute(value, 'dp', pairs)  35.6 us
    ppermute x10, waiting for transfers between devices, over_inner(): return lax.ppermute(value, 'dp', pairs)  30 us
    ppermute x10, starting transfers between devices, over_outer(): return lax.ppermute(value, 'dp', pairs)  20.2 us
    ppermute x10, starting transfers between devices, over_inner(): return lax.ppermute(value, 'dp', pairs)  13 us
    ppermute x18, waiting for transfers between devices, over_etp(): return lax.ppermute(value, 'etp', pairs)  11.6 us
    ppermute x18, starting transfers between devices, over_etp(): return lax.ppermute(value, 'etp', pairs)  11.2 us
    pallas_call x4, Pallas kernels, place_call(): pl.pallas_call(place_kernel, out_shape=jax.ShapeDtypeStruct((tok, columns...  8.24 us
    ppermute x4, starting transfers between devices, outer_pairs(): return lax.ppermute(value, 'dp', pairs)  6.48 us
  transfers between devices with their start and end apart: 42, of which 21 were waited for; matrix products, arithmetic and copies ran while one was open for 8% of the time, Pallas kernels for 4%

profile of v3, /device:TPU:0, one launch (start us, length us, event | category | flops | bytes accessed | tf_op | source)
XLA Modules:
  0.0 158.5 jit_solution(13329046957824665083)
XLA Ops:
  0.7 3.7 %convolution_convert_fusion = bf16[64,5120]{1,0:T(8,128)(2,1)S(1)} fusion(bf16[512,5120]{1,0:T(8,128)(2,1)} %param.7, s32[64]{0:T(128)} %param.8), kind=kOutput, calls=%fused_computation | convolution fusion | flops 335904768 | bytes 5898496 | tf_op jit(solution)/shard_map/dot_general | solution.py:165
  4.3 3.0 %collective-permute-start.3 = (bf16[640,384]{1,0:T(8,128)(2,1)S(1)}, bf16[640,384]{1,0:T(8,128)(2,1)S(1)}, u32[]{:S(2)}, u32[]{:S(2)}) collective-permute-start(bf16[640,384]{1,0:T(8,128)(2,1)S(1)} %copy-done.3), channel_id=1, source_target_pairs={{0,4},{4,0},{8,12},{12,8},{16,20},{20,16},{24,28},{28,24},{1,5},{5... | collective-permute-start | bytes 1474568 | tf_op jit(solution)/shard_map/ppermute | solution.py:116
  7.5 2.1 %collective-permute-start = (bf16[64,1280]{1,0:T(8,128)(2,1)S(1)}, bf16[64,1280]{1,0:T(8,128)(2,1)S(1)}, u32[]{:S(2)}, u32[]{:S(2)}) collective-permute-start(bf16[64,1280]{1,0:T(8,128)(2,1)S(1)} %pad_maximum_fusion.5), channel_id=1, source_target_pairs={{0,8},{4,12},{8,0},{12,4},{16,24},{20,28},{24,16},{28,20},{1,9},{5... | collective-permute-start | bytes 491528 | tf_op jit(solution)/shard_map/ppermute | solution.py:108
  9.6 2.5 %collective-permute-start.7 = (bf16[64,1280]{1,0:T(8,128)(2,1)S(1)}, bf16[64,1280]{1,0:T(8,128)(2,1)S(1)}, u32[]{:S(2)}, u32[]{:S(2)}) collective-permute-start(bf16[64,1280]{1,0:T(8,128)(2,1)S(1)} %pad_maximum_fusion.6), channel_id=1, source_target_pairs={{0,24},{4,28},{8,16},{12,20},{16,8},{20,12},{24,0},{28,4},{1,25},{... | collective-permute-start | bytes 491528 | tf_op jit(solution)/shard_map/ppermute | solution.py:108
  15.3 5.4 %collective-permute-done.7 = bf16[64,1280]{1,0:T(8,128)(2,1)S(1)} collective-permute-done((bf16[64,1280]{1,0:T(8,128)(2,1)S(1)}, bf16[64,1280]{1,0:T(8,128)(2,1)S(1)}, u32[]{:S(2)}, u32[]{:S(2)}) %collective-permute-start.7) | collective-permute-done | bytes 163872 | tf_op jit(solution)/shard_map/ppermute | solution.py:108
  22.3 3.9 %collective-permute-done.11 = bf16[64,1280]{1,0:T(8,128)(2,1)S(1)} collective-permute-done((bf16[64,1280]{1,0:T(8,128)(2,1)S(1)}, bf16[64,1280]{1,0:T(8,128)(2,1)S(1)}, u32[]{:S(2)}, u32[]{:S(2)}) %collective-permute-start.11) | collective-permute-done | bytes 163872 | tf_op jit(solution)/shard_map/ppermute | solution.py:108
  28.5 4.1 %collective-permute-done.12 = bf16[64,1280]{1,0:T(8,128)(2,1)S(1)} collective-permute-done((bf16[64,1280]{1,0:T(8,128)(2,1)S(1)}, bf16[64,1280]{1,0:T(8,128)(2,1)S(1)}, u32[]{:S(2)}, u32[]{:S(2)}) %collective-permute-start.12) | collective-permute-done | bytes 163872 | tf_op jit(solution)/shard_map/ppermute | solution.py:120
  37.2 3.7 %collective-permute-start.20 = (bf16[256,768]{1,0:T(8,128)(2,1)S(1)}, bf16[256,768]{1,0:T(8,128)(2,1)S(1)}, u32[]{:S(2)}, u32[]{:S(2)}) collective-permute-start(bf16[256,768]{1,0:T(8,128)(2,1)S(1)} %convolution_convert_fusion.2), channel_id=1, source_target_pairs={{0,8},{4,12},{24,16},{28,20},{1,9},{5,13},{25,17},{29,21},{2,10},{... | collective-permute-start | bytes 1179656 | tf_op jit(solution)/shard_map/ppermute | solution.py:112
  47.0 2.6 %collective-permute-done.20 = bf16[256,768]{1,0:T(8,128)(2,1)S(1)} collective-permute-done((bf16[256,768]{1,0:T(8,128)(2,1)S(1)}, bf16[256,768]{1,0:T(8,128)(2,1)S(1)}, u32[]{:S(2)}, u32[]{:S(2)}) %collective-permute-start.20) | collective-permute-done | bytes 393248 | tf_op jit(solution)/shard_map/ppermute | solution.py:112
  52.2 1.7 %collective-permute-done.18 = bf16[256,640]{1,0:T(8,128)(2,1)S(1)} collective-permute-done((bf16[256,640]{1,0:T(8,128)(2,1)S(1)}, bf16[256,640]{1,0:T(8,128)(2,1)S(1)}, u32[]{:S(2)}, u32[]{:S(2)}) %collective-permute-start.18) | collective-permute-done | bytes 327712 | tf_op jit(solution)/shard_map/ppermute | solution.py:116
  53.9 2.0 %collective-permute-start.22 = (bf16[256,768]{1,0:T(8,128)(2,1)S(1)}, bf16[256,768]{1,0:T(8,128)(2,1)S(1)}, u32[]{:S(2)}, u32[]{:S(2)}) collective-permute-start(bf16[256,768]{1,0:T(8,128)(2,1)S(1)} %fusion), channel_id=1, source_target_pairs={{0,16},{4,20},{8,24},{12,28},{16,0},{20,4},{24,8},{28,12},{1,17},{... | collective-permute-start | bytes 1179656 | tf_op jit(solution)/shard_map/ppermute | solution.py:108
  56.0 5.0 %collective-permute-done.10 = bf16[256,640]{1,0:T(8,128)(2,1)S(1)} collective-permute-done((bf16[256,640]{1,0:T(8,128)(2,1)S(1)}, bf16[256,640]{1,0:T(8,128)(2,1)S(1)}, u32[]{:S(2)}, u32[]{:S(2)}) %collective-permute-start.10) | collective-permute-done | bytes 327712 | tf_op jit(solution)/shard_map/ppermute | solution.py:116
  63.0 4.9 %collective-permute-done.14 = bf16[256,640]{1,0:T(8,128)(2,1)S(1)} collective-permute-done((bf16[256,640]{1,0:T(8,128)(2,1)S(1)}, bf16[256,640]{1,0:T(8,128)(2,1)S(1)}, u32[]{:S(2)}, u32[]{:S(2)}) %collective-permute-start.14) | collective-permute-done | bytes 327712 | tf_op jit(solution)/shard_map/ppermute | solution.py:116
  68.0 5.6 %collective-permute-done.17 = bf16[256,640]{1,0:T(8,128)(2,1)S(1)} collective-permute-done((bf16[256,640]{1,0:T(8,128)(2,1)S(1)}, bf16[256,640]{1,0:T(8,128)(2,1)S(1)}, u32[]{:S(2)}, u32[]{:S(2)}) %collective-permute-start.17) | collective-permute-done | bytes 327712 | tf_op jit(solution)/shard_map/ppermute | solution.py:116
  73.7 2.0 %collective-permute-done.21.refs_1_ = bf16[256,768]{1,0:T(8,128)(2,1)S(1)} collective-permute-done((bf16[256,768]{1,0:T(8,128)(2,1)S(1)}, bf16[256,768]{1,0:T(8,128)(2,1)S(1)}, u32[]{:S(2)}, u32[]{:S(2)}) %collective-permute-start.21) | collective-permute-done | bytes 393248 | tf_op jit(solution)/shard_map/ppermute | solution.py:108
  78.8 2.9 %collective-permute-start.23 = (bf16[256,768]{1,0:T(8,128)(2,1)S(1)}, bf16[256,768]{1,0:T(8,128)(2,1)S(1)}, u32[]{:S(2)}, u32[]{:S(2)}) collective-permute-start(bf16[256,768]{1,0:T(8,128)(2,1)S(1)} %get-tuple-element.35), channel_id=1, source_target_pairs={{0,16},{4,20},{8,24},{12,28},{16,0},{20,4},{24,8},{28,12},{1,17},{... | collective-permute-start | bytes 1179656 | tf_op jit(solution)/shard_map/ppermute | solution.py:108
  82.2 9.7 %collective-permute-done.24 = bf16[256,768]{1,0:T(8,128)(2,1)S(1)} collective-permute-done((bf16[256,768]{1,0:T(8,128)(2,1)S(1)}, bf16[256,768]{1,0:T(8,128)(2,1)S(1)}, u32[]{:S(2)}, u32[]{:S(2)}) %collective-permute-start.24) | collective-permute-done | bytes 393248 | tf_op jit(solution)/shard_map/ppermute | solution.py:108
  93.4 3.4 %collective-permute-done.23 = bf16[256,768]{1,0:T(8,128)(2,1)S(1)} collective-permute-done((bf16[256,768]{1,0:T(8,128)(2,1)S(1)}, bf16[256,768]{1,0:T(8,128)(2,1)S(1)}, u32[]{:S(2)}, u32[]{:S(2)}) %collective-permute-start.23) | collective-permute-done | bytes 393248 | tf_op jit(solution)/shard_map/ppermute | solution.py:108
  101.5 1.7 %collective-permute-start.40 = (bf16[256,768]{1,0:T(8,128)(2,1)S(1)}, bf16[256,768]{1,0:T(8,128)(2,1)S(1)}, u32[]{:S(2)}, u32[]{:S(2)}) collective-permute-start(bf16[256,768]{1,0:T(8,128)(2,1)S(1)} %collective-permute-done.23), channel_id=1, source_target_pairs={{0,4},{4,0},{8,12},{12,8},{16,20},{20,16},{24,28},{28,24},{1,5},{5... | collective-permute-start | bytes 1179656 | tf_op jit(solution)/shard_map/ppermute | solution.py:116
  103.9 8.6 %collective-permute-done.27 = bf16[256,768]{1,0:T(8,128)(2,1)S(1)} collective-permute-done((bf16[256,768]{1,0:T(8,128)(2,1)S(1)}, bf16[256,768]{1,0:T(8,128)(2,1)S(1)}, u32[]{:S(2)}, u32[]{:S(2)}) %collective-permute-start.27) | collective-permute-done | bytes 393248 | tf_op jit(solution)/shard_map/ppermute | solution.py:116
  116.8 4.1 %collective-permute-done.40 = bf16[256,768]{1,0:T(8,128)(2,1)S(1)} collective-permute-done((bf16[256,768]{1,0:T(8,128)(2,1)S(1)}, bf16[256,768]{1,0:T(8,128)(2,1)S(1)}, u32[]{:S(2)}, u32[]{:S(2)}) %collective-permute-start.40) | collective-permute-done | bytes 393248 | tf_op jit(solution)/shard_map/ppermute | solution.py:116
  121.5 5.3 %collective-permute-start.36 = (bf16[64,1280]{1,0:T(8,128)(2,1)S(1)}, bf16[64,1280]{1,0:T(8,128)(2,1)S(1)}, u32[]{:S(2)}, u32[]{:S(2)}) collective-permute-start(bf16[64,1280]{1,0:T(8,128)(2,1)S(1)} %fusion.10), channel_id=1, source_target_pairs={{0,8},{4,12},{8,0},{12,4},{16,24},{20,28},{24,16},{28,20},{1,9},{5... | collective-permute-start | bytes 491528 | tf_op jit(solution)/shard_map/ppermute | solution.py:108
  126.8 2.1 %shard_map.103.refs_0_ = bf16[512,5120]{1,0:T(8,128)(2,1)} custom-call(s32[2]{0:T(128)S(1)} %iota_xor_fusion.place_ref, s32[1,64]{1,0:T(1,128)S(1)} %bitcast.30, bf16[64,1280]{1,0:T(8,128)(2,1)S(1)} %fusion.9.chunk_ref), custom_call_target="tpu_custom_call" | custom-call | flops 83886080 | bytes 1310720 | tf_op jit(solution)/shard_map/pallas_call | solution.py:85
  128.9 2.8 %collective-permute-done.36.chunk_ref = bf16[64,1280]{1,0:T(8,128)(2,1)S(1)} collective-permute-done((bf16[64,1280]{1,0:T(8,128)(2,1)S(1)}, bf16[64,1280]{1,0:T(8,128)(2,1)S(1)}, u32[]{:S(2)}, u32[]{:S(2)}) %collective-permute-start.36) | collective-permute-done | bytes 163872 | tf_op jit(solution)/shard_map/ppermute | solution.py:108
  131.7 2.1 %shard_map.104.refs_0_ = bf16[512,5120]{1,0:T(8,128)(2,1)} custom-call(s32[2]{0:T(128)S(1)} %add_xor_fusion.place_ref, s32[1,64]{1,0:T(1,128)S(1)} %bitcast.31, bf16[64,1280]{1,0:T(8,128)(2,1)S(1)} %collective-permute-done.36.chunk_ref, bf16[512,5120]{1,0:T(8,128)(2,1)} %shard_map.103.refs_0_), custom_call_target="tpu_custom_call", output_to_operand_aliasing={{}: (3, {})} | custom-call | flops 83886080 | bytes 1310720 | tf_op jit(solution)/shard_map/pallas_call | solution.py:85
  136.6 4.4 %collective-permute-done.32 = bf16[64,1280]{1,0:T(8,128)(2,1)S(1)} collective-permute-done((bf16[64,1280]{1,0:T(8,128)(2,1)S(1)}, bf16[64,1280]{1,0:T(8,128)(2,1)S(1)}, u32[]{:S(2)}, u32[]{:S(2)}) %collective-permute-start.32) | collective-permute-done | bytes 163872 | tf_op jit(solution)/shard_map/ppermute | solution.py:120
  141.0 2.0 %collective-permute-start.33 = (bf16[64,1280]{1,0:T(8,128)(2,1)S(1)}, bf16[64,1280]{1,0:T(8,128)(2,1)S(1)}, u32[]{:S(2)}, u32[]{:S(2)}) collective-permute-start(bf16[64,1280]{1,0:T(8,128)(2,1)S(1)} %fusion.11), channel_id=1, source_target_pairs={{0,16},{4,20},{8,24},{12,28},{16,0},{20,4},{24,8},{28,12},{1,17},{... | collective-permute-start | bytes 491528 | tf_op jit(solution)/shard_map/ppermute | solution.py:108
  143.5 1.8 %collective-permute-start.30 = (bf16[64,1280]{1,0:T(8,128)(2,1)S(1)}, bf16[64,1280]{1,0:T(8,128)(2,1)S(1)}, u32[]{:S(2)}, u32[]{:S(2)}) collective-permute-start(bf16[64,1280]{1,0:T(8,128)(2,1)S(1)} %fusion.12), channel_id=1, source_target_pairs={{0,24},{4,28},{8,16},{12,20},{16,8},{20,12},{24,0},{28,4},{1,25},{... | collective-permute-start | bytes 491528 | tf_op jit(solution)/shard_map/ppermute | solution.py:108
  145.3 1.9 %slice_add_fusion = (f32[640,384]{1,0:T(8,128)}, f32[640,384]{1,0:T(8,128)}) fusion(f32[640,768]{1,0:T(8,128)S(1)} %fusion.22, f32[640,768]{1,0:T(8,128)S(1)} %fusion.1, f32[640,768]{1,0:T(8,128)S(1)} %fusion.21, f32[640,768]{1,0:T(8,128)S(1)} %fusion.3, f32[640,768]{1,0:T(8,128)S(1)} %fusion.20, f32[640,768]{1,0:T(8,128)S(1)} %fusion.5, ...), kind=kLoop, calls=%fused_computation.6 | loop fusion | flops 3440640 | bytes 17694720 | tf_op jit(solution)/shard_map/add | solution.py:261
  147.2 7.1 %collective-permute-done.33.chunk_ref = bf16[64,1280]{1,0:T(8,128)(2,1)S(1)} collective-permute-done((bf16[64,1280]{1,0:T(8,128)(2,1)S(1)}, bf16[64,1280]{1,0:T(8,128)(2,1)S(1)}, u32[]{:S(2)}, u32[]{:S(2)}) %collective-permute-start.33) | collective-permute-done | bytes 163872 | tf_op jit(solution)/shard_map/ppermute | solution.py:108
  154.4 2.1 %shard_map.105.refs_0_ = bf16[512,5120]{1,0:T(8,128)(2,1)} custom-call(s32[2]{0:T(128)S(1)} %add_xor_fusion.1.place_ref, s32[1,64]{1,0:T(1,128)S(1)} %bitcast.32, bf16[64,1280]{1,0:T(8,128)(2,1)S(1)} %collective-permute-done.33.chunk_ref, bf16[512,5120]{1,0:T(8,128)(2,1)} %shard_map.104.refs_0_), custom_call_target="tpu_custom_call", output_to_operand_aliasing={{}: (3, {})} | custom-call | flops 83886080 | bytes 1310720 | tf_op jit(solution)/shard_map/pallas_call | solution.py:85
  156.4 2.1 %shard_map.106 = bf16[512,5120]{1,0:T(8,128)(2,1)} custom-call(s32[2]{0:T(128)S(1)} %add_xor_fusion.2.place_ref, s32[1,64]{1,0:T(1,128)S(1)} %bitcast.33, bf16[64,1280]{1,0:T(8,128)(2,1)S(1)} %collective-permute-done.30.chunk_ref, bf16[512,5120]{1,0:T(8,128)(2,1)} %shard_map.105.refs_0_), custom_call_target="tpu_custom_call", output_to_operand_aliasing={{}: (3, {})} | custom-call | flops 83886080 | bytes 1310720 | tf_op jit(solution)/shard_map/pallas_call | solution.py:85
  (138 shorter events, 41.0 us)
Async XLA Ops:
  4.3 30.1 %collective-permute-start.3 = (bf16[640,384]{1,0:T(8,128)(2,1)S(1)}, bf16[640,384]{1,0:T(8,128)(2,1)S(1)}, u32[]{:S(2)}, u32[]{:S(2)}) collective-permute-start(bf16[640,384]{1,0:T(8,128)(2,1)S(1)} %copy-done.3), channel_id=1, source_target_pairs={{0,4},{4,0},{8,12},{12,8},{16,20},{20,16},{24,28},{28,24},{1,5},{5... | collective-permute-start | bytes 1474568 | tf_op jit(solution)/shard_map/ppermute | solution.py:116
  7.3 27.6 %collective-permute-start.4 = (bf16[640,384]{1,0:T(8,128)(2,1)S(1)}, bf16[640,384]{1,0:T(8,128)(2,1)S(1)}, u32[]{:S(2)}, u32[]{:S(2)}) collective-permute-start(bf16[640,384]{1,0:T(8,128)(2,1)S(1)} %copy-done.2), channel_id=1, source_target_pairs={{0,4},{4,0},{8,12},{12,8},{16,20},{20,16},{24,28},{28,24},{1,5},{5... | collective-permute-start | bytes 1474568 | tf_op jit(solution)/shard_map/ppermute | solution.py:116
  9.6 11.1 %collective-permute-start.7 = (bf16[64,1280]{1,0:T(8,128)(2,1)S(1)}, bf16[64,1280]{1,0:T(8,128)(2,1)S(1)}, u32[]{:S(2)}, u32[]{:S(2)}) collective-permute-start(bf16[64,1280]{1,0:T(8,128)(2,1)S(1)} %pad_maximum_fusion.6), channel_id=1, source_target_pairs={{0,24},{4,28},{8,16},{12,20},{16,8},{20,12},{24,0},{28,4},{1,25},{... | collective-permute-start | bytes 491528 | tf_op jit(solution)/shard_map/ppermute | solution.py:108
  12.2 14.0 %collective-permute-start.11 = (bf16[64,1280]{1,0:T(8,128)(2,1)S(1)}, bf16[64,1280]{1,0:T(8,128)(2,1)S(1)}, u32[]{:S(2)}, u32[]{:S(2)}) collective-permute-start(bf16[64,1280]{1,0:T(8,128)(2,1)S(1)} %pad_maximum_fusion.7), channel_id=1, source_target_pairs={{0,16},{4,20},{8,24},{12,28},{16,0},{20,4},{24,8},{28,12},{1,17},{... | collective-permute-start | bytes 491528 | tf_op jit(solution)/shard_map/ppermute | solution.py:108
  13.8 13.9 %collective-permute-start.1 = (bf16[64,1280]{1,0:T(8,128)(2,1)S(1)}, bf16[64,1280]{1,0:T(8,128)(2,1)S(1)}, u32[]{:S(2)}, u32[]{:S(2)}) collective-permute-start(bf16[64,1280]{1,0:T(8,128)(2,1)S(1)} %pad_maximum_fusion.4), channel_id=1, source_target_pairs={{0,2},{1,3},{2,0},{3,1},{4,6},{5,7},{6,4},{7,5},{8,10},{9,11},{10,... | collective-permute-start | bytes 491528 | tf_op jit(solution)/shard_map/ppermute | solution.py:120
  20.7 7.6 %collective-permute-start.8 = (bf16[64,1280]{1,0:T(8,128)(2,1)S(1)}, bf16[64,1280]{1,0:T(8,128)(2,1)S(1)}, u32[]{:S(2)}, u32[]{:S(2)}) collective-permute-start(bf16[64,1280]{1,0:T(8,128)(2,1)S(1)} %collective-permute-done.7), channel_id=1, source_target_pairs={{0,2},{1,3},{2,0},{3,1},{4,6},{5,7},{6,4},{7,5},{8,10},{9,11},{10,... | collective-permute-start | bytes 491528 | tf_op jit(solution)/shard_map/ppermute | solution.py:120
  28.4 13.2 %collective-permute-start.2 = (bf16[128,1280]{1,0:T(8,128)(2,1)S(1)}, bf16[128,1280]{1,0:T(8,128)(2,1)S(1)}, u32[]{:S(2)}, u32[]{:S(2)}) collective-permute-start(bf16[128,1280]{1,0:T(8,128)(2,1)S(1)} %pad_maximum_fusion), channel_id=1, source_target_pairs={{0,1},{1,0},{2,3},{3,2},{4,5},{5,4},{6,7},{7,6},{8,9},{9,8},{10,11... | collective-permute-start | bytes 983048 | tf_op jit(solution)/shard_map/ppermute | solution.py:120
  34.3 10.4 %collective-permute-start.13 = (bf16[128,1280]{1,0:T(8,128)(2,1)S(1)}, bf16[128,1280]{1,0:T(8,128)(2,1)S(1)}, u32[]{:S(2)}, u32[]{:S(2)}) collective-permute-start(bf16[128,1280]{1,0:T(8,128)(2,1)S(1)} %pad_maximum_fusion.2), channel_id=1, source_target_pairs={{0,1},{1,0},{2,3},{3,2},{4,5},{5,4},{6,7},{7,6},{8,9},{9,8},{10,11... | collective-permute-start | bytes 983048 | tf_op jit(solution)/shard_map/ppermute | solution.py:120
  37.2 12.3 %collective-permute-start.20 = (bf16[256,768]{1,0:T(8,128)(2,1)S(1)}, bf16[256,768]{1,0:T(8,128)(2,1)S(1)}, u32[]{:S(2)}, u32[]{:S(2)}) collective-permute-start(bf16[256,768]{1,0:T(8,128)(2,1)S(1)} %convolution_convert_fusion.2), channel_id=1, source_target_pairs={{0,8},{4,12},{24,16},{28,20},{1,9},{5,13},{25,17},{29,21},{2,10},{... | collective-permute-start | bytes 1179656 | tf_op jit(solution)/shard_map/ppermute | solution.py:112
  40.9 32.8 %collective-permute-start.19 = (bf16[256,768]{1,0:T(8,128)(2,1)S(1)}, bf16[256,768]{1,0:T(8,128)(2,1)S(1)}, u32[]{:S(2)}, u32[]{:S(2)}) collective-permute-start(bf16[256,768]{1,0:T(8,128)(2,1)S(1)} %convolution_convert_fusion.2), channel_id=1, source_target_pairs={{8,16},{12,20},{16,8},{20,12},{9,17},{13,21},{17,9},{21,13},{10,18... | collective-permute-start | bytes 1179656 | tf_op jit(solution)/shard_map/ppermute | solution.py:112
  43.3 10.6 %collective-permute-start.18 = (bf16[256,640]{1,0:T(8,128)(2,1)S(1)}, bf16[256,640]{1,0:T(8,128)(2,1)S(1)}, u32[]{:S(2)}, u32[]{:S(2)}) collective-permute-start(bf16[256,640]{1,0:T(8,128)(2,1)S(1)} %slice.171), channel_id=1, source_target_pairs={{0,4},{4,0},{8,12},{12,8},{16,20},{20,16},{24,28},{28,24},{1,5},{5... | collective-permute-start | bytes 983048 | tf_op jit(solution)/shard_map/ppermute | solution.py:116
  44.8 16.2 %collective-permute-start.10 = (bf16[256,640]{1,0:T(8,128)(2,1)S(1)}, bf16[256,640]{1,0:T(8,128)(2,1)S(1)}, u32[]{:S(2)}, u32[]{:S(2)}) collective-permute-start(bf16[256,640]{1,0:T(8,128)(2,1)S(1)} %slice.168), channel_id=1, source_target_pairs={{0,4},{4,0},{8,12},{12,8},{16,20},{20,16},{24,28},{28,24},{1,5},{5... | collective-permute-start | bytes 983048 | tf_op jit(solution)/shard_map/ppermute | solution.py:116
  45.4 22.6 %collective-permute-start.14 = (bf16[256,640]{1,0:T(8,128)(2,1)S(1)}, bf16[256,640]{1,0:T(8,128)(2,1)S(1)}, u32[]{:S(2)}, u32[]{:S(2)}) collective-permute-start(bf16[256,640]{1,0:T(8,128)(2,1)S(1)} %slice.169), channel_id=1, source_target_pairs={{0,4},{4,0},{8,12},{12,8},{16,20},{20,16},{24,28},{28,24},{1,5},{5... | collective-permute-start | bytes 983048 | tf_op jit(solution)/shard_map/ppermute | solution.py:116
  50.7 22.9 %collective-permute-start.17 = (bf16[256,640]{1,0:T(8,128)(2,1)S(1)}, bf16[256,640]{1,0:T(8,128)(2,1)S(1)}, u32[]{:S(2)}, u32[]{:S(2)}) collective-permute-start(bf16[256,640]{1,0:T(8,128)(2,1)S(1)} %slice.170), channel_id=1, source_target_pairs={{0,4},{4,0},{8,12},{12,8},{16,20},{20,16},{24,28},{28,24},{1,5},{5... | collective-permute-start | bytes 983048 | tf_op jit(solution)/shard_map/ppermute | solution.py:116
  53.9 19.8 %collective-permute-start.22 = (bf16[256,768]{1,0:T(8,128)(2,1)S(1)}, bf16[256,768]{1,0:T(8,128)(2,1)S(1)}, u32[]{:S(2)}, u32[]{:S(2)}) collective-permute-start(bf16[256,768]{1,0:T(8,128)(2,1)S(1)} %fusion), channel_id=1, source_target_pairs={{0,16},{4,20},{8,24},{12,28},{16,0},{20,4},{24,8},{28,12},{1,17},{... | collective-permute-start | bytes 1179656 | tf_op jit(solution)/shard_map/ppermute | solution.py:108
  60.9 14.7 %collective-permute-start.21 = (bf16[256,768]{1,0:T(8,128)(2,1)S(1)}, bf16[256,768]{1,0:T(8,128)(2,1)S(1)}, u32[]{:S(2)}, u32[]{:S(2)}) collective-permute-start(bf16[256,768]{1,0:T(8,128)(2,1)S(1)} %convolution_convert_fusion.1), channel_id=1, source_target_pairs={{0,8},{4,12},{8,0},{12,4},{16,24},{20,28},{24,16},{28,20},{1,9},{5... | collective-permute-start | bytes 1179656 | tf_op jit(solution)/shard_map/ppermute | solution.py:108
  77.3 14.6 %collective-permute-start.24 = (bf16[256,768]{1,0:T(8,128)(2,1)S(1)}, bf16[256,768]{1,0:T(8,128)(2,1)S(1)}, u32[]{:S(2)}, u32[]{:S(2)}) collective-permute-start(bf16[256,768]{1,0:T(8,128)(2,1)S(1)} %get-tuple-element.35), channel_id=1, source_target_pairs={{0,8},{4,12},{8,0},{12,4},{16,24},{20,28},{24,16},{28,20},{1,9},{5... | collective-permute-start | bytes 1179656 | tf_op jit(solution)/shard_map/ppermute | solution.py:108
  77.3 23.2 %collective-permute-start.39 = (bf16[256,768]{1,0:T(8,128)(2,1)S(1)}, bf16[256,768]{1,0:T(8,128)(2,1)S(1)}, u32[]{:S(2)}, u32[]{:S(2)}) collective-permute-start(bf16[256,768]{1,0:T(8,128)(2,1)S(1)} %get-tuple-element.35), channel_id=1, source_target_pairs={{0,4},{4,0},{8,12},{12,8},{16,20},{20,16},{24,28},{28,24},{1,5},{5... | collective-permute-start | bytes 1179656 | tf_op jit(solution)/shard_map/ppermute | solution.py:116
  78.8 18.0 %collective-permute-start.23 = (bf16[256,768]{1,0:T(8,128)(2,1)S(1)}, bf16[256,768]{1,0:T(8,128)(2,1)S(1)}, u32[]{:S(2)}, u32[]{:S(2)}) collective-permute-start(bf16[256,768]{1,0:T(8,128)(2,1)S(1)} %get-tuple-element.35), channel_id=1, source_target_pairs={{0,16},{4,20},{8,24},{12,28},{16,0},{20,4},{24,8},{28,12},{1,17},{... | collective-permute-start | bytes 1179656 | tf_op jit(solution)/shard_map/ppermute | solution.py:108
  96.8 17.0 %collective-permute-start.26 = (bf16[256,768]{1,0:T(8,128)(2,1)S(1)}, bf16[256,768]{1,0:T(8,128)(2,1)S(1)}, u32[]{:S(2)}, u32[]{:S(2)}) collective-permute-start(bf16[256,768]{1,0:T(8,128)(2,1)S(1)} %collective-permute-done.23), channel_id=1, source_target_pairs={{16,24},{20,28},{8,0},{12,4},{17,25},{21,29},{9,1},{13,5},{18,26},... | collective-permute-start | bytes 1179656 | tf_op jit(solution)/shard_map/ppermute | solution.py:112
  98.7 15.1 %collective-permute-start.25 = (bf16[256,768]{1,0:T(8,128)(2,1)S(1)}, bf16[256,768]{1,0:T(8,128)(2,1)S(1)}, u32[]{:S(2)}, u32[]{:S(2)}) collective-permute-start(bf16[256,768]{1,0:T(8,128)(2,1)S(1)} %get-tuple-element.35), channel_id=1, source_target_pairs={{8,16},{12,20},{16,8},{20,12},{9,17},{13,21},{17,9},{21,13},{10,18... | collective-permute-start | bytes 1179656 | tf_op jit(solution)/shard_map/ppermute | solution.py:112
  100.5 12.0 %collective-permute-start.27 = (bf16[256,768]{1,0:T(8,128)(2,1)S(1)}, bf16[256,768]{1,0:T(8,128)(2,1)S(1)}, u32[]{:S(2)}, u32[]{:S(2)}) collective-permute-start(bf16[256,768]{1,0:T(8,128)(2,1)S(1)} %collective-permute-done.24), channel_id=1, source_target_pairs={{0,4},{4,0},{8,12},{12,8},{16,20},{20,16},{24,28},{28,24},{1,5},{5... | collective-permute-start | bytes 1179656 | tf_op jit(solution)/shard_map/ppermute | solution.py:116
  101.5 19.5 %collective-permute-start.40 = (bf16[256,768]{1,0:T(8,128)(2,1)S(1)}, bf16[256,768]{1,0:T(8,128)(2,1)S(1)}, u32[]{:S(2)}, u32[]{:S(2)}) collective-permute-start(bf16[256,768]{1,0:T(8,128)(2,1)S(1)} %collective-permute-done.23), channel_id=1, source_target_pairs={{0,4},{4,0},{8,12},{12,8},{16,20},{20,16},{24,28},{28,24},{1,5},{5... | collective-permute-start | bytes 1179656 | tf_op jit(solution)/shard_map/ppermute | solution.py:116
  103.3 23.5 %collective-permute-start.38 = (bf16[64,1280]{1,0:T(8,128)(2,1)S(1)}, bf16[64,1280]{1,0:T(8,128)(2,1)S(1)}, u32[]{:S(2)}, u32[]{:S(2)}) collective-permute-start(bf16[64,1280]{1,0:T(8,128)(2,1)S(1)} %slice.284), channel_id=1, source_target_pairs={{0,2},{1,3},{2,0},{3,1},{4,6},{5,7},{6,4},{7,5},{8,10},{9,11},{10,... | collective-permute-start | bytes 491528 | tf_op jit(solution)/shard_map/ppermute | solution.py:120
  112.5 8.9 %collective-permute-start.35 = (bf16[64,1280]{1,0:T(8,128)(2,1)S(1)}, bf16[64,1280]{1,0:T(8,128)(2,1)S(1)}, u32[]{:S(2)}, u32[]{:S(2)}) collective-permute-start(bf16[64,1280]{1,0:T(8,128)(2,1)S(1)} %slice.285), channel_id=1, source_target_pairs={{0,2},{1,3},{2,0},{3,1},{4,6},{5,7},{6,4},{7,5},{8,10},{9,11},{10,... | collective-permute-start | bytes 491528 | tf_op jit(solution)/shard_map/ppermute | solution.py:120
  113.9 22.2 %collective-permute-start.41 = (bf16[256,768]{1,0:T(8,128)(2,1)S(1)}, bf16[256,768]{1,0:T(8,128)(2,1)S(1)}, u32[]{:S(2)}, u32[]{:S(2)}) collective-permute-start(bf16[256,768]{1,0:T(8,128)(2,1)S(1)} %add.153), channel_id=1, source_target_pairs={{0,4},{4,0},{8,12},{12,8},{16,20},{20,16},{24,28},{28,24},{1,5},{5... | collective-permute-start | bytes 1179656 | tf_op jit(solution)/shard_map/ppermute | solution.py:116
  115.5 18.2 %collective-permute-start.31 = (bf16[128,1280]{1,0:T(8,128)(2,1)S(1)}, bf16[128,1280]{1,0:T(8,128)(2,1)S(1)}, u32[]{:S(2)}, u32[]{:S(2)}) collective-permute-start(bf16[128,1280]{1,0:T(8,128)(2,1)S(1)} %slice.282), channel_id=1, source_target_pairs={{0,1},{1,0},{2,3},{3,2},{4,5},{5,4},{6,7},{7,6},{8,9},{9,8},{10,11... | collective-permute-start | bytes 983048 | tf_op jit(solution)/shard_map/ppermute | solution.py:120
  121.0 13.4 %collective-permute-start.28 = (bf16[128,1280]{1,0:T(8,128)(2,1)S(1)}, bf16[128,1280]{1,0:T(8,128)(2,1)S(1)}, u32[]{:S(2)}, u32[]{:S(2)}) collective-permute-start(bf16[128,1280]{1,0:T(8,128)(2,1)S(1)} %slice.283), channel_id=1, source_target_pairs={{0,1},{1,0},{2,3},{3,2},{4,5},{5,4},{6,7},{7,6},{8,9},{9,8},{10,11... | collective-permute-start | bytes 983048 | tf_op jit(solution)/shard_map/ppermute | solution.py:120
  121.5 10.2 %collective-permute-start.36 = (bf16[64,1280]{1,0:T(8,128)(2,1)S(1)}, bf16[64,1280]{1,0:T(8,128)(2,1)S(1)}, u32[]{:S(2)}, u32[]{:S(2)}) collective-permute-start(bf16[64,1280]{1,0:T(8,128)(2,1)S(1)} %fusion.10), channel_id=1, source_target_pairs={{0,8},{4,12},{8,0},{12,4},{16,24},{20,28},{24,16},{28,20},{1,9},{5... | collective-permute-start | bytes 491528 | tf_op jit(solution)/shard_map/ppermute | solution.py:108
  134.5 8.9 %collective-permute-start.29 = (bf16[64,1280]{1,0:T(8,128)(2,1)S(1)}, bf16[64,1280]{1,0:T(8,128)(2,1)S(1)}, u32[]{:S(2)}, u32[]{:S(2)}) collective-permute-start(bf16[64,1280]{1,0:T(8,128)(2,1)S(1)} %slice.287), channel_id=1, source_target_pairs={{0,2},{1,3},{2,0},{3,1},{4,6},{5,7},{6,4},{7,5},{8,10},{9,11},{10,... | collective-permute-start | bytes 491528 | tf_op jit(solution)/shard_map/ppermute | solution.py:120
  141.0 13.4 %collective-permute-start.33 = (bf16[64,1280]{1,0:T(8,128)(2,1)S(1)}, bf16[64,1280]{1,0:T(8,128)(2,1)S(1)}, u32[]{:S(2)}, u32[]{:S(2)}) collective-permute-start(bf16[64,1280]{1,0:T(8,128)(2,1)S(1)} %fusion.11), channel_id=1, source_target_pairs={{0,16},{4,20},{8,24},{12,28},{16,0},{20,4},{24,8},{28,12},{1,17},{... | collective-permute-start | bytes 491528 | tf_op jit(solution)/shard_map/ppermute | solution.py:108
  143.5 13.0 %collective-permute-start.30 = (bf16[64,1280]{1,0:T(8,128)(2,1)S(1)}, bf16[64,1280]{1,0:T(8,128)(2,1)S(1)}, u32[]{:S(2)}, u32[]{:S(2)}) collective-permute-start(bf16[64,1280]{1,0:T(8,128)(2,1)S(1)} %fusion.12), channel_id=1, source_target_pairs={{0,24},{4,28},{8,16},{12,20},{16,8},{20,12},{24,0},{28,4},{1,25},{... | collective-permute-start | bytes 491528 | tf_op jit(solution)/shard_map/ppermute | solution.py:108
  (16 other events, 102.6 us)

commit v4 on v2

v4 whole, which is shorter than its diff:
```python
import functools

import jax
import jax.numpy as jnp
from jax import lax
from jax.experimental import pallas as pl
from jax.experimental.pallas import tpu as pltpu
from jax.sharding import PartitionSpec as P

F32 = jnp.float32
BF16 = jnp.bfloat16
HALVES = 2
VMEM = pl.BlockSpec(memory_space=pltpu.VMEM)
SMEM = pl.BlockSpec(memory_space=pltpu.SMEM)
PARAMS = pltpu.CompilerParams(vmem_limit_bytes=40 * 2**20)


def split_dp(dp):
    outer = 1
    while 4 * outer * outer <= 2 * dp:
        outer *= 2
    return outer, dp // outer


def after(value, *others):
    return lax.optimization_barrier((value,) + others)[0]


def shape(rows, columns, kind):
    return jax.ShapeDtypeStruct((rows, columns), kind)


def cost(flops, size):
    return pl.CostEstimate(flops=flops, bytes_accessed=size, transcendentals=0)


def forward_kernel(parts, outer, n, *refs):
    x_refs, w_refs = refs[:parts], refs[parts : -outer - 1]
    out_refs, keep_ref = refs[-outer - 1 : -1], refs[-1]
    etp = 0
    for x_ref in x_refs:
        for first in range(0, x_ref.shape[0], outer * n):
            x = x_ref[first : first + outer * n, :]
            total, start = None, 0
            for w_ref in w_refs:
                stop = start + w_ref.shape[0]
                product = jnp.dot(x[:, start:stop], w_ref[...], preferred_element_type=F32)
                total = product if total is None else total + product
                start = stop
            for k in range(outer):
                rows = slice(k * n, (k + 1) * n)
                out_refs[k][etp * n : (etp + 1) * n, :] = total[rows].astype(out_refs[k].dtype)
                at = (k * keep_ref.shape[0] // outer) + etp * n
                keep_ref[at : at + n, :] = x[rows]
            etp += 1


def forward_call(x_parts, w_parts, outer):
    rows = sum(x.shape[0] for x in x_parts)
    span, columns = x_parts[0].shape[1], w_parts[0].shape[1]
    n = x_parts[0].shape[0] // outer
    each = rows // outer
    kinds = [F32] + [BF16] * (outer - 1)
    return pl.pallas_call(
        functools.partial(forward_kernel, len(x_parts), outer, n),
        out_shape=[shape(each, columns, kind) for kind in kinds] + [shape(rows, span, BF16)],
        in_specs=[VMEM] * (len(x_parts) + len(w_parts)),
        out_specs=[VMEM] * (outer + 1),
        compiler_params=PARAMS,
        cost_estimate=cost(2 * rows * span * columns, 2 * (2 * rows * span + span * columns)),
    )(*x_parts, *w_parts)


def gate_kernel(steps, half, order_ref, pre_ref, prob_ref, cot_ref, *refs):
    part_refs, (hidden_ref, grad_ref) = refs[:-2], refs[-2:]
    if half:
        hidden_ref[...] = part_refs[0][...]
        part_refs = part_refs[1:]
    rows, width = cot_ref.shape
    cap = rows // steps
    n = cap // HALVES
    for i in range(steps):
        here = slice(i * n, (i + 1) * n)
        there = pl.ds(pl.multiple_of(order_ref[i] * cap + half * n, n), n)
        total = pre_ref[here, :]
        for part_ref in part_refs:
            total = total + part_ref[here, :].astype(F32)
        gate, up = total[:, :width], total[:, width:]
        prob = prob_ref[i * cap + half * n : i * cap + (half + 1) * n, :].astype(F32)
        sig = jax.nn.sigmoid(gate)
        act = gate * sig
        hidden_ref[there, :] = (prob * act * up).astype(BF16)
        scaled = cot_ref[there, :].astype(F32) * prob
        grad_ref[here, :width] = (scaled * up * sig * (1.0 + gate * (1.0 - sig))).astype(BF16)
        grad_ref[here, width:] = (scaled * act).astype(BF16)


def gate_call(half, order, pre, prob, cotangent, before, parts):
    rows, width = cotangent.shape
    operands = [pre, prob, cotangent] + ([before] if half else []) + parts
    return pl.pallas_call(
        functools.partial(gate_kernel, order.shape[0], half),
        out_shape=(shape(rows, width, BF16), shape(pre.shape[0], 2 * width, BF16)),
        in_specs=[SMEM] + [VMEM] * len(operands),
        out_specs=(VMEM, VMEM),
        compiler_params=PARAMS,
        cost_estimate=cost(20 * rows * width, rows * width * 8),
    )(order, *operands)


def backward_kernel(outer, steps, n, *refs):
    grad_refs, w_refs = refs[:outer], refs[outer : -steps // 2 - 2]
    keep_refs, (send_ref, all_ref) = refs[-steps // 2 - 2 : -2], refs[-2:]
    each = steps * n
    contract = (((1,), (1,)), ((), ()))
    for k in range(outer):
        grad = grad_refs[k][...]
        all_ref[k * each : (k + 1) * each, :] = grad
        start = 0
        for w_ref in w_refs:
            stop = start + w_ref.shape[0]
            product = lax.dot_general(grad, w_ref[...], contract, preferred_element_type=F32)
            for i in range(steps):
                part = product[i * n : (i + 1) * n]
                if i < steps // 2:
                    keep_refs[i][k * n : (k + 1) * n, start:stop] = part
                else:
                    at = ((i - steps // 2) * outer + k) * n
                    send_ref[at : at + n, start:stop] = part.astype(BF16)
            start = stop


def backward_call(grads, w_parts, steps):
    outer = len(grads)
    n = grads[0].shape[0] // steps
    rows, columns = outer * grads[0].shape[0], grads[0].shape[1]
    span = sum(w.shape[0] for w in w_parts)
    return pl.pallas_call(
        functools.partial(backward_kernel, outer, steps, n),
        out_shape=[shape(outer * n, span, F32)] * (steps // 2)
        + [shape(rows // 2, span, BF16), shape(rows, columns, BF16)],
        in_specs=[VMEM] * (outer + len(w_parts)),
        out_specs=[VMEM] * (steps // 2 + 2),
        compiler_params=PARAMS,
        cost_estimate=cost(2 * rows * span * columns, 2 * (2 * rows * span + span * columns)),
    )(*grads, *w_parts)


def place_kernel(outer, inner, place_ref, slots_ref, *refs):
    out_ref = refs[-1]
    depth = out_ref.shape[1]
    rows = lax.broadcasted_iota(jnp.int32, (out_ref.shape[0], slots_ref.shape[1]), 0)
    onehot = (rows == slots_ref[...]).astype(BF16)
    for i in range(outer * inner):
        k, j = i // inner, i % inner

        @pl.when(pl.program_id(0) == i)
        def _():
            columns = slice(j * depth, (j + 1) * depth)
            halves = [refs[k * HALVES + h][:, columns] for h in range(HALVES)]
            block = jnp.concatenate(halves, axis=0)
            out_ref[...] = jnp.dot(onehot, block, preferred_element_type=F32).astype(BF16)


def place_call(place, slots, chunks, tok, outer, inner):
    span = chunks[0].shape[1]
    depth = span // inner
    whole = lambda array: pl.BlockSpec(array.shape, lambda i, place: (0, 0))
    slots = slots[None, :]
    return pl.pallas_call(
        functools.partial(place_kernel, outer, inner),
        out_shape=shape(tok, outer * span, BF16),
        grid_spec=pltpu.PrefetchScalarGridSpec(
            num_scalar_prefetch=1,
            grid=(outer * inner,),
            in_specs=[whole(slots)] + [whole(c) for c in chunks],
            out_specs=pl.BlockSpec((tok, depth), lambda i, place: (0, place[i])),
        ),
        compiler_params=PARAMS,
        cost_estimate=cost(2 * tok * slots.shape[1] * outer * span, 2 * tok * outer * span),
    )(place, slots, *chunks)


def make_shards(dp_size, etp_size):
    outer, inner = split_dp(dp_size)

    def over_outer(value, k):
        pairs = [(i, i ^ (k * inner)) for i in range(dp_size)]
        return lax.ppermute(value, "dp", pairs)

    def over_inner(value, j):
        pairs = [(i, i ^ j) for i in range(dp_size)]
        return lax.ppermute(value, "dp", pairs)

    def over_etp(value, e):
        pairs = [(i, i ^ e) for i in range(etp_size)]
        return lax.ppermute(value, "etp", pairs)

    part_order = [0]
    bit = etp_size // 2
    bits = []
    while bit:
        bits.append(bit)
        part_order = part_order + [c ^ bit for c in part_order]
        bit //= 2

    def gather_etp(value, order=None):
        pieces = [value]
        for i, b in enumerate(bits):
            joined = jnp.concatenate(pieces, axis=0) if len(pieces) > 1 else pieces[0]
            if order:
                joined = after(joined, order[i + 1])
            pieces = pieces + [over_etp(joined, b)]
        return pieces

    def reduce_etp(keep, sent):
        for b in reversed(bits):
            got = over_etp(sent, b)
            n = keep[0].shape[0]
            keep = [own + got[i * n : (i + 1) * n].astype(F32) for i, own in enumerate(keep)]
            half = len(keep) // 2
            if half:
                sent = jnp.concatenate([v.astype(BF16) for v in keep[half:]], axis=0)
                keep = keep[:half]
        return keep[0].astype(BF16)

    near_first = sorted(range(1, outer))
    far_first = near_first[::-1]
    keys = [0] + near_first
    halves = range(HALVES)

    def shards(tokens, slots, gate_probs, w_gate, w_up, d_hidden):
        dp = lax.axis_index("dp")
        etp = lax.axis_index("etp")
        a, b = dp // inner, dp % inner
        depth, width = w_gate.shape
        cap = slots.shape[0]
        n = cap // HALVES
        tok = tokens.shape[0]
        span = depth * inner
        wide = depth % 128 == 0

        onehot = (slots[:, None] == jnp.arange(tok, dtype=slots.dtype)[None, :]).astype(BF16)
        rows = jnp.dot(onehot, tokens, preferred_element_type=F32).astype(BF16)
        pieces = {}
        for h in halves:
            for k in keys:
                blocks = [
                    lax.dynamic_slice(rows, (h * n, (a ^ k) * span + (b ^ j) * depth), (n, depth))
                    for j in range(inner)
                ]
                pieces[h, k] = jnp.concatenate(blocks, axis=1)

        w_own = jnp.concatenate([w_gate, w_up], axis=1)
        w_parts = [w_own] + [over_inner(after(w_own, rows), j) for j in range(1, inner)]
        if not wide:
            w_parts = [jnp.concatenate(w_parts, axis=0)]

        x_parts = []
        for h in halves:
            got = {k: over_outer(pieces[h, k], k) for k in far_first}
            mine = jnp.concatenate([pieces[h, 0]] + [got[k] for k in near_first], axis=0)
            x_parts.append(gather_etp(mine, x_parts[0] if h else None))
        probs = jnp.concatenate(gather_etp(after(gate_probs, x_parts[0][-1])), axis=0)[:, None]
        order = etp ^ jnp.array(part_order, jnp.int32)

        kept, grads, hidden = [], [], None
        products = []
        for h in halves:
            if h:
                x_parts[h][0] = after(x_parts[h][0], products[0][0])
            *product, x_all = forward_call(x_parts[h], w_parts, outer)
            kept.append(x_all)
            parts = [over_outer(product[k], k) for k in far_first]
            products.append((product[0], parts))
        probs = after(probs, products[1][0])
        for h in halves:
            if h and outer > 1:
                probs = after(probs, grads[0][1])
            hidden, paired = gate_call(h, order, products[h][0], probs, d_hidden, hidden, products[h][1])
            grads.append([over_outer(paired, k) if k else paired for k in keys])

        chunks = [None] * (outer * HALVES)
        totals = [None] * inner
        for h in halves:
            grads[h][0] = after(grads[h][0], own if h else grads[1][0])
            *keep, sent, grad_all = backward_call(grads[h], w_parts, etp_size)
            own = reduce_etp(keep, sent)
            for k in far_first + [0]:
                block = own[k * n : (k + 1) * n]
                chunks[k * HALVES + h] = over_outer(block, k) if k else block
            for j in reversed(range(inner)):
                product = lax.dot_general(
                    kept[h][:, j * depth : (j + 1) * depth],
                    grad_all,
                    (((0,), (0,)), ((), ())),
                    preferred_element_type=F32,
                )
                totals[j] = product if h == 0 else totals[j] + product
        total = totals[0]
        for j in range(1, inner):
            total = total + over_inner(totals[j].astype(BF16), j).astype(F32)

        if wide:
            place = dp ^ jnp.arange(outer * inner, dtype=jnp.int32)
            grad_tokens = place_call(place, slots, chunks, tok, outer, inner)
        else:
            dx = jnp.zeros((cap, outer * span), BF16)
            for k in keys:
                chunk = jnp.concatenate(chunks[k * HALVES : (k + 1) * HALVES], axis=0)
                for j in range(inner):
                    block = chunk[:, j * depth : (j + 1) * depth]
                    dx = lax.dynamic_update_slice(dx, block, (0, (a ^ k) * span + (b ^ j) * depth))
            grad_tokens = lax.dot_general(
                onehot, dx, (((0,), (0,)), ((), ())), preferred_element_type=F32
            ).astype(BF16)
        return (hidden, grad_tokens, total[:, :width], total[:, width:])

    return shards


def solution(mesh):
    in_specs = (
        P(("dp", "etp"), None),
        P(("dp", "etp")),
        P(("dp", "etp")),
        P("dp", "etp"),
        P("dp", "etp"),
        P("dp", "etp"),
    )
    out_specs = (P("dp", "etp"), P(("dp", "etp"), None), P("dp", "etp"), P("dp", "etp"))
    shards = make_shards(mesh.shape["dp"], mesh.shape["etp"])
    return jax.shard_map(shards, mesh=mesh, in_specs=in_specs, out_specs=out_specs, check_vma=False)
```

time: 146 us -> 182 us (1.25)
  Pallas kernels: 1.65 us -> 20.4 us
  local copies, waits for them, and re-layouts: 2.38 us -> 19.7 us
  matrix products: 15.4 us -> 6.59 us
  starting transfers between devices: 39.6 us -> 46.6 us
  waiting for transfers between devices: 83.1 us -> 85.7 us
    pallas_call x1 -> x7, Pallas kernels: 1.65 us -> 20.4 us  [the longest x2 5.92 us: backward_call(): pl.pallas_call(functools.partial(backward_kernel, outer, steps, n), out_s...]
    unnamed x23 -> x55, local copies, waits for them, and re-layouts: 0.25 us -> 17 us
    ppermute x3 -> x2, waiting for transfers between devices: 0.01 us -> 15.6 us  [over_inner(): return lax.ppermute(value, 'dp', pairs)]
    ppermute x12 -> x24, starting transfers between devices: 21.5 us -> 36.3 us  [over_outer(): return lax.ppermute(value, 'dp', pairs)]
    ppermute x12 -> x24, waiting for transfers between devices: 65.7 us -> 51.5 us  [over_outer(): return lax.ppermute(value, 'dp', pairs)]
    dot_general x10 -> x4, matrix products: 11.9 us -> 3.02 us  [shards(): lax.dot_general(kept[h][:, j * depth:(j + 1) * depth], grad_all, (((0,),...]
    ppermute x18 -> x10, starting transfers between devices: 13.5 us -> 7.28 us  [over_etp(): return lax.ppermute(value, 'etp', pairs)]
    ppermute x3 -> x2, starting transfers between devices: 4.66 us -> 3.06 us  [over_inner(): return lax.ppermute(value, 'dp', pairs)]
  transfers between devices with their start and end apart: 33 -> 36, of which waited for: 15 -> 14; matrix products, arithmetic and copies ran while one was open for 11% -> 5% of each run, Pallas kernels for 0% -> 4%
where the time goes in v4:
time: 182 us
  waiting for transfers between devices  85.7 us (47%)
  starting transfers between devices  46.6 us (26%)
  Pallas kernels  20.4 us (11%)
  local copies, waits for them, and re-layouts  19.7 us (11%)
  matrix products  6.59 us (4%)
    ppermute x24, waiting for transfers between devices, over_outer(): return lax.ppermute(value, 'dp', pairs)  51.5 us
    ppermute x24, starting transfers between devices, over_outer(): return lax.ppermute(value, 'dp', pairs)  36.3 us
    ppermute x10, waiting for transfers between devices, over_etp(): return lax.ppermute(value, 'etp', pairs)  18.5 us
    unnamed x55, local copies, waits for them, and re-layouts  17 us
    ppermute x2, waiting for transfers between devices, over_inner(): return lax.ppermute(value, 'dp', pairs)  15.6 us
    ppermute x10, starting transfers between devices, over_etp(): return lax.ppermute(value, 'etp', pairs)  7.28 us
    pallas_call x2, Pallas kernels, backward_call(): pl.pallas_call(functools.partial(backward_kernel, outer, steps, n), out_s...  5.92 us
    pallas_call x1, Pallas kernels, place_call(): pl.pallas_call(functools.partial(place_kernel, outer, inner), out_shape=s...  5.84 us
  transfers between devices with their start and end apart: 36, of which 14 were waited for; matrix products, arithmetic and copies ran while one was open for 5% of the time, Pallas kernels for 4%

profile of v4, /device:TPU:0, one launch (start us, length us, event | category | flops | bytes accessed | tf_op | source)
XLA Modules:
  0.0 181.7 jit_solution(13202749332895842576)
XLA Ops:
  0.7 3.6 %convolution_convert_fusion = bf16[64,5120]{1,0:T(8,128)(2,1)S(1)} fusion(bf16[512,5120]{1,0:T(8,128)(2,1)} %param.7, s32[64]{0:T(128)} %param.8), kind=kOutput, calls=%fused_computation | convolution fusion | flops 335904768 | bytes 5898496 | tf_op jit(solution)/shard_map/dot_general | solution.py:244
  4.4 3.1 %collective-permute-start = (bf16[32,1280]{1,0:T(8,128)(2,1)S(1)}, bf16[32,1280]{1,0:T(8,128)(2,1)S(1)}, u32[]{:S(2)}, u32[]{:S(2)}) collective-permute-start(bf16[32,1280]{1,0:T(8,128)(2,1)S(1)} %pad_maximum_fusion.2), channel_id=1, source_target_pairs={{0,8},{4,12},{8,0},{12,4},{16,24},{20,28},{24,16},{28,20},{1,9},{5... | collective-permute-start | bytes 245768 | tf_op jit(solution)/shard_map/ppermute | solution.py:189
  7.5 2.7 %collective-permute-start.1 = (bf16[32,1280]{1,0:T(8,128)(2,1)S(1)}, bf16[32,1280]{1,0:T(8,128)(2,1)S(1)}, u32[]{:S(2)}, u32[]{:S(2)}) collective-permute-start(bf16[32,1280]{1,0:T(8,128)(2,1)S(1)} %pad_maximum_fusion.3), channel_id=1, source_target_pairs={{0,16},{4,20},{8,24},{12,28},{16,0},{20,4},{24,8},{28,12},{1,17},{... | collective-permute-start | bytes 245768 | tf_op jit(solution)/shard_map/ppermute | solution.py:189
  10.8 4.0 %collective-permute-start.5 = (bf16[32,1280]{1,0:T(8,128)(2,1)S(1)}, bf16[32,1280]{1,0:T(8,128)(2,1)S(1)}, u32[]{:S(2)}, u32[]{:S(2)}) collective-permute-start(bf16[32,1280]{1,0:T(8,128)(2,1)S(1)} %pad_maximum_fusion.7), channel_id=1, source_target_pairs={{0,24},{4,28},{8,16},{12,20},{16,8},{20,12},{24,0},{28,4},{1,25},{... | collective-permute-start | bytes 245768 | tf_op jit(solution)/shard_map/ppermute | solution.py:189
  15.7 1.7 collective-permute-start.2
  17.3 3.7 %collective-permute-done.4 = bf16[32,1280]{1,0:T(8,128)(2,1)S(1)} collective-permute-done((bf16[32,1280]{1,0:T(8,128)(2,1)S(1)}, bf16[32,1280]{1,0:T(8,128)(2,1)S(1)}, u32[]{:S(2)}, u32[]{:S(2)}) %collective-permute-start.4) | collective-permute-done | bytes 81952 | tf_op jit(solution)/shard_map/ppermute | solution.py:189
  24.9 8.1 %collective-permute-done.6.refs_1_ = bf16[128,1280]{1,0:T(8,128)(2,1)S(1)} collective-permute-done((bf16[128,1280]{1,0:T(8,128)(2,1)S(1)}, bf16[128,1280]{1,0:T(8,128)(2,1)S(1)}, u32[]{:S(2)}, u32[]{:S(2)}) %collective-permute-start.6) | collective-permute-done | bytes 327712 | tf_op jit(solution)/shard_map/ppermute | solution.py:197
  36.0 4.2 %collective-permute-done.9.refs_1_ = bf16[128,1280]{1,0:T(8,128)(2,1)S(1)} collective-permute-done((bf16[128,1280]{1,0:T(8,128)(2,1)S(1)}, bf16[128,1280]{1,0:T(8,128)(2,1)S(1)}, u32[]{:S(2)}, u32[]{:S(2)}) %collective-permute-start.9) | collective-permute-done | bytes 327712 | tf_op jit(solution)/shard_map/ppermute | solution.py:197
  47.3 2.2 %shard_map.102 = (f32[128,768]{1,0:T(8,128)S(1)}, bf16[128,768]{1,0:T(8,128)(2,1)}, bf16[128,768]{1,0:T(8,128)(2,1)}, bf16[128,768]{1,0:T(8,128)(2,1)}, bf16[512,1280]{1,0:T(8,128)(2,1)S(1)}) custom-call(bf16[128,1280]{1,0:T(8,128)(2,1)S(1)} %pad_maximum_fusion.1.refs_0_, bf16[128,1280]{1,0:T(8,128)(2,1)S(1)} %collective-permute-done.6.refs_1_, ...), custom_call_target="tpu_custom_call" | custom-call | flops 1006632960 | bytes 4587520 | tf_op jit(solution)/shard_map/pallas_call | solution.py:64
  50.5 3.0 %collective-permute-start.13 = (bf16[128,768]{1,0:T(8,128)(2,1)}, bf16[128,768]{1,0:T(8,128)(2,1)}, u32[]{:S(2)}, u32[]{:S(2)}) collective-permute-start(bf16[128,768]{1,0:T(8,128)(2,1)} %get-tuple-element.43), channel_id=1, source_target_pairs={{0,24},{4,28},{8,16},{12,20},{16,8},{20,12},{24,0},{28,4},{1,25},{... | collective-permute-start | bytes 589832 | tf_op jit(solution)/shard_map/ppermute | solution.py:189
  57.4 2.5 %shard_map.103 = (f32[128,768]{1,0:T(8,128)S(1)}, bf16[128,768]{1,0:T(8,128)(2,1)S(1)}, bf16[128,768]{1,0:T(8,128)(2,1)S(1)}, bf16[128,768]{1,0:T(8,128)(2,1)S(1)}, bf16[512,1280]{1,0:T(8,128)(2,1)S(1)}) custom-call(bf16[128,1280]{1,0:T(8,128)(2,1)S(1)} %pad_maximum_fusion.refs_0_, bf16[128,1280]{1,0:T(8,128)(2,1)S(1)} %copy-done.4, ...), custom_call_target="tpu_custom_call" | custom-call | flops 1006632960 | bytes 4587520 | tf_op jit(solution)/shard_map/pallas_call | solution.py:64
  62.1 7.6 %collective-permute-done.14.refs_1_ = bf16[128,768]{1,0:T(8,128)(2,1)} collective-permute-done((bf16[128,768]{1,0:T(8,128)(2,1)}, bf16[128,768]{1,0:T(8,128)(2,1)}, u32[]{:S(2)}, u32[]{:S(2)}) %collective-permute-start.14) | collective-permute-done | bytes 196640 | tf_op jit(solution)/shard_map/ppermute | solution.py:189
  70.7 2.0 %shard_map.104 = (bf16[256,384]{1,0:T(8,128)(2,1)S(1)}, bf16[128,768]{1,0:T(8,128)(2,1)}) custom-call(s32[4]{0:T(128)S(1)} %broadcast_xor_fusion.order_ref, f32[128,768]{1,0:T(8,128)S(1)} %copy-done.2, bf16[256,1]{1,0:T(8,128)(2,1)S(1)} %copy.11.prob_ref, bf16[256,384]{1,0:T(8,128)(2,1)S(1)} %copy-done, bf16[128,768]{1,0:T(8,128)(2,1)} %collective-permute-done.13.refs_0_, ...), custom_call_target="tpu_custom_call" | custom-call | flops 1966080 | bytes 786432 | tf_op jit(solution)/shard_map/pallas_call | solution.py:101
  72.7 2.2 %collective-permute-start.17 = (bf16[128,768]{1,0:T(8,128)(2,1)}, bf16[128,768]{1,0:T(8,128)(2,1)}, u32[]{:S(2)}, u32[]{:S(2)}) collective-permute-start(bf16[128,768]{1,0:T(8,128)(2,1)} %copy-done.19), channel_id=1, source_target_pairs={{0,24},{4,28},{8,16},{12,20},{16,8},{20,12},{24,0},{28,4},{1,25},{... | collective-permute-start | bytes 589832 | tf_op jit(solution)/shard_map/ppermute | solution.py:189
  77.1 2.2 %collective-permute-start.21 = (bf16[128,768]{1,0:T(8,128)(2,1)}, bf16[128,768]{1,0:T(8,128)(2,1)}, u32[]{:S(2)}, u32[]{:S(2)}) collective-permute-start(bf16[128,768]{1,0:T(8,128)(2,1)} %get-tuple-element.54.refs_0_), channel_id=1, source_target_pairs={{0,24},{4,28},{8,16},{12,20},{16,8},{20,12},{24,0},{28,4},{1,25},{... | collective-permute-start | bytes 589832 | tf_op jit(solution)/shard_map/ppermute | solution.py:189
  79.3 6.3 %collective-permute-done.16.refs_1_ = bf16[128,768]{1,0:T(8,128)(2,1)S(1)} collective-permute-done((bf16[128,768]{1,0:T(8,128)(2,1)}, bf16[128,768]{1,0:T(8,128)(2,1)S(1)}, u32[]{:S(2)}, u32[]{:S(2)}) %collective-permute-start.16) | collective-permute-done | bytes 196640 | tf_op jit(solution)/shard_map/ppermute | solution.py:189
  86.4 17.0 %collective-permute-done.18.refs_2_ = bf16[128,768]{1,0:T(8,128)(2,1)} collective-permute-done((bf16[128,768]{1,0:T(8,128)(2,1)}, bf16[128,768]{1,0:T(8,128)(2,1)}, u32[]{:S(2)}, u32[]{:S(2)}) %collective-permute-start.18) | collective-permute-done | bytes 196640 | tf_op jit(solution)/shard_map/ppermute | solution.py:189
  103.4 2.0 %shard_map.105 = (bf16[256,384]{1,0:T(8,128)(2,1)}, bf16[128,768]{1,0:T(8,128)(2,1)S(1)}) custom-call(s32[4]{0:T(128)S(1)} %broadcast_xor_fusion.order_ref, f32[128,768]{1,0:T(8,128)S(1)} %get-tuple-element.40.pre_ref, bf16[256,1]{1,0:T(8,128)(2,1)S(1)} %copy.12.prob_ref, bf16[256,384]{1,0:T(8,128)(2,1)S(1)} %copy-done, ...), custom_call_target="tpu_custom_call" | custom-call | flops 1966080 | bytes 786432 | tf_op jit(solution)/shard_map/pallas_call | solution.py:101
  105.4 4.6 %collective-permute-done.20.refs_2_ = bf16[128,768]{1,0:T(8,128)(2,1)} collective-permute-done((bf16[128,768]{1,0:T(8,128)(2,1)}, bf16[128,768]{1,0:T(8,128)(2,1)}, u32[]{:S(2)}, u32[]{:S(2)}) %collective-permute-start.20) | collective-permute-done | bytes 196640 | tf_op jit(solution)/shard_map/ppermute | solution.py:189
  113.3 3.5 %shard_map.106 = (f32[128,1280]{1,0:T(8,128)S(1)}, f32[128,1280]{1,0:T(8,128)S(1)}, bf16[256,1280]{1,0:T(8,128)(2,1)S(1)}, bf16[512,768]{1,0:T(8,128)(2,1)S(1)}) custom-call(bf16[128,768]{1,0:T(8,128)(2,1)} %get-tuple-element.54.refs_0_, bf16[128,768]{1,0:T(8,128)(2,1)S(1)} %copy-done.18, bf16[128,768]{1,0:T(8,128)(2,1)} %collective-permute-done.20.refs_2_, ...), custom_call_target="tpu_custom_call" | custom-call | flops 1006632960 | bytes 4587520 | tf_op jit(solution)/shard_map/pallas_call | solution.py:138
  116.9 2.1 %collective-permute-done.22 = bf16[256,1280]{1,0:T(8,128)(2,1)S(1)} collective-permute-done((bf16[256,1280]{1,0:T(8,128)(2,1)S(1)}, bf16[256,1280]{1,0:T(8,128)(2,1)S(1)}, u32[]{:S(2)}, u32[]{:S(2)}) %collective-permute-start.22) | collective-permute-done | bytes 655392 | tf_op jit(solution)/shard_map/ppermute | solution.py:197
  119.6 2.2 %collective-permute-start.26 = (bf16[128,768]{1,0:T(8,128)(2,1)S(1)}, bf16[128,768]{1,0:T(8,128)(2,1)S(1)}, u32[]{:S(2)}, u32[]{:S(2)}) collective-permute-start(bf16[128,768]{1,0:T(8,128)(2,1)S(1)} %get-tuple-element.58.refs_0_), channel_id=1, source_target_pairs={{0,24},{4,28},{8,16},{12,20},{16,8},{20,12},{24,0},{28,4},{1,25},{... | collective-permute-start | bytes 589832 | tf_op jit(solution)/shard_map/ppermute | solution.py:189
  121.9 2.2 %collective-permute-start.24 = (bf16[128,768]{1,0:T(8,128)(2,1)S(1)}, bf16[128,768]{1,0:T(8,128)(2,1)S(1)}, u32[]{:S(2)}, u32[]{:S(2)}) collective-permute-start(bf16[128,768]{1,0:T(8,128)(2,1)S(1)} %get-tuple-element.58.refs_0_), channel_id=1, source_target_pairs={{0,8},{4,12},{8,0},{12,4},{16,24},{20,28},{24,16},{28,20},{1,9},{5... | collective-permute-start | bytes 589832 | tf_op jit(solution)/shard_map/ppermute | solution.py:189
  124.7 4.1 %collective-permute-done.23 = bf16[128,1280]{1,0:T(8,128)(2,1)S(1)} collective-permute-done((bf16[128,1280]{1,0:T(8,128)(2,1)S(1)}, bf16[128,1280]{1,0:T(8,128)(2,1)S(1)}, u32[]{:S(2)}, u32[]{:S(2)}) %collective-permute-start.23) | collective-permute-done | bytes 327712 | tf_op jit(solution)/shard_map/ppermute | solution.py:197
  129.3 8.5 %collective-permute-done.25.refs_2_ = bf16[128,768]{1,0:T(8,128)(2,1)S(1)} collective-permute-done((bf16[128,768]{1,0:T(8,128)(2,1)S(1)}, bf16[128,768]{1,0:T(8,128)(2,1)S(1)}, u32[]{:S(2)}, u32[]{:S(2)}) %collective-permute-start.25) | collective-permute-done | bytes 196640 | tf_op jit(solution)/shard_map/ppermute | solution.py:189
  137.8 2.4 %shard_map.107 = (f32[128,1280]{1,0:T(8,128)S(1)}, f32[128,1280]{1,0:T(8,128)S(1)}, bf16[256,1280]{1,0:T(8,128)(2,1)S(1)}, bf16[512,768]{1,0:T(8,128)(2,1)S(1)}) custom-call(bf16[128,768]{1,0:T(8,128)(2,1)S(1)} %get-tuple-element.58.refs_0_, bf16[128,768]{1,0:T(8,128)(2,1)S(1)} %collective-permute-done.24.refs_1_, ...), custom_call_target="tpu_custom_call" | custom-call | flops 1006632960 | bytes 4587520 | tf_op jit(solution)/shard_map/pallas_call | solution.py:138
  145.0 2.8 %collective-permute-start.29 = (bf16[32,1280]{1,0:T(8,128)(2,1)S(1)}, bf16[32,1280]{1,0:T(8,128)(2,1)S(1)}, u32[]{:S(2)}, u32[]{:S(2)}) collective-permute-start(bf16[32,1280]{1,0:T(8,128)(2,1)S(1)} %get-tuple-element.90), channel_id=1, source_target_pairs={{0,8},{4,12},{8,0},{12,4},{16,24},{20,28},{24,16},{28,20},{1,9},{5... | collective-permute-start | bytes 245768 | tf_op jit(solution)/shard_map/ppermute | solution.py:189
  150.3 15.6 %collective-permute-done.35 = bf16[640,768]{1,0:T(8,128)(2,1)S(1)} collective-permute-done((bf16[640,768]{1,0:T(8,128)(2,1)S(1)}, bf16[640,768]{1,0:T(8,128)(2,1)S(1)}, u32[]{:S(2)}, u32[]{:S(2)}) %collective-permute-start.35) | collective-permute-done | bytes 983072 | tf_op jit(solution)/shard_map/ppermute | solution.py:193
  166.4 1.6 collective-permute-start.34
  168.1 2.8 %collective-permute-start.30 = (bf16[32,1280]{1,0:T(8,128)(2,1)S(1)}, bf16[32,1280]{1,0:T(8,128)(2,1)S(1)}, u32[]{:S(2)}, u32[]{:S(2)}) collective-permute-start(bf16[32,1280]{1,0:T(8,128)(2,1)S(1)} %get-tuple-element.86), channel_id=1, source_target_pairs={{0,8},{4,12},{8,0},{12,4},{16,24},{20,28},{24,16},{28,20},{1,9},{5... | collective-permute-start | bytes 245768 | tf_op jit(solution)/shard_map/ppermute | solution.py:189
  173.7 2.1 %collective-permute-done.32.refs_5_ = bf16[32,1280]{1,0:T(8,128)(2,1)S(1)} collective-permute-done((bf16[32,1280]{1,0:T(8,128)(2,1)S(1)}, bf16[32,1280]{1,0:T(8,128)(2,1)S(1)}, u32[]{:S(2)}, u32[]{:S(2)}) %collective-permute-start.32) | collective-permute-done | bytes 81952 | tf_op jit(solution)/shard_map/ppermute | solution.py:189
  175.9 5.8 %shard_map.108 = bf16[512,5120]{1,0:T(8,128)(2,1)} custom-call(s32[8]{0:T(128)S(1)} %iota_xor_fusion.place_ref, s32[1,64]{1,0:T(1,128)S(1)} %bitcast.6, bf16[32,1280]{1,0:T(8,128)(2,1)S(1)} %get-tuple-element.91.refs_0_, bf16[32,1280]{1,0:T(8,128)(2,1)S(1)} %get-tuple-element.87.refs_1_, bf16[32,1280]{1,0:T(8,128)(2,1)S(1)} %collective-permute-done.29.refs_2_, ...), custom_call_target="tpu_custom_call" | custom-call | flops 335544320 | bytes 5242880 | tf_op jit(solution)/shard_map/pallas_call | solution.py:170
  (135 shorter events, 42.3 us)
Async XLA Ops:
  4.4 19.8 %collective-permute-start = (bf16[32,1280]{1,0:T(8,128)(2,1)S(1)}, bf16[32,1280]{1,0:T(8,128)(2,1)S(1)}, u32[]{:S(2)}, u32[]{:S(2)}) collective-permute-start(bf16[32,1280]{1,0:T(8,128)(2,1)S(1)} %pad_maximum_fusion.2), channel_id=1, source_target_pairs={{0,8},{4,12},{8,0},{12,4},{16,24},{20,28},{24,16},{28,20},{1,9},{5... | collective-permute-start | bytes 245768 | tf_op jit(solution)/shard_map/ppermute | solution.py:189
  7.5 17.4 %collective-permute-start.1 = (bf16[32,1280]{1,0:T(8,128)(2,1)S(1)}, bf16[32,1280]{1,0:T(8,128)(2,1)S(1)}, u32[]{:S(2)}, u32[]{:S(2)}) collective-permute-start(bf16[32,1280]{1,0:T(8,128)(2,1)S(1)} %pad_maximum_fusion.3), channel_id=1, source_target_pairs={{0,16},{4,20},{8,24},{12,28},{16,0},{20,4},{24,8},{28,12},{1,17},{... | collective-permute-start | bytes 245768 | tf_op jit(solution)/shard_map/ppermute | solution.py:189
  10.7 10.4 %collective-permute-start.4 = (bf16[32,1280]{1,0:T(8,128)(2,1)S(1)}, bf16[32,1280]{1,0:T(8,128)(2,1)S(1)}, u32[]{:S(2)}, u32[]{:S(2)}) collective-permute-start(bf16[32,1280]{1,0:T(8,128)(2,1)S(1)} %pad_maximum_fusion.6), channel_id=1, source_target_pairs={{0,16},{4,20},{8,24},{12,28},{16,0},{20,4},{24,8},{28,12},{1,17},{... | collective-permute-start | bytes 245768 | tf_op jit(solution)/shard_map/ppermute | solution.py:189
  10.8 11.8 %collective-permute-start.5 = (bf16[32,1280]{1,0:T(8,128)(2,1)S(1)}, bf16[32,1280]{1,0:T(8,128)(2,1)S(1)}, u32[]{:S(2)}, u32[]{:S(2)}) collective-permute-start(bf16[32,1280]{1,0:T(8,128)(2,1)S(1)} %pad_maximum_fusion.7), channel_id=1, source_target_pairs={{0,24},{4,28},{8,16},{12,20},{16,8},{20,12},{24,0},{28,4},{1,25},{... | collective-permute-start | bytes 245768 | tf_op jit(solution)/shard_map/ppermute | solution.py:189
  15.7 9.2 %collective-permute-start.2 = (bf16[32,1280]{1,0:T(8,128)(2,1)S(1)}, bf16[32,1280]{1,0:T(8,128)(2,1)S(1)}, u32[]{:S(2)}, u32[]{:S(2)}) collective-permute-start(bf16[32,1280]{1,0:T(8,128)(2,1)S(1)} %pad_maximum_fusion.4), channel_id=1, source_target_pairs={{0,24},{4,28},{8,16},{12,20},{16,8},{20,12},{24,0},{28,4},{1,25},{... | collective-permute-start | bytes 245768 | tf_op jit(solution)/shard_map/ppermute | solution.py:189
  21.1 23.0 %collective-permute-start.8 = (bf16[640,768]{1,0:T(8,128)(2,1)S(1)}, bf16[640,768]{1,0:T(8,128)(2,1)S(1)}, u32[]{:S(2)}, u32[]{:S(2)}) collective-permute-start(bf16[640,768]{1,0:T(8,128)(2,1)S(1)} %constant_dynamic-update-slice_fusion.4.refs_3_.refs_4_), channel_id=1, source_target_pairs={{0,4},{4,0},{8,12},{12,8},{16,20},{20,16},{24,28},{28,24},{1,5},{5... | collective-permute-start | bytes 2949128 | tf_op jit(solution)/shard_map/ppermute | solution.py:193
  22.6 10.4 %collective-permute-start.6 = (bf16[128,1280]{1,0:T(8,128)(2,1)S(1)}, bf16[128,1280]{1,0:T(8,128)(2,1)S(1)}, u32[]{:S(2)}, u32[]{:S(2)}) collective-permute-start(bf16[128,1280]{1,0:T(8,128)(2,1)S(1)} %pad_maximum_fusion.1.refs_0_), channel_id=1, source_target_pairs={{0,2},{1,3},{2,0},{3,1},{4,6},{5,7},{6,4},{7,5},{8,10},{9,11},{10,... | collective-permute-start | bytes 983048 | tf_op jit(solution)/shard_map/ppermute | solution.py:197
  33.1 7.1 %collective-permute-start.9 = (bf16[128,1280]{1,0:T(8,128)(2,1)S(1)}, bf16[128,1280]{1,0:T(8,128)(2,1)S(1)}, u32[]{:S(2)}, u32[]{:S(2)}) collective-permute-start(bf16[128,1280]{1,0:T(8,128)(2,1)S(1)} %pad_maximum_fusion.refs_0_), channel_id=1, source_target_pairs={{0,2},{1,3},{2,0},{3,1},{4,6},{5,7},{6,4},{7,5},{8,10},{9,11},{10,... | collective-permute-start | bytes 983048 | tf_op jit(solution)/shard_map/ppermute | solution.py:197
  42.5 12.6 %collective-permute-start.10 = (bf16[256,1280]{1,0:T(8,128)(2,1)}, bf16[256,1280]{1,0:T(8,128)(2,1)}, u32[]{:S(2)}, u32[]{:S(2)}) collective-permute-start(bf16[256,1280]{1,0:T(8,128)(2,1)} %constant_dynamic-update-slice_fusion.6), channel_id=1, source_target_pairs={{0,1},{1,0},{2,3},{3,2},{4,5},{5,4},{6,7},{7,6},{8,9},{9,8},{10,11... | collective-permute-start | bytes 1966088 | tf_op jit(solution)/shard_map/ppermute | solution.py:197
  42.5 7.8 %collective-permute-start.11 = (bf16[64]{0:T(256)(128)(2,1)S(1)}, bf16[64]{0:T(256)(128)(2,1)S(1)}, u32[]{:S(2)}, u32[]{:S(2)}) collective-permute-start(bf16[64]{0:T(256)(128)(2,1)S(1)} %copy-done.22), channel_id=1, source_target_pairs={{0,2},{1,3},{2,0},{3,1},{4,6},{5,7},{6,4},{7,5},{8,10},{9,11},{10,... | collective-permute-start | bytes 392 | tf_op jit(solution)/shard_map/ppermute | solution.py:197
  50.5 11.6 %collective-permute-start.13 = (bf16[128,768]{1,0:T(8,128)(2,1)}, bf16[128,768]{1,0:T(8,128)(2,1)}, u32[]{:S(2)}, u32[]{:S(2)}) collective-permute-start(bf16[128,768]{1,0:T(8,128)(2,1)} %get-tuple-element.43), channel_id=1, source_target_pairs={{0,24},{4,28},{8,16},{12,20},{16,8},{20,12},{24,0},{28,4},{1,25},{... | collective-permute-start | bytes 589832 | tf_op jit(solution)/shard_map/ppermute | solution.py:189
  53.5 16.2 %collective-permute-start.14 = (bf16[128,768]{1,0:T(8,128)(2,1)}, bf16[128,768]{1,0:T(8,128)(2,1)}, u32[]{:S(2)}, u32[]{:S(2)}) collective-permute-start(bf16[128,768]{1,0:T(8,128)(2,1)} %get-tuple-element.44), channel_id=1, source_target_pairs={{0,16},{4,20},{8,24},{12,28},{16,0},{20,4},{24,8},{28,12},{1,17},{... | collective-permute-start | bytes 589832 | tf_op jit(solution)/shard_map/ppermute | solution.py:189
  53.5 16.2 %collective-permute-start.15 = (bf16[128,768]{1,0:T(8,128)(2,1)}, bf16[128,768]{1,0:T(8,128)(2,1)}, u32[]{:S(2)}, u32[]{:S(2)}) collective-permute-start(bf16[128,768]{1,0:T(8,128)(2,1)} %get-tuple-element.45), channel_id=1, source_target_pairs={{0,8},{4,12},{8,0},{12,4},{16,24},{20,28},{24,16},{28,20},{1,9},{5... | collective-permute-start | bytes 589832 | tf_op jit(solution)/shard_map/ppermute | solution.py:189
  72.7 12.9 %collective-permute-start.16 = (bf16[128,768]{1,0:T(8,128)(2,1)}, bf16[128,768]{1,0:T(8,128)(2,1)S(1)}, u32[]{:S(2)}, u32[]{:S(2)}) collective-permute-start(bf16[128,768]{1,0:T(8,128)(2,1)} %get-tuple-element.54.refs_0_), channel_id=1, source_target_pairs={{0,8},{4,12},{8,0},{12,4},{16,24},{20,28},{24,16},{28,20},{1,9},{5... | collective-permute-start | bytes 589832 | tf_op jit(solution)/shard_map/ppermute | solution.py:189
  72.7 13.7 %collective-permute-start.17 = (bf16[128,768]{1,0:T(8,128)(2,1)}, bf16[128,768]{1,0:T(8,128)(2,1)}, u32[]{:S(2)}, u32[]{:S(2)}) collective-permute-start(bf16[128,768]{1,0:T(8,128)(2,1)} %copy-done.19), channel_id=1, source_target_pairs={{0,24},{4,28},{8,16},{12,20},{16,8},{20,12},{24,0},{28,4},{1,25},{... | collective-permute-start | bytes 589832 | tf_op jit(solution)/shard_map/ppermute | solution.py:189
  74.9 28.4 %collective-permute-start.18 = (bf16[128,768]{1,0:T(8,128)(2,1)}, bf16[128,768]{1,0:T(8,128)(2,1)}, u32[]{:S(2)}, u32[]{:S(2)}) collective-permute-start(bf16[128,768]{1,0:T(8,128)(2,1)} %copy-done.16), channel_id=1, source_target_pairs={{0,16},{4,20},{8,24},{12,28},{16,0},{20,4},{24,8},{28,12},{1,17},{... | collective-permute-start | bytes 589832 | tf_op jit(solution)/shard_map/ppermute | solution.py:189
  76.2 27.2 %collective-permute-start.19 = (bf16[128,768]{1,0:T(8,128)(2,1)}, bf16[128,768]{1,0:T(8,128)(2,1)}, u32[]{:S(2)}, u32[]{:S(2)}) collective-permute-start(bf16[128,768]{1,0:T(8,128)(2,1)} %copy-done.15), channel_id=1, source_target_pairs={{0,8},{4,12},{8,0},{12,4},{16,24},{20,28},{24,16},{28,20},{1,9},{5... | collective-permute-start | bytes 589832 | tf_op jit(solution)/shard_map/ppermute | solution.py:189
  77.1 28.3 %collective-permute-start.21 = (bf16[128,768]{1,0:T(8,128)(2,1)}, bf16[128,768]{1,0:T(8,128)(2,1)}, u32[]{:S(2)}, u32[]{:S(2)}) collective-permute-start(bf16[128,768]{1,0:T(8,128)(2,1)} %get-tuple-element.54.refs_0_), channel_id=1, source_target_pairs={{0,24},{4,28},{8,16},{12,20},{16,8},{20,12},{24,0},{28,4},{1,25},{... | collective-permute-start | bytes 589832 | tf_op jit(solution)/shard_map/ppermute | solution.py:189
  86.3 23.7 %collective-permute-start.20 = (bf16[128,768]{1,0:T(8,128)(2,1)}, bf16[128,768]{1,0:T(8,128)(2,1)}, u32[]{:S(2)}, u32[]{:S(2)}) collective-permute-start(bf16[128,768]{1,0:T(8,128)(2,1)} %get-tuple-element.54.refs_0_), channel_id=1, source_target_pairs={{0,16},{4,20},{8,24},{12,28},{16,0},{20,4},{24,8},{28,12},{1,17},{... | collective-permute-start | bytes 589832 | tf_op jit(solution)/shard_map/ppermute | solution.py:189
  119.1 9.8 %collective-permute-start.23 = (bf16[128,1280]{1,0:T(8,128)(2,1)S(1)}, bf16[128,1280]{1,0:T(8,128)(2,1)S(1)}, u32[]{:S(2)}, u32[]{:S(2)}) collective-permute-start(bf16[128,1280]{1,0:T(8,128)(2,1)S(1)} %add_convert_fusion.4), channel_id=1, source_target_pairs={{0,2},{1,3},{2,0},{3,1},{4,6},{5,7},{6,4},{7,5},{8,10},{9,11},{10,... | collective-permute-start | bytes 983048 | tf_op jit(solution)/shard_map/ppermute | solution.py:197
  119.6 9.7 %collective-permute-start.26 = (bf16[128,768]{1,0:T(8,128)(2,1)S(1)}, bf16[128,768]{1,0:T(8,128)(2,1)S(1)}, u32[]{:S(2)}, u32[]{:S(2)}) collective-permute-start(bf16[128,768]{1,0:T(8,128)(2,1)S(1)} %get-tuple-element.58.refs_0_), channel_id=1, source_target_pairs={{0,24},{4,28},{8,16},{12,20},{16,8},{20,12},{24,0},{28,4},{1,25},{... | collective-permute-start | bytes 589832 | tf_op jit(solution)/shard_map/ppermute | solution.py:189
  121.9 15.9 %collective-permute-start.25 = (bf16[128,768]{1,0:T(8,128)(2,1)S(1)}, bf16[128,768]{1,0:T(8,128)(2,1)S(1)}, u32[]{:S(2)}, u32[]{:S(2)}) collective-permute-start(bf16[128,768]{1,0:T(8,128)(2,1)S(1)} %get-tuple-element.58.refs_0_), channel_id=1, source_target_pairs={{0,16},{4,20},{8,24},{12,28},{16,0},{20,4},{24,8},{28,12},{1,17},{... | collective-permute-start | bytes 589832 | tf_op jit(solution)/shard_map/ppermute | solution.py:189
  121.9 15.9 %collective-permute-start.24 = (bf16[128,768]{1,0:T(8,128)(2,1)S(1)}, bf16[128,768]{1,0:T(8,128)(2,1)S(1)}, u32[]{:S(2)}, u32[]{:S(2)}) collective-permute-start(bf16[128,768]{1,0:T(8,128)(2,1)S(1)} %get-tuple-element.58.refs_0_), channel_id=1, source_target_pairs={{0,8},{4,12},{8,0},{12,4},{16,24},{20,28},{24,16},{28,20},{1,9},{5... | collective-permute-start | bytes 589832 | tf_op jit(solution)/shard_map/ppermute | solution.py:189
  140.2 8.5 %collective-permute-start.27 = (bf16[256,1280]{1,0:T(8,128)(2,1)S(1)}, bf16[256,1280]{1,0:T(8,128)(2,1)S(1)}, u32[]{:S(2)}, u32[]{:S(2)}) collective-permute-start(bf16[256,1280]{1,0:T(8,128)(2,1)S(1)} %get-tuple-element.60), channel_id=1, source_target_pairs={{0,1},{1,0},{2,3},{3,2},{4,5},{5,4},{6,7},{7,6},{8,9},{9,8},{10,11... | collective-permute-start | bytes 1966088 | tf_op jit(solution)/shard_map/ppermute | solution.py:197
  141.7 24.2 %collective-permute-start.35 = (bf16[640,768]{1,0:T(8,128)(2,1)S(1)}, bf16[640,768]{1,0:T(8,128)(2,1)S(1)}, u32[]{:S(2)}, u32[]{:S(2)}) collective-permute-start(bf16[640,768]{1,0:T(8,128)(2,1)S(1)} %add_convert_fusion), channel_id=1, source_target_pairs={{0,4},{4,0},{8,12},{12,8},{16,20},{20,16},{24,28},{28,24},{1,5},{5... | collective-permute-start | bytes 2949128 | tf_op jit(solution)/shard_map/ppermute | solution.py:193
  143.3 24.7 %collective-permute-start.33 = (bf16[32,1280]{1,0:T(8,128)(2,1)S(1)}, bf16[32,1280]{1,0:T(8,128)(2,1)S(1)}, u32[]{:S(2)}, u32[]{:S(2)}) collective-permute-start(bf16[32,1280]{1,0:T(8,128)(2,1)S(1)} %get-tuple-element.88), channel_id=1, source_target_pairs={{0,24},{4,28},{8,16},{12,20},{16,8},{20,12},{24,0},{28,4},{1,25},{... | collective-permute-start | bytes 245768 | tf_op jit(solution)/shard_map/ppermute | solution.py:189
  145.0 27.3 %collective-permute-start.31 = (bf16[32,1280]{1,0:T(8,128)(2,1)S(1)}, bf16[32,1280]{1,0:T(8,128)(2,1)S(1)}, u32[]{:S(2)}, u32[]{:S(2)}) collective-permute-start(bf16[32,1280]{1,0:T(8,128)(2,1)S(1)} %get-tuple-element.89), channel_id=1, source_target_pairs={{0,16},{4,20},{8,24},{12,28},{16,0},{20,4},{24,8},{28,12},{1,17},{... | collective-permute-start | bytes 245768 | tf_op jit(solution)/shard_map/ppermute | solution.py:189
  145.0 27.3 %collective-permute-start.29 = (bf16[32,1280]{1,0:T(8,128)(2,1)S(1)}, bf16[32,1280]{1,0:T(8,128)(2,1)S(1)}, u32[]{:S(2)}, u32[]{:S(2)}) collective-permute-start(bf16[32,1280]{1,0:T(8,128)(2,1)S(1)} %get-tuple-element.90), channel_id=1, source_target_pairs={{0,8},{4,12},{8,0},{12,4},{16,24},{20,28},{24,16},{28,20},{1,9},{5... | collective-permute-start | bytes 245768 | tf_op jit(solution)/shard_map/ppermute | solution.py:189
  148.7 17.5 %collective-permute-start.28 = (bf16[128,1280]{1,0:T(8,128)(2,1)S(1)}, bf16[128,1280]{1,0:T(8,128)(2,1)S(1)}, u32[]{:S(2)}, u32[]{:S(2)}) collective-permute-start(bf16[128,1280]{1,0:T(8,128)(2,1)S(1)} %add_convert_fusion.2), channel_id=1, source_target_pairs={{0,2},{1,3},{2,0},{3,1},{4,6},{5,7},{6,4},{7,5},{8,10},{9,11},{10,... | collective-permute-start | bytes 983048 | tf_op jit(solution)/shard_map/ppermute | solution.py:197
  166.4 7.3 %collective-permute-start.34 = (bf16[32,1280]{1,0:T(8,128)(2,1)S(1)}, bf16[32,1280]{1,0:T(8,128)(2,1)S(1)}, u32[]{:S(2)}, u32[]{:S(2)}) collective-permute-start(bf16[32,1280]{1,0:T(8,128)(2,1)S(1)} %get-tuple-element.84), channel_id=1, source_target_pairs={{0,24},{4,28},{8,16},{12,20},{16,8},{20,12},{24,0},{28,4},{1,25},{... | collective-permute-start | bytes 245768 | tf_op jit(solution)/shard_map/ppermute | solution.py:189
  168.1 7.8 %collective-permute-start.32 = (bf16[32,1280]{1,0:T(8,128)(2,1)S(1)}, bf16[32,1280]{1,0:T(8,128)(2,1)S(1)}, u32[]{:S(2)}, u32[]{:S(2)}) collective-permute-start(bf16[32,1280]{1,0:T(8,128)(2,1)S(1)} %get-tuple-element.85), channel_id=1, source_target_pairs={{0,16},{4,20},{8,24},{12,28},{16,0},{20,4},{24,8},{28,12},{1,17},{... | collective-permute-start | bytes 245768 | tf_op jit(solution)/shard_map/ppermute | solution.py:189
  168.1 7.8 %collective-permute-start.30 = (bf16[32,1280]{1,0:T(8,128)(2,1)S(1)}, bf16[32,1280]{1,0:T(8,128)(2,1)S(1)}, u32[]{:S(2)}, u32[]{:S(2)}) collective-permute-start(bf16[32,1280]{1,0:T(8,128)(2,1)S(1)} %get-tuple-element.86), channel_id=1, source_target_pairs={{0,8},{4,12},{8,0},{12,4},{16,24},{20,28},{24,16},{28,20},{1,9},{5... | collective-permute-start | bytes 245768 | tf_op jit(solution)/shard_map/ppermute | solution.py:189
  (28 other events, 183.4 us)

commit v5 on v2

--- a/solution.py
+++ b/solution.py
@@ -98,6 +98,9 @@
 
     far_first = sorted(range(1, outer), key=lambda k: -k)
     near_first = sorted(range(1, outer))
+    keys = [0] + near_first
+    outer_groups = [[i * inner + j for i in range(outer)] for j in range(inner)]
+    inner_groups = [[i * inner + j for j in range(inner)] for i in range(outer)]
 
     def shards(tokens, slots, gate_probs, w_gate, w_up, d_hidden):
         dp = lax.axis_index("dp")
@@ -107,23 +110,15 @@
         cap = slots.shape[0]
         tok = tokens.shape[0]
         span = depth * inner
+        each = cap * etp_size
 
-        weights = [jnp.concatenate([w_gate, w_up], axis=1)]
-        for j in range(1, inner):
-            weights.append(jnp.concatenate([over_inner(w_gate, j), over_inner(w_up, j)], axis=1))
-        weights = jnp.concatenate(weights, axis=0)
+        weights = jnp.concatenate([w_gate, w_up], axis=1)
+        if inner > 1:
+            weights = lax.all_gather(weights, "dp", axis_index_groups=inner_groups, axis=0, tiled=True)
 
         onehot = (slots[:, None] == jnp.arange(tok, dtype=slots.dtype)[None, :]).astype(BF16)
         rows = jnp.dot(onehot, tokens, preferred_element_type=F32).astype(BF16)
-        pieces = {}
-        for k in far_first + [0]:
-            pieces[k] = jnp.concatenate(
-                [
-                    lax.dynamic_slice(rows, (0, (a ^ k) * span + (b ^ j) * depth), (cap, depth))
-                    for j in range(inner)
-                ],
-                axis=1,
-            )
+        pieces = {k: lax.dynamic_slice(rows, (0, (a ^ k) * span), (cap, span)) for k in far_first + [0]}
         got = {k: over_outer(pieces[k], k) for k in far_first}
         x_chunks = {k: gather_etp(got[k]) for k in far_first}
         x_chunks[0] = gather_etp(after(pieces[0], got[near_first[0]]))
@@ -135,41 +130,43 @@
         }
         pre = jnp.dot(x_chunks[0], weights, preferred_element_type=F32)
         order = etp ^ jnp.array(chunk_order, jnp.int32)
+        x_all = jnp.zeros((outer * each, span), BF16)
+        for k in keys:
+            x_all = lax.dynamic_update_slice(x_all, x_chunks[k], ((a ^ k) * each, 0))
         hidden, paired = gate_call(
-            order, pre, probs[:, None], d_hidden, [parts[k] for k in near_first]
+            order, pre, after(probs, x_all)[:, None], d_hidden, [parts[k] for k in near_first]
         )
+        grads = lax.all_gather(paired, "dp", axis_index_groups=outer_groups, axis=0, tiled=True)
 
-        grads = {k: over_outer(paired, k) for k in far_first}
-        grads[0] = paired
+        def weight_grad(j):
+            x_part = lax.dynamic_slice(x_all, (0, (b ^ j) * depth), (outer * each, depth))
+            return lax.dot_general(
+                x_part, grads, (((0,), (0,)), ((), ())), preferred_element_type=F32
+            )
+
+        leaving = [weight_grad(j).astype(BF16) for j in range(1, inner)]
+        arriving = [over_inner(leaving[j - 1], j) for j in range(1, inner)]
 
         dx = jnp.zeros((cap, outer * span), BF16)
-        last = paired
-        for k in [0] + near_first:
+        last = leaving[0] if inner > 1 else grads
+        for k in far_first + [0]:
+            block = lax.dynamic_slice(after(grads, last), ((a ^ k) * each, 0), (each, 2 * width))
             partial = lax.dot_general(
-                after(grads[k], last), weights, (((1,), (1,)), ((), ())), preferred_element_type=F32
+                block, weights, (((1,), (1,)), ((), ())), preferred_element_type=F32
             )
             last = partial
             own = reduce_etp(partial).astype(BF16)
             own = over_outer(own, k) if k else own
-            for j in range(inner):
-                block = own[:, j * depth : (j + 1) * depth]
-                dx = lax.dynamic_update_slice(dx, block, (0, (a ^ k) * span + (b ^ j) * depth))
+            dx = lax.dynamic_update_slice(dx, own, (0, (a ^ k) * span))
         grad_tokens = lax.dot_general(
             onehot, dx, (((0,), (0,)), ((), ())), preferred_element_type=F32
         ).astype(BF16)
-
-        keys = [0] + near_first
-        summed = lax.dot_general(
-            jnp.concatenate([x_chunks[k] for k in keys], axis=0),
-            after(jnp.concatenate([grads[k] for k in keys], axis=0), last),
-            (((0,), (0,)), ((), ())),
-            preferred_element_type=F32,
-        )
-        total = summed[:depth]
-        for j in range(1, inner):
-            part = summed[j * depth : (j + 1) * depth]
-            total = total + over_inner(part.astype(BF16), j).astype(F32)
-        return (hidden, grad_tokens, total[:, :width], total[:, width:])
+        total = after(weight_grad(0), last)
+        gate_total, up_total = total[:, :width], total[:, width:]
+        for part in arriving:
+            gate_total = gate_total + part[:, :width].astype(F32)
+            up_total = up_total + part[:, width:].astype(F32)
+        return (hidden, grad_tokens, gate_total, up_total)
 
     return shards
 

time: 146 us -> 196 us (1.34)
  waiting for transfers between devices: 83.1 us -> 114 us
  between operations: 1.18 us -> 14.7 us
  starting transfers between devices: 39.6 us -> 26.1 us
  matrix products: 15.4 us -> 24.9 us
  local copies, waits for them, and re-layouts: 2.38 us -> 10.1 us
  other arithmetic: 1.13 us -> 4.09 us
    all_gather x0 -> x2, waiting for transfers between devices: none -> 49.5 us  [the longest x1 42.4 us: shards(): lax.all_gather(paired, 'dp', axis_index_groups=outer_groups, axis=0, tile...]
    ppermute x12 -> x9, waiting for transfers between devices: 65.7 us -> 48.3 us  [over_outer(): return lax.ppermute(value, 'dp', pairs)]
    ppermute x12 -> x9, starting transfers between devices: 21.5 us -> 12.9 us  [over_outer(): return lax.ppermute(value, 'dp', pairs)]
    dot_general x5 -> x6, matrix products: 5.16 us -> 11.8 us  [the longest x2 6.81 us: weight_grad(): lax.dot_general(x_part, grads, (((0,), (0,)), ((), ())), preferred_elemen...]
    dynamic_update_slice x8 -> x7, local copies, waits for them, and re-layouts: 0.15 us -> 3.56 us  [the longest x4 3.51 us: shards(): x_all = lax.dynamic_update_slice(x_all, x_chunks[k], ((a ^ k) * each, 0))]
    ppermute x3 -> x1, starting transfers between devices: 4.66 us -> 1.48 us  [over_inner(): return lax.ppermute(value, 'dp', pairs)]
    slice x8, local copies, waits for them, and re-layouts: 0.23 us -> 3.12 us  [reduce_etp(): sent = over_etp(value[half:].astype(BF16), b)]
    dot_general x3, matrix products: 2.03 us -> 4.8 us  [shards(): jnp.dot(x_chunks[k], weights, preferred_element_type=F32).astype(BF16)]
  transfers between devices with their start and end apart: 33 -> 30, of which waited for: 15 -> 12; matrix products, arithmetic and copies ran while one was open for 11% -> 12% of each run, Pallas kernels for 0% -> 0%
where the time goes in v5:
time: 196 us
  waiting for transfers between devices  114 us (58%)
  starting transfers between devices  26.1 us (13%)
  matrix products  24.9 us (13%)
  between operations  14.7 us (8%)
  local copies, waits for them, and re-layouts  10.1 us (5%)
  other arithmetic  4.09 us (2%)
    ppermute x9, waiting for transfers between devices, over_outer(): return lax.ppermute(value, 'dp', pairs)  48.3 us
    all_gather x1, waiting for transfers between devices, shards(): lax.all_gather(paired, 'dp', axis_index_groups=outer_groups, axis=0, tile...  42.4 us
    ppermute x18, waiting for transfers between devices, over_etp(): return lax.ppermute(value, 'etp', pairs)  16.1 us
    ppermute x9, starting transfers between devices, over_outer(): return lax.ppermute(value, 'dp', pairs)  12.9 us
    ppermute x18, starting transfers between devices, over_etp(): return lax.ppermute(value, 'etp', pairs)  11.7 us
    all_gather x1, waiting for transfers between devices, shards(): lax.all_gather(weights, 'dp', axis_index_groups=inner_groups, axis=0, til...  7.14 us
    dot_general x2, matrix products, weight_grad(): lax.dot_general(x_part, grads, (((0,), (0,)), ((), ())), preferred_elemen...  6.81 us
    dot_general x4, matrix products, shards(): lax.dot_general(block, weights, (((1,), (1,)), ((), ())), preferred_eleme...  4.98 us
  transfers between devices with their start and end apart: 30, of which 12 were waited for; matrix products, arithmetic and copies ran while one was open for 12% of the time, Pallas kernels for 0%

profile of v5, /device:TPU:0, one launch (start us, length us, event | category | flops | bytes accessed | tf_op | source)
XLA Modules:
  0.0 195.7 jit_solution(12954290669388594255)
XLA Ops:
  7.3 3.7 %convolution_convert_fusion.1 = bf16[64,5120]{1,0:T(8,128)(2,1)S(1)} fusion(bf16[512,5120]{1,0:T(8,128)(2,1)} %param.7, s32[64]{0:T(128)} %param.8), kind=kOutput, calls=%fused_computation.1 | convolution fusion | flops 335904768 | bytes 5898496 | tf_op jit(solution)/shard_map/dot_general | solution.py:120
  11.0 3.1 %collective-permute-start = (bf16[64,1280]{1,0:T(8,128)(2,1)S(1)}, bf16[64,1280]{1,0:T(8,128)(2,1)S(1)}, u32[]{:S(2)}, u32[]{:S(2)}) collective-permute-start(bf16[64,1280]{1,0:T(8,128)(2,1)S(1)} %get-tuple-element.28), channel_id=1, source_target_pairs={{0,8},{4,12},{8,0},{12,4},{16,24},{20,28},{24,16},{28,20},{1,9},{5... | collective-permute-start | bytes 491528 | tf_op jit(solution)/shard_map/ppermute | solution.py:69
  14.1 2.6 %collective-permute-start.7 = (bf16[64,1280]{1,0:T(8,128)(2,1)S(1)}, bf16[64,1280]{1,0:T(8,128)(2,1)S(1)}, u32[]{:S(2)}, u32[]{:S(2)}) collective-permute-start(bf16[64,1280]{1,0:T(8,128)(2,1)S(1)} %get-tuple-element.27), channel_id=1, source_target_pairs={{0,16},{4,20},{8,24},{12,28},{16,0},{20,4},{24,8},{28,12},{1,17},{... | collective-permute-start | bytes 491528 | tf_op jit(solution)/shard_map/ppermute | solution.py:69
  17.9 2.9 %collective-permute-done = bf16[64,1280]{1,0:T(8,128)(2,1)S(1)} collective-permute-done((bf16[64,1280]{1,0:T(8,128)(2,1)S(1)}, bf16[64,1280]{1,0:T(8,128)(2,1)S(1)}, u32[]{:S(2)}, u32[]{:S(2)}) %collective-permute-start) | collective-permute-done | bytes 163872 | tf_op jit(solution)/shard_map/ppermute | solution.py:69
  20.8 1.7 collective-permute-start.1
  22.9 6.3 %collective-permute-done.7 = bf16[64,1280]{1,0:T(8,128)(2,1)S(1)} collective-permute-done((bf16[64,1280]{1,0:T(8,128)(2,1)S(1)}, bf16[64,1280]{1,0:T(8,128)(2,1)S(1)}, u32[]{:S(2)}, u32[]{:S(2)}) %collective-permute-start.7) | collective-permute-done | bytes 163872 | tf_op jit(solution)/shard_map/ppermute | solution.py:69
  29.2 1.5 collective-permute-start.8
  32.0 2.6 %collective-permute-done.8 = bf16[64,1280]{1,0:T(8,128)(2,1)S(1)} collective-permute-done((bf16[64,1280]{1,0:T(8,128)(2,1)S(1)}, bf16[64,1280]{1,0:T(8,128)(2,1)S(1)}, u32[]{:S(2)}, u32[]{:S(2)}) %collective-permute-start.8) | collective-permute-done | bytes 163872 | tf_op jit(solution)/shard_map/ppermute | solution.py:77
  34.8 1.7 collective-permute-done.11
  38.2 1.9 broadcast_in_dim.11
  43.9 7.1 %all-gather.3.cloned.1.call-done = bf16[1280,768]{1,0:T(8,128)(2,1)} async-done(((bf16[640,768]{1,0:T(8,128)(2,1)}), bf16[1280,768]{1,0:T(8,128)(2,1)}) %all-gather.3.cloned.1.call-update) | async-done | bytes 1966096 | tf_op jit(solution)/shard_map/all_gather | solution.py:117
  51.0 2.4 %convolution_convert_fusion.5 = bf16[256,768]{1,0:T(8,128)(2,1)S(1)} fusion(bf16[256,1280]{1,0:T(8,128)(2,1)S(1)} %constant_dynamic-update-slice_fusion.3, bf16[1280,768]{1,0:T(8,128)(2,1)} %all-gather.3.cloned.1.call-done), kind=kOutput, calls=%fused_computation.8 | convolution fusion | flops 503513088 | bytes 3014656 | tf_op jit(solution)/shard_map/dot_general | solution.py:128
  53.4 1.6 collective-permute-start.13
  55.0 1.8 convolution_convert_fusion.4
  56.7 2.5 %collective-permute-start.14 = (bf16[256,768]{1,0:T(8,128)(2,1)S(1)}, bf16[256,768]{1,0:T(8,128)(2,1)S(1)}, u32[]{:S(2)}, u32[]{:S(2)}) collective-permute-start(bf16[256,768]{1,0:T(8,128)(2,1)S(1)} %convolution_convert_fusion.4), channel_id=1, source_target_pairs={{0,16},{4,20},{8,24},{12,28},{16,0},{20,4},{24,8},{28,12},{1,17},{... | collective-permute-start | bytes 1179656 | tf_op jit(solution)/shard_map/ppermute | solution.py:69
  61.3 9.4 %collective-permute-done.13.refs_0_ = bf16[256,768]{1,0:T(8,128)(2,1)S(1)} collective-permute-done((bf16[256,768]{1,0:T(8,128)(2,1)S(1)}, bf16[256,768]{1,0:T(8,128)(2,1)S(1)}, u32[]{:S(2)}, u32[]{:S(2)}) %collective-permute-start.13) | collective-permute-done | bytes 393248 | tf_op jit(solution)/shard_map/ppermute | solution.py:69
  70.7 15.9 %collective-permute-done.14.refs_1_ = bf16[256,768]{1,0:T(8,128)(2,1)S(1)} collective-permute-done((bf16[256,768]{1,0:T(8,128)(2,1)S(1)}, bf16[256,768]{1,0:T(8,128)(2,1)S(1)}, u32[]{:S(2)}, u32[]{:S(2)}) %collective-permute-start.14) | collective-permute-done | bytes 393248 | tf_op jit(solution)/shard_map/ppermute | solution.py:69
  86.6 1.8 shard_map.102
  88.4 42.4 %all-gather.5.cloned.1.call-done = bf16[1024,768]{1,0:T(8,128)(2,1)} async-done(((bf16[256,768]{1,0:T(8,128)(2,1)}), bf16[1024,768]{1,0:T(8,128)(2,1)}) %all-gather.5.cloned.1.call-update) | async-done | bytes 1572880 | tf_op jit(solution)/shard_map/all_gather | solution.py:139
  130.8 4.1 %convolution_convert_fusion.2 = bf16[640,768]{1,0:T(8,128)(2,1)} fusion(bf16[1024,768]{1,0:T(8,128)(2,1)} %all-gather.5.cloned.1.call-done, bf16[1024,1280]{1,0:T(8,128)(2,1)} %constant_dynamic-update-slice_fusion.15, s32[]{:T(128)S(6)} %select_n.59), kind=kOutput, calls=%fused_computation.2 | convolution fusion | flops 1007124480 | bytes 3866628 | tf_op jit(solution)/shard_map/dot_general | solution.py:143
  135.6 1.8 fusion.7
  137.4 1.8 fusion.5
  141.8 1.5 collective-permute-start.27
  145.6 2.7 %fusion = f32[640,768]{1,0:T(8,128)S(1)} fusion(bf16[1024,768]{1,0:T(8,128)(2,1)S(1)} %copy-done.7, bf16[1024,1280]{1,0:T(8,128)(2,1)} %constant_dynamic-update-slice_fusion.15, s32[]{:T(128)S(6)} %select_n.60), kind=kOutput, calls=%fused_computation.3 | convolution fusion | flops 1006632960 | bytes 4849668 | tf_op jit(solution)/shard_map/dot_general | solution.py:143
  150.2 1.5 collective-permute-start.26
  152.5 1.5 collective-permute-start.20
  154.8 6.0 %collective-permute-done.23 = bf16[64,1280]{1,0:T(8,128)(2,1)S(1)} collective-permute-done((bf16[64,1280]{1,0:T(8,128)(2,1)S(1)}, bf16[64,1280]{1,0:T(8,128)(2,1)S(1)}, u32[]{:S(2)}, u32[]{:S(2)}) %collective-permute-start.23) | collective-permute-done | bytes 163872 | tf_op jit(solution)/shard_map/ppermute | solution.py:77
  161.4 5.8 %collective-permute-done.17 = bf16[64,1280]{1,0:T(8,128)(2,1)S(1)} collective-permute-done((bf16[64,1280]{1,0:T(8,128)(2,1)S(1)}, bf16[64,1280]{1,0:T(8,128)(2,1)S(1)}, u32[]{:S(2)}, u32[]{:S(2)}) %collective-permute-start.17) | collective-permute-done | bytes 163872 | tf_op jit(solution)/shard_map/ppermute | solution.py:77
  169.3 7.0 %collective-permute-done.18 = bf16[64,1280]{1,0:T(8,128)(2,1)S(1)} collective-permute-done((bf16[64,1280]{1,0:T(8,128)(2,1)S(1)}, bf16[64,1280]{1,0:T(8,128)(2,1)S(1)}, u32[]{:S(2)}, u32[]{:S(2)}) %collective-permute-start.18) | collective-permute-done | bytes 163872 | tf_op jit(solution)/shard_map/ppermute | solution.py:69
  176.3 6.9 %collective-permute-done.21 = bf16[64,1280]{1,0:T(8,128)(2,1)S(1)} collective-permute-done((bf16[64,1280]{1,0:T(8,128)(2,1)S(1)}, bf16[64,1280]{1,0:T(8,128)(2,1)S(1)}, u32[]{:S(2)}, u32[]{:S(2)}) %collective-permute-start.21) | collective-permute-done | bytes 163872 | tf_op jit(solution)/shard_map/ppermute | solution.py:69
  183.4 4.0 %convolution_convert_fusion = bf16[512,5120]{1,0:T(8,128)(2,1)} fusion(bf16[64,5120]{1,0:T(8,128)(2,1)S(1)} %fusion.15, s32[64]{0:T(128)S(1)} %copy-done.13), kind=kOutput, calls=%fused_computation | convolution fusion | flops 338198528 | bytes 5898496 | tf_op jit(solution)/shard_map/dot_general | solution.py:161
  187.4 1.4 convert_add_fusion
  (123 shorter events, 22.3 us)
Async XLA Ops:
  7.2 43.9 %all-gather.3.cloned.1.call-start = ((), (), s32[]{:S(2)}) async-start(), calls=%async_computation | async-start | bytes 2949120 | tf_op jit(solution)/shard_map/all_gather | solution.py:117
  11.0 9.8 %collective-permute-start = (bf16[64,1280]{1,0:T(8,128)(2,1)S(1)}, bf16[64,1280]{1,0:T(8,128)(2,1)S(1)}, u32[]{:S(2)}, u32[]{:S(2)}) collective-permute-start(bf16[64,1280]{1,0:T(8,128)(2,1)S(1)} %get-tuple-element.28), channel_id=1, source_target_pairs={{0,8},{4,12},{8,0},{12,4},{16,24},{20,28},{24,16},{28,20},{1,9},{5... | collective-permute-start | bytes 491528 | tf_op jit(solution)/shard_map/ppermute | solution.py:69
  14.1 15.0 %collective-permute-start.7 = (bf16[64,1280]{1,0:T(8,128)(2,1)S(1)}, bf16[64,1280]{1,0:T(8,128)(2,1)S(1)}, u32[]{:S(2)}, u32[]{:S(2)}) collective-permute-start(bf16[64,1280]{1,0:T(8,128)(2,1)S(1)} %get-tuple-element.27), channel_id=1, source_target_pairs={{0,16},{4,20},{8,24},{12,28},{16,0},{20,4},{24,8},{28,12},{1,17},{... | collective-permute-start | bytes 491528 | tf_op jit(solution)/shard_map/ppermute | solution.py:69
  16.7 14.0 %collective-permute-start.10 = (bf16[64,1280]{1,0:T(8,128)(2,1)S(1)}, bf16[64,1280]{1,0:T(8,128)(2,1)S(1)}, u32[]{:S(2)}, u32[]{:S(2)}) collective-permute-start(bf16[64,1280]{1,0:T(8,128)(2,1)S(1)} %get-tuple-element.26), channel_id=1, source_target_pairs={{0,24},{4,28},{8,16},{12,20},{16,8},{20,12},{24,0},{28,4},{1,25},{... | collective-permute-start | bytes 491528 | tf_op jit(solution)/shard_map/ppermute | solution.py:69
  17.8 113.0 %all-gather.5.cloned.1.call-start = ((), (), s32[]{:S(2)}) async-start(), calls=%async_computation.1 | async-start | bytes 1966080 | tf_op jit(solution)/shard_map/all_gather | solution.py:139
  20.8 10.5 %collective-permute-start.1 = (bf16[64,1280]{1,0:T(8,128)(2,1)S(1)}, bf16[64,1280]{1,0:T(8,128)(2,1)S(1)}, u32[]{:S(2)}, u32[]{:S(2)}) collective-permute-start(bf16[64,1280]{1,0:T(8,128)(2,1)S(1)} %get-tuple-element.14), channel_id=1, source_target_pairs={{0,2},{1,3},{2,0},{3,1},{4,6},{5,7},{6,4},{7,5},{8,10},{9,11},{10,... | collective-permute-start | bytes 491528 | tf_op jit(solution)/shard_map/ppermute | solution.py:77
  22.5 8.9 %collective-permute-start.5 = (bf16[64,1280]{1,0:T(8,128)(2,1)S(1)}, bf16[64,1280]{1,0:T(8,128)(2,1)S(1)}, u32[]{:S(2)}, u32[]{:S(2)}) collective-permute-start(bf16[64,1280]{1,0:T(8,128)(2,1)S(1)} %collective-permute-done), channel_id=1, source_target_pairs={{0,2},{1,3},{2,0},{3,1},{4,6},{5,7},{6,4},{7,5},{8,10},{9,11},{10,... | collective-permute-start | bytes 491528 | tf_op jit(solution)/shard_map/ppermute | solution.py:77
  29.2 5.5 %collective-permute-start.8 = (bf16[64,1280]{1,0:T(8,128)(2,1)S(1)}, bf16[64,1280]{1,0:T(8,128)(2,1)S(1)}, u32[]{:S(2)}, u32[]{:S(2)}) collective-permute-start(bf16[64,1280]{1,0:T(8,128)(2,1)S(1)} %collective-permute-done.7), channel_id=1, source_target_pairs={{0,2},{1,3},{2,0},{3,1},{4,6},{5,7},{6,4},{7,5},{8,10},{9,11},{10,... | collective-permute-start | bytes 491528 | tf_op jit(solution)/shard_map/ppermute | solution.py:77
  30.7 5.7 %collective-permute-start.11 = (bf16[64,1280]{1,0:T(8,128)(2,1)S(1)}, bf16[64,1280]{1,0:T(8,128)(2,1)S(1)}, u32[]{:S(2)}, u32[]{:S(2)}) collective-permute-start(bf16[64,1280]{1,0:T(8,128)(2,1)S(1)} %collective-permute-done.10), channel_id=1, source_target_pairs={{0,2},{1,3},{2,0},{3,1},{4,6},{5,7},{6,4},{7,5},{8,10},{9,11},{10,... | collective-permute-start | bytes 491528 | tf_op jit(solution)/shard_map/ppermute | solution.py:77
  31.3 5.3 %collective-permute-start.2 = (bf16[128,1280]{1,0:T(8,128)(2,1)S(1)}, bf16[128,1280]{1,0:T(8,128)(2,1)S(1)}, u32[]{:S(2)}, u32[]{:S(2)}) collective-permute-start(bf16[128,1280]{1,0:T(8,128)(2,1)S(1)} %pad_maximum_fusion.1), channel_id=1, source_target_pairs={{0,1},{1,0},{2,3},{3,2},{4,5},{5,4},{6,7},{7,6},{8,9},{9,8},{10,11... | collective-permute-start | bytes 983048 | tf_op jit(solution)/shard_map/ppermute | solution.py:77
  31.5 6.6 %collective-permute-start.6 = (bf16[128,1280]{1,0:T(8,128)(2,1)S(1)}, bf16[128,1280]{1,0:T(8,128)(2,1)S(1)}, u32[]{:S(2)}, u32[]{:S(2)}) collective-permute-start(bf16[128,1280]{1,0:T(8,128)(2,1)S(1)} %pad_maximum_fusion.2), channel_id=1, source_target_pairs={{0,1},{1,0},{2,3},{3,2},{4,5},{5,4},{6,7},{7,6},{8,9},{9,8},{10,11... | collective-permute-start | bytes 983048 | tf_op jit(solution)/shard_map/ppermute | solution.py:77
  34.7 3.4 %collective-permute-start.9 = (bf16[128,1280]{1,0:T(8,128)(2,1)S(1)}, bf16[128,1280]{1,0:T(8,128)(2,1)S(1)}, u32[]{:S(2)}, u32[]{:S(2)}) collective-permute-start(bf16[128,1280]{1,0:T(8,128)(2,1)S(1)} %pad_maximum_fusion.3), channel_id=1, source_target_pairs={{0,1},{1,0},{2,3},{3,2},{4,5},{5,4},{6,7},{7,6},{8,9},{9,8},{10,11... | collective-permute-start | bytes 983048 | tf_op jit(solution)/shard_map/ppermute | solution.py:77
  36.4 1.7 collective-permute-start.12
  36.7 6.9 %collective-permute-start.3 = (bf16[64]{0:T(256)(128)(2,1)S(1)}, bf16[64]{0:T(256)(128)(2,1)S(1)}, u32[]{:S(2)}, u32[]{:S(2)}) collective-permute-start(bf16[64]{0:T(256)(128)(2,1)S(1)} %copy-done.14), channel_id=1, source_target_pairs={{0,2},{1,3},{2,0},{3,1},{4,6},{5,7},{6,4},{7,5},{8,10},{9,11},{10,... | collective-permute-start | bytes 392 | tf_op jit(solution)/shard_map/ppermute | solution.py:77
  43.7 16.8 %collective-permute-start.4 = (bf16[128]{0:T(256)(128)(2,1)S(1)}, bf16[128]{0:T(256)(128)(2,1)S(1)}, u32[]{:S(2)}, u32[]{:S(2)}) collective-permute-start(bf16[128]{0:T(256)(128)(2,1)S(1)} %pad_maximum_fusion.5), channel_id=1, source_target_pairs={{0,1},{1,0},{2,3},{3,2},{4,5},{5,4},{6,7},{7,6},{8,9},{9,8},{10,11... | collective-permute-start | bytes 776 | tf_op jit(solution)/shard_map/ppermute | solution.py:77
  53.4 17.3 %collective-permute-start.13 = (bf16[256,768]{1,0:T(8,128)(2,1)S(1)}, bf16[256,768]{1,0:T(8,128)(2,1)S(1)}, u32[]{:S(2)}, u32[]{:S(2)}) collective-permute-start(bf16[256,768]{1,0:T(8,128)(2,1)S(1)} %convolution_convert_fusion.5), channel_id=1, source_target_pairs={{0,8},{4,12},{8,0},{12,4},{16,24},{20,28},{24,16},{28,20},{1,9},{5... | collective-permute-start | bytes 1179656 | tf_op jit(solution)/shard_map/ppermute | solution.py:69
  56.7 29.9 %collective-permute-start.14 = (bf16[256,768]{1,0:T(8,128)(2,1)S(1)}, bf16[256,768]{1,0:T(8,128)(2,1)S(1)}, u32[]{:S(2)}, u32[]{:S(2)}) collective-permute-start(bf16[256,768]{1,0:T(8,128)(2,1)S(1)} %convolution_convert_fusion.4), channel_id=1, source_target_pairs={{0,16},{4,20},{8,24},{12,28},{16,0},{20,4},{24,8},{28,12},{1,17},{... | collective-permute-start | bytes 1179656 | tf_op jit(solution)/shard_map/ppermute | solution.py:69
  59.9 26.7 %copy-start = (bf16[256,384]{1,0:T(8,128)(2,1)S(1)}, bf16[256,384]{1,0:T(8,128)(2,1)}, u32[]{:S(2)}) copy-start(bf16[256,384]{1,0:T(8,128)(2,1)} %cot_ref.1) | copy-start | bytes 589828
  59.9 26.7 %collective-permute-start.15 = (bf16[256,768]{1,0:T(8,128)(2,1)S(1)}, bf16[256,768]{1,0:T(8,128)(2,1)S(1)}, u32[]{:S(2)}, u32[]{:S(2)}) collective-permute-start(bf16[256,768]{1,0:T(8,128)(2,1)S(1)} %convolution_convert_fusion.3), channel_id=1, source_target_pairs={{0,24},{4,28},{8,16},{12,20},{16,8},{20,12},{24,0},{28,4},{1,25},{... | collective-permute-start | bytes 1179656 | tf_op jit(solution)/shard_map/ppermute | solution.py:69
  141.8 7.3 %collective-permute-start.25 = (bf16[128,1280]{1,0:T(8,128)(2,1)}, bf16[128,1280]{1,0:T(8,128)(2,1)}, u32[]{:S(2)}, u32[]{:S(2)}) collective-permute-start(bf16[128,1280]{1,0:T(8,128)(2,1)} %slice.136), channel_id=1, source_target_pairs={{0,1},{1,0},{2,3},{3,2},{4,5},{5,4},{6,7},{7,6},{8,9},{9,8},{10,11... | collective-permute-start | bytes 983048 | tf_op jit(solution)/shard_map/ppermute | solution.py:77
  141.8 45.6 %collective-permute-start.27 = (bf16[640,768]{1,0:T(8,128)(2,1)}, bf16[640,768]{1,0:T(8,128)(2,1)S(1)}, u32[]{:S(2)}, u32[]{:S(2)}) collective-permute-start(bf16[640,768]{1,0:T(8,128)(2,1)} %convolution_convert_fusion.2), channel_id=1, source_target_pairs={{0,4},{4,0},{8,12},{12,8},{16,20},{20,16},{24,28},{28,24},{1,5},{5... | collective-permute-start | bytes 2949128 | tf_op jit(solution)/shard_map/ppermute | solution.py:73
  148.3 3.4 %collective-permute-start.22 = (bf16[128,1280]{1,0:T(8,128)(2,1)S(1)}, bf16[128,1280]{1,0:T(8,128)(2,1)S(1)}, u32[]{:S(2)}, u32[]{:S(2)}) collective-permute-start(bf16[128,1280]{1,0:T(8,128)(2,1)S(1)} %slice.137), channel_id=1, source_target_pairs={{0,1},{1,0},{2,3},{3,2},{4,5},{5,4},{6,7},{7,6},{8,9},{9,8},{10,11... | collective-permute-start | bytes 983048 | tf_op jit(solution)/shard_map/ppermute | solution.py:77
  148.6 3.9 %collective-permute-start.19 = (bf16[128,1280]{1,0:T(8,128)(2,1)S(1)}, bf16[128,1280]{1,0:T(8,128)(2,1)S(1)}, u32[]{:S(2)}, u32[]{:S(2)}) collective-permute-start(bf16[128,1280]{1,0:T(8,128)(2,1)S(1)} %slice.138), channel_id=1, source_target_pairs={{0,1},{1,0},{2,3},{3,2},{4,5},{5,4},{6,7},{7,6},{8,9},{9,8},{10,11... | collective-permute-start | bytes 983048 | tf_op jit(solution)/shard_map/ppermute | solution.py:77
  148.9 5.2 %collective-permute-start.16 = (bf16[128,1280]{1,0:T(8,128)(2,1)S(1)}, bf16[128,1280]{1,0:T(8,128)(2,1)S(1)}, u32[]{:S(2)}, u32[]{:S(2)}) collective-permute-start(bf16[128,1280]{1,0:T(8,128)(2,1)S(1)} %slice.139), channel_id=1, source_target_pairs={{0,1},{1,0},{2,3},{3,2},{4,5},{5,4},{6,7},{7,6},{8,9},{9,8},{10,11... | collective-permute-start | bytes 983048 | tf_op jit(solution)/shard_map/ppermute | solution.py:77
  150.2 33.2 %collective-permute-start.26 = (bf16[64,1280]{1,0:T(8,128)(2,1)S(1)}, bf16[64,1280]{1,0:T(8,128)(2,1)S(1)}, u32[]{:S(2)}, u32[]{:S(2)}) collective-permute-start(bf16[64,1280]{1,0:T(8,128)(2,1)S(1)} %slice.140), channel_id=1, source_target_pairs={{0,2},{1,3},{2,0},{3,1},{4,6},{5,7},{6,4},{7,5},{8,10},{9,11},{10,... | collective-permute-start | bytes 491528 | tf_op jit(solution)/shard_map/ppermute | solution.py:77
  151.8 9.0 %collective-permute-start.23 = (bf16[64,1280]{1,0:T(8,128)(2,1)S(1)}, bf16[64,1280]{1,0:T(8,128)(2,1)S(1)}, u32[]{:S(2)}, u32[]{:S(2)}) collective-permute-start(bf16[64,1280]{1,0:T(8,128)(2,1)S(1)} %slice.141), channel_id=1, source_target_pairs={{0,2},{1,3},{2,0},{3,1},{4,6},{5,7},{6,4},{7,5},{8,10},{9,11},{10,... | collective-permute-start | bytes 491528 | tf_op jit(solution)/shard_map/ppermute | solution.py:77
  152.5 16.0 %collective-permute-start.20 = (bf16[64,1280]{1,0:T(8,128)(2,1)S(1)}, bf16[64,1280]{1,0:T(8,128)(2,1)S(1)}, u32[]{:S(2)}, u32[]{:S(2)}) collective-permute-start(bf16[64,1280]{1,0:T(8,128)(2,1)S(1)} %slice.142), channel_id=1, source_target_pairs={{0,2},{1,3},{2,0},{3,1},{4,6},{5,7},{6,4},{7,5},{8,10},{9,11},{10,... | collective-permute-start | bytes 491528 | tf_op jit(solution)/shard_map/ppermute | solution.py:77
  154.2 13.0 %collective-permute-start.17 = (bf16[64,1280]{1,0:T(8,128)(2,1)S(1)}, bf16[64,1280]{1,0:T(8,128)(2,1)S(1)}, u32[]{:S(2)}, u32[]{:S(2)}) collective-permute-start(bf16[64,1280]{1,0:T(8,128)(2,1)S(1)} %slice.143), channel_id=1, source_target_pairs={{0,2},{1,3},{2,0},{3,1},{4,6},{5,7},{6,4},{7,5},{8,10},{9,11},{10,... | collective-permute-start | bytes 491528 | tf_op jit(solution)/shard_map/ppermute | solution.py:77
  160.8 22.6 %copy-start.13 = (s32[64]{0:T(128)S(1)}, s32[64]{0:T(128)}, u32[]{:S(2)}) copy-start(s32[64]{0:T(128)} %param.8) | copy-start | bytes 772
  160.8 22.5 %collective-permute-start.24 = (bf16[64,1280]{1,0:T(8,128)(2,1)S(1)}, bf16[64,1280]{1,0:T(8,128)(2,1)S(1)}, u32[]{:S(2)}, u32[]{:S(2)}) collective-permute-start(bf16[64,1280]{1,0:T(8,128)(2,1)S(1)} %fusion.12), channel_id=1, source_target_pairs={{0,8},{4,12},{8,0},{12,4},{16,24},{20,28},{24,16},{28,20},{1,9},{5... | collective-permute-start | bytes 491528 | tf_op jit(solution)/shard_map/ppermute | solution.py:69
  167.2 9.1 %collective-permute-start.18 = (bf16[64,1280]{1,0:T(8,128)(2,1)S(1)}, bf16[64,1280]{1,0:T(8,128)(2,1)S(1)}, u32[]{:S(2)}, u32[]{:S(2)}) collective-permute-start(bf16[64,1280]{1,0:T(8,128)(2,1)S(1)} %fusion.14), channel_id=1, source_target_pairs={{0,24},{4,28},{8,16},{12,20},{16,8},{20,12},{24,0},{28,4},{1,25},{... | collective-permute-start | bytes 491528 | tf_op jit(solution)/shard_map/ppermute | solution.py:69
  168.6 14.7 %collective-permute-start.21 = (bf16[64,1280]{1,0:T(8,128)(2,1)S(1)}, bf16[64,1280]{1,0:T(8,128)(2,1)S(1)}, u32[]{:S(2)}, u32[]{:S(2)}) collective-permute-start(bf16[64,1280]{1,0:T(8,128)(2,1)S(1)} %fusion.13), channel_id=1, source_target_pairs={{0,16},{4,20},{8,24},{12,28},{16,0},{20,4},{24,8},{28,12},{1,17},{... | collective-permute-start | bytes 491528 | tf_op jit(solution)/shard_map/ppermute | solution.py:69
  (14 other events, 72.7 us)
Sparse Core Ops, SparseCore 0:
  17.9 33.0 all-gather.2
  88.5 42.2 all-gather.4

commit v6 on v2

--- a/solution.py
+++ b/solution.py
@@ -96,8 +96,14 @@
             value = value[:half] + sent.astype(F32)
         return value
 
-    far_first = sorted(range(1, outer), key=lambda k: -k)
     near_first = sorted(range(1, outer))
+    far_first = near_first[::-1]
+    keys = [0] + near_first
+    relay = outer == 4
+
+    def outer_pairs(value, pairs):
+        pairs = [(s * inner + i, t * inner + i) for s, t in pairs for i in range(inner)]
+        return lax.ppermute(value, "dp", pairs)
 
     def shards(tokens, slots, gate_probs, w_gate, w_up, d_hidden):
         dp = lax.axis_index("dp")
@@ -116,60 +122,103 @@
         onehot = (slots[:, None] == jnp.arange(tok, dtype=slots.dtype)[None, :]).astype(BF16)
         rows = jnp.dot(onehot, tokens, preferred_element_type=F32).astype(BF16)
         pieces = {}
+        for k in keys:
+            blocks = [
+                lax.dynamic_slice(rows, (0, (a ^ k) * span + (b ^ j) * depth), (cap, depth))
+                for j in range(inner)
+            ]
+            pieces[k] = jnp.concatenate(blocks, axis=1)
+        got = {}
+        for k in far_first:
+            got[k] = over_outer(after(pieces[k], got[3]) if relay and k == 1 else pieces[k], k)
+        got[0] = pieces[0]
+
+        x_chunks, products, last = {}, {}, rows
         for k in far_first + [0]:
-            pieces[k] = jnp.concatenate(
-                [
-                    lax.dynamic_slice(rows, (0, (a ^ k) * span + (b ^ j) * depth), (cap, depth))
-                    for j in range(inner)
-                ],
-                axis=1,
-            )
-        got = {k: over_outer(pieces[k], k) for k in far_first}
-        x_chunks = {k: gather_etp(got[k]) for k in far_first}
-        x_chunks[0] = gather_etp(after(pieces[0], got[near_first[0]]))
-        probs = gather_etp(after(gate_probs, x_chunks[0]))
-
-        parts = {
-            k: over_outer(jnp.dot(x_chunks[k], weights, preferred_element_type=F32).astype(BF16), k)
-            for k in far_first
-        }
-        pre = jnp.dot(x_chunks[0], weights, preferred_element_type=F32)
+            x_chunks[k] = gather_etp(after(got[k], last))
+            product = jnp.dot(x_chunks[k], weights, preferred_element_type=F32)
+            products[k] = last = product.astype(BF16) if k and not (relay and k == 2) else product
+            if relay and k == 3:
+                carried = outer_pairs(products[3], [(0, 1), (3, 2)])
+                middle = outer_pairs(products[3], [(1, 2), (2, 1)])
+            if relay and k == 2:
+                last = after(products[2], carried, middle)
+        if relay:
+            two = over_outer((products[2] + carried.astype(F32)).astype(BF16), 2)
+            one = over_outer(after(products[1], carried), 1)
+            parts = [middle, one, two]
+        else:
+            parts = [over_outer(products[k], k) for k in far_first]
+        probs = gather_etp(after(gate_probs, products[0]))
         order = etp ^ jnp.array(chunk_order, jnp.int32)
-        hidden, paired = gate_call(
-            order, pre, probs[:, None], d_hidden, [parts[k] for k in near_first]
-        )
-
-        grads = {k: over_outer(paired, k) for k in far_first}
-        grads[0] = paired
-
-        dx = jnp.zeros((cap, outer * span), BF16)
-        last = paired
-        for k in [0] + near_first:
-            partial = lax.dot_general(
+        hidden, paired = gate_call(order, products[0], probs[:, None], d_hidden, parts)
+
+        grads = {0: paired}
+        if relay:
+            grads[2] = over_outer(paired, 2)
+            grads[1] = over_outer(paired, 1)
+        else:
+            for k in near_first:
+                grads[k] = over_outer(paired, k)
+        sums, partials = {}, {}
+
+        def advance(k, last):
+            partials[k] = lax.dot_general(
                 after(grads[k], last), weights, (((1,), (1,)), ((), ())), preferred_element_type=F32
             )
-            last = partial
-            own = reduce_etp(partial).astype(BF16)
-            own = over_outer(own, k) if k else own
+            sums[k] = reduce_etp(partials[k]).astype(BF16)
+            return partials[k]
+
+        def weight_grad(ks, j, last):
+            x_part = jnp.concatenate([x_chunks[k][:, j * depth : (j + 1) * depth] for k in ks], axis=0)
+            grad_part = jnp.concatenate([grads[k] for k in ks], axis=0)
+            return lax.dot_general(
+                x_part, after(grad_part, last), (((0,), (0,)), ((), ())), preferred_element_type=F32
+            )
+
+        early, late = keys[: max(outer - 1, 1)], keys[max(outer - 1, 1) :]
+        last = grads[near_first[0]] if outer > 1 else paired
+        for k in [0] + near_first[:1]:
+            last = advance(k, last)
+        if relay:
+            turn = after(grads[2], last)
+            ends = outer_pairs(turn, [(2, 3), (1, 0)])
+            middle = outer_pairs(after(paired, turn), [(1, 2), (2, 1)])
+            last = sums[1]
+            advance(2, last)
+            last = sums[2]
+            early_sums = [weight_grad(early, j, last) for j in range(1, inner)]
+            grads[3] = middle + after(ends, *early_sums)
+        else:
+            for k in early[2:]:
+                last = advance(k, last)
+            early_sums = [weight_grad(early, j, last) for j in range(1, inner)]
+
+        leaving = [
+            ((early_sums[j - 1] + weight_grad(late, j, grads[late[-1]])) if late else early_sums[j - 1])
+            for j in range(1, inner)
+        ]
+        leaving = [v.astype(BF16) for v in leaving]
+        arriving = [over_inner(leaving[j - 1], j) for j in range(1, inner)]
+        last = leaving[0] if inner > 1 else last
+        for k in late:
+            last = advance(k, last)
+        total = weight_grad(keys, 0, last)
+        gate_total, up_total = total[:, :width], total[:, width:]
+        for part in arriving:
+            gate_total = gate_total + part[:, :width].astype(F32)
+            up_total = up_total + part[:, width:].astype(F32)
+
+        dx = jnp.zeros((cap, outer * span), BF16)
+        for k in keys:
+            own = over_outer(sums[k], k) if k else sums[k]
             for j in range(inner):
                 block = own[:, j * depth : (j + 1) * depth]
                 dx = lax.dynamic_update_slice(dx, block, (0, (a ^ k) * span + (b ^ j) * depth))
         grad_tokens = lax.dot_general(
             onehot, dx, (((0,), (0,)), ((), ())), preferred_element_type=F32
         ).astype(BF16)
-
-        keys = [0] + near_first
-        summed = lax.dot_general(
-            jnp.concatenate([x_chunks[k] for k in keys], axis=0),
-            after(jnp.concatenate([grads[k] for k in keys], axis=0), last),
-            (((0,), (0,)), ((), ())),
-            preferred_element_type=F32,
-        )
-        total = summed[:depth]
-        for j in range(1, inner):
-            part = summed[j * depth : (j + 1) * depth]
-            total = total + over_inner(part.astype(BF16), j).astype(F32)
-        return (hidden, grad_tokens, total[:, :width], total[:, width:])
+        return (hidden, grad_tokens, gate_total, up_total)
 
     return shards
 

time: 146 us -> 146 us (level); the launches traced: 144 us -> 146 us
  starting transfers between devices: 39.6 us -> 46 us
  waiting for transfers between devices: 83.1 us -> 77.8 us
  other arithmetic: 1.13 us -> 2.63 us
    ppermute x12 -> x10, waiting for transfers between devices: 65.7 us -> 49.8 us  [over_outer(): return lax.ppermute(value, 'dp', pairs)]
    ppermute x18, waiting for transfers between devices: 17.4 us -> 27.9 us  [over_etp(): return lax.ppermute(value, 'etp', pairs)]
    ppermute x12 -> x10, starting transfers between devices: 21.5 us -> 26.3 us  [over_outer(): return lax.ppermute(value, 'dp', pairs)]
    ppermute x0 -> x4, starting transfers between devices: none -> 4.39 us  [outer_pairs(): return lax.ppermute(value, 'dp', pairs)]
    ppermute x18, starting transfers between devices: 13.5 us -> 10.7 us  [over_etp(): return lax.ppermute(value, 'etp', pairs)]
    dot_general x9 -> x11, matrix products: 7.87 us -> 8.21 us  [the longest x4 2.83 us: advance(): lax.dot_general(after(grads[k], last), weights, (((1,), (1,)), ((), ())),...]
  transfers between devices with their start and end apart: 33 -> 35, of which waited for: 15 -> 17; matrix products, arithmetic and copies ran while one was open for 11% -> 12% of each run, Pallas kernels for 0% -> 0%
where the time goes in v6:
time: 146 us
  waiting for transfers between devices  77.8 us (53%)
  starting transfers between devices  46 us (32%)
  matrix products  15.8 us (11%)
  other arithmetic  2.63 us (2%)
  Pallas kernels  1.65 us (1%)
    ppermute x10, waiting for transfers between devices, over_outer(): return lax.ppermute(value, 'dp', pairs)  49.8 us
    ppermute x18, waiting for transfers between devices, over_etp(): return lax.ppermute(value, 'etp', pairs)  27.9 us
    ppermute x10, starting transfers between devices, over_outer(): return lax.ppermute(value, 'dp', pairs)  26.3 us
    ppermute x18, starting transfers between devices, over_etp(): return lax.ppermute(value, 'etp', pairs)  10.7 us
    ppermute x3, starting transfers between devices, over_inner(): return lax.ppermute(value, 'dp', pairs)  4.65 us
    ppermute x4, starting transfers between devices, outer_pairs(): return lax.ppermute(value, 'dp', pairs)  4.39 us
    dot_general x1, matrix products, shards(): lax.dot_general(onehot, dx, (((0,), (0,)), ((), ())), preferred_element_t...  3.99 us
    dot_general x1, matrix products, shards(): rows = jnp.dot(onehot, tokens, preferred_element_type=F32).astype(BF16)  3.57 us
  transfers between devices with their start and end apart: 35, of which 17 were waited for; matrix products, arithmetic and copies ran while one was open for 12% of the time, Pallas kernels for 0%

profile of v6, /device:TPU:0, one launch (start us, length us, event | category | flops | bytes accessed | tf_op | source)
XLA Modules:
  0.0 146.2 jit_solution(10054053000522592015)
XLA Ops:
  0.6 3.0 %collective-permute-start.4 = (bf16[640,384]{1,0:T(8,128)(2,1)}, bf16[640,384]{1,0:T(8,128)(2,1)S(1)}, u32[]{:S(2)}, u32[]{:S(2)}) collective-permute-start(bf16[640,384]{1,0:T(8,128)(2,1)} %param.10), channel_id=1, source_target_pairs={{0,4},{4,0},{8,12},{12,8},{16,20},{20,16},{24,28},{28,24},{1,5},{5... | collective-permute-start | bytes 1474568 | tf_op jit(solution)/shard_map/ppermute | solution.py:73
  3.7 3.6 %convolution_convert_fusion.1 = bf16[64,5120]{1,0:T(8,128)(2,1)S(1)} fusion(bf16[512,5120]{1,0:T(8,128)(2,1)} %param.7, s32[64]{0:T(128)} %param.8), kind=kOutput, calls=%fused_computation.1 | convolution fusion | flops 335904768 | bytes 5898496 | tf_op jit(solution)/shard_map/dot_general | solution.py:123
  7.5 4.1 %collective-permute-start = (bf16[64,1280]{1,0:T(8,128)(2,1)S(1)}, bf16[64,1280]{1,0:T(8,128)(2,1)S(1)}, u32[]{:S(2)}, u32[]{:S(2)}) collective-permute-start(bf16[64,1280]{1,0:T(8,128)(2,1)S(1)} %pad_maximum_fusion.9), channel_id=1, source_target_pairs={{0,24},{4,28},{8,16},{12,20},{16,8},{20,12},{24,0},{28,4},{1,25},{... | collective-permute-start | bytes 491528 | tf_op jit(solution)/shard_map/ppermute | solution.py:69
  11.7 5.0 %collective-permute-done = bf16[64,1280]{1,0:T(8,128)(2,1)S(1)} collective-permute-done((bf16[64,1280]{1,0:T(8,128)(2,1)S(1)}, bf16[64,1280]{1,0:T(8,128)(2,1)S(1)}, u32[]{:S(2)}, u32[]{:S(2)}) %collective-permute-start) | collective-permute-done | bytes 163872 | tf_op jit(solution)/shard_map/ppermute | solution.py:69
  16.7 6.2 %collective-permute-start.1 = (bf16[64,1280]{1,0:T(8,128)(2,1)S(1)}, bf16[64,1280]{1,0:T(8,128)(2,1)S(1)}, u32[]{:S(2)}, u32[]{:S(2)}) collective-permute-start(bf16[64,1280]{1,0:T(8,128)(2,1)S(1)} %pad_maximum_fusion.8), channel_id=1, source_target_pairs={{0,8},{4,12},{8,0},{12,4},{16,24},{20,28},{24,16},{28,20},{1,9},{5... | collective-permute-start | bytes 491528 | tf_op jit(solution)/shard_map/ppermute | solution.py:69
  23.0 1.5 %collective-permute-start.10 = (bf16[64,1280]{1,0:T(8,128)(2,1)S(1)}, bf16[64,1280]{1,0:T(8,128)(2,1)S(1)}, u32[]{:S(2)}, u32[]{:S(2)}) collective-permute-start(bf16[64,1280]{1,0:T(8,128)(2,1)S(1)} %collective-permute-done), channel_id=1, source_target_pairs={{0,2},{1,3},{2,0},{3,1},{4,6},{5,7},{6,4},{7,5},{8,10},{9,11},{10,... | collective-permute-start | bytes 491528 | tf_op jit(solution)/shard_map/ppermute | solution.py:77
  24.5 3.7 %collective-permute-done.1 = bf16[64,1280]{1,0:T(8,128)(2,1)S(1)} collective-permute-done((bf16[64,1280]{1,0:T(8,128)(2,1)S(1)}, bf16[64,1280]{1,0:T(8,128)(2,1)S(1)}, u32[]{:S(2)}, u32[]{:S(2)}) %collective-permute-start.1) | collective-permute-done | bytes 163872 | tf_op jit(solution)/shard_map/ppermute | solution.py:69
  28.2 1.5 %collective-permute-start.2 = (bf16[64,1280]{1,0:T(8,128)(2,1)S(1)}, bf16[64,1280]{1,0:T(8,128)(2,1)S(1)}, u32[]{:S(2)}, u32[]{:S(2)}) collective-permute-start(bf16[64,1280]{1,0:T(8,128)(2,1)S(1)} %collective-permute-done.1), channel_id=1, source_target_pairs={{0,2},{1,3},{2,0},{3,1},{4,6},{5,7},{6,4},{7,5},{8,10},{9,11},{10,... | collective-permute-start | bytes 491528 | tf_op jit(solution)/shard_map/ppermute | solution.py:77
  29.8 4.2 %collective-permute-done.2 = bf16[64,1280]{1,0:T(8,128)(2,1)S(1)} collective-permute-done((bf16[64,1280]{1,0:T(8,128)(2,1)S(1)}, bf16[64,1280]{1,0:T(8,128)(2,1)S(1)}, u32[]{:S(2)}, u32[]{:S(2)}) %collective-permute-start.2) | collective-permute-done | bytes 163872 | tf_op jit(solution)/shard_map/ppermute | solution.py:77
  35.0 1.6 %collective-permute-start.13 = (bf16[256,768]{1,0:T(8,128)(2,1)S(1)}, bf16[256,768]{1,0:T(8,128)(2,1)S(1)}, u32[]{:S(2)}, u32[]{:S(2)}) collective-permute-start(bf16[256,768]{1,0:T(8,128)(2,1)S(1)} %convolution_convert_fusion.2), channel_id=1, source_target_pairs={{0,8},{4,12},{24,16},{28,20},{1,9},{5,13},{25,17},{29,21},{2,10},{... | collective-permute-start | bytes 1179656 | tf_op jit(solution)/shard_map/ppermute | solution.py:106
  37.3 1.6 %collective-permute-start.16 = (bf16[64,1280]{1,0:T(8,128)(2,1)S(1)}, bf16[64,1280]{1,0:T(8,128)(2,1)S(1)}, u32[]{:S(2)}, u32[]{:S(2)}) collective-permute-start(bf16[64,1280]{1,0:T(8,128)(2,1)S(1)} %collective-permute-done.15), channel_id=1, source_target_pairs={{0,2},{1,3},{2,0},{3,1},{4,6},{5,7},{6,4},{7,5},{8,10},{9,11},{10,... | collective-permute-start | bytes 491528 | tf_op jit(solution)/shard_map/ppermute | solution.py:77
  40.2 4.2 %collective-permute-done.16 = bf16[64,1280]{1,0:T(8,128)(2,1)S(1)} collective-permute-done((bf16[64,1280]{1,0:T(8,128)(2,1)S(1)}, bf16[64,1280]{1,0:T(8,128)(2,1)S(1)}, u32[]{:S(2)}, u32[]{:S(2)}) %collective-permute-start.16) | collective-permute-done | bytes 163872 | tf_op jit(solution)/shard_map/ppermute | solution.py:77
  44.5 2.7 %collective-permute-done.6 = bf16[64,1280]{1,0:T(8,128)(2,1)S(1)} collective-permute-done((bf16[64,1280]{1,0:T(8,128)(2,1)S(1)}, bf16[64,1280]{1,0:T(8,128)(2,1)S(1)}, u32[]{:S(2)}, u32[]{:S(2)}) %collective-permute-start.6) | collective-permute-done | bytes 163872 | tf_op jit(solution)/shard_map/ppermute | solution.py:77
  47.4 2.9 %collective-permute-start.14 = (bf16[256,768]{1,0:T(8,128)(2,1)S(1)}, bf16[256,768]{1,0:T(8,128)(2,1)S(1)}, u32[]{:S(2)}, u32[]{:S(2)}) collective-permute-start(bf16[256,768]{1,0:T(8,128)(2,1)S(1)} %convolution_convert_fusion.3), channel_id=1, source_target_pairs={{0,8},{4,12},{8,0},{12,4},{16,24},{20,28},{24,16},{28,20},{1,9},{5... | collective-permute-start | bytes 1179656 | tf_op jit(solution)/shard_map/ppermute | solution.py:69
  51.1 1.6 %collective-permute-start.8 = (bf16[64]{0:T(256)(128)(2,1)S(1)}, bf16[64]{0:T(256)(128)(2,1)S(1)}, u32[]{:S(2)}, u32[]{:S(2)}) collective-permute-start(bf16[64]{0:T(256)(128)(2,1)S(1)} %copy-done.4), channel_id=1, source_target_pairs={{0,2},{1,3},{2,0},{3,1},{4,6},{5,7},{6,4},{7,5},{8,10},{9,11},{10,... | collective-permute-start | bytes 392 | tf_op jit(solution)/shard_map/ppermute | solution.py:77
  56.1 8.2 %collective-permute-done.14.refs_1_ = bf16[256,768]{1,0:T(8,128)(2,1)S(1)} collective-permute-done((bf16[256,768]{1,0:T(8,128)(2,1)S(1)}, bf16[256,768]{1,0:T(8,128)(2,1)S(1)}, u32[]{:S(2)}, u32[]{:S(2)}) %collective-permute-start.14) | collective-permute-done | bytes 393248 | tf_op jit(solution)/shard_map/ppermute | solution.py:69
  64.3 9.5 %collective-permute-done.18.refs_2_ = bf16[256,768]{1,0:T(8,128)(2,1)S(1)} collective-permute-done((bf16[256,768]{1,0:T(8,128)(2,1)S(1)}, bf16[256,768]{1,0:T(8,128)(2,1)S(1)}, u32[]{:S(2)}, u32[]{:S(2)}) %collective-permute-start.18) | collective-permute-done | bytes 393248 | tf_op jit(solution)/shard_map/ppermute | solution.py:69
  73.8 1.6 %shard_map.102 = (bf16[256,384]{1,0:T(8,128)(2,1)}, bf16[256,768]{1,0:T(8,128)(2,1)S(1)}) custom-call(s32[4]{0:T(128)S(1)} %broadcast_xor_fusion.order_ref, f32[256,768]{1,0:T(8,128)S(1)} %fusion.27.pre_ref, bf16[256,1]{1,0:T(8,128)(2,1)S(1)} %broadcast_in_dim.10.prob_ref, bf16[256,384]{1,0:T(8,128)(2,1)S(1)} %copy-done, ...), custom_call_target="tpu_custom_call" | custom-call | flops 1966080 | bytes 2949120 | tf_op jit(solution)/shard_map/pallas_call | solution.py:49
  75.5 2.3 %collective-permute-start.25 = (bf16[256,768]{1,0:T(8,128)(2,1)S(1)}, bf16[256,768]{1,0:T(8,128)(2,1)S(1)}, u32[]{:S(2)}, u32[]{:S(2)}) collective-permute-start(bf16[256,768]{1,0:T(8,128)(2,1)S(1)} %get-tuple-element.34), channel_id=1, source_target_pairs={{0,16},{4,20},{8,24},{12,28},{16,0},{20,4},{24,8},{28,12},{1,17},{... | collective-permute-start | bytes 1179656 | tf_op jit(solution)/shard_map/ppermute | solution.py:69
  77.9 14.9 %collective-permute-done.19 = bf16[256,768]{1,0:T(8,128)(2,1)S(1)} collective-permute-done((bf16[256,768]{1,0:T(8,128)(2,1)S(1)}, bf16[256,768]{1,0:T(8,128)(2,1)S(1)}, u32[]{:S(2)}, u32[]{:S(2)}) %collective-permute-start.19) | collective-permute-done | bytes 393248 | tf_op jit(solution)/shard_map/ppermute | solution.py:69
  98.2 1.6 %collective-permute-start.21 = (bf16[64,1280]{1,0:T(8,128)(2,1)S(1)}, bf16[64,1280]{1,0:T(8,128)(2,1)S(1)}, u32[]{:S(2)}, u32[]{:S(2)}) collective-permute-start(bf16[64,1280]{1,0:T(8,128)(2,1)S(1)} %slice.233), channel_id=1, source_target_pairs={{0,2},{1,3},{2,0},{3,1},{4,6},{5,7},{6,4},{7,5},{8,10},{9,11},{10,... | collective-permute-start | bytes 491528 | tf_op jit(solution)/shard_map/ppermute | solution.py:77
  99.8 4.8 %collective-permute-done.23 = bf16[64,1280]{1,0:T(8,128)(2,1)S(1)} collective-permute-done((bf16[64,1280]{1,0:T(8,128)(2,1)S(1)}, bf16[64,1280]{1,0:T(8,128)(2,1)S(1)}, u32[]{:S(2)}, u32[]{:S(2)}) %collective-permute-start.23) | collective-permute-done | bytes 163872 | tf_op jit(solution)/shard_map/ppermute | solution.py:77
  104.6 4.9 %collective-permute-start.24 = (bf16[64,1280]{1,0:T(8,128)(2,1)S(1)}, bf16[64,1280]{1,0:T(8,128)(2,1)S(1)}, u32[]{:S(2)}, u32[]{:S(2)}) collective-permute-start(bf16[64,1280]{1,0:T(8,128)(2,1)S(1)} %fusion.18), channel_id=1, source_target_pairs={{0,8},{4,12},{8,0},{12,4},{16,24},{20,28},{24,16},{28,20},{1,9},{5... | collective-permute-start | bytes 491528 | tf_op jit(solution)/shard_map/ppermute | solution.py:69
  110.5 2.3 %collective-permute-done.24 = bf16[64,1280]{1,0:T(8,128)(2,1)S(1)} collective-permute-done((bf16[64,1280]{1,0:T(8,128)(2,1)S(1)}, bf16[64,1280]{1,0:T(8,128)(2,1)S(1)}, u32[]{:S(2)}, u32[]{:S(2)}) %collective-permute-start.24) | collective-permute-done | bytes 163872 | tf_op jit(solution)/shard_map/ppermute | solution.py:69
  113.5 4.9 %collective-permute-done.27 = bf16[64,1280]{1,0:T(8,128)(2,1)S(1)} collective-permute-done((bf16[64,1280]{1,0:T(8,128)(2,1)S(1)}, bf16[64,1280]{1,0:T(8,128)(2,1)S(1)}, u32[]{:S(2)}, u32[]{:S(2)}) %collective-permute-start.27) | collective-permute-done | bytes 163872 | tf_op jit(solution)/shard_map/ppermute | solution.py:77
  118.4 2.6 %collective-permute-start.28 = (bf16[64,1280]{1,0:T(8,128)(2,1)S(1)}, bf16[64,1280]{1,0:T(8,128)(2,1)S(1)}, u32[]{:S(2)}, u32[]{:S(2)}) collective-permute-start(bf16[64,1280]{1,0:T(8,128)(2,1)S(1)} %fusion.17), channel_id=1, source_target_pairs={{0,16},{4,20},{8,24},{12,28},{16,0},{20,4},{24,8},{28,12},{1,17},{... | collective-permute-start | bytes 491528 | tf_op jit(solution)/shard_map/ppermute | solution.py:69
  122.6 1.6 %collective-permute-start.34 = (bf16[640,768]{1,0:T(8,128)(2,1)S(1)}, bf16[640,768]{1,0:T(8,128)(2,1)S(1)}, u32[]{:S(2)}, u32[]{:S(2)}) collective-permute-start(bf16[640,768]{1,0:T(8,128)(2,1)S(1)} %add_convert_fusion), channel_id=1, source_target_pairs={{0,4},{4,0},{8,12},{12,8},{16,20},{20,16},{24,28},{28,24},{1,5},{5... | collective-permute-start | bytes 2949128 | tf_op jit(solution)/shard_map/ppermute | solution.py:73
  127.3 5.8 %collective-permute-done.32 = bf16[64,1280]{1,0:T(8,128)(2,1)S(1)} collective-permute-done((bf16[64,1280]{1,0:T(8,128)(2,1)S(1)}, bf16[64,1280]{1,0:T(8,128)(2,1)S(1)}, u32[]{:S(2)}, u32[]{:S(2)}) %collective-permute-start.32) | collective-permute-done | bytes 163872 | tf_op jit(solution)/shard_map/ppermute | solution.py:77
  133.2 1.9 %collective-permute-start.33 = (bf16[64,1280]{1,0:T(8,128)(2,1)S(1)}, bf16[64,1280]{1,0:T(8,128)(2,1)S(1)}, u32[]{:S(2)}, u32[]{:S(2)}) collective-permute-start(bf16[64,1280]{1,0:T(8,128)(2,1)S(1)} %fusion.15), channel_id=1, source_target_pairs={{0,24},{4,28},{8,16},{12,20},{16,8},{20,12},{24,0},{28,4},{1,25},{... | collective-permute-start | bytes 491528 | tf_op jit(solution)/shard_map/ppermute | solution.py:69
  135.1 5.6 %collective-permute-done.33 = bf16[64,1280]{1,0:T(8,128)(2,1)S(1)} collective-permute-done((bf16[64,1280]{1,0:T(8,128)(2,1)S(1)}, bf16[64,1280]{1,0:T(8,128)(2,1)S(1)}, u32[]{:S(2)}, u32[]{:S(2)}) %collective-permute-start.33) | collective-permute-done | bytes 163872 | tf_op jit(solution)/shard_map/ppermute | solution.py:69
  140.8 4.0 %convolution_convert_fusion = bf16[512,5120]{1,0:T(8,128)(2,1)} fusion(bf16[64,5120]{1,0:T(8,128)(2,1)S(1)} %slice_dynamic-update-slice_fusion, s32[64]{0:T(128)S(1)} %copy-done.3), kind=kOutput, calls=%fused_computation | convolution fusion | flops 338198528 | bytes 5898496 | tf_op jit(solution)/shard_map/dot_general | solution.py:218
  144.8 1.4 slice_add_fusion
  (121 shorter events, 19.6 us)
Async XLA Ops:
  0.6 33.4 %collective-permute-start.4 = (bf16[640,384]{1,0:T(8,128)(2,1)}, bf16[640,384]{1,0:T(8,128)(2,1)S(1)}, u32[]{:S(2)}, u32[]{:S(2)}) collective-permute-start(bf16[640,384]{1,0:T(8,128)(2,1)} %param.10), channel_id=1, source_target_pairs={{0,4},{4,0},{8,12},{12,8},{16,20},{20,16},{24,28},{28,24},{1,5},{5... | collective-permute-start | bytes 1474568 | tf_op jit(solution)/shard_map/ppermute | solution.py:73
  3.6 30.5 %collective-permute-start.5 = (bf16[640,384]{1,0:T(8,128)(2,1)}, bf16[640,384]{1,0:T(8,128)(2,1)S(1)}, u32[]{:S(2)}, u32[]{:S(2)}) collective-permute-start(bf16[640,384]{1,0:T(8,128)(2,1)} %param.11), channel_id=1, source_target_pairs={{0,4},{4,0},{8,12},{12,8},{16,20},{20,16},{24,28},{28,24},{1,5},{5... | collective-permute-start | bytes 1474568 | tf_op jit(solution)/shard_map/ppermute | solution.py:73
  7.5 9.3 %collective-permute-start = (bf16[64,1280]{1,0:T(8,128)(2,1)S(1)}, bf16[64,1280]{1,0:T(8,128)(2,1)S(1)}, u32[]{:S(2)}, u32[]{:S(2)}) collective-permute-start(bf16[64,1280]{1,0:T(8,128)(2,1)S(1)} %pad_maximum_fusion.9), channel_id=1, source_target_pairs={{0,24},{4,28},{8,16},{12,20},{16,8},{20,12},{24,0},{28,4},{1,25},{... | collective-permute-start | bytes 491528 | tf_op jit(solution)/shard_map/ppermute | solution.py:69
  11.6 25.7 %collective-permute-start.15 = (bf16[64,1280]{1,0:T(8,128)(2,1)S(1)}, bf16[64,1280]{1,0:T(8,128)(2,1)S(1)}, u32[]{:S(2)}, u32[]{:S(2)}) collective-permute-start(bf16[64,1280]{1,0:T(8,128)(2,1)S(1)} %pad_maximum_fusion.10), channel_id=1, source_target_pairs={{0,16},{4,20},{8,24},{12,28},{16,0},{20,4},{24,8},{28,12},{1,17},{... | collective-permute-start | bytes 491528 | tf_op jit(solution)/shard_map/ppermute | solution.py:69
  16.7 11.4 %collective-permute-start.1 = (bf16[64,1280]{1,0:T(8,128)(2,1)S(1)}, bf16[64,1280]{1,0:T(8,128)(2,1)S(1)}, u32[]{:S(2)}, u32[]{:S(2)}) collective-permute-start(bf16[64,1280]{1,0:T(8,128)(2,1)S(1)} %pad_maximum_fusion.8), channel_id=1, source_target_pairs={{0,8},{4,12},{8,0},{12,4},{16,24},{20,28},{24,16},{28,20},{1,9},{5... | collective-permute-start | bytes 491528 | tf_op jit(solution)/shard_map/ppermute | solution.py:69
  23.0 6.7 %collective-permute-start.10 = (bf16[64,1280]{1,0:T(8,128)(2,1)S(1)}, bf16[64,1280]{1,0:T(8,128)(2,1)S(1)}, u32[]{:S(2)}, u32[]{:S(2)}) collective-permute-start(bf16[64,1280]{1,0:T(8,128)(2,1)S(1)} %collective-permute-done), channel_id=1, source_target_pairs={{0,2},{1,3},{2,0},{3,1},{4,6},{5,7},{6,4},{7,5},{8,10},{9,11},{10,... | collective-permute-start | bytes 491528 | tf_op jit(solution)/shard_map/ppermute | solution.py:77
  28.2 5.8 %collective-permute-start.2 = (bf16[64,1280]{1,0:T(8,128)(2,1)S(1)}, bf16[64,1280]{1,0:T(8,128)(2,1)S(1)}, u32[]{:S(2)}, u32[]{:S(2)}) collective-permute-start(bf16[64,1280]{1,0:T(8,128)(2,1)S(1)} %collective-permute-done.1), channel_id=1, source_target_pairs={{0,2},{1,3},{2,0},{3,1},{4,6},{5,7},{6,4},{7,5},{8,10},{9,11},{10,... | collective-permute-start | bytes 491528 | tf_op jit(solution)/shard_map/ppermute | solution.py:77
  29.7 4.6 %collective-permute-start.11 = (bf16[128,1280]{1,0:T(8,128)(2,1)S(1)}, bf16[128,1280]{1,0:T(8,128)(2,1)S(1)}, u32[]{:S(2)}, u32[]{:S(2)}) collective-permute-start(bf16[128,1280]{1,0:T(8,128)(2,1)S(1)} %pad_maximum_fusion.5), channel_id=1, source_target_pairs={{0,1},{1,0},{2,3},{3,2},{4,5},{5,4},{6,7},{7,6},{8,9},{9,8},{10,11... | collective-permute-start | bytes 983048 | tf_op jit(solution)/shard_map/ppermute | solution.py:77
  34.0 4.9 %collective-permute-start.3 = (bf16[128,1280]{1,0:T(8,128)(2,1)S(1)}, bf16[128,1280]{1,0:T(8,128)(2,1)S(1)}, u32[]{:S(2)}, u32[]{:S(2)}) collective-permute-start(bf16[128,1280]{1,0:T(8,128)(2,1)S(1)} %pad_maximum_fusion.3), channel_id=1, source_target_pairs={{0,1},{1,0},{2,3},{3,2},{4,5},{5,4},{6,7},{7,6},{8,9},{9,8},{10,11... | collective-permute-start | bytes 983048 | tf_op jit(solution)/shard_map/ppermute | solution.py:77
  35.0 12.3 %collective-permute-start.13 = (bf16[256,768]{1,0:T(8,128)(2,1)S(1)}, bf16[256,768]{1,0:T(8,128)(2,1)S(1)}, u32[]{:S(2)}, u32[]{:S(2)}) collective-permute-start(bf16[256,768]{1,0:T(8,128)(2,1)S(1)} %convolution_convert_fusion.2), channel_id=1, source_target_pairs={{0,8},{4,12},{24,16},{28,20},{1,9},{5,13},{25,17},{29,21},{2,10},{... | collective-permute-start | bytes 1179656 | tf_op jit(solution)/shard_map/ppermute | solution.py:106
  36.6 19.5 %collective-permute-start.12 = (bf16[256,768]{1,0:T(8,128)(2,1)S(1)}, bf16[256,768]{1,0:T(8,128)(2,1)S(1)}, u32[]{:S(2)}, u32[]{:S(2)}) collective-permute-start(bf16[256,768]{1,0:T(8,128)(2,1)S(1)} %convolution_convert_fusion.2), channel_id=1, source_target_pairs={{8,16},{12,20},{16,8},{20,12},{9,17},{13,21},{17,9},{21,13},{10,18... | collective-permute-start | bytes 1179656 | tf_op jit(solution)/shard_map/ppermute | solution.py:106
  37.3 7.1 %collective-permute-start.16 = (bf16[64,1280]{1,0:T(8,128)(2,1)S(1)}, bf16[64,1280]{1,0:T(8,128)(2,1)S(1)}, u32[]{:S(2)}, u32[]{:S(2)}) collective-permute-start(bf16[64,1280]{1,0:T(8,128)(2,1)S(1)} %collective-permute-done.15), channel_id=1, source_target_pairs={{0,2},{1,3},{2,0},{3,1},{4,6},{5,7},{6,4},{7,5},{8,10},{9,11},{10,... | collective-permute-start | bytes 491528 | tf_op jit(solution)/shard_map/ppermute | solution.py:77
  39.6 7.6 %collective-permute-start.6 = (bf16[64,1280]{1,0:T(8,128)(2,1)S(1)}, bf16[64,1280]{1,0:T(8,128)(2,1)S(1)}, u32[]{:S(2)}, u32[]{:S(2)}) collective-permute-start(bf16[64,1280]{1,0:T(8,128)(2,1)S(1)} %pad_maximum_fusion.7), channel_id=1, source_target_pairs={{0,2},{1,3},{2,0},{3,1},{4,6},{5,7},{6,4},{7,5},{8,10},{9,11},{10,... | collective-permute-start | bytes 491528 | tf_op jit(solution)/shard_map/ppermute | solution.py:77
  44.4 5.9 %collective-permute-start.17 = (bf16[128,1280]{1,0:T(8,128)(2,1)S(1)}, bf16[128,1280]{1,0:T(8,128)(2,1)S(1)}, u32[]{:S(2)}, u32[]{:S(2)}) collective-permute-start(bf16[128,1280]{1,0:T(8,128)(2,1)S(1)} %pad_maximum_fusion.6), channel_id=1, source_target_pairs={{0,1},{1,0},{2,3},{3,2},{4,5},{5,4},{6,7},{7,6},{8,9},{9,8},{10,11... | collective-permute-start | bytes 983048 | tf_op jit(solution)/shard_map/ppermute | solution.py:77
  47.3 3.1 %collective-permute-start.7 = (bf16[128,1280]{1,0:T(8,128)(2,1)S(1)}, bf16[128,1280]{1,0:T(8,128)(2,1)S(1)}, u32[]{:S(2)}, u32[]{:S(2)}) collective-permute-start(bf16[128,1280]{1,0:T(8,128)(2,1)S(1)} %pad_maximum_fusion.4), channel_id=1, source_target_pairs={{0,1},{1,0},{2,3},{3,2},{4,5},{5,4},{6,7},{7,6},{8,9},{9,8},{10,11... | collective-permute-start | bytes 983048 | tf_op jit(solution)/shard_map/ppermute | solution.py:77
  47.4 16.9 %collective-permute-start.14 = (bf16[256,768]{1,0:T(8,128)(2,1)S(1)}, bf16[256,768]{1,0:T(8,128)(2,1)S(1)}, u32[]{:S(2)}, u32[]{:S(2)}) collective-permute-start(bf16[256,768]{1,0:T(8,128)(2,1)S(1)} %convolution_convert_fusion.3), channel_id=1, source_target_pairs={{0,8},{4,12},{8,0},{12,4},{16,24},{20,28},{24,16},{28,20},{1,9},{5... | collective-permute-start | bytes 1179656 | tf_op jit(solution)/shard_map/ppermute | solution.py:69
  51.1 3.6 %collective-permute-start.8 = (bf16[64]{0:T(256)(128)(2,1)S(1)}, bf16[64]{0:T(256)(128)(2,1)S(1)}, u32[]{:S(2)}, u32[]{:S(2)}) collective-permute-start(bf16[64]{0:T(256)(128)(2,1)S(1)} %copy-done.4), channel_id=1, source_target_pairs={{0,2},{1,3},{2,0},{3,1},{4,6},{5,7},{6,4},{7,5},{8,10},{9,11},{10,... | collective-permute-start | bytes 392 | tf_op jit(solution)/shard_map/ppermute | solution.py:77
  53.4 20.4 %collective-permute-start.18 = (bf16[256,768]{1,0:T(8,128)(2,1)S(1)}, bf16[256,768]{1,0:T(8,128)(2,1)S(1)}, u32[]{:S(2)}, u32[]{:S(2)}) collective-permute-start(bf16[256,768]{1,0:T(8,128)(2,1)S(1)} %fusion.8), channel_id=1, source_target_pairs={{0,16},{4,20},{8,24},{12,28},{16,0},{20,4},{24,8},{28,12},{1,17},{... | collective-permute-start | bytes 1179656 | tf_op jit(solution)/shard_map/ppermute | solution.py:69
  75.4 17.4 %collective-permute-start.19 = (bf16[256,768]{1,0:T(8,128)(2,1)S(1)}, bf16[256,768]{1,0:T(8,128)(2,1)S(1)}, u32[]{:S(2)}, u32[]{:S(2)}) collective-permute-start(bf16[256,768]{1,0:T(8,128)(2,1)S(1)} %get-tuple-element.34), channel_id=1, source_target_pairs={{0,8},{4,12},{8,0},{12,4},{16,24},{20,28},{24,16},{28,20},{1,9},{5... | collective-permute-start | bytes 1179656 | tf_op jit(solution)/shard_map/ppermute | solution.py:69
  75.5 19.6 %collective-permute-start.25 = (bf16[256,768]{1,0:T(8,128)(2,1)S(1)}, bf16[256,768]{1,0:T(8,128)(2,1)S(1)}, u32[]{:S(2)}, u32[]{:S(2)}) collective-permute-start(bf16[256,768]{1,0:T(8,128)(2,1)S(1)} %get-tuple-element.34), channel_id=1, source_target_pairs={{0,16},{4,20},{8,24},{12,28},{16,0},{20,4},{24,8},{28,12},{1,17},{... | collective-permute-start | bytes 1179656 | tf_op jit(solution)/shard_map/ppermute | solution.py:69
  94.3 3.2 %collective-permute-start.22 = (bf16[128,1280]{1,0:T(8,128)(2,1)S(1)}, bf16[128,1280]{1,0:T(8,128)(2,1)S(1)}, u32[]{:S(2)}, u32[]{:S(2)}) collective-permute-start(bf16[128,1280]{1,0:T(8,128)(2,1)S(1)} %slice.228), channel_id=1, source_target_pairs={{0,1},{1,0},{2,3},{3,2},{4,5},{5,4},{6,7},{7,6},{8,9},{9,8},{10,11... | collective-permute-start | bytes 983048 | tf_op jit(solution)/shard_map/ppermute | solution.py:77
  95.1 26.9 %collective-permute-start.30 = (bf16[256,768]{1,0:T(8,128)(2,1)S(1)}, bf16[256,768]{1,0:T(8,128)(2,1)S(1)}, u32[]{:S(2)}, u32[]{:S(2)}) collective-permute-start(bf16[256,768]{1,0:T(8,128)(2,1)S(1)} %collective-permute-done.25), channel_id=1, source_target_pairs={{16,24},{20,28},{8,0},{12,4},{17,25},{21,29},{9,1},{13,5},{18,26},... | collective-permute-start | bytes 1179656 | tf_op jit(solution)/shard_map/ppermute | solution.py:106
  96.5 25.5 %collective-permute-start.29 = (bf16[256,768]{1,0:T(8,128)(2,1)S(1)}, bf16[256,768]{1,0:T(8,128)(2,1)S(1)}, u32[]{:S(2)}, u32[]{:S(2)}) collective-permute-start(bf16[256,768]{1,0:T(8,128)(2,1)S(1)} %get-tuple-element.34), channel_id=1, source_target_pairs={{8,16},{12,20},{16,8},{20,12},{9,17},{13,21},{17,9},{21,13},{10,18... | collective-permute-start | bytes 1179656 | tf_op jit(solution)/shard_map/ppermute | solution.py:106
  97.5 7.1 %collective-permute-start.23 = (bf16[64,1280]{1,0:T(8,128)(2,1)S(1)}, bf16[64,1280]{1,0:T(8,128)(2,1)S(1)}, u32[]{:S(2)}, u32[]{:S(2)}) collective-permute-start(bf16[64,1280]{1,0:T(8,128)(2,1)S(1)} %slice.232), channel_id=1, source_target_pairs={{0,2},{1,3},{2,0},{3,1},{4,6},{5,7},{6,4},{7,5},{8,10},{9,11},{10,... | collective-permute-start | bytes 491528 | tf_op jit(solution)/shard_map/ppermute | solution.py:77
  98.2 12.2 %collective-permute-start.21 = (bf16[64,1280]{1,0:T(8,128)(2,1)S(1)}, bf16[64,1280]{1,0:T(8,128)(2,1)S(1)}, u32[]{:S(2)}, u32[]{:S(2)}) collective-permute-start(bf16[64,1280]{1,0:T(8,128)(2,1)S(1)} %slice.233), channel_id=1, source_target_pairs={{0,2},{1,3},{2,0},{3,1},{4,6},{5,7},{6,4},{7,5},{8,10},{9,11},{10,... | collective-permute-start | bytes 491528 | tf_op jit(solution)/shard_map/ppermute | solution.py:77
  104.6 8.2 %collective-permute-start.24 = (bf16[64,1280]{1,0:T(8,128)(2,1)S(1)}, bf16[64,1280]{1,0:T(8,128)(2,1)S(1)}, u32[]{:S(2)}, u32[]{:S(2)}) collective-permute-start(bf16[64,1280]{1,0:T(8,128)(2,1)S(1)} %fusion.18), channel_id=1, source_target_pairs={{0,8},{4,12},{8,0},{12,4},{16,24},{20,28},{24,16},{28,20},{1,9},{5... | collective-permute-start | bytes 491528 | tf_op jit(solution)/shard_map/ppermute | solution.py:69
  110.3 2.6 %collective-permute-start.26 = (bf16[128,1280]{1,0:T(8,128)(2,1)S(1)}, bf16[128,1280]{1,0:T(8,128)(2,1)S(1)}, u32[]{:S(2)}, u32[]{:S(2)}) collective-permute-start(bf16[128,1280]{1,0:T(8,128)(2,1)S(1)} %slice.227), channel_id=1, source_target_pairs={{0,1},{1,0},{2,3},{3,2},{4,5},{5,4},{6,7},{7,6},{8,9},{9,8},{10,11... | collective-permute-start | bytes 983048 | tf_op jit(solution)/shard_map/ppermute | solution.py:77
  113.0 5.4 %collective-permute-start.27 = (bf16[64,1280]{1,0:T(8,128)(2,1)S(1)}, bf16[64,1280]{1,0:T(8,128)(2,1)S(1)}, u32[]{:S(2)}, u32[]{:S(2)}) collective-permute-start(bf16[64,1280]{1,0:T(8,128)(2,1)S(1)} %slice.231), channel_id=1, source_target_pairs={{0,2},{1,3},{2,0},{3,1},{4,6},{5,7},{6,4},{7,5},{8,10},{9,11},{10,... | collective-permute-start | bytes 491528 | tf_op jit(solution)/shard_map/ppermute | solution.py:77
  118.4 8.9 %collective-permute-start.28 = (bf16[64,1280]{1,0:T(8,128)(2,1)S(1)}, bf16[64,1280]{1,0:T(8,128)(2,1)S(1)}, u32[]{:S(2)}, u32[]{:S(2)}) collective-permute-start(bf16[64,1280]{1,0:T(8,128)(2,1)S(1)} %fusion.17), channel_id=1, source_target_pairs={{0,16},{4,20},{8,24},{12,28},{16,0},{20,4},{24,8},{28,12},{1,17},{... | collective-permute-start | bytes 491528 | tf_op jit(solution)/shard_map/ppermute | solution.py:69
  122.6 22.1 %collective-permute-start.34 = (bf16[640,768]{1,0:T(8,128)(2,1)S(1)}, bf16[640,768]{1,0:T(8,128)(2,1)S(1)}, u32[]{:S(2)}, u32[]{:S(2)}) collective-permute-start(bf16[640,768]{1,0:T(8,128)(2,1)S(1)} %add_convert_fusion), channel_id=1, source_target_pairs={{0,4},{4,0},{8,12},{12,8},{16,20},{20,16},{24,28},{28,24},{1,5},{5... | collective-permute-start | bytes 2949128 | tf_op jit(solution)/shard_map/ppermute | solution.py:73
  126.7 6.4 %collective-permute-start.32 = (bf16[64,1280]{1,0:T(8,128)(2,1)S(1)}, bf16[64,1280]{1,0:T(8,128)(2,1)S(1)}, u32[]{:S(2)}, u32[]{:S(2)}) collective-permute-start(bf16[64,1280]{1,0:T(8,128)(2,1)S(1)} %slice.230), channel_id=1, source_target_pairs={{0,2},{1,3},{2,0},{3,1},{4,6},{5,7},{6,4},{7,5},{8,10},{9,11},{10,... | collective-permute-start | bytes 491528 | tf_op jit(solution)/shard_map/ppermute | solution.py:77
  133.2 7.5 %collective-permute-start.33 = (bf16[64,1280]{1,0:T(8,128)(2,1)S(1)}, bf16[64,1280]{1,0:T(8,128)(2,1)S(1)}, u32[]{:S(2)}, u32[]{:S(2)}) collective-permute-start(bf16[64,1280]{1,0:T(8,128)(2,1)S(1)} %fusion.15), channel_id=1, source_target_pairs={{0,24},{4,28},{8,16},{12,20},{16,8},{20,12},{24,0},{28,4},{1,25},{... | collective-permute-start | bytes 491528 | tf_op jit(solution)/shard_map/ppermute | solution.py:69
  (9 other events, 100.1 us)

commit v7 on v6

--- a/solution.py
+++ b/solution.py
@@ -130,28 +130,39 @@
             pieces[k] = jnp.concatenate(blocks, axis=1)
         got = {}
         for k in far_first:
-            got[k] = over_outer(after(pieces[k], got[3]) if relay and k == 1 else pieces[k], k)
+            got[k] = over_outer(pieces[k], k)
         got[0] = pieces[0]
 
-        x_chunks, products, last = {}, {}, rows
-        for k in far_first + [0]:
-            x_chunks[k] = gather_etp(after(got[k], last))
-            product = jnp.dot(x_chunks[k], weights, preferred_element_type=F32)
-            products[k] = last = product.astype(BF16) if k and not (relay and k == 2) else product
-            if relay and k == 3:
-                carried = outer_pairs(products[3], [(0, 1), (3, 2)])
-                middle = outer_pairs(products[3], [(1, 2), (2, 1)])
-            if relay and k == 2:
-                last = after(products[2], carried, middle)
+        x_chunks, products = {}, {}
+
+        def multiply(k, last):
+            return jnp.dot(after(x_chunks[k], last), weights, preferred_element_type=F32)
+
         if relay:
-            two = over_outer((products[2] + carried.astype(F32)).astype(BF16), 2)
-            one = over_outer(after(products[1], carried), 1)
-            parts = [middle, one, two]
+            x_chunks[3] = gather_etp(got[3])
+            far = multiply(3, rows).astype(BF16)
+            carried = outer_pairs(far, [(0, 1), (3, 2)])
+            middle = outer_pairs(far, [(1, 2), (2, 1)])
+            x_chunks[2] = gather_etp(after(got[2], far))
+            product = multiply(2, far)
+            x_chunks[1] = gather_etp(after(got[1], product))
+            summed = (product + carried.astype(F32)).astype(BF16)
+            two = over_outer(summed, 2)
+            one = over_outer(multiply(1, summed).astype(BF16), 1)
+            x_chunks[0] = gather_etp(after(got[0], summed))
+            own = multiply(0, summed)
+            parts = [after(middle, own), one, two]
         else:
-            parts = [over_outer(products[k], k) for k in far_first]
-        probs = gather_etp(after(gate_probs, products[0]))
+            last, parts = rows, []
+            for k in far_first:
+                x_chunks[k] = gather_etp(after(got[k], last))
+                last = multiply(k, last).astype(BF16)
+                parts.append(over_outer(last, k))
+            x_chunks[0] = gather_etp(after(got[0], last))
+            own = multiply(0, last)
+        probs = gather_etp(after(gate_probs, own))
         order = etp ^ jnp.array(chunk_order, jnp.int32)
-        hidden, paired = gate_call(order, products[0], probs[:, None], d_hidden, parts)
+        hidden, paired = gate_call(order, own, probs[:, None], d_hidden, parts)
 
         grads = {0: paired}
         if relay:
@@ -184,9 +195,7 @@
             turn = after(grads[2], last)
             ends = outer_pairs(turn, [(2, 3), (1, 0)])
             middle = outer_pairs(after(paired, turn), [(1, 2), (2, 1)])
-            last = sums[1]
-            advance(2, last)
-            last = sums[2]
+            last = advance(2, last)
             early_sums = [weight_grad(early, j, last) for j in range(1, inner)]
             grads[3] = middle + after(ends, *early_sums)
         else:

time: 146 us -> 150 us (1.027)
  starting transfers between devices: 46 us -> 47.9 us
    ppermute x4, starting transfers between devices: 4.39 us -> 14.6 us  [outer_pairs(): return lax.ppermute(value, 'dp', pairs)]
    ppermute x4, waiting for transfers between devices: 0.01 us -> 9.19 us  [outer_pairs(): return lax.ppermute(value, 'dp', pairs)]
    ppermute x18, waiting for transfers between devices: 27.9 us -> 19.1 us  [over_etp(): return lax.ppermute(value, 'etp', pairs)]
    ppermute x10, starting transfers between devices: 26.3 us -> 19.6 us  [over_outer(): return lax.ppermute(value, 'dp', pairs)]
  transfers between devices with their start and end apart: 35 -> 35, of which waited for: 17 -> 18; matrix products, arithmetic and copies ran while one was open for 12% -> 12% of each run, Pallas kernels for 0% -> 0%
where the time goes in v7:
time: 150 us
  waiting for transfers between devices  79.1 us (53%)
  starting transfers between devices  47.9 us (32%)
  matrix products  15.8 us (11%)
  other arithmetic  2.68 us (2%)
  Pallas kernels  1.65 us (1%)
    ppermute x10, waiting for transfers between devices, over_outer(): return lax.ppermute(value, 'dp', pairs)  50.8 us
    ppermute x10, starting transfers between devices, over_outer(): return lax.ppermute(value, 'dp', pairs)  19.6 us
    ppermute x18, waiting for transfers between devices, over_etp(): return lax.ppermute(value, 'etp', pairs)  19.1 us
    ppermute x4, starting transfers between devices, outer_pairs(): return lax.ppermute(value, 'dp', pairs)  14.6 us
    ppermute x4, waiting for transfers between devices, outer_pairs(): return lax.ppermute(value, 'dp', pairs)  9.19 us
    ppermute x18, starting transfers between devices, over_etp(): return lax.ppermute(value, 'etp', pairs)  9.16 us
    ppermute x3, starting transfers between devices, over_inner(): return lax.ppermute(value, 'dp', pairs)  4.64 us
    dot_general x1, matrix products, shards(): lax.dot_general(onehot, dx, (((0,), (0,)), ((), ())), preferred_element_t...  4 us
  transfers between devices with their start and end apart: 35, of which 18 were waited for; matrix products, arithmetic and copies ran while one was open for 12% of the time, Pallas kernels for 0%

profile of v7, /device:TPU:0, one launch (start us, length us, event | category | flops | bytes accessed | tf_op | source)
XLA Modules:
  0.0 149.5 jit_solution(2651266160925275682)
XLA Ops:
  0.6 3.0 %collective-permute-start.4 = (bf16[640,384]{1,0:T(8,128)(2,1)}, bf16[640,384]{1,0:T(8,128)(2,1)S(1)}, u32[]{:S(2)}, u32[]{:S(2)}) collective-permute-start(bf16[640,384]{1,0:T(8,128)(2,1)} %param.10), channel_id=1, source_target_pairs={{0,4},{4,0},{8,12},{12,8},{16,20},{20,16},{24,28},{28,24},{1,5},{5... | collective-permute-start | bytes 1474568 | tf_op jit(solution)/shard_map/ppermute | solution.py:73
  3.7 3.6 %convolution_convert_fusion.1 = bf16[64,5120]{1,0:T(8,128)(2,1)S(1)} fusion(bf16[512,5120]{1,0:T(8,128)(2,1)} %param.7, s32[64]{0:T(128)} %param.8), kind=kOutput, calls=%fused_computation.1 | convolution fusion | flops 335904768 | bytes 5898496 | tf_op jit(solution)/shard_map/dot_general | solution.py:123
  7.4 3.1 %collective-permute-start = (bf16[64,1280]{1,0:T(8,128)(2,1)S(1)}, bf16[64,1280]{1,0:T(8,128)(2,1)S(1)}, u32[]{:S(2)}, u32[]{:S(2)}) collective-permute-start(bf16[64,1280]{1,0:T(8,128)(2,1)S(1)} %pad_maximum_fusion.7), channel_id=1, source_target_pairs={{0,16},{4,20},{8,24},{12,28},{16,0},{20,4},{24,8},{28,12},{1,17},{... | collective-permute-start | bytes 491528 | tf_op jit(solution)/shard_map/ppermute | solution.py:69
  10.6 1.4 collective-permute-start.1
  12.3 7.8 %collective-permute-done.1 = bf16[64,1280]{1,0:T(8,128)(2,1)S(1)} collective-permute-done((bf16[64,1280]{1,0:T(8,128)(2,1)S(1)}, bf16[64,1280]{1,0:T(8,128)(2,1)S(1)}, u32[]{:S(2)}, u32[]{:S(2)}) %collective-permute-start.1) | collective-permute-done | bytes 163872 | tf_op jit(solution)/shard_map/ppermute | solution.py:69
  20.2 1.5 %collective-permute-start.2 = (bf16[64,1280]{1,0:T(8,128)(2,1)S(1)}, bf16[64,1280]{1,0:T(8,128)(2,1)S(1)}, u32[]{:S(2)}, u32[]{:S(2)}) collective-permute-start(bf16[64,1280]{1,0:T(8,128)(2,1)S(1)} %collective-permute-done.1), channel_id=1, source_target_pairs={{0,2},{1,3},{2,0},{3,1},{4,6},{5,7},{6,4},{7,5},{8,10},{9,11},{10,... | collective-permute-start | bytes 491528 | tf_op jit(solution)/shard_map/ppermute | solution.py:77
  21.7 3.8 %collective-permute-done.2 = bf16[64,1280]{1,0:T(8,128)(2,1)S(1)} collective-permute-done((bf16[64,1280]{1,0:T(8,128)(2,1)S(1)}, bf16[64,1280]{1,0:T(8,128)(2,1)S(1)}, u32[]{:S(2)}, u32[]{:S(2)}) %collective-permute-start.2) | collective-permute-done | bytes 163872 | tf_op jit(solution)/shard_map/ppermute | solution.py:77
  25.8 1.4 collective-permute-done.3
  27.9 1.6 %collective-permute-start.6 = (bf16[64,1280]{1,0:T(8,128)(2,1)S(1)}, bf16[64,1280]{1,0:T(8,128)(2,1)S(1)}, u32[]{:S(2)}, u32[]{:S(2)}) collective-permute-start(bf16[64,1280]{1,0:T(8,128)(2,1)S(1)} %collective-permute-done), channel_id=1, source_target_pairs={{0,2},{1,3},{2,0},{3,1},{4,6},{5,7},{6,4},{7,5},{8,10},{9,11},{10,... | collective-permute-start | bytes 491528 | tf_op jit(solution)/shard_map/ppermute | solution.py:77
  30.3 11.7 %collective-permute-start.8 = (bf16[256,768]{1,0:T(8,128)(2,1)S(1)}, bf16[256,768]{1,0:T(8,128)(2,1)S(1)}, u32[]{:S(2)}, u32[]{:S(2)}) collective-permute-start(bf16[256,768]{1,0:T(8,128)(2,1)S(1)} %convolution_convert_fusion.3), channel_id=1, source_target_pairs={{0,8},{4,12},{24,16},{28,20},{1,9},{5,13},{25,17},{29,21},{2,10},{... | collective-permute-start | bytes 1179656 | tf_op jit(solution)/shard_map/ppermute | solution.py:106
  42.2 1.6 %collective-permute-done.7 = bf16[128,1280]{1,0:T(8,128)(2,1)S(1)} collective-permute-done((bf16[128,1280]{1,0:T(8,128)(2,1)S(1)}, bf16[128,1280]{1,0:T(8,128)(2,1)S(1)}, u32[]{:S(2)}, u32[]{:S(2)}) %collective-permute-start.7) | collective-permute-done | bytes 327712 | tf_op jit(solution)/shard_map/ppermute | solution.py:77
  45.1 5.0 %collective-permute-done.8 = bf16[256,768]{1,0:T(8,128)(2,1)S(1)} collective-permute-done((bf16[256,768]{1,0:T(8,128)(2,1)S(1)}, bf16[256,768]{1,0:T(8,128)(2,1)S(1)}, u32[]{:S(2)}, u32[]{:S(2)}) %collective-permute-start.8) | collective-permute-done | bytes 393248 | tf_op jit(solution)/shard_map/ppermute | solution.py:106
  50.2 2.3 %collective-permute-start.18 = (bf16[256,768]{1,0:T(8,128)(2,1)S(1)}, bf16[256,768]{1,0:T(8,128)(2,1)S(1)}, u32[]{:S(2)}, u32[]{:S(2)}) collective-permute-start(bf16[256,768]{1,0:T(8,128)(2,1)S(1)} %add_convert_fusion.1), channel_id=1, source_target_pairs={{0,16},{4,20},{8,24},{12,28},{16,0},{20,4},{24,8},{28,12},{1,17},{... | collective-permute-start | bytes 1179656 | tf_op jit(solution)/shard_map/ppermute | solution.py:69
  53.1 4.7 %collective-permute-done.9 = bf16[64,1280]{1,0:T(8,128)(2,1)S(1)} collective-permute-done((bf16[64,1280]{1,0:T(8,128)(2,1)S(1)}, bf16[64,1280]{1,0:T(8,128)(2,1)S(1)}, u32[]{:S(2)}, u32[]{:S(2)}) %collective-permute-start.9) | collective-permute-done | bytes 163872 | tf_op jit(solution)/shard_map/ppermute | solution.py:77
  58.0 1.5 %collective-permute-done.10 = bf16[128,1280]{1,0:T(8,128)(2,1)S(1)} collective-permute-done((bf16[128,1280]{1,0:T(8,128)(2,1)S(1)}, bf16[128,1280]{1,0:T(8,128)(2,1)S(1)}, u32[]{:S(2)}, u32[]{:S(2)}) %collective-permute-start.10) | collective-permute-done | bytes 327712 | tf_op jit(solution)/shard_map/ppermute | solution.py:77
  61.9 1.9 %collective-permute-done.11 = bf16[64]{0:T(256)(128)(2,1)S(1)} collective-permute-done((bf16[64]{0:T(256)(128)(2,1)S(1)}, bf16[64]{0:T(256)(128)(2,1)S(1)}, u32[]{:S(2)}, u32[]{:S(2)}) %collective-permute-start.11) | collective-permute-done | bytes 160 | tf_op jit(solution)/shard_map/ppermute | solution.py:77
  65.2 4.1 %collective-permute-done.18.refs_2_ = bf16[256,768]{1,0:T(8,128)(2,1)S(1)} collective-permute-done((bf16[256,768]{1,0:T(8,128)(2,1)S(1)}, bf16[256,768]{1,0:T(8,128)(2,1)S(1)}, u32[]{:S(2)}, u32[]{:S(2)}) %collective-permute-start.18) | collective-permute-done | bytes 393248 | tf_op jit(solution)/shard_map/ppermute | solution.py:69
  69.4 8.3 %collective-permute-done.17.refs_1_ = bf16[256,768]{1,0:T(8,128)(2,1)S(1)} collective-permute-done((bf16[256,768]{1,0:T(8,128)(2,1)S(1)}, bf16[256,768]{1,0:T(8,128)(2,1)S(1)}, u32[]{:S(2)}, u32[]{:S(2)}) %collective-permute-start.17) | collective-permute-done | bytes 393248 | tf_op jit(solution)/shard_map/ppermute | solution.py:69
  77.7 1.7 %shard_map.102 = (bf16[256,384]{1,0:T(8,128)(2,1)}, bf16[256,768]{1,0:T(8,128)(2,1)S(1)}) custom-call(s32[4]{0:T(128)S(1)} %broadcast_xor_fusion.order_ref, f32[256,768]{1,0:T(8,128)S(1)} %fusion.27.pre_ref, bf16[256,1]{1,0:T(8,128)(2,1)S(1)} %broadcast_in_dim.10.prob_ref, bf16[256,384]{1,0:T(8,128)(2,1)S(1)} %copy-done, ...), custom_call_target="tpu_custom_call" | custom-call | flops 1966080 | bytes 2949120 | tf_op jit(solution)/shard_map/pallas_call | solution.py:49
  79.5 2.8 %collective-permute-start.25 = (bf16[256,768]{1,0:T(8,128)(2,1)S(1)}, bf16[256,768]{1,0:T(8,128)(2,1)S(1)}, u32[]{:S(2)}, u32[]{:S(2)}) collective-permute-start(bf16[256,768]{1,0:T(8,128)(2,1)S(1)} %get-tuple-element.38), channel_id=1, source_target_pairs={{0,16},{4,20},{8,24},{12,28},{16,0},{20,4},{24,8},{28,12},{1,17},{... | collective-permute-start | bytes 1179656 | tf_op jit(solution)/shard_map/ppermute | solution.py:69
  82.3 15.9 %collective-permute-done.19 = bf16[256,768]{1,0:T(8,128)(2,1)S(1)} collective-permute-done((bf16[256,768]{1,0:T(8,128)(2,1)S(1)}, bf16[256,768]{1,0:T(8,128)(2,1)S(1)}, u32[]{:S(2)}, u32[]{:S(2)}) %collective-permute-start.19) | collective-permute-done | bytes 393248 | tf_op jit(solution)/shard_map/ppermute | solution.py:69
  105.4 1.6 %collective-permute-start.23 = (bf16[64,1280]{1,0:T(8,128)(2,1)S(1)}, bf16[64,1280]{1,0:T(8,128)(2,1)S(1)}, u32[]{:S(2)}, u32[]{:S(2)}) collective-permute-start(bf16[64,1280]{1,0:T(8,128)(2,1)S(1)} %slice.232), channel_id=1, source_target_pairs={{0,2},{1,3},{2,0},{3,1},{4,6},{5,7},{6,4},{7,5},{8,10},{9,11},{10,... | collective-permute-start | bytes 491528 | tf_op jit(solution)/shard_map/ppermute | solution.py:77
  107.7 4.2 %collective-permute-done.30 = bf16[256,768]{1,0:T(8,128)(2,1)S(1)} collective-permute-done((bf16[256,768]{1,0:T(8,128)(2,1)S(1)}, bf16[256,768]{1,0:T(8,128)(2,1)S(1)}, u32[]{:S(2)}, u32[]{:S(2)}) %collective-permute-start.30) | collective-permute-done | bytes 393248 | tf_op jit(solution)/shard_map/ppermute | solution.py:106
  112.4 1.6 %collective-permute-start.34 = (bf16[640,768]{1,0:T(8,128)(2,1)S(1)}, bf16[640,768]{1,0:T(8,128)(2,1)S(1)}, u32[]{:S(2)}, u32[]{:S(2)}) collective-permute-start(bf16[640,768]{1,0:T(8,128)(2,1)S(1)} %add_convert_fusion), channel_id=1, source_target_pairs={{0,4},{4,0},{8,12},{12,8},{16,20},{20,16},{24,28},{28,24},{1,5},{5... | collective-permute-start | bytes 2949128 | tf_op jit(solution)/shard_map/ppermute | solution.py:73
  116.3 6.4 %collective-permute-start.24 = (bf16[64,1280]{1,0:T(8,128)(2,1)S(1)}, bf16[64,1280]{1,0:T(8,128)(2,1)S(1)}, u32[]{:S(2)}, u32[]{:S(2)}) collective-permute-start(bf16[64,1280]{1,0:T(8,128)(2,1)S(1)} %fusion.17), channel_id=1, source_target_pairs={{0,8},{4,12},{8,0},{12,4},{16,24},{20,28},{24,16},{28,20},{1,9},{5... | collective-permute-start | bytes 491528 | tf_op jit(solution)/shard_map/ppermute | solution.py:69
  124.0 6.5 %collective-permute-done.24 = bf16[64,1280]{1,0:T(8,128)(2,1)S(1)} collective-permute-done((bf16[64,1280]{1,0:T(8,128)(2,1)S(1)}, bf16[64,1280]{1,0:T(8,128)(2,1)S(1)}, u32[]{:S(2)}, u32[]{:S(2)}) %collective-permute-start.24) | collective-permute-done | bytes 163872 | tf_op jit(solution)/shard_map/ppermute | solution.py:69
  131.2 2.3 %collective-permute-done.28 = bf16[64,1280]{1,0:T(8,128)(2,1)S(1)} collective-permute-done((bf16[64,1280]{1,0:T(8,128)(2,1)S(1)}, bf16[64,1280]{1,0:T(8,128)(2,1)S(1)}, u32[]{:S(2)}, u32[]{:S(2)}) %collective-permute-start.28) | collective-permute-done | bytes 163872 | tf_op jit(solution)/shard_map/ppermute | solution.py:69
  133.5 3.2 %collective-permute-done.32 = bf16[64,1280]{1,0:T(8,128)(2,1)S(1)} collective-permute-done((bf16[64,1280]{1,0:T(8,128)(2,1)S(1)}, bf16[64,1280]{1,0:T(8,128)(2,1)S(1)}, u32[]{:S(2)}, u32[]{:S(2)}) %collective-permute-start.32) | collective-permute-done | bytes 163872 | tf_op jit(solution)/shard_map/ppermute | solution.py:77
  136.8 1.7 %collective-permute-start.33 = (bf16[64,1280]{1,0:T(8,128)(2,1)S(1)}, bf16[64,1280]{1,0:T(8,128)(2,1)S(1)}, u32[]{:S(2)}, u32[]{:S(2)}) collective-permute-start(bf16[64,1280]{1,0:T(8,128)(2,1)S(1)} %fusion.14), channel_id=1, source_target_pairs={{0,24},{4,28},{8,16},{12,20},{16,8},{20,12},{24,0},{28,4},{1,25},{... | collective-permute-start | bytes 491528 | tf_op jit(solution)/shard_map/ppermute | solution.py:69
  138.5 5.6 %collective-permute-done.33 = bf16[64,1280]{1,0:T(8,128)(2,1)S(1)} collective-permute-done((bf16[64,1280]{1,0:T(8,128)(2,1)S(1)}, bf16[64,1280]{1,0:T(8,128)(2,1)S(1)}, u32[]{:S(2)}, u32[]{:S(2)}) %collective-permute-start.33) | collective-permute-done | bytes 163872 | tf_op jit(solution)/shard_map/ppermute | solution.py:69
  144.1 4.0 %convolution_convert_fusion = bf16[512,5120]{1,0:T(8,128)(2,1)} fusion(bf16[64,5120]{1,0:T(8,128)(2,1)S(1)} %slice_dynamic-update-slice_fusion, s32[64]{0:T(128)S(1)} %copy-done.3), kind=kOutput, calls=%fused_computation | convolution fusion | flops 338198528 | bytes 5898496 | tf_op jit(solution)/shard_map/dot_general | solution.py:227
  148.1 1.4 slice_add_fusion
  (124 shorter events, 21.0 us)
Async XLA Ops:
  0.6 25.0 %collective-permute-start.4 = (bf16[640,384]{1,0:T(8,128)(2,1)}, bf16[640,384]{1,0:T(8,128)(2,1)S(1)}, u32[]{:S(2)}, u32[]{:S(2)}) collective-permute-start(bf16[640,384]{1,0:T(8,128)(2,1)} %param.10), channel_id=1, source_target_pairs={{0,4},{4,0},{8,12},{12,8},{16,20},{20,16},{24,28},{28,24},{1,5},{5... | collective-permute-start | bytes 1474568 | tf_op jit(solution)/shard_map/ppermute | solution.py:73
  3.6 22.0 %collective-permute-start.5 = (bf16[640,384]{1,0:T(8,128)(2,1)}, bf16[640,384]{1,0:T(8,128)(2,1)S(1)}, u32[]{:S(2)}, u32[]{:S(2)}) collective-permute-start(bf16[640,384]{1,0:T(8,128)(2,1)} %param.11), channel_id=1, source_target_pairs={{0,4},{4,0},{8,12},{12,8},{16,20},{20,16},{24,28},{28,24},{1,5},{5... | collective-permute-start | bytes 1474568 | tf_op jit(solution)/shard_map/ppermute | solution.py:73
  7.4 20.5 %collective-permute-start = (bf16[64,1280]{1,0:T(8,128)(2,1)S(1)}, bf16[64,1280]{1,0:T(8,128)(2,1)S(1)}, u32[]{:S(2)}, u32[]{:S(2)}) collective-permute-start(bf16[64,1280]{1,0:T(8,128)(2,1)S(1)} %pad_maximum_fusion.7), channel_id=1, source_target_pairs={{0,16},{4,20},{8,24},{12,28},{16,0},{20,4},{24,8},{28,12},{1,17},{... | collective-permute-start | bytes 491528 | tf_op jit(solution)/shard_map/ppermute | solution.py:69
  10.6 9.6 %collective-permute-start.1 = (bf16[64,1280]{1,0:T(8,128)(2,1)S(1)}, bf16[64,1280]{1,0:T(8,128)(2,1)S(1)}, u32[]{:S(2)}, u32[]{:S(2)}) collective-permute-start(bf16[64,1280]{1,0:T(8,128)(2,1)S(1)} %pad_maximum_fusion.8), channel_id=1, source_target_pairs={{0,24},{4,28},{8,16},{12,20},{16,8},{20,12},{24,0},{28,4},{1,25},{... | collective-permute-start | bytes 491528 | tf_op jit(solution)/shard_map/ppermute | solution.py:69
  12.0 32.5 %collective-permute-start.14 = (bf16[64,1280]{1,0:T(8,128)(2,1)S(1)}, bf16[64,1280]{1,0:T(8,128)(2,1)S(1)}, u32[]{:S(2)}, u32[]{:S(2)}) collective-permute-start(bf16[64,1280]{1,0:T(8,128)(2,1)S(1)} %pad_maximum_fusion.9), channel_id=1, source_target_pairs={{0,8},{4,12},{8,0},{12,4},{16,24},{20,28},{24,16},{28,20},{1,9},{5... | collective-permute-start | bytes 491528 | tf_op jit(solution)/shard_map/ppermute | solution.py:69
  20.2 5.3 %collective-permute-start.2 = (bf16[64,1280]{1,0:T(8,128)(2,1)S(1)}, bf16[64,1280]{1,0:T(8,128)(2,1)S(1)}, u32[]{:S(2)}, u32[]{:S(2)}) collective-permute-start(bf16[64,1280]{1,0:T(8,128)(2,1)S(1)} %collective-permute-done.1), channel_id=1, source_target_pairs={{0,2},{1,3},{2,0},{3,1},{4,6},{5,7},{6,4},{7,5},{8,10},{9,11},{10,... | collective-permute-start | bytes 491528 | tf_op jit(solution)/shard_map/ppermute | solution.py:77
  25.5 1.7 %collective-permute-start.3 = (bf16[128,1280]{1,0:T(8,128)(2,1)S(1)}, bf16[128,1280]{1,0:T(8,128)(2,1)S(1)}, u32[]{:S(2)}, u32[]{:S(2)}) collective-permute-start(bf16[128,1280]{1,0:T(8,128)(2,1)S(1)} %pad_maximum_fusion.2), channel_id=1, source_target_pairs={{0,1},{1,0},{2,3},{3,2},{4,5},{5,4},{6,7},{7,6},{8,9},{9,8},{10,11... | collective-permute-start | bytes 983048 | tf_op jit(solution)/shard_map/ppermute | solution.py:77
  27.9 14.1 %collective-permute-start.6 = (bf16[64,1280]{1,0:T(8,128)(2,1)S(1)}, bf16[64,1280]{1,0:T(8,128)(2,1)S(1)}, u32[]{:S(2)}, u32[]{:S(2)}) collective-permute-start(bf16[64,1280]{1,0:T(8,128)(2,1)S(1)} %collective-permute-done), channel_id=1, source_target_pairs={{0,2},{1,3},{2,0},{3,1},{4,6},{5,7},{6,4},{7,5},{8,10},{9,11},{10,... | collective-permute-start | bytes 491528 | tf_op jit(solution)/shard_map/ppermute | solution.py:77
  29.6 34.4 %collective-permute-start.13 = (bf16[256,768]{1,0:T(8,128)(2,1)S(1)}, bf16[256,768]{1,0:T(8,128)(2,1)S(1)}, u32[]{:S(2)}, u32[]{:S(2)}) collective-permute-start(bf16[256,768]{1,0:T(8,128)(2,1)S(1)} %convolution_convert_fusion.3), channel_id=1, source_target_pairs={{8,16},{12,20},{16,8},{20,12},{9,17},{13,21},{17,9},{21,13},{10,18... | collective-permute-start | bytes 1179656 | tf_op jit(solution)/shard_map/ppermute | solution.py:106
  30.3 19.8 %collective-permute-start.8 = (bf16[256,768]{1,0:T(8,128)(2,1)S(1)}, bf16[256,768]{1,0:T(8,128)(2,1)S(1)}, u32[]{:S(2)}, u32[]{:S(2)}) collective-permute-start(bf16[256,768]{1,0:T(8,128)(2,1)S(1)} %convolution_convert_fusion.3), channel_id=1, source_target_pairs={{0,8},{4,12},{24,16},{28,20},{1,9},{5,13},{25,17},{29,21},{2,10},{... | collective-permute-start | bytes 1179656 | tf_op jit(solution)/shard_map/ppermute | solution.py:106
  44.5 8.5 %collective-permute-start.15 = (bf16[64,1280]{1,0:T(8,128)(2,1)S(1)}, bf16[64,1280]{1,0:T(8,128)(2,1)S(1)}, u32[]{:S(2)}, u32[]{:S(2)}) collective-permute-start(bf16[64,1280]{1,0:T(8,128)(2,1)S(1)} %collective-permute-done.14), channel_id=1, source_target_pairs={{0,2},{1,3},{2,0},{3,1},{4,6},{5,7},{6,4},{7,5},{8,10},{9,11},{10,... | collective-permute-start | bytes 491528 | tf_op jit(solution)/shard_map/ppermute | solution.py:77
  50.2 19.2 %collective-permute-start.18 = (bf16[256,768]{1,0:T(8,128)(2,1)S(1)}, bf16[256,768]{1,0:T(8,128)(2,1)S(1)}, u32[]{:S(2)}, u32[]{:S(2)}) collective-permute-start(bf16[256,768]{1,0:T(8,128)(2,1)S(1)} %add_convert_fusion.1), channel_id=1, source_target_pairs={{0,16},{4,20},{8,24},{12,28},{16,0},{20,4},{24,8},{28,12},{1,17},{... | collective-permute-start | bytes 1179656 | tf_op jit(solution)/shard_map/ppermute | solution.py:69
  52.5 5.3 %collective-permute-start.9 = (bf16[64,1280]{1,0:T(8,128)(2,1)S(1)}, bf16[64,1280]{1,0:T(8,128)(2,1)S(1)}, u32[]{:S(2)}, u32[]{:S(2)}) collective-permute-start(bf16[64,1280]{1,0:T(8,128)(2,1)S(1)} %pad_maximum_fusion.6), channel_id=1, source_target_pairs={{0,2},{1,3},{2,0},{3,1},{4,6},{5,7},{6,4},{7,5},{8,10},{9,11},{10,... | collective-permute-start | bytes 491528 | tf_op jit(solution)/shard_map/ppermute | solution.py:77
  53.0 4.9 %collective-permute-start.16 = (bf16[128,1280]{1,0:T(8,128)(2,1)S(1)}, bf16[128,1280]{1,0:T(8,128)(2,1)S(1)}, u32[]{:S(2)}, u32[]{:S(2)}) collective-permute-start(bf16[128,1280]{1,0:T(8,128)(2,1)S(1)} %pad_maximum_fusion.5), channel_id=1, source_target_pairs={{0,1},{1,0},{2,3},{3,2},{4,5},{5,4},{6,7},{7,6},{8,9},{9,8},{10,11... | collective-permute-start | bytes 983048 | tf_op jit(solution)/shard_map/ppermute | solution.py:77
  60.2 3.6 %collective-permute-start.11 = (bf16[64]{0:T(256)(128)(2,1)S(1)}, bf16[64]{0:T(256)(128)(2,1)S(1)}, u32[]{:S(2)}, u32[]{:S(2)}) collective-permute-start(bf16[64]{0:T(256)(128)(2,1)S(1)} %copy-done.4), channel_id=1, source_target_pairs={{0,2},{1,3},{2,0},{3,1},{4,6},{5,7},{6,4},{7,5},{8,10},{9,11},{10,... | collective-permute-start | bytes 392 | tf_op jit(solution)/shard_map/ppermute | solution.py:77
  61.5 16.2 %collective-permute-start.17 = (bf16[256,768]{1,0:T(8,128)(2,1)S(1)}, bf16[256,768]{1,0:T(8,128)(2,1)S(1)}, u32[]{:S(2)}, u32[]{:S(2)}) collective-permute-start(bf16[256,768]{1,0:T(8,128)(2,1)S(1)} %convolution_convert_fusion.2), channel_id=1, source_target_pairs={{0,8},{4,12},{8,0},{12,4},{16,24},{20,28},{24,16},{28,20},{1,9},{5... | collective-permute-start | bytes 1179656 | tf_op jit(solution)/shard_map/ppermute | solution.py:69
  79.3 18.9 %collective-permute-start.19 = (bf16[256,768]{1,0:T(8,128)(2,1)S(1)}, bf16[256,768]{1,0:T(8,128)(2,1)S(1)}, u32[]{:S(2)}, u32[]{:S(2)}) collective-permute-start(bf16[256,768]{1,0:T(8,128)(2,1)S(1)} %get-tuple-element.38), channel_id=1, source_target_pairs={{0,8},{4,12},{8,0},{12,4},{16,24},{20,28},{24,16},{28,20},{1,9},{5... | collective-permute-start | bytes 1179656 | tf_op jit(solution)/shard_map/ppermute | solution.py:69
  79.5 20.5 %collective-permute-start.25 = (bf16[256,768]{1,0:T(8,128)(2,1)S(1)}, bf16[256,768]{1,0:T(8,128)(2,1)S(1)}, u32[]{:S(2)}, u32[]{:S(2)}) collective-permute-start(bf16[256,768]{1,0:T(8,128)(2,1)S(1)} %get-tuple-element.38), channel_id=1, source_target_pairs={{0,16},{4,20},{8,24},{12,28},{16,0},{20,4},{24,8},{28,12},{1,17},{... | collective-permute-start | bytes 1179656 | tf_op jit(solution)/shard_map/ppermute | solution.py:69
  99.9 11.9 %collective-permute-start.30 = (bf16[256,768]{1,0:T(8,128)(2,1)S(1)}, bf16[256,768]{1,0:T(8,128)(2,1)S(1)}, u32[]{:S(2)}, u32[]{:S(2)}) collective-permute-start(bf16[256,768]{1,0:T(8,128)(2,1)S(1)} %collective-permute-done.25), channel_id=1, source_target_pairs={{16,24},{20,28},{8,0},{12,4},{17,25},{21,29},{9,1},{13,5},{18,26},... | collective-permute-start | bytes 1179656 | tf_op jit(solution)/shard_map/ppermute | solution.py:106
  101.9 2.7 %collective-permute-start.20 = (bf16[128,1280]{1,0:T(8,128)(2,1)S(1)}, bf16[128,1280]{1,0:T(8,128)(2,1)S(1)}, u32[]{:S(2)}, u32[]{:S(2)}) collective-permute-start(bf16[128,1280]{1,0:T(8,128)(2,1)S(1)} %slice.229), channel_id=1, source_target_pairs={{0,1},{1,0},{2,3},{3,2},{4,5},{5,4},{6,7},{7,6},{8,9},{9,8},{10,11... | collective-permute-start | bytes 983048 | tf_op jit(solution)/shard_map/ppermute | solution.py:77
  102.0 3.3 %collective-permute-start.22 = (bf16[128,1280]{1,0:T(8,128)(2,1)S(1)}, bf16[128,1280]{1,0:T(8,128)(2,1)S(1)}, u32[]{:S(2)}, u32[]{:S(2)}) collective-permute-start(bf16[128,1280]{1,0:T(8,128)(2,1)S(1)} %slice.228), channel_id=1, source_target_pairs={{0,1},{1,0},{2,3},{3,2},{4,5},{5,4},{6,7},{7,6},{8,9},{9,8},{10,11... | collective-permute-start | bytes 983048 | tf_op jit(solution)/shard_map/ppermute | solution.py:77
  102.5 9.3 %collective-permute-start.29 = (bf16[256,768]{1,0:T(8,128)(2,1)S(1)}, bf16[256,768]{1,0:T(8,128)(2,1)S(1)}, u32[]{:S(2)}, u32[]{:S(2)}) collective-permute-start(bf16[256,768]{1,0:T(8,128)(2,1)S(1)} %get-tuple-element.38), channel_id=1, source_target_pairs={{8,16},{12,20},{16,8},{20,12},{9,17},{13,21},{17,9},{21,13},{10,18... | collective-permute-start | bytes 1179656 | tf_op jit(solution)/shard_map/ppermute | solution.py:106
  103.5 3.5 %collective-permute-start.26 = (bf16[128,1280]{1,0:T(8,128)(2,1)S(1)}, bf16[128,1280]{1,0:T(8,128)(2,1)S(1)}, u32[]{:S(2)}, u32[]{:S(2)}) collective-permute-start(bf16[128,1280]{1,0:T(8,128)(2,1)S(1)} %slice.227), channel_id=1, source_target_pairs={{0,1},{1,0},{2,3},{3,2},{4,5},{5,4},{6,7},{7,6},{8,9},{9,8},{10,11... | collective-permute-start | bytes 983048 | tf_op jit(solution)/shard_map/ppermute | solution.py:77
  104.8 19.1 %collective-permute-start.21 = (bf16[64,1280]{1,0:T(8,128)(2,1)S(1)}, bf16[64,1280]{1,0:T(8,128)(2,1)S(1)}, u32[]{:S(2)}, u32[]{:S(2)}) collective-permute-start(bf16[64,1280]{1,0:T(8,128)(2,1)S(1)} %slice.233), channel_id=1, source_target_pairs={{0,2},{1,3},{2,0},{3,1},{4,6},{5,7},{6,4},{7,5},{8,10},{9,11},{10,... | collective-permute-start | bytes 491528 | tf_op jit(solution)/shard_map/ppermute | solution.py:77
  105.4 10.8 %collective-permute-start.23 = (bf16[64,1280]{1,0:T(8,128)(2,1)S(1)}, bf16[64,1280]{1,0:T(8,128)(2,1)S(1)}, u32[]{:S(2)}, u32[]{:S(2)}) collective-permute-start(bf16[64,1280]{1,0:T(8,128)(2,1)S(1)} %slice.232), channel_id=1, source_target_pairs={{0,2},{1,3},{2,0},{3,1},{4,6},{5,7},{6,4},{7,5},{8,10},{9,11},{10,... | collective-permute-start | bytes 491528 | tf_op jit(solution)/shard_map/ppermute | solution.py:77
  107.1 15.5 %collective-permute-start.27 = (bf16[64,1280]{1,0:T(8,128)(2,1)S(1)}, bf16[64,1280]{1,0:T(8,128)(2,1)S(1)}, u32[]{:S(2)}, u32[]{:S(2)}) collective-permute-start(bf16[64,1280]{1,0:T(8,128)(2,1)S(1)} %slice.231), channel_id=1, source_target_pairs={{0,2},{1,3},{2,0},{3,1},{4,6},{5,7},{6,4},{7,5},{8,10},{9,11},{10,... | collective-permute-start | bytes 491528 | tf_op jit(solution)/shard_map/ppermute | solution.py:77
  112.4 35.7 %collective-permute-start.34 = (bf16[640,768]{1,0:T(8,128)(2,1)S(1)}, bf16[640,768]{1,0:T(8,128)(2,1)S(1)}, u32[]{:S(2)}, u32[]{:S(2)}) collective-permute-start(bf16[640,768]{1,0:T(8,128)(2,1)S(1)} %add_convert_fusion), channel_id=1, source_target_pairs={{0,4},{4,0},{8,12},{12,8},{16,20},{20,16},{24,28},{28,24},{1,5},{5... | collective-permute-start | bytes 2949128 | tf_op jit(solution)/shard_map/ppermute | solution.py:73
  114.7 15.8 %collective-permute-start.31 = (bf16[128,1280]{1,0:T(8,128)(2,1)S(1)}, bf16[128,1280]{1,0:T(8,128)(2,1)S(1)}, u32[]{:S(2)}, u32[]{:S(2)}) collective-permute-start(bf16[128,1280]{1,0:T(8,128)(2,1)S(1)} %slice.226), channel_id=1, source_target_pairs={{0,1},{1,0},{2,3},{3,2},{4,5},{5,4},{6,7},{7,6},{8,9},{9,8},{10,11... | collective-permute-start | bytes 983048 | tf_op jit(solution)/shard_map/ppermute | solution.py:77
  116.3 14.3 %collective-permute-start.24 = (bf16[64,1280]{1,0:T(8,128)(2,1)S(1)}, bf16[64,1280]{1,0:T(8,128)(2,1)S(1)}, u32[]{:S(2)}, u32[]{:S(2)}) collective-permute-start(bf16[64,1280]{1,0:T(8,128)(2,1)S(1)} %fusion.17), channel_id=1, source_target_pairs={{0,8},{4,12},{8,0},{12,4},{16,24},{20,28},{24,16},{28,20},{1,9},{5... | collective-permute-start | bytes 491528 | tf_op jit(solution)/shard_map/ppermute | solution.py:69
  122.7 10.8 %collective-permute-start.28 = (bf16[64,1280]{1,0:T(8,128)(2,1)S(1)}, bf16[64,1280]{1,0:T(8,128)(2,1)S(1)}, u32[]{:S(2)}, u32[]{:S(2)}) collective-permute-start(bf16[64,1280]{1,0:T(8,128)(2,1)S(1)} %fusion.16), channel_id=1, source_target_pairs={{0,16},{4,20},{8,24},{12,28},{16,0},{20,4},{24,8},{28,12},{1,17},{... | collective-permute-start | bytes 491528 | tf_op jit(solution)/shard_map/ppermute | solution.py:69
  130.7 6.1 %collective-permute-start.32 = (bf16[64,1280]{1,0:T(8,128)(2,1)S(1)}, bf16[64,1280]{1,0:T(8,128)(2,1)S(1)}, u32[]{:S(2)}, u32[]{:S(2)}) collective-permute-start(bf16[64,1280]{1,0:T(8,128)(2,1)S(1)} %slice.230), channel_id=1, source_target_pairs={{0,2},{1,3},{2,0},{3,1},{4,6},{5,7},{6,4},{7,5},{8,10},{9,11},{10,... | collective-permute-start | bytes 491528 | tf_op jit(solution)/shard_map/ppermute | solution.py:77
  136.8 7.2 %collective-permute-start.33 = (bf16[64,1280]{1,0:T(8,128)(2,1)S(1)}, bf16[64,1280]{1,0:T(8,128)(2,1)S(1)}, u32[]{:S(2)}, u32[]{:S(2)}) collective-permute-start(bf16[64,1280]{1,0:T(8,128)(2,1)S(1)} %fusion.14), channel_id=1, source_target_pairs={{0,24},{4,28},{8,16},{12,20},{16,8},{20,12},{24,0},{28,4},{1,25},{... | collective-permute-start | bytes 491528 | tf_op jit(solution)/shard_map/ppermute | solution.py:69
  (9 other events, 84.8 us)

commit v8 on v7

--- a/solution.py
+++ b/solution.py
@@ -105,14 +105,25 @@
         pairs = [(s * inner + i, t * inner + i) for s, t in pairs for i in range(inner)]
         return lax.ppermute(value, "dp", pairs)
 
+    swap = [(0, 1), (1, 0), (2, 3), (3, 2)]
+    cycle = [(0, 2), (2, 3), (3, 1), (1, 0)]
+    back = [(t, s) for s, t in cycle]
+    middle = [(1, 2), (2, 1)]
+    inward = [(0, 2), (3, 1)]
+    outward = [(2, 0), (1, 3)]
+
     def shards(tokens, slots, gate_probs, w_gate, w_up, d_hidden):
         dp = lax.axis_index("dp")
         etp = lax.axis_index("etp")
         a, b = dp // inner, dp % inner
+        at_end = (a == 0) | (a == outer - 1)
         depth, width = w_gate.shape
         cap = slots.shape[0]
         tok = tokens.shape[0]
         span = depth * inner
+
+        def pick(first, second):
+            return jnp.where(at_end, first, second)
 
         weights = [jnp.concatenate([w_gate, w_up], axis=1)]
         for j in range(1, inner):
@@ -128,57 +139,48 @@
                 for j in range(inner)
             ]
             pieces[k] = jnp.concatenate(blocks, axis=1)
-        got = {}
-        for k in far_first:
-            got[k] = over_outer(pieces[k], k)
+        got = {k: over_outer(pieces[k], k) for k in far_first}
+        if relay:
+            got[3], got[1] = pick(got[3], got[1]), pick(got[1], got[3])
         got[0] = pieces[0]
 
-        x_chunks, products = {}, {}
+        x_chunks = {}
 
         def multiply(k, last):
-            return jnp.dot(after(x_chunks[k], last), weights, preferred_element_type=F32)
-
-        if relay:
-            x_chunks[3] = gather_etp(got[3])
+            x_chunks[k] = gather_etp(after(got[k], last))
+            return jnp.dot(x_chunks[k], weights, preferred_element_type=F32)
+
+        if relay:
             far = multiply(3, rows).astype(BF16)
-            carried = outer_pairs(far, [(0, 1), (3, 2)])
-            middle = outer_pairs(far, [(1, 2), (2, 1)])
-            x_chunks[2] = gather_etp(after(got[2], far))
-            product = multiply(2, far)
-            x_chunks[1] = gather_etp(after(got[1], product))
-            summed = (product + carried.astype(F32)).astype(BF16)
-            two = over_outer(summed, 2)
-            one = over_outer(multiply(1, summed).astype(BF16), 1)
-            x_chunks[0] = gather_etp(after(got[0], summed))
-            own = multiply(0, summed)
-            parts = [after(middle, own), one, two]
+            swapped = outer_pairs(far, swap)
+            near = after(multiply(1, rows).astype(BF16), far)
+            crossed = outer_pairs(near, middle)
+            two = after(multiply(2, near), near)
+            inwards = outer_pairs(after(two.astype(BF16), near), inward)
+            own = multiply(0, two)
+            relayed = pick(near, (two + swapped.astype(F32)).astype(BF16))
+            cycled = outer_pairs(relayed, back)
+            own = own + crossed.astype(F32) + inwards.astype(F32)
+            own = own + jnp.where(at_end, swapped.astype(F32), 0.0)
+            parts = [cycled]
         else:
             last, parts = rows, []
             for k in far_first:
-                x_chunks[k] = gather_etp(after(got[k], last))
                 last = multiply(k, last).astype(BF16)
                 parts.append(over_outer(last, k))
-            x_chunks[0] = gather_etp(after(got[0], last))
             own = multiply(0, last)
-        probs = gather_etp(after(gate_probs, own))
+        probs = gather_etp(after(gate_probs, x_chunks[0]))
         order = etp ^ jnp.array(chunk_order, jnp.int32)
         hidden, paired = gate_call(order, own, probs[:, None], d_hidden, parts)
 
-        grads = {0: paired}
-        if relay:
-            grads[2] = over_outer(paired, 2)
-            grads[1] = over_outer(paired, 1)
-        else:
-            for k in near_first:
-                grads[k] = over_outer(paired, k)
-        sums, partials = {}, {}
+        grads, sums = {0: paired}, {}
 
         def advance(k, last):
-            partials[k] = lax.dot_general(
+            partial = lax.dot_general(
                 after(grads[k], last), weights, (((1,), (1,)), ((), ())), preferred_element_type=F32
             )
-            sums[k] = reduce_etp(partials[k]).astype(BF16)
-            return partials[k]
+            sums[k] = reduce_etp(partial).astype(BF16)
+            return partial
 
         def weight_grad(ks, j, last):
             x_part = jnp.concatenate([x_chunks[k][:, j * depth : (j + 1) * depth] for k in ks], axis=0)
@@ -187,40 +189,50 @@
                 x_part, after(grad_part, last), (((0,), (0,)), ((), ())), preferred_element_type=F32
             )
 
-        early, late = keys[: max(outer - 1, 1)], keys[max(outer - 1, 1) :]
-        last = grads[near_first[0]] if outer > 1 else paired
-        for k in [0] + near_first[:1]:
-            last = advance(k, last)
-        if relay:
-            turn = after(grads[2], last)
-            ends = outer_pairs(turn, [(2, 3), (1, 0)])
-            middle = outer_pairs(after(paired, turn), [(1, 2), (2, 1)])
-            last = advance(2, last)
-            early_sums = [weight_grad(early, j, last) for j in range(1, inner)]
-            grads[3] = middle + after(ends, *early_sums)
+        if relay:
+            cycled = outer_pairs(paired, cycle)
+            last = advance(0, paired)
+            crossed = outer_pairs(after(paired, last), middle)
+            outwards = outer_pairs(after(paired, sums[0]), outward)
+            turn = after(pick(paired, cycled), paired)
+            grads[3] = outer_pairs(turn, swap)
+            grads[1] = pick(after(cycled, turn), crossed)
+            grads[2] = pick(outwards, after(cycled, grads[1]))
+            sequence = [0, 1, 3, 2]
+            last = turn
         else:
-            for k in early[2:]:
-                last = advance(k, last)
-            early_sums = [weight_grad(early, j, last) for j in range(1, inner)]
-
-        leaving = [
-            ((early_sums[j - 1] + weight_grad(late, j, grads[late[-1]])) if late else early_sums[j - 1])
-            for j in range(1, inner)
-        ]
-        leaving = [v.astype(BF16) for v in leaving]
+            for k in near_first:
+                grads[k] = over_outer(paired, k)
+            sequence = keys
+            last = grads[near_first[0]] if outer > 1 else paired
+        early, late = sequence[: max(outer - 1, 1)], sequence[max(outer - 1, 1) :]
+        for k in early:
+            last = advance(k, last) if k not in sums else last
+
+        leaving = []
+        for j in range(1, inner):
+            value = weight_grad(early, j, last)
+            for k in late:
+                value = after(value, last) + weight_grad([k], j, value)
+            leaving.append(value.astype(BF16))
         arriving = [over_inner(leaving[j - 1], j) for j in range(1, inner)]
         last = leaving[0] if inner > 1 else last
         for k in late:
             last = advance(k, last)
-        total = weight_grad(keys, 0, last)
+        total = weight_grad(sequence, 0, last)
         gate_total, up_total = total[:, :width], total[:, width:]
         for part in arriving:
             gate_total = gate_total + part[:, :width].astype(F32)
             up_total = up_total + part[:, width:].astype(F32)
 
+        last = sums[sequence[-1]]
+        if relay:
+            sums[3], sums[1] = pick(sums[3], sums[1]), pick(sums[1], sums[3])
         dx = jnp.zeros((cap, outer * span), BF16)
         for k in keys:
             own = over_outer(sums[k], k) if k else sums[k]
+            if k != sequence[-1]:
+                own = after(own, last)
             for j in range(inner):
                 block = own[:, j * depth : (j + 1) * depth]
                 dx = lax.dynamic_update_slice(dx, block, (0, (a ^ k) * span + (b ^ j) * depth))

time: 150 us -> 142 us (0.947)
  starting transfers between devices: 47.9 us -> 38 us
  waiting for transfers between devices: 79.1 us -> 81.4 us
    ppermute x10 -> x6, waiting for transfers between devices: 50.8 us -> 16.7 us  [over_outer(): return lax.ppermute(value, 'dp', pairs)]
    ppermute x4 -> x8, waiting for transfers between devices: 9.19 us -> 36.9 us  [outer_pairs(): return lax.ppermute(value, 'dp', pairs)]
    ppermute x10 -> x6, starting transfers between devices: 19.6 us -> 9.92 us  [over_outer(): return lax.ppermute(value, 'dp', pairs)]
    ppermute x3, waiting for transfers between devices: 0.01 us -> 6.7 us  [over_inner(): return lax.ppermute(value, 'dp', pairs)]
    ppermute x18, starting transfers between devices: 9.16 us -> 12.8 us  [over_etp(): return lax.ppermute(value, 'etp', pairs)]
    ppermute x4 -> x8, starting transfers between devices: 14.6 us -> 11.7 us  [outer_pairs(): return lax.ppermute(value, 'dp', pairs)]
    ppermute x18, waiting for transfers between devices: 19.1 us -> 21.1 us  [over_etp(): return lax.ppermute(value, 'etp', pairs)]
  transfers between devices with their start and end apart: 35 -> 35, of which waited for: 18 -> 20; matrix products, arithmetic and copies ran while one was open for 12% -> 10% of each run, Pallas kernels for 0% -> 0%
where the time goes in v8:
time: 142 us
  waiting for transfers between devices  81.4 us (57%)
  starting transfers between devices  38 us (27%)
  matrix products  15.8 us (11%)
  other arithmetic  2.84 us (2%)
  Pallas kernels  1.51 us (1%)
    ppermute x8, waiting for transfers between devices, outer_pairs(): return lax.ppermute(value, 'dp', pairs)  36.9 us
    ppermute x18, waiting for transfers between devices, over_etp(): return lax.ppermute(value, 'etp', pairs)  21.1 us
    ppermute x6, waiting for transfers between devices, over_outer(): return lax.ppermute(value, 'dp', pairs)  16.7 us
    ppermute x18, starting transfers between devices, over_etp(): return lax.ppermute(value, 'etp', pairs)  12.8 us
    ppermute x8, starting transfers between devices, outer_pairs(): return lax.ppermute(value, 'dp', pairs)  11.7 us
    ppermute x6, starting transfers between devices, over_outer(): return lax.ppermute(value, 'dp', pairs)  9.92 us
    ppermute x3, waiting for transfers between devices, over_inner(): return lax.ppermute(value, 'dp', pairs)  6.7 us
    dot_general x1, matrix products, shards(): lax.dot_general(onehot, dx, (((0,), (0,)), ((), ())), preferred_element_t...  4 us
  transfers between devices with their start and end apart: 35, of which 20 were waited for; matrix products, arithmetic and copies ran while one was open for 10% of the time, Pallas kernels for 0%

profile of v8, /device:TPU:0, one launch (start us, length us, event | category | flops | bytes accessed | tf_op | source)
XLA Modules:
  0.0 142.0 jit_solution(7706131221089482369)
XLA Ops:
  0.7 3.6 %convolution_convert_fusion.1 = bf16[64,5120]{1,0:T(8,128)(2,1)S(1)} fusion(bf16[512,5120]{1,0:T(8,128)(2,1)} %param.7, s32[64]{0:T(128)} %param.8), kind=kOutput, calls=%fused_computation.1 | convolution fusion | flops 335904768 | bytes 5898496 | tf_op jit(solution)/shard_map/dot_general | solution.py:134
  4.4 3.1 %collective-permute-start.1 = (bf16[64,1280]{1,0:T(8,128)(2,1)S(1)}, bf16[64,1280]{1,0:T(8,128)(2,1)S(1)}, u32[]{:S(2)}, u32[]{:S(2)}) collective-permute-start(bf16[64,1280]{1,0:T(8,128)(2,1)S(1)} %pad_maximum_fusion.8), channel_id=1, source_target_pairs={{0,8},{4,12},{8,0},{12,4},{16,24},{20,28},{24,16},{28,20},{1,9},{5... | collective-permute-start | bytes 491528 | tf_op jit(solution)/shard_map/ppermute | solution.py:69
  7.5 2.5 %collective-permute-start.2 = (bf16[64,1280]{1,0:T(8,128)(2,1)S(1)}, bf16[64,1280]{1,0:T(8,128)(2,1)S(1)}, u32[]{:S(2)}, u32[]{:S(2)}) collective-permute-start(bf16[64,1280]{1,0:T(8,128)(2,1)S(1)} %pad_maximum_fusion.9), channel_id=1, source_target_pairs={{0,24},{4,28},{8,16},{12,20},{16,8},{20,12},{24,0},{28,4},{1,25},{... | collective-permute-start | bytes 491528 | tf_op jit(solution)/shard_map/ppermute | solution.py:69
  10.1 1.5 %collective-permute-start.5 = (bf16[640,384]{1,0:T(8,128)(2,1)S(1)}, bf16[640,384]{1,0:T(8,128)(2,1)S(1)}, u32[]{:S(2)}, u32[]{:S(2)}) collective-permute-start(bf16[640,384]{1,0:T(8,128)(2,1)S(1)} %copy-done.2), channel_id=1, source_target_pairs={{0,4},{4,0},{8,12},{12,8},{16,20},{20,16},{24,28},{28,24},{1,5},{5... | collective-permute-start | bytes 1474568 | tf_op jit(solution)/shard_map/ppermute | solution.py:73
  12.4 6.2 %collective-permute-done.2 = bf16[64,1280]{1,0:T(8,128)(2,1)S(1)} collective-permute-done((bf16[64,1280]{1,0:T(8,128)(2,1)S(1)}, bf16[64,1280]{1,0:T(8,128)(2,1)S(1)}, u32[]{:S(2)}, u32[]{:S(2)}) %collective-permute-start.2) | collective-permute-done | bytes 163872 | tf_op jit(solution)/shard_map/ppermute | solution.py:69
  18.7 1.6 %collective-permute-start.7 = (bf16[64,1280]{1,0:T(8,128)(2,1)S(1)}, bf16[64,1280]{1,0:T(8,128)(2,1)S(1)}, u32[]{:S(2)}, u32[]{:S(2)}) collective-permute-start(bf16[64,1280]{1,0:T(8,128)(2,1)S(1)} %get-tuple-element.31), channel_id=1, source_target_pairs={{0,2},{1,3},{2,0},{3,1},{4,6},{5,7},{6,4},{7,5},{8,10},{9,11},{10,... | collective-permute-start | bytes 491528 | tf_op jit(solution)/shard_map/ppermute | solution.py:77
  20.8 3.6 %collective-permute-done.7 = bf16[64,1280]{1,0:T(8,128)(2,1)S(1)} collective-permute-done((bf16[64,1280]{1,0:T(8,128)(2,1)S(1)}, bf16[64,1280]{1,0:T(8,128)(2,1)S(1)}, u32[]{:S(2)}, u32[]{:S(2)}) %collective-permute-start.7) | collective-permute-done | bytes 163872 | tf_op jit(solution)/shard_map/ppermute | solution.py:77
  24.5 1.6 %collective-permute-done.3 = bf16[64,1280]{1,0:T(8,128)(2,1)S(1)} collective-permute-done((bf16[64,1280]{1,0:T(8,128)(2,1)S(1)}, bf16[64,1280]{1,0:T(8,128)(2,1)S(1)}, u32[]{:S(2)}, u32[]{:S(2)}) %collective-permute-start.3) | collective-permute-done | bytes 163872 | tf_op jit(solution)/shard_map/ppermute | solution.py:77
  26.3 6.7 %collective-permute-done.6 = bf16[640,384]{1,0:T(8,128)(2,1)S(1)} collective-permute-done((bf16[640,384]{1,0:T(8,128)(2,1)S(1)}, bf16[640,384]{1,0:T(8,128)(2,1)S(1)}, u32[]{:S(2)}, u32[]{:S(2)}) %collective-permute-start.6) | collective-permute-done | bytes 491552 | tf_op jit(solution)/shard_map/ppermute | solution.py:73
  34.7 1.6 %collective-permute-start.9 = (bf16[64,1280]{1,0:T(8,128)(2,1)S(1)}, bf16[64,1280]{1,0:T(8,128)(2,1)S(1)}, u32[]{:S(2)}, u32[]{:S(2)}) collective-permute-start(bf16[64,1280]{1,0:T(8,128)(2,1)S(1)} %collective-permute-done), channel_id=1, source_target_pairs={{0,2},{1,3},{2,0},{3,1},{4,6},{5,7},{6,4},{7,5},{8,10},{9,11},{10,... | collective-permute-start | bytes 491528 | tf_op jit(solution)/shard_map/ppermute | solution.py:77
  36.3 3.8 %collective-permute-done.9 = bf16[64,1280]{1,0:T(8,128)(2,1)S(1)} collective-permute-done((bf16[64,1280]{1,0:T(8,128)(2,1)S(1)}, bf16[64,1280]{1,0:T(8,128)(2,1)S(1)}, u32[]{:S(2)}, u32[]{:S(2)}) %collective-permute-start.9) | collective-permute-done | bytes 163872 | tf_op jit(solution)/shard_map/ppermute | solution.py:77
  42.5 1.6 %collective-permute-start.11 = (bf16[64,1280]{1,0:T(8,128)(2,1)S(1)}, bf16[64,1280]{1,0:T(8,128)(2,1)S(1)}, u32[]{:S(2)}, u32[]{:S(2)}) collective-permute-start(bf16[64,1280]{1,0:T(8,128)(2,1)S(1)} %pad_maximum_fusion.6), channel_id=1, source_target_pairs={{0,2},{1,3},{2,0},{3,1},{4,6},{5,7},{6,4},{7,5},{8,10},{9,11},{10,... | collective-permute-start | bytes 491528 | tf_op jit(solution)/shard_map/ppermute | solution.py:77
  44.1 4.7 %collective-permute-done.11 = bf16[64,1280]{1,0:T(8,128)(2,1)S(1)} collective-permute-done((bf16[64,1280]{1,0:T(8,128)(2,1)S(1)}, bf16[64,1280]{1,0:T(8,128)(2,1)S(1)}, u32[]{:S(2)}, u32[]{:S(2)}) %collective-permute-start.11) | collective-permute-done | bytes 163872 | tf_op jit(solution)/shard_map/ppermute | solution.py:77
  49.0 5.6 %collective-permute-start.14 = (bf16[256,768]{1,0:T(8,128)(2,1)S(1)}, bf16[256,768]{1,0:T(8,128)(2,1)S(1)}, u32[]{:S(2)}, u32[]{:S(2)}) collective-permute-start(bf16[256,768]{1,0:T(8,128)(2,1)S(1)} %convert_element_type.86), channel_id=1, source_target_pairs={{0,16},{4,20},{24,8},{28,12},{1,17},{5,21},{25,9},{29,13},{2,18},{... | collective-permute-start | bytes 1179656 | tf_op jit(solution)/shard_map/ppermute | solution.py:106
  54.7 1.6 %collective-permute-start.16 = (bf16[64]{0:T(256)(128)(2,1)S(1)}, bf16[64]{0:T(256)(128)(2,1)S(1)}, u32[]{:S(2)}, u32[]{:S(2)}) collective-permute-start(bf16[64]{0:T(256)(128)(2,1)S(1)} %copy-done.4), channel_id=1, source_target_pairs={{0,2},{1,3},{2,0},{3,1},{4,6},{5,7},{6,4},{7,5},{8,10},{9,11},{10,... | collective-permute-start | bytes 392 | tf_op jit(solution)/shard_map/ppermute | solution.py:77
  56.5 1.8 %collective-permute-done.16 = bf16[64]{0:T(256)(128)(2,1)S(1)} collective-permute-done((bf16[64]{0:T(256)(128)(2,1)S(1)}, bf16[64]{0:T(256)(128)(2,1)S(1)}, u32[]{:S(2)}, u32[]{:S(2)}) %collective-permute-start.16) | collective-permute-done | bytes 160 | tf_op jit(solution)/shard_map/ppermute | solution.py:77
  58.4 5.6 %collective-permute-done.14 = bf16[256,768]{1,0:T(8,128)(2,1)S(1)} collective-permute-done((bf16[256,768]{1,0:T(8,128)(2,1)S(1)}, bf16[256,768]{1,0:T(8,128)(2,1)S(1)}, u32[]{:S(2)}, u32[]{:S(2)}) %collective-permute-start.14) | collective-permute-done | bytes 393248 | tf_op jit(solution)/shard_map/ppermute | solution.py:106
  64.9 8.9 %collective-permute-done.18.refs_0_ = bf16[256,768]{1,0:T(8,128)(2,1)S(1)} collective-permute-done((bf16[256,768]{1,0:T(8,128)(2,1)S(1)}, bf16[256,768]{1,0:T(8,128)(2,1)S(1)}, u32[]{:S(2)}, u32[]{:S(2)}) %collective-permute-start.18) | collective-permute-done | bytes 393248 | tf_op jit(solution)/shard_map/ppermute | solution.py:106
  73.8 1.5 %shard_map.102 = (bf16[256,384]{1,0:T(8,128)(2,1)}, bf16[256,768]{1,0:T(8,128)(2,1)S(1)}) custom-call(s32[4]{0:T(128)S(1)} %broadcast_xor_fusion.order_ref, f32[256,768]{1,0:T(8,128)S(1)} %fusion.9.pre_ref, bf16[256,1]{1,0:T(8,128)(2,1)S(1)} %broadcast_in_dim.15.prob_ref, bf16[256,384]{1,0:T(8,128)(2,1)S(1)} %copy-done, ...), custom_call_target="tpu_custom_call" | custom-call | flops 1966080 | bytes 2949120 | tf_op jit(solution)/shard_map/pallas_call | solution.py:49
  77.9 1.6 %collective-permute-start.20 = (bf16[64,1280]{1,0:T(8,128)(2,1)S(1)}, bf16[64,1280]{1,0:T(8,128)(2,1)S(1)}, u32[]{:S(2)}, u32[]{:S(2)}) collective-permute-start(bf16[64,1280]{1,0:T(8,128)(2,1)S(1)} %slice.235), channel_id=1, source_target_pairs={{0,2},{1,3},{2,0},{3,1},{4,6},{5,7},{6,4},{7,5},{8,10},{9,11},{10,... | collective-permute-start | bytes 491528 | tf_op jit(solution)/shard_map/ppermute | solution.py:77
  79.5 8.4 %collective-permute-done.22 = bf16[256,768]{1,0:T(8,128)(2,1)S(1)} collective-permute-done((bf16[256,768]{1,0:T(8,128)(2,1)S(1)}, bf16[256,768]{1,0:T(8,128)(2,1)S(1)}, u32[]{:S(2)}, u32[]{:S(2)}) %collective-permute-start.22) | collective-permute-done | bytes 393248 | tf_op jit(solution)/shard_map/ppermute | solution.py:106
  88.0 1.8 %collective-permute-start.24 = (bf16[256,768]{1,0:T(8,128)(2,1)S(1)}, bf16[256,768]{1,0:T(8,128)(2,1)S(1)}, u32[]{:S(2)}, u32[]{:S(2)}) collective-permute-start(bf16[256,768]{1,0:T(8,128)(2,1)S(1)} %broadcast_select_fusion.2), channel_id=1, source_target_pairs={{0,8},{4,12},{8,0},{12,4},{16,24},{20,28},{24,16},{28,20},{1,9},{5... | collective-permute-start | bytes 1179656 | tf_op jit(solution)/shard_map/ppermute | solution.py:106
  92.4 1.6 %collective-permute-start.28 = (bf16[64,1280]{1,0:T(8,128)(2,1)S(1)}, bf16[64,1280]{1,0:T(8,128)(2,1)S(1)}, u32[]{:S(2)}, u32[]{:S(2)}) collective-permute-start(bf16[64,1280]{1,0:T(8,128)(2,1)S(1)} %slice.233), channel_id=1, source_target_pairs={{0,2},{1,3},{2,0},{3,1},{4,6},{5,7},{6,4},{7,5},{8,10},{9,11},{10,... | collective-permute-start | bytes 491528 | tf_op jit(solution)/shard_map/ppermute | solution.py:77
  93.9 4.8 %collective-permute-done.24 = bf16[256,768]{1,0:T(8,128)(2,1)S(1)} collective-permute-done((bf16[256,768]{1,0:T(8,128)(2,1)S(1)}, bf16[256,768]{1,0:T(8,128)(2,1)S(1)}, u32[]{:S(2)}, u32[]{:S(2)}) %collective-permute-start.24) | collective-permute-done | bytes 393248 | tf_op jit(solution)/shard_map/ppermute | solution.py:106
  100.6 9.2 %collective-permute-done.21 = bf16[256,768]{1,0:T(8,128)(2,1)S(1)} collective-permute-done((bf16[256,768]{1,0:T(8,128)(2,1)S(1)}, bf16[256,768]{1,0:T(8,128)(2,1)S(1)}, u32[]{:S(2)}, u32[]{:S(2)}) %collective-permute-start.21) | collective-permute-done | bytes 393248 | tf_op jit(solution)/shard_map/ppermute | solution.py:106
  110.4 1.6 %collective-permute-start.34 = (bf16[640,768]{1,0:T(8,128)(2,1)S(1)}, bf16[640,768]{1,0:T(8,128)(2,1)S(1)}, u32[]{:S(2)}, u32[]{:S(2)}) collective-permute-start(bf16[640,768]{1,0:T(8,128)(2,1)S(1)} %add_convert_fusion), channel_id=1, source_target_pairs={{0,4},{4,0},{8,12},{12,8},{16,20},{20,16},{24,28},{28,24},{1,5},{5... | collective-permute-start | bytes 2949128 | tf_op jit(solution)/shard_map/ppermute | solution.py:73
  114.2 1.6 %collective-permute-start.30 = (bf16[64,1280]{1,0:T(8,128)(2,1)S(1)}, bf16[64,1280]{1,0:T(8,128)(2,1)S(1)}, u32[]{:S(2)}, u32[]{:S(2)}) collective-permute-start(bf16[64,1280]{1,0:T(8,128)(2,1)S(1)} %slice.232), channel_id=1, source_target_pairs={{0,2},{1,3},{2,0},{3,1},{4,6},{5,7},{6,4},{7,5},{8,10},{9,11},{10,... | collective-permute-start | bytes 491528 | tf_op jit(solution)/shard_map/ppermute | solution.py:77
  116.5 4.8 %collective-permute-done.30 = bf16[64,1280]{1,0:T(8,128)(2,1)S(1)} collective-permute-done((bf16[64,1280]{1,0:T(8,128)(2,1)S(1)}, bf16[64,1280]{1,0:T(8,128)(2,1)S(1)}, u32[]{:S(2)}, u32[]{:S(2)}) %collective-permute-start.30) | collective-permute-done | bytes 163872 | tf_op jit(solution)/shard_map/ppermute | solution.py:77
  121.3 2.5 %collective-permute-start.33 = (bf16[64,1280]{1,0:T(8,128)(2,1)S(1)}, bf16[64,1280]{1,0:T(8,128)(2,1)S(1)}, u32[]{:S(2)}, u32[]{:S(2)}) collective-permute-start(bf16[64,1280]{1,0:T(8,128)(2,1)S(1)} %get-tuple-element.58), channel_id=1, source_target_pairs={{0,24},{4,28},{8,16},{12,20},{16,8},{20,12},{24,0},{28,4},{1,25},{... | collective-permute-start | bytes 491528 | tf_op jit(solution)/shard_map/ppermute | solution.py:69
  126.0 4.4 %collective-permute-done.33 = bf16[64,1280]{1,0:T(8,128)(2,1)S(1)} collective-permute-done((bf16[64,1280]{1,0:T(8,128)(2,1)S(1)}, bf16[64,1280]{1,0:T(8,128)(2,1)S(1)}, u32[]{:S(2)}, u32[]{:S(2)}) %collective-permute-start.33) | collective-permute-done | bytes 163872 | tf_op jit(solution)/shard_map/ppermute | solution.py:69
  130.4 4.6 %collective-permute-done.31 = bf16[64,1280]{1,0:T(8,128)(2,1)S(1)} collective-permute-done((bf16[64,1280]{1,0:T(8,128)(2,1)S(1)}, bf16[64,1280]{1,0:T(8,128)(2,1)S(1)}, u32[]{:S(2)}, u32[]{:S(2)}) %collective-permute-start.31) | collective-permute-done | bytes 163872 | tf_op jit(solution)/shard_map/ppermute | solution.py:69
  136.6 4.0 %convolution_convert_fusion = bf16[512,5120]{1,0:T(8,128)(2,1)} fusion(bf16[64,5120]{1,0:T(8,128)(2,1)S(1)} %slice_dynamic-update-slice_fusion.2, s32[64]{0:T(128)S(1)} %copy-done.3), kind=kOutput, calls=%fused_computation | convolution fusion | flops 338198528 | bytes 5898496 | tf_op jit(solution)/shard_map/dot_general | solution.py:239
  (127 shorter events, 22.7 us)
Async XLA Ops:
  4.4 8.0 %collective-permute-start.1 = (bf16[64,1280]{1,0:T(8,128)(2,1)S(1)}, bf16[64,1280]{1,0:T(8,128)(2,1)S(1)}, u32[]{:S(2)}, u32[]{:S(2)}) collective-permute-start(bf16[64,1280]{1,0:T(8,128)(2,1)S(1)} %pad_maximum_fusion.8), channel_id=1, source_target_pairs={{0,8},{4,12},{8,0},{12,4},{16,24},{20,28},{24,16},{28,20},{1,9},{5... | collective-permute-start | bytes 491528 | tf_op jit(solution)/shard_map/ppermute | solution.py:69
  7.5 11.1 %collective-permute-start.2 = (bf16[64,1280]{1,0:T(8,128)(2,1)S(1)}, bf16[64,1280]{1,0:T(8,128)(2,1)S(1)}, u32[]{:S(2)}, u32[]{:S(2)}) collective-permute-start(bf16[64,1280]{1,0:T(8,128)(2,1)S(1)} %pad_maximum_fusion.9), channel_id=1, source_target_pairs={{0,24},{4,28},{8,16},{12,20},{16,8},{20,12},{24,0},{28,4},{1,25},{... | collective-permute-start | bytes 491528 | tf_op jit(solution)/shard_map/ppermute | solution.py:69
  10.1 16.2 %collective-permute-start.5 = (bf16[640,384]{1,0:T(8,128)(2,1)S(1)}, bf16[640,384]{1,0:T(8,128)(2,1)S(1)}, u32[]{:S(2)}, u32[]{:S(2)}) collective-permute-start(bf16[640,384]{1,0:T(8,128)(2,1)S(1)} %copy-done.2), channel_id=1, source_target_pairs={{0,4},{4,0},{8,12},{12,8},{16,20},{20,16},{24,28},{28,24},{1,5},{5... | collective-permute-start | bytes 1474568 | tf_op jit(solution)/shard_map/ppermute | solution.py:73
  11.6 21.4 %collective-permute-start.6 = (bf16[640,384]{1,0:T(8,128)(2,1)S(1)}, bf16[640,384]{1,0:T(8,128)(2,1)S(1)}, u32[]{:S(2)}, u32[]{:S(2)}) collective-permute-start(bf16[640,384]{1,0:T(8,128)(2,1)S(1)} %copy-done.1), channel_id=1, source_target_pairs={{0,4},{4,0},{8,12},{12,8},{16,20},{20,16},{24,28},{28,24},{1,5},{5... | collective-permute-start | bytes 1474568 | tf_op jit(solution)/shard_map/ppermute | solution.py:73
  12.1 22.5 %collective-permute-start = (bf16[64,1280]{1,0:T(8,128)(2,1)S(1)}, bf16[64,1280]{1,0:T(8,128)(2,1)S(1)}, u32[]{:S(2)}, u32[]{:S(2)}) collective-permute-start(bf16[64,1280]{1,0:T(8,128)(2,1)S(1)} %pad_maximum_fusion.7), channel_id=1, source_target_pairs={{0,16},{4,20},{8,24},{12,28},{16,0},{20,4},{24,8},{28,12},{1,17},{... | collective-permute-start | bytes 491528 | tf_op jit(solution)/shard_map/ppermute | solution.py:69
  18.7 5.7 %collective-permute-start.7 = (bf16[64,1280]{1,0:T(8,128)(2,1)S(1)}, bf16[64,1280]{1,0:T(8,128)(2,1)S(1)}, u32[]{:S(2)}, u32[]{:S(2)}) collective-permute-start(bf16[64,1280]{1,0:T(8,128)(2,1)S(1)} %get-tuple-element.31), channel_id=1, source_target_pairs={{0,2},{1,3},{2,0},{3,1},{4,6},{5,7},{6,4},{7,5},{8,10},{9,11},{10,... | collective-permute-start | bytes 491528 | tf_op jit(solution)/shard_map/ppermute | solution.py:77
  20.3 5.9 %collective-permute-start.3 = (bf16[64,1280]{1,0:T(8,128)(2,1)S(1)}, bf16[64,1280]{1,0:T(8,128)(2,1)S(1)}, u32[]{:S(2)}, u32[]{:S(2)}) collective-permute-start(bf16[64,1280]{1,0:T(8,128)(2,1)S(1)} %get-tuple-element.30), channel_id=1, source_target_pairs={{0,2},{1,3},{2,0},{3,1},{4,6},{5,7},{6,4},{7,5},{8,10},{9,11},{10,... | collective-permute-start | bytes 491528 | tf_op jit(solution)/shard_map/ppermute | solution.py:77
  24.4 8.7 %collective-permute-start.8 = (bf16[128,1280]{1,0:T(8,128)(2,1)S(1)}, bf16[128,1280]{1,0:T(8,128)(2,1)S(1)}, u32[]{:S(2)}, u32[]{:S(2)}) collective-permute-start(bf16[128,1280]{1,0:T(8,128)(2,1)S(1)} %pad_maximum_fusion.3), channel_id=1, source_target_pairs={{0,1},{1,0},{2,3},{3,2},{4,5},{5,4},{6,7},{7,6},{8,9},{9,8},{10,11... | collective-permute-start | bytes 983048 | tf_op jit(solution)/shard_map/ppermute | solution.py:77
  26.2 7.7 %collective-permute-start.4 = (bf16[128,1280]{1,0:T(8,128)(2,1)S(1)}, bf16[128,1280]{1,0:T(8,128)(2,1)S(1)}, u32[]{:S(2)}, u32[]{:S(2)}) collective-permute-start(bf16[128,1280]{1,0:T(8,128)(2,1)S(1)} %pad_maximum_fusion.2), channel_id=1, source_target_pairs={{0,1},{1,0},{2,3},{3,2},{4,5},{5,4},{6,7},{7,6},{8,9},{9,8},{10,11... | collective-permute-start | bytes 983048 | tf_op jit(solution)/shard_map/ppermute | solution.py:77
  34.7 5.4 %collective-permute-start.9 = (bf16[64,1280]{1,0:T(8,128)(2,1)S(1)}, bf16[64,1280]{1,0:T(8,128)(2,1)S(1)}, u32[]{:S(2)}, u32[]{:S(2)}) collective-permute-start(bf16[64,1280]{1,0:T(8,128)(2,1)S(1)} %collective-permute-done), channel_id=1, source_target_pairs={{0,2},{1,3},{2,0},{3,1},{4,6},{5,7},{6,4},{7,5},{8,10},{9,11},{10,... | collective-permute-start | bytes 491528 | tf_op jit(solution)/shard_map/ppermute | solution.py:77
  40.2 16.1 %collective-permute-start.15 = (bf16[256,768]{1,0:T(8,128)(2,1)S(1)}, bf16[256,768]{1,0:T(8,128)(2,1)S(1)}, u32[]{:S(2)}, u32[]{:S(2)}) collective-permute-start(bf16[256,768]{1,0:T(8,128)(2,1)S(1)} %convolution_convert_fusion.2), channel_id=1, source_target_pairs={{0,8},{4,12},{8,0},{12,4},{16,24},{20,28},{24,16},{28,20},{1,9},{5... | collective-permute-start | bytes 1179656 | tf_op jit(solution)/shard_map/ppermute | solution.py:106
  40.9 17.5 %collective-permute-start.13 = (bf16[256,768]{1,0:T(8,128)(2,1)S(1)}, bf16[256,768]{1,0:T(8,128)(2,1)S(1)}, u32[]{:S(2)}, u32[]{:S(2)}) collective-permute-start(bf16[256,768]{1,0:T(8,128)(2,1)S(1)} %convolution_convert_fusion.3), channel_id=1, source_target_pairs={{8,16},{12,20},{16,8},{20,12},{9,17},{13,21},{17,9},{21,13},{10,18... | collective-permute-start | bytes 1179656 | tf_op jit(solution)/shard_map/ppermute | solution.py:106
  42.5 6.3 %collective-permute-start.11 = (bf16[64,1280]{1,0:T(8,128)(2,1)S(1)}, bf16[64,1280]{1,0:T(8,128)(2,1)S(1)}, u32[]{:S(2)}, u32[]{:S(2)}) collective-permute-start(bf16[64,1280]{1,0:T(8,128)(2,1)S(1)} %pad_maximum_fusion.6), channel_id=1, source_target_pairs={{0,2},{1,3},{2,0},{3,1},{4,6},{5,7},{6,4},{7,5},{8,10},{9,11},{10,... | collective-permute-start | bytes 491528 | tf_op jit(solution)/shard_map/ppermute | solution.py:77
  48.8 5.8 %collective-permute-start.12 = (bf16[128,1280]{1,0:T(8,128)(2,1)S(1)}, bf16[128,1280]{1,0:T(8,128)(2,1)S(1)}, u32[]{:S(2)}, u32[]{:S(2)}) collective-permute-start(bf16[128,1280]{1,0:T(8,128)(2,1)S(1)} %pad_maximum_fusion.5), channel_id=1, source_target_pairs={{0,1},{1,0},{2,3},{3,2},{4,5},{5,4},{6,7},{7,6},{8,9},{9,8},{10,11... | collective-permute-start | bytes 983048 | tf_op jit(solution)/shard_map/ppermute | solution.py:77
  49.0 15.1 %collective-permute-start.14 = (bf16[256,768]{1,0:T(8,128)(2,1)S(1)}, bf16[256,768]{1,0:T(8,128)(2,1)S(1)}, u32[]{:S(2)}, u32[]{:S(2)}) collective-permute-start(bf16[256,768]{1,0:T(8,128)(2,1)S(1)} %convert_element_type.86), channel_id=1, source_target_pairs={{0,16},{4,20},{24,8},{28,12},{1,17},{5,21},{25,9},{29,13},{2,18},{... | collective-permute-start | bytes 1179656 | tf_op jit(solution)/shard_map/ppermute | solution.py:106
  54.7 3.6 %collective-permute-start.16 = (bf16[64]{0:T(256)(128)(2,1)S(1)}, bf16[64]{0:T(256)(128)(2,1)S(1)}, u32[]{:S(2)}, u32[]{:S(2)}) collective-permute-start(bf16[64]{0:T(256)(128)(2,1)S(1)} %copy-done.4), channel_id=1, source_target_pairs={{0,2},{1,3},{2,0},{3,1},{4,6},{5,7},{6,4},{7,5},{8,10},{9,11},{10,... | collective-permute-start | bytes 392 | tf_op jit(solution)/shard_map/ppermute | solution.py:77
  56.4 17.4 %collective-permute-start.18 = (bf16[256,768]{1,0:T(8,128)(2,1)S(1)}, bf16[256,768]{1,0:T(8,128)(2,1)S(1)}, u32[]{:S(2)}, u32[]{:S(2)}) collective-permute-start(bf16[256,768]{1,0:T(8,128)(2,1)S(1)} %fusion.17), channel_id=1, source_target_pairs={{16,0},{20,4},{24,16},{28,20},{8,24},{12,28},{0,8},{4,12},{17,1},{... | collective-permute-start | bytes 1179656 | tf_op jit(solution)/shard_map/ppermute | solution.py:106
  58.4 6.4 %collective-permute-start.17 = (bf16[128]{0:T(256)(128)(2,1)S(1)}, bf16[128]{0:T(256)(128)(2,1)S(1)}, u32[]{:S(2)}, u32[]{:S(2)}) collective-permute-start(bf16[128]{0:T(256)(128)(2,1)S(1)} %pad_maximum_fusion.10), channel_id=1, source_target_pairs={{0,1},{1,0},{2,3},{3,2},{4,5},{5,4},{6,7},{7,6},{8,9},{9,8},{10,11... | collective-permute-start | bytes 776 | tf_op jit(solution)/shard_map/ppermute | solution.py:77
  76.3 11.6 %collective-permute-start.22 = (bf16[256,768]{1,0:T(8,128)(2,1)S(1)}, bf16[256,768]{1,0:T(8,128)(2,1)S(1)}, u32[]{:S(2)}, u32[]{:S(2)}) collective-permute-start(bf16[256,768]{1,0:T(8,128)(2,1)S(1)} %get-tuple-element.44), channel_id=1, source_target_pairs={{0,16},{4,20},{16,24},{20,28},{24,8},{28,12},{8,0},{12,4},{1,17},{... | collective-permute-start | bytes 1179656 | tf_op jit(solution)/shard_map/ppermute | solution.py:106
  77.0 12.7 %collective-permute-start.23 = (bf16[256,768]{1,0:T(8,128)(2,1)S(1)}, bf16[256,768]{1,0:T(8,128)(2,1)S(1)}, u32[]{:S(2)}, u32[]{:S(2)}) collective-permute-start(bf16[256,768]{1,0:T(8,128)(2,1)S(1)} %get-tuple-element.44), channel_id=1, source_target_pairs={{8,16},{12,20},{16,8},{20,12},{9,17},{13,21},{17,9},{21,13},{10,18... | collective-permute-start | bytes 1179656 | tf_op jit(solution)/shard_map/ppermute | solution.py:106
  77.9 12.7 %collective-permute-start.20 = (bf16[64,1280]{1,0:T(8,128)(2,1)S(1)}, bf16[64,1280]{1,0:T(8,128)(2,1)S(1)}, u32[]{:S(2)}, u32[]{:S(2)}) collective-permute-start(bf16[64,1280]{1,0:T(8,128)(2,1)S(1)} %slice.235), channel_id=1, source_target_pairs={{0,2},{1,3},{2,0},{3,1},{4,6},{5,7},{6,4},{7,5},{8,10},{9,11},{10,... | collective-permute-start | bytes 491528 | tf_op jit(solution)/shard_map/ppermute | solution.py:77
  88.0 10.8 %collective-permute-start.24 = (bf16[256,768]{1,0:T(8,128)(2,1)S(1)}, bf16[256,768]{1,0:T(8,128)(2,1)S(1)}, u32[]{:S(2)}, u32[]{:S(2)}) collective-permute-start(bf16[256,768]{1,0:T(8,128)(2,1)S(1)} %broadcast_select_fusion.2), channel_id=1, source_target_pairs={{0,8},{4,12},{8,0},{12,4},{16,24},{20,28},{24,16},{28,20},{1,9},{5... | collective-permute-start | bytes 1179656 | tf_op jit(solution)/shard_map/ppermute | solution.py:106
  90.7 19.1 %collective-permute-start.21 = (bf16[256,768]{1,0:T(8,128)(2,1)S(1)}, bf16[256,768]{1,0:T(8,128)(2,1)S(1)}, u32[]{:S(2)}, u32[]{:S(2)}) collective-permute-start(bf16[256,768]{1,0:T(8,128)(2,1)S(1)} %get-tuple-element.44), channel_id=1, source_target_pairs={{16,0},{20,4},{8,24},{12,28},{17,1},{21,5},{9,25},{13,29},{18,2},{... | collective-permute-start | bytes 1179656 | tf_op jit(solution)/shard_map/ppermute | solution.py:106
  92.4 24.1 %collective-permute-start.28 = (bf16[64,1280]{1,0:T(8,128)(2,1)S(1)}, bf16[64,1280]{1,0:T(8,128)(2,1)S(1)}, u32[]{:S(2)}, u32[]{:S(2)}) collective-permute-start(bf16[64,1280]{1,0:T(8,128)(2,1)S(1)} %slice.233), channel_id=1, source_target_pairs={{0,2},{1,3},{2,0},{3,1},{4,6},{5,7},{6,4},{7,5},{8,10},{9,11},{10,... | collective-permute-start | bytes 491528 | tf_op jit(solution)/shard_map/ppermute | solution.py:77
  100.6 13.5 %collective-permute-start.29 = (bf16[128,1280]{1,0:T(8,128)(2,1)S(1)}, bf16[128,1280]{1,0:T(8,128)(2,1)S(1)}, u32[]{:S(2)}, u32[]{:S(2)}) collective-permute-start(bf16[128,1280]{1,0:T(8,128)(2,1)S(1)} %slice.228), channel_id=1, source_target_pairs={{0,1},{1,0},{2,3},{3,2},{4,5},{5,4},{6,7},{7,6},{8,9},{9,8},{10,11... | collective-permute-start | bytes 983048 | tf_op jit(solution)/shard_map/ppermute | solution.py:77
  110.4 30.2 %collective-permute-start.34 = (bf16[640,768]{1,0:T(8,128)(2,1)S(1)}, bf16[640,768]{1,0:T(8,128)(2,1)S(1)}, u32[]{:S(2)}, u32[]{:S(2)}) collective-permute-start(bf16[640,768]{1,0:T(8,128)(2,1)S(1)} %add_convert_fusion), channel_id=1, source_target_pairs={{0,4},{4,0},{8,12},{12,8},{16,20},{20,16},{24,28},{28,24},{1,5},{5... | collective-permute-start | bytes 2949128 | tf_op jit(solution)/shard_map/ppermute | solution.py:73
  112.8 3.0 %collective-permute-start.25 = (bf16[128,1280]{1,0:T(8,128)(2,1)S(1)}, bf16[128,1280]{1,0:T(8,128)(2,1)S(1)}, u32[]{:S(2)}, u32[]{:S(2)}) collective-permute-start(bf16[128,1280]{1,0:T(8,128)(2,1)S(1)} %slice.230), channel_id=1, source_target_pairs={{0,1},{1,0},{2,3},{3,2},{4,5},{5,4},{6,7},{7,6},{8,9},{9,8},{10,11... | collective-permute-start | bytes 983048 | tf_op jit(solution)/shard_map/ppermute | solution.py:77
  114.2 7.1 %collective-permute-start.30 = (bf16[64,1280]{1,0:T(8,128)(2,1)S(1)}, bf16[64,1280]{1,0:T(8,128)(2,1)S(1)}, u32[]{:S(2)}, u32[]{:S(2)}) collective-permute-start(bf16[64,1280]{1,0:T(8,128)(2,1)S(1)} %slice.232), channel_id=1, source_target_pairs={{0,2},{1,3},{2,0},{3,1},{4,6},{5,7},{6,4},{7,5},{8,10},{9,11},{10,... | collective-permute-start | bytes 491528 | tf_op jit(solution)/shard_map/ppermute | solution.py:77
  115.9 8.5 %collective-permute-start.26 = (bf16[64,1280]{1,0:T(8,128)(2,1)S(1)}, bf16[64,1280]{1,0:T(8,128)(2,1)S(1)}, u32[]{:S(2)}, u32[]{:S(2)}) collective-permute-start(bf16[64,1280]{1,0:T(8,128)(2,1)S(1)} %slice.234), channel_id=1, source_target_pairs={{0,2},{1,3},{2,0},{3,1},{4,6},{5,7},{6,4},{7,5},{8,10},{9,11},{10,... | collective-permute-start | bytes 491528 | tf_op jit(solution)/shard_map/ppermute | solution.py:77
  121.3 9.1 %collective-permute-start.33 = (bf16[64,1280]{1,0:T(8,128)(2,1)S(1)}, bf16[64,1280]{1,0:T(8,128)(2,1)S(1)}, u32[]{:S(2)}, u32[]{:S(2)}) collective-permute-start(bf16[64,1280]{1,0:T(8,128)(2,1)S(1)} %get-tuple-element.58), channel_id=1, source_target_pairs={{0,24},{4,28},{8,16},{12,20},{16,8},{20,12},{24,0},{28,4},{1,25},{... | collective-permute-start | bytes 491528 | tf_op jit(solution)/shard_map/ppermute | solution.py:69
  123.9 11.1 %collective-permute-start.31 = (bf16[64,1280]{1,0:T(8,128)(2,1)S(1)}, bf16[64,1280]{1,0:T(8,128)(2,1)S(1)}, u32[]{:S(2)}, u32[]{:S(2)}) collective-permute-start(bf16[64,1280]{1,0:T(8,128)(2,1)S(1)} %get-tuple-element.59), channel_id=1, source_target_pairs={{0,8},{4,12},{8,0},{12,4},{16,24},{20,28},{24,16},{28,20},{1,9},{5... | collective-permute-start | bytes 491528 | tf_op jit(solution)/shard_map/ppermute | solution.py:69
  124.4 12.0 %collective-permute-start.32 = (bf16[64,1280]{1,0:T(8,128)(2,1)S(1)}, bf16[64,1280]{1,0:T(8,128)(2,1)S(1)}, u32[]{:S(2)}, u32[]{:S(2)}) collective-permute-start(bf16[64,1280]{1,0:T(8,128)(2,1)S(1)} %fusion.20), channel_id=1, source_target_pairs={{0,16},{4,20},{8,24},{12,28},{16,0},{20,4},{24,8},{28,12},{1,17},{... | collective-permute-start | bytes 491528 | tf_op jit(solution)/shard_map/ppermute | solution.py:69
  (9 other events, 68.8 us)

commit v9 on v8

--- a/solution.py
+++ b/solution.py
@@ -84,8 +84,9 @@
         chunk_order = chunk_order + [c ^ bit for c in chunk_order]
         bit //= 2
 
-    def gather_etp(value):
-        for b in bits:
+    def gather_etp(value, ties=()):
+        for i, b in enumerate(bits):
+            value = after(value, *ties[i]) if i < len(ties) else value
             value = jnp.concatenate([value, over_etp(value, b)], axis=0)
         return value
 
@@ -126,8 +127,7 @@
             return jnp.where(at_end, first, second)
 
         weights = [jnp.concatenate([w_gate, w_up], axis=1)]
-        for j in range(1, inner):
-            weights.append(jnp.concatenate([over_inner(w_gate, j), over_inner(w_up, j)], axis=1))
+        weights += [over_inner(weights[0], j) for j in range(1, inner)]
         weights = jnp.concatenate(weights, axis=0)
 
         onehot = (slots[:, None] == jnp.arange(tok, dtype=slots.dtype)[None, :]).astype(BF16)
@@ -146,30 +146,36 @@
 
         x_chunks = {}
 
-        def multiply(k, last):
-            x_chunks[k] = gather_etp(after(got[k], last))
+        def multiply(k, *ties):
+            x_chunks[k] = after(x_chunks[k], *ties)
             return jnp.dot(x_chunks[k], weights, preferred_element_type=F32)
 
         if relay:
-            far = multiply(3, rows).astype(BF16)
+            x_chunks[3] = gather_etp(got[3])
+            x_chunks[1] = gather_etp(got[1])
+            far = multiply(3).astype(BF16)
             swapped = outer_pairs(far, swap)
-            near = after(multiply(1, rows).astype(BF16), far)
+            near = after(multiply(1, far).astype(BF16), far)
             crossed = outer_pairs(near, middle)
-            two = after(multiply(2, near), near)
-            inwards = outer_pairs(after(two.astype(BF16), near), inward)
-            own = multiply(0, two)
-            relayed = pick(near, (two + swapped.astype(F32)).astype(BF16))
+            x_chunks[2] = gather_etp(got[2], [[], [near]])
+            x_chunks[0] = gather_etp(got[0], [[got[2]], [near]])
+            two = after(multiply(2, swapped, crossed), swapped)
+            inwards = outer_pairs(two.astype(BF16), inward)
+            relayed = pick(near, (after(two, swapped) + swapped.astype(F32)).astype(BF16))
             cycled = outer_pairs(relayed, back)
-            own = own + crossed.astype(F32) + inwards.astype(F32)
+            own = multiply(0, relayed) + crossed.astype(F32) + inwards.astype(F32)
             own = own + jnp.where(at_end, swapped.astype(F32), 0.0)
             parts = [cycled]
+            last = relayed
         else:
             last, parts = rows, []
+            x_chunks[0] = gather_etp(got[0])
             for k in far_first:
-                last = multiply(k, last).astype(BF16)
+                x_chunks[k] = gather_etp(got[k], [[last]])
+                last = multiply(k).astype(BF16)
                 parts.append(over_outer(last, k))
             own = multiply(0, last)
-        probs = gather_etp(after(gate_probs, x_chunks[0]))
+        probs = gather_etp(after(gate_probs, last))
         order = etp ^ jnp.array(chunk_order, jnp.int32)
         hidden, paired = gate_call(order, own, probs[:, None], d_hidden, parts)
 
@@ -193,27 +199,28 @@
             cycled = outer_pairs(paired, cycle)
             last = advance(0, paired)
             crossed = outer_pairs(after(paired, last), middle)
-            outwards = outer_pairs(after(paired, sums[0]), outward)
+            outwards = outer_pairs(after(paired, last), outward)
             turn = after(pick(paired, cycled), paired)
             grads[3] = outer_pairs(turn, swap)
-            grads[1] = pick(after(cycled, turn), crossed)
-            grads[2] = pick(outwards, after(cycled, grads[1]))
-            sequence = [0, 1, 3, 2]
+            grads[2] = pick(outwards, after(cycled, turn))
+            grads[1] = pick(after(cycled, grads[2]), crossed)
+            sequence = [0, 2, 3, 1]
+            early, late = [0, 2], [3, 1]
             last = turn
         else:
             for k in near_first:
                 grads[k] = over_outer(paired, k)
             sequence = keys
+            early, late = keys[: max(outer - 1, 1)], keys[max(outer - 1, 1) :]
             last = grads[near_first[0]] if outer > 1 else paired
-        early, late = sequence[: max(outer - 1, 1)], sequence[max(outer - 1, 1) :]
         for k in early:
             last = advance(k, last) if k not in sums else last
 
         leaving = []
         for j in range(1, inner):
             value = weight_grad(early, j, last)
-            for k in late:
-                value = after(value, last) + weight_grad([k], j, value)
+            if late:
+                value = after(value, last) + weight_grad(late, j, value)
             leaving.append(value.astype(BF16))
         arriving = [over_inner(leaving[j - 1], j) for j in range(1, inner)]
         last = leaving[0] if inner > 1 else last

time: 142 us -> 144 us (1.014)
  starting transfers between devices: 38 us -> 40.9 us
    ppermute x8, waiting for transfers between devices: 36.9 us -> 45.1 us  [outer_pairs(): return lax.ppermute(value, 'dp', pairs)]
    ppermute x3 -> x2, waiting for transfers between devices: 6.7 us -> 0.01 us  [over_inner(): return lax.ppermute(value, 'dp', pairs)]
    ppermute x8, starting transfers between devices: 11.7 us -> 17.4 us  [outer_pairs(): return lax.ppermute(value, 'dp', pairs)]
    ppermute x18, starting transfers between devices: 12.8 us -> 10.3 us  [over_etp(): return lax.ppermute(value, 'etp', pairs)]
    ppermute x18, waiting for transfers between devices: 21.1 us -> 18.8 us  [over_etp(): return lax.ppermute(value, 'etp', pairs)]
    ppermute x3 -> x2, starting transfers between devices: 3.59 us -> 3.12 us  [over_inner(): return lax.ppermute(value, 'dp', pairs)]
  transfers between devices with their start and end apart: 35 -> 34, of which waited for: 20 -> 17; matrix products, arithmetic and copies ran while one was open for 10% -> 10% of each run, Pallas kernels for 0% -> 0%
where the time goes in v9:
time: 144 us
  waiting for transfers between devices  80 us (56%)
  starting transfers between devices  40.9 us (28%)
  matrix products  15.9 us (11%)
  other arithmetic  2.95 us (2%)
  local copies, waits for them, and re-layouts  1.53 us (1%)
  Pallas kernels  1.51 us (1%)
    ppermute x8, waiting for transfers between devices, outer_pairs(): return lax.ppermute(value, 'dp', pairs)  45.1 us
    ppermute x18, waiting for transfers between devices, over_etp(): return lax.ppermute(value, 'etp', pairs)  18.8 us
    ppermute x8, starting transfers between devices, outer_pairs(): return lax.ppermute(value, 'dp', pairs)  17.4 us
    ppermute x6, waiting for transfers between devices, over_outer(): return lax.ppermute(value, 'dp', pairs)  16.1 us
    ppermute x18, starting transfers between devices, over_etp(): return lax.ppermute(value, 'etp', pairs)  10.3 us
    ppermute x6, starting transfers between devices, over_outer(): return lax.ppermute(value, 'dp', pairs)  10.1 us
    dot_general x1, matrix products, shards(): lax.dot_general(onehot, dx, (((0,), (0,)), ((), ())), preferred_element_t...  4 us
    dot_general x1, matrix products, shards(): rows = jnp.dot(onehot, tokens, preferred_element_type=F32).astype(BF16)  3.57 us
  transfers between devices with their start and end apart: 34, of which 17 were waited for; matrix products, arithmetic and copies ran while one was open for 10% of the time, Pallas kernels for 0%

profile of v9, /device:TPU:0, one launch (start us, length us, event | category | flops | bytes accessed | tf_op | source)
XLA Modules:
  0.0 144.0 jit_solution(8210925071321016943)
XLA Ops:
  0.7 3.6 %convolution_convert_fusion.1 = bf16[64,5120]{1,0:T(8,128)(2,1)S(1)} fusion(bf16[512,5120]{1,0:T(8,128)(2,1)} %param.7, s32[64]{0:T(128)} %param.8), kind=kOutput, calls=%fused_computation.1 | convolution fusion | flops 335904768 | bytes 5898496 | tf_op jit(solution)/shard_map/dot_general | solution.py:134
  4.5 4.1 %collective-permute-start = (bf16[64,1280]{1,0:T(8,128)(2,1)S(1)}, bf16[64,1280]{1,0:T(8,128)(2,1)S(1)}, u32[]{:S(2)}, u32[]{:S(2)}) collective-permute-start(bf16[64,1280]{1,0:T(8,128)(2,1)S(1)} %pad_maximum_fusion.13), channel_id=1, source_target_pairs={{0,16},{4,20},{8,24},{12,28},{16,0},{20,4},{24,8},{28,12},{1,17},{... | collective-permute-start | bytes 491528 | tf_op jit(solution)/shard_map/ppermute | solution.py:69
  8.6 1.4 collective-permute-start.3
  10.5 1.6 %collective-permute-start.8 = (bf16[640,768]{1,0:T(8,128)(2,1)S(1)}, bf16[640,768]{1,0:T(8,128)(2,1)S(1)}, u32[]{:S(2)}, u32[]{:S(2)}) collective-permute-start(bf16[640,768]{1,0:T(8,128)(2,1)S(1)} %constant_dynamic-update-slice_fusion), channel_id=1, source_target_pairs={{0,4},{4,0},{8,12},{12,8},{16,20},{20,16},{24,28},{28,24},{1,5},{5... | collective-permute-start | bytes 2949128 | tf_op jit(solution)/shard_map/ppermute | solution.py:73
  12.1 6.5 %collective-permute-done.3 = bf16[64,1280]{1,0:T(8,128)(2,1)S(1)} collective-permute-done((bf16[64,1280]{1,0:T(8,128)(2,1)S(1)}, bf16[64,1280]{1,0:T(8,128)(2,1)S(1)}, u32[]{:S(2)}, u32[]{:S(2)}) %collective-permute-start.3) | collective-permute-done | bytes 163872 | tf_op jit(solution)/shard_map/ppermute | solution.py:69
  18.6 2.8 %collective-permute-done.2 = bf16[64,1280]{1,0:T(8,128)(2,1)S(1)} collective-permute-done((bf16[64,1280]{1,0:T(8,128)(2,1)S(1)}, bf16[64,1280]{1,0:T(8,128)(2,1)S(1)}, u32[]{:S(2)}, u32[]{:S(2)}) %collective-permute-start.2) | collective-permute-done | bytes 163872 | tf_op jit(solution)/shard_map/ppermute | solution.py:69
  21.4 1.6 %collective-permute-start.6 = (bf16[64,1280]{1,0:T(8,128)(2,1)S(1)}, bf16[64,1280]{1,0:T(8,128)(2,1)S(1)}, u32[]{:S(2)}, u32[]{:S(2)}) collective-permute-start(bf16[64,1280]{1,0:T(8,128)(2,1)S(1)} %get-tuple-element.78), channel_id=1, source_target_pairs={{0,2},{1,3},{2,0},{3,1},{4,6},{5,7},{6,4},{7,5},{8,10},{9,11},{10,... | collective-permute-start | bytes 491528 | tf_op jit(solution)/shard_map/ppermute | solution.py:77
  23.5 1.6 %collective-permute-start.4 = (bf16[64,1280]{1,0:T(8,128)(2,1)S(1)}, bf16[64,1280]{1,0:T(8,128)(2,1)S(1)}, u32[]{:S(2)}, u32[]{:S(2)}) collective-permute-start(bf16[64,1280]{1,0:T(8,128)(2,1)S(1)} %get-tuple-element.79), channel_id=1, source_target_pairs={{0,2},{1,3},{2,0},{3,1},{4,6},{5,7},{6,4},{7,5},{8,10},{9,11},{10,... | collective-permute-start | bytes 491528 | tf_op jit(solution)/shard_map/ppermute | solution.py:77
  25.6 3.0 %collective-permute-done.6 = bf16[64,1280]{1,0:T(8,128)(2,1)S(1)} collective-permute-done((bf16[64,1280]{1,0:T(8,128)(2,1)S(1)}, bf16[64,1280]{1,0:T(8,128)(2,1)S(1)}, u32[]{:S(2)}, u32[]{:S(2)}) %collective-permute-start.6) | collective-permute-done | bytes 163872 | tf_op jit(solution)/shard_map/ppermute | solution.py:77
  28.7 5.7 %collective-permute-done.4 = bf16[64,1280]{1,0:T(8,128)(2,1)S(1)} collective-permute-done((bf16[64,1280]{1,0:T(8,128)(2,1)S(1)}, bf16[64,1280]{1,0:T(8,128)(2,1)S(1)}, u32[]{:S(2)}, u32[]{:S(2)}) %collective-permute-start.4) | collective-permute-done | bytes 163872 | tf_op jit(solution)/shard_map/ppermute | solution.py:77
  34.5 1.7 %collective-permute-done.10 = bf16[64,1280]{1,0:T(8,128)(2,1)S(1)} collective-permute-done((bf16[64,1280]{1,0:T(8,128)(2,1)S(1)}, bf16[64,1280]{1,0:T(8,128)(2,1)S(1)}, u32[]{:S(2)}, u32[]{:S(2)}) %collective-permute-start.10) | collective-permute-done | bytes 163872 | tf_op jit(solution)/shard_map/ppermute | solution.py:77
  37.8 4.8 %collective-permute-start.12 = (bf16[256,768]{1,0:T(8,128)(2,1)S(1)}, bf16[256,768]{1,0:T(8,128)(2,1)S(1)}, u32[]{:S(2)}, u32[]{:S(2)}) collective-permute-start(bf16[256,768]{1,0:T(8,128)(2,1)S(1)} %convolution_convert_fusion.3), channel_id=1, source_target_pairs={{0,8},{4,12},{8,0},{12,4},{16,24},{20,28},{24,16},{28,20},{1,9},{5... | collective-permute-start | bytes 1179656 | tf_op jit(solution)/shard_map/ppermute | solution.py:107
  43.6 8.7 %collective-permute-done.12 = bf16[256,768]{1,0:T(8,128)(2,1)S(1)} collective-permute-done((bf16[256,768]{1,0:T(8,128)(2,1)S(1)}, bf16[256,768]{1,0:T(8,128)(2,1)S(1)}, u32[]{:S(2)}, u32[]{:S(2)}) %collective-permute-start.12) | collective-permute-done | bytes 393248 | tf_op jit(solution)/shard_map/ppermute | solution.py:107
  53.7 1.5 %collective-permute-start.15 = (bf16[64]{0:T(256)(128)(2,1)S(1)}, bf16[64]{0:T(256)(128)(2,1)S(1)}, u32[]{:S(2)}, u32[]{:S(2)}) collective-permute-start(bf16[64]{0:T(256)(128)(2,1)S(1)} %copy-done.4), channel_id=1, source_target_pairs={{0,2},{1,3},{2,0},{3,1},{4,6},{5,7},{6,4},{7,5},{8,10},{9,11},{10,... | collective-permute-start | bytes 392 | tf_op jit(solution)/shard_map/ppermute | solution.py:77
  55.2 7.5 %collective-permute-start.14 = (bf16[256,768]{1,0:T(8,128)(2,1)S(1)}, bf16[256,768]{1,0:T(8,128)(2,1)S(1)}, u32[]{:S(2)}, u32[]{:S(2)}) collective-permute-start(bf16[256,768]{1,0:T(8,128)(2,1)S(1)} %convert_element_type.88), channel_id=1, source_target_pairs={{0,16},{4,20},{24,8},{28,12},{1,17},{5,21},{25,9},{29,13},{2,18},{... | collective-permute-start | bytes 1179656 | tf_op jit(solution)/shard_map/ppermute | solution.py:107
  64.1 8.2 %collective-permute-done.14 = bf16[256,768]{1,0:T(8,128)(2,1)S(1)} collective-permute-done((bf16[256,768]{1,0:T(8,128)(2,1)S(1)}, bf16[256,768]{1,0:T(8,128)(2,1)S(1)}, u32[]{:S(2)}, u32[]{:S(2)}) %collective-permute-start.14) | collective-permute-done | bytes 393248 | tf_op jit(solution)/shard_map/ppermute | solution.py:107
  73.0 7.9 %collective-permute-done.17.refs_0_ = bf16[256,768]{1,0:T(8,128)(2,1)S(1)} collective-permute-done((bf16[256,768]{1,0:T(8,128)(2,1)S(1)}, bf16[256,768]{1,0:T(8,128)(2,1)S(1)}, u32[]{:S(2)}, u32[]{:S(2)}) %collective-permute-start.17) | collective-permute-done | bytes 393248 | tf_op jit(solution)/shard_map/ppermute | solution.py:107
  80.9 1.5 %shard_map.102 = (bf16[256,384]{1,0:T(8,128)(2,1)}, bf16[256,768]{1,0:T(8,128)(2,1)S(1)}) custom-call(s32[4]{0:T(128)S(1)} %broadcast_xor_fusion.order_ref, f32[256,768]{1,0:T(8,128)S(1)} %fusion.9.pre_ref, bf16[256,1]{1,0:T(8,128)(2,1)S(1)} %broadcast_in_dim.15.prob_ref, bf16[256,384]{1,0:T(8,128)(2,1)S(1)} %copy-done, ...), custom_call_target="tpu_custom_call" | custom-call | flops 1966080 | bytes 2949120 | tf_op jit(solution)/shard_map/pallas_call | solution.py:49
  87.0 8.2 %collective-permute-done.20 = bf16[256,768]{1,0:T(8,128)(2,1)S(1)} collective-permute-done((bf16[256,768]{1,0:T(8,128)(2,1)S(1)}, bf16[256,768]{1,0:T(8,128)(2,1)S(1)}, u32[]{:S(2)}, u32[]{:S(2)}) %collective-permute-start.20) | collective-permute-done | bytes 393248 | tf_op jit(solution)/shard_map/ppermute | solution.py:107
  95.2 1.6 %collective-permute-start.23 = (bf16[256,768]{1,0:T(8,128)(2,1)S(1)}, bf16[256,768]{1,0:T(8,128)(2,1)S(1)}, u32[]{:S(2)}, u32[]{:S(2)}) collective-permute-start(bf16[256,768]{1,0:T(8,128)(2,1)S(1)} %broadcast_select_fusion.2), channel_id=1, source_target_pairs={{0,8},{4,12},{8,0},{12,4},{16,24},{20,28},{24,16},{28,20},{1,9},{5... | collective-permute-start | bytes 1179656 | tf_op jit(solution)/shard_map/ppermute | solution.py:107
  96.8 7.8 %collective-permute-done.21 = bf16[256,768]{1,0:T(8,128)(2,1)S(1)} collective-permute-done((bf16[256,768]{1,0:T(8,128)(2,1)S(1)}, bf16[256,768]{1,0:T(8,128)(2,1)S(1)}, u32[]{:S(2)}, u32[]{:S(2)}) %collective-permute-start.21) | collective-permute-done | bytes 393248 | tf_op jit(solution)/shard_map/ppermute | solution.py:107
  106.3 1.5 %collective-permute-done.29 = bf16[128,1280]{1,0:T(8,128)(2,1)S(1)} collective-permute-done((bf16[128,1280]{1,0:T(8,128)(2,1)S(1)}, bf16[128,1280]{1,0:T(8,128)(2,1)S(1)}, u32[]{:S(2)}, u32[]{:S(2)}) %collective-permute-start.29) | collective-permute-done | bytes 327712 | tf_op jit(solution)/shard_map/ppermute | solution.py:77
  108.5 4.4 %collective-permute-done.23 = bf16[256,768]{1,0:T(8,128)(2,1)S(1)} collective-permute-done((bf16[256,768]{1,0:T(8,128)(2,1)S(1)}, bf16[256,768]{1,0:T(8,128)(2,1)S(1)}, u32[]{:S(2)}, u32[]{:S(2)}) %collective-permute-start.23) | collective-permute-done | bytes 393248 | tf_op jit(solution)/shard_map/ppermute | solution.py:107
  114.5 1.6 %collective-permute-start.33 = (bf16[640,768]{1,0:T(8,128)(2,1)S(1)}, bf16[640,768]{1,0:T(8,128)(2,1)S(1)}, u32[]{:S(2)}, u32[]{:S(2)}) collective-permute-start(bf16[640,768]{1,0:T(8,128)(2,1)S(1)} %add_convert_fusion), channel_id=1, source_target_pairs={{0,4},{4,0},{8,12},{12,8},{16,20},{20,16},{24,28},{28,24},{1,5},{5... | collective-permute-start | bytes 2949128 | tf_op jit(solution)/shard_map/ppermute | solution.py:73
  119.5 1.6 %collective-permute-start.25 = (bf16[64,1280]{1,0:T(8,128)(2,1)S(1)}, bf16[64,1280]{1,0:T(8,128)(2,1)S(1)}, u32[]{:S(2)}, u32[]{:S(2)}) collective-permute-start(bf16[64,1280]{1,0:T(8,128)(2,1)S(1)} %slice.222), channel_id=1, source_target_pairs={{0,2},{1,3},{2,0},{3,1},{4,6},{5,7},{6,4},{7,5},{8,10},{9,11},{10,... | collective-permute-start | bytes 491528 | tf_op jit(solution)/shard_map/ppermute | solution.py:77
  122.5 3.4 %collective-permute-done.27 = bf16[64,1280]{1,0:T(8,128)(2,1)S(1)} collective-permute-done((bf16[64,1280]{1,0:T(8,128)(2,1)S(1)}, bf16[64,1280]{1,0:T(8,128)(2,1)S(1)}, u32[]{:S(2)}, u32[]{:S(2)}) %collective-permute-start.27) | collective-permute-done | bytes 163872 | tf_op jit(solution)/shard_map/ppermute | solution.py:77
  125.9 2.6 %collective-permute-done.25 = bf16[64,1280]{1,0:T(8,128)(2,1)S(1)} collective-permute-done((bf16[64,1280]{1,0:T(8,128)(2,1)S(1)}, bf16[64,1280]{1,0:T(8,128)(2,1)S(1)}, u32[]{:S(2)}, u32[]{:S(2)}) %collective-permute-start.25) | collective-permute-done | bytes 163872 | tf_op jit(solution)/shard_map/ppermute | solution.py:77
  128.7 1.5 %collective-permute-start.28 = (bf16[64,1280]{1,0:T(8,128)(2,1)S(1)}, bf16[64,1280]{1,0:T(8,128)(2,1)S(1)}, u32[]{:S(2)}, u32[]{:S(2)}) collective-permute-start(bf16[64,1280]{1,0:T(8,128)(2,1)S(1)} %broadcast_select_fusion.4), channel_id=1, source_target_pairs={{0,8},{4,12},{8,0},{12,4},{16,24},{20,28},{24,16},{28,20},{1,9},{5... | collective-permute-start | bytes 491528 | tf_op jit(solution)/shard_map/ppermute | solution.py:69
  131.2 1.4 collective-permute-start.32
  132.8 5.7 %collective-permute-done.32 = bf16[64,1280]{1,0:T(8,128)(2,1)S(1)} collective-permute-done((bf16[64,1280]{1,0:T(8,128)(2,1)S(1)}, bf16[64,1280]{1,0:T(8,128)(2,1)S(1)}, u32[]{:S(2)}, u32[]{:S(2)}) %collective-permute-start.32) | collective-permute-done | bytes 163872 | tf_op jit(solution)/shard_map/ppermute | solution.py:69
  138.6 4.0 %convolution_convert_fusion = bf16[512,5120]{1,0:T(8,128)(2,1)} fusion(bf16[64,5120]{1,0:T(8,128)(2,1)S(1)} %slice_dynamic-update-slice_fusion.2, s32[64]{0:T(128)S(1)} %copy-done.3), kind=kOutput, calls=%fused_computation | convolution fusion | flops 338198528 | bytes 5898496 | tf_op jit(solution)/shard_map/dot_general | solution.py:246
  142.6 1.4 slice_add_fusion
  (119 shorter events, 22.6 us)
Async XLA Ops:
  4.5 18.5 %collective-permute-start = (bf16[64,1280]{1,0:T(8,128)(2,1)S(1)}, bf16[64,1280]{1,0:T(8,128)(2,1)S(1)}, u32[]{:S(2)}, u32[]{:S(2)}) collective-permute-start(bf16[64,1280]{1,0:T(8,128)(2,1)S(1)} %pad_maximum_fusion.13), channel_id=1, source_target_pairs={{0,16},{4,20},{8,24},{12,28},{16,0},{20,4},{24,8},{28,12},{1,17},{... | collective-permute-start | bytes 491528 | tf_op jit(solution)/shard_map/ppermute | solution.py:69
  8.6 10.0 %collective-permute-start.3 = (bf16[64,1280]{1,0:T(8,128)(2,1)S(1)}, bf16[64,1280]{1,0:T(8,128)(2,1)S(1)}, u32[]{:S(2)}, u32[]{:S(2)}) collective-permute-start(bf16[64,1280]{1,0:T(8,128)(2,1)S(1)} %pad_maximum_fusion.15), channel_id=1, source_target_pairs={{0,24},{4,28},{8,16},{12,20},{16,8},{20,12},{24,0},{28,4},{1,25},{... | collective-permute-start | bytes 491528 | tf_op jit(solution)/shard_map/ppermute | solution.py:69
  10.0 11.3 %collective-permute-start.2 = (bf16[64,1280]{1,0:T(8,128)(2,1)S(1)}, bf16[64,1280]{1,0:T(8,128)(2,1)S(1)}, u32[]{:S(2)}, u32[]{:S(2)}) collective-permute-start(bf16[64,1280]{1,0:T(8,128)(2,1)S(1)} %pad_maximum_fusion.14), channel_id=1, source_target_pairs={{0,8},{4,12},{8,0},{12,4},{16,24},{20,28},{24,16},{28,20},{1,9},{5... | collective-permute-start | bytes 491528 | tf_op jit(solution)/shard_map/ppermute | solution.py:69
  10.5 25.8 %collective-permute-start.8 = (bf16[640,768]{1,0:T(8,128)(2,1)S(1)}, bf16[640,768]{1,0:T(8,128)(2,1)S(1)}, u32[]{:S(2)}, u32[]{:S(2)}) collective-permute-start(bf16[640,768]{1,0:T(8,128)(2,1)S(1)} %constant_dynamic-update-slice_fusion), channel_id=1, source_target_pairs={{0,4},{4,0},{8,12},{12,8},{16,20},{20,16},{24,28},{28,24},{1,5},{5... | collective-permute-start | bytes 2949128 | tf_op jit(solution)/shard_map/ppermute | solution.py:73
  21.4 7.2 %collective-permute-start.6 = (bf16[64,1280]{1,0:T(8,128)(2,1)S(1)}, bf16[64,1280]{1,0:T(8,128)(2,1)S(1)}, u32[]{:S(2)}, u32[]{:S(2)}) collective-permute-start(bf16[64,1280]{1,0:T(8,128)(2,1)S(1)} %get-tuple-element.78), channel_id=1, source_target_pairs={{0,2},{1,3},{2,0},{3,1},{4,6},{5,7},{6,4},{7,5},{8,10},{9,11},{10,... | collective-permute-start | bytes 491528 | tf_op jit(solution)/shard_map/ppermute | solution.py:77
  23.0 14.7 %collective-permute-start.1 = (bf16[64,1280]{1,0:T(8,128)(2,1)S(1)}, bf16[64,1280]{1,0:T(8,128)(2,1)S(1)}, u32[]{:S(2)}, u32[]{:S(2)}) collective-permute-start(bf16[64,1280]{1,0:T(8,128)(2,1)S(1)} %pad_maximum_fusion.12), channel_id=1, source_target_pairs={{0,2},{1,3},{2,0},{3,1},{4,6},{5,7},{6,4},{7,5},{8,10},{9,11},{10,... | collective-permute-start | bytes 491528 | tf_op jit(solution)/shard_map/ppermute | solution.py:77
  23.5 10.8 %collective-permute-start.4 = (bf16[64,1280]{1,0:T(8,128)(2,1)S(1)}, bf16[64,1280]{1,0:T(8,128)(2,1)S(1)}, u32[]{:S(2)}, u32[]{:S(2)}) collective-permute-start(bf16[64,1280]{1,0:T(8,128)(2,1)S(1)} %get-tuple-element.79), channel_id=1, source_target_pairs={{0,2},{1,3},{2,0},{3,1},{4,6},{5,7},{6,4},{7,5},{8,10},{9,11},{10,... | collective-permute-start | bytes 491528 | tf_op jit(solution)/shard_map/ppermute | solution.py:77
  25.1 11.0 %collective-permute-start.10 = (bf16[64,1280]{1,0:T(8,128)(2,1)S(1)}, bf16[64,1280]{1,0:T(8,128)(2,1)S(1)}, u32[]{:S(2)}, u32[]{:S(2)}) collective-permute-start(bf16[64,1280]{1,0:T(8,128)(2,1)S(1)} %collective-permute-done), channel_id=1, source_target_pairs={{0,2},{1,3},{2,0},{3,1},{4,6},{5,7},{6,4},{7,5},{8,10},{9,11},{10,... | collective-permute-start | bytes 491528 | tf_op jit(solution)/shard_map/ppermute | solution.py:77
  28.6 7.6 %collective-permute-start.7 = (bf16[128,1280]{1,0:T(8,128)(2,1)S(1)}, bf16[128,1280]{1,0:T(8,128)(2,1)S(1)}, u32[]{:S(2)}, u32[]{:S(2)}) collective-permute-start(bf16[128,1280]{1,0:T(8,128)(2,1)S(1)} %pad_maximum_fusion.10), channel_id=1, source_target_pairs={{0,1},{1,0},{2,3},{3,2},{4,5},{5,4},{6,7},{7,6},{8,9},{9,8},{10,11... | collective-permute-start | bytes 983048 | tf_op jit(solution)/shard_map/ppermute | solution.py:77
  34.4 1.8 %collective-permute-start.5 = (bf16[128,1280]{1,0:T(8,128)(2,1)S(1)}, bf16[128,1280]{1,0:T(8,128)(2,1)S(1)}, u32[]{:S(2)}, u32[]{:S(2)}) collective-permute-start(bf16[128,1280]{1,0:T(8,128)(2,1)S(1)} %pad_maximum_fusion.9), channel_id=1, source_target_pairs={{0,1},{1,0},{2,3},{3,2},{4,5},{5,4},{6,7},{7,6},{8,9},{9,8},{10,11... | collective-permute-start | bytes 983048 | tf_op jit(solution)/shard_map/ppermute | solution.py:77
  37.6 5.9 %collective-permute-start.11 = (bf16[128,1280]{1,0:T(8,128)(2,1)S(1)}, bf16[128,1280]{1,0:T(8,128)(2,1)S(1)}, u32[]{:S(2)}, u32[]{:S(2)}) collective-permute-start(bf16[128,1280]{1,0:T(8,128)(2,1)S(1)} %pad_maximum_fusion.11), channel_id=1, source_target_pairs={{0,1},{1,0},{2,3},{3,2},{4,5},{5,4},{6,7},{7,6},{8,9},{9,8},{10,11... | collective-permute-start | bytes 983048 | tf_op jit(solution)/shard_map/ppermute | solution.py:77
  37.8 14.6 %collective-permute-start.12 = (bf16[256,768]{1,0:T(8,128)(2,1)S(1)}, bf16[256,768]{1,0:T(8,128)(2,1)S(1)}, u32[]{:S(2)}, u32[]{:S(2)}) collective-permute-start(bf16[256,768]{1,0:T(8,128)(2,1)S(1)} %convolution_convert_fusion.3), channel_id=1, source_target_pairs={{0,8},{4,12},{8,0},{12,4},{16,24},{20,28},{24,16},{28,20},{1,9},{5... | collective-permute-start | bytes 1179656 | tf_op jit(solution)/shard_map/ppermute | solution.py:107
  42.6 9.8 %collective-permute-start.13 = (bf16[256,768]{1,0:T(8,128)(2,1)S(1)}, bf16[256,768]{1,0:T(8,128)(2,1)S(1)}, u32[]{:S(2)}, u32[]{:S(2)}) collective-permute-start(bf16[256,768]{1,0:T(8,128)(2,1)S(1)} %convolution_convert_fusion.2), channel_id=1, source_target_pairs={{8,16},{12,20},{16,8},{20,12},{9,17},{13,21},{17,9},{21,13},{10,18... | collective-permute-start | bytes 1179656 | tf_op jit(solution)/shard_map/ppermute | solution.py:107
  43.3 19.5 %collective-permute-start.9 = (bf16[128,1280]{1,0:T(8,128)(2,1)S(1)}, bf16[128,1280]{1,0:T(8,128)(2,1)S(1)}, u32[]{:S(2)}, u32[]{:S(2)}) collective-permute-start(bf16[128,1280]{1,0:T(8,128)(2,1)S(1)} %pad_maximum_fusion.8), channel_id=1, source_target_pairs={{0,1},{1,0},{2,3},{3,2},{4,5},{5,4},{6,7},{7,6},{8,9},{9,8},{10,11... | collective-permute-start | bytes 983048 | tf_op jit(solution)/shard_map/ppermute | solution.py:77
  53.7 9.1 %collective-permute-start.15 = (bf16[64]{0:T(256)(128)(2,1)S(1)}, bf16[64]{0:T(256)(128)(2,1)S(1)}, u32[]{:S(2)}, u32[]{:S(2)}) collective-permute-start(bf16[64]{0:T(256)(128)(2,1)S(1)} %copy-done.4), channel_id=1, source_target_pairs={{0,2},{1,3},{2,0},{3,1},{4,6},{5,7},{6,4},{7,5},{8,10},{9,11},{10,... | collective-permute-start | bytes 392 | tf_op jit(solution)/shard_map/ppermute | solution.py:77
  55.2 17.1 %collective-permute-start.14 = (bf16[256,768]{1,0:T(8,128)(2,1)S(1)}, bf16[256,768]{1,0:T(8,128)(2,1)S(1)}, u32[]{:S(2)}, u32[]{:S(2)}) collective-permute-start(bf16[256,768]{1,0:T(8,128)(2,1)S(1)} %convert_element_type.88), channel_id=1, source_target_pairs={{0,16},{4,20},{24,8},{28,12},{1,17},{5,21},{25,9},{29,13},{2,18},{... | collective-permute-start | bytes 1179656 | tf_op jit(solution)/shard_map/ppermute | solution.py:107
  62.9 18.0 %collective-permute-start.17 = (bf16[256,768]{1,0:T(8,128)(2,1)S(1)}, bf16[256,768]{1,0:T(8,128)(2,1)S(1)}, u32[]{:S(2)}, u32[]{:S(2)}) collective-permute-start(bf16[256,768]{1,0:T(8,128)(2,1)S(1)} %fusion.18), channel_id=1, source_target_pairs={{16,0},{20,4},{24,16},{28,20},{8,24},{12,28},{0,8},{4,12},{17,1},{... | collective-permute-start | bytes 1179656 | tf_op jit(solution)/shard_map/ppermute | solution.py:107
  83.2 3.1 %collective-permute-start.18 = (bf16[128,1280]{1,0:T(8,128)(2,1)S(1)}, bf16[128,1280]{1,0:T(8,128)(2,1)S(1)}, u32[]{:S(2)}, u32[]{:S(2)}) collective-permute-start(bf16[128,1280]{1,0:T(8,128)(2,1)S(1)} %slice.219), channel_id=1, source_target_pairs={{0,1},{1,0},{2,3},{3,2},{4,5},{5,4},{6,7},{7,6},{8,9},{9,8},{10,11... | collective-permute-start | bytes 983048 | tf_op jit(solution)/shard_map/ppermute | solution.py:77
  83.5 11.6 %collective-permute-start.20 = (bf16[256,768]{1,0:T(8,128)(2,1)S(1)}, bf16[256,768]{1,0:T(8,128)(2,1)S(1)}, u32[]{:S(2)}, u32[]{:S(2)}) collective-permute-start(bf16[256,768]{1,0:T(8,128)(2,1)S(1)} %get-tuple-element.44), channel_id=1, source_target_pairs={{0,16},{4,20},{16,24},{20,28},{24,8},{28,12},{8,0},{12,4},{1,17},{... | collective-permute-start | bytes 1179656 | tf_op jit(solution)/shard_map/ppermute | solution.py:107
  84.1 20.4 %collective-permute-start.21 = (bf16[256,768]{1,0:T(8,128)(2,1)S(1)}, bf16[256,768]{1,0:T(8,128)(2,1)S(1)}, u32[]{:S(2)}, u32[]{:S(2)}) collective-permute-start(bf16[256,768]{1,0:T(8,128)(2,1)S(1)} %get-tuple-element.44), channel_id=1, source_target_pairs={{16,0},{20,4},{8,24},{12,28},{17,1},{21,5},{9,25},{13,29},{18,2},{... | collective-permute-start | bytes 1179656 | tf_op jit(solution)/shard_map/ppermute | solution.py:107
  85.4 20.8 %collective-permute-start.22 = (bf16[256,768]{1,0:T(8,128)(2,1)S(1)}, bf16[256,768]{1,0:T(8,128)(2,1)S(1)}, u32[]{:S(2)}, u32[]{:S(2)}) collective-permute-start(bf16[256,768]{1,0:T(8,128)(2,1)S(1)} %get-tuple-element.44), channel_id=1, source_target_pairs={{8,16},{12,20},{16,8},{20,12},{9,17},{13,21},{17,9},{21,13},{10,18... | collective-permute-start | bytes 1179656 | tf_op jit(solution)/shard_map/ppermute | solution.py:107
  86.4 19.9 %collective-permute-start.19 = (bf16[64,1280]{1,0:T(8,128)(2,1)S(1)}, bf16[64,1280]{1,0:T(8,128)(2,1)S(1)}, u32[]{:S(2)}, u32[]{:S(2)}) collective-permute-start(bf16[64,1280]{1,0:T(8,128)(2,1)S(1)} %slice.223), channel_id=1, source_target_pairs={{0,2},{1,3},{2,0},{3,1},{4,6},{5,7},{6,4},{7,5},{8,10},{9,11},{10,... | collective-permute-start | bytes 491528 | tf_op jit(solution)/shard_map/ppermute | solution.py:77
  95.2 17.7 %collective-permute-start.23 = (bf16[256,768]{1,0:T(8,128)(2,1)S(1)}, bf16[256,768]{1,0:T(8,128)(2,1)S(1)}, u32[]{:S(2)}, u32[]{:S(2)}) collective-permute-start(bf16[256,768]{1,0:T(8,128)(2,1)S(1)} %broadcast_select_fusion.2), channel_id=1, source_target_pairs={{0,8},{4,12},{8,0},{12,4},{16,24},{20,28},{24,16},{28,20},{1,9},{5... | collective-permute-start | bytes 1179656 | tf_op jit(solution)/shard_map/ppermute | solution.py:107
  107.9 13.1 %collective-permute-start.30 = (bf16[64,1280]{1,0:T(8,128)(2,1)S(1)}, bf16[64,1280]{1,0:T(8,128)(2,1)S(1)}, u32[]{:S(2)}, u32[]{:S(2)}) collective-permute-start(bf16[64,1280]{1,0:T(8,128)(2,1)S(1)} %slice.220), channel_id=1, source_target_pairs={{0,2},{1,3},{2,0},{3,1},{4,6},{5,7},{6,4},{7,5},{8,10},{9,11},{10,... | collective-permute-start | bytes 491528 | tf_op jit(solution)/shard_map/ppermute | solution.py:77
  114.5 28.1 %collective-permute-start.33 = (bf16[640,768]{1,0:T(8,128)(2,1)S(1)}, bf16[640,768]{1,0:T(8,128)(2,1)S(1)}, u32[]{:S(2)}, u32[]{:S(2)}) collective-permute-start(bf16[640,768]{1,0:T(8,128)(2,1)S(1)} %add_convert_fusion), channel_id=1, source_target_pairs={{0,4},{4,0},{8,12},{12,8},{16,20},{20,16},{24,28},{28,24},{1,5},{5... | collective-permute-start | bytes 2949128 | tf_op jit(solution)/shard_map/ppermute | solution.py:73
  116.0 2.7 %collective-permute-start.26 = (bf16[128,1280]{1,0:T(8,128)(2,1)S(1)}, bf16[128,1280]{1,0:T(8,128)(2,1)S(1)}, u32[]{:S(2)}, u32[]{:S(2)}) collective-permute-start(bf16[128,1280]{1,0:T(8,128)(2,1)S(1)} %slice.217), channel_id=1, source_target_pairs={{0,1},{1,0},{2,3},{3,2},{4,5},{5,4},{6,7},{7,6},{8,9},{9,8},{10,11... | collective-permute-start | bytes 983048 | tf_op jit(solution)/shard_map/ppermute | solution.py:77
  116.8 2.6 %collective-permute-start.24 = (bf16[128,1280]{1,0:T(8,128)(2,1)S(1)}, bf16[128,1280]{1,0:T(8,128)(2,1)S(1)}, u32[]{:S(2)}, u32[]{:S(2)}) collective-permute-start(bf16[128,1280]{1,0:T(8,128)(2,1)S(1)} %slice.218), channel_id=1, source_target_pairs={{0,1},{1,0},{2,3},{3,2},{4,5},{5,4},{6,7},{7,6},{8,9},{9,8},{10,11... | collective-permute-start | bytes 983048 | tf_op jit(solution)/shard_map/ppermute | solution.py:77
  118.8 7.1 %collective-permute-start.27 = (bf16[64,1280]{1,0:T(8,128)(2,1)S(1)}, bf16[64,1280]{1,0:T(8,128)(2,1)S(1)}, u32[]{:S(2)}, u32[]{:S(2)}) collective-permute-start(bf16[64,1280]{1,0:T(8,128)(2,1)S(1)} %slice.221), channel_id=1, source_target_pairs={{0,2},{1,3},{2,0},{3,1},{4,6},{5,7},{6,4},{7,5},{8,10},{9,11},{10,... | collective-permute-start | bytes 491528 | tf_op jit(solution)/shard_map/ppermute | solution.py:77
  119.5 9.0 %collective-permute-start.25 = (bf16[64,1280]{1,0:T(8,128)(2,1)S(1)}, bf16[64,1280]{1,0:T(8,128)(2,1)S(1)}, u32[]{:S(2)}, u32[]{:S(2)}) collective-permute-start(bf16[64,1280]{1,0:T(8,128)(2,1)S(1)} %slice.222), channel_id=1, source_target_pairs={{0,2},{1,3},{2,0},{3,1},{4,6},{5,7},{6,4},{7,5},{8,10},{9,11},{10,... | collective-permute-start | bytes 491528 | tf_op jit(solution)/shard_map/ppermute | solution.py:77
  121.1 10.1 %collective-permute-start.31 = (bf16[64,1280]{1,0:T(8,128)(2,1)S(1)}, bf16[64,1280]{1,0:T(8,128)(2,1)S(1)}, u32[]{:S(2)}, u32[]{:S(2)}) collective-permute-start(bf16[64,1280]{1,0:T(8,128)(2,1)S(1)} %fusion.19), channel_id=1, source_target_pairs={{0,16},{4,20},{8,24},{12,28},{16,0},{20,4},{24,8},{28,12},{1,17},{... | collective-permute-start | bytes 491528 | tf_op jit(solution)/shard_map/ppermute | solution.py:69
  128.7 9.8 %collective-permute-start.28 = (bf16[64,1280]{1,0:T(8,128)(2,1)S(1)}, bf16[64,1280]{1,0:T(8,128)(2,1)S(1)}, u32[]{:S(2)}, u32[]{:S(2)}) collective-permute-start(bf16[64,1280]{1,0:T(8,128)(2,1)S(1)} %broadcast_select_fusion.4), channel_id=1, source_target_pairs={{0,8},{4,12},{8,0},{12,4},{16,24},{20,28},{24,16},{28,20},{1,9},{5... | collective-permute-start | bytes 491528 | tf_op jit(solution)/shard_map/ppermute | solution.py:69
  131.2 7.2 %collective-permute-start.32 = (bf16[64,1280]{1,0:T(8,128)(2,1)S(1)}, bf16[64,1280]{1,0:T(8,128)(2,1)S(1)}, u32[]{:S(2)}, u32[]{:S(2)}) collective-permute-start(bf16[64,1280]{1,0:T(8,128)(2,1)S(1)} %get-tuple-element.58), channel_id=1, source_target_pairs={{0,24},{4,28},{8,16},{12,20},{16,8},{20,12},{24,0},{28,4},{1,25},{... | collective-permute-start | bytes 491528 | tf_op jit(solution)/shard_map/ppermute | solution.py:69
  (8 other events, 68.5 us)

commit v10 on v9

--- a/solution.py
+++ b/solution.py
@@ -20,6 +20,13 @@
 
 def after(value, *others):
     return lax.optimization_barrier((value,) + others)[0]
+
+
+def tied(value, *others):
+    for other in others:
+        first = other[(0,) * other.ndim]
+        value = jnp.where(first != first, first.astype(value.dtype), value)
+    return value
 
 
 def gate_kernel(steps, order_ref, pre_ref, prob_ref, cot_ref, *refs):
@@ -86,16 +93,17 @@
 
     def gather_etp(value, ties=()):
         for i, b in enumerate(bits):
-            value = after(value, *ties[i]) if i < len(ties) else value
+            value = tied(value, *ties[i]) if i < len(ties) else value
             value = jnp.concatenate([value, over_etp(value, b)], axis=0)
         return value
 
-    def reduce_etp(value):
+    def reduce_etp(*values):
         for b in reversed(bits):
-            half = value.shape[0] // 2
-            sent = over_etp(value[half:].astype(BF16), b)
-            value = value[:half] + sent.astype(F32)
-        return value
+            half = values[0].shape[0] // 2
+            leaving = [value[half:].astype(BF16) for value in values]
+            got = over_etp(jnp.concatenate(leaving, axis=0) if len(leaving) > 1 else leaving[0], b)
+            values = [v[:half] + got[i * half : (i + 1) * half].astype(F32) for i, v in enumerate(values)]
+        return [value.astype(BF16) for value in values]
 
     near_first = sorted(range(1, outer))
     far_first = near_first[::-1]
@@ -151,14 +159,14 @@
             return jnp.dot(x_chunks[k], weights, preferred_element_type=F32)
 
         if relay:
-            x_chunks[3] = gather_etp(got[3])
+            x_chunks[3] = gather_etp(got[3], [[], [weights[-1:]]])
             x_chunks[1] = gather_etp(got[1])
             far = multiply(3).astype(BF16)
             swapped = outer_pairs(far, swap)
             near = after(multiply(1, far).astype(BF16), far)
             crossed = outer_pairs(near, middle)
-            x_chunks[2] = gather_etp(got[2], [[], [near]])
-            x_chunks[0] = gather_etp(got[0], [[got[2]], [near]])
+            x_chunks[2] = gather_etp(got[2], [[], [swapped, crossed]])
+            x_chunks[0] = gather_etp(got[0], [[], [swapped, crossed]])
             two = after(multiply(2, swapped, crossed), swapped)
             inwards = outer_pairs(two.astype(BF16), inward)
             relayed = pick(near, (after(two, swapped) + swapped.astype(F32)).astype(BF16))
@@ -181,12 +189,15 @@
 
         grads, sums = {0: paired}, {}
 
-        def advance(k, last):
-            partial = lax.dot_general(
-                after(grads[k], last), weights, (((1,), (1,)), ((), ())), preferred_element_type=F32
-            )
-            sums[k] = reduce_etp(partial).astype(BF16)
-            return partial
+        def advance(ks, last):
+            partials = [
+                lax.dot_general(
+                    after(grads[k], last), weights, (((1,), (1,)), ((), ())), preferred_element_type=F32
+                )
+                for k in ks
+            ]
+            sums.update(zip(ks, reduce_etp(*partials)))
+            return partials[-1]
 
         def weight_grad(ks, j, last):
             x_part = jnp.concatenate([x_chunks[k][:, j * depth : (j + 1) * depth] for k in ks], axis=0)
@@ -197,7 +208,7 @@
 
         if relay:
             cycled = outer_pairs(paired, cycle)
-            last = advance(0, paired)
+            last = advance([0], paired)
             crossed = outer_pairs(after(paired, last), middle)
             outwards = outer_pairs(after(paired, last), outward)
             turn = after(pick(paired, cycled), paired)
@@ -214,7 +225,7 @@
             early, late = keys[: max(outer - 1, 1)], keys[max(outer - 1, 1) :]
             last = grads[near_first[0]] if outer > 1 else paired
         for k in early:
-            last = advance(k, last) if k not in sums else last
+            last = advance([k], last) if k not in sums else last
 
         leaving = []
         for j in range(1, inner):
@@ -224,8 +235,8 @@
             leaving.append(value.astype(BF16))
         arriving = [over_inner(leaving[j - 1], j) for j in range(1, inner)]
         last = leaving[0] if inner > 1 else last
-        for k in late:
-            last = advance(k, last)
+        if late:
+            last = advance(late, last)
         total = weight_grad(sequence, 0, last)
         gate_total, up_total = total[:, :width], total[:, width:]
         for part in arriving:

time: 144 us -> 160 us (1.11)
  matrix products: 15.9 us -> 26.3 us
  other arithmetic: 2.95 us -> 9.61 us
  waiting for transfers between devices: 80 us -> 75.3 us
  between operations: 1.34 us -> 5.26 us
  starting transfers between devices: 40.9 us -> 37.1 us
  local copies, waits for them, and re-layouts: 1.53 us -> 4.34 us
    ppermute x2, waiting for transfers between devices: 0.01 us -> 14.6 us  [over_inner(): return lax.ppermute(value, 'dp', pairs)]
    ppermute x8, waiting for transfers between devices: 45.1 us -> 37.3 us  [outer_pairs(): return lax.ppermute(value, 'dp', pairs)]
    ppermute x6, waiting for transfers between devices: 16.1 us -> 9.37 us  [over_outer(): return lax.ppermute(value, 'dp', pairs)]
    dot_general x4, matrix products: 2.75 us -> 8.43 us  [multiply(): return jnp.dot(x_chunks[k], weights, preferred_element_type=F32)]
    select_n x0 -> x3, other arithmetic: none -> 5.28 us  [tied(): value = jnp.where(first != first, first.astype(value.dtype), value)]
    ppermute x18 -> x16, waiting for transfers between devices: 18.8 us -> 13.9 us  [over_etp(): return lax.ppermute(value, 'etp', pairs)]
    dot_general x4, matrix products: 2.84 us -> 7.64 us  [advance(): lax.dot_general(after(grads[k], last), weights, (((1,), (1,)), ((), ())),...]
    slice x8 -> x11, local copies, waits for them, and re-layouts: 0.23 us -> 3.1 us  [the longest x3 2.88 us: tied(): first = other[(0,) * other.ndim]]
  transfers between devices with their start and end apart: 34 -> 32, of which waited for: 17 -> 17; matrix products, arithmetic and copies ran while one was open for 10% -> 19% of each run, Pallas kernels for 0% -> 0%
where the time goes in v10:
time: 160 us; the launch traced here: 159 us
  waiting for transfers between devices  75.3 us (47%)
  starting transfers between devices  37.1 us (23%)
  matrix products  26.3 us (16%)
  other arithmetic  9.61 us (6%)
  between operations  5.26 us (3%)
  local copies, waits for them, and re-layouts  4.34 us (3%)
    ppermute x8, waiting for transfers between devices, outer_pairs(): return lax.ppermute(value, 'dp', pairs)  37.3 us
    ppermute x8, starting transfers between devices, outer_pairs(): return lax.ppermute(value, 'dp', pairs)  14.7 us
    ppermute x2, waiting for transfers between devices, over_inner(): return lax.ppermute(value, 'dp', pairs)  14.6 us
    ppermute x16, waiting for transfers between devices, over_etp(): return lax.ppermute(value, 'etp', pairs)  13.9 us
    ppermute x16, starting transfers between devices, over_etp(): return lax.ppermute(value, 'etp', pairs)  10.4 us
    ppermute x6, waiting for transfers between devices, over_outer(): return lax.ppermute(value, 'dp', pairs)  9.37 us
    ppermute x6, starting transfers between devices, over_outer(): return lax.ppermute(value, 'dp', pairs)  9.06 us
    dot_general x4, matrix products, multiply(): return jnp.dot(x_chunks[k], weights, preferred_element_type=F32)  8.43 us
  transfers between devices with their start and end apart: 32, of which 17 were waited for; matrix products, arithmetic and copies ran while one was open for 19% of the time, Pallas kernels for 0%

profile of v10, /device:TPU:0, one launch (start us, length us, event | category | flops | bytes accessed | tf_op | source)
XLA Modules:
  0.0 159.5 jit_solution(2045637089351084291)
XLA Ops:
  0.7 3.6 %convolution_convert_fusion.1 = bf16[64,5120]{1,0:T(8,128)(2,1)S(1)} fusion(bf16[512,5120]{1,0:T(8,128)(2,1)} %param.7, s32[64]{0:T(128)} %param.8), kind=kOutput, calls=%fused_computation.1 | convolution fusion | flops 335904768 | bytes 5898496 | tf_op jit(solution)/shard_map/dot_general | solution.py:142
  4.5 3.1 %collective-permute-start = (bf16[64,1280]{1,0:T(8,128)(2,1)S(1)}, bf16[64,1280]{1,0:T(8,128)(2,1)S(1)}, u32[]{:S(2)}, u32[]{:S(2)}) collective-permute-start(bf16[64,1280]{1,0:T(8,128)(2,1)S(1)} %pad_maximum_fusion.11), channel_id=1, source_target_pairs={{0,8},{4,12},{8,0},{12,4},{16,24},{20,28},{24,16},{28,20},{1,9},{5... | collective-permute-start | bytes 491528 | tf_op jit(solution)/shard_map/ppermute | solution.py:76
  7.6 2.5 %collective-permute-start.1 = (bf16[64,1280]{1,0:T(8,128)(2,1)S(1)}, bf16[64,1280]{1,0:T(8,128)(2,1)S(1)}, u32[]{:S(2)}, u32[]{:S(2)}) collective-permute-start(bf16[64,1280]{1,0:T(8,128)(2,1)S(1)} %pad_maximum_fusion.12), channel_id=1, source_target_pairs={{0,24},{4,28},{8,16},{12,20},{16,8},{20,12},{24,0},{28,4},{1,25},{... | collective-permute-start | bytes 491528 | tf_op jit(solution)/shard_map/ppermute | solution.py:76
  10.3 1.6 collective-permute-start.4
  12.2 5.4 %collective-permute-done.1 = bf16[64,1280]{1,0:T(8,128)(2,1)S(1)} collective-permute-done((bf16[64,1280]{1,0:T(8,128)(2,1)S(1)}, bf16[64,1280]{1,0:T(8,128)(2,1)S(1)}, u32[]{:S(2)}, u32[]{:S(2)}) %collective-permute-start.1) | collective-permute-done | bytes 163872 | tf_op jit(solution)/shard_map/ppermute | solution.py:76
  17.6 1.6 collective-permute-start.2
  19.7 4.7 %collective-permute-done.2 = bf16[64,1280]{1,0:T(8,128)(2,1)S(1)} collective-permute-done((bf16[64,1280]{1,0:T(8,128)(2,1)S(1)}, bf16[64,1280]{1,0:T(8,128)(2,1)S(1)}, u32[]{:S(2)}, u32[]{:S(2)}) %collective-permute-start.2) | collective-permute-done | bytes 163872 | tf_op jit(solution)/shard_map/ppermute | solution.py:84
  24.5 8.8 %collective-permute-done.4 = bf16[640,768]{1,0:T(8,128)(2,1)} collective-permute-done((bf16[640,768]{1,0:T(8,128)(2,1)S(1)}, bf16[640,768]{1,0:T(8,128)(2,1)}, u32[]{:S(2)}, u32[]{:S(2)}) %collective-permute-start.4) | collective-permute-done | bytes 983072 | tf_op jit(solution)/shard_map/ppermute | solution.py:80
  38.3 2.6 %convolution_convert_fusion.3 = bf16[256,768]{1,0:T(8,128)(2,1)} fusion(bf16[256,1280]{1,0:T(8,128)(2,1)S(1)} %pad_maximum_fusion.5, bf16[640,768]{1,0:T(8,128)(2,1)} %collective-permute-done.4, bf16[640,768]{1,0:T(8,128)(2,1)S(1)} %constant_dynamic-update-slice_fusion), kind=kOutput, calls=%fused_computation.17 | convolution fusion | flops 507445248 | bytes 3014656 | tf_op jit(solution)/shard_map/dot_general | solution.py:159
  42.0 1.9 %convolution_convert_fusion.2 = bf16[256,768]{1,0:T(8,128)(2,1)S(1)} fusion(bf16[256,1280]{1,0:T(8,128)(2,1)S(1)} %pad_maximum_fusion.4, bf16[640,768]{1,0:T(8,128)(2,1)} %collective-permute-done.4, bf16[640,768]{1,0:T(8,128)(2,1)S(1)} %constant_dynamic-update-slice_fusion), kind=kOutput, calls=%fused_computation.16 | convolution fusion | flops 507445248 | bytes 3014656 | tf_op jit(solution)/shard_map/dot_general | solution.py:159
  50.2 5.4 %collective-permute-done.8 = bf16[256,768]{1,0:T(8,128)(2,1)S(1)} collective-permute-done((bf16[256,768]{1,0:T(8,128)(2,1)}, bf16[256,768]{1,0:T(8,128)(2,1)S(1)}, u32[]{:S(2)}, u32[]{:S(2)}) %collective-permute-start.8) | collective-permute-done | bytes 393248 | tf_op jit(solution)/shard_map/ppermute | solution.py:115
  59.9 2.3 %fusion.24 = bf16[128,1280]{1,0:T(8,128)(2,1)S(1)} fusion(bf16[64,1280]{1,0:T(8,128)(2,1)} %collective-permute-done.12, bf16[64,1280]{1,0:T(8,128)(2,1)S(1)} %collective-permute-done.11, pred[]{:T(512)S(6)} %ne.27, pred[]{:T(512)S(6)} %ne.26, bf16[]{:T(256)} %bitcast.2, bf16[]{:T(256)} %bitcast.1), kind=kLoop, calls=%fused_computation.66 | loop fusion | flops 983040 | bytes 655366 | tf_op jit(solution)/shard_map/jit(_where)/select_n | solution.py:28
  62.4 2.3 %fusion.23 = bf16[128,1280]{1,0:T(8,128)(2,1)S(1)} fusion(bf16[64,1280]{1,0:T(8,128)(2,1)} %collective-permute-done.9, bf16[64,640]{1,0:T(8,128)(2,1)S(1)} %get-tuple-element.68, bf16[64,640]{1,0:T(8,128)(2,1)S(1)} %get-tuple-element.69, pred[]{:T(512)S(6)} %ne.27, pred[]{:T(512)S(6)} %ne.26, bf16[]{:T(256)} %bitcast.2, bf16[]{:T(256)} %bitcast.1), kind=kLoop, calls=%fused_computation.64 | loop fusion | flops 1310720 | bytes 655366 | tf_op jit(solution)/shard_map/jit(_where)/select_n | solution.py:28
  65.3 1.9 %fusion.34 = f32[256,768]{1,0:T(8,128)S(1)} fusion(bf16[256,1280]{1,0:T(8,128)(2,1)S(1)} %pad_maximum_fusion.7, bf16[640,768]{1,0:T(8,128)(2,1)} %collective-permute-done.4, bf16[640,768]{1,0:T(8,128)(2,1)S(1)} %constant_dynamic-update-slice_fusion), kind=kOutput, calls=%fused_computation.107 | convolution fusion | flops 507248640 | bytes 3407872 | tf_op jit(solution)/shard_map/dot_general | solution.py:159
  69.7 4.5 %collective-permute-start.14 = (bf16[256,768]{1,0:T(8,128)(2,1)S(1)}, bf16[256,768]{1,0:T(8,128)(2,1)S(1)}, u32[]{:S(2)}, u32[]{:S(2)}) collective-permute-start(bf16[256,768]{1,0:T(8,128)(2,1)S(1)} %convert_element_type.88), channel_id=1, source_target_pairs={{0,16},{4,20},{24,8},{28,12},{1,17},{5,21},{25,9},{29,13},{2,18},{... | collective-permute-start | bytes 1179656 | tf_op jit(solution)/shard_map/ppermute | solution.py:115
  75.6 10.8 %collective-permute-done.14 = bf16[256,768]{1,0:T(8,128)(2,1)S(1)} collective-permute-done((bf16[256,768]{1,0:T(8,128)(2,1)S(1)}, bf16[256,768]{1,0:T(8,128)(2,1)S(1)}, u32[]{:S(2)}, u32[]{:S(2)}) %collective-permute-start.14) | collective-permute-done | bytes 393248 | tf_op jit(solution)/shard_map/ppermute | solution.py:115
  86.4 2.0 %fusion.9.pre_ref = f32[256,768]{1,0:T(8,128)S(1)} fusion(bf16[256,1280]{1,0:T(8,128)(2,1)S(1)} %pad_maximum_fusion.6, bf16[256,768]{1,0:T(8,128)(2,1)S(1)} %collective-permute-done.8, bf16[256,768]{1,0:T(8,128)(2,1)S(1)} %collective-permute-done.14, bf16[256,768]{1,0:T(8,128)(2,1)} %collective-permute-done.7, pred[]{:T(512)S(6)} %or.3, ...), kind=kOutput, calls=%fused_computation.15 | convolution fusion | flops 508624896 | bytes 4587521 | tf_op jit(solution)/shard_map/dot_general | solution.py:159
  90.9 1.9 %fusion.33 = f32[256,1280]{1,0:T(8,128)S(1)} fusion(bf16[256,768]{1,0:T(8,128)(2,1)S(1)} %get-tuple-element.38, bf16[640,768]{1,0:T(8,128)(2,1)} %collective-permute-done.4, bf16[640,768]{1,0:T(8,128)(2,1)S(1)} %constant_dynamic-update-slice_fusion), kind=kOutput, calls=%fused_computation.106 | convolution fusion | flops 507248640 | bytes 3670016 | tf_op jit(solution)/shard_map/dot_general | solution.py:194
  93.2 2.5 %collective-permute-start.20 = (bf16[256,768]{1,0:T(8,128)(2,1)S(1)}, bf16[256,768]{1,0:T(8,128)(2,1)S(1)}, u32[]{:S(2)}, u32[]{:S(2)}) collective-permute-start(bf16[256,768]{1,0:T(8,128)(2,1)S(1)} %get-tuple-element.38), channel_id=1, source_target_pairs={{0,16},{4,20},{16,24},{20,28},{24,8},{28,12},{8,0},{12,4},{1,17},{... | collective-permute-start | bytes 1179656 | tf_op jit(solution)/shard_map/ppermute | solution.py:115
  98.5 7.0 %collective-permute-done.20 = bf16[256,768]{1,0:T(8,128)(2,1)S(1)} collective-permute-done((bf16[256,768]{1,0:T(8,128)(2,1)S(1)}, bf16[256,768]{1,0:T(8,128)(2,1)S(1)}, u32[]{:S(2)}, u32[]{:S(2)}) %collective-permute-start.20) | collective-permute-done | bytes 393248 | tf_op jit(solution)/shard_map/ppermute | solution.py:115
  105.6 2.7 %collective-permute-start.23 = (bf16[256,768]{1,0:T(8,128)(2,1)S(1)}, bf16[256,768]{1,0:T(8,128)(2,1)S(1)}, u32[]{:S(2)}, u32[]{:S(2)}) collective-permute-start(bf16[256,768]{1,0:T(8,128)(2,1)S(1)} %broadcast_select_fusion.2), channel_id=1, source_target_pairs={{0,8},{4,12},{8,0},{12,4},{16,24},{20,28},{24,16},{28,20},{1,9},{5... | collective-permute-start | bytes 1179656 | tf_op jit(solution)/shard_map/ppermute | solution.py:115
  108.3 7.7 %collective-permute-done.21 = bf16[256,768]{1,0:T(8,128)(2,1)S(1)} collective-permute-done((bf16[256,768]{1,0:T(8,128)(2,1)S(1)}, bf16[256,768]{1,0:T(8,128)(2,1)S(1)}, u32[]{:S(2)}, u32[]{:S(2)}) %collective-permute-start.21) | collective-permute-done | bytes 393248 | tf_op jit(solution)/shard_map/ppermute | solution.py:115
  116.1 1.9 %fusion.32 = f32[256,1280]{1,0:T(8,128)S(1)} fusion(bf16[256,768]{1,0:T(8,128)(2,1)S(1)} %broadcast_select_fusion.1, bf16[640,768]{1,0:T(8,128)(2,1)} %collective-permute-done.4, bf16[640,768]{1,0:T(8,128)(2,1)S(1)} %constant_dynamic-update-slice_fusion), kind=kOutput, calls=%fused_computation.105 | convolution fusion | flops 507248640 | bytes 3670016 | tf_op jit(solution)/shard_map/dot_general | solution.py:194
  119.1 5.3 %collective-permute-done.23 = bf16[256,768]{1,0:T(8,128)(2,1)S(1)} collective-permute-done((bf16[256,768]{1,0:T(8,128)(2,1)S(1)}, bf16[256,768]{1,0:T(8,128)(2,1)S(1)}, u32[]{:S(2)}, u32[]{:S(2)}) %collective-permute-start.23) | collective-permute-done | bytes 393248 | tf_op jit(solution)/shard_map/ppermute | solution.py:115
  125.2 1.9 %fusion.30 = f32[256,1280]{1,0:T(8,128)S(1)} fusion(bf16[256,768]{1,0:T(8,128)(2,1)S(1)} %collective-permute-done.23, bf16[640,768]{1,0:T(8,128)(2,1)} %collective-permute-done.4, bf16[640,768]{1,0:T(8,128)(2,1)S(1)} %constant_dynamic-update-slice_fusion), kind=kOutput, calls=%fused_computation.103 | convolution fusion | flops 507248640 | bytes 3670016 | tf_op jit(solution)/shard_map/dot_general | solution.py:194
  127.1 1.9 %fusion.31 = f32[256,1280]{1,0:T(8,128)S(1)} fusion(bf16[256,768]{1,0:T(8,128)(2,1)S(1)} %broadcast_select_fusion, bf16[640,768]{1,0:T(8,128)(2,1)} %collective-permute-done.4, bf16[640,768]{1,0:T(8,128)(2,1)S(1)} %constant_dynamic-update-slice_fusion), kind=kOutput, calls=%fused_computation.104 | convolution fusion | flops 507248640 | bytes 3670016 | tf_op jit(solution)/shard_map/dot_general | solution.py:194
  133.0 1.6 collective-permute-start.25
  134.6 1.8 %collective-permute-done.28 = bf16[64,1280]{1,0:T(8,128)(2,1)S(1)} collective-permute-done((bf16[64,1280]{1,0:T(8,128)(2,1)S(1)}, bf16[64,1280]{1,0:T(8,128)(2,1)S(1)}, u32[]{:S(2)}, u32[]{:S(2)}) %collective-permute-start.28) | collective-permute-done | bytes 163872 | tf_op jit(solution)/shard_map/ppermute | solution.py:84
  137.2 5.8 %collective-permute-done.25 = bf16[128,1280]{1,0:T(8,128)(2,1)S(1)} collective-permute-done((bf16[128,1280]{1,0:T(8,128)(2,1)S(1)}, bf16[128,1280]{1,0:T(8,128)(2,1)S(1)}, u32[]{:S(2)}, u32[]{:S(2)}) %collective-permute-start.25) | collective-permute-done | bytes 327712 | tf_op jit(solution)/shard_map/ppermute | solution.py:84
  144.0 2.5 %collective-permute-done.29 = bf16[64,1280]{1,0:T(8,128)(2,1)S(1)} collective-permute-done((bf16[64,1280]{1,0:T(8,128)(2,1)S(1)}, bf16[64,1280]{1,0:T(8,128)(2,1)S(1)}, u32[]{:S(2)}, u32[]{:S(2)}) %collective-permute-start.29) | collective-permute-done | bytes 163872 | tf_op jit(solution)/shard_map/ppermute | solution.py:76
  148.0 5.8 %collective-permute-done.31 = bf16[640,768]{1,0:T(8,128)(2,1)S(1)} collective-permute-done((bf16[640,768]{1,0:T(8,128)(2,1)S(1)}, bf16[640,768]{1,0:T(8,128)(2,1)S(1)}, u32[]{:S(2)}, u32[]{:S(2)}) %collective-permute-start.31) | collective-permute-done | bytes 983072 | tf_op jit(solution)/shard_map/ppermute | solution.py:80
  155.5 4.0 %convolution_convert_fusion = bf16[512,5120]{1,0:T(8,128)(2,1)} fusion(bf16[64,5120]{1,0:T(8,128)(2,1)S(1)} %slice_dynamic-update-slice_fusion.2, s32[64]{0:T(128)S(1)} %copy-done.3), kind=kOutput, calls=%fused_computation | convolution fusion | flops 338198528 | bytes 5898496 | tf_op jit(solution)/shard_map/dot_general | solution.py:257
  (119 shorter events, 34.6 us)
Async XLA Ops:
  4.5 7.7 %collective-permute-start = (bf16[64,1280]{1,0:T(8,128)(2,1)S(1)}, bf16[64,1280]{1,0:T(8,128)(2,1)S(1)}, u32[]{:S(2)}, u32[]{:S(2)}) collective-permute-start(bf16[64,1280]{1,0:T(8,128)(2,1)S(1)} %pad_maximum_fusion.11), channel_id=1, source_target_pairs={{0,8},{4,12},{8,0},{12,4},{16,24},{20,28},{24,16},{28,20},{1,9},{5... | collective-permute-start | bytes 491528 | tf_op jit(solution)/shard_map/ppermute | solution.py:76
  7.6 10.0 %collective-permute-start.1 = (bf16[64,1280]{1,0:T(8,128)(2,1)S(1)}, bf16[64,1280]{1,0:T(8,128)(2,1)S(1)}, u32[]{:S(2)}, u32[]{:S(2)}) collective-permute-start(bf16[64,1280]{1,0:T(8,128)(2,1)S(1)} %pad_maximum_fusion.12), channel_id=1, source_target_pairs={{0,24},{4,28},{8,16},{12,20},{16,8},{20,12},{24,0},{28,4},{1,25},{... | collective-permute-start | bytes 491528 | tf_op jit(solution)/shard_map/ppermute | solution.py:76
  10.3 23.1 %collective-permute-start.4 = (bf16[640,768]{1,0:T(8,128)(2,1)S(1)}, bf16[640,768]{1,0:T(8,128)(2,1)}, u32[]{:S(2)}, u32[]{:S(2)}) collective-permute-start(bf16[640,768]{1,0:T(8,128)(2,1)S(1)} %constant_dynamic-update-slice_fusion), channel_id=1, source_target_pairs={{0,4},{4,0},{8,12},{12,8},{16,20},{20,16},{24,28},{28,24},{1,5},{5... | collective-permute-start | bytes 2949128 | tf_op jit(solution)/shard_map/ppermute | solution.py:80
  17.6 6.8 %collective-permute-start.2 = (bf16[64,1280]{1,0:T(8,128)(2,1)S(1)}, bf16[64,1280]{1,0:T(8,128)(2,1)S(1)}, u32[]{:S(2)}, u32[]{:S(2)}) collective-permute-start(bf16[64,1280]{1,0:T(8,128)(2,1)S(1)} %get-tuple-element.74), channel_id=1, source_target_pairs={{0,2},{1,3},{2,0},{3,1},{4,6},{5,7},{6,4},{7,5},{8,10},{9,11},{10,... | collective-permute-start | bytes 491528 | tf_op jit(solution)/shard_map/ppermute | solution.py:84
  19.2 16.7 %collective-permute-start.5 = (bf16[64,1280]{1,0:T(8,128)(2,1)S(1)}, bf16[64,1280]{1,0:T(8,128)(2,1)S(1)}, u32[]{:S(2)}, u32[]{:S(2)}) collective-permute-start(bf16[64,1280]{1,0:T(8,128)(2,1)S(1)} %get-tuple-element.75), channel_id=1, source_target_pairs={{0,2},{1,3},{2,0},{3,1},{4,6},{5,7},{6,4},{7,5},{8,10},{9,11},{10,... | collective-permute-start | bytes 491528 | tf_op jit(solution)/shard_map/ppermute | solution.py:84
  24.4 13.3 %collective-permute-start.3 = (bf16[128,1280]{1,0:T(8,128)(2,1)S(1)}, bf16[128,1280]{1,0:T(8,128)(2,1)S(1)}, u32[]{:S(2)}, u32[]{:S(2)}) collective-permute-start(bf16[128,1280]{1,0:T(8,128)(2,1)S(1)} %pad_maximum_fusion.9), channel_id=1, source_target_pairs={{0,1},{1,0},{2,3},{3,2},{4,5},{5,4},{6,7},{7,6},{8,9},{9,8},{10,11... | collective-permute-start | bytes 983048 | tf_op jit(solution)/shard_map/ppermute | solution.py:84
  36.6 1.7 %collective-permute-start.6 = (bf16[128,1280]{1,0:T(8,128)(2,1)S(1)}, bf16[128,1280]{1,0:T(8,128)(2,1)S(1)}, u32[]{:S(2)}, u32[]{:S(2)}) collective-permute-start(bf16[128,1280]{1,0:T(8,128)(2,1)S(1)} %maximum_select_fusion), channel_id=1, source_target_pairs={{0,1},{1,0},{2,3},{3,2},{4,5},{5,4},{6,7},{7,6},{8,9},{9,8},{10,11... | collective-permute-start | bytes 983048 | tf_op jit(solution)/shard_map/ppermute | solution.py:84
  37.3 11.3 %collective-permute-start.11 = (bf16[64,1280]{1,0:T(8,128)(2,1)}, bf16[64,1280]{1,0:T(8,128)(2,1)S(1)}, u32[]{:S(2)}, u32[]{:S(2)}) collective-permute-start(bf16[64,1280]{1,0:T(8,128)(2,1)} %pad_maximum_fusion.14), channel_id=1, source_target_pairs={{0,16},{4,20},{8,24},{12,28},{16,0},{20,4},{24,8},{28,12},{1,17},{... | collective-permute-start | bytes 491528 | tf_op jit(solution)/shard_map/ppermute | solution.py:76
  41.0 14.6 %collective-permute-start.8 = (bf16[256,768]{1,0:T(8,128)(2,1)}, bf16[256,768]{1,0:T(8,128)(2,1)S(1)}, u32[]{:S(2)}, u32[]{:S(2)}) collective-permute-start(bf16[256,768]{1,0:T(8,128)(2,1)} %convolution_convert_fusion.3), channel_id=1, source_target_pairs={{0,8},{4,12},{8,0},{12,4},{16,24},{20,28},{24,16},{28,20},{1,9},{5... | collective-permute-start | bytes 1179656 | tf_op jit(solution)/shard_map/ppermute | solution.py:115
  43.9 13.5 %collective-permute-start.7 = (bf16[256,768]{1,0:T(8,128)(2,1)S(1)}, bf16[256,768]{1,0:T(8,128)(2,1)}, u32[]{:S(2)}, u32[]{:S(2)}) collective-permute-start(bf16[256,768]{1,0:T(8,128)(2,1)S(1)} %convolution_convert_fusion.2), channel_id=1, source_target_pairs={{8,16},{12,20},{16,8},{20,12},{9,17},{13,21},{17,9},{21,13},{10,18... | collective-permute-start | bytes 1179656 | tf_op jit(solution)/shard_map/ppermute | solution.py:115
  46.0 16.4 %collective-permute-start.9 = (bf16[64,1280]{1,0:T(8,128)(2,1)}, bf16[64,1280]{1,0:T(8,128)(2,1)}, u32[]{:S(2)}, u32[]{:S(2)}) collective-permute-start(bf16[64,1280]{1,0:T(8,128)(2,1)} %pad_maximum_fusion.13), channel_id=1, source_target_pairs={{0,2},{1,3},{2,0},{3,1},{4,6},{5,7},{6,4},{7,5},{8,10},{9,11},{10,... | collective-permute-start | bytes 491528 | tf_op jit(solution)/shard_map/ppermute | solution.py:84
  48.7 11.3 %collective-permute-start.12 = (bf16[64,1280]{1,0:T(8,128)(2,1)S(1)}, bf16[64,1280]{1,0:T(8,128)(2,1)}, u32[]{:S(2)}, u32[]{:S(2)}) collective-permute-start(bf16[64,1280]{1,0:T(8,128)(2,1)S(1)} %collective-permute-done.11), channel_id=1, source_target_pairs={{0,2},{1,3},{2,0},{3,1},{4,6},{5,7},{6,4},{7,5},{8,10},{9,11},{10,... | collective-permute-start | bytes 491528 | tf_op jit(solution)/shard_map/ppermute | solution.py:84
  62.2 3.0 %collective-permute-start.13 = (bf16[128,1280]{1,0:T(8,128)(2,1)S(1)}, bf16[128,1280]{1,0:T(8,128)(2,1)S(1)}, u32[]{:S(2)}, u32[]{:S(2)}) collective-permute-start(bf16[128,1280]{1,0:T(8,128)(2,1)S(1)} %fusion.24), channel_id=1, source_target_pairs={{0,1},{1,0},{2,3},{3,2},{4,5},{5,4},{6,7},{7,6},{8,9},{9,8},{10,11... | collective-permute-start | bytes 983048 | tf_op jit(solution)/shard_map/ppermute | solution.py:84
  64.7 9.6 %collective-permute-start.10 = (bf16[128,1280]{1,0:T(8,128)(2,1)S(1)}, bf16[128,1280]{1,0:T(8,128)(2,1)S(1)}, u32[]{:S(2)}, u32[]{:S(2)}) collective-permute-start(bf16[128,1280]{1,0:T(8,128)(2,1)S(1)} %fusion.23), channel_id=1, source_target_pairs={{0,1},{1,0},{2,3},{3,2},{4,5},{5,4},{6,7},{7,6},{8,9},{9,8},{10,11... | collective-permute-start | bytes 983048 | tf_op jit(solution)/shard_map/ppermute | solution.py:84
  67.8 6.4 %collective-permute-start.15 = (bf16[64]{0:T(256)(128)(2,1)S(1)}, bf16[64]{0:T(256)(128)(2,1)S(1)}, u32[]{:S(2)}, u32[]{:S(2)}) collective-permute-start(bf16[64]{0:T(256)(128)(2,1)S(1)} %copy-done.4), channel_id=1, source_target_pairs={{0,2},{1,3},{2,0},{3,1},{4,6},{5,7},{6,4},{7,5},{8,10},{9,11},{10,... | collective-permute-start | bytes 392 | tf_op jit(solution)/shard_map/ppermute | solution.py:84
  69.4 20.1 %collective-permute-start.17 = (bf16[256,768]{1,0:T(8,128)(2,1)S(1)}, bf16[256,768]{1,0:T(8,128)(2,1)S(1)}, u32[]{:S(2)}, u32[]{:S(2)}) collective-permute-start(bf16[256,768]{1,0:T(8,128)(2,1)S(1)} %fusion.18), channel_id=1, source_target_pairs={{16,0},{20,4},{24,16},{28,20},{8,24},{12,28},{0,8},{4,12},{17,1},{... | collective-permute-start | bytes 1179656 | tf_op jit(solution)/shard_map/ppermute | solution.py:115
  69.7 16.8 %collective-permute-start.14 = (bf16[256,768]{1,0:T(8,128)(2,1)S(1)}, bf16[256,768]{1,0:T(8,128)(2,1)S(1)}, u32[]{:S(2)}, u32[]{:S(2)}) collective-permute-start(bf16[256,768]{1,0:T(8,128)(2,1)S(1)} %convert_element_type.88), channel_id=1, source_target_pairs={{0,16},{4,20},{24,8},{28,12},{1,17},{5,21},{25,9},{29,13},{2,18},{... | collective-permute-start | bytes 1179656 | tf_op jit(solution)/shard_map/ppermute | solution.py:115
  74.3 1.1 collective-permute-start.16
  92.9 4.9 %collective-permute-start.18 = (bf16[128,1280]{1,0:T(8,128)(2,1)S(1)}, bf16[128,1280]{1,0:T(8,128)(2,1)S(1)}, u32[]{:S(2)}, u32[]{:S(2)}) collective-permute-start(bf16[128,1280]{1,0:T(8,128)(2,1)S(1)} %slice.266), channel_id=1, source_target_pairs={{0,1},{1,0},{2,3},{3,2},{4,5},{5,4},{6,7},{7,6},{8,9},{9,8},{10,11... | collective-permute-start | bytes 983048 | tf_op jit(solution)/shard_map/ppermute | solution.py:84
  93.2 12.4 %collective-permute-start.20 = (bf16[256,768]{1,0:T(8,128)(2,1)S(1)}, bf16[256,768]{1,0:T(8,128)(2,1)S(1)}, u32[]{:S(2)}, u32[]{:S(2)}) collective-permute-start(bf16[256,768]{1,0:T(8,128)(2,1)S(1)} %get-tuple-element.38), channel_id=1, source_target_pairs={{0,16},{4,20},{16,24},{20,28},{24,8},{28,12},{8,0},{12,4},{1,17},{... | collective-permute-start | bytes 1179656 | tf_op jit(solution)/shard_map/ppermute | solution.py:115
  95.7 20.4 %collective-permute-start.21 = (bf16[256,768]{1,0:T(8,128)(2,1)S(1)}, bf16[256,768]{1,0:T(8,128)(2,1)S(1)}, u32[]{:S(2)}, u32[]{:S(2)}) collective-permute-start(bf16[256,768]{1,0:T(8,128)(2,1)S(1)} %get-tuple-element.38), channel_id=1, source_target_pairs={{16,0},{20,4},{8,24},{12,28},{17,1},{21,5},{9,25},{13,29},{18,2},{... | collective-permute-start | bytes 1179656 | tf_op jit(solution)/shard_map/ppermute | solution.py:115
  97.0 22.0 %collective-permute-start.22 = (bf16[256,768]{1,0:T(8,128)(2,1)S(1)}, bf16[256,768]{1,0:T(8,128)(2,1)S(1)}, u32[]{:S(2)}, u32[]{:S(2)}) collective-permute-start(bf16[256,768]{1,0:T(8,128)(2,1)S(1)} %get-tuple-element.38), channel_id=1, source_target_pairs={{8,16},{12,20},{16,8},{20,12},{9,17},{13,21},{17,9},{21,13},{10,18... | collective-permute-start | bytes 1179656 | tf_op jit(solution)/shard_map/ppermute | solution.py:115
  98.0 21.1 %collective-permute-start.19 = (bf16[64,1280]{1,0:T(8,128)(2,1)S(1)}, bf16[64,1280]{1,0:T(8,128)(2,1)S(1)}, u32[]{:S(2)}, u32[]{:S(2)}) collective-permute-start(bf16[64,1280]{1,0:T(8,128)(2,1)S(1)} %slice.270), channel_id=1, source_target_pairs={{0,2},{1,3},{2,0},{3,1},{4,6},{5,7},{6,4},{7,5},{8,10},{9,11},{10,... | collective-permute-start | bytes 491528 | tf_op jit(solution)/shard_map/ppermute | solution.py:84
  105.6 18.8 %collective-permute-start.23 = (bf16[256,768]{1,0:T(8,128)(2,1)S(1)}, bf16[256,768]{1,0:T(8,128)(2,1)S(1)}, u32[]{:S(2)}, u32[]{:S(2)}) collective-permute-start(bf16[256,768]{1,0:T(8,128)(2,1)S(1)} %broadcast_select_fusion.2), channel_id=1, source_target_pairs={{0,8},{4,12},{8,0},{12,4},{16,24},{20,28},{24,16},{28,20},{1,9},{5... | collective-permute-start | bytes 1179656 | tf_op jit(solution)/shard_map/ppermute | solution.py:115
  118.9 10.4 %collective-permute-start.27 = (bf16[128,1280]{1,0:T(8,128)(2,1)S(1)}, bf16[128,1280]{1,0:T(8,128)(2,1)S(1)}, u32[]{:S(2)}, u32[]{:S(2)}) collective-permute-start(bf16[128,1280]{1,0:T(8,128)(2,1)S(1)} %slice.263), channel_id=1, source_target_pairs={{0,1},{1,0},{2,3},{3,2},{4,5},{5,4},{6,7},{7,6},{8,9},{9,8},{10,11... | collective-permute-start | bytes 983048 | tf_op jit(solution)/shard_map/ppermute | solution.py:84
  129.2 3.6 %collective-permute-start.24 = (bf16[256,1280]{1,0:T(8,128)(2,1)S(1)}, bf16[256,1280]{1,0:T(8,128)(2,1)S(1)}, u32[]{:S(2)}, u32[]{:S(2)}) collective-permute-start(bf16[256,1280]{1,0:T(8,128)(2,1)S(1)} %pad_maximum_fusion.8), channel_id=1, source_target_pairs={{0,1},{1,0},{2,3},{3,2},{4,5},{5,4},{6,7},{7,6},{8,9},{9,8},{10,11... | collective-permute-start | bytes 1966088 | tf_op jit(solution)/shard_map/ppermute | solution.py:84
  129.4 7.1 %collective-permute-start.28 = (bf16[64,1280]{1,0:T(8,128)(2,1)S(1)}, bf16[64,1280]{1,0:T(8,128)(2,1)S(1)}, u32[]{:S(2)}, u32[]{:S(2)}) collective-permute-start(bf16[64,1280]{1,0:T(8,128)(2,1)S(1)} %slice.267), channel_id=1, source_target_pairs={{0,2},{1,3},{2,0},{3,1},{4,6},{5,7},{6,4},{7,5},{8,10},{9,11},{10,... | collective-permute-start | bytes 491528 | tf_op jit(solution)/shard_map/ppermute | solution.py:84
  129.9 23.9 %collective-permute-start.31 = (bf16[640,768]{1,0:T(8,128)(2,1)S(1)}, bf16[640,768]{1,0:T(8,128)(2,1)S(1)}, u32[]{:S(2)}, u32[]{:S(2)}) collective-permute-start(bf16[640,768]{1,0:T(8,128)(2,1)S(1)} %add_convert_fusion), channel_id=1, source_target_pairs={{0,4},{4,0},{8,12},{12,8},{16,20},{20,16},{24,28},{28,24},{1,5},{5... | collective-permute-start | bytes 2949128 | tf_op jit(solution)/shard_map/ppermute | solution.py:80
  133.0 10.0 %collective-permute-start.25 = (bf16[128,1280]{1,0:T(8,128)(2,1)S(1)}, bf16[128,1280]{1,0:T(8,128)(2,1)S(1)}, u32[]{:S(2)}, u32[]{:S(2)}) collective-permute-start(bf16[128,1280]{1,0:T(8,128)(2,1)S(1)} %pad_maximum_fusion.10), channel_id=1, source_target_pairs={{0,2},{1,3},{2,0},{3,1},{4,6},{5,7},{6,4},{7,5},{8,10},{9,11},{10,... | collective-permute-start | bytes 983048 | tf_op jit(solution)/shard_map/ppermute | solution.py:84
  136.5 10.0 %collective-permute-start.29 = (bf16[64,1280]{1,0:T(8,128)(2,1)S(1)}, bf16[64,1280]{1,0:T(8,128)(2,1)S(1)}, u32[]{:S(2)}, u32[]{:S(2)}) collective-permute-start(bf16[64,1280]{1,0:T(8,128)(2,1)S(1)} %fusion.19), channel_id=1, source_target_pairs={{0,16},{4,20},{8,24},{12,28},{16,0},{20,4},{24,8},{28,12},{1,17},{... | collective-permute-start | bytes 491528 | tf_op jit(solution)/shard_map/ppermute | solution.py:76
  143.2 12.1 %collective-permute-start.26 = (bf16[64,1280]{1,0:T(8,128)(2,1)S(1)}, bf16[64,1280]{1,0:T(8,128)(2,1)S(1)}, u32[]{:S(2)}, u32[]{:S(2)}) collective-permute-start(bf16[64,1280]{1,0:T(8,128)(2,1)S(1)} %broadcast_select_fusion.4), channel_id=1, source_target_pairs={{0,8},{4,12},{8,0},{12,4},{16,24},{20,28},{24,16},{28,20},{1,9},{5... | collective-permute-start | bytes 491528 | tf_op jit(solution)/shard_map/ppermute | solution.py:76
  146.4 9.0 %collective-permute-start.30 = (bf16[64,1280]{1,0:T(8,128)(2,1)S(1)}, bf16[64,1280]{1,0:T(8,128)(2,1)S(1)}, u32[]{:S(2)}, u32[]{:S(2)}) collective-permute-start(bf16[64,1280]{1,0:T(8,128)(2,1)S(1)} %get-tuple-element.52), channel_id=1, source_target_pairs={{0,24},{4,28},{8,16},{12,20},{16,8},{20,12},{24,0},{28,4},{1,25},{... | collective-permute-start | bytes 491528 | tf_op jit(solution)/shard_map/ppermute | solution.py:76
  (6 other events, 42.9 us)

commit v11 on v10

--- a/solution.py
+++ b/solution.py
@@ -20,13 +20,6 @@
 
 def after(value, *others):
     return lax.optimization_barrier((value,) + others)[0]
-
-
-def tied(value, *others):
-    for other in others:
-        first = other[(0,) * other.ndim]
-        value = jnp.where(first != first, first.astype(value.dtype), value)
-    return value
 
 
 def gate_kernel(steps, order_ref, pre_ref, prob_ref, cot_ref, *refs):
@@ -93,7 +86,7 @@
 
     def gather_etp(value, ties=()):
         for i, b in enumerate(bits):
-            value = tied(value, *ties[i]) if i < len(ties) else value
+            value = after(value, *ties[i]) if i < len(ties) else value
             value = jnp.concatenate([value, over_etp(value, b)], axis=0)
         return value
 
@@ -159,14 +152,14 @@
             return jnp.dot(x_chunks[k], weights, preferred_element_type=F32)
 
         if relay:
-            x_chunks[3] = gather_etp(got[3], [[], [weights[-1:]]])
+            x_chunks[3] = gather_etp(got[3])
             x_chunks[1] = gather_etp(got[1])
             far = multiply(3).astype(BF16)
             swapped = outer_pairs(far, swap)
             near = after(multiply(1, far).astype(BF16), far)
             crossed = outer_pairs(near, middle)
-            x_chunks[2] = gather_etp(got[2], [[], [swapped, crossed]])
-            x_chunks[0] = gather_etp(got[0], [[], [swapped, crossed]])
+            x_chunks[2] = gather_etp(got[2], [[], [near]])
+            x_chunks[0] = gather_etp(after(got[0], near))
             two = after(multiply(2, swapped, crossed), swapped)
             inwards = outer_pairs(two.astype(BF16), inward)
             relayed = pick(near, (after(two, swapped) + swapped.astype(F32)).astype(BF16))
@@ -183,7 +176,7 @@
                 last = multiply(k).astype(BF16)
                 parts.append(over_outer(last, k))
             own = multiply(0, last)
-        probs = gather_etp(after(gate_probs, last))
+        probs = gather_etp(after(gate_probs, rows))
         order = etp ^ jnp.array(chunk_order, jnp.int32)
         hidden, paired = gate_call(order, own, probs[:, None], d_hidden, parts)
 

time: 160 us -> 145 us (0.906)
  other arithmetic: 9.61 us -> 3.06 us
  between operations: 5.26 us -> 1.4 us
  local copies, waits for them, and re-layouts: 4.34 us -> 1.03 us
  starting transfers between devices: 37.1 us -> 35.1 us
    ppermute x8, waiting for transfers between devices: 37.3 us -> 46.1 us  [outer_pairs(): return lax.ppermute(value, 'dp', pairs)]
    ppermute x2, waiting for transfers between devices: 14.6 us -> 6.23 us  [over_inner(): return lax.ppermute(value, 'dp', pairs)]
    select_n x3 -> x0, other arithmetic: 5.28 us -> none  [tied(): value = jnp.where(first != first, first.astype(value.dtype), value)]
    ppermute x8, starting transfers between devices: 14.7 us -> 11.2 us  [outer_pairs(): return lax.ppermute(value, 'dp', pairs)]
    slice x3 -> x0, local copies, waits for them, and re-layouts: 2.88 us -> none  [tied(): first = other[(0,) * other.ndim]]
    ppermute x16, waiting for transfers between devices: 13.9 us -> 16.5 us  [over_etp(): return lax.ppermute(value, 'etp', pairs)]
    ppermute x6, starting transfers between devices: 9.06 us -> 10.9 us  [over_outer(): return lax.ppermute(value, 'dp', pairs)]
    ppermute x6, waiting for transfers between devices: 9.37 us -> 7.68 us  [over_outer(): return lax.ppermute(value, 'dp', pairs)]
  transfers between devices with their start and end apart: 32 -> 32, of which waited for: 17 -> 18; matrix products, arithmetic and copies ran while one was open for 19% -> 11% of each run, Pallas kernels for 0% -> 0%
where the time goes in v11:
time: 145 us; the launch traced here: 144 us
  waiting for transfers between devices  76.5 us (53%)
  starting transfers between devices  35.1 us (24%)
  matrix products  25.5 us (18%)
  other arithmetic  3.06 us (2%)
  Pallas kernels  1.51 us (1%)
    ppermute x8, waiting for transfers between devices, outer_pairs(): return lax.ppermute(value, 'dp', pairs)  46.1 us
    ppermute x16, waiting for transfers between devices, over_etp(): return lax.ppermute(value, 'etp', pairs)  16.5 us
    ppermute x8, starting transfers between devices, outer_pairs(): return lax.ppermute(value, 'dp', pairs)  11.2 us
    ppermute x6, starting transfers between devices, over_outer(): return lax.ppermute(value, 'dp', pairs)  10.9 us
    ppermute x16, starting transfers between devices, over_etp(): return lax.ppermute(value, 'etp', pairs)  9.97 us
    ppermute x6, waiting for transfers between devices, over_outer(): return lax.ppermute(value, 'dp', pairs)  7.68 us
    dot_general x4, matrix products, advance(): lax.dot_general(after(grads[k], last), weights, (((1,), (1,)), ((), ())),...  7.64 us
    dot_general x4, matrix products, multiply(): return jnp.dot(x_chunks[k], weights, preferred_element_type=F32)  7.56 us
  transfers between devices with their start and end apart: 32, of which 18 were waited for; matrix products, arithmetic and copies ran while one was open for 11% of the time, Pallas kernels for 0%

profile of v11, /device:TPU:0, one launch (start us, length us, event | category | flops | bytes accessed | tf_op | source)
XLA Modules:
  0.0 144.2 jit_solution(7035071440006326153)
XLA Ops:
  0.7 3.6 %convolution_convert_fusion.1 = bf16[64,5120]{1,0:T(8,128)(2,1)S(1)} fusion(bf16[512,5120]{1,0:T(8,128)(2,1)} %param.7, s32[64]{0:T(128)} %param.8), kind=kOutput, calls=%fused_computation.1 | convolution fusion | flops 335904768 | bytes 5898496 | tf_op jit(solution)/shard_map/dot_general | solution.py:135
  4.5 5.1 %collective-permute-start.1 = (bf16[64,1280]{1,0:T(8,128)(2,1)S(1)}, bf16[64,1280]{1,0:T(8,128)(2,1)S(1)}, u32[]{:S(2)}, u32[]{:S(2)}) collective-permute-start(bf16[64,1280]{1,0:T(8,128)(2,1)S(1)} %pad_maximum_fusion.16), channel_id=1, source_target_pairs={{0,24},{4,28},{8,16},{12,20},{16,8},{20,12},{24,0},{28,4},{1,25},{... | collective-permute-start | bytes 491528 | tf_op jit(solution)/shard_map/ppermute | solution.py:69
  13.8 2.0 %collective-permute-done.15 = bf16[64]{0:T(256)(128)(2,1)S(1)} collective-permute-done((bf16[64]{0:T(256)(128)(2,1)S(1)}, bf16[64]{0:T(256)(128)(2,1)S(1)}, u32[]{:S(2)}, u32[]{:S(2)}) %collective-permute-start.15) | collective-permute-done | bytes 160 | tf_op jit(solution)/shard_map/ppermute | solution.py:77
  15.9 2.5 %collective-permute-done = bf16[64,1280]{1,0:T(8,128)(2,1)S(1)} collective-permute-done((bf16[64,1280]{1,0:T(8,128)(2,1)S(1)}, bf16[64,1280]{1,0:T(8,128)(2,1)S(1)}, u32[]{:S(2)}, u32[]{:S(2)}) %collective-permute-start) | collective-permute-done | bytes 163872 | tf_op jit(solution)/shard_map/ppermute | solution.py:69
  20.8 2.7 %collective-permute-done.9 = bf16[64,1280]{1,0:T(8,128)(2,1)S(1)} collective-permute-done((bf16[64,1280]{1,0:T(8,128)(2,1)S(1)}, bf16[64,1280]{1,0:T(8,128)(2,1)S(1)}, u32[]{:S(2)}, u32[]{:S(2)}) %collective-permute-start.9) | collective-permute-done | bytes 163872 | tf_op jit(solution)/shard_map/ppermute | solution.py:69
  25.7 3.4 %collective-permute-done.2 = bf16[64,1280]{1,0:T(8,128)(2,1)S(1)} collective-permute-done((bf16[64,1280]{1,0:T(8,128)(2,1)S(1)}, bf16[64,1280]{1,0:T(8,128)(2,1)S(1)}, u32[]{:S(2)}, u32[]{:S(2)}) %collective-permute-start.2) | collective-permute-done | bytes 163872 | tf_op jit(solution)/shard_map/ppermute | solution.py:77
  29.2 2.6 %collective-permute-done.10 = bf16[64,1280]{1,0:T(8,128)(2,1)S(1)} collective-permute-done((bf16[64,1280]{1,0:T(8,128)(2,1)S(1)}, bf16[64,1280]{1,0:T(8,128)(2,1)S(1)}, u32[]{:S(2)}, u32[]{:S(2)}) %collective-permute-start.10) | collective-permute-done | bytes 163872 | tf_op jit(solution)/shard_map/ppermute | solution.py:77
  33.3 1.9 %convolution_convert_fusion.3 = bf16[256,768]{1,0:T(8,128)(2,1)S(1)} fusion(bf16[256,1280]{1,0:T(8,128)(2,1)S(1)} %pad_maximum_fusion.5, bf16[640,768]{1,0:T(8,128)(2,1)} %collective-permute-done.6, bf16[640,768]{1,0:T(8,128)(2,1)S(1)} %constant_dynamic-update-slice_fusion), kind=kOutput, calls=%fused_computation.17 | convolution fusion | flops 507445248 | bytes 3014656 | tf_op jit(solution)/shard_map/dot_general | solution.py:152
  35.1 1.9 %convolution_convert_fusion.2 = bf16[256,768]{1,0:T(8,128)(2,1)S(1)} fusion(bf16[256,1280]{1,0:T(8,128)(2,1)S(1)} %pad_maximum_fusion.4, bf16[640,768]{1,0:T(8,128)(2,1)} %collective-permute-done.6, bf16[640,768]{1,0:T(8,128)(2,1)S(1)} %constant_dynamic-update-slice_fusion), kind=kOutput, calls=%fused_computation.16 | convolution fusion | flops 507445248 | bytes 3014656 | tf_op jit(solution)/shard_map/dot_general | solution.py:152
  37.0 1.6 %collective-permute-start.7 = (bf16[64,1280]{1,0:T(8,128)(2,1)S(1)}, bf16[64,1280]{1,0:T(8,128)(2,1)S(1)}, u32[]{:S(2)}, u32[]{:S(2)}) collective-permute-start(bf16[64,1280]{1,0:T(8,128)(2,1)S(1)} %pad_maximum_fusion.14), channel_id=1, source_target_pairs={{0,2},{1,3},{2,0},{3,1},{4,6},{5,7},{6,4},{7,5},{8,10},{9,11},{10,... | collective-permute-start | bytes 491528 | tf_op jit(solution)/shard_map/ppermute | solution.py:77
  38.7 1.8 %collective-permute-start.12 = (bf16[256,768]{1,0:T(8,128)(2,1)S(1)}, bf16[256,768]{1,0:T(8,128)(2,1)S(1)}, u32[]{:S(2)}, u32[]{:S(2)}) collective-permute-start(bf16[256,768]{1,0:T(8,128)(2,1)S(1)} %convolution_convert_fusion.3), channel_id=1, source_target_pairs={{0,8},{4,12},{8,0},{12,4},{16,24},{20,28},{24,16},{28,20},{1,9},{5... | collective-permute-start | bytes 1179656 | tf_op jit(solution)/shard_map/ppermute | solution.py:108
  42.6 7.7 %collective-permute-done.12 = bf16[256,768]{1,0:T(8,128)(2,1)S(1)} collective-permute-done((bf16[256,768]{1,0:T(8,128)(2,1)S(1)}, bf16[256,768]{1,0:T(8,128)(2,1)S(1)}, u32[]{:S(2)}, u32[]{:S(2)}) %collective-permute-start.12) | collective-permute-done | bytes 393248 | tf_op jit(solution)/shard_map/ppermute | solution.py:108
  50.3 1.9 %fusion.32 = f32[256,768]{1,0:T(8,128)S(1)} fusion(bf16[256,1280]{1,0:T(8,128)(2,1)S(1)} %pad_maximum_fusion.7, bf16[640,768]{1,0:T(8,128)(2,1)} %collective-permute-done.6, bf16[640,768]{1,0:T(8,128)(2,1)S(1)} %constant_dynamic-update-slice_fusion), kind=kOutput, calls=%fused_computation.105 | convolution fusion | flops 507248640 | bytes 3407872 | tf_op jit(solution)/shard_map/dot_general | solution.py:152
  52.2 5.3 %collective-permute-start.14 = (bf16[256,768]{1,0:T(8,128)(2,1)S(1)}, bf16[256,768]{1,0:T(8,128)(2,1)S(1)}, u32[]{:S(2)}, u32[]{:S(2)}) collective-permute-start(bf16[256,768]{1,0:T(8,128)(2,1)S(1)} %convert_element_type.88), channel_id=1, source_target_pairs={{0,16},{4,20},{24,8},{28,12},{1,17},{5,21},{25,9},{29,13},{2,18},{... | collective-permute-start | bytes 1179656 | tf_op jit(solution)/shard_map/ppermute | solution.py:108
  57.8 9.3 %collective-permute-done.14 = bf16[256,768]{1,0:T(8,128)(2,1)S(1)} collective-permute-done((bf16[256,768]{1,0:T(8,128)(2,1)S(1)}, bf16[256,768]{1,0:T(8,128)(2,1)S(1)}, u32[]{:S(2)}, u32[]{:S(2)}) %collective-permute-start.14) | collective-permute-done | bytes 393248 | tf_op jit(solution)/shard_map/ppermute | solution.py:108
  67.0 1.9 %fusion.9.pre_ref = f32[256,768]{1,0:T(8,128)S(1)} fusion(bf16[256,1280]{1,0:T(8,128)(2,1)S(1)} %pad_maximum_fusion.6, bf16[256,768]{1,0:T(8,128)(2,1)S(1)} %collective-permute-done.12, bf16[256,768]{1,0:T(8,128)(2,1)S(1)} %collective-permute-done.14, bf16[256,768]{1,0:T(8,128)(2,1)S(1)} %collective-permute-done.13, pred[]{:T(512)S(6)} %or.3, ...), kind=kOutput, calls=%fused_computation.15 | convolution fusion | flops 508624896 | bytes 4587521 | tf_op jit(solution)/shard_map/dot_general | solution.py:152
  69.0 7.9 %collective-permute-done.17.refs_0_ = bf16[256,768]{1,0:T(8,128)(2,1)S(1)} collective-permute-done((bf16[256,768]{1,0:T(8,128)(2,1)S(1)}, bf16[256,768]{1,0:T(8,128)(2,1)S(1)}, u32[]{:S(2)}, u32[]{:S(2)}) %collective-permute-start.17) | collective-permute-done | bytes 393248 | tf_op jit(solution)/shard_map/ppermute | solution.py:108
  78.4 1.9 %fusion.31 = f32[256,1280]{1,0:T(8,128)S(1)} fusion(bf16[256,768]{1,0:T(8,128)(2,1)S(1)} %get-tuple-element.42, bf16[640,768]{1,0:T(8,128)(2,1)} %collective-permute-done.6, bf16[640,768]{1,0:T(8,128)(2,1)S(1)} %constant_dynamic-update-slice_fusion), kind=kOutput, calls=%fused_computation.104 | convolution fusion | flops 507248640 | bytes 3670016 | tf_op jit(solution)/shard_map/dot_general | solution.py:187
  84.2 8.2 %collective-permute-done.20 = bf16[256,768]{1,0:T(8,128)(2,1)S(1)} collective-permute-done((bf16[256,768]{1,0:T(8,128)(2,1)S(1)}, bf16[256,768]{1,0:T(8,128)(2,1)S(1)}, u32[]{:S(2)}, u32[]{:S(2)}) %collective-permute-start.20) | collective-permute-done | bytes 393248 | tf_op jit(solution)/shard_map/ppermute | solution.py:108
  93.0 7.7 %collective-permute-done.21 = bf16[256,768]{1,0:T(8,128)(2,1)S(1)} collective-permute-done((bf16[256,768]{1,0:T(8,128)(2,1)S(1)}, bf16[256,768]{1,0:T(8,128)(2,1)S(1)}, u32[]{:S(2)}, u32[]{:S(2)}) %collective-permute-start.21) | collective-permute-done | bytes 393248 | tf_op jit(solution)/shard_map/ppermute | solution.py:108
  100.8 1.9 %fusion.30 = f32[256,1280]{1,0:T(8,128)S(1)} fusion(bf16[256,768]{1,0:T(8,128)(2,1)S(1)} %broadcast_select_fusion.1, bf16[640,768]{1,0:T(8,128)(2,1)} %collective-permute-done.6, bf16[640,768]{1,0:T(8,128)(2,1)S(1)} %constant_dynamic-update-slice_fusion), kind=kOutput, calls=%fused_computation.103 | convolution fusion | flops 507248640 | bytes 3670016 | tf_op jit(solution)/shard_map/dot_general | solution.py:187
  103.8 5.3 %collective-permute-done.23 = bf16[256,768]{1,0:T(8,128)(2,1)S(1)} collective-permute-done((bf16[256,768]{1,0:T(8,128)(2,1)S(1)}, bf16[256,768]{1,0:T(8,128)(2,1)S(1)}, u32[]{:S(2)}, u32[]{:S(2)}) %collective-permute-start.23) | collective-permute-done | bytes 393248 | tf_op jit(solution)/shard_map/ppermute | solution.py:108
  109.9 1.9 %fusion.28 = f32[256,1280]{1,0:T(8,128)S(1)} fusion(bf16[256,768]{1,0:T(8,128)(2,1)S(1)} %collective-permute-done.23, bf16[640,768]{1,0:T(8,128)(2,1)} %collective-permute-done.6, bf16[640,768]{1,0:T(8,128)(2,1)S(1)} %constant_dynamic-update-slice_fusion), kind=kOutput, calls=%fused_computation.101 | convolution fusion | flops 507248640 | bytes 3670016 | tf_op jit(solution)/shard_map/dot_general | solution.py:187
  111.8 1.9 %fusion.29 = f32[256,1280]{1,0:T(8,128)S(1)} fusion(bf16[256,768]{1,0:T(8,128)(2,1)S(1)} %broadcast_select_fusion, bf16[640,768]{1,0:T(8,128)(2,1)} %collective-permute-done.6, bf16[640,768]{1,0:T(8,128)(2,1)S(1)} %constant_dynamic-update-slice_fusion), kind=kOutput, calls=%fused_computation.102 | convolution fusion | flops 507248640 | bytes 3670016 | tf_op jit(solution)/shard_map/dot_general | solution.py:187
  117.7 1.6 %collective-permute-start.25 = (bf16[128,1280]{1,0:T(8,128)(2,1)S(1)}, bf16[128,1280]{1,0:T(8,128)(2,1)S(1)}, u32[]{:S(2)}, u32[]{:S(2)}) collective-permute-start(bf16[128,1280]{1,0:T(8,128)(2,1)S(1)} %pad_maximum_fusion.13), channel_id=1, source_target_pairs={{0,2},{1,3},{2,0},{3,1},{4,6},{5,7},{6,4},{7,5},{8,10},{9,11},{10,... | collective-permute-start | bytes 983048 | tf_op jit(solution)/shard_map/ppermute | solution.py:77
  119.3 1.8 %collective-permute-done.28 = bf16[64,1280]{1,0:T(8,128)(2,1)S(1)} collective-permute-done((bf16[64,1280]{1,0:T(8,128)(2,1)S(1)}, bf16[64,1280]{1,0:T(8,128)(2,1)S(1)}, u32[]{:S(2)}, u32[]{:S(2)}) %collective-permute-start.28) | collective-permute-done | bytes 163872 | tf_op jit(solution)/shard_map/ppermute | solution.py:77
  121.1 1.7 %collective-permute-start.29 = (bf16[64,1280]{1,0:T(8,128)(2,1)S(1)}, bf16[64,1280]{1,0:T(8,128)(2,1)S(1)}, u32[]{:S(2)}, u32[]{:S(2)}) collective-permute-start(bf16[64,1280]{1,0:T(8,128)(2,1)S(1)} %fusion.19), channel_id=1, source_target_pairs={{0,16},{4,20},{8,24},{12,28},{16,0},{20,4},{24,8},{28,12},{1,17},{... | collective-permute-start | bytes 491528 | tf_op jit(solution)/shard_map/ppermute | solution.py:69
  122.8 4.9 %collective-permute-done.25 = bf16[128,1280]{1,0:T(8,128)(2,1)S(1)} collective-permute-done((bf16[128,1280]{1,0:T(8,128)(2,1)S(1)}, bf16[128,1280]{1,0:T(8,128)(2,1)S(1)}, u32[]{:S(2)}, u32[]{:S(2)}) %collective-permute-start.25) | collective-permute-done | bytes 327712 | tf_op jit(solution)/shard_map/ppermute | solution.py:77
  128.6 2.5 %collective-permute-done.29 = bf16[64,1280]{1,0:T(8,128)(2,1)S(1)} collective-permute-done((bf16[64,1280]{1,0:T(8,128)(2,1)S(1)}, bf16[64,1280]{1,0:T(8,128)(2,1)S(1)}, u32[]{:S(2)}, u32[]{:S(2)}) %collective-permute-start.29) | collective-permute-done | bytes 163872 | tf_op jit(solution)/shard_map/ppermute | solution.py:69
  131.1 2.4 %collective-permute-start.30 = (bf16[64,1280]{1,0:T(8,128)(2,1)S(1)}, bf16[64,1280]{1,0:T(8,128)(2,1)S(1)}, u32[]{:S(2)}, u32[]{:S(2)}) collective-permute-start(bf16[64,1280]{1,0:T(8,128)(2,1)S(1)} %get-tuple-element.56), channel_id=1, source_target_pairs={{0,24},{4,28},{8,16},{12,20},{16,8},{20,12},{24,0},{28,4},{1,25},{... | collective-permute-start | bytes 491528 | tf_op jit(solution)/shard_map/ppermute | solution.py:69
  133.6 4.9 %collective-permute-done.31 = bf16[640,768]{1,0:T(8,128)(2,1)S(1)} collective-permute-done((bf16[640,768]{1,0:T(8,128)(2,1)S(1)}, bf16[640,768]{1,0:T(8,128)(2,1)S(1)}, u32[]{:S(2)}, u32[]{:S(2)}) %collective-permute-start.31) | collective-permute-done | bytes 983072 | tf_op jit(solution)/shard_map/ppermute | solution.py:73
  140.2 4.0 %convolution_convert_fusion = bf16[512,5120]{1,0:T(8,128)(2,1)} fusion(bf16[64,5120]{1,0:T(8,128)(2,1)S(1)} %slice_dynamic-update-slice_fusion.2, s32[64]{0:T(128)S(1)} %copy-done.3), kind=kOutput, calls=%fused_computation | convolution fusion | flops 338198528 | bytes 5898496 | tf_op jit(solution)/shard_map/dot_general | solution.py:250
  (116 shorter events, 27.2 us)
Async XLA Ops:
  4.5 11.4 %collective-permute-start.1 = (bf16[64,1280]{1,0:T(8,128)(2,1)S(1)}, bf16[64,1280]{1,0:T(8,128)(2,1)S(1)}, u32[]{:S(2)}, u32[]{:S(2)}) collective-permute-start(bf16[64,1280]{1,0:T(8,128)(2,1)S(1)} %pad_maximum_fusion.16), channel_id=1, source_target_pairs={{0,24},{4,28},{8,16},{12,20},{16,8},{20,12},{24,0},{28,4},{1,25},{... | collective-permute-start | bytes 491528 | tf_op jit(solution)/shard_map/ppermute | solution.py:69
  9.6 8.8 %collective-permute-start = (bf16[64,1280]{1,0:T(8,128)(2,1)S(1)}, bf16[64,1280]{1,0:T(8,128)(2,1)S(1)}, u32[]{:S(2)}, u32[]{:S(2)}) collective-permute-start(bf16[64,1280]{1,0:T(8,128)(2,1)S(1)} %pad_maximum_fusion.15), channel_id=1, source_target_pairs={{0,8},{4,12},{8,0},{12,4},{16,24},{20,28},{24,16},{28,20},{1,9},{5... | collective-permute-start | bytes 491528 | tf_op jit(solution)/shard_map/ppermute | solution.py:69
  9.9 23.4 %collective-permute-start.6 = (bf16[640,768]{1,0:T(8,128)(2,1)S(1)}, bf16[640,768]{1,0:T(8,128)(2,1)}, u32[]{:S(2)}, u32[]{:S(2)}) collective-permute-start(bf16[640,768]{1,0:T(8,128)(2,1)S(1)} %constant_dynamic-update-slice_fusion), channel_id=1, source_target_pairs={{0,4},{4,0},{8,12},{12,8},{16,20},{20,16},{24,28},{28,24},{1,5},{5... | collective-permute-start | bytes 2949128 | tf_op jit(solution)/shard_map/ppermute | solution.py:73
  11.4 12.0 %collective-permute-start.9 = (bf16[64,1280]{1,0:T(8,128)(2,1)S(1)}, bf16[64,1280]{1,0:T(8,128)(2,1)S(1)}, u32[]{:S(2)}, u32[]{:S(2)}) collective-permute-start(bf16[64,1280]{1,0:T(8,128)(2,1)S(1)} %pad_maximum_fusion.17), channel_id=1, source_target_pairs={{0,16},{4,20},{8,24},{12,28},{16,0},{20,4},{24,8},{28,12},{1,17},{... | collective-permute-start | bytes 491528 | tf_op jit(solution)/shard_map/ppermute | solution.py:69
  12.3 3.5 %collective-permute-start.15 = (bf16[64]{0:T(256)(128)(2,1)S(1)}, bf16[64]{0:T(256)(128)(2,1)S(1)}, u32[]{:S(2)}, u32[]{:S(2)}) collective-permute-start(bf16[64]{0:T(256)(128)(2,1)S(1)} %copy-done.4), channel_id=1, source_target_pairs={{0,2},{1,3},{2,0},{3,1},{4,6},{5,7},{6,4},{7,5},{8,10},{9,11},{10,... | collective-permute-start | bytes 392 | tf_op jit(solution)/shard_map/ppermute | solution.py:77
  15.9 4.1 %collective-permute-start.16 = (bf16[128]{0:T(256)(128)(2,1)S(1)}, bf16[128]{0:T(256)(128)(2,1)S(1)}, u32[]{:S(2)}, u32[]{:S(2)}) collective-permute-start(bf16[128]{0:T(256)(128)(2,1)S(1)} %pad_maximum_fusion.18), channel_id=1, source_target_pairs={{0,1},{1,0},{2,3},{3,2},{4,5},{5,4},{6,7},{7,6},{8,9},{9,8},{10,11... | collective-permute-start | bytes 776 | tf_op jit(solution)/shard_map/ppermute | solution.py:77
  18.4 7.1 %collective-permute-start.4 = (bf16[64,1280]{1,0:T(8,128)(2,1)S(1)}, bf16[64,1280]{1,0:T(8,128)(2,1)S(1)}, u32[]{:S(2)}, u32[]{:S(2)}) collective-permute-start(bf16[64,1280]{1,0:T(8,128)(2,1)S(1)} %get-tuple-element.78), channel_id=1, source_target_pairs={{0,2},{1,3},{2,0},{3,1},{4,6},{5,7},{6,4},{7,5},{8,10},{9,11},{10,... | collective-permute-start | bytes 491528 | tf_op jit(solution)/shard_map/ppermute | solution.py:77
  20.1 8.9 %collective-permute-start.2 = (bf16[64,1280]{1,0:T(8,128)(2,1)S(1)}, bf16[64,1280]{1,0:T(8,128)(2,1)S(1)}, u32[]{:S(2)}, u32[]{:S(2)}) collective-permute-start(bf16[64,1280]{1,0:T(8,128)(2,1)S(1)} %get-tuple-element.79), channel_id=1, source_target_pairs={{0,2},{1,3},{2,0},{3,1},{4,6},{5,7},{6,4},{7,5},{8,10},{9,11},{10,... | collective-permute-start | bytes 491528 | tf_op jit(solution)/shard_map/ppermute | solution.py:77
  23.5 8.2 %collective-permute-start.10 = (bf16[64,1280]{1,0:T(8,128)(2,1)S(1)}, bf16[64,1280]{1,0:T(8,128)(2,1)S(1)}, u32[]{:S(2)}, u32[]{:S(2)}) collective-permute-start(bf16[64,1280]{1,0:T(8,128)(2,1)S(1)} %collective-permute-done.9), channel_id=1, source_target_pairs={{0,2},{1,3},{2,0},{3,1},{4,6},{5,7},{6,4},{7,5},{8,10},{9,11},{10,... | collective-permute-start | bytes 491528 | tf_op jit(solution)/shard_map/ppermute | solution.py:77
  25.6 6.2 %collective-permute-start.5 = (bf16[128,1280]{1,0:T(8,128)(2,1)S(1)}, bf16[128,1280]{1,0:T(8,128)(2,1)S(1)}, u32[]{:S(2)}, u32[]{:S(2)}) collective-permute-start(bf16[128,1280]{1,0:T(8,128)(2,1)S(1)} %pad_maximum_fusion.10), channel_id=1, source_target_pairs={{0,1},{1,0},{2,3},{3,2},{4,5},{5,4},{6,7},{7,6},{8,9},{9,8},{10,11... | collective-permute-start | bytes 983048 | tf_op jit(solution)/shard_map/ppermute | solution.py:77
  29.1 2.7 %collective-permute-start.3 = (bf16[128,1280]{1,0:T(8,128)(2,1)S(1)}, bf16[128,1280]{1,0:T(8,128)(2,1)S(1)}, u32[]{:S(2)}, u32[]{:S(2)}) collective-permute-start(bf16[128,1280]{1,0:T(8,128)(2,1)S(1)} %pad_maximum_fusion.9), channel_id=1, source_target_pairs={{0,1},{1,0},{2,3},{3,2},{4,5},{5,4},{6,7},{7,6},{8,9},{9,8},{10,11... | collective-permute-start | bytes 983048 | tf_op jit(solution)/shard_map/ppermute | solution.py:77
  37.0 5.4 %collective-permute-start.7 = (bf16[64,1280]{1,0:T(8,128)(2,1)S(1)}, bf16[64,1280]{1,0:T(8,128)(2,1)S(1)}, u32[]{:S(2)}, u32[]{:S(2)}) collective-permute-start(bf16[64,1280]{1,0:T(8,128)(2,1)S(1)} %pad_maximum_fusion.14), channel_id=1, source_target_pairs={{0,2},{1,3},{2,0},{3,1},{4,6},{5,7},{6,4},{7,5},{8,10},{9,11},{10,... | collective-permute-start | bytes 491528 | tf_op jit(solution)/shard_map/ppermute | solution.py:77
  38.6 3.9 %collective-permute-start.11 = (bf16[128,1280]{1,0:T(8,128)(2,1)S(1)}, bf16[128,1280]{1,0:T(8,128)(2,1)S(1)}, u32[]{:S(2)}, u32[]{:S(2)}) collective-permute-start(bf16[128,1280]{1,0:T(8,128)(2,1)S(1)} %pad_maximum_fusion.12), channel_id=1, source_target_pairs={{0,1},{1,0},{2,3},{3,2},{4,5},{5,4},{6,7},{7,6},{8,9},{9,8},{10,11... | collective-permute-start | bytes 983048 | tf_op jit(solution)/shard_map/ppermute | solution.py:77
  38.7 11.6 %collective-permute-start.12 = (bf16[256,768]{1,0:T(8,128)(2,1)S(1)}, bf16[256,768]{1,0:T(8,128)(2,1)S(1)}, u32[]{:S(2)}, u32[]{:S(2)}) collective-permute-start(bf16[256,768]{1,0:T(8,128)(2,1)S(1)} %convolution_convert_fusion.3), channel_id=1, source_target_pairs={{0,8},{4,12},{8,0},{12,4},{16,24},{20,28},{24,16},{28,20},{1,9},{5... | collective-permute-start | bytes 1179656 | tf_op jit(solution)/shard_map/ppermute | solution.py:108
  40.5 9.8 %collective-permute-start.13 = (bf16[256,768]{1,0:T(8,128)(2,1)S(1)}, bf16[256,768]{1,0:T(8,128)(2,1)S(1)}, u32[]{:S(2)}, u32[]{:S(2)}) collective-permute-start(bf16[256,768]{1,0:T(8,128)(2,1)S(1)} %convolution_convert_fusion.2), channel_id=1, source_target_pairs={{8,16},{12,20},{16,8},{20,12},{9,17},{13,21},{17,9},{21,13},{10,18... | collective-permute-start | bytes 1179656 | tf_op jit(solution)/shard_map/ppermute | solution.py:108
  42.4 15.3 %collective-permute-start.8 = (bf16[128,1280]{1,0:T(8,128)(2,1)S(1)}, bf16[128,1280]{1,0:T(8,128)(2,1)S(1)}, u32[]{:S(2)}, u32[]{:S(2)}) collective-permute-start(bf16[128,1280]{1,0:T(8,128)(2,1)S(1)} %pad_maximum_fusion.11), channel_id=1, source_target_pairs={{0,1},{1,0},{2,3},{3,2},{4,5},{5,4},{6,7},{7,6},{8,9},{9,8},{10,11... | collective-permute-start | bytes 983048 | tf_op jit(solution)/shard_map/ppermute | solution.py:77
  52.2 14.8 %collective-permute-start.14 = (bf16[256,768]{1,0:T(8,128)(2,1)S(1)}, bf16[256,768]{1,0:T(8,128)(2,1)S(1)}, u32[]{:S(2)}, u32[]{:S(2)}) collective-permute-start(bf16[256,768]{1,0:T(8,128)(2,1)S(1)} %convert_element_type.88), channel_id=1, source_target_pairs={{0,16},{4,20},{24,8},{28,12},{1,17},{5,21},{25,9},{29,13},{2,18},{... | collective-permute-start | bytes 1179656 | tf_op jit(solution)/shard_map/ppermute | solution.py:108
  57.6 19.3 %collective-permute-start.17 = (bf16[256,768]{1,0:T(8,128)(2,1)S(1)}, bf16[256,768]{1,0:T(8,128)(2,1)S(1)}, u32[]{:S(2)}, u32[]{:S(2)}) collective-permute-start(bf16[256,768]{1,0:T(8,128)(2,1)S(1)} %fusion.18), channel_id=1, source_target_pairs={{16,0},{20,4},{24,16},{28,20},{8,24},{12,28},{0,8},{4,12},{17,1},{... | collective-permute-start | bytes 1179656 | tf_op jit(solution)/shard_map/ppermute | solution.py:108
  80.4 3.1 %collective-permute-start.18 = (bf16[128,1280]{1,0:T(8,128)(2,1)S(1)}, bf16[128,1280]{1,0:T(8,128)(2,1)S(1)}, u32[]{:S(2)}, u32[]{:S(2)}) collective-permute-start(bf16[128,1280]{1,0:T(8,128)(2,1)S(1)} %slice.247), channel_id=1, source_target_pairs={{0,1},{1,0},{2,3},{3,2},{4,5},{5,4},{6,7},{7,6},{8,9},{9,8},{10,11... | collective-permute-start | bytes 983048 | tf_op jit(solution)/shard_map/ppermute | solution.py:77
  80.7 11.7 %collective-permute-start.20 = (bf16[256,768]{1,0:T(8,128)(2,1)S(1)}, bf16[256,768]{1,0:T(8,128)(2,1)S(1)}, u32[]{:S(2)}, u32[]{:S(2)}) collective-permute-start(bf16[256,768]{1,0:T(8,128)(2,1)S(1)} %get-tuple-element.42), channel_id=1, source_target_pairs={{0,16},{4,20},{16,24},{20,28},{24,8},{28,12},{8,0},{12,4},{1,17},{... | collective-permute-start | bytes 1179656 | tf_op jit(solution)/shard_map/ppermute | solution.py:108
  81.3 19.4 %collective-permute-start.21 = (bf16[256,768]{1,0:T(8,128)(2,1)S(1)}, bf16[256,768]{1,0:T(8,128)(2,1)S(1)}, u32[]{:S(2)}, u32[]{:S(2)}) collective-permute-start(bf16[256,768]{1,0:T(8,128)(2,1)S(1)} %get-tuple-element.42), channel_id=1, source_target_pairs={{16,0},{20,4},{8,24},{12,28},{17,1},{21,5},{9,25},{13,29},{18,2},{... | collective-permute-start | bytes 1179656 | tf_op jit(solution)/shard_map/ppermute | solution.py:108
  82.6 21.0 %collective-permute-start.22 = (bf16[256,768]{1,0:T(8,128)(2,1)S(1)}, bf16[256,768]{1,0:T(8,128)(2,1)S(1)}, u32[]{:S(2)}, u32[]{:S(2)}) collective-permute-start(bf16[256,768]{1,0:T(8,128)(2,1)S(1)} %get-tuple-element.42), channel_id=1, source_target_pairs={{8,16},{12,20},{16,8},{20,12},{9,17},{13,21},{17,9},{21,13},{10,18... | collective-permute-start | bytes 1179656 | tf_op jit(solution)/shard_map/ppermute | solution.py:108
  83.6 20.1 %collective-permute-start.19 = (bf16[64,1280]{1,0:T(8,128)(2,1)S(1)}, bf16[64,1280]{1,0:T(8,128)(2,1)S(1)}, u32[]{:S(2)}, u32[]{:S(2)}) collective-permute-start(bf16[64,1280]{1,0:T(8,128)(2,1)S(1)} %slice.251), channel_id=1, source_target_pairs={{0,2},{1,3},{2,0},{3,1},{4,6},{5,7},{6,4},{7,5},{8,10},{9,11},{10,... | collective-permute-start | bytes 491528 | tf_op jit(solution)/shard_map/ppermute | solution.py:77
  92.4 16.7 %collective-permute-start.23 = (bf16[256,768]{1,0:T(8,128)(2,1)S(1)}, bf16[256,768]{1,0:T(8,128)(2,1)S(1)}, u32[]{:S(2)}, u32[]{:S(2)}) collective-permute-start(bf16[256,768]{1,0:T(8,128)(2,1)S(1)} %broadcast_select_fusion.2), channel_id=1, source_target_pairs={{0,8},{4,12},{8,0},{12,4},{16,24},{20,28},{24,16},{28,20},{1,9},{5... | collective-permute-start | bytes 1179656 | tf_op jit(solution)/shard_map/ppermute | solution.py:108
  103.6 10.4 %collective-permute-start.27 = (bf16[128,1280]{1,0:T(8,128)(2,1)S(1)}, bf16[128,1280]{1,0:T(8,128)(2,1)S(1)}, u32[]{:S(2)}, u32[]{:S(2)}) collective-permute-start(bf16[128,1280]{1,0:T(8,128)(2,1)S(1)} %slice.244), channel_id=1, source_target_pairs={{0,1},{1,0},{2,3},{3,2},{4,5},{5,4},{6,7},{7,6},{8,9},{9,8},{10,11... | collective-permute-start | bytes 983048 | tf_op jit(solution)/shard_map/ppermute | solution.py:77
  113.9 3.6 %collective-permute-start.24 = (bf16[256,1280]{1,0:T(8,128)(2,1)S(1)}, bf16[256,1280]{1,0:T(8,128)(2,1)S(1)}, u32[]{:S(2)}, u32[]{:S(2)}) collective-permute-start(bf16[256,1280]{1,0:T(8,128)(2,1)S(1)} %pad_maximum_fusion.8), channel_id=1, source_target_pairs={{0,1},{1,0},{2,3},{3,2},{4,5},{5,4},{6,7},{7,6},{8,9},{9,8},{10,11... | collective-permute-start | bytes 1966088 | tf_op jit(solution)/shard_map/ppermute | solution.py:77
  114.0 7.1 %collective-permute-start.28 = (bf16[64,1280]{1,0:T(8,128)(2,1)S(1)}, bf16[64,1280]{1,0:T(8,128)(2,1)S(1)}, u32[]{:S(2)}, u32[]{:S(2)}) collective-permute-start(bf16[64,1280]{1,0:T(8,128)(2,1)S(1)} %slice.248), channel_id=1, source_target_pairs={{0,2},{1,3},{2,0},{3,1},{4,6},{5,7},{6,4},{7,5},{8,10},{9,11},{10,... | collective-permute-start | bytes 491528 | tf_op jit(solution)/shard_map/ppermute | solution.py:77
  114.6 23.9 %collective-permute-start.31 = (bf16[640,768]{1,0:T(8,128)(2,1)S(1)}, bf16[640,768]{1,0:T(8,128)(2,1)S(1)}, u32[]{:S(2)}, u32[]{:S(2)}) collective-permute-start(bf16[640,768]{1,0:T(8,128)(2,1)S(1)} %add_convert_fusion), channel_id=1, source_target_pairs={{0,4},{4,0},{8,12},{12,8},{16,20},{20,16},{24,28},{28,24},{1,5},{5... | collective-permute-start | bytes 2949128 | tf_op jit(solution)/shard_map/ppermute | solution.py:73
  117.7 10.0 %collective-permute-start.25 = (bf16[128,1280]{1,0:T(8,128)(2,1)S(1)}, bf16[128,1280]{1,0:T(8,128)(2,1)S(1)}, u32[]{:S(2)}, u32[]{:S(2)}) collective-permute-start(bf16[128,1280]{1,0:T(8,128)(2,1)S(1)} %pad_maximum_fusion.13), channel_id=1, source_target_pairs={{0,2},{1,3},{2,0},{3,1},{4,6},{5,7},{6,4},{7,5},{8,10},{9,11},{10,... | collective-permute-start | bytes 983048 | tf_op jit(solution)/shard_map/ppermute | solution.py:77
  121.1 10.0 %collective-permute-start.29 = (bf16[64,1280]{1,0:T(8,128)(2,1)S(1)}, bf16[64,1280]{1,0:T(8,128)(2,1)S(1)}, u32[]{:S(2)}, u32[]{:S(2)}) collective-permute-start(bf16[64,1280]{1,0:T(8,128)(2,1)S(1)} %fusion.19), channel_id=1, source_target_pairs={{0,16},{4,20},{8,24},{12,28},{16,0},{20,4},{24,8},{28,12},{1,17},{... | collective-permute-start | bytes 491528 | tf_op jit(solution)/shard_map/ppermute | solution.py:69
  127.8 12.1 %collective-permute-start.26 = (bf16[64,1280]{1,0:T(8,128)(2,1)S(1)}, bf16[64,1280]{1,0:T(8,128)(2,1)S(1)}, u32[]{:S(2)}, u32[]{:S(2)}) collective-permute-start(bf16[64,1280]{1,0:T(8,128)(2,1)S(1)} %broadcast_select_fusion.4), channel_id=1, source_target_pairs={{0,8},{4,12},{8,0},{12,4},{16,24},{20,28},{24,16},{28,20},{1,9},{5... | collective-permute-start | bytes 491528 | tf_op jit(solution)/shard_map/ppermute | solution.py:69
  131.1 9.0 %collective-permute-start.30 = (bf16[64,1280]{1,0:T(8,128)(2,1)S(1)}, bf16[64,1280]{1,0:T(8,128)(2,1)S(1)}, u32[]{:S(2)}, u32[]{:S(2)}) collective-permute-start(bf16[64,1280]{1,0:T(8,128)(2,1)S(1)} %get-tuple-element.56), channel_id=1, source_target_pairs={{0,24},{4,28},{8,16},{12,20},{16,8},{20,12},{24,0},{28,4},{1,25},{... | collective-permute-start | bytes 491528 | tf_op jit(solution)/shard_map/ppermute | solution.py:69
  (6 other events, 60.0 us)

commit v12 on v11

--- a/solution.py
+++ b/solution.py
@@ -129,7 +129,7 @@
 
         weights = [jnp.concatenate([w_gate, w_up], axis=1)]
         weights += [over_inner(weights[0], j) for j in range(1, inner)]
-        weights = jnp.concatenate(weights, axis=0)
+        weights = lax.optimization_barrier(jnp.concatenate(weights, axis=0))
 
         onehot = (slots[:, None] == jnp.arange(tok, dtype=slots.dtype)[None, :]).astype(BF16)
         rows = jnp.dot(onehot, tokens, preferred_element_type=F32).astype(BF16)
@@ -159,8 +159,8 @@
             near = after(multiply(1, far).astype(BF16), far)
             crossed = outer_pairs(near, middle)
             x_chunks[2] = gather_etp(got[2], [[], [near]])
-            x_chunks[0] = gather_etp(after(got[0], near))
-            two = after(multiply(2, swapped, crossed), swapped)
+            two = lax.optimization_barrier(multiply(2, near))
+            x_chunks[0] = gather_etp(after(got[0], two))
             inwards = outer_pairs(two.astype(BF16), inward)
             relayed = pick(near, (after(two, swapped) + swapped.astype(F32)).astype(BF16))
             cycled = outer_pairs(relayed, back)

time: 145 us -> 153 us (1.055)
  waiting for transfers between devices: 76.5 us -> 99.9 us
  starting transfers between devices: 35.1 us -> 26 us
  matrix products: 25.5 us -> 17.4 us
  other arithmetic: 3.06 us -> 4.95 us
    ppermute x2, waiting for transfers between devices: 6.23 us -> 16.7 us  [over_inner(): return lax.ppermute(value, 'dp', pairs)]
    ppermute x16, waiting for transfers between devices: 16.5 us -> 22.4 us  [over_etp(): return lax.ppermute(value, 'etp', pairs)]
    dot_general x4, matrix products: 7.64 us -> 2.84 us  [advance(): lax.dot_general(after(grads[k], last), weights, (((1,), (1,)), ((), ())),...]
    ppermute x6, starting transfers between devices: 10.9 us -> 6.56 us  [over_outer(): return lax.ppermute(value, 'dp', pairs)]
    ppermute x6, waiting for transfers between devices: 7.68 us -> 12 us  [over_outer(): return lax.ppermute(value, 'dp', pairs)]
    ppermute x8, starting transfers between devices: 11.2 us -> 7.89 us  [outer_pairs(): return lax.ppermute(value, 'dp', pairs)]
    dot_general x4, matrix products: 7.56 us -> 4.25 us  [multiply(): return jnp.dot(x_chunks[k], weights, preferred_element_type=F32)]
    ppermute x8, waiting for transfers between devices: 46.1 us -> 48.9 us  [outer_pairs(): return lax.ppermute(value, 'dp', pairs)]
  transfers between devices with their start and end apart: 32 -> 32, of which waited for: 18 -> 17; matrix products, arithmetic and copies ran while one was open for 11% -> 10% of each run, Pallas kernels for 0% -> 0%
where the time goes in v12:
time: 153 us
  waiting for transfers between devices  99.9 us (65%)
  starting transfers between devices  26 us (17%)
  matrix products  17.4 us (11%)
  other arithmetic  4.95 us (3%)
  local copies, waits for them, and re-layouts  1.74 us (1%)
    ppermute x8, waiting for transfers between devices, outer_pairs(): return lax.ppermute(value, 'dp', pairs)  48.9 us
    ppermute x16, waiting for transfers between devices, over_etp(): return lax.ppermute(value, 'etp', pairs)  22.4 us
    ppermute x2, waiting for transfers between devices, over_inner(): return lax.ppermute(value, 'dp', pairs)  16.7 us
    ppermute x6, waiting for transfers between devices, over_outer(): return lax.ppermute(value, 'dp', pairs)  12 us
    ppermute x16, starting transfers between devices, over_etp(): return lax.ppermute(value, 'etp', pairs)  8.48 us
    ppermute x8, starting transfers between devices, outer_pairs(): return lax.ppermute(value, 'dp', pairs)  7.89 us
    ppermute x6, starting transfers between devices, over_outer(): return lax.ppermute(value, 'dp', pairs)  6.56 us
    dot_general x4, matrix products, multiply(): return jnp.dot(x_chunks[k], weights, preferred_element_type=F32)  4.25 us
  transfers between devices with their start and end apart: 32, of which 17 were waited for; matrix products, arithmetic and copies ran while one was open for 10% of the time, Pallas kernels for 0%

profile of v12, /device:TPU:0, one launch (start us, length us, event | category | flops | bytes accessed | tf_op | source)
XLA Modules:
  0.0 152.8 jit_solution(6128017625203293056)
XLA Ops:
  0.7 3.6 %convolution_convert_fusion.1 = bf16[64,5120]{1,0:T(8,128)(2,1)S(1)} fusion(bf16[512,5120]{1,0:T(8,128)(2,1)} %param.7, s32[64]{0:T(128)} %param.8), kind=kOutput, calls=%fused_computation.1 | convolution fusion | flops 335904768 | bytes 5898496 | tf_op jit(solution)/shard_map/dot_general | solution.py:135
  5.1 5.1 %collective-permute-start.3 = (bf16[64,1280]{1,0:T(8,128)(2,1)S(1)}, bf16[64,1280]{1,0:T(8,128)(2,1)S(1)}, u32[]{:S(2)}, u32[]{:S(2)}) collective-permute-start(bf16[64,1280]{1,0:T(8,128)(2,1)S(1)} %pad_maximum_fusion.17), channel_id=1, source_target_pairs={{0,24},{4,28},{8,16},{12,20},{16,8},{20,12},{24,0},{28,4},{1,25},{... | collective-permute-start | bytes 491528 | tf_op jit(solution)/shard_map/ppermute | solution.py:69
  11.0 4.3 %collective-permute-done.3 = bf16[64,1280]{1,0:T(8,128)(2,1)S(1)} collective-permute-done((bf16[64,1280]{1,0:T(8,128)(2,1)S(1)}, bf16[64,1280]{1,0:T(8,128)(2,1)S(1)}, u32[]{:S(2)}, u32[]{:S(2)}) %collective-permute-start.3) | collective-permute-done | bytes 163872 | tf_op jit(solution)/shard_map/ppermute | solution.py:69
  15.3 3.7 %collective-permute-done.2 = bf16[64,1280]{1,0:T(8,128)(2,1)S(1)} collective-permute-done((bf16[64,1280]{1,0:T(8,128)(2,1)S(1)}, bf16[64,1280]{1,0:T(8,128)(2,1)S(1)}, u32[]{:S(2)}, u32[]{:S(2)}) %collective-permute-start.2) | collective-permute-done | bytes 163872 | tf_op jit(solution)/shard_map/ppermute | solution.py:69
  19.0 1.5 collective-permute-start.6
  20.7 1.6 %collective-permute-start.8 = (bf16[640,768]{1,0:T(8,128)(2,1)S(1)}, bf16[640,768]{1,0:T(8,128)(2,1)S(1)}, u32[]{:S(2)}, u32[]{:S(2)}) collective-permute-start(bf16[640,768]{1,0:T(8,128)(2,1)S(1)} %constant_dynamic-update-slice_fusion), channel_id=1, source_target_pairs={{0,4},{4,0},{8,12},{12,8},{16,20},{20,16},{24,28},{28,24},{1,5},{5... | collective-permute-start | bytes 2949128 | tf_op jit(solution)/shard_map/ppermute | solution.py:73
  22.8 1.3 collective-permute-done
  24.1 1.5 collective-permute-start.1
  26.2 6.6 %collective-permute-done.4 = bf16[64,1280]{1,0:T(8,128)(2,1)S(1)} collective-permute-done((bf16[64,1280]{1,0:T(8,128)(2,1)S(1)}, bf16[64,1280]{1,0:T(8,128)(2,1)S(1)}, u32[]{:S(2)}, u32[]{:S(2)}) %collective-permute-start.4) | collective-permute-done | bytes 163872 | tf_op jit(solution)/shard_map/ppermute | solution.py:77
  34.6 9.4 %collective-permute-done.8 = bf16[640,768]{1,0:T(8,128)(2,1)S(1)} collective-permute-done((bf16[640,768]{1,0:T(8,128)(2,1)S(1)}, bf16[640,768]{1,0:T(8,128)(2,1)S(1)}, u32[]{:S(2)}, u32[]{:S(2)}) %collective-permute-start.8) | collective-permute-done | bytes 983072 | tf_op jit(solution)/shard_map/ppermute | solution.py:73
  44.2 1.4 convolution_convert_fusion.3
  45.6 1.4 convolution_convert_fusion.2
  47.6 1.3 collective-permute-done.9
  49.0 1.1 pad_maximum_fusion.6
  51.9 5.3 %collective-permute-done.10 = bf16[64,1280]{1,0:T(8,128)(2,1)S(1)} collective-permute-done((bf16[64,1280]{1,0:T(8,128)(2,1)S(1)}, bf16[64,1280]{1,0:T(8,128)(2,1)S(1)}, u32[]{:S(2)}, u32[]{:S(2)}) %collective-permute-start.10) | collective-permute-done | bytes 163872 | tf_op jit(solution)/shard_map/ppermute | solution.py:77
  58.1 4.5 %collective-permute-start.14 = (bf16[256,768]{1,0:T(8,128)(2,1)S(1)}, bf16[256,768]{1,0:T(8,128)(2,1)S(1)}, u32[]{:S(2)}, u32[]{:S(2)}) collective-permute-start(bf16[256,768]{1,0:T(8,128)(2,1)S(1)} %convert_element_type.88), channel_id=1, source_target_pairs={{0,16},{4,20},{24,8},{28,12},{1,17},{5,21},{25,9},{29,13},{2,18},{... | collective-permute-start | bytes 1179656 | tf_op jit(solution)/shard_map/ppermute | solution.py:108
  63.3 8.8 %collective-permute-done.14 = bf16[256,768]{1,0:T(8,128)(2,1)S(1)} collective-permute-done((bf16[256,768]{1,0:T(8,128)(2,1)S(1)}, bf16[256,768]{1,0:T(8,128)(2,1)S(1)}, u32[]{:S(2)}, u32[]{:S(2)}) %collective-permute-start.14) | collective-permute-done | bytes 393248 | tf_op jit(solution)/shard_map/ppermute | solution.py:108
  72.8 14.1 %collective-permute-done.17.refs_0_ = bf16[256,768]{1,0:T(8,128)(2,1)S(1)} collective-permute-done((bf16[256,768]{1,0:T(8,128)(2,1)S(1)}, bf16[256,768]{1,0:T(8,128)(2,1)S(1)}, u32[]{:S(2)}, u32[]{:S(2)}) %collective-permute-start.17) | collective-permute-done | bytes 393248 | tf_op jit(solution)/shard_map/ppermute | solution.py:108
  86.9 1.5 shard_map.102
  89.4 1.3 collective-permute-start.21
  90.7 0.9 collective-permute-start.22
  92.4 16.9 %collective-permute-done.20 = bf16[256,768]{1,0:T(8,128)(2,1)S(1)} collective-permute-done((bf16[256,768]{1,0:T(8,128)(2,1)S(1)}, bf16[256,768]{1,0:T(8,128)(2,1)S(1)}, u32[]{:S(2)}, u32[]{:S(2)}) %collective-permute-start.20) | collective-permute-done | bytes 393248 | tf_op jit(solution)/shard_map/ppermute | solution.py:108
  111.2 8.9 %collective-permute-done.23 = bf16[256,768]{1,0:T(8,128)(2,1)S(1)} collective-permute-done((bf16[256,768]{1,0:T(8,128)(2,1)S(1)}, bf16[256,768]{1,0:T(8,128)(2,1)S(1)}, u32[]{:S(2)}, u32[]{:S(2)}) %collective-permute-start.23) | collective-permute-done | bytes 393248 | tf_op jit(solution)/shard_map/ppermute | solution.py:108
  123.3 1.5 collective-permute-start.31
  124.9 1.2 fusion
  126.4 1.6 %collective-permute-start.25 = (bf16[128,1280]{1,0:T(8,128)(2,1)S(1)}, bf16[128,1280]{1,0:T(8,128)(2,1)S(1)}, u32[]{:S(2)}, u32[]{:S(2)}) collective-permute-start(bf16[128,1280]{1,0:T(8,128)(2,1)S(1)} %pad_maximum_fusion.13), channel_id=1, source_target_pairs={{0,2},{1,3},{2,0},{3,1},{4,6},{5,7},{6,4},{7,5},{8,10},{9,11},{10,... | collective-permute-start | bytes 983048 | tf_op jit(solution)/shard_map/ppermute | solution.py:77
  127.9 1.8 %collective-permute-done.28 = bf16[64,1280]{1,0:T(8,128)(2,1)S(1)} collective-permute-done((bf16[64,1280]{1,0:T(8,128)(2,1)S(1)}, bf16[64,1280]{1,0:T(8,128)(2,1)S(1)}, u32[]{:S(2)}, u32[]{:S(2)}) %collective-permute-start.28) | collective-permute-done | bytes 163872 | tf_op jit(solution)/shard_map/ppermute | solution.py:77
  129.9 6.5 %collective-permute-done.25 = bf16[128,1280]{1,0:T(8,128)(2,1)S(1)} collective-permute-done((bf16[128,1280]{1,0:T(8,128)(2,1)S(1)}, bf16[128,1280]{1,0:T(8,128)(2,1)S(1)}, u32[]{:S(2)}, u32[]{:S(2)}) %collective-permute-start.25) | collective-permute-done | bytes 327712 | tf_op jit(solution)/shard_map/ppermute | solution.py:77
  136.9 2.6 %collective-permute-done.29 = bf16[64,1280]{1,0:T(8,128)(2,1)S(1)} collective-permute-done((bf16[64,1280]{1,0:T(8,128)(2,1)S(1)}, bf16[64,1280]{1,0:T(8,128)(2,1)S(1)}, u32[]{:S(2)}, u32[]{:S(2)}) %collective-permute-start.29) | collective-permute-done | bytes 163872 | tf_op jit(solution)/shard_map/ppermute | solution.py:69
  139.9 7.3 %collective-permute-done.31 = bf16[640,768]{1,0:T(8,128)(2,1)S(1)} collective-permute-done((bf16[640,768]{1,0:T(8,128)(2,1)S(1)}, bf16[640,768]{1,0:T(8,128)(2,1)S(1)}, u32[]{:S(2)}, u32[]{:S(2)}) %collective-permute-start.31) | collective-permute-done | bytes 983072 | tf_op jit(solution)/shard_map/ppermute | solution.py:73
  147.2 1.5 slice_add_fusion
  148.8 4.0 %convolution_convert_fusion = bf16[512,5120]{1,0:T(8,128)(2,1)} fusion(bf16[64,5120]{1,0:T(8,128)(2,1)S(1)} %slice_dynamic-update-slice_fusion.2, s32[64]{0:T(128)S(1)} %copy-done.5), kind=kOutput, calls=%fused_computation | convolution fusion | flops 338198528 | bytes 5898496 | tf_op jit(solution)/shard_map/dot_general | solution.py:250
  (123 shorter events, 17.3 us)
Async XLA Ops:
  5.1 10.2 %collective-permute-start.3 = (bf16[64,1280]{1,0:T(8,128)(2,1)S(1)}, bf16[64,1280]{1,0:T(8,128)(2,1)S(1)}, u32[]{:S(2)}, u32[]{:S(2)}) collective-permute-start(bf16[64,1280]{1,0:T(8,128)(2,1)S(1)} %pad_maximum_fusion.17), channel_id=1, source_target_pairs={{0,24},{4,28},{8,16},{12,20},{16,8},{20,12},{24,0},{28,4},{1,25},{... | collective-permute-start | bytes 491528 | tf_op jit(solution)/shard_map/ppermute | solution.py:69
  10.2 8.8 %collective-permute-start.2 = (bf16[64,1280]{1,0:T(8,128)(2,1)S(1)}, bf16[64,1280]{1,0:T(8,128)(2,1)S(1)}, u32[]{:S(2)}, u32[]{:S(2)}) collective-permute-start(bf16[64,1280]{1,0:T(8,128)(2,1)S(1)} %pad_maximum_fusion.16), channel_id=1, source_target_pairs={{0,8},{4,12},{8,0},{12,4},{16,24},{20,28},{24,16},{28,20},{1,9},{5... | collective-permute-start | bytes 491528 | tf_op jit(solution)/shard_map/ppermute | solution.py:69
  10.3 13.8 %collective-permute-start = (bf16[64,1280]{1,0:T(8,128)(2,1)S(1)}, bf16[64,1280]{1,0:T(8,128)(2,1)S(1)}, u32[]{:S(2)}, u32[]{:S(2)}) collective-permute-start(bf16[64,1280]{1,0:T(8,128)(2,1)S(1)} %pad_maximum_fusion.15), channel_id=1, source_target_pairs={{0,16},{4,20},{8,24},{12,28},{16,0},{20,4},{24,8},{28,12},{1,17},{... | collective-permute-start | bytes 491528 | tf_op jit(solution)/shard_map/ppermute | solution.py:69
  19.0 7.1 %collective-permute-start.6 = (bf16[64,1280]{1,0:T(8,128)(2,1)S(1)}, bf16[64,1280]{1,0:T(8,128)(2,1)S(1)}, u32[]{:S(2)}, u32[]{:S(2)}) collective-permute-start(bf16[64,1280]{1,0:T(8,128)(2,1)S(1)} %get-tuple-element.76), channel_id=1, source_target_pairs={{0,2},{1,3},{2,0},{3,1},{4,6},{5,7},{6,4},{7,5},{8,10},{9,11},{10,... | collective-permute-start | bytes 491528 | tf_op jit(solution)/shard_map/ppermute | solution.py:77
  20.7 23.3 %collective-permute-start.8 = (bf16[640,768]{1,0:T(8,128)(2,1)S(1)}, bf16[640,768]{1,0:T(8,128)(2,1)S(1)}, u32[]{:S(2)}, u32[]{:S(2)}) collective-permute-start(bf16[640,768]{1,0:T(8,128)(2,1)S(1)} %constant_dynamic-update-slice_fusion), channel_id=1, source_target_pairs={{0,4},{4,0},{8,12},{12,8},{16,20},{20,16},{24,28},{28,24},{1,5},{5... | collective-permute-start | bytes 2949128 | tf_op jit(solution)/shard_map/ppermute | solution.py:73
  22.3 24.8 %collective-permute-start.15 = (bf16[64]{0:T(256)(128)(2,1)S(1)}, bf16[64]{0:T(256)(128)(2,1)S(1)}, u32[]{:S(2)}, u32[]{:S(2)}) collective-permute-start(bf16[64]{0:T(256)(128)(2,1)S(1)} %copy-done.6), channel_id=1, source_target_pairs={{0,2},{1,3},{2,0},{3,1},{4,6},{5,7},{6,4},{7,5},{8,10},{9,11},{10,... | collective-permute-start | bytes 392 | tf_op jit(solution)/shard_map/ppermute | solution.py:77
  24.1 8.9 %collective-permute-start.1 = (bf16[64,1280]{1,0:T(8,128)(2,1)S(1)}, bf16[64,1280]{1,0:T(8,128)(2,1)S(1)}, u32[]{:S(2)}, u32[]{:S(2)}) collective-permute-start(bf16[64,1280]{1,0:T(8,128)(2,1)S(1)} %collective-permute-done), channel_id=1, source_target_pairs={{0,2},{1,3},{2,0},{3,1},{4,6},{5,7},{6,4},{7,5},{8,10},{9,11},{10,... | collective-permute-start | bytes 491528 | tf_op jit(solution)/shard_map/ppermute | solution.py:77
  25.6 7.2 %collective-permute-start.4 = (bf16[64,1280]{1,0:T(8,128)(2,1)S(1)}, bf16[64,1280]{1,0:T(8,128)(2,1)S(1)}, u32[]{:S(2)}, u32[]{:S(2)}) collective-permute-start(bf16[64,1280]{1,0:T(8,128)(2,1)S(1)} %get-tuple-element.77), channel_id=1, source_target_pairs={{0,2},{1,3},{2,0},{3,1},{4,6},{5,7},{6,4},{7,5},{8,10},{9,11},{10,... | collective-permute-start | bytes 491528 | tf_op jit(solution)/shard_map/ppermute | solution.py:77
  26.2 7.5 %collective-permute-start.7 = (bf16[128,1280]{1,0:T(8,128)(2,1)S(1)}, bf16[128,1280]{1,0:T(8,128)(2,1)S(1)}, u32[]{:S(2)}, u32[]{:S(2)}) collective-permute-start(bf16[128,1280]{1,0:T(8,128)(2,1)S(1)} %pad_maximum_fusion.11), channel_id=1, source_target_pairs={{0,1},{1,0},{2,3},{3,2},{4,5},{5,4},{6,7},{7,6},{8,9},{9,8},{10,11... | collective-permute-start | bytes 983048 | tf_op jit(solution)/shard_map/ppermute | solution.py:77
  32.9 1.7 %collective-permute-start.5 = (bf16[128,1280]{1,0:T(8,128)(2,1)S(1)}, bf16[128,1280]{1,0:T(8,128)(2,1)S(1)}, u32[]{:S(2)}, u32[]{:S(2)}) collective-permute-start(bf16[128,1280]{1,0:T(8,128)(2,1)S(1)} %pad_maximum_fusion.10), channel_id=1, source_target_pairs={{0,1},{1,0},{2,3},{3,2},{4,5},{5,4},{6,7},{7,6},{8,9},{9,8},{10,11... | collective-permute-start | bytes 983048 | tf_op jit(solution)/shard_map/ppermute | solution.py:77
  47.0 2.0 %collective-permute-start.9 = (bf16[128,1280]{1,0:T(8,128)(2,1)}, bf16[128,1280]{1,0:T(8,128)(2,1)}, u32[]{:S(2)}, u32[]{:S(2)}) collective-permute-start(bf16[128,1280]{1,0:T(8,128)(2,1)} %pad_maximum_fusion.9), channel_id=1, source_target_pairs={{0,1},{1,0},{2,3},{3,2},{4,5},{5,4},{6,7},{7,6},{8,9},{9,8},{10,11... | collective-permute-start | bytes 983048 | tf_op jit(solution)/shard_map/ppermute | solution.py:77
  47.1 4.5 %collective-permute-start.16 = (bf16[128]{0:T(256)(128)(2,1)S(1)}, bf16[128]{0:T(256)(128)(2,1)S(1)}, u32[]{:S(2)}, u32[]{:S(2)}) collective-permute-start(bf16[128]{0:T(256)(128)(2,1)S(1)} %pad_maximum_fusion.18), channel_id=1, source_target_pairs={{0,1},{1,0},{2,3},{3,2},{4,5},{5,4},{6,7},{7,6},{8,9},{9,8},{10,11... | collective-permute-start | bytes 776 | tf_op jit(solution)/shard_map/ppermute | solution.py:77
  50.8 6.3 %collective-permute-start.10 = (bf16[64,1280]{1,0:T(8,128)(2,1)S(1)}, bf16[64,1280]{1,0:T(8,128)(2,1)S(1)}, u32[]{:S(2)}, u32[]{:S(2)}) collective-permute-start(bf16[64,1280]{1,0:T(8,128)(2,1)S(1)} %pad_maximum_fusion.14), channel_id=1, source_target_pairs={{0,2},{1,3},{2,0},{3,1},{4,6},{5,7},{6,4},{7,5},{8,10},{9,11},{10,... | collective-permute-start | bytes 491528 | tf_op jit(solution)/shard_map/ppermute | solution.py:77
  51.8 10.9 %collective-permute-start.12 = (bf16[256,768]{1,0:T(8,128)(2,1)S(1)}, bf16[256,768]{1,0:T(8,128)(2,1)S(1)}, u32[]{:S(2)}, u32[]{:S(2)}) collective-permute-start(bf16[256,768]{1,0:T(8,128)(2,1)S(1)} %copy-done.7), channel_id=1, source_target_pairs={{0,8},{4,12},{8,0},{12,4},{16,24},{20,28},{24,16},{28,20},{1,9},{5... | collective-permute-start | bytes 1179656 | tf_op jit(solution)/shard_map/ppermute | solution.py:108
  57.2 6.1 %collective-permute-start.11 = (bf16[128,1280]{1,0:T(8,128)(2,1)S(1)}, bf16[128,1280]{1,0:T(8,128)(2,1)S(1)}, u32[]{:S(2)}, u32[]{:S(2)}) collective-permute-start(bf16[128,1280]{1,0:T(8,128)(2,1)S(1)} %pad_maximum_fusion.12), channel_id=1, source_target_pairs={{0,1},{1,0},{2,3},{3,2},{4,5},{5,4},{6,7},{7,6},{8,9},{9,8},{10,11... | collective-permute-start | bytes 983048 | tf_op jit(solution)/shard_map/ppermute | solution.py:77
  57.3 6.0 %collective-permute-start.13 = (bf16[256,768]{1,0:T(8,128)(2,1)S(1)}, bf16[256,768]{1,0:T(8,128)(2,1)S(1)}, u32[]{:S(2)}, u32[]{:S(2)}) collective-permute-start(bf16[256,768]{1,0:T(8,128)(2,1)S(1)} %copy-done.3), channel_id=1, source_target_pairs={{8,16},{12,20},{16,8},{20,12},{9,17},{13,21},{17,9},{21,13},{10,18... | collective-permute-start | bytes 1179656 | tf_op jit(solution)/shard_map/ppermute | solution.py:108
  58.1 14.0 %collective-permute-start.14 = (bf16[256,768]{1,0:T(8,128)(2,1)S(1)}, bf16[256,768]{1,0:T(8,128)(2,1)S(1)}, u32[]{:S(2)}, u32[]{:S(2)}) collective-permute-start(bf16[256,768]{1,0:T(8,128)(2,1)S(1)} %convert_element_type.88), channel_id=1, source_target_pairs={{0,16},{4,20},{24,8},{28,12},{1,17},{5,21},{25,9},{29,13},{2,18},{... | collective-permute-start | bytes 1179656 | tf_op jit(solution)/shard_map/ppermute | solution.py:108
  62.9 24.0 %collective-permute-start.17 = (bf16[256,768]{1,0:T(8,128)(2,1)S(1)}, bf16[256,768]{1,0:T(8,128)(2,1)S(1)}, u32[]{:S(2)}, u32[]{:S(2)}) collective-permute-start(bf16[256,768]{1,0:T(8,128)(2,1)S(1)} %fusion.18), channel_id=1, source_target_pairs={{16,0},{20,4},{24,16},{28,20},{8,24},{12,28},{0,8},{4,12},{17,1},{... | collective-permute-start | bytes 1179656 | tf_op jit(solution)/shard_map/ppermute | solution.py:108
  89.2 2.6 %collective-permute-start.18 = (bf16[128,1280]{1,0:T(8,128)(2,1)S(1)}, bf16[128,1280]{1,0:T(8,128)(2,1)S(1)}, u32[]{:S(2)}, u32[]{:S(2)}) collective-permute-start(bf16[128,1280]{1,0:T(8,128)(2,1)S(1)} %slice.247), channel_id=1, source_target_pairs={{0,1},{1,0},{2,3},{3,2},{4,5},{5,4},{6,7},{7,6},{8,9},{9,8},{10,11... | collective-permute-start | bytes 983048 | tf_op jit(solution)/shard_map/ppermute | solution.py:77
  89.3 20.0 %collective-permute-start.20 = (bf16[256,768]{1,0:T(8,128)(2,1)S(1)}, bf16[256,768]{1,0:T(8,128)(2,1)S(1)}, u32[]{:S(2)}, u32[]{:S(2)}) collective-permute-start(bf16[256,768]{1,0:T(8,128)(2,1)S(1)} %get-tuple-element.40), channel_id=1, source_target_pairs={{0,16},{4,20},{16,24},{20,28},{24,8},{28,12},{8,0},{12,4},{1,17},{... | collective-permute-start | bytes 1179656 | tf_op jit(solution)/shard_map/ppermute | solution.py:108
  89.4 20.1 %collective-permute-start.21 = (bf16[256,768]{1,0:T(8,128)(2,1)S(1)}, bf16[256,768]{1,0:T(8,128)(2,1)S(1)}, u32[]{:S(2)}, u32[]{:S(2)}) collective-permute-start(bf16[256,768]{1,0:T(8,128)(2,1)S(1)} %get-tuple-element.40), channel_id=1, source_target_pairs={{16,0},{20,4},{8,24},{12,28},{17,1},{21,5},{9,25},{13,29},{18,2},{... | collective-permute-start | bytes 1179656 | tf_op jit(solution)/shard_map/ppermute | solution.py:108
  90.7 20.4 %collective-permute-start.22 = (bf16[256,768]{1,0:T(8,128)(2,1)S(1)}, bf16[256,768]{1,0:T(8,128)(2,1)S(1)}, u32[]{:S(2)}, u32[]{:S(2)}) collective-permute-start(bf16[256,768]{1,0:T(8,128)(2,1)S(1)} %get-tuple-element.40), channel_id=1, source_target_pairs={{8,16},{12,20},{16,8},{20,12},{9,17},{13,21},{17,9},{21,13},{10,18... | collective-permute-start | bytes 1179656 | tf_op jit(solution)/shard_map/ppermute | solution.py:108
  91.9 19.3 %collective-permute-start.19 = (bf16[64,1280]{1,0:T(8,128)(2,1)S(1)}, bf16[64,1280]{1,0:T(8,128)(2,1)S(1)}, u32[]{:S(2)}, u32[]{:S(2)}) collective-permute-start(bf16[64,1280]{1,0:T(8,128)(2,1)S(1)} %slice.251), channel_id=1, source_target_pairs={{0,2},{1,3},{2,0},{3,1},{4,6},{5,7},{6,4},{7,5},{8,10},{9,11},{10,... | collective-permute-start | bytes 491528 | tf_op jit(solution)/shard_map/ppermute | solution.py:77
  109.4 10.8 %collective-permute-start.23 = (bf16[256,768]{1,0:T(8,128)(2,1)S(1)}, bf16[256,768]{1,0:T(8,128)(2,1)S(1)}, u32[]{:S(2)}, u32[]{:S(2)}) collective-permute-start(bf16[256,768]{1,0:T(8,128)(2,1)S(1)} %broadcast_select_fusion.2), channel_id=1, source_target_pairs={{0,8},{4,12},{8,0},{12,4},{16,24},{20,28},{24,16},{28,20},{1,9},{5... | collective-permute-start | bytes 1179656 | tf_op jit(solution)/shard_map/ppermute | solution.py:108
  111.0 11.6 %collective-permute-start.27 = (bf16[128,1280]{1,0:T(8,128)(2,1)S(1)}, bf16[128,1280]{1,0:T(8,128)(2,1)S(1)}, u32[]{:S(2)}, u32[]{:S(2)}) collective-permute-start(bf16[128,1280]{1,0:T(8,128)(2,1)S(1)} %slice.244), channel_id=1, source_target_pairs={{0,1},{1,0},{2,3},{3,2},{4,5},{5,4},{6,7},{7,6},{8,9},{9,8},{10,11... | collective-permute-start | bytes 983048 | tf_op jit(solution)/shard_map/ppermute | solution.py:77
  122.5 3.6 %collective-permute-start.24 = (bf16[256,1280]{1,0:T(8,128)(2,1)S(1)}, bf16[256,1280]{1,0:T(8,128)(2,1)S(1)}, u32[]{:S(2)}, u32[]{:S(2)}) collective-permute-start(bf16[256,1280]{1,0:T(8,128)(2,1)S(1)} %pad_maximum_fusion.8), channel_id=1, source_target_pairs={{0,1},{1,0},{2,3},{3,2},{4,5},{5,4},{6,7},{7,6},{8,9},{9,8},{10,11... | collective-permute-start | bytes 1966088 | tf_op jit(solution)/shard_map/ppermute | solution.py:77
  122.7 7.1 %collective-permute-start.28 = (bf16[64,1280]{1,0:T(8,128)(2,1)S(1)}, bf16[64,1280]{1,0:T(8,128)(2,1)S(1)}, u32[]{:S(2)}, u32[]{:S(2)}) collective-permute-start(bf16[64,1280]{1,0:T(8,128)(2,1)S(1)} %slice.248), channel_id=1, source_target_pairs={{0,2},{1,3},{2,0},{3,1},{4,6},{5,7},{6,4},{7,5},{8,10},{9,11},{10,... | collective-permute-start | bytes 491528 | tf_op jit(solution)/shard_map/ppermute | solution.py:77
  123.3 23.9 %collective-permute-start.31 = (bf16[640,768]{1,0:T(8,128)(2,1)S(1)}, bf16[640,768]{1,0:T(8,128)(2,1)S(1)}, u32[]{:S(2)}, u32[]{:S(2)}) collective-permute-start(bf16[640,768]{1,0:T(8,128)(2,1)S(1)} %add_convert_fusion), channel_id=1, source_target_pairs={{0,4},{4,0},{8,12},{12,8},{16,20},{20,16},{24,28},{28,24},{1,5},{5... | collective-permute-start | bytes 2949128 | tf_op jit(solution)/shard_map/ppermute | solution.py:73
  126.4 10.0 %collective-permute-start.25 = (bf16[128,1280]{1,0:T(8,128)(2,1)S(1)}, bf16[128,1280]{1,0:T(8,128)(2,1)S(1)}, u32[]{:S(2)}, u32[]{:S(2)}) collective-permute-start(bf16[128,1280]{1,0:T(8,128)(2,1)S(1)} %pad_maximum_fusion.13), channel_id=1, source_target_pairs={{0,2},{1,3},{2,0},{3,1},{4,6},{5,7},{6,4},{7,5},{8,10},{9,11},{10,... | collective-permute-start | bytes 983048 | tf_op jit(solution)/shard_map/ppermute | solution.py:77
  129.8 9.7 %collective-permute-start.29 = (bf16[64,1280]{1,0:T(8,128)(2,1)S(1)}, bf16[64,1280]{1,0:T(8,128)(2,1)S(1)}, u32[]{:S(2)}, u32[]{:S(2)}) collective-permute-start(bf16[64,1280]{1,0:T(8,128)(2,1)S(1)} %fusion.19), channel_id=1, source_target_pairs={{0,16},{4,20},{8,24},{12,28},{16,0},{20,4},{24,8},{28,12},{1,17},{... | collective-permute-start | bytes 491528 | tf_op jit(solution)/shard_map/ppermute | solution.py:69
  136.5 12.1 %collective-permute-start.26 = (bf16[64,1280]{1,0:T(8,128)(2,1)S(1)}, bf16[64,1280]{1,0:T(8,128)(2,1)S(1)}, u32[]{:S(2)}, u32[]{:S(2)}) collective-permute-start(bf16[64,1280]{1,0:T(8,128)(2,1)S(1)} %broadcast_select_fusion.4), channel_id=1, source_target_pairs={{0,8},{4,12},{8,0},{12,4},{16,24},{20,28},{24,16},{28,20},{1,9},{5... | collective-permute-start | bytes 491528 | tf_op jit(solution)/shard_map/ppermute | solution.py:69
  139.5 9.3 %collective-permute-start.30 = (bf16[64,1280]{1,0:T(8,128)(2,1)S(1)}, bf16[64,1280]{1,0:T(8,128)(2,1)S(1)}, u32[]{:S(2)}, u32[]{:S(2)}) collective-permute-start(bf16[64,1280]{1,0:T(8,128)(2,1)S(1)} %get-tuple-element.54), channel_id=1, source_target_pairs={{0,24},{4,28},{8,16},{12,20},{16,8},{20,12},{24,0},{28,4},{1,25},{... | collective-permute-start | bytes 491528 | tf_op jit(solution)/shard_map/ppermute | solution.py:69
  (9 other events, 87.5 us)

commit v13 on v11

--- a/solution.py
+++ b/solution.py
@@ -111,7 +111,6 @@
     cycle = [(0, 2), (2, 3), (3, 1), (1, 0)]
     back = [(t, s) for s, t in cycle]
     middle = [(1, 2), (2, 1)]
-    inward = [(0, 2), (3, 1)]
     outward = [(2, 0), (1, 3)]
 
     def shards(tokens, slots, gate_probs, w_gate, w_up, d_hidden):
@@ -128,7 +127,8 @@
             return jnp.where(at_end, first, second)
 
         weights = [jnp.concatenate([w_gate, w_up], axis=1)]
-        weights += [over_inner(weights[0], j) for j in range(1, inner)]
+        for j in range(1, inner):
+            weights.append(jnp.concatenate([over_inner(w_gate, j), over_inner(w_up, j)], axis=1))
         weights = jnp.concatenate(weights, axis=0)
 
         onehot = (slots[:, None] == jnp.arange(tok, dtype=slots.dtype)[None, :]).astype(BF16)
@@ -141,42 +141,22 @@
             ]
             pieces[k] = jnp.concatenate(blocks, axis=1)
         got = {k: over_outer(pieces[k], k) for k in far_first}
-        if relay:
-            got[3], got[1] = pick(got[3], got[1]), pick(got[1], got[3])
         got[0] = pieces[0]
 
         x_chunks = {}
 
-        def multiply(k, *ties):
-            x_chunks[k] = after(x_chunks[k], *ties)
-            return jnp.dot(x_chunks[k], weights, preferred_element_type=F32)
-
-        if relay:
-            x_chunks[3] = gather_etp(got[3])
-            x_chunks[1] = gather_etp(got[1])
-            far = multiply(3).astype(BF16)
-            swapped = outer_pairs(far, swap)
-            near = after(multiply(1, far).astype(BF16), far)
-            crossed = outer_pairs(near, middle)
-            x_chunks[2] = gather_etp(got[2], [[], [near]])
-            x_chunks[0] = gather_etp(after(got[0], near))
-            two = after(multiply(2, swapped, crossed), swapped)
-            inwards = outer_pairs(two.astype(BF16), inward)
-            relayed = pick(near, (after(two, swapped) + swapped.astype(F32)).astype(BF16))
-            cycled = outer_pairs(relayed, back)
-            own = multiply(0, relayed) + crossed.astype(F32) + inwards.astype(F32)
-            own = own + jnp.where(at_end, swapped.astype(F32), 0.0)
-            parts = [cycled]
-            last = relayed
-        else:
-            last, parts = rows, []
-            x_chunks[0] = gather_etp(got[0])
-            for k in far_first:
-                x_chunks[k] = gather_etp(got[k], [[last]])
-                last = multiply(k).astype(BF16)
+        parts, last = [], None
+        for k in far_first + [0]:
+            x_chunks[k] = gather_etp(got[k] if last is None else after(got[k], last))
+            product = jnp.dot(x_chunks[k], weights, preferred_element_type=F32)
+            if k:
+                last = product.astype(BF16)
                 parts.append(over_outer(last, k))
-            own = multiply(0, last)
-        probs = gather_etp(after(gate_probs, rows))
+        own = product
+        for part in parts[:-1]:
+            own = own + part.astype(F32)
+        parts = parts[-1:]
+        probs = gather_etp(after(gate_probs, product))
         order = etp ^ jnp.array(chunk_order, jnp.int32)
         hidden, paired = gate_call(order, own, probs[:, None], d_hidden, parts)
 
@@ -200,6 +180,7 @@
             )
 
         if relay:
+            x_chunks[3], x_chunks[1] = pick(x_chunks[3], x_chunks[1]), pick(x_chunks[1], x_chunks[3])
             cycled = outer_pairs(paired, cycle)
             last = advance([0], paired)
             crossed = outer_pairs(after(paired, last), middle)

time: 145 us -> 144 us (level)
  waiting for transfers between devices: 76.5 us -> 91.3 us
  matrix products: 25.5 us -> 15.8 us
  starting transfers between devices: 35.1 us -> 30.1 us
    ppermute x8 -> x4, waiting for transfers between devices: 46.1 us -> 23 us  [outer_pairs(): return lax.ppermute(value, 'dp', pairs)]
    ppermute x6 -> x9, waiting for transfers between devices: 7.68 us -> 25.2 us  [over_outer(): return lax.ppermute(value, 'dp', pairs)]
    ppermute x16, waiting for transfers between devices: 16.5 us -> 28.3 us  [over_etp(): return lax.ppermute(value, 'etp', pairs)]
    ppermute x2 -> x3, waiting for transfers between devices: 6.23 us -> 14.8 us  [over_inner(): return lax.ppermute(value, 'dp', pairs)]
    ppermute x8 -> x4, starting transfers between devices: 11.2 us -> 3.67 us  [outer_pairs(): return lax.ppermute(value, 'dp', pairs)]
    dot_general x4, matrix products: 7.56 us -> 2.71 us  [shards(): product = jnp.dot(x_chunks[k], weights, preferred_element_type=F32)]
    dot_general x4, matrix products: 7.64 us -> 2.84 us  [advance(): lax.dot_general(after(grads[k], last), weights, (((1,), (1,)), ((), ())),...]
    ppermute x6 -> x9, starting transfers between devices: 10.9 us -> 11.8 us  [over_outer(): return lax.ppermute(value, 'dp', pairs)]
  transfers between devices with their start and end apart: 32 -> 32, of which waited for: 18 -> 19; matrix products, arithmetic and copies ran while one was open for 11% -> 8% of each run, Pallas kernels for 0% -> 0%
where the time goes in v13:
time: 144 us
  waiting for transfers between devices  91.3 us (63%)
  starting transfers between devices  30.1 us (21%)
  matrix products  15.8 us (11%)
  other arithmetic  3 us (2%)
  Pallas kernels  1.51 us (1%)
    ppermute x16, waiting for transfers between devices, over_etp(): return lax.ppermute(value, 'etp', pairs)  28.3 us
    ppermute x9, waiting for transfers between devices, over_outer(): return lax.ppermute(value, 'dp', pairs)  25.2 us
    ppermute x4, waiting for transfers between devices, outer_pairs(): return lax.ppermute(value, 'dp', pairs)  23 us
    ppermute x3, waiting for transfers between devices, over_inner(): return lax.ppermute(value, 'dp', pairs)  14.8 us
    ppermute x9, starting transfers between devices, over_outer(): return lax.ppermute(value, 'dp', pairs)  11.8 us
    ppermute x16, starting transfers between devices, over_etp(): return lax.ppermute(value, 'etp', pairs)  11.1 us
    dot_general x1, matrix products, shards(): lax.dot_general(onehot, dx, (((0,), (0,)), ((), ())), preferred_element_t...  4 us
    ppermute x4, starting transfers between devices, outer_pairs(): return lax.ppermute(value, 'dp', pairs)  3.67 us
  transfers between devices with their start and end apart: 32, of which 19 were waited for; matrix products, arithmetic and copies ran while one was open for 8% of the time, Pallas kernels for 0%

profile of v13, /device:TPU:0, one launch (start us, length us, event | category | flops | bytes accessed | tf_op | source)
XLA Modules:
  0.0 144.2 jit_solution(14404927784983288076)
XLA Ops:
  0.7 3.6 %convolution_convert_fusion.1 = bf16[64,5120]{1,0:T(8,128)(2,1)S(1)} fusion(bf16[512,5120]{1,0:T(8,128)(2,1)} %param.7, s32[64]{0:T(128)} %param.8), kind=kOutput, calls=%fused_computation.1 | convolution fusion | flops 335904768 | bytes 5898496 | tf_op jit(solution)/shard_map/dot_general | solution.py:135
  4.5 4.1 %collective-permute-start.1 = (bf16[64,1280]{1,0:T(8,128)(2,1)S(1)}, bf16[64,1280]{1,0:T(8,128)(2,1)S(1)}, u32[]{:S(2)}, u32[]{:S(2)}) collective-permute-start(bf16[64,1280]{1,0:T(8,128)(2,1)S(1)} %pad_maximum_fusion.11), channel_id=1, source_target_pairs={{0,16},{4,20},{8,24},{12,28},{16,0},{20,4},{24,8},{28,12},{1,17},{... | collective-permute-start | bytes 491528 | tf_op jit(solution)/shard_map/ppermute | solution.py:69
  10.0 1.5 %collective-permute-start.6 = (bf16[640,384]{1,0:T(8,128)(2,1)S(1)}, bf16[640,384]{1,0:T(8,128)(2,1)S(1)}, u32[]{:S(2)}, u32[]{:S(2)}) collective-permute-start(bf16[640,384]{1,0:T(8,128)(2,1)S(1)} %copy-done.1), channel_id=1, source_target_pairs={{0,4},{4,0},{8,12},{12,8},{16,20},{20,16},{24,28},{28,24},{1,5},{5... | collective-permute-start | bytes 1474568 | tf_op jit(solution)/shard_map/ppermute | solution.py:73
  12.4 6.1 %collective-permute-done.2 = bf16[64,1280]{1,0:T(8,128)(2,1)S(1)} collective-permute-done((bf16[64,1280]{1,0:T(8,128)(2,1)S(1)}, bf16[64,1280]{1,0:T(8,128)(2,1)S(1)}, u32[]{:S(2)}, u32[]{:S(2)}) %collective-permute-start.2) | collective-permute-done | bytes 163872 | tf_op jit(solution)/shard_map/ppermute | solution.py:69
  18.6 1.5 %collective-permute-start.3 = (bf16[64,1280]{1,0:T(8,128)(2,1)S(1)}, bf16[64,1280]{1,0:T(8,128)(2,1)S(1)}, u32[]{:S(2)}, u32[]{:S(2)}) collective-permute-start(bf16[64,1280]{1,0:T(8,128)(2,1)S(1)} %collective-permute-done.2), channel_id=1, source_target_pairs={{0,2},{1,3},{2,0},{3,1},{4,6},{5,7},{6,4},{7,5},{8,10},{9,11},{10,... | collective-permute-start | bytes 491528 | tf_op jit(solution)/shard_map/ppermute | solution.py:77
  20.1 3.8 %collective-permute-done.3 = bf16[64,1280]{1,0:T(8,128)(2,1)S(1)} collective-permute-done((bf16[64,1280]{1,0:T(8,128)(2,1)S(1)}, bf16[64,1280]{1,0:T(8,128)(2,1)S(1)}, u32[]{:S(2)}, u32[]{:S(2)}) %collective-permute-start.3) | collective-permute-done | bytes 163872 | tf_op jit(solution)/shard_map/ppermute | solution.py:77
  24.2 8.8 %collective-permute-done.5 = bf16[640,384]{1,0:T(8,128)(2,1)S(1)} collective-permute-done((bf16[640,384]{1,0:T(8,128)(2,1)S(1)}, bf16[640,384]{1,0:T(8,128)(2,1)S(1)}, u32[]{:S(2)}, u32[]{:S(2)}) %collective-permute-start.5) | collective-permute-done | bytes 491552 | tf_op jit(solution)/shard_map/ppermute | solution.py:73
  33.8 1.6 %collective-permute-start.7 = (bf16[64,1280]{1,0:T(8,128)(2,1)S(1)}, bf16[64,1280]{1,0:T(8,128)(2,1)S(1)}, u32[]{:S(2)}, u32[]{:S(2)}) collective-permute-start(bf16[64,1280]{1,0:T(8,128)(2,1)S(1)} %collective-permute-done.1), channel_id=1, source_target_pairs={{0,2},{1,3},{2,0},{3,1},{4,6},{5,7},{6,4},{7,5},{8,10},{9,11},{10,... | collective-permute-start | bytes 491528 | tf_op jit(solution)/shard_map/ppermute | solution.py:77
  35.4 3.8 %collective-permute-done.7 = bf16[64,1280]{1,0:T(8,128)(2,1)S(1)} collective-permute-done((bf16[64,1280]{1,0:T(8,128)(2,1)S(1)}, bf16[64,1280]{1,0:T(8,128)(2,1)S(1)}, u32[]{:S(2)}, u32[]{:S(2)}) %collective-permute-start.7) | collective-permute-done | bytes 163872 | tf_op jit(solution)/shard_map/ppermute | solution.py:77
  39.4 1.6 %collective-permute-done.8 = bf16[128,1280]{1,0:T(8,128)(2,1)S(1)} collective-permute-done((bf16[128,1280]{1,0:T(8,128)(2,1)S(1)}, bf16[128,1280]{1,0:T(8,128)(2,1)S(1)}, u32[]{:S(2)}, u32[]{:S(2)}) %collective-permute-start.8) | collective-permute-done | bytes 327712 | tf_op jit(solution)/shard_map/ppermute | solution.py:77
  41.7 1.6 %collective-permute-start.9 = (bf16[64,1280]{1,0:T(8,128)(2,1)S(1)}, bf16[64,1280]{1,0:T(8,128)(2,1)S(1)}, u32[]{:S(2)}, u32[]{:S(2)}) collective-permute-start(bf16[64,1280]{1,0:T(8,128)(2,1)S(1)} %collective-permute-done), channel_id=1, source_target_pairs={{0,2},{1,3},{2,0},{3,1},{4,6},{5,7},{6,4},{7,5},{8,10},{9,11},{10,... | collective-permute-start | bytes 491528 | tf_op jit(solution)/shard_map/ppermute | solution.py:77
  43.3 2.5 %collective-permute-start.13 = (bf16[256,768]{1,0:T(8,128)(2,1)S(1)}, bf16[256,768]{1,0:T(8,128)(2,1)S(1)}, u32[]{:S(2)}, u32[]{:S(2)}) collective-permute-start(bf16[256,768]{1,0:T(8,128)(2,1)S(1)} %convolution_convert_fusion.4), channel_id=1, source_target_pairs={{0,24},{4,28},{8,16},{12,20},{16,8},{20,12},{24,0},{28,4},{1,25},{... | collective-permute-start | bytes 1179656 | tf_op jit(solution)/shard_map/ppermute | solution.py:69
  45.7 2.2 %collective-permute-done.9 = bf16[64,1280]{1,0:T(8,128)(2,1)S(1)} collective-permute-done((bf16[64,1280]{1,0:T(8,128)(2,1)S(1)}, bf16[64,1280]{1,0:T(8,128)(2,1)S(1)}, u32[]{:S(2)}, u32[]{:S(2)}) %collective-permute-start.9) | collective-permute-done | bytes 163872 | tf_op jit(solution)/shard_map/ppermute | solution.py:77
  48.1 1.6 %collective-permute-done.10 = bf16[128,1280]{1,0:T(8,128)(2,1)S(1)} collective-permute-done((bf16[128,1280]{1,0:T(8,128)(2,1)S(1)}, bf16[128,1280]{1,0:T(8,128)(2,1)S(1)}, u32[]{:S(2)}, u32[]{:S(2)}) %collective-permute-start.10) | collective-permute-done | bytes 327712 | tf_op jit(solution)/shard_map/ppermute | solution.py:77
  50.4 1.6 %collective-permute-start.11 = (bf16[64,1280]{1,0:T(8,128)(2,1)S(1)}, bf16[64,1280]{1,0:T(8,128)(2,1)S(1)}, u32[]{:S(2)}, u32[]{:S(2)}) collective-permute-start(bf16[64,1280]{1,0:T(8,128)(2,1)S(1)} %pad_maximum_fusion.9), channel_id=1, source_target_pairs={{0,2},{1,3},{2,0},{3,1},{4,6},{5,7},{6,4},{7,5},{8,10},{9,11},{10,... | collective-permute-start | bytes 491528 | tf_op jit(solution)/shard_map/ppermute | solution.py:77
  52.0 4.7 %collective-permute-done.11 = bf16[64,1280]{1,0:T(8,128)(2,1)S(1)} collective-permute-done((bf16[64,1280]{1,0:T(8,128)(2,1)S(1)}, bf16[64,1280]{1,0:T(8,128)(2,1)S(1)}, u32[]{:S(2)}, u32[]{:S(2)}) %collective-permute-start.11) | collective-permute-done | bytes 163872 | tf_op jit(solution)/shard_map/ppermute | solution.py:77
  59.2 1.6 %collective-permute-start.15 = (bf16[64]{0:T(256)(128)(2,1)S(1)}, bf16[64]{0:T(256)(128)(2,1)S(1)}, u32[]{:S(2)}, u32[]{:S(2)}) collective-permute-start(bf16[64]{0:T(256)(128)(2,1)S(1)} %copy-done.4), channel_id=1, source_target_pairs={{0,2},{1,3},{2,0},{3,1},{4,6},{5,7},{6,4},{7,5},{8,10},{9,11},{10,... | collective-permute-start | bytes 392 | tf_op jit(solution)/shard_map/ppermute | solution.py:77
  60.8 1.9 %collective-permute-done.15 = bf16[64]{0:T(256)(128)(2,1)S(1)} collective-permute-done((bf16[64]{0:T(256)(128)(2,1)S(1)}, bf16[64]{0:T(256)(128)(2,1)S(1)}, u32[]{:S(2)}, u32[]{:S(2)}) %collective-permute-start.15) | collective-permute-done | bytes 160 | tf_op jit(solution)/shard_map/ppermute | solution.py:77
  62.9 16.6 %collective-permute-done.14 = bf16[256,768]{1,0:T(8,128)(2,1)S(1)} collective-permute-done((bf16[256,768]{1,0:T(8,128)(2,1)S(1)}, bf16[256,768]{1,0:T(8,128)(2,1)S(1)}, u32[]{:S(2)}, u32[]{:S(2)}) %collective-permute-start.14) | collective-permute-done | bytes 393248 | tf_op jit(solution)/shard_map/ppermute | solution.py:69
  79.8 1.5 %shard_map.102 = (bf16[256,384]{1,0:T(8,128)(2,1)}, bf16[256,768]{1,0:T(8,128)(2,1)S(1)}) custom-call(s32[4]{0:T(128)S(1)} %broadcast_xor_fusion.order_ref, f32[256,768]{1,0:T(8,128)S(1)} %convert_add_fusion.pre_ref, bf16[256,1]{1,0:T(8,128)(2,1)S(1)} %broadcast_in_dim.10.prob_ref, bf16[256,384]{1,0:T(8,128)(2,1)S(1)} %copy-done, ...), custom_call_target="tpu_custom_call" | custom-call | flops 1966080 | bytes 2949120 | tf_op jit(solution)/shard_map/pallas_call | solution.py:49
  85.2 8.7 %collective-permute-done.20 = bf16[256,768]{1,0:T(8,128)(2,1)S(1)} collective-permute-done((bf16[256,768]{1,0:T(8,128)(2,1)S(1)}, bf16[256,768]{1,0:T(8,128)(2,1)S(1)}, u32[]{:S(2)}, u32[]{:S(2)}) %collective-permute-start.20) | collective-permute-done | bytes 393248 | tf_op jit(solution)/shard_map/ppermute | solution.py:108
  94.0 1.4 %collective-permute-start.23 = (bf16[256,768]{1,0:T(8,128)(2,1)S(1)}, bf16[256,768]{1,0:T(8,128)(2,1)S(1)}, u32[]{:S(2)}, u32[]{:S(2)}) collective-permute-start(bf16[256,768]{1,0:T(8,128)(2,1)S(1)} %broadcast_select_fusion.4), channel_id=1, source_target_pairs={{0,8},{4,12},{8,0},{12,4},{16,24},{20,28},{24,16},{28,20},{1,9},{5... | collective-permute-start | bytes 1179656 | tf_op jit(solution)/shard_map/ppermute | solution.py:108
  95.5 7.8 %collective-permute-done.21 = bf16[256,768]{1,0:T(8,128)(2,1)S(1)} collective-permute-done((bf16[256,768]{1,0:T(8,128)(2,1)S(1)}, bf16[256,768]{1,0:T(8,128)(2,1)S(1)}, u32[]{:S(2)}, u32[]{:S(2)}) %collective-permute-start.21) | collective-permute-done | bytes 393248 | tf_op jit(solution)/shard_map/ppermute | solution.py:108
  105.0 6.5 %collective-permute-done.23 = bf16[256,768]{1,0:T(8,128)(2,1)S(1)} collective-permute-done((bf16[256,768]{1,0:T(8,128)(2,1)S(1)}, bf16[256,768]{1,0:T(8,128)(2,1)S(1)}, u32[]{:S(2)}, u32[]{:S(2)}) %collective-permute-start.23) | collective-permute-done | bytes 393248 | tf_op jit(solution)/shard_map/ppermute | solution.py:108
  114.7 1.5 %collective-permute-start.31 = (bf16[640,768]{1,0:T(8,128)(2,1)S(1)}, bf16[640,768]{1,0:T(8,128)(2,1)S(1)}, u32[]{:S(2)}, u32[]{:S(2)}) collective-permute-start(bf16[640,768]{1,0:T(8,128)(2,1)S(1)} %add_convert_fusion), channel_id=1, source_target_pairs={{0,4},{4,0},{8,12},{12,8},{16,20},{20,16},{24,28},{28,24},{1,5},{5... | collective-permute-start | bytes 2949128 | tf_op jit(solution)/shard_map/ppermute | solution.py:73
  117.7 1.6 %collective-permute-start.25 = (bf16[128,1280]{1,0:T(8,128)(2,1)S(1)}, bf16[128,1280]{1,0:T(8,128)(2,1)S(1)}, u32[]{:S(2)}, u32[]{:S(2)}) collective-permute-start(bf16[128,1280]{1,0:T(8,128)(2,1)S(1)} %pad_maximum_fusion.8), channel_id=1, source_target_pairs={{0,2},{1,3},{2,0},{3,1},{4,6},{5,7},{6,4},{7,5},{8,10},{9,11},{10,... | collective-permute-start | bytes 983048 | tf_op jit(solution)/shard_map/ppermute | solution.py:77
  119.3 1.8 %collective-permute-done.28 = bf16[64,1280]{1,0:T(8,128)(2,1)S(1)} collective-permute-done((bf16[64,1280]{1,0:T(8,128)(2,1)S(1)}, bf16[64,1280]{1,0:T(8,128)(2,1)S(1)}, u32[]{:S(2)}, u32[]{:S(2)}) %collective-permute-start.28) | collective-permute-done | bytes 163872 | tf_op jit(solution)/shard_map/ppermute | solution.py:77
  121.8 6.0 %collective-permute-done.25 = bf16[128,1280]{1,0:T(8,128)(2,1)S(1)} collective-permute-done((bf16[128,1280]{1,0:T(8,128)(2,1)S(1)}, bf16[128,1280]{1,0:T(8,128)(2,1)S(1)}, u32[]{:S(2)}, u32[]{:S(2)}) %collective-permute-start.25) | collective-permute-done | bytes 327712 | tf_op jit(solution)/shard_map/ppermute | solution.py:77
  128.7 2.4 %collective-permute-done.29 = bf16[64,1280]{1,0:T(8,128)(2,1)S(1)} collective-permute-done((bf16[64,1280]{1,0:T(8,128)(2,1)S(1)}, bf16[64,1280]{1,0:T(8,128)(2,1)S(1)}, u32[]{:S(2)}, u32[]{:S(2)}) %collective-permute-start.29) | collective-permute-done | bytes 163872 | tf_op jit(solution)/shard_map/ppermute | solution.py:69
  132.6 5.9 %collective-permute-done.31 = bf16[640,768]{1,0:T(8,128)(2,1)S(1)} collective-permute-done((bf16[640,768]{1,0:T(8,128)(2,1)S(1)}, bf16[640,768]{1,0:T(8,128)(2,1)S(1)}, u32[]{:S(2)}, u32[]{:S(2)}) %collective-permute-start.31) | collective-permute-done | bytes 983072 | tf_op jit(solution)/shard_map/ppermute | solution.py:73
  138.5 1.5 %slice_add_fusion = (f32[640,384]{1,0:T(8,128)}, f32[640,384]{1,0:T(8,128)}) fusion(f32[640,768]{1,0:T(8,128)S(1)} %fusion, bf16[640,768]{1,0:T(8,128)(2,1)S(1)} %collective-permute-done.31), kind=kLoop, calls=%fused_computation.16 | loop fusion | flops 983040 | bytes 4915200 | tf_op jit(solution)/shard_map/add | solution.py:218
  140.2 4.0 %convolution_convert_fusion = bf16[512,5120]{1,0:T(8,128)(2,1)} fusion(bf16[64,5120]{1,0:T(8,128)(2,1)S(1)} %slice_dynamic-update-slice_fusion.2, s32[64]{0:T(128)S(1)} %copy-done.3), kind=kOutput, calls=%fused_computation | convolution fusion | flops 338198528 | bytes 5898496 | tf_op jit(solution)/shard_map/dot_general | solution.py:231
  (122 shorter events, 21.6 us)
Async XLA Ops:
  4.5 29.4 %collective-permute-start.1 = (bf16[64,1280]{1,0:T(8,128)(2,1)S(1)}, bf16[64,1280]{1,0:T(8,128)(2,1)S(1)}, u32[]{:S(2)}, u32[]{:S(2)}) collective-permute-start(bf16[64,1280]{1,0:T(8,128)(2,1)S(1)} %pad_maximum_fusion.11), channel_id=1, source_target_pairs={{0,16},{4,20},{8,24},{12,28},{16,0},{20,4},{24,8},{28,12},{1,17},{... | collective-permute-start | bytes 491528 | tf_op jit(solution)/shard_map/ppermute | solution.py:69
  8.6 10.0 %collective-permute-start.2 = (bf16[64,1280]{1,0:T(8,128)(2,1)S(1)}, bf16[64,1280]{1,0:T(8,128)(2,1)S(1)}, u32[]{:S(2)}, u32[]{:S(2)}) collective-permute-start(bf16[64,1280]{1,0:T(8,128)(2,1)S(1)} %pad_maximum_fusion.12), channel_id=1, source_target_pairs={{0,24},{4,28},{8,16},{12,20},{16,8},{20,12},{24,0},{28,4},{1,25},{... | collective-permute-start | bytes 491528 | tf_op jit(solution)/shard_map/ppermute | solution.py:69
  10.0 14.2 %collective-permute-start.6 = (bf16[640,384]{1,0:T(8,128)(2,1)S(1)}, bf16[640,384]{1,0:T(8,128)(2,1)S(1)}, u32[]{:S(2)}, u32[]{:S(2)}) collective-permute-start(bf16[640,384]{1,0:T(8,128)(2,1)S(1)} %copy-done.1), channel_id=1, source_target_pairs={{0,4},{4,0},{8,12},{12,8},{16,20},{20,16},{24,28},{28,24},{1,5},{5... | collective-permute-start | bytes 1474568 | tf_op jit(solution)/shard_map/ppermute | solution.py:73
  11.5 21.4 %collective-permute-start.5 = (bf16[640,384]{1,0:T(8,128)(2,1)S(1)}, bf16[640,384]{1,0:T(8,128)(2,1)S(1)}, u32[]{:S(2)}, u32[]{:S(2)}) collective-permute-start(bf16[640,384]{1,0:T(8,128)(2,1)S(1)} %copy-done.2), channel_id=1, source_target_pairs={{0,4},{4,0},{8,12},{12,8},{16,20},{20,16},{24,28},{28,24},{1,5},{5... | collective-permute-start | bytes 1474568 | tf_op jit(solution)/shard_map/ppermute | solution.py:73
  12.0 29.6 %collective-permute-start = (bf16[64,1280]{1,0:T(8,128)(2,1)S(1)}, bf16[64,1280]{1,0:T(8,128)(2,1)S(1)}, u32[]{:S(2)}, u32[]{:S(2)}) collective-permute-start(bf16[64,1280]{1,0:T(8,128)(2,1)S(1)} %pad_maximum_fusion.10), channel_id=1, source_target_pairs={{0,8},{4,12},{8,0},{12,4},{16,24},{20,28},{24,16},{28,20},{1,9},{5... | collective-permute-start | bytes 491528 | tf_op jit(solution)/shard_map/ppermute | solution.py:69
  18.6 5.3 %collective-permute-start.3 = (bf16[64,1280]{1,0:T(8,128)(2,1)S(1)}, bf16[64,1280]{1,0:T(8,128)(2,1)S(1)}, u32[]{:S(2)}, u32[]{:S(2)}) collective-permute-start(bf16[64,1280]{1,0:T(8,128)(2,1)S(1)} %collective-permute-done.2), channel_id=1, source_target_pairs={{0,2},{1,3},{2,0},{3,1},{4,6},{5,7},{6,4},{7,5},{8,10},{9,11},{10,... | collective-permute-start | bytes 491528 | tf_op jit(solution)/shard_map/ppermute | solution.py:77
  23.9 9.2 %collective-permute-start.4 = (bf16[128,1280]{1,0:T(8,128)(2,1)S(1)}, bf16[128,1280]{1,0:T(8,128)(2,1)S(1)}, u32[]{:S(2)}, u32[]{:S(2)}) collective-permute-start(bf16[128,1280]{1,0:T(8,128)(2,1)S(1)} %pad_maximum_fusion.4), channel_id=1, source_target_pairs={{0,1},{1,0},{2,3},{3,2},{4,5},{5,4},{6,7},{7,6},{8,9},{9,8},{10,11... | collective-permute-start | bytes 983048 | tf_op jit(solution)/shard_map/ppermute | solution.py:77
  33.8 5.4 %collective-permute-start.7 = (bf16[64,1280]{1,0:T(8,128)(2,1)S(1)}, bf16[64,1280]{1,0:T(8,128)(2,1)S(1)}, u32[]{:S(2)}, u32[]{:S(2)}) collective-permute-start(bf16[64,1280]{1,0:T(8,128)(2,1)S(1)} %collective-permute-done.1), channel_id=1, source_target_pairs={{0,2},{1,3},{2,0},{3,1},{4,6},{5,7},{6,4},{7,5},{8,10},{9,11},{10,... | collective-permute-start | bytes 491528 | tf_op jit(solution)/shard_map/ppermute | solution.py:77
  39.2 1.7 %collective-permute-start.8 = (bf16[128,1280]{1,0:T(8,128)(2,1)S(1)}, bf16[128,1280]{1,0:T(8,128)(2,1)S(1)}, u32[]{:S(2)}, u32[]{:S(2)}) collective-permute-start(bf16[128,1280]{1,0:T(8,128)(2,1)S(1)} %pad_maximum_fusion.5), channel_id=1, source_target_pairs={{0,1},{1,0},{2,3},{3,2},{4,5},{5,4},{6,7},{7,6},{8,9},{9,8},{10,11... | collective-permute-start | bytes 983048 | tf_op jit(solution)/shard_map/ppermute | solution.py:77
  41.7 6.3 %collective-permute-start.9 = (bf16[64,1280]{1,0:T(8,128)(2,1)S(1)}, bf16[64,1280]{1,0:T(8,128)(2,1)S(1)}, u32[]{:S(2)}, u32[]{:S(2)}) collective-permute-start(bf16[64,1280]{1,0:T(8,128)(2,1)S(1)} %collective-permute-done), channel_id=1, source_target_pairs={{0,2},{1,3},{2,0},{3,1},{4,6},{5,7},{6,4},{7,5},{8,10},{9,11},{10,... | collective-permute-start | bytes 491528 | tf_op jit(solution)/shard_map/ppermute | solution.py:77
  43.3 19.6 %collective-permute-start.13 = (bf16[256,768]{1,0:T(8,128)(2,1)S(1)}, bf16[256,768]{1,0:T(8,128)(2,1)S(1)}, u32[]{:S(2)}, u32[]{:S(2)}) collective-permute-start(bf16[256,768]{1,0:T(8,128)(2,1)S(1)} %convolution_convert_fusion.4), channel_id=1, source_target_pairs={{0,24},{4,28},{8,16},{12,20},{16,8},{20,12},{24,0},{28,4},{1,25},{... | collective-permute-start | bytes 1179656 | tf_op jit(solution)/shard_map/ppermute | solution.py:69
  45.7 33.7 %collective-permute-start.14 = (bf16[256,768]{1,0:T(8,128)(2,1)S(1)}, bf16[256,768]{1,0:T(8,128)(2,1)S(1)}, u32[]{:S(2)}, u32[]{:S(2)}) collective-permute-start(bf16[256,768]{1,0:T(8,128)(2,1)S(1)} %convolution_convert_fusion.3), channel_id=1, source_target_pairs={{0,16},{4,20},{8,24},{12,28},{16,0},{20,4},{24,8},{28,12},{1,17},{... | collective-permute-start | bytes 1179656 | tf_op jit(solution)/shard_map/ppermute | solution.py:69
  48.0 1.7 %collective-permute-start.10 = (bf16[128,1280]{1,0:T(8,128)(2,1)S(1)}, bf16[128,1280]{1,0:T(8,128)(2,1)S(1)}, u32[]{:S(2)}, u32[]{:S(2)}) collective-permute-start(bf16[128,1280]{1,0:T(8,128)(2,1)S(1)} %pad_maximum_fusion.6), channel_id=1, source_target_pairs={{0,1},{1,0},{2,3},{3,2},{4,5},{5,4},{6,7},{7,6},{8,9},{9,8},{10,11... | collective-permute-start | bytes 983048 | tf_op jit(solution)/shard_map/ppermute | solution.py:77
  50.4 6.3 %collective-permute-start.11 = (bf16[64,1280]{1,0:T(8,128)(2,1)S(1)}, bf16[64,1280]{1,0:T(8,128)(2,1)S(1)}, u32[]{:S(2)}, u32[]{:S(2)}) collective-permute-start(bf16[64,1280]{1,0:T(8,128)(2,1)S(1)} %pad_maximum_fusion.9), channel_id=1, source_target_pairs={{0,2},{1,3},{2,0},{3,1},{4,6},{5,7},{6,4},{7,5},{8,10},{9,11},{10,... | collective-permute-start | bytes 491528 | tf_op jit(solution)/shard_map/ppermute | solution.py:77
  56.7 1.7 %collective-permute-start.12 = (bf16[128,1280]{1,0:T(8,128)(2,1)S(1)}, bf16[128,1280]{1,0:T(8,128)(2,1)S(1)}, u32[]{:S(2)}, u32[]{:S(2)}) collective-permute-start(bf16[128,1280]{1,0:T(8,128)(2,1)S(1)} %pad_maximum_fusion.7), channel_id=1, source_target_pairs={{0,1},{1,0},{2,3},{3,2},{4,5},{5,4},{6,7},{7,6},{8,9},{9,8},{10,11... | collective-permute-start | bytes 983048 | tf_op jit(solution)/shard_map/ppermute | solution.py:77
  56.8 22.9 %collective-permute-start.17 = (bf16[256,768]{1,0:T(8,128)(2,1)S(1)}, bf16[256,768]{1,0:T(8,128)(2,1)S(1)}, u32[]{:S(2)}, u32[]{:S(2)}) collective-permute-start(bf16[256,768]{1,0:T(8,128)(2,1)S(1)} %convolution_convert_fusion.2), channel_id=1, source_target_pairs={{0,8},{4,12},{8,0},{12,4},{16,24},{20,28},{24,16},{28,20},{1,9},{5... | collective-permute-start | bytes 1179656 | tf_op jit(solution)/shard_map/ppermute | solution.py:69
  59.2 3.6 %collective-permute-start.15 = (bf16[64]{0:T(256)(128)(2,1)S(1)}, bf16[64]{0:T(256)(128)(2,1)S(1)}, u32[]{:S(2)}, u32[]{:S(2)}) collective-permute-start(bf16[64]{0:T(256)(128)(2,1)S(1)} %copy-done.4), channel_id=1, source_target_pairs={{0,2},{1,3},{2,0},{3,1},{4,6},{5,7},{6,4},{7,5},{8,10},{9,11},{10,... | collective-permute-start | bytes 392 | tf_op jit(solution)/shard_map/ppermute | solution.py:77
  62.8 16.7 %collective-permute-start.16 = (bf16[128]{0:T(256)(128)(2,1)S(1)}, bf16[128]{0:T(256)(128)(2,1)S(1)}, u32[]{:S(2)}, u32[]{:S(2)}) collective-permute-start(bf16[128]{0:T(256)(128)(2,1)S(1)} %pad_maximum_fusion.13), channel_id=1, source_target_pairs={{0,1},{1,0},{2,3},{3,2},{4,5},{5,4},{6,7},{7,6},{8,9},{9,8},{10,11... | collective-permute-start | bytes 776 | tf_op jit(solution)/shard_map/ppermute | solution.py:77
  82.0 2.5 %collective-permute-start.18 = (bf16[128,1280]{1,0:T(8,128)(2,1)S(1)}, bf16[128,1280]{1,0:T(8,128)(2,1)S(1)}, u32[]{:S(2)}, u32[]{:S(2)}) collective-permute-start(bf16[128,1280]{1,0:T(8,128)(2,1)S(1)} %slice.253), channel_id=1, source_target_pairs={{0,1},{1,0},{2,3},{3,2},{4,5},{5,4},{6,7},{7,6},{8,9},{9,8},{10,11... | collective-permute-start | bytes 983048 | tf_op jit(solution)/shard_map/ppermute | solution.py:77
  82.3 11.7 %collective-permute-start.20 = (bf16[256,768]{1,0:T(8,128)(2,1)S(1)}, bf16[256,768]{1,0:T(8,128)(2,1)S(1)}, u32[]{:S(2)}, u32[]{:S(2)}) collective-permute-start(bf16[256,768]{1,0:T(8,128)(2,1)S(1)} %get-tuple-element.32), channel_id=1, source_target_pairs={{0,16},{4,20},{16,24},{20,28},{24,8},{28,12},{8,0},{12,4},{1,17},{... | collective-permute-start | bytes 1179656 | tf_op jit(solution)/shard_map/ppermute | solution.py:108
  82.4 20.8 %collective-permute-start.21 = (bf16[256,768]{1,0:T(8,128)(2,1)S(1)}, bf16[256,768]{1,0:T(8,128)(2,1)S(1)}, u32[]{:S(2)}, u32[]{:S(2)}) collective-permute-start(bf16[256,768]{1,0:T(8,128)(2,1)S(1)} %get-tuple-element.32), channel_id=1, source_target_pairs={{16,0},{20,4},{8,24},{12,28},{17,1},{21,5},{9,25},{13,29},{18,2},{... | collective-permute-start | bytes 1179656 | tf_op jit(solution)/shard_map/ppermute | solution.py:108
  83.7 21.2 %collective-permute-start.22 = (bf16[256,768]{1,0:T(8,128)(2,1)S(1)}, bf16[256,768]{1,0:T(8,128)(2,1)S(1)}, u32[]{:S(2)}, u32[]{:S(2)}) collective-permute-start(bf16[256,768]{1,0:T(8,128)(2,1)S(1)} %get-tuple-element.32), channel_id=1, source_target_pairs={{8,16},{12,20},{16,8},{20,12},{9,17},{13,21},{17,9},{21,13},{10,18... | collective-permute-start | bytes 1179656 | tf_op jit(solution)/shard_map/ppermute | solution.py:108
  84.7 20.3 %collective-permute-start.19 = (bf16[64,1280]{1,0:T(8,128)(2,1)S(1)}, bf16[64,1280]{1,0:T(8,128)(2,1)S(1)}, u32[]{:S(2)}, u32[]{:S(2)}) collective-permute-start(bf16[64,1280]{1,0:T(8,128)(2,1)S(1)} %slice.257), channel_id=1, source_target_pairs={{0,2},{1,3},{2,0},{3,1},{4,6},{5,7},{6,4},{7,5},{8,10},{9,11},{10,... | collective-permute-start | bytes 491528 | tf_op jit(solution)/shard_map/ppermute | solution.py:77
  94.0 17.5 %collective-permute-start.23 = (bf16[256,768]{1,0:T(8,128)(2,1)S(1)}, bf16[256,768]{1,0:T(8,128)(2,1)S(1)}, u32[]{:S(2)}, u32[]{:S(2)}) collective-permute-start(bf16[256,768]{1,0:T(8,128)(2,1)S(1)} %broadcast_select_fusion.4), channel_id=1, source_target_pairs={{0,8},{4,12},{8,0},{12,4},{16,24},{20,28},{24,16},{28,20},{1,9},{5... | collective-permute-start | bytes 1179656 | tf_op jit(solution)/shard_map/ppermute | solution.py:108
  104.8 9.2 %collective-permute-start.27 = (bf16[128,1280]{1,0:T(8,128)(2,1)S(1)}, bf16[128,1280]{1,0:T(8,128)(2,1)S(1)}, u32[]{:S(2)}, u32[]{:S(2)}) collective-permute-start(bf16[128,1280]{1,0:T(8,128)(2,1)S(1)} %slice.250), channel_id=1, source_target_pairs={{0,1},{1,0},{2,3},{3,2},{4,5},{5,4},{6,7},{7,6},{8,9},{9,8},{10,11... | collective-permute-start | bytes 983048 | tf_op jit(solution)/shard_map/ppermute | solution.py:77
  113.9 3.6 %collective-permute-start.24 = (bf16[256,1280]{1,0:T(8,128)(2,1)S(1)}, bf16[256,1280]{1,0:T(8,128)(2,1)S(1)}, u32[]{:S(2)}, u32[]{:S(2)}) collective-permute-start(bf16[256,1280]{1,0:T(8,128)(2,1)S(1)} %pad_maximum_fusion.3), channel_id=1, source_target_pairs={{0,1},{1,0},{2,3},{3,2},{4,5},{5,4},{6,7},{7,6},{8,9},{9,8},{10,11... | collective-permute-start | bytes 1966088 | tf_op jit(solution)/shard_map/ppermute | solution.py:77
  114.1 7.1 %collective-permute-start.28 = (bf16[64,1280]{1,0:T(8,128)(2,1)S(1)}, bf16[64,1280]{1,0:T(8,128)(2,1)S(1)}, u32[]{:S(2)}, u32[]{:S(2)}) collective-permute-start(bf16[64,1280]{1,0:T(8,128)(2,1)S(1)} %slice.254), channel_id=1, source_target_pairs={{0,2},{1,3},{2,0},{3,1},{4,6},{5,7},{6,4},{7,5},{8,10},{9,11},{10,... | collective-permute-start | bytes 491528 | tf_op jit(solution)/shard_map/ppermute | solution.py:77
  114.7 23.9 %collective-permute-start.31 = (bf16[640,768]{1,0:T(8,128)(2,1)S(1)}, bf16[640,768]{1,0:T(8,128)(2,1)S(1)}, u32[]{:S(2)}, u32[]{:S(2)}) collective-permute-start(bf16[640,768]{1,0:T(8,128)(2,1)S(1)} %add_convert_fusion), channel_id=1, source_target_pairs={{0,4},{4,0},{8,12},{12,8},{16,20},{20,16},{24,28},{28,24},{1,5},{5... | collective-permute-start | bytes 2949128 | tf_op jit(solution)/shard_map/ppermute | solution.py:73
  117.7 10.0 %collective-permute-start.25 = (bf16[128,1280]{1,0:T(8,128)(2,1)S(1)}, bf16[128,1280]{1,0:T(8,128)(2,1)S(1)}, u32[]{:S(2)}, u32[]{:S(2)}) collective-permute-start(bf16[128,1280]{1,0:T(8,128)(2,1)S(1)} %pad_maximum_fusion.8), channel_id=1, source_target_pairs={{0,2},{1,3},{2,0},{3,1},{4,6},{5,7},{6,4},{7,5},{8,10},{9,11},{10,... | collective-permute-start | bytes 983048 | tf_op jit(solution)/shard_map/ppermute | solution.py:77
  121.2 10.0 %collective-permute-start.29 = (bf16[64,1280]{1,0:T(8,128)(2,1)S(1)}, bf16[64,1280]{1,0:T(8,128)(2,1)S(1)}, u32[]{:S(2)}, u32[]{:S(2)}) collective-permute-start(bf16[64,1280]{1,0:T(8,128)(2,1)S(1)} %fusion.15), channel_id=1, source_target_pairs={{0,16},{4,20},{8,24},{12,28},{16,0},{20,4},{24,8},{28,12},{1,17},{... | collective-permute-start | bytes 491528 | tf_op jit(solution)/shard_map/ppermute | solution.py:69
  127.9 12.1 %collective-permute-start.26 = (bf16[64,1280]{1,0:T(8,128)(2,1)S(1)}, bf16[64,1280]{1,0:T(8,128)(2,1)S(1)}, u32[]{:S(2)}, u32[]{:S(2)}) collective-permute-start(bf16[64,1280]{1,0:T(8,128)(2,1)S(1)} %broadcast_select_fusion.6), channel_id=1, source_target_pairs={{0,8},{4,12},{8,0},{12,4},{16,24},{20,28},{24,16},{28,20},{1,9},{5... | collective-permute-start | bytes 491528 | tf_op jit(solution)/shard_map/ppermute | solution.py:69
  131.2 9.0 %collective-permute-start.30 = (bf16[64,1280]{1,0:T(8,128)(2,1)S(1)}, bf16[64,1280]{1,0:T(8,128)(2,1)S(1)}, u32[]{:S(2)}, u32[]{:S(2)}) collective-permute-start(bf16[64,1280]{1,0:T(8,128)(2,1)S(1)} %get-tuple-element.46), channel_id=1, source_target_pairs={{0,24},{4,28},{8,16},{12,20},{16,8},{20,12},{24,0},{28,4},{1,25},{... | collective-permute-start | bytes 491528 | tf_op jit(solution)/shard_map/ppermute | solution.py:69
  (6 other events, 46.7 us)

commit v14 on v13

--- a/solution.py
+++ b/solution.py
@@ -143,20 +143,20 @@
         got = {k: over_outer(pieces[k], k) for k in far_first}
         got[0] = pieces[0]
 
-        x_chunks = {}
-
-        parts, last = [], None
-        for k in far_first + [0]:
-            x_chunks[k] = gather_etp(got[k] if last is None else after(got[k], last))
-            product = jnp.dot(x_chunks[k], weights, preferred_element_type=F32)
-            if k:
-                last = product.astype(BF16)
-                parts.append(over_outer(last, k))
-        own = product
+        x_chunks = {k: gather_etp(got[k]) for k in [0] + far_first}
+        each = cap * etp_size
+        product = jnp.dot(
+            jnp.concatenate([x_chunks[k] for k in [0] + far_first], axis=0),
+            weights,
+            preferred_element_type=F32,
+        )
+        products = {k: product[i * each : (i + 1) * each] for i, k in enumerate([0] + far_first)}
+        parts = [over_outer(products[k].astype(BF16), k) for k in far_first]
+        probs = gather_etp(after(gate_probs, product))
+        own = products[0]
         for part in parts[:-1]:
             own = own + part.astype(F32)
         parts = parts[-1:]
-        probs = gather_etp(after(gate_probs, product))
         order = etp ^ jnp.array(chunk_order, jnp.int32)
         hidden, paired = gate_call(order, own, probs[:, None], d_hidden, parts)
 

time: 144 us -> 147 us (1.021)
  waiting for transfers between devices: 91.3 us -> 74.7 us
  starting transfers between devices: 30.1 us -> 44.1 us
  local copies, waits for them, and re-layouts: 1.09 us -> 5.62 us
    ppermute x16, waiting for transfers between devices: 28.3 us -> 20.1 us  [over_etp(): return lax.ppermute(value, 'etp', pairs)]
    ppermute x3, waiting for transfers between devices: 14.8 us -> 6.93 us  [over_inner(): return lax.ppermute(value, 'dp', pairs)]
    ppermute x4, starting transfers between devices: 3.67 us -> 11.4 us  [outer_pairs(): return lax.ppermute(value, 'dp', pairs)]
    unnamed x20 -> x22, local copies, waits for them, and re-layouts: 0.14 us -> 4.49 us
    ppermute x9, starting transfers between devices: 11.8 us -> 15.3 us  [over_outer(): return lax.ppermute(value, 'dp', pairs)]
    ppermute x4, waiting for transfers between devices: 23 us -> 20.4 us  [outer_pairs(): return lax.ppermute(value, 'dp', pairs)]
    ppermute x9, waiting for transfers between devices: 25.2 us -> 27.2 us  [over_outer(): return lax.ppermute(value, 'dp', pairs)]
    ppermute x16, starting transfers between devices: 11.1 us -> 12.7 us  [over_etp(): return lax.ppermute(value, 'etp', pairs)]
  transfers between devices with their start and end apart: 32 -> 32, of which waited for: 19 -> 16; matrix products, arithmetic and copies ran while one was open for 8% -> 8% of each run, Pallas kernels for 0% -> 0%
where the time goes in v14:
time: 147 us; the launch traced here: 146 us
  waiting for transfers between devices  74.7 us (51%)
  starting transfers between devices  44.1 us (30%)
  matrix products  15.3 us (10%)
  local copies, waits for them, and re-layouts  5.62 us (4%)
  other arithmetic  3.82 us (3%)
  Pallas kernels  1.51 us (1%)
    ppermute x9, waiting for transfers between devices, over_outer(): return lax.ppermute(value, 'dp', pairs)  27.2 us
    ppermute x4, waiting for transfers between devices, outer_pairs(): return lax.ppermute(value, 'dp', pairs)  20.4 us
    ppermute x16, waiting for transfers between devices, over_etp(): return lax.ppermute(value, 'etp', pairs)  20.1 us
    ppermute x9, starting transfers between devices, over_outer(): return lax.ppermute(value, 'dp', pairs)  15.3 us
    ppermute x16, starting transfers between devices, over_etp(): return lax.ppermute(value, 'etp', pairs)  12.7 us
    ppermute x4, starting transfers between devices, outer_pairs(): return lax.ppermute(value, 'dp', pairs)  11.4 us
    ppermute x3, waiting for transfers between devices, over_inner(): return lax.ppermute(value, 'dp', pairs)  6.93 us
    ppermute x3, starting transfers between devices, over_inner(): return lax.ppermute(value, 'dp', pairs)  4.64 us
  transfers between devices with their start and end apart: 32, of which 16 were waited for; matrix products, arithmetic and copies ran while one was open for 8% of the time, Pallas kernels for 0%

profile of v14, /device:TPU:0, one launch (start us, length us, event | category | flops | bytes accessed | tf_op | source)
XLA Modules:
  0.0 146.3 jit_solution(5546535883676233102)
XLA Ops:
  0.7 3.6 %convolution_convert_fusion.1 = bf16[64,5120]{1,0:T(8,128)(2,1)S(1)} fusion(bf16[512,5120]{1,0:T(8,128)(2,1)} %param.7, s32[64]{0:T(128)} %param.8), kind=kOutput, calls=%fused_computation.1 | convolution fusion | flops 335904768 | bytes 5898496 | tf_op jit(solution)/shard_map/dot_general | solution.py:135
  4.5 3.1 %collective-permute-start.8 = (bf16[64,1280]{1,0:T(8,128)(2,1)S(1)}, bf16[64,1280]{1,0:T(8,128)(2,1)S(1)}, u32[]{:S(2)}, u32[]{:S(2)}) collective-permute-start(bf16[64,1280]{1,0:T(8,128)(2,1)S(1)} %pad_maximum_fusion.12), channel_id=1, source_target_pairs={{0,8},{4,12},{8,0},{12,4},{16,24},{20,28},{24,16},{28,20},{1,9},{5... | collective-permute-start | bytes 491528 | tf_op jit(solution)/shard_map/ppermute | solution.py:69
  7.6 2.7 %collective-permute-start.5 = (bf16[64,1280]{1,0:T(8,128)(2,1)S(1)}, bf16[64,1280]{1,0:T(8,128)(2,1)S(1)}, u32[]{:S(2)}, u32[]{:S(2)}) collective-permute-start(bf16[64,1280]{1,0:T(8,128)(2,1)S(1)} %pad_maximum_fusion.11), channel_id=1, source_target_pairs={{0,16},{4,20},{8,24},{12,28},{16,0},{20,4},{24,8},{28,12},{1,17},{... | collective-permute-start | bytes 491528 | tf_op jit(solution)/shard_map/ppermute | solution.py:69
  11.0 1.7 %collective-permute-start = (bf16[64,1280]{1,0:T(8,128)(2,1)S(1)}, bf16[64,1280]{1,0:T(8,128)(2,1)S(1)}, u32[]{:S(2)}, u32[]{:S(2)}) collective-permute-start(bf16[64,1280]{1,0:T(8,128)(2,1)S(1)} %get-tuple-element.85), channel_id=1, source_target_pairs={{0,2},{1,3},{2,0},{3,1},{4,6},{5,7},{6,4},{7,5},{8,10},{9,11},{10,... | collective-permute-start | bytes 491528 | tf_op jit(solution)/shard_map/ppermute | solution.py:77
  12.8 1.5 %collective-permute-start.12 = (bf16[640,384]{1,0:T(8,128)(2,1)S(1)}, bf16[640,384]{1,0:T(8,128)(2,1)S(1)}, u32[]{:S(2)}, u32[]{:S(2)}) collective-permute-start(bf16[640,384]{1,0:T(8,128)(2,1)S(1)} %copy-done.1), channel_id=1, source_target_pairs={{0,4},{4,0},{8,12},{12,8},{16,20},{20,16},{24,28},{28,24},{1,5},{5... | collective-permute-start | bytes 1474568 | tf_op jit(solution)/shard_map/ppermute | solution.py:73
  14.3 2.1 %collective-permute-done = bf16[64,1280]{1,0:T(8,128)(2,1)S(1)} collective-permute-done((bf16[64,1280]{1,0:T(8,128)(2,1)S(1)}, bf16[64,1280]{1,0:T(8,128)(2,1)S(1)}, u32[]{:S(2)}, u32[]{:S(2)}) %collective-permute-start) | collective-permute-done | bytes 163872 | tf_op jit(solution)/shard_map/ppermute | solution.py:77
  16.4 1.6 %collective-permute-start.11 = (bf16[640,384]{1,0:T(8,128)(2,1)S(1)}, bf16[640,384]{1,0:T(8,128)(2,1)S(1)}, u32[]{:S(2)}, u32[]{:S(2)}) collective-permute-start(bf16[640,384]{1,0:T(8,128)(2,1)S(1)} %copy-done.2), channel_id=1, source_target_pairs={{0,4},{4,0},{8,12},{12,8},{16,20},{20,16},{24,28},{28,24},{1,5},{5... | collective-permute-start | bytes 1474568 | tf_op jit(solution)/shard_map/ppermute | solution.py:73
  18.1 3.0 %collective-permute-done.2 = bf16[64,1280]{1,0:T(8,128)(2,1)S(1)} collective-permute-done((bf16[64,1280]{1,0:T(8,128)(2,1)S(1)}, bf16[64,1280]{1,0:T(8,128)(2,1)S(1)}, u32[]{:S(2)}, u32[]{:S(2)}) %collective-permute-start.2) | collective-permute-done | bytes 163872 | tf_op jit(solution)/shard_map/ppermute | solution.py:69
  21.1 1.5 %collective-permute-start.3 = (bf16[64,1280]{1,0:T(8,128)(2,1)S(1)}, bf16[64,1280]{1,0:T(8,128)(2,1)S(1)}, u32[]{:S(2)}, u32[]{:S(2)}) collective-permute-start(bf16[64,1280]{1,0:T(8,128)(2,1)S(1)} %collective-permute-done.2), channel_id=1, source_target_pairs={{0,2},{1,3},{2,0},{3,1},{4,6},{5,7},{6,4},{7,5},{8,10},{9,11},{10,... | collective-permute-start | bytes 491528 | tf_op jit(solution)/shard_map/ppermute | solution.py:77
  24.2 2.3 %collective-permute-done.3 = bf16[64,1280]{1,0:T(8,128)(2,1)S(1)} collective-permute-done((bf16[64,1280]{1,0:T(8,128)(2,1)S(1)}, bf16[64,1280]{1,0:T(8,128)(2,1)S(1)}, u32[]{:S(2)}, u32[]{:S(2)}) %collective-permute-start.3) | collective-permute-done | bytes 163872 | tf_op jit(solution)/shard_map/ppermute | solution.py:77
  26.5 2.5 %collective-permute-start.9 = (bf16[64,1280]{1,0:T(8,128)(2,1)S(1)}, bf16[64,1280]{1,0:T(8,128)(2,1)S(1)}, u32[]{:S(2)}, u32[]{:S(2)}) collective-permute-start(bf16[64,1280]{1,0:T(8,128)(2,1)S(1)} %collective-permute-done.8), channel_id=1, source_target_pairs={{0,2},{1,3},{2,0},{3,1},{4,6},{5,7},{6,4},{7,5},{8,10},{9,11},{10,... | collective-permute-start | bytes 491528 | tf_op jit(solution)/shard_map/ppermute | solution.py:77
  30.4 3.0 %collective-permute-done.9 = bf16[64,1280]{1,0:T(8,128)(2,1)S(1)} collective-permute-done((bf16[64,1280]{1,0:T(8,128)(2,1)S(1)}, bf16[64,1280]{1,0:T(8,128)(2,1)S(1)}, u32[]{:S(2)}, u32[]{:S(2)}) %collective-permute-start.9) | collective-permute-done | bytes 163872 | tf_op jit(solution)/shard_map/ppermute | solution.py:77
  36.4 1.6 %copy-done.3 = bf16[1024,1280]{1,0:T(8,128)(2,1)S(1)} copy-done((bf16[1024,1280]{1,0:T(8,128)(2,1)S(1)}, bf16[1024,1280]{1,0:T(8,128)(2,1)}, u32[]{:S(2)}) %copy-start.3) | copy-done | bytes 2621464
  38.2 2.2 %fusion.31 = (bf16[1024,768]{1,0:T(8,128)(2,1)S(1)}, f32[1024,768]{1,0:T(8,128)S(1)}) fusion(bf16[1024,1280]{1,0:T(8,128)(2,1)S(1)} %get-tuple-element.70, bf16[1280,768]{1,0:T(8,128)(2,1)S(1)} %maximum_maximum_fusion), kind=kOutput, calls=%fused_computation.115 | convolution fusion | flops 2014052352 | bytes 9306112 | tf_op jit(solution)/shard_map/dot_general | solution.py:148
  40.6 5.4 %collective-permute-start.14 = (bf16[256,768]{1,0:T(8,128)(2,1)S(1)}, bf16[256,768]{1,0:T(8,128)(2,1)S(1)}, u32[]{:S(2)}, u32[]{:S(2)}) collective-permute-start(bf16[256,768]{1,0:T(8,128)(2,1)S(1)} %get-tuple-element.45), channel_id=1, source_target_pairs={{0,16},{4,20},{8,24},{12,28},{16,0},{20,4},{24,8},{28,12},{1,17},{... | collective-permute-start | bytes 1179656 | tf_op jit(solution)/shard_map/ppermute | solution.py:69
  47.3 1.5 %collective-permute-start.15 = (bf16[64]{0:T(256)(128)(2,1)S(1)}, bf16[64]{0:T(256)(128)(2,1)S(1)}, u32[]{:S(2)}, u32[]{:S(2)}) collective-permute-start(bf16[64]{0:T(256)(128)(2,1)S(1)} %copy-done.5), channel_id=1, source_target_pairs={{0,2},{1,3},{2,0},{3,1},{4,6},{5,7},{6,4},{7,5},{8,10},{9,11},{10,... | collective-permute-start | bytes 392 | tf_op jit(solution)/shard_map/ppermute | solution.py:77
  48.8 2.0 %collective-permute-done.15 = bf16[64]{0:T(256)(128)(2,1)S(1)} collective-permute-done((bf16[64]{0:T(256)(128)(2,1)S(1)}, bf16[64]{0:T(256)(128)(2,1)S(1)}, u32[]{:S(2)}, u32[]{:S(2)}) %collective-permute-start.15) | collective-permute-done | bytes 160 | tf_op jit(solution)/shard_map/ppermute | solution.py:77
  52.2 20.5 %collective-permute-done.14 = bf16[256,768]{1,0:T(8,128)(2,1)S(1)} collective-permute-done((bf16[256,768]{1,0:T(8,128)(2,1)S(1)}, bf16[256,768]{1,0:T(8,128)(2,1)S(1)}, u32[]{:S(2)}, u32[]{:S(2)}) %collective-permute-start.14) | collective-permute-done | bytes 393248 | tf_op jit(solution)/shard_map/ppermute | solution.py:69
  72.9 1.8 %collective-permute-done.17.refs_0_ = bf16[256,768]{1,0:T(8,128)(2,1)S(1)} collective-permute-done((bf16[256,768]{1,0:T(8,128)(2,1)S(1)}, bf16[256,768]{1,0:T(8,128)(2,1)S(1)}, u32[]{:S(2)}, u32[]{:S(2)}) %collective-permute-start.17) | collective-permute-done | bytes 393248 | tf_op jit(solution)/shard_map/ppermute | solution.py:69
  74.7 1.5 %shard_map.102 = (bf16[256,384]{1,0:T(8,128)(2,1)}, bf16[256,768]{1,0:T(8,128)(2,1)S(1)}) custom-call(s32[4]{0:T(128)S(1)} %broadcast_xor_fusion.order_ref, f32[256,768]{1,0:T(8,128)S(1)} %fusion.8.pre_ref, bf16[256,1]{1,0:T(8,128)(2,1)S(1)} %broadcast_in_dim.10.prob_ref, bf16[256,384]{1,0:T(8,128)(2,1)S(1)} %copy-done, ...), custom_call_target="tpu_custom_call" | custom-call | flops 1966080 | bytes 2949120 | tf_op jit(solution)/shard_map/pallas_call | solution.py:49
  77.3 6.5 %collective-permute-start.20 = (bf16[256,768]{1,0:T(8,128)(2,1)S(1)}, bf16[256,768]{1,0:T(8,128)(2,1)S(1)}, u32[]{:S(2)}, u32[]{:S(2)}) collective-permute-start(bf16[256,768]{1,0:T(8,128)(2,1)S(1)} %get-tuple-element.26), channel_id=1, source_target_pairs={{0,16},{4,20},{16,24},{20,28},{24,8},{28,12},{8,0},{12,4},{1,17},{... | collective-permute-start | bytes 1179656 | tf_op jit(solution)/shard_map/ppermute | solution.py:108
  86.1 1.6 %collective-permute-start.19 = (bf16[64,1280]{1,0:T(8,128)(2,1)S(1)}, bf16[64,1280]{1,0:T(8,128)(2,1)S(1)}, u32[]{:S(2)}, u32[]{:S(2)}) collective-permute-start(bf16[64,1280]{1,0:T(8,128)(2,1)S(1)} %slice.283), channel_id=1, source_target_pairs={{0,2},{1,3},{2,0},{3,1},{4,6},{5,7},{6,4},{7,5},{8,10},{9,11},{10,... | collective-permute-start | bytes 491528 | tf_op jit(solution)/shard_map/ppermute | solution.py:77
  87.7 6.1 %collective-permute-done.20 = bf16[256,768]{1,0:T(8,128)(2,1)S(1)} collective-permute-done((bf16[256,768]{1,0:T(8,128)(2,1)S(1)}, bf16[256,768]{1,0:T(8,128)(2,1)S(1)}, u32[]{:S(2)}, u32[]{:S(2)}) %collective-permute-start.20) | collective-permute-done | bytes 393248 | tf_op jit(solution)/shard_map/ppermute | solution.py:108
  93.9 2.7 %collective-permute-start.23 = (bf16[256,768]{1,0:T(8,128)(2,1)S(1)}, bf16[256,768]{1,0:T(8,128)(2,1)S(1)}, u32[]{:S(2)}, u32[]{:S(2)}) collective-permute-start(bf16[256,768]{1,0:T(8,128)(2,1)S(1)} %broadcast_select_fusion.4), channel_id=1, source_target_pairs={{0,8},{4,12},{8,0},{12,4},{16,24},{20,28},{24,16},{28,20},{1,9},{5... | collective-permute-start | bytes 1179656 | tf_op jit(solution)/shard_map/ppermute | solution.py:108
  96.6 7.8 %collective-permute-done.21 = bf16[256,768]{1,0:T(8,128)(2,1)S(1)} collective-permute-done((bf16[256,768]{1,0:T(8,128)(2,1)S(1)}, bf16[256,768]{1,0:T(8,128)(2,1)S(1)}, u32[]{:S(2)}, u32[]{:S(2)}) %collective-permute-start.21) | collective-permute-done | bytes 393248 | tf_op jit(solution)/shard_map/ppermute | solution.py:108
  106.1 6.5 %collective-permute-done.23 = bf16[256,768]{1,0:T(8,128)(2,1)S(1)} collective-permute-done((bf16[256,768]{1,0:T(8,128)(2,1)S(1)}, bf16[256,768]{1,0:T(8,128)(2,1)S(1)}, u32[]{:S(2)}, u32[]{:S(2)}) %collective-permute-start.23) | collective-permute-done | bytes 393248 | tf_op jit(solution)/shard_map/ppermute | solution.py:108
  115.2 1.6 %collective-permute-start.28 = (bf16[64,1280]{1,0:T(8,128)(2,1)S(1)}, bf16[64,1280]{1,0:T(8,128)(2,1)S(1)}, u32[]{:S(2)}, u32[]{:S(2)}) collective-permute-start(bf16[64,1280]{1,0:T(8,128)(2,1)S(1)} %slice.280), channel_id=1, source_target_pairs={{0,2},{1,3},{2,0},{3,1},{4,6},{5,7},{6,4},{7,5},{8,10},{9,11},{10,... | collective-permute-start | bytes 491528 | tf_op jit(solution)/shard_map/ppermute | solution.py:77
  116.8 1.5 %collective-permute-start.31 = (bf16[640,768]{1,0:T(8,128)(2,1)S(1)}, bf16[640,768]{1,0:T(8,128)(2,1)S(1)}, u32[]{:S(2)}, u32[]{:S(2)}) collective-permute-start(bf16[640,768]{1,0:T(8,128)(2,1)S(1)} %add_convert_fusion), channel_id=1, source_target_pairs={{0,4},{4,0},{8,12},{12,8},{16,20},{20,16},{24,28},{28,24},{1,5},{5... | collective-permute-start | bytes 2949128 | tf_op jit(solution)/shard_map/ppermute | solution.py:73
  122.6 6.9 %collective-permute-done.25 = bf16[128,1280]{1,0:T(8,128)(2,1)S(1)} collective-permute-done((bf16[128,1280]{1,0:T(8,128)(2,1)S(1)}, bf16[128,1280]{1,0:T(8,128)(2,1)S(1)}, u32[]{:S(2)}, u32[]{:S(2)}) %collective-permute-start.25) | collective-permute-done | bytes 327712 | tf_op jit(solution)/shard_map/ppermute | solution.py:77
  130.4 1.8 %collective-permute-done.29 = bf16[64,1280]{1,0:T(8,128)(2,1)S(1)} collective-permute-done((bf16[64,1280]{1,0:T(8,128)(2,1)S(1)}, bf16[64,1280]{1,0:T(8,128)(2,1)S(1)}, u32[]{:S(2)}, u32[]{:S(2)}) %collective-permute-start.29) | collective-permute-done | bytes 163872 | tf_op jit(solution)/shard_map/ppermute | solution.py:69
  133.7 6.9 %collective-permute-done.31 = bf16[640,768]{1,0:T(8,128)(2,1)S(1)} collective-permute-done((bf16[640,768]{1,0:T(8,128)(2,1)S(1)}, bf16[640,768]{1,0:T(8,128)(2,1)S(1)}, u32[]{:S(2)}, u32[]{:S(2)}) %collective-permute-start.31) | collective-permute-done | bytes 983072 | tf_op jit(solution)/shard_map/ppermute | solution.py:73
  142.3 4.0 %convolution_convert_fusion = bf16[512,5120]{1,0:T(8,128)(2,1)} fusion(bf16[64,5120]{1,0:T(8,128)(2,1)S(1)} %slice_dynamic-update-slice_fusion.2, s32[64]{0:T(128)S(1)} %copy-done.4), kind=kOutput, calls=%fused_computation | convolution fusion | flops 338198528 | bytes 5898496 | tf_op jit(solution)/shard_map/dot_general | solution.py:231
  (121 shorter events, 25.8 us)
Async XLA Ops:
  4.5 18.8 %collective-permute-start.8 = (bf16[64,1280]{1,0:T(8,128)(2,1)S(1)}, bf16[64,1280]{1,0:T(8,128)(2,1)S(1)}, u32[]{:S(2)}, u32[]{:S(2)}) collective-permute-start(bf16[64,1280]{1,0:T(8,128)(2,1)S(1)} %pad_maximum_fusion.12), channel_id=1, source_target_pairs={{0,8},{4,12},{8,0},{12,4},{16,24},{20,28},{24,16},{28,20},{1,9},{5... | collective-permute-start | bytes 491528 | tf_op jit(solution)/shard_map/ppermute | solution.py:69
  7.6 15.7 %collective-permute-start.5 = (bf16[64,1280]{1,0:T(8,128)(2,1)S(1)}, bf16[64,1280]{1,0:T(8,128)(2,1)S(1)}, u32[]{:S(2)}, u32[]{:S(2)}) collective-permute-start(bf16[64,1280]{1,0:T(8,128)(2,1)S(1)} %pad_maximum_fusion.11), channel_id=1, source_target_pairs={{0,16},{4,20},{8,24},{12,28},{16,0},{20,4},{24,8},{28,12},{1,17},{... | collective-permute-start | bytes 491528 | tf_op jit(solution)/shard_map/ppermute | solution.py:69
  10.3 10.8 %collective-permute-start.2 = (bf16[64,1280]{1,0:T(8,128)(2,1)S(1)}, bf16[64,1280]{1,0:T(8,128)(2,1)S(1)}, u32[]{:S(2)}, u32[]{:S(2)}) collective-permute-start(bf16[64,1280]{1,0:T(8,128)(2,1)S(1)} %pad_maximum_fusion.10), channel_id=1, source_target_pairs={{0,24},{4,28},{8,16},{12,20},{16,8},{20,12},{24,0},{28,4},{1,25},{... | collective-permute-start | bytes 491528 | tf_op jit(solution)/shard_map/ppermute | solution.py:69
  11.0 5.4 %collective-permute-start = (bf16[64,1280]{1,0:T(8,128)(2,1)S(1)}, bf16[64,1280]{1,0:T(8,128)(2,1)S(1)}, u32[]{:S(2)}, u32[]{:S(2)}) collective-permute-start(bf16[64,1280]{1,0:T(8,128)(2,1)S(1)} %get-tuple-element.85), channel_id=1, source_target_pairs={{0,2},{1,3},{2,0},{3,1},{4,6},{5,7},{6,4},{7,5},{8,10},{9,11},{10,... | collective-permute-start | bytes 491528 | tf_op jit(solution)/shard_map/ppermute | solution.py:77
  12.8 23.5 %collective-permute-start.12 = (bf16[640,384]{1,0:T(8,128)(2,1)S(1)}, bf16[640,384]{1,0:T(8,128)(2,1)S(1)}, u32[]{:S(2)}, u32[]{:S(2)}) collective-permute-start(bf16[640,384]{1,0:T(8,128)(2,1)S(1)} %copy-done.1), channel_id=1, source_target_pairs={{0,4},{4,0},{8,12},{12,8},{16,20},{20,16},{24,28},{28,24},{1,5},{5... | collective-permute-start | bytes 1474568 | tf_op jit(solution)/shard_map/ppermute | solution.py:73
  16.4 19.8 %collective-permute-start.11 = (bf16[640,384]{1,0:T(8,128)(2,1)S(1)}, bf16[640,384]{1,0:T(8,128)(2,1)S(1)}, u32[]{:S(2)}, u32[]{:S(2)}) collective-permute-start(bf16[640,384]{1,0:T(8,128)(2,1)S(1)} %copy-done.2), channel_id=1, source_target_pairs={{0,4},{4,0},{8,12},{12,8},{16,20},{20,16},{24,28},{28,24},{1,5},{5... | collective-permute-start | bytes 1474568 | tf_op jit(solution)/shard_map/ppermute | solution.py:73
  21.1 5.4 %collective-permute-start.3 = (bf16[64,1280]{1,0:T(8,128)(2,1)S(1)}, bf16[64,1280]{1,0:T(8,128)(2,1)S(1)}, u32[]{:S(2)}, u32[]{:S(2)}) collective-permute-start(bf16[64,1280]{1,0:T(8,128)(2,1)S(1)} %collective-permute-done.2), channel_id=1, source_target_pairs={{0,2},{1,3},{2,0},{3,1},{4,6},{5,7},{6,4},{7,5},{8,10},{9,11},{10,... | collective-permute-start | bytes 491528 | tf_op jit(solution)/shard_map/ppermute | solution.py:77
  23.3 10.2 %collective-permute-start.1 = (bf16[128,1280]{1,0:T(8,128)(2,1)S(1)}, bf16[128,1280]{1,0:T(8,128)(2,1)S(1)}, u32[]{:S(2)}, u32[]{:S(2)}) collective-permute-start(bf16[128,1280]{1,0:T(8,128)(2,1)S(1)} %pad_maximum_fusion.5), channel_id=1, source_target_pairs={{0,1},{1,0},{2,3},{3,2},{4,5},{5,4},{6,7},{7,6},{8,9},{9,8},{10,11... | collective-permute-start | bytes 983048 | tf_op jit(solution)/shard_map/ppermute | solution.py:77
  23.3 7.1 %collective-permute-start.6 = (bf16[64,1280]{1,0:T(8,128)(2,1)S(1)}, bf16[64,1280]{1,0:T(8,128)(2,1)S(1)}, u32[]{:S(2)}, u32[]{:S(2)}) collective-permute-start(bf16[64,1280]{1,0:T(8,128)(2,1)S(1)} %collective-permute-done.5), channel_id=1, source_target_pairs={{0,2},{1,3},{2,0},{3,1},{4,6},{5,7},{6,4},{7,5},{8,10},{9,11},{10,... | collective-permute-start | bytes 491528 | tf_op jit(solution)/shard_map/ppermute | solution.py:77
  26.5 6.9 %collective-permute-start.9 = (bf16[64,1280]{1,0:T(8,128)(2,1)S(1)}, bf16[64,1280]{1,0:T(8,128)(2,1)S(1)}, u32[]{:S(2)}, u32[]{:S(2)}) collective-permute-start(bf16[64,1280]{1,0:T(8,128)(2,1)S(1)} %collective-permute-done.8), channel_id=1, source_target_pairs={{0,2},{1,3},{2,0},{3,1},{4,6},{5,7},{6,4},{7,5},{8,10},{9,11},{10,... | collective-permute-start | bytes 491528 | tf_op jit(solution)/shard_map/ppermute | solution.py:77
  30.4 6.0 %collective-permute-start.4 = (bf16[128,1280]{1,0:T(8,128)(2,1)S(1)}, bf16[128,1280]{1,0:T(8,128)(2,1)S(1)}, u32[]{:S(2)}, u32[]{:S(2)}) collective-permute-start(bf16[128,1280]{1,0:T(8,128)(2,1)S(1)} %pad_maximum_fusion.6), channel_id=1, source_target_pairs={{0,1},{1,0},{2,3},{3,2},{4,5},{5,4},{6,7},{7,6},{8,9},{9,8},{10,11... | collective-permute-start | bytes 983048 | tf_op jit(solution)/shard_map/ppermute | solution.py:77
  33.4 4.6 %collective-permute-start.7 = (bf16[128,1280]{1,0:T(8,128)(2,1)S(1)}, bf16[128,1280]{1,0:T(8,128)(2,1)S(1)}, u32[]{:S(2)}, u32[]{:S(2)}) collective-permute-start(bf16[128,1280]{1,0:T(8,128)(2,1)S(1)} %pad_maximum_fusion.7), channel_id=1, source_target_pairs={{0,1},{1,0},{2,3},{3,2},{4,5},{5,4},{6,7},{7,6},{8,9},{9,8},{10,11... | collective-permute-start | bytes 983048 | tf_op jit(solution)/shard_map/ppermute | solution.py:77
  33.5 4.7 %collective-permute-start.10 = (bf16[128,1280]{1,0:T(8,128)(2,1)S(1)}, bf16[128,1280]{1,0:T(8,128)(2,1)S(1)}, u32[]{:S(2)}, u32[]{:S(2)}) collective-permute-start(bf16[128,1280]{1,0:T(8,128)(2,1)S(1)} %pad_maximum_fusion.8), channel_id=1, source_target_pairs={{0,1},{1,0},{2,3},{3,2},{4,5},{5,4},{6,7},{7,6},{8,9},{9,8},{10,11... | collective-permute-start | bytes 983048 | tf_op jit(solution)/shard_map/ppermute | solution.py:77
  40.6 32.2 %collective-permute-start.14 = (bf16[256,768]{1,0:T(8,128)(2,1)S(1)}, bf16[256,768]{1,0:T(8,128)(2,1)S(1)}, u32[]{:S(2)}, u32[]{:S(2)}) collective-permute-start(bf16[256,768]{1,0:T(8,128)(2,1)S(1)} %get-tuple-element.45), channel_id=1, source_target_pairs={{0,16},{4,20},{8,24},{12,28},{16,0},{20,4},{24,8},{28,12},{1,17},{... | collective-permute-start | bytes 1179656 | tf_op jit(solution)/shard_map/ppermute | solution.py:69
  45.9 26.8 %collective-permute-start.13 = (bf16[256,768]{1,0:T(8,128)(2,1)S(1)}, bf16[256,768]{1,0:T(8,128)(2,1)S(1)}, u32[]{:S(2)}, u32[]{:S(2)}) collective-permute-start(bf16[256,768]{1,0:T(8,128)(2,1)S(1)} %get-tuple-element.46), channel_id=1, source_target_pairs={{0,24},{4,28},{8,16},{12,20},{16,8},{20,12},{24,0},{28,4},{1,25},{... | collective-permute-start | bytes 1179656 | tf_op jit(solution)/shard_map/ppermute | solution.py:69
  47.3 3.5 %collective-permute-start.15 = (bf16[64]{0:T(256)(128)(2,1)S(1)}, bf16[64]{0:T(256)(128)(2,1)S(1)}, u32[]{:S(2)}, u32[]{:S(2)}) collective-permute-start(bf16[64]{0:T(256)(128)(2,1)S(1)} %copy-done.5), channel_id=1, source_target_pairs={{0,2},{1,3},{2,0},{3,1},{4,6},{5,7},{6,4},{7,5},{8,10},{9,11},{10,... | collective-permute-start | bytes 392 | tf_op jit(solution)/shard_map/ppermute | solution.py:77
  48.8 25.9 %collective-permute-start.17 = (bf16[256,768]{1,0:T(8,128)(2,1)S(1)}, bf16[256,768]{1,0:T(8,128)(2,1)S(1)}, u32[]{:S(2)}, u32[]{:S(2)}) collective-permute-start(bf16[256,768]{1,0:T(8,128)(2,1)S(1)} %get-tuple-element.44), channel_id=1, source_target_pairs={{0,8},{4,12},{8,0},{12,4},{16,24},{20,28},{24,16},{28,20},{1,9},{5... | collective-permute-start | bytes 1179656 | tf_op jit(solution)/shard_map/ppermute | solution.py:69
  50.9 1.1 collective-permute-start.16
  76.9 9.1 %collective-permute-start.18 = (bf16[128,1280]{1,0:T(8,128)(2,1)S(1)}, bf16[128,1280]{1,0:T(8,128)(2,1)S(1)}, u32[]{:S(2)}, u32[]{:S(2)}) collective-permute-start(bf16[128,1280]{1,0:T(8,128)(2,1)S(1)} %slice.279), channel_id=1, source_target_pairs={{0,1},{1,0},{2,3},{3,2},{4,5},{5,4},{6,7},{7,6},{8,9},{9,8},{10,11... | collective-permute-start | bytes 983048 | tf_op jit(solution)/shard_map/ppermute | solution.py:77
  77.3 16.5 %collective-permute-start.20 = (bf16[256,768]{1,0:T(8,128)(2,1)S(1)}, bf16[256,768]{1,0:T(8,128)(2,1)S(1)}, u32[]{:S(2)}, u32[]{:S(2)}) collective-permute-start(bf16[256,768]{1,0:T(8,128)(2,1)S(1)} %get-tuple-element.26), channel_id=1, source_target_pairs={{0,16},{4,20},{16,24},{20,28},{24,8},{28,12},{8,0},{12,4},{1,17},{... | collective-permute-start | bytes 1179656 | tf_op jit(solution)/shard_map/ppermute | solution.py:108
  83.9 20.5 %collective-permute-start.21 = (bf16[256,768]{1,0:T(8,128)(2,1)S(1)}, bf16[256,768]{1,0:T(8,128)(2,1)S(1)}, u32[]{:S(2)}, u32[]{:S(2)}) collective-permute-start(bf16[256,768]{1,0:T(8,128)(2,1)S(1)} %get-tuple-element.26), channel_id=1, source_target_pairs={{16,0},{20,4},{8,24},{12,28},{17,1},{21,5},{9,25},{13,29},{18,2},{... | collective-permute-start | bytes 1179656 | tf_op jit(solution)/shard_map/ppermute | solution.py:108
  85.2 20.9 %collective-permute-start.22 = (bf16[256,768]{1,0:T(8,128)(2,1)S(1)}, bf16[256,768]{1,0:T(8,128)(2,1)S(1)}, u32[]{:S(2)}, u32[]{:S(2)}) collective-permute-start(bf16[256,768]{1,0:T(8,128)(2,1)S(1)} %get-tuple-element.26), channel_id=1, source_target_pairs={{8,16},{12,20},{16,8},{20,12},{9,17},{13,21},{17,9},{21,13},{10,18... | collective-permute-start | bytes 1179656 | tf_op jit(solution)/shard_map/ppermute | solution.py:108
  86.1 20.0 %collective-permute-start.19 = (bf16[64,1280]{1,0:T(8,128)(2,1)S(1)}, bf16[64,1280]{1,0:T(8,128)(2,1)S(1)}, u32[]{:S(2)}, u32[]{:S(2)}) collective-permute-start(bf16[64,1280]{1,0:T(8,128)(2,1)S(1)} %slice.283), channel_id=1, source_target_pairs={{0,2},{1,3},{2,0},{3,1},{4,6},{5,7},{6,4},{7,5},{8,10},{9,11},{10,... | collective-permute-start | bytes 491528 | tf_op jit(solution)/shard_map/ppermute | solution.py:77
  93.9 18.8 %collective-permute-start.23 = (bf16[256,768]{1,0:T(8,128)(2,1)S(1)}, bf16[256,768]{1,0:T(8,128)(2,1)S(1)}, u32[]{:S(2)}, u32[]{:S(2)}) collective-permute-start(bf16[256,768]{1,0:T(8,128)(2,1)S(1)} %broadcast_select_fusion.4), channel_id=1, source_target_pairs={{0,8},{4,12},{8,0},{12,4},{16,24},{20,28},{24,16},{28,20},{1,9},{5... | collective-permute-start | bytes 1179656 | tf_op jit(solution)/shard_map/ppermute | solution.py:108
  105.9 9.2 %collective-permute-start.27 = (bf16[128,1280]{1,0:T(8,128)(2,1)S(1)}, bf16[128,1280]{1,0:T(8,128)(2,1)S(1)}, u32[]{:S(2)}, u32[]{:S(2)}) collective-permute-start(bf16[128,1280]{1,0:T(8,128)(2,1)S(1)} %slice.276), channel_id=1, source_target_pairs={{0,1},{1,0},{2,3},{3,2},{4,5},{5,4},{6,7},{7,6},{8,9},{9,8},{10,11... | collective-permute-start | bytes 983048 | tf_op jit(solution)/shard_map/ppermute | solution.py:77
  115.0 4.6 %collective-permute-start.24 = (bf16[256,1280]{1,0:T(8,128)(2,1)S(1)}, bf16[256,1280]{1,0:T(8,128)(2,1)S(1)}, u32[]{:S(2)}, u32[]{:S(2)}) collective-permute-start(bf16[256,1280]{1,0:T(8,128)(2,1)S(1)} %pad_maximum_fusion.4), channel_id=1, source_target_pairs={{0,1},{1,0},{2,3},{3,2},{4,5},{5,4},{6,7},{7,6},{8,9},{9,8},{10,11... | collective-permute-start | bytes 1966088 | tf_op jit(solution)/shard_map/ppermute | solution.py:77
  115.2 6.7 %collective-permute-start.28 = (bf16[64,1280]{1,0:T(8,128)(2,1)S(1)}, bf16[64,1280]{1,0:T(8,128)(2,1)S(1)}, u32[]{:S(2)}, u32[]{:S(2)}) collective-permute-start(bf16[64,1280]{1,0:T(8,128)(2,1)S(1)} %slice.280), channel_id=1, source_target_pairs={{0,2},{1,3},{2,0},{3,1},{4,6},{5,7},{6,4},{7,5},{8,10},{9,11},{10,... | collective-permute-start | bytes 491528 | tf_op jit(solution)/shard_map/ppermute | solution.py:77
  116.8 23.9 %collective-permute-start.31 = (bf16[640,768]{1,0:T(8,128)(2,1)S(1)}, bf16[640,768]{1,0:T(8,128)(2,1)S(1)}, u32[]{:S(2)}, u32[]{:S(2)}) collective-permute-start(bf16[640,768]{1,0:T(8,128)(2,1)S(1)} %add_convert_fusion), channel_id=1, source_target_pairs={{0,4},{4,0},{8,12},{12,8},{16,20},{20,16},{24,28},{28,24},{1,5},{5... | collective-permute-start | bytes 2949128 | tf_op jit(solution)/shard_map/ppermute | solution.py:73
  119.9 9.6 %collective-permute-start.25 = (bf16[128,1280]{1,0:T(8,128)(2,1)S(1)}, bf16[128,1280]{1,0:T(8,128)(2,1)S(1)}, u32[]{:S(2)}, u32[]{:S(2)}) collective-permute-start(bf16[128,1280]{1,0:T(8,128)(2,1)S(1)} %pad_maximum_fusion.9), channel_id=1, source_target_pairs={{0,2},{1,3},{2,0},{3,1},{4,6},{5,7},{6,4},{7,5},{8,10},{9,11},{10,... | collective-permute-start | bytes 983048 | tf_op jit(solution)/shard_map/ppermute | solution.py:77
  121.9 10.4 %collective-permute-start.29 = (bf16[64,1280]{1,0:T(8,128)(2,1)S(1)}, bf16[64,1280]{1,0:T(8,128)(2,1)S(1)}, u32[]{:S(2)}, u32[]{:S(2)}) collective-permute-start(bf16[64,1280]{1,0:T(8,128)(2,1)S(1)} %fusion.16), channel_id=1, source_target_pairs={{0,16},{4,20},{8,24},{12,28},{16,0},{20,4},{24,8},{28,12},{1,17},{... | collective-permute-start | bytes 491528 | tf_op jit(solution)/shard_map/ppermute | solution.py:69
  129.7 12.5 %collective-permute-start.26 = (bf16[64,1280]{1,0:T(8,128)(2,1)S(1)}, bf16[64,1280]{1,0:T(8,128)(2,1)S(1)}, u32[]{:S(2)}, u32[]{:S(2)}) collective-permute-start(bf16[64,1280]{1,0:T(8,128)(2,1)S(1)} %broadcast_select_fusion.6), channel_id=1, source_target_pairs={{0,8},{4,12},{8,0},{12,4},{16,24},{20,28},{24,16},{28,20},{1,9},{5... | collective-permute-start | bytes 491528 | tf_op jit(solution)/shard_map/ppermute | solution.py:69
  132.3 10.0 %collective-permute-start.30 = (bf16[64,1280]{1,0:T(8,128)(2,1)S(1)}, bf16[64,1280]{1,0:T(8,128)(2,1)S(1)}, u32[]{:S(2)}, u32[]{:S(2)}) collective-permute-start(bf16[64,1280]{1,0:T(8,128)(2,1)S(1)} %get-tuple-element.40), channel_id=1, source_target_pairs={{0,24},{4,28},{8,16},{12,20},{16,8},{20,12},{24,0},{28,4},{1,25},{... | collective-permute-start | bytes 491528 | tf_op jit(solution)/shard_map/ppermute | solution.py:69
  (7 other events, 71.5 us)

commit v15 on v11

--- a/solution.py
+++ b/solution.py
@@ -128,7 +128,8 @@
             return jnp.where(at_end, first, second)
 
         weights = [jnp.concatenate([w_gate, w_up], axis=1)]
-        weights += [over_inner(weights[0], j) for j in range(1, inner)]
+        for j in range(1, inner):
+            weights.append(jnp.concatenate([over_inner(w_gate, j), over_inner(w_up, j)], axis=1))
         weights = jnp.concatenate(weights, axis=0)
 
         onehot = (slots[:, None] == jnp.arange(tok, dtype=slots.dtype)[None, :]).astype(BF16)

time: 145 us -> 133 us (0.917)
  matrix products: 25.5 us -> 15.8 us
  waiting for transfers between devices: 76.5 us -> 74.1 us
    ppermute x8, waiting for transfers between devices: 46.1 us -> 38.9 us  [outer_pairs(): return lax.ppermute(value, 'dp', pairs)]
    dot_general x4, matrix products: 7.56 us -> 2.74 us  [multiply(): return jnp.dot(x_chunks[k], weights, preferred_element_type=F32)]
    dot_general x4, matrix products: 7.64 us -> 2.84 us  [advance(): lax.dot_general(after(grads[k], last), weights, (((1,), (1,)), ((), ())),...]
    ppermute x16, waiting for transfers between devices: 16.5 us -> 19.8 us  [over_etp(): return lax.ppermute(value, 'etp', pairs)]
    ppermute x6, starting transfers between devices: 10.9 us -> 9.09 us  [over_outer(): return lax.ppermute(value, 'dp', pairs)]
    ppermute x2 -> x3, waiting for transfers between devices: 6.23 us -> 7.82 us  [over_inner(): return lax.ppermute(value, 'dp', pairs)]
    ppermute x8, starting transfers between devices: 11.2 us -> 12.7 us  [outer_pairs(): return lax.ppermute(value, 'dp', pairs)]
    ppermute x2 -> x3, starting transfers between devices: 3.05 us -> 3.59 us  [over_inner(): return lax.ppermute(value, 'dp', pairs)]
  transfers between devices with their start and end apart: 32 -> 33, of which waited for: 18 -> 18; matrix products, arithmetic and copies ran while one was open for 11% -> 9% of each run, Pallas kernels for 0% -> 0%
where the time goes in v15:
time: 133 us
  waiting for transfers between devices  74.1 us (56%)
  starting transfers between devices  36.4 us (27%)
  matrix products  15.8 us (12%)
  other arithmetic  3.17 us (2%)
  Pallas kernels  1.51 us (1%)
  between operations  1.38 us (1%)
    ppermute x8, waiting for transfers between devices, outer_pairs(): return lax.ppermute(value, 'dp', pairs)  38.9 us
    ppermute x16, waiting for transfers between devices, over_etp(): return lax.ppermute(value, 'etp', pairs)  19.8 us
    ppermute x8, starting transfers between devices, outer_pairs(): return lax.ppermute(value, 'dp', pairs)  12.7 us
    ppermute x16, starting transfers between devices, over_etp(): return lax.ppermute(value, 'etp', pairs)  11 us
    ppermute x6, starting transfers between devices, over_outer(): return lax.ppermute(value, 'dp', pairs)  9.09 us
    ppermute x3, waiting for transfers between devices, over_inner(): return lax.ppermute(value, 'dp', pairs)  7.82 us
    ppermute x6, waiting for transfers between devices, over_outer(): return lax.ppermute(value, 'dp', pairs)  7.57 us
    dot_general x1, matrix products, shards(): lax.dot_general(onehot, dx, (((0,), (0,)), ((), ())), preferred_element_t...  4 us
  transfers between devices with their start and end apart: 33, of which 18 were waited for; matrix products, arithmetic and copies ran while one was open for 9% of the time, Pallas kernels for 0%

profile of v15, /device:TPU:0, one launch (start us, length us, event | category | flops | bytes accessed | tf_op | source)
XLA Modules:
  0.0 133.3 jit_solution(13962347013897915973)
XLA Ops:
  0.7 3.6 %convolution_convert_fusion.1 = bf16[64,5120]{1,0:T(8,128)(2,1)S(1)} fusion(bf16[512,5120]{1,0:T(8,128)(2,1)} %param.7, s32[64]{0:T(128)} %param.8), kind=kOutput, calls=%fused_computation.1 | convolution fusion | flops 335904768 | bytes 5898496 | tf_op jit(solution)/shard_map/dot_general | solution.py:136
  4.5 5.1 %collective-permute-start.1 = (bf16[64,1280]{1,0:T(8,128)(2,1)S(1)}, bf16[64,1280]{1,0:T(8,128)(2,1)S(1)}, u32[]{:S(2)}, u32[]{:S(2)}) collective-permute-start(bf16[64,1280]{1,0:T(8,128)(2,1)S(1)} %pad_maximum_fusion.15), channel_id=1, source_target_pairs={{0,24},{4,28},{8,16},{12,20},{16,8},{20,12},{24,0},{28,4},{1,25},{... | collective-permute-start | bytes 491528 | tf_op jit(solution)/shard_map/ppermute | solution.py:69
  9.7 1.6 %collective-permute-start.7 = (bf16[640,384]{1,0:T(8,128)(2,1)S(1)}, bf16[640,384]{1,0:T(8,128)(2,1)S(1)}, u32[]{:S(2)}, u32[]{:S(2)}) collective-permute-start(bf16[640,384]{1,0:T(8,128)(2,1)S(1)} %copy-done.1), channel_id=1, source_target_pairs={{0,4},{4,0},{8,12},{12,8},{16,20},{20,16},{24,28},{28,24},{1,5},{5... | collective-permute-start | bytes 1474568 | tf_op jit(solution)/shard_map/ppermute | solution.py:73
  11.8 1.5 %collective-permute-start.16 = (bf16[64]{0:T(256)(128)(2,1)S(1)}, bf16[64]{0:T(256)(128)(2,1)S(1)}, u32[]{:S(2)}, u32[]{:S(2)}) collective-permute-start(bf16[64]{0:T(256)(128)(2,1)S(1)} %copy-done.4), channel_id=1, source_target_pairs={{0,2},{1,3},{2,0},{3,1},{4,6},{5,7},{6,4},{7,5},{8,10},{9,11},{10,... | collective-permute-start | bytes 392 | tf_op jit(solution)/shard_map/ppermute | solution.py:77
  13.4 2.0 %collective-permute-done.16 = bf16[64]{0:T(256)(128)(2,1)S(1)} collective-permute-done((bf16[64]{0:T(256)(128)(2,1)S(1)}, bf16[64]{0:T(256)(128)(2,1)S(1)}, u32[]{:S(2)}, u32[]{:S(2)}) %collective-permute-start.16) | collective-permute-done | bytes 160 | tf_op jit(solution)/shard_map/ppermute | solution.py:77
  16.0 2.6 %collective-permute-done = bf16[64,1280]{1,0:T(8,128)(2,1)S(1)} collective-permute-done((bf16[64,1280]{1,0:T(8,128)(2,1)S(1)}, bf16[64,1280]{1,0:T(8,128)(2,1)S(1)}, u32[]{:S(2)}, u32[]{:S(2)}) %collective-permute-start) | collective-permute-done | bytes 163872 | tf_op jit(solution)/shard_map/ppermute | solution.py:69
  18.6 1.6 %collective-permute-start.2 = (bf16[64,1280]{1,0:T(8,128)(2,1)S(1)}, bf16[64,1280]{1,0:T(8,128)(2,1)S(1)}, u32[]{:S(2)}, u32[]{:S(2)}) collective-permute-start(bf16[64,1280]{1,0:T(8,128)(2,1)S(1)} %get-tuple-element.79), channel_id=1, source_target_pairs={{0,2},{1,3},{2,0},{3,1},{4,6},{5,7},{6,4},{7,5},{8,10},{9,11},{10,... | collective-permute-start | bytes 491528 | tf_op jit(solution)/shard_map/ppermute | solution.py:77
  21.0 3.1 %collective-permute-done.10 = bf16[64,1280]{1,0:T(8,128)(2,1)S(1)} collective-permute-done((bf16[64,1280]{1,0:T(8,128)(2,1)S(1)}, bf16[64,1280]{1,0:T(8,128)(2,1)S(1)}, u32[]{:S(2)}, u32[]{:S(2)}) %collective-permute-start.10) | collective-permute-done | bytes 163872 | tf_op jit(solution)/shard_map/ppermute | solution.py:69
  24.1 1.5 %collective-permute-start.11 = (bf16[64,1280]{1,0:T(8,128)(2,1)S(1)}, bf16[64,1280]{1,0:T(8,128)(2,1)S(1)}, u32[]{:S(2)}, u32[]{:S(2)}) collective-permute-start(bf16[64,1280]{1,0:T(8,128)(2,1)S(1)} %collective-permute-done.10), channel_id=1, source_target_pairs={{0,2},{1,3},{2,0},{3,1},{4,6},{5,7},{6,4},{7,5},{8,10},{9,11},{10,... | collective-permute-start | bytes 491528 | tf_op jit(solution)/shard_map/ppermute | solution.py:77
  25.8 3.4 %collective-permute-done.4 = bf16[64,1280]{1,0:T(8,128)(2,1)S(1)} collective-permute-done((bf16[64,1280]{1,0:T(8,128)(2,1)S(1)}, bf16[64,1280]{1,0:T(8,128)(2,1)S(1)}, u32[]{:S(2)}, u32[]{:S(2)}) %collective-permute-start.4) | collective-permute-done | bytes 163872 | tf_op jit(solution)/shard_map/ppermute | solution.py:77
  29.3 2.5 %collective-permute-done.11 = bf16[64,1280]{1,0:T(8,128)(2,1)S(1)} collective-permute-done((bf16[64,1280]{1,0:T(8,128)(2,1)S(1)}, bf16[64,1280]{1,0:T(8,128)(2,1)S(1)}, u32[]{:S(2)}, u32[]{:S(2)}) %collective-permute-start.11) | collective-permute-done | bytes 163872 | tf_op jit(solution)/shard_map/ppermute | solution.py:77
  33.9 1.7 %collective-permute-start.13 = (bf16[256,768]{1,0:T(8,128)(2,1)S(1)}, bf16[256,768]{1,0:T(8,128)(2,1)S(1)}, u32[]{:S(2)}, u32[]{:S(2)}) collective-permute-start(bf16[256,768]{1,0:T(8,128)(2,1)S(1)} %convolution_convert_fusion.3), channel_id=1, source_target_pairs={{0,8},{4,12},{8,0},{12,4},{16,24},{20,28},{24,16},{28,20},{1,9},{5... | collective-permute-start | bytes 1179656 | tf_op jit(solution)/shard_map/ppermute | solution.py:108
  37.1 1.6 %collective-permute-start.8 = (bf16[64,1280]{1,0:T(8,128)(2,1)S(1)}, bf16[64,1280]{1,0:T(8,128)(2,1)S(1)}, u32[]{:S(2)}, u32[]{:S(2)}) collective-permute-start(bf16[64,1280]{1,0:T(8,128)(2,1)S(1)} %pad_maximum_fusion.13), channel_id=1, source_target_pairs={{0,2},{1,3},{2,0},{3,1},{4,6},{5,7},{6,4},{7,5},{8,10},{9,11},{10,... | collective-permute-start | bytes 491528 | tf_op jit(solution)/shard_map/ppermute | solution.py:77
  38.7 3.7 %collective-permute-done.8 = bf16[64,1280]{1,0:T(8,128)(2,1)S(1)} collective-permute-done((bf16[64,1280]{1,0:T(8,128)(2,1)S(1)}, bf16[64,1280]{1,0:T(8,128)(2,1)S(1)}, u32[]{:S(2)}, u32[]{:S(2)}) %collective-permute-start.8) | collective-permute-done | bytes 163872 | tf_op jit(solution)/shard_map/ppermute | solution.py:77
  44.4 6.0 %collective-permute-start.15 = (bf16[256,768]{1,0:T(8,128)(2,1)S(1)}, bf16[256,768]{1,0:T(8,128)(2,1)S(1)}, u32[]{:S(2)}, u32[]{:S(2)}) collective-permute-start(bf16[256,768]{1,0:T(8,128)(2,1)S(1)} %convert_element_type.88), channel_id=1, source_target_pairs={{0,16},{4,20},{24,8},{28,12},{1,17},{5,21},{25,9},{29,13},{2,18},{... | collective-permute-start | bytes 1179656 | tf_op jit(solution)/shard_map/ppermute | solution.py:108
  50.7 9.3 %collective-permute-done.15 = bf16[256,768]{1,0:T(8,128)(2,1)S(1)} collective-permute-done((bf16[256,768]{1,0:T(8,128)(2,1)S(1)}, bf16[256,768]{1,0:T(8,128)(2,1)S(1)}, u32[]{:S(2)}, u32[]{:S(2)}) %collective-permute-start.15) | collective-permute-done | bytes 393248 | tf_op jit(solution)/shard_map/ppermute | solution.py:108
  60.7 7.2 %collective-permute-done.18.refs_0_ = bf16[256,768]{1,0:T(8,128)(2,1)S(1)} collective-permute-done((bf16[256,768]{1,0:T(8,128)(2,1)S(1)}, bf16[256,768]{1,0:T(8,128)(2,1)S(1)}, u32[]{:S(2)}, u32[]{:S(2)}) %collective-permute-start.18) | collective-permute-done | bytes 393248 | tf_op jit(solution)/shard_map/ppermute | solution.py:108
  67.9 1.5 %shard_map.102 = (bf16[256,384]{1,0:T(8,128)(2,1)}, bf16[256,768]{1,0:T(8,128)(2,1)S(1)}) custom-call(s32[4]{0:T(128)S(1)} %broadcast_xor_fusion.order_ref, f32[256,768]{1,0:T(8,128)S(1)} %fusion.9.pre_ref, bf16[256,1]{1,0:T(8,128)(2,1)S(1)} %broadcast_in_dim.15.prob_ref, bf16[256,384]{1,0:T(8,128)(2,1)S(1)} %copy-done, ...), custom_call_target="tpu_custom_call" | custom-call | flops 1966080 | bytes 2949120 | tf_op jit(solution)/shard_map/pallas_call | solution.py:49
  73.3 1.6 %collective-permute-start.20 = (bf16[64,1280]{1,0:T(8,128)(2,1)S(1)}, bf16[64,1280]{1,0:T(8,128)(2,1)S(1)}, u32[]{:S(2)}, u32[]{:S(2)}) collective-permute-start(bf16[64,1280]{1,0:T(8,128)(2,1)S(1)} %slice.251), channel_id=1, source_target_pairs={{0,2},{1,3},{2,0},{3,1},{4,6},{5,7},{6,4},{7,5},{8,10},{9,11},{10,... | collective-permute-start | bytes 491528 | tf_op jit(solution)/shard_map/ppermute | solution.py:77
  74.9 7.1 %collective-permute-done.21 = bf16[256,768]{1,0:T(8,128)(2,1)S(1)} collective-permute-done((bf16[256,768]{1,0:T(8,128)(2,1)S(1)}, bf16[256,768]{1,0:T(8,128)(2,1)S(1)}, u32[]{:S(2)}, u32[]{:S(2)}) %collective-permute-start.21) | collective-permute-done | bytes 393248 | tf_op jit(solution)/shard_map/ppermute | solution.py:108
  82.1 1.4 %collective-permute-start.24 = (bf16[256,768]{1,0:T(8,128)(2,1)S(1)}, bf16[256,768]{1,0:T(8,128)(2,1)S(1)}, u32[]{:S(2)}, u32[]{:S(2)}) collective-permute-start(bf16[256,768]{1,0:T(8,128)(2,1)S(1)} %broadcast_select_fusion.2), channel_id=1, source_target_pairs={{0,8},{4,12},{8,0},{12,4},{16,24},{20,28},{24,16},{28,20},{1,9},{5... | collective-permute-start | bytes 1179656 | tf_op jit(solution)/shard_map/ppermute | solution.py:108
  83.5 7.8 %collective-permute-done.22 = bf16[256,768]{1,0:T(8,128)(2,1)S(1)} collective-permute-done((bf16[256,768]{1,0:T(8,128)(2,1)S(1)}, bf16[256,768]{1,0:T(8,128)(2,1)S(1)}, u32[]{:S(2)}, u32[]{:S(2)}) %collective-permute-start.22) | collective-permute-done | bytes 393248 | tf_op jit(solution)/shard_map/ppermute | solution.py:108
  93.0 6.5 %collective-permute-done.24 = bf16[256,768]{1,0:T(8,128)(2,1)S(1)} collective-permute-done((bf16[256,768]{1,0:T(8,128)(2,1)S(1)}, bf16[256,768]{1,0:T(8,128)(2,1)S(1)}, u32[]{:S(2)}, u32[]{:S(2)}) %collective-permute-start.24) | collective-permute-done | bytes 393248 | tf_op jit(solution)/shard_map/ppermute | solution.py:108
  102.1 1.6 %collective-permute-start.29 = (bf16[64,1280]{1,0:T(8,128)(2,1)S(1)}, bf16[64,1280]{1,0:T(8,128)(2,1)S(1)}, u32[]{:S(2)}, u32[]{:S(2)}) collective-permute-start(bf16[64,1280]{1,0:T(8,128)(2,1)S(1)} %slice.248), channel_id=1, source_target_pairs={{0,2},{1,3},{2,0},{3,1},{4,6},{5,7},{6,4},{7,5},{8,10},{9,11},{10,... | collective-permute-start | bytes 491528 | tf_op jit(solution)/shard_map/ppermute | solution.py:77
  103.7 1.5 %collective-permute-start.32 = (bf16[640,768]{1,0:T(8,128)(2,1)S(1)}, bf16[640,768]{1,0:T(8,128)(2,1)S(1)}, u32[]{:S(2)}, u32[]{:S(2)}) collective-permute-start(bf16[640,768]{1,0:T(8,128)(2,1)S(1)} %add_convert_fusion), channel_id=1, source_target_pairs={{0,4},{4,0},{8,12},{12,8},{16,20},{20,16},{24,28},{28,24},{1,5},{5... | collective-permute-start | bytes 2949128 | tf_op jit(solution)/shard_map/ppermute | solution.py:73
  107.4 1.4 %collective-permute-done.29 = bf16[64,1280]{1,0:T(8,128)(2,1)S(1)} collective-permute-done((bf16[64,1280]{1,0:T(8,128)(2,1)S(1)}, bf16[64,1280]{1,0:T(8,128)(2,1)S(1)}, u32[]{:S(2)}, u32[]{:S(2)}) %collective-permute-start.29) | collective-permute-done | bytes 163872 | tf_op jit(solution)/shard_map/ppermute | solution.py:77
  109.8 6.6 %collective-permute-done.26 = bf16[128,1280]{1,0:T(8,128)(2,1)S(1)} collective-permute-done((bf16[128,1280]{1,0:T(8,128)(2,1)S(1)}, bf16[128,1280]{1,0:T(8,128)(2,1)S(1)}, u32[]{:S(2)}, u32[]{:S(2)}) %collective-permute-start.26) | collective-permute-done | bytes 327712 | tf_op jit(solution)/shard_map/ppermute | solution.py:77
  117.4 1.8 %collective-permute-done.30 = bf16[64,1280]{1,0:T(8,128)(2,1)S(1)} collective-permute-done((bf16[64,1280]{1,0:T(8,128)(2,1)S(1)}, bf16[64,1280]{1,0:T(8,128)(2,1)S(1)}, u32[]{:S(2)}, u32[]{:S(2)}) %collective-permute-start.30) | collective-permute-done | bytes 163872 | tf_op jit(solution)/shard_map/ppermute | solution.py:69
  119.2 1.6 %collective-permute-start.31 = (bf16[64,1280]{1,0:T(8,128)(2,1)S(1)}, bf16[64,1280]{1,0:T(8,128)(2,1)S(1)}, u32[]{:S(2)}, u32[]{:S(2)}) collective-permute-start(bf16[64,1280]{1,0:T(8,128)(2,1)S(1)} %get-tuple-element.56), channel_id=1, source_target_pairs={{0,24},{4,28},{8,16},{12,20},{16,8},{20,12},{24,0},{28,4},{1,25},{... | collective-permute-start | bytes 491528 | tf_op jit(solution)/shard_map/ppermute | solution.py:69
  120.9 6.7 %collective-permute-done.32 = bf16[640,768]{1,0:T(8,128)(2,1)S(1)} collective-permute-done((bf16[640,768]{1,0:T(8,128)(2,1)S(1)}, bf16[640,768]{1,0:T(8,128)(2,1)S(1)}, u32[]{:S(2)}, u32[]{:S(2)}) %collective-permute-start.32) | collective-permute-done | bytes 983072 | tf_op jit(solution)/shard_map/ppermute | solution.py:73
  127.6 1.5 %slice_add_fusion = (f32[640,384]{1,0:T(8,128)}, f32[640,384]{1,0:T(8,128)}) fusion(f32[640,768]{1,0:T(8,128)S(1)} %fusion, bf16[640,768]{1,0:T(8,128)(2,1)S(1)} %collective-permute-done.32), kind=kLoop, calls=%fused_computation.18 | loop fusion | flops 983040 | bytes 4915200 | tf_op jit(solution)/shard_map/add | solution.py:238
  129.3 4.0 %convolution_convert_fusion = bf16[512,5120]{1,0:T(8,128)(2,1)} fusion(bf16[64,5120]{1,0:T(8,128)(2,1)S(1)} %slice_dynamic-update-slice_fusion.2, s32[64]{0:T(128)S(1)} %copy-done.3), kind=kOutput, calls=%fused_computation | convolution fusion | flops 338198528 | bytes 5898496 | tf_op jit(solution)/shard_map/dot_general | solution.py:251
  (117 shorter events, 21.3 us)
Async XLA Ops:
  4.5 11.4 %collective-permute-start.1 = (bf16[64,1280]{1,0:T(8,128)(2,1)S(1)}, bf16[64,1280]{1,0:T(8,128)(2,1)S(1)}, u32[]{:S(2)}, u32[]{:S(2)}) collective-permute-start(bf16[64,1280]{1,0:T(8,128)(2,1)S(1)} %pad_maximum_fusion.15), channel_id=1, source_target_pairs={{0,24},{4,28},{8,16},{12,20},{16,8},{20,12},{24,0},{28,4},{1,25},{... | collective-permute-start | bytes 491528 | tf_op jit(solution)/shard_map/ppermute | solution.py:69
  9.6 8.9 %collective-permute-start = (bf16[64,1280]{1,0:T(8,128)(2,1)S(1)}, bf16[64,1280]{1,0:T(8,128)(2,1)S(1)}, u32[]{:S(2)}, u32[]{:S(2)}) collective-permute-start(bf16[64,1280]{1,0:T(8,128)(2,1)S(1)} %pad_maximum_fusion.14), channel_id=1, source_target_pairs={{0,8},{4,12},{8,0},{12,4},{16,24},{20,28},{24,16},{28,20},{1,9},{5... | collective-permute-start | bytes 491528 | tf_op jit(solution)/shard_map/ppermute | solution.py:69
  9.7 22.1 %collective-permute-start.7 = (bf16[640,384]{1,0:T(8,128)(2,1)S(1)}, bf16[640,384]{1,0:T(8,128)(2,1)S(1)}, u32[]{:S(2)}, u32[]{:S(2)}) collective-permute-start(bf16[640,384]{1,0:T(8,128)(2,1)S(1)} %copy-done.1), channel_id=1, source_target_pairs={{0,4},{4,0},{8,12},{12,8},{16,20},{20,16},{24,28},{28,24},{1,5},{5... | collective-permute-start | bytes 1474568 | tf_op jit(solution)/shard_map/ppermute | solution.py:73
  11.3 21.7 %collective-permute-start.6 = (bf16[640,384]{1,0:T(8,128)(2,1)S(1)}, bf16[640,384]{1,0:T(8,128)(2,1)S(1)}, u32[]{:S(2)}, u32[]{:S(2)}) collective-permute-start(bf16[640,384]{1,0:T(8,128)(2,1)S(1)} %copy-done.2), channel_id=1, source_target_pairs={{0,4},{4,0},{8,12},{12,8},{16,20},{20,16},{24,28},{28,24},{1,5},{5... | collective-permute-start | bytes 1474568 | tf_op jit(solution)/shard_map/ppermute | solution.py:73
  11.8 3.5 %collective-permute-start.16 = (bf16[64]{0:T(256)(128)(2,1)S(1)}, bf16[64]{0:T(256)(128)(2,1)S(1)}, u32[]{:S(2)}, u32[]{:S(2)}) collective-permute-start(bf16[64]{0:T(256)(128)(2,1)S(1)} %copy-done.4), channel_id=1, source_target_pairs={{0,2},{1,3},{2,0},{3,1},{4,6},{5,7},{6,4},{7,5},{8,10},{9,11},{10,... | collective-permute-start | bytes 392 | tf_op jit(solution)/shard_map/ppermute | solution.py:77
  15.4 8.7 %collective-permute-start.10 = (bf16[64,1280]{1,0:T(8,128)(2,1)S(1)}, bf16[64,1280]{1,0:T(8,128)(2,1)S(1)}, u32[]{:S(2)}, u32[]{:S(2)}) collective-permute-start(bf16[64,1280]{1,0:T(8,128)(2,1)S(1)} %pad_maximum_fusion.16), channel_id=1, source_target_pairs={{0,16},{4,20},{8,24},{12,28},{16,0},{20,4},{24,8},{28,12},{1,17},{... | collective-permute-start | bytes 491528 | tf_op jit(solution)/shard_map/ppermute | solution.py:69
  15.9 4.3 %collective-permute-start.17 = (bf16[128]{0:T(256)(128)(2,1)S(1)}, bf16[128]{0:T(256)(128)(2,1)S(1)}, u32[]{:S(2)}, u32[]{:S(2)}) collective-permute-start(bf16[128]{0:T(256)(128)(2,1)S(1)} %pad_maximum_fusion.17), channel_id=1, source_target_pairs={{0,1},{1,0},{2,3},{3,2},{4,5},{5,4},{6,7},{7,6},{8,9},{9,8},{10,11... | collective-permute-start | bytes 776 | tf_op jit(solution)/shard_map/ppermute | solution.py:77
  18.6 7.1 %collective-permute-start.2 = (bf16[64,1280]{1,0:T(8,128)(2,1)S(1)}, bf16[64,1280]{1,0:T(8,128)(2,1)S(1)}, u32[]{:S(2)}, u32[]{:S(2)}) collective-permute-start(bf16[64,1280]{1,0:T(8,128)(2,1)S(1)} %get-tuple-element.79), channel_id=1, source_target_pairs={{0,2},{1,3},{2,0},{3,1},{4,6},{5,7},{6,4},{7,5},{8,10},{9,11},{10,... | collective-permute-start | bytes 491528 | tf_op jit(solution)/shard_map/ppermute | solution.py:77
  20.4 8.9 %collective-permute-start.4 = (bf16[64,1280]{1,0:T(8,128)(2,1)S(1)}, bf16[64,1280]{1,0:T(8,128)(2,1)S(1)}, u32[]{:S(2)}, u32[]{:S(2)}) collective-permute-start(bf16[64,1280]{1,0:T(8,128)(2,1)S(1)} %get-tuple-element.78), channel_id=1, source_target_pairs={{0,2},{1,3},{2,0},{3,1},{4,6},{5,7},{6,4},{7,5},{8,10},{9,11},{10,... | collective-permute-start | bytes 491528 | tf_op jit(solution)/shard_map/ppermute | solution.py:77
  24.1 7.8 %collective-permute-start.11 = (bf16[64,1280]{1,0:T(8,128)(2,1)S(1)}, bf16[64,1280]{1,0:T(8,128)(2,1)S(1)}, u32[]{:S(2)}, u32[]{:S(2)}) collective-permute-start(bf16[64,1280]{1,0:T(8,128)(2,1)S(1)} %collective-permute-done.10), channel_id=1, source_target_pairs={{0,2},{1,3},{2,0},{3,1},{4,6},{5,7},{6,4},{7,5},{8,10},{9,11},{10,... | collective-permute-start | bytes 491528 | tf_op jit(solution)/shard_map/ppermute | solution.py:77
  25.8 9.9 %collective-permute-start.3 = (bf16[128,1280]{1,0:T(8,128)(2,1)S(1)}, bf16[128,1280]{1,0:T(8,128)(2,1)S(1)}, u32[]{:S(2)}, u32[]{:S(2)}) collective-permute-start(bf16[128,1280]{1,0:T(8,128)(2,1)S(1)} %pad_maximum_fusion.8), channel_id=1, source_target_pairs={{0,1},{1,0},{2,3},{3,2},{4,5},{5,4},{6,7},{7,6},{8,9},{9,8},{10,11... | collective-permute-start | bytes 983048 | tf_op jit(solution)/shard_map/ppermute | solution.py:77
  29.3 3.9 %collective-permute-start.5 = (bf16[128,1280]{1,0:T(8,128)(2,1)S(1)}, bf16[128,1280]{1,0:T(8,128)(2,1)S(1)}, u32[]{:S(2)}, u32[]{:S(2)}) collective-permute-start(bf16[128,1280]{1,0:T(8,128)(2,1)S(1)} %pad_maximum_fusion.9), channel_id=1, source_target_pairs={{0,1},{1,0},{2,3},{3,2},{4,5},{5,4},{6,7},{7,6},{8,9},{9,8},{10,11... | collective-permute-start | bytes 983048 | tf_op jit(solution)/shard_map/ppermute | solution.py:77
  33.9 9.7 %collective-permute-start.13 = (bf16[256,768]{1,0:T(8,128)(2,1)S(1)}, bf16[256,768]{1,0:T(8,128)(2,1)S(1)}, u32[]{:S(2)}, u32[]{:S(2)}) collective-permute-start(bf16[256,768]{1,0:T(8,128)(2,1)S(1)} %convolution_convert_fusion.3), channel_id=1, source_target_pairs={{0,8},{4,12},{8,0},{12,4},{16,24},{20,28},{24,16},{28,20},{1,9},{5... | collective-permute-start | bytes 1179656 | tf_op jit(solution)/shard_map/ppermute | solution.py:108
  36.4 7.3 %collective-permute-start.14 = (bf16[256,768]{1,0:T(8,128)(2,1)S(1)}, bf16[256,768]{1,0:T(8,128)(2,1)S(1)}, u32[]{:S(2)}, u32[]{:S(2)}) collective-permute-start(bf16[256,768]{1,0:T(8,128)(2,1)S(1)} %convolution_convert_fusion.2), channel_id=1, source_target_pairs={{8,16},{12,20},{16,8},{20,12},{9,17},{13,21},{17,9},{21,13},{10,18... | collective-permute-start | bytes 1179656 | tf_op jit(solution)/shard_map/ppermute | solution.py:108
  37.1 5.4 %collective-permute-start.8 = (bf16[64,1280]{1,0:T(8,128)(2,1)S(1)}, bf16[64,1280]{1,0:T(8,128)(2,1)S(1)}, u32[]{:S(2)}, u32[]{:S(2)}) collective-permute-start(bf16[64,1280]{1,0:T(8,128)(2,1)S(1)} %pad_maximum_fusion.13), channel_id=1, source_target_pairs={{0,2},{1,3},{2,0},{3,1},{4,6},{5,7},{6,4},{7,5},{8,10},{9,11},{10,... | collective-permute-start | bytes 491528 | tf_op jit(solution)/shard_map/ppermute | solution.py:77
  38.6 3.9 %collective-permute-start.12 = (bf16[128,1280]{1,0:T(8,128)(2,1)S(1)}, bf16[128,1280]{1,0:T(8,128)(2,1)S(1)}, u32[]{:S(2)}, u32[]{:S(2)}) collective-permute-start(bf16[128,1280]{1,0:T(8,128)(2,1)S(1)} %pad_maximum_fusion.11), channel_id=1, source_target_pairs={{0,1},{1,0},{2,3},{3,2},{4,5},{5,4},{6,7},{7,6},{8,9},{9,8},{10,11... | collective-permute-start | bytes 983048 | tf_op jit(solution)/shard_map/ppermute | solution.py:77
  42.5 8.1 %collective-permute-start.9 = (bf16[128,1280]{1,0:T(8,128)(2,1)S(1)}, bf16[128,1280]{1,0:T(8,128)(2,1)S(1)}, u32[]{:S(2)}, u32[]{:S(2)}) collective-permute-start(bf16[128,1280]{1,0:T(8,128)(2,1)S(1)} %pad_maximum_fusion.10), channel_id=1, source_target_pairs={{0,1},{1,0},{2,3},{3,2},{4,5},{5,4},{6,7},{7,6},{8,9},{9,8},{10,11... | collective-permute-start | bytes 983048 | tf_op jit(solution)/shard_map/ppermute | solution.py:77
  44.4 15.6 %collective-permute-start.15 = (bf16[256,768]{1,0:T(8,128)(2,1)S(1)}, bf16[256,768]{1,0:T(8,128)(2,1)S(1)}, u32[]{:S(2)}, u32[]{:S(2)}) collective-permute-start(bf16[256,768]{1,0:T(8,128)(2,1)S(1)} %convert_element_type.88), channel_id=1, source_target_pairs={{0,16},{4,20},{24,8},{28,12},{1,17},{5,21},{25,9},{29,13},{2,18},{... | collective-permute-start | bytes 1179656 | tf_op jit(solution)/shard_map/ppermute | solution.py:108
  50.5 17.3 %collective-permute-start.18 = (bf16[256,768]{1,0:T(8,128)(2,1)S(1)}, bf16[256,768]{1,0:T(8,128)(2,1)S(1)}, u32[]{:S(2)}, u32[]{:S(2)}) collective-permute-start(bf16[256,768]{1,0:T(8,128)(2,1)S(1)} %fusion.18), channel_id=1, source_target_pairs={{16,0},{20,4},{24,16},{28,20},{8,24},{12,28},{0,8},{4,12},{17,1},{... | collective-permute-start | bytes 1179656 | tf_op jit(solution)/shard_map/ppermute | solution.py:108
  70.4 11.7 %collective-permute-start.21 = (bf16[256,768]{1,0:T(8,128)(2,1)S(1)}, bf16[256,768]{1,0:T(8,128)(2,1)S(1)}, u32[]{:S(2)}, u32[]{:S(2)}) collective-permute-start(bf16[256,768]{1,0:T(8,128)(2,1)S(1)} %get-tuple-element.42), channel_id=1, source_target_pairs={{0,16},{4,20},{16,24},{20,28},{24,8},{28,12},{8,0},{12,4},{1,17},{... | collective-permute-start | bytes 1179656 | tf_op jit(solution)/shard_map/ppermute | solution.py:108
  71.1 20.2 %collective-permute-start.22 = (bf16[256,768]{1,0:T(8,128)(2,1)S(1)}, bf16[256,768]{1,0:T(8,128)(2,1)S(1)}, u32[]{:S(2)}, u32[]{:S(2)}) collective-permute-start(bf16[256,768]{1,0:T(8,128)(2,1)S(1)} %get-tuple-element.42), channel_id=1, source_target_pairs={{16,0},{20,4},{8,24},{12,28},{17,1},{21,5},{9,25},{13,29},{18,2},{... | collective-permute-start | bytes 1179656 | tf_op jit(solution)/shard_map/ppermute | solution.py:108
  72.3 20.6 %collective-permute-start.23 = (bf16[256,768]{1,0:T(8,128)(2,1)S(1)}, bf16[256,768]{1,0:T(8,128)(2,1)S(1)}, u32[]{:S(2)}, u32[]{:S(2)}) collective-permute-start(bf16[256,768]{1,0:T(8,128)(2,1)S(1)} %get-tuple-element.42), channel_id=1, source_target_pairs={{8,16},{12,20},{16,8},{20,12},{9,17},{13,21},{17,9},{21,13},{10,18... | collective-permute-start | bytes 1179656 | tf_op jit(solution)/shard_map/ppermute | solution.py:108
  73.3 19.7 %collective-permute-start.20 = (bf16[64,1280]{1,0:T(8,128)(2,1)S(1)}, bf16[64,1280]{1,0:T(8,128)(2,1)S(1)}, u32[]{:S(2)}, u32[]{:S(2)}) collective-permute-start(bf16[64,1280]{1,0:T(8,128)(2,1)S(1)} %slice.251), channel_id=1, source_target_pairs={{0,2},{1,3},{2,0},{3,1},{4,6},{5,7},{6,4},{7,5},{8,10},{9,11},{10,... | collective-permute-start | bytes 491528 | tf_op jit(solution)/shard_map/ppermute | solution.py:77
  82.1 17.5 %collective-permute-start.24 = (bf16[256,768]{1,0:T(8,128)(2,1)S(1)}, bf16[256,768]{1,0:T(8,128)(2,1)S(1)}, u32[]{:S(2)}, u32[]{:S(2)}) collective-permute-start(bf16[256,768]{1,0:T(8,128)(2,1)S(1)} %broadcast_select_fusion.2), channel_id=1, source_target_pairs={{0,8},{4,12},{8,0},{12,4},{16,24},{20,28},{24,16},{28,20},{1,9},{5... | collective-permute-start | bytes 1179656 | tf_op jit(solution)/shard_map/ppermute | solution.py:108
  92.8 9.2 %collective-permute-start.28 = (bf16[128,1280]{1,0:T(8,128)(2,1)S(1)}, bf16[128,1280]{1,0:T(8,128)(2,1)S(1)}, u32[]{:S(2)}, u32[]{:S(2)}) collective-permute-start(bf16[128,1280]{1,0:T(8,128)(2,1)S(1)} %slice.244), channel_id=1, source_target_pairs={{0,1},{1,0},{2,3},{3,2},{4,5},{5,4},{6,7},{7,6},{8,9},{9,8},{10,11... | collective-permute-start | bytes 983048 | tf_op jit(solution)/shard_map/ppermute | solution.py:77
  102.0 4.6 %collective-permute-start.25 = (bf16[256,1280]{1,0:T(8,128)(2,1)S(1)}, bf16[256,1280]{1,0:T(8,128)(2,1)S(1)}, u32[]{:S(2)}, u32[]{:S(2)}) collective-permute-start(bf16[256,1280]{1,0:T(8,128)(2,1)S(1)} %pad_maximum_fusion.7), channel_id=1, source_target_pairs={{0,1},{1,0},{2,3},{3,2},{4,5},{5,4},{6,7},{7,6},{8,9},{9,8},{10,11... | collective-permute-start | bytes 1966088 | tf_op jit(solution)/shard_map/ppermute | solution.py:77
  102.1 6.7 %collective-permute-start.29 = (bf16[64,1280]{1,0:T(8,128)(2,1)S(1)}, bf16[64,1280]{1,0:T(8,128)(2,1)S(1)}, u32[]{:S(2)}, u32[]{:S(2)}) collective-permute-start(bf16[64,1280]{1,0:T(8,128)(2,1)S(1)} %slice.248), channel_id=1, source_target_pairs={{0,2},{1,3},{2,0},{3,1},{4,6},{5,7},{6,4},{7,5},{8,10},{9,11},{10,... | collective-permute-start | bytes 491528 | tf_op jit(solution)/shard_map/ppermute | solution.py:77
  103.7 23.9 %collective-permute-start.32 = (bf16[640,768]{1,0:T(8,128)(2,1)S(1)}, bf16[640,768]{1,0:T(8,128)(2,1)S(1)}, u32[]{:S(2)}, u32[]{:S(2)}) collective-permute-start(bf16[640,768]{1,0:T(8,128)(2,1)S(1)} %add_convert_fusion), channel_id=1, source_target_pairs={{0,4},{4,0},{8,12},{12,8},{16,20},{20,16},{24,28},{28,24},{1,5},{5... | collective-permute-start | bytes 2949128 | tf_op jit(solution)/shard_map/ppermute | solution.py:73
  106.8 9.6 %collective-permute-start.26 = (bf16[128,1280]{1,0:T(8,128)(2,1)S(1)}, bf16[128,1280]{1,0:T(8,128)(2,1)S(1)}, u32[]{:S(2)}, u32[]{:S(2)}) collective-permute-start(bf16[128,1280]{1,0:T(8,128)(2,1)S(1)} %pad_maximum_fusion.12), channel_id=1, source_target_pairs={{0,2},{1,3},{2,0},{3,1},{4,6},{5,7},{6,4},{7,5},{8,10},{9,11},{10,... | collective-permute-start | bytes 983048 | tf_op jit(solution)/shard_map/ppermute | solution.py:77
  108.8 10.4 %collective-permute-start.30 = (bf16[64,1280]{1,0:T(8,128)(2,1)S(1)}, bf16[64,1280]{1,0:T(8,128)(2,1)S(1)}, u32[]{:S(2)}, u32[]{:S(2)}) collective-permute-start(bf16[64,1280]{1,0:T(8,128)(2,1)S(1)} %fusion.19), channel_id=1, source_target_pairs={{0,16},{4,20},{8,24},{12,28},{16,0},{20,4},{24,8},{28,12},{1,17},{... | collective-permute-start | bytes 491528 | tf_op jit(solution)/shard_map/ppermute | solution.py:69
  116.6 12.5 %collective-permute-start.27 = (bf16[64,1280]{1,0:T(8,128)(2,1)S(1)}, bf16[64,1280]{1,0:T(8,128)(2,1)S(1)}, u32[]{:S(2)}, u32[]{:S(2)}) collective-permute-start(bf16[64,1280]{1,0:T(8,128)(2,1)S(1)} %broadcast_select_fusion.4), channel_id=1, source_target_pairs={{0,8},{4,12},{8,0},{12,4},{16,24},{20,28},{24,16},{28,20},{1,9},{5... | collective-permute-start | bytes 491528 | tf_op jit(solution)/shard_map/ppermute | solution.py:69
  119.2 10.0 %collective-permute-start.31 = (bf16[64,1280]{1,0:T(8,128)(2,1)S(1)}, bf16[64,1280]{1,0:T(8,128)(2,1)S(1)}, u32[]{:S(2)}, u32[]{:S(2)}) collective-permute-start(bf16[64,1280]{1,0:T(8,128)(2,1)S(1)} %get-tuple-element.56), channel_id=1, source_target_pairs={{0,24},{4,28},{8,16},{12,20},{16,8},{20,12},{24,0},{28,4},{1,25},{... | collective-permute-start | bytes 491528 | tf_op jit(solution)/shard_map/ppermute | solution.py:69
  (7 other events, 64.5 us)

commit v16 on v15

--- a/solution.py
+++ b/solution.py
@@ -20,6 +20,18 @@
 
 def after(value, *others):
     return lax.optimization_barrier((value,) + others)[0]
+
+
+def behind(value, *others):
+    anywhere = pl.BlockSpec(memory_space=pl.ANY)
+    return pl.pallas_call(
+        lambda *refs: None,
+        out_shape=jax.ShapeDtypeStruct(value.shape, value.dtype),
+        in_specs=[anywhere] * (1 + len(others)),
+        out_specs=anywhere,
+        input_output_aliases={0: 0},
+        cost_estimate=pl.CostEstimate(flops=0, bytes_accessed=0, transcendentals=0),
+    )(value, *others)
 
 
 def gate_kernel(steps, order_ref, pre_ref, prob_ref, cot_ref, *refs):
@@ -90,11 +102,12 @@
             value = jnp.concatenate([value, over_etp(value, b)], axis=0)
         return value
 
-    def reduce_etp(*values):
+    def reduce_etp(values, last=()):
         for b in reversed(bits):
             half = values[0].shape[0] // 2
             leaving = [value[half:].astype(BF16) for value in values]
-            got = over_etp(jnp.concatenate(leaving, axis=0) if len(leaving) > 1 else leaving[0], b)
+            leaving = jnp.concatenate(leaving, axis=0) if len(leaving) > 1 else leaving[0]
+            got = over_etp(behind(leaving, *last) if last and b == bits[0] else leaving, b)
             values = [v[:half] + got[i * half : (i + 1) * half].astype(F32) for i, v in enumerate(values)]
         return [value.astype(BF16) for value in values]
 
@@ -153,14 +166,14 @@
             return jnp.dot(x_chunks[k], weights, preferred_element_type=F32)
 
         if relay:
+            x_chunks[1] = gather_etp(got[1])
             x_chunks[3] = gather_etp(got[3])
-            x_chunks[1] = gather_etp(got[1])
-            far = multiply(3).astype(BF16)
+            near = multiply(1).astype(BF16)
+            crossed = outer_pairs(near, middle)
+            far = after(multiply(3, near).astype(BF16), near)
             swapped = outer_pairs(far, swap)
-            near = after(multiply(1, far).astype(BF16), far)
-            crossed = outer_pairs(near, middle)
-            x_chunks[2] = gather_etp(got[2], [[], [near]])
-            x_chunks[0] = gather_etp(after(got[0], near))
+            x_chunks[2] = gather_etp(got[2], [[], [far]])
+            x_chunks[0] = gather_etp(after(got[0], far))
             two = after(multiply(2, swapped, crossed), swapped)
             inwards = outer_pairs(two.astype(BF16), inward)
             relayed = pick(near, (after(two, swapped) + swapped.astype(F32)).astype(BF16))
@@ -183,14 +196,14 @@
 
         grads, sums = {0: paired}, {}
 
-        def advance(ks, last):
+        def advance(ks, last, before=()):
             partials = [
                 lax.dot_general(
                     after(grads[k], last), weights, (((1,), (1,)), ((), ())), preferred_element_type=F32
                 )
                 for k in ks
             ]
-            sums.update(zip(ks, reduce_etp(*partials)))
+            sums.update(zip(ks, reduce_etp(partials, before)))
             return partials[-1]
 
         def weight_grad(ks, j, last):
@@ -230,7 +243,7 @@
         arriving = [over_inner(leaving[j - 1], j) for j in range(1, inner)]
         last = leaving[0] if inner > 1 else last
         if late:
-            last = advance(late, last)
+            last = advance(late, last, [sums[k] for k in early[1:]])
         total = weight_grad(sequence, 0, last)
         gate_total, up_total = total[:, :width], total[:, width:]
         for part in arriving:

time: 133 us -> 137 us (1.030)
  waiting for transfers between devices: 74.1 us -> 67.8 us
  starting transfers between devices: 36.4 us -> 39.4 us
  other arithmetic: 3.17 us -> 5.81 us
  matrix products: 15.8 us -> 18 us
  local copies, waits for them, and re-layouts: 0.9 us -> 2.48 us
    ppermute x16, waiting for transfers between devices: 19.8 us -> 12.9 us  [over_etp(): return lax.ppermute(value, 'etp', pairs)]
    ppermute x6, starting transfers between devices: 9.09 us -> 13.4 us  [over_outer(): return lax.ppermute(value, 'dp', pairs)]
    ppermute x8, starting transfers between devices: 12.7 us -> 10 us  [outer_pairs(): return lax.ppermute(value, 'dp', pairs)]
    dot_general x3, matrix products: 2.69 us -> 4.84 us  [weight_grad(): lax.dot_general(x_part, after(grad_part, last), (((0,), (0,)), ((), ())),...]
    slice x3, local copies, waits for them, and re-layouts: 0.23 us -> 1.81 us  [weight_grad(): x_chunks[k][:, j * depth:(j + 1) * depth]]
    ppermute x16, starting transfers between devices: 11 us -> 12.3 us  [over_etp(): return lax.ppermute(value, 'etp', pairs)]
  transfers between devices with their start and end apart: 33 -> 33, of which waited for: 18 -> 15; matrix products, arithmetic and copies ran while one was open for 9% -> 13% of each run, Pallas kernels for 0% -> 0%
where the time goes in v16:
time: 137 us; the launch traced here: 136 us
  waiting for transfers between devices  67.8 us (49%)
  starting transfers between devices  39.4 us (29%)
  matrix products  18 us (13%)
  other arithmetic  5.81 us (4%)
  local copies, waits for them, and re-layouts  2.48 us (2%)
  Pallas kernels  1.51 us (1%)
  between operations  1.37 us (1%)
    ppermute x8, waiting for transfers between devices, outer_pairs(): return lax.ppermute(value, 'dp', pairs)  39.5 us
    ppermute x6, starting transfers between devices, over_outer(): return lax.ppermute(value, 'dp', pairs)  13.4 us
    ppermute x16, waiting for transfers between devices, over_etp(): return lax.ppermute(value, 'etp', pairs)  12.9 us
    ppermute x16, starting transfers between devices, over_etp(): return lax.ppermute(value, 'etp', pairs)  12.3 us
    ppermute x8, starting transfers between devices, outer_pairs(): return lax.ppermute(value, 'dp', pairs)  10 us
    ppermute x6, waiting for transfers between devices, over_outer(): return lax.ppermute(value, 'dp', pairs)  8.44 us
    ppermute x3, waiting for transfers between devices, over_inner(): return lax.ppermute(value, 'dp', pairs)  7.02 us
    dot_general x3, matrix products, weight_grad(): lax.dot_general(x_part, after(grad_part, last), (((0,), (0,)), ((), ())),...  4.84 us
  transfers between devices with their start and end apart: 33, of which 15 were waited for; matrix products, arithmetic and copies ran while one was open for 13% of the time, Pallas kernels for 0%

profile of v16, /device:TPU:0, one launch (start us, length us, event | category | flops | bytes accessed | tf_op | source)
XLA Modules:
  0.0 136.4 jit_solution(5698746825363224077)
XLA Ops:
  0.7 3.6 %convolution_convert_fusion.1 = bf16[64,5120]{1,0:T(8,128)(2,1)S(1)} fusion(bf16[512,5120]{1,0:T(8,128)(2,1)} %param.7, s32[64]{0:T(128)} %param.8), kind=kOutput, calls=%fused_computation.1 | convolution fusion | flops 335904768 | bytes 5898496 | tf_op jit(solution)/shard_map/dot_general | solution.py:149
  4.5 3.1 %collective-permute-start.1 = (bf16[64,1280]{1,0:T(8,128)(2,1)S(1)}, bf16[64,1280]{1,0:T(8,128)(2,1)S(1)}, u32[]{:S(2)}, u32[]{:S(2)}) collective-permute-start(bf16[64,1280]{1,0:T(8,128)(2,1)S(1)} %pad_maximum_fusion.15), channel_id=1, source_target_pairs={{0,8},{4,12},{8,0},{12,4},{16,24},{20,28},{24,16},{28,20},{1,9},{5... | collective-permute-start | bytes 491528 | tf_op jit(solution)/shard_map/ppermute | solution.py:81
  7.6 2.5 %collective-permute-start = (bf16[64,1280]{1,0:T(8,128)(2,1)S(1)}, bf16[64,1280]{1,0:T(8,128)(2,1)S(1)}, u32[]{:S(2)}, u32[]{:S(2)}) collective-permute-start(bf16[64,1280]{1,0:T(8,128)(2,1)S(1)} %pad_maximum_fusion.14), channel_id=1, source_target_pairs={{0,24},{4,28},{8,16},{12,20},{16,8},{20,12},{24,0},{28,4},{1,25},{... | collective-permute-start | bytes 491528 | tf_op jit(solution)/shard_map/ppermute | solution.py:81
  12.2 1.5 %collective-permute-start.16 = (bf16[64]{0:T(256)(128)(2,1)S(1)}, bf16[64]{0:T(256)(128)(2,1)S(1)}, u32[]{:S(2)}, u32[]{:S(2)}) collective-permute-start(bf16[64]{0:T(256)(128)(2,1)S(1)} %copy-done.5), channel_id=1, source_target_pairs={{0,2},{1,3},{2,0},{3,1},{4,6},{5,7},{6,4},{7,5},{8,10},{9,11},{10,... | collective-permute-start | bytes 392 | tf_op jit(solution)/shard_map/ppermute | solution.py:89
  13.7 2.0 %collective-permute-done.16 = bf16[64]{0:T(256)(128)(2,1)S(1)} collective-permute-done((bf16[64]{0:T(256)(128)(2,1)S(1)}, bf16[64]{0:T(256)(128)(2,1)S(1)}, u32[]{:S(2)}, u32[]{:S(2)}) %collective-permute-start.16) | collective-permute-done | bytes 160 | tf_op jit(solution)/shard_map/ppermute | solution.py:89
  16.0 1.8 %collective-permute-done = bf16[64,1280]{1,0:T(8,128)(2,1)S(1)} collective-permute-done((bf16[64,1280]{1,0:T(8,128)(2,1)S(1)}, bf16[64,1280]{1,0:T(8,128)(2,1)S(1)}, u32[]{:S(2)}, u32[]{:S(2)}) %collective-permute-start) | collective-permute-done | bytes 163872 | tf_op jit(solution)/shard_map/ppermute | solution.py:81
  17.9 1.6 %collective-permute-start.2 = (bf16[64,1280]{1,0:T(8,128)(2,1)S(1)}, bf16[64,1280]{1,0:T(8,128)(2,1)S(1)}, u32[]{:S(2)}, u32[]{:S(2)}) collective-permute-start(bf16[64,1280]{1,0:T(8,128)(2,1)S(1)} %get-tuple-element.79), channel_id=1, source_target_pairs={{0,2},{1,3},{2,0},{3,1},{4,6},{5,7},{6,4},{7,5},{8,10},{9,11},{10,... | collective-permute-start | bytes 491528 | tf_op jit(solution)/shard_map/ppermute | solution.py:89
  20.2 4.5 %collective-permute-done.10 = bf16[64,1280]{1,0:T(8,128)(2,1)S(1)} collective-permute-done((bf16[64,1280]{1,0:T(8,128)(2,1)S(1)}, bf16[64,1280]{1,0:T(8,128)(2,1)S(1)}, u32[]{:S(2)}, u32[]{:S(2)}) %collective-permute-start.10) | collective-permute-done | bytes 163872 | tf_op jit(solution)/shard_map/ppermute | solution.py:81
  24.7 1.5 %collective-permute-start.11 = (bf16[64,1280]{1,0:T(8,128)(2,1)S(1)}, bf16[64,1280]{1,0:T(8,128)(2,1)S(1)}, u32[]{:S(2)}, u32[]{:S(2)}) collective-permute-start(bf16[64,1280]{1,0:T(8,128)(2,1)S(1)} %collective-permute-done.10), channel_id=1, source_target_pairs={{0,2},{1,3},{2,0},{3,1},{4,6},{5,7},{6,4},{7,5},{8,10},{9,11},{10,... | collective-permute-start | bytes 491528 | tf_op jit(solution)/shard_map/ppermute | solution.py:89
  26.9 3.2 %collective-permute-done.11 = bf16[64,1280]{1,0:T(8,128)(2,1)S(1)} collective-permute-done((bf16[64,1280]{1,0:T(8,128)(2,1)S(1)}, bf16[64,1280]{1,0:T(8,128)(2,1)S(1)}, u32[]{:S(2)}, u32[]{:S(2)}) %collective-permute-start.11) | collective-permute-done | bytes 163872 | tf_op jit(solution)/shard_map/ppermute | solution.py:89
  30.2 2.9 %collective-permute-done.6 = bf16[640,384]{1,0:T(8,128)(2,1)S(1)} collective-permute-done((bf16[640,384]{1,0:T(8,128)(2,1)S(1)}, bf16[640,384]{1,0:T(8,128)(2,1)S(1)}, u32[]{:S(2)}, u32[]{:S(2)}) %collective-permute-start.6) | collective-permute-done | bytes 491552 | tf_op jit(solution)/shard_map/ppermute | solution.py:85
  35.4 2.3 %collective-permute-start.13 = (bf16[256,768]{1,0:T(8,128)(2,1)S(1)}, bf16[256,768]{1,0:T(8,128)(2,1)S(1)}, u32[]{:S(2)}, u32[]{:S(2)}) collective-permute-start(bf16[256,768]{1,0:T(8,128)(2,1)S(1)} %convolution_convert_fusion.2), channel_id=1, source_target_pairs={{0,8},{4,12},{8,0},{12,4},{16,24},{20,28},{24,16},{28,20},{1,9},{5... | collective-permute-start | bytes 1179656 | tf_op jit(solution)/shard_map/ppermute | solution.py:121
  39.3 3.7 %collective-permute-done.8 = bf16[64,1280]{1,0:T(8,128)(2,1)S(1)} collective-permute-done((bf16[64,1280]{1,0:T(8,128)(2,1)S(1)}, bf16[64,1280]{1,0:T(8,128)(2,1)S(1)}, u32[]{:S(2)}, u32[]{:S(2)}) %collective-permute-start.8) | collective-permute-done | bytes 163872 | tf_op jit(solution)/shard_map/ppermute | solution.py:89
  43.3 3.2 %collective-permute-done.13 = bf16[256,768]{1,0:T(8,128)(2,1)S(1)} collective-permute-done((bf16[256,768]{1,0:T(8,128)(2,1)S(1)}, bf16[256,768]{1,0:T(8,128)(2,1)S(1)}, u32[]{:S(2)}, u32[]{:S(2)}) %collective-permute-start.13) | collective-permute-done | bytes 393248 | tf_op jit(solution)/shard_map/ppermute | solution.py:121
  47.2 4.1 %collective-permute-start.15 = (bf16[256,768]{1,0:T(8,128)(2,1)S(1)}, bf16[256,768]{1,0:T(8,128)(2,1)S(1)}, u32[]{:S(2)}, u32[]{:S(2)}) collective-permute-start(bf16[256,768]{1,0:T(8,128)(2,1)S(1)} %convert_element_type.88), channel_id=1, source_target_pairs={{0,16},{4,20},{24,8},{28,12},{1,17},{5,21},{25,9},{29,13},{2,18},{... | collective-permute-start | bytes 1179656 | tf_op jit(solution)/shard_map/ppermute | solution.py:121
  51.6 9.3 %collective-permute-done.15 = bf16[256,768]{1,0:T(8,128)(2,1)S(1)} collective-permute-done((bf16[256,768]{1,0:T(8,128)(2,1)S(1)}, bf16[256,768]{1,0:T(8,128)(2,1)S(1)}, u32[]{:S(2)}, u32[]{:S(2)}) %collective-permute-start.15) | collective-permute-done | bytes 393248 | tf_op jit(solution)/shard_map/ppermute | solution.py:121
  61.6 7.5 %collective-permute-done.18.refs_0_ = bf16[256,768]{1,0:T(8,128)(2,1)S(1)} collective-permute-done((bf16[256,768]{1,0:T(8,128)(2,1)S(1)}, bf16[256,768]{1,0:T(8,128)(2,1)S(1)}, u32[]{:S(2)}, u32[]{:S(2)}) %collective-permute-start.18) | collective-permute-done | bytes 393248 | tf_op jit(solution)/shard_map/ppermute | solution.py:121
  76.1 1.6 %collective-permute-start.20 = (bf16[64,1280]{1,0:T(8,128)(2,1)S(1)}, bf16[64,1280]{1,0:T(8,128)(2,1)S(1)}, u32[]{:S(2)}, u32[]{:S(2)}) collective-permute-start(bf16[64,1280]{1,0:T(8,128)(2,1)S(1)} %slice.251), channel_id=1, source_target_pairs={{0,2},{1,3},{2,0},{3,1},{4,6},{5,7},{6,4},{7,5},{8,10},{9,11},{10,... | collective-permute-start | bytes 491528 | tf_op jit(solution)/shard_map/ppermute | solution.py:89
  77.7 15.5 %collective-permute-done.21 = bf16[256,768]{1,0:T(8,128)(2,1)S(1)} collective-permute-done((bf16[256,768]{1,0:T(8,128)(2,1)S(1)}, bf16[256,768]{1,0:T(8,128)(2,1)S(1)}, u32[]{:S(2)}, u32[]{:S(2)}) %collective-permute-start.21) | collective-permute-done | bytes 393248 | tf_op jit(solution)/shard_map/ppermute | solution.py:121
  96.0 1.6 %collective-permute-start.27 = (bf16[64,1280]{1,0:T(8,128)(2,1)S(1)}, bf16[64,1280]{1,0:T(8,128)(2,1)S(1)}, u32[]{:S(2)}, u32[]{:S(2)}) collective-permute-start(bf16[64,1280]{1,0:T(8,128)(2,1)S(1)} %slice.248), channel_id=1, source_target_pairs={{0,2},{1,3},{2,0},{3,1},{4,6},{5,7},{6,4},{7,5},{8,10},{9,11},{10,... | collective-permute-start | bytes 491528 | tf_op jit(solution)/shard_map/ppermute | solution.py:89
  97.6 4.0 %collective-permute-done.24 = bf16[256,768]{1,0:T(8,128)(2,1)S(1)} collective-permute-done((bf16[256,768]{1,0:T(8,128)(2,1)S(1)}, bf16[256,768]{1,0:T(8,128)(2,1)S(1)}, u32[]{:S(2)}, u32[]{:S(2)}) %collective-permute-start.24) | collective-permute-done | bytes 393248 | tf_op jit(solution)/shard_map/ppermute | solution.py:121
  101.6 1.7 %add_convert_fusion = bf16[640,768]{1,0:T(8,128)(2,1)} fusion(f32[640,768]{1,0:T(8,128)S(1)} %fusion.11, bf16[512,768]{1,0:T(8,128)(2,1)S(1)} %pad_maximum_fusion.2, bf16[256,640]{1,0:T(8,128)(2,1)S(1)} %get-tuple-element.67, bf16[256,640]{1,0:T(8,128)(2,1)S(1)} %get-tuple-element.65), kind=kOutput, calls=%fused_computation.3 | convolution fusion | flops 505610240 | bytes 4390912 | tf_op jit(solution)/shard_map/dot_general | solution.py:212
  105.0 1.6 %collective-permute-start.32 = (bf16[640,768]{1,0:T(8,128)(2,1)}, bf16[640,768]{1,0:T(8,128)(2,1)}, u32[]{:S(2)}, u32[]{:S(2)}) collective-permute-start(bf16[640,768]{1,0:T(8,128)(2,1)} %add_convert_fusion), channel_id=1, source_target_pairs={{0,4},{4,0},{8,12},{12,8},{16,20},{20,16},{24,28},{28,24},{1,5},{5... | collective-permute-start | bytes 2949128 | tf_op jit(solution)/shard_map/ppermute | solution.py:85
  109.9 2.5 %fusion = f32[640,768]{1,0:T(8,128)S(1)} fusion(bf16[1024,768]{1,0:T(8,128)(2,1)S(1)} %pad_maximum_fusion, bf16[256,640]{1,0:T(8,128)(2,1)S(1)} %get-tuple-element.66, bf16[256,640]{1,0:T(8,128)(2,1)} %get-tuple-element.64, bf16[256,640]{1,0:T(8,128)(2,1)} %get-tuple-element.81, bf16[256,640]{1,0:T(8,128)(2,1)} %get-tuple-element.60), kind=kOutput, calls=%fused_computation.5 | convolution fusion | flops 1011875840 | bytes 4849664 | tf_op jit(solution)/shard_map/dot_general | solution.py:212
  112.3 2.9 %collective-permute-start.30 = (bf16[64,1280]{1,0:T(8,128)(2,1)S(1)}, bf16[64,1280]{1,0:T(8,128)(2,1)S(1)}, u32[]{:S(2)}, u32[]{:S(2)}) collective-permute-start(bf16[64,1280]{1,0:T(8,128)(2,1)S(1)} %copy-done.1), channel_id=1, source_target_pairs={{0,16},{4,20},{8,24},{12,28},{16,0},{20,4},{24,8},{28,12},{1,17},{... | collective-permute-start | bytes 491528 | tf_op jit(solution)/shard_map/ppermute | solution.py:81
  115.2 3.2 %collective-permute-done.28 = bf16[128,1280]{1,0:T(8,128)(2,1)S(1)} collective-permute-done((bf16[128,1280]{1,0:T(8,128)(2,1)}, bf16[128,1280]{1,0:T(8,128)(2,1)S(1)}, u32[]{:S(2)}, u32[]{:S(2)}) %collective-permute-start.28) | collective-permute-done | bytes 327712 | tf_op jit(solution)/shard_map/ppermute | solution.py:89
  118.5 2.3 %collective-permute-start.29 = (bf16[64,1280]{1,0:T(8,128)(2,1)S(1)}, bf16[64,1280]{1,0:T(8,128)(2,1)S(1)}, u32[]{:S(2)}, u32[]{:S(2)}) collective-permute-start(bf16[64,1280]{1,0:T(8,128)(2,1)S(1)} %broadcast_select_fusion.4), channel_id=1, source_target_pairs={{0,8},{4,12},{8,0},{12,4},{16,24},{20,28},{24,16},{28,20},{1,9},{5... | collective-permute-start | bytes 491528 | tf_op jit(solution)/shard_map/ppermute | solution.py:81
  120.8 2.1 %collective-permute-done.30 = bf16[64,1280]{1,0:T(8,128)(2,1)S(1)} collective-permute-done((bf16[64,1280]{1,0:T(8,128)(2,1)S(1)}, bf16[64,1280]{1,0:T(8,128)(2,1)S(1)}, u32[]{:S(2)}, u32[]{:S(2)}) %collective-permute-start.30) | collective-permute-done | bytes 163872 | tf_op jit(solution)/shard_map/ppermute | solution.py:81
  122.9 2.4 %collective-permute-start.31 = (bf16[64,1280]{1,0:T(8,128)(2,1)S(1)}, bf16[64,1280]{1,0:T(8,128)(2,1)S(1)}, u32[]{:S(2)}, u32[]{:S(2)}) collective-permute-start(bf16[64,1280]{1,0:T(8,128)(2,1)S(1)} %get-tuple-element.56), channel_id=1, source_target_pairs={{0,24},{4,28},{8,16},{12,20},{16,8},{20,12},{24,0},{28,4},{1,25},{... | collective-permute-start | bytes 491528 | tf_op jit(solution)/shard_map/ppermute | solution.py:81
  125.4 4.1 %collective-permute-done.32 = bf16[640,768]{1,0:T(8,128)(2,1)} collective-permute-done((bf16[640,768]{1,0:T(8,128)(2,1)}, bf16[640,768]{1,0:T(8,128)(2,1)}, u32[]{:S(2)}, u32[]{:S(2)}) %collective-permute-start.32) | collective-permute-done | bytes 983072 | tf_op jit(solution)/shard_map/ppermute | solution.py:85
  129.5 2.7 %slice_add_fusion = (f32[640,384]{1,0:T(8,128)}, f32[640,384]{1,0:T(8,128)}) fusion(f32[640,768]{1,0:T(8,128)S(1)} %fusion, bf16[640,768]{1,0:T(8,128)(2,1)} %collective-permute-done.32), kind=kLoop, calls=%fused_computation.18 | loop fusion | flops 983040 | bytes 4915200 | tf_op jit(solution)/shard_map/add | solution.py:251
  132.4 4.0 %convolution_convert_fusion = bf16[512,5120]{1,0:T(8,128)(2,1)} fusion(bf16[64,5120]{1,0:T(8,128)(2,1)S(1)} %slice_dynamic-update-slice_fusion.2, s32[64]{0:T(128)S(1)} %copy-done.4), kind=kOutput, calls=%fused_computation | convolution fusion | flops 338198528 | bytes 5898496 | tf_op jit(solution)/shard_map/dot_general | solution.py:264
  (120 shorter events, 24.7 us)
Async XLA Ops:
  4.5 11.5 %collective-permute-start.1 = (bf16[64,1280]{1,0:T(8,128)(2,1)S(1)}, bf16[64,1280]{1,0:T(8,128)(2,1)S(1)}, u32[]{:S(2)}, u32[]{:S(2)}) collective-permute-start(bf16[64,1280]{1,0:T(8,128)(2,1)S(1)} %pad_maximum_fusion.15), channel_id=1, source_target_pairs={{0,8},{4,12},{8,0},{12,4},{16,24},{20,28},{24,16},{28,20},{1,9},{5... | collective-permute-start | bytes 491528 | tf_op jit(solution)/shard_map/ppermute | solution.py:81
  7.6 10.3 %collective-permute-start = (bf16[64,1280]{1,0:T(8,128)(2,1)S(1)}, bf16[64,1280]{1,0:T(8,128)(2,1)S(1)}, u32[]{:S(2)}, u32[]{:S(2)}) collective-permute-start(bf16[64,1280]{1,0:T(8,128)(2,1)S(1)} %pad_maximum_fusion.14), channel_id=1, source_target_pairs={{0,24},{4,28},{8,16},{12,20},{16,8},{20,12},{24,0},{28,4},{1,25},{... | collective-permute-start | bytes 491528 | tf_op jit(solution)/shard_map/ppermute | solution.py:81
  10.1 20.0 %collective-permute-start.7 = (bf16[640,384]{1,0:T(8,128)(2,1)S(1)}, bf16[640,384]{1,0:T(8,128)(2,1)S(1)}, u32[]{:S(2)}, u32[]{:S(2)}) collective-permute-start(bf16[640,384]{1,0:T(8,128)(2,1)S(1)} %copy-done.2), channel_id=1, source_target_pairs={{0,4},{4,0},{8,12},{12,8},{16,20},{20,16},{24,28},{28,24},{1,5},{5... | collective-permute-start | bytes 1474568 | tf_op jit(solution)/shard_map/ppermute | solution.py:85
  11.6 21.4 %collective-permute-start.6 = (bf16[640,384]{1,0:T(8,128)(2,1)S(1)}, bf16[640,384]{1,0:T(8,128)(2,1)S(1)}, u32[]{:S(2)}, u32[]{:S(2)}) collective-permute-start(bf16[640,384]{1,0:T(8,128)(2,1)S(1)} %copy-done.3), channel_id=1, source_target_pairs={{0,4},{4,0},{8,12},{12,8},{16,20},{20,16},{24,28},{28,24},{1,5},{5... | collective-permute-start | bytes 1474568 | tf_op jit(solution)/shard_map/ppermute | solution.py:85
  12.2 3.5 %collective-permute-start.16 = (bf16[64]{0:T(256)(128)(2,1)S(1)}, bf16[64]{0:T(256)(128)(2,1)S(1)}, u32[]{:S(2)}, u32[]{:S(2)}) collective-permute-start(bf16[64]{0:T(256)(128)(2,1)S(1)} %copy-done.5), channel_id=1, source_target_pairs={{0,2},{1,3},{2,0},{3,1},{4,6},{5,7},{6,4},{7,5},{8,10},{9,11},{10,... | collective-permute-start | bytes 392 | tf_op jit(solution)/shard_map/ppermute | solution.py:89
  15.7 9.0 %collective-permute-start.10 = (bf16[64,1280]{1,0:T(8,128)(2,1)S(1)}, bf16[64,1280]{1,0:T(8,128)(2,1)S(1)}, u32[]{:S(2)}, u32[]{:S(2)}) collective-permute-start(bf16[64,1280]{1,0:T(8,128)(2,1)S(1)} %pad_maximum_fusion.16), channel_id=1, source_target_pairs={{0,16},{4,20},{8,24},{12,28},{16,0},{20,4},{24,8},{28,12},{1,17},{... | collective-permute-start | bytes 491528 | tf_op jit(solution)/shard_map/ppermute | solution.py:81
  16.0 3.5 %collective-permute-start.17 = (bf16[128]{0:T(256)(128)(2,1)S(1)}, bf16[128]{0:T(256)(128)(2,1)S(1)}, u32[]{:S(2)}, u32[]{:S(2)}) collective-permute-start(bf16[128]{0:T(256)(128)(2,1)S(1)} %pad_maximum_fusion.17), channel_id=1, source_target_pairs={{0,1},{1,0},{2,3},{3,2},{4,5},{5,4},{6,7},{7,6},{8,9},{9,8},{10,11... | collective-permute-start | bytes 776 | tf_op jit(solution)/shard_map/ppermute | solution.py:89
  17.9 8.3 %collective-permute-start.2 = (bf16[64,1280]{1,0:T(8,128)(2,1)S(1)}, bf16[64,1280]{1,0:T(8,128)(2,1)S(1)}, u32[]{:S(2)}, u32[]{:S(2)}) collective-permute-start(bf16[64,1280]{1,0:T(8,128)(2,1)S(1)} %get-tuple-element.79), channel_id=1, source_target_pairs={{0,2},{1,3},{2,0},{3,1},{4,6},{5,7},{6,4},{7,5},{8,10},{9,11},{10,... | collective-permute-start | bytes 491528 | tf_op jit(solution)/shard_map/ppermute | solution.py:89
  19.7 6.7 %collective-permute-start.4 = (bf16[64,1280]{1,0:T(8,128)(2,1)S(1)}, bf16[64,1280]{1,0:T(8,128)(2,1)S(1)}, u32[]{:S(2)}, u32[]{:S(2)}) collective-permute-start(bf16[64,1280]{1,0:T(8,128)(2,1)S(1)} %get-tuple-element.78), channel_id=1, source_target_pairs={{0,2},{1,3},{2,0},{3,1},{4,6},{5,7},{6,4},{7,5},{8,10},{9,11},{10,... | collective-permute-start | bytes 491528 | tf_op jit(solution)/shard_map/ppermute | solution.py:89
  24.7 5.4 %collective-permute-start.11 = (bf16[64,1280]{1,0:T(8,128)(2,1)S(1)}, bf16[64,1280]{1,0:T(8,128)(2,1)S(1)}, u32[]{:S(2)}, u32[]{:S(2)}) collective-permute-start(bf16[64,1280]{1,0:T(8,128)(2,1)S(1)} %collective-permute-done.10), channel_id=1, source_target_pairs={{0,2},{1,3},{2,0},{3,1},{4,6},{5,7},{6,4},{7,5},{8,10},{9,11},{10,... | collective-permute-start | bytes 491528 | tf_op jit(solution)/shard_map/ppermute | solution.py:89
  26.3 8.4 %collective-permute-start.3 = (bf16[128,1280]{1,0:T(8,128)(2,1)S(1)}, bf16[128,1280]{1,0:T(8,128)(2,1)S(1)}, u32[]{:S(2)}, u32[]{:S(2)}) collective-permute-start(bf16[128,1280]{1,0:T(8,128)(2,1)S(1)} %pad_maximum_fusion.8), channel_id=1, source_target_pairs={{0,1},{1,0},{2,3},{3,2},{4,5},{5,4},{6,7},{7,6},{8,9},{9,8},{10,11... | collective-permute-start | bytes 983048 | tf_op jit(solution)/shard_map/ppermute | solution.py:89
  26.4 6.9 %collective-permute-start.5 = (bf16[128,1280]{1,0:T(8,128)(2,1)S(1)}, bf16[128,1280]{1,0:T(8,128)(2,1)S(1)}, u32[]{:S(2)}, u32[]{:S(2)}) collective-permute-start(bf16[128,1280]{1,0:T(8,128)(2,1)S(1)} %pad_maximum_fusion.9), channel_id=1, source_target_pairs={{0,1},{1,0},{2,3},{3,2},{4,5},{5,4},{6,7},{7,6},{8,9},{9,8},{10,11... | collective-permute-start | bytes 983048 | tf_op jit(solution)/shard_map/ppermute | solution.py:89
  34.0 12.5 %collective-permute-start.14 = (bf16[256,768]{1,0:T(8,128)(2,1)S(1)}, bf16[256,768]{1,0:T(8,128)(2,1)S(1)}, u32[]{:S(2)}, u32[]{:S(2)}) collective-permute-start(bf16[256,768]{1,0:T(8,128)(2,1)S(1)} %convolution_convert_fusion.3), channel_id=1, source_target_pairs={{8,16},{12,20},{16,8},{20,12},{9,17},{13,21},{17,9},{21,13},{10,18... | collective-permute-start | bytes 1179656 | tf_op jit(solution)/shard_map/ppermute | solution.py:121
  35.4 11.0 %collective-permute-start.13 = (bf16[256,768]{1,0:T(8,128)(2,1)S(1)}, bf16[256,768]{1,0:T(8,128)(2,1)S(1)}, u32[]{:S(2)}, u32[]{:S(2)}) collective-permute-start(bf16[256,768]{1,0:T(8,128)(2,1)S(1)} %convolution_convert_fusion.2), channel_id=1, source_target_pairs={{0,8},{4,12},{8,0},{12,4},{16,24},{20,28},{24,16},{28,20},{1,9},{5... | collective-permute-start | bytes 1179656 | tf_op jit(solution)/shard_map/ppermute | solution.py:121
  37.8 5.3 %collective-permute-start.8 = (bf16[64,1280]{1,0:T(8,128)(2,1)S(1)}, bf16[64,1280]{1,0:T(8,128)(2,1)S(1)}, u32[]{:S(2)}, u32[]{:S(2)}) collective-permute-start(bf16[64,1280]{1,0:T(8,128)(2,1)S(1)} %pad_maximum_fusion.13), channel_id=1, source_target_pairs={{0,2},{1,3},{2,0},{3,1},{4,6},{5,7},{6,4},{7,5},{8,10},{9,11},{10,... | collective-permute-start | bytes 491528 | tf_op jit(solution)/shard_map/ppermute | solution.py:89
  39.3 3.9 %collective-permute-start.12 = (bf16[128,1280]{1,0:T(8,128)(2,1)S(1)}, bf16[128,1280]{1,0:T(8,128)(2,1)S(1)}, u32[]{:S(2)}, u32[]{:S(2)}) collective-permute-start(bf16[128,1280]{1,0:T(8,128)(2,1)S(1)} %pad_maximum_fusion.11), channel_id=1, source_target_pairs={{0,1},{1,0},{2,3},{3,2},{4,5},{5,4},{6,7},{7,6},{8,9},{9,8},{10,11... | collective-permute-start | bytes 983048 | tf_op jit(solution)/shard_map/ppermute | solution.py:89
  43.1 8.4 %collective-permute-start.9 = (bf16[128,1280]{1,0:T(8,128)(2,1)S(1)}, bf16[128,1280]{1,0:T(8,128)(2,1)S(1)}, u32[]{:S(2)}, u32[]{:S(2)}) collective-permute-start(bf16[128,1280]{1,0:T(8,128)(2,1)S(1)} %pad_maximum_fusion.10), channel_id=1, source_target_pairs={{0,1},{1,0},{2,3},{3,2},{4,5},{5,4},{6,7},{7,6},{8,9},{9,8},{10,11... | collective-permute-start | bytes 983048 | tf_op jit(solution)/shard_map/ppermute | solution.py:89
  47.2 13.7 %collective-permute-start.15 = (bf16[256,768]{1,0:T(8,128)(2,1)S(1)}, bf16[256,768]{1,0:T(8,128)(2,1)S(1)}, u32[]{:S(2)}, u32[]{:S(2)}) collective-permute-start(bf16[256,768]{1,0:T(8,128)(2,1)S(1)} %convert_element_type.88), channel_id=1, source_target_pairs={{0,16},{4,20},{24,8},{28,12},{1,17},{5,21},{25,9},{29,13},{2,18},{... | collective-permute-start | bytes 1179656 | tf_op jit(solution)/shard_map/ppermute | solution.py:121
  51.5 17.6 %collective-permute-start.18 = (bf16[256,768]{1,0:T(8,128)(2,1)S(1)}, bf16[256,768]{1,0:T(8,128)(2,1)S(1)}, u32[]{:S(2)}, u32[]{:S(2)}) collective-permute-start(bf16[256,768]{1,0:T(8,128)(2,1)S(1)} %fusion.18), channel_id=1, source_target_pairs={{16,0},{20,4},{24,16},{28,20},{8,24},{12,28},{0,8},{4,12},{17,1},{... | collective-permute-start | bytes 1179656 | tf_op jit(solution)/shard_map/ppermute | solution.py:121
  71.4 4.6 %collective-permute-start.19 = (bf16[128,1280]{1,0:T(8,128)(2,1)S(1)}, bf16[128,1280]{1,0:T(8,128)(2,1)S(1)}, u32[]{:S(2)}, u32[]{:S(2)}) collective-permute-start(bf16[128,1280]{1,0:T(8,128)(2,1)S(1)} %slice.247), channel_id=1, source_target_pairs={{0,1},{1,0},{2,3},{3,2},{4,5},{5,4},{6,7},{7,6},{8,9},{9,8},{10,11... | collective-permute-start | bytes 983048 | tf_op jit(solution)/shard_map/ppermute | solution.py:89
  73.2 19.9 %collective-permute-start.21 = (bf16[256,768]{1,0:T(8,128)(2,1)S(1)}, bf16[256,768]{1,0:T(8,128)(2,1)S(1)}, u32[]{:S(2)}, u32[]{:S(2)}) collective-permute-start(bf16[256,768]{1,0:T(8,128)(2,1)S(1)} %get-tuple-element.42), channel_id=1, source_target_pairs={{0,16},{4,20},{16,24},{20,28},{24,8},{28,12},{8,0},{12,4},{1,17},{... | collective-permute-start | bytes 1179656 | tf_op jit(solution)/shard_map/ppermute | solution.py:121
  73.8 19.5 %collective-permute-start.22 = (bf16[256,768]{1,0:T(8,128)(2,1)S(1)}, bf16[256,768]{1,0:T(8,128)(2,1)S(1)}, u32[]{:S(2)}, u32[]{:S(2)}) collective-permute-start(bf16[256,768]{1,0:T(8,128)(2,1)S(1)} %get-tuple-element.42), channel_id=1, source_target_pairs={{16,0},{20,4},{8,24},{12,28},{17,1},{21,5},{9,25},{13,29},{18,2},{... | collective-permute-start | bytes 1179656 | tf_op jit(solution)/shard_map/ppermute | solution.py:121
  75.1 19.9 %collective-permute-start.23 = (bf16[256,768]{1,0:T(8,128)(2,1)S(1)}, bf16[256,768]{1,0:T(8,128)(2,1)S(1)}, u32[]{:S(2)}, u32[]{:S(2)}) collective-permute-start(bf16[256,768]{1,0:T(8,128)(2,1)S(1)} %get-tuple-element.42), channel_id=1, source_target_pairs={{8,16},{12,20},{16,8},{20,12},{9,17},{13,21},{17,9},{21,13},{10,18... | collective-permute-start | bytes 1179656 | tf_op jit(solution)/shard_map/ppermute | solution.py:121
  76.1 28.9 %collective-permute-start.20 = (bf16[64,1280]{1,0:T(8,128)(2,1)S(1)}, bf16[64,1280]{1,0:T(8,128)(2,1)S(1)}, u32[]{:S(2)}, u32[]{:S(2)}) collective-permute-start(bf16[64,1280]{1,0:T(8,128)(2,1)S(1)} %slice.251), channel_id=1, source_target_pairs={{0,2},{1,3},{2,0},{3,1},{4,6},{5,7},{6,4},{7,5},{8,10},{9,11},{10,... | collective-permute-start | bytes 491528 | tf_op jit(solution)/shard_map/ppermute | solution.py:89
  93.2 8.4 %collective-permute-start.24 = (bf16[256,768]{1,0:T(8,128)(2,1)S(1)}, bf16[256,768]{1,0:T(8,128)(2,1)S(1)}, u32[]{:S(2)}, u32[]{:S(2)}) collective-permute-start(bf16[256,768]{1,0:T(8,128)(2,1)S(1)} %broadcast_select_fusion.2), channel_id=1, source_target_pairs={{0,8},{4,12},{8,0},{12,4},{16,24},{20,28},{24,16},{28,20},{1,9},{5... | collective-permute-start | bytes 1179656 | tf_op jit(solution)/shard_map/ppermute | solution.py:121
  96.0 10.7 %collective-permute-start.27 = (bf16[64,1280]{1,0:T(8,128)(2,1)S(1)}, bf16[64,1280]{1,0:T(8,128)(2,1)S(1)}, u32[]{:S(2)}, u32[]{:S(2)}) collective-permute-start(bf16[64,1280]{1,0:T(8,128)(2,1)S(1)} %slice.248), channel_id=1, source_target_pairs={{0,2},{1,3},{2,0},{3,1},{4,6},{5,7},{6,4},{7,5},{8,10},{9,11},{10,... | collective-permute-start | bytes 491528 | tf_op jit(solution)/shard_map/ppermute | solution.py:89
  104.9 2.5 %collective-permute-start.25 = (bf16[256,1280]{1,0:T(8,128)(2,1)S(1)}, bf16[256,1280]{1,0:T(8,128)(2,1)S(1)}, u32[]{:S(2)}, u32[]{:S(2)}) collective-permute-start(bf16[256,1280]{1,0:T(8,128)(2,1)S(1)} %pad_maximum_fusion.7), channel_id=1, source_target_pairs={{0,1},{1,0},{2,3},{3,2},{4,5},{5,4},{6,7},{7,6},{8,9},{9,8},{10,11... | collective-permute-start | bytes 1966088 | tf_op jit(solution)/shard_map/ppermute | solution.py:89
  105.0 24.5 %collective-permute-start.32 = (bf16[640,768]{1,0:T(8,128)(2,1)}, bf16[640,768]{1,0:T(8,128)(2,1)}, u32[]{:S(2)}, u32[]{:S(2)}) collective-permute-start(bf16[640,768]{1,0:T(8,128)(2,1)} %add_convert_fusion), channel_id=1, source_target_pairs={{0,4},{4,0},{8,12},{12,8},{16,20},{20,16},{24,28},{28,24},{1,5},{5... | collective-permute-start | bytes 2949128 | tf_op jit(solution)/shard_map/ppermute | solution.py:85
  108.3 10.0 %collective-permute-start.28 = (bf16[128,1280]{1,0:T(8,128)(2,1)}, bf16[128,1280]{1,0:T(8,128)(2,1)S(1)}, u32[]{:S(2)}, u32[]{:S(2)}) collective-permute-start(bf16[128,1280]{1,0:T(8,128)(2,1)} %shard_map.103), channel_id=1, source_target_pairs={{0,2},{1,3},{2,0},{3,1},{4,6},{5,7},{6,4},{7,5},{8,10},{9,11},{10,... | collective-permute-start | bytes 983048 | tf_op jit(solution)/shard_map/ppermute | solution.py:89
  112.3 10.6 %collective-permute-start.30 = (bf16[64,1280]{1,0:T(8,128)(2,1)S(1)}, bf16[64,1280]{1,0:T(8,128)(2,1)S(1)}, u32[]{:S(2)}, u32[]{:S(2)}) collective-permute-start(bf16[64,1280]{1,0:T(8,128)(2,1)S(1)} %copy-done.1), channel_id=1, source_target_pairs={{0,16},{4,20},{8,24},{12,28},{16,0},{20,4},{24,8},{28,12},{1,17},{... | collective-permute-start | bytes 491528 | tf_op jit(solution)/shard_map/ppermute | solution.py:81
  118.5 13.7 %collective-permute-start.29 = (bf16[64,1280]{1,0:T(8,128)(2,1)S(1)}, bf16[64,1280]{1,0:T(8,128)(2,1)S(1)}, u32[]{:S(2)}, u32[]{:S(2)}) collective-permute-start(bf16[64,1280]{1,0:T(8,128)(2,1)S(1)} %broadcast_select_fusion.4), channel_id=1, source_target_pairs={{0,8},{4,12},{8,0},{12,4},{16,24},{20,28},{24,16},{28,20},{1,9},{5... | collective-permute-start | bytes 491528 | tf_op jit(solution)/shard_map/ppermute | solution.py:81
  122.9 9.4 %collective-permute-start.31 = (bf16[64,1280]{1,0:T(8,128)(2,1)S(1)}, bf16[64,1280]{1,0:T(8,128)(2,1)S(1)}, u32[]{:S(2)}, u32[]{:S(2)}) collective-permute-start(bf16[64,1280]{1,0:T(8,128)(2,1)S(1)} %get-tuple-element.56), channel_id=1, source_target_pairs={{0,24},{4,28},{8,16},{12,20},{16,8},{20,12},{24,0},{28,4},{1,25},{... | collective-permute-start | bytes 491528 | tf_op jit(solution)/shard_map/ppermute | solution.py:81
  (8 other events, 64.9 us)

commit v17 on v15

--- a/solution.py
+++ b/solution.py
@@ -20,6 +20,18 @@
 
 def after(value, *others):
     return lax.optimization_barrier((value,) + others)[0]
+
+
+def behind(value, *others):
+    anywhere = pl.BlockSpec(memory_space=pl.ANY)
+    return pl.pallas_call(
+        lambda *refs: None,
+        out_shape=jax.ShapeDtypeStruct(value.shape, value.dtype),
+        in_specs=[anywhere] * (1 + len(others)),
+        out_specs=anywhere,
+        input_output_aliases={0: 0},
+        cost_estimate=pl.CostEstimate(flops=0, bytes_accessed=0, transcendentals=0),
+    )(value, *others)
 
 
 def gate_kernel(steps, order_ref, pre_ref, prob_ref, cot_ref, *refs):
@@ -84,10 +96,12 @@
         chunk_order = chunk_order + [c ^ bit for c in chunk_order]
         bit //= 2
 
-    def gather_etp(value, ties=()):
+    def gather_etp(value, ties=(), arrived=None):
+        arrived = [] if arrived is None else arrived
         for i, b in enumerate(bits):
             value = after(value, *ties[i]) if i < len(ties) else value
-            value = jnp.concatenate([value, over_etp(value, b)], axis=0)
+            arrived.append(over_etp(value, b))
+            value = jnp.concatenate([value, arrived[-1]], axis=0)
         return value
 
     def reduce_etp(*values):
@@ -144,7 +158,9 @@
         got = {k: over_outer(pieces[k], k) for k in far_first}
         if relay:
             got[3], got[1] = pick(got[3], got[1]), pick(got[1], got[3])
-        got[0] = pieces[0]
+        got[0] = jnp.concatenate(
+            [pieces[0], jnp.broadcast_to(gate_probs[:, None], (cap, 128))], axis=1
+        )
 
         x_chunks = {}
 
@@ -153,17 +169,19 @@
             return jnp.dot(x_chunks[k], weights, preferred_element_type=F32)
 
         if relay:
+            arrived = []
             x_chunks[3] = gather_etp(got[3])
-            x_chunks[1] = gather_etp(got[1])
+            x_chunks[1] = gather_etp(got[1], (), arrived)
             far = multiply(3).astype(BF16)
             swapped = outer_pairs(far, swap)
             near = after(multiply(1, far).astype(BF16), far)
             crossed = outer_pairs(near, middle)
             x_chunks[2] = gather_etp(got[2], [[], [near]])
-            x_chunks[0] = gather_etp(after(got[0], near))
-            two = after(multiply(2, swapped, crossed), swapped)
+            joined = gather_etp(behind(got[0], arrived[0]))
+            x_chunks[0], probs = joined[:, :span], joined[:, span : span + 1]
+            two = after(multiply(2, near), near)
             inwards = outer_pairs(two.astype(BF16), inward)
-            relayed = pick(near, (after(two, swapped) + swapped.astype(F32)).astype(BF16))
+            relayed = pick(near, (after(two, swapped, crossed) + swapped.astype(F32)).astype(BF16))
             cycled = outer_pairs(relayed, back)
             own = multiply(0, relayed) + crossed.astype(F32) + inwards.astype(F32)
             own = own + jnp.where(at_end, swapped.astype(F32), 0.0)
@@ -171,15 +189,15 @@
             last = relayed
         else:
             last, parts = rows, []
-            x_chunks[0] = gather_etp(got[0])
+            joined = gather_etp(got[0])
+            x_chunks[0], probs = joined[:, :span], joined[:, span : span + 1]
             for k in far_first:
                 x_chunks[k] = gather_etp(got[k], [[last]])
                 last = multiply(k).astype(BF16)
                 parts.append(over_outer(last, k))
             own = multiply(0, last)
-        probs = gather_etp(after(gate_probs, rows))
         order = etp ^ jnp.array(chunk_order, jnp.int32)
-        hidden, paired = gate_call(order, own, probs[:, None], d_hidden, parts)
+        hidden, paired = gate_call(order, own, probs, d_hidden, parts)
 
         grads, sums = {0: paired}, {}
 

time: 133 us -> 135 us (1.015)
  waiting for transfers between devices: 74.1 us -> 61.8 us
  starting transfers between devices: 36.4 us -> 48 us
  other arithmetic: 3.17 us -> 4.64 us
    ppermute x8, starting transfers between devices: 12.7 us -> 26 us  [outer_pairs(): return lax.ppermute(value, 'dp', pairs)]
    ppermute x8, waiting for transfers between devices: 38.9 us -> 30.8 us  [outer_pairs(): return lax.ppermute(value, 'dp', pairs)]
    ppermute x16 -> x14, waiting for transfers between devices: 19.8 us -> 13.7 us  [over_etp(): return lax.ppermute(value, 'etp', pairs)]
    ppermute x6, waiting for transfers between devices: 7.57 us -> 10.1 us  [over_outer(): return lax.ppermute(value, 'dp', pairs)]
    ppermute x16 -> x14, starting transfers between devices: 11 us -> 9.5 us  [over_etp(): return lax.ppermute(value, 'etp', pairs)]
    concatenate x10 -> x9, other arithmetic: 0.42 us -> 1.9 us  [the longest x8 1.2 us: gather_etp(): value = jnp.concatenate([value, arrived[-1]], axis=0)]
  transfers between devices with their start and end apart: 33 -> 31, of which waited for: 18 -> 17; matrix products, arithmetic and copies ran while one was open for 9% -> 10% of each run, Pallas kernels for 0% -> 0%
where the time goes in v17:
time: 135 us
  waiting for transfers between devices  61.8 us (46%)
  starting transfers between devices  48 us (36%)
  matrix products  15.8 us (12%)
  other arithmetic  4.64 us (3%)
  local copies, waits for them, and re-layouts  1.82 us (1%)
  Pallas kernels  1.51 us (1%)
  between operations  1.35 us (1%)
    ppermute x8, waiting for transfers between devices, outer_pairs(): return lax.ppermute(value, 'dp', pairs)  30.8 us
    ppermute x8, starting transfers between devices, outer_pairs(): return lax.ppermute(value, 'dp', pairs)  26 us
    ppermute x14, waiting for transfers between devices, over_etp(): return lax.ppermute(value, 'etp', pairs)  13.7 us
    ppermute x6, waiting for transfers between devices, over_outer(): return lax.ppermute(value, 'dp', pairs)  10.1 us
    ppermute x14, starting transfers between devices, over_etp(): return lax.ppermute(value, 'etp', pairs)  9.5 us
    ppermute x6, starting transfers between devices, over_outer(): return lax.ppermute(value, 'dp', pairs)  8.9 us
    ppermute x3, waiting for transfers between devices, over_inner(): return lax.ppermute(value, 'dp', pairs)  7.07 us
    dot_general x1, matrix products, shards(): lax.dot_general(onehot, dx, (((0,), (0,)), ((), ())), preferred_element_t...  3.99 us
  transfers between devices with their start and end apart: 31, of which 17 were waited for; matrix products, arithmetic and copies ran while one was open for 10% of the time, Pallas kernels for 0%

profile of v17, /device:TPU:0, one launch (start us, length us, event | category | flops | bytes accessed | tf_op | source)
XLA Modules:
  0.0 134.9 jit_solution(6356158660246397986)
XLA Ops:
  0.7 3.6 %convolution_convert_fusion.1 = bf16[64,5120]{1,0:T(8,128)(2,1)S(1)} fusion(bf16[512,5120]{1,0:T(8,128)(2,1)} %param.7, s32[64]{0:T(128)} %param.8), kind=kOutput, calls=%fused_computation.1 | convolution fusion | flops 335904768 | bytes 5898496 | tf_op jit(solution)/shard_map/dot_general | solution.py:150
  4.5 5.1 %collective-permute-start.1 = (bf16[64,1280]{1,0:T(8,128)(2,1)S(1)}, bf16[64,1280]{1,0:T(8,128)(2,1)S(1)}, u32[]{:S(2)}, u32[]{:S(2)}) collective-permute-start(bf16[64,1280]{1,0:T(8,128)(2,1)S(1)} %pad_maximum_fusion.15), channel_id=1, source_target_pairs={{0,24},{4,28},{8,16},{12,20},{16,8},{20,12},{24,0},{28,4},{1,25},{... | collective-permute-start | bytes 491528 | tf_op jit(solution)/shard_map/ppermute | solution.py:81
  9.7 1.6 %collective-permute-start.9 = (bf16[640,384]{1,0:T(8,128)(2,1)S(1)}, bf16[640,384]{1,0:T(8,128)(2,1)S(1)}, u32[]{:S(2)}, u32[]{:S(2)}) collective-permute-start(bf16[640,384]{1,0:T(8,128)(2,1)S(1)} %copy-done.4), channel_id=1, source_target_pairs={{0,4},{4,0},{8,12},{12,8},{16,20},{20,16},{24,28},{28,24},{1,5},{5... | collective-permute-start | bytes 1474568 | tf_op jit(solution)/shard_map/ppermute | solution.py:85
  13.2 1.5 %collective-permute-done.1 = bf16[64,1280]{1,0:T(8,128)(2,1)S(1)} collective-permute-done((bf16[64,1280]{1,0:T(8,128)(2,1)S(1)}, bf16[64,1280]{1,0:T(8,128)(2,1)S(1)}, u32[]{:S(2)}, u32[]{:S(2)}) %collective-permute-start.1) | collective-permute-done | bytes 163872 | tf_op jit(solution)/shard_map/ppermute | solution.py:81
  14.7 3.7 %collective-permute-done = bf16[64,1280]{1,0:T(8,128)(2,1)S(1)} collective-permute-done((bf16[64,1280]{1,0:T(8,128)(2,1)S(1)}, bf16[64,1280]{1,0:T(8,128)(2,1)S(1)}, u32[]{:S(2)}, u32[]{:S(2)}) %collective-permute-start) | collective-permute-done | bytes 163872 | tf_op jit(solution)/shard_map/ppermute | solution.py:81
  18.4 1.5 %collective-permute-start.2 = (bf16[64,1280]{1,0:T(8,128)(2,1)S(1)}, bf16[64,1280]{1,0:T(8,128)(2,1)S(1)}, u32[]{:S(2)}, u32[]{:S(2)}) collective-permute-start(bf16[64,1280]{1,0:T(8,128)(2,1)S(1)} %get-tuple-element.75), channel_id=1, source_target_pairs={{0,2},{1,3},{2,0},{3,1},{4,6},{5,7},{6,4},{7,5},{8,10},{9,11},{10,... | collective-permute-start | bytes 491528 | tf_op jit(solution)/shard_map/ppermute | solution.py:89
  20.5 3.0 %collective-permute-done.10 = bf16[64,1280]{1,0:T(8,128)(2,1)S(1)} collective-permute-done((bf16[64,1280]{1,0:T(8,128)(2,1)S(1)}, bf16[64,1280]{1,0:T(8,128)(2,1)S(1)}, u32[]{:S(2)}, u32[]{:S(2)}) %collective-permute-start.10) | collective-permute-done | bytes 163872 | tf_op jit(solution)/shard_map/ppermute | solution.py:81
  23.5 1.5 %collective-permute-start.11 = (bf16[64,1280]{1,0:T(8,128)(2,1)S(1)}, bf16[64,1280]{1,0:T(8,128)(2,1)S(1)}, u32[]{:S(2)}, u32[]{:S(2)}) collective-permute-start(bf16[64,1280]{1,0:T(8,128)(2,1)S(1)} %collective-permute-done.10), channel_id=1, source_target_pairs={{0,2},{1,3},{2,0},{3,1},{4,6},{5,7},{6,4},{7,5},{8,10},{9,11},{10,... | collective-permute-start | bytes 491528 | tf_op jit(solution)/shard_map/ppermute | solution.py:89
  26.2 1.4 %collective-permute-start.3 = (bf16[64,1408]{1,0:T(8,128)(2,1)}, bf16[64,1408]{1,0:T(8,128)(2,1)S(1)}, u32[]{:S(2)}, u32[]{:S(2)}) collective-permute-start(bf16[64,1408]{1,0:T(8,128)(2,1)} %shard_map.102), channel_id=1, source_target_pairs={{0,2},{1,3},{2,0},{3,1},{4,6},{5,7},{6,4},{7,5},{8,10},{9,11},{10,... | collective-permute-start | bytes 540680 | tf_op jit(solution)/shard_map/ppermute | solution.py:89
  29.1 3.5 %collective-permute-done.11 = bf16[64,1280]{1,0:T(8,128)(2,1)S(1)} collective-permute-done((bf16[64,1280]{1,0:T(8,128)(2,1)S(1)}, bf16[64,1280]{1,0:T(8,128)(2,1)S(1)}, u32[]{:S(2)}, u32[]{:S(2)}) %collective-permute-start.11) | collective-permute-done | bytes 163872 | tf_op jit(solution)/shard_map/ppermute | solution.py:89
  38.8 6.0 %collective-permute-start.15 = (bf16[256,768]{1,0:T(8,128)(2,1)S(1)}, bf16[256,768]{1,0:T(8,128)(2,1)S(1)}, u32[]{:S(2)}, u32[]{:S(2)}) collective-permute-start(bf16[256,768]{1,0:T(8,128)(2,1)S(1)} %convert_element_type.88), channel_id=1, source_target_pairs={{0,16},{4,20},{24,8},{28,12},{1,17},{5,21},{25,9},{29,13},{2,18},{... | collective-permute-start | bytes 1179656 | tf_op jit(solution)/shard_map/ppermute | solution.py:122
  44.9 2.9 %collective-permute-done.13 = bf16[256,768]{1,0:T(8,128)(2,1)S(1)} collective-permute-done((bf16[256,768]{1,0:T(8,128)(2,1)S(1)}, bf16[256,768]{1,0:T(8,128)(2,1)S(1)}, u32[]{:S(2)}, u32[]{:S(2)}) %collective-permute-start.13) | collective-permute-done | bytes 393248 | tf_op jit(solution)/shard_map/ppermute | solution.py:122
  47.9 12.1 %collective-permute-start.16 = (bf16[256,768]{1,0:T(8,128)(2,1)S(1)}, bf16[256,768]{1,0:T(8,128)(2,1)S(1)}, u32[]{:S(2)}, u32[]{:S(2)}) collective-permute-start(bf16[256,768]{1,0:T(8,128)(2,1)S(1)} %fusion.18), channel_id=1, source_target_pairs={{16,0},{20,4},{24,16},{28,20},{8,24},{12,28},{0,8},{4,12},{17,1},{... | collective-permute-start | bytes 1179656 | tf_op jit(solution)/shard_map/ppermute | solution.py:122
  60.8 7.5 %collective-permute-done.16.refs_0_ = bf16[256,768]{1,0:T(8,128)(2,1)S(1)} collective-permute-done((bf16[256,768]{1,0:T(8,128)(2,1)S(1)}, bf16[256,768]{1,0:T(8,128)(2,1)S(1)}, u32[]{:S(2)}, u32[]{:S(2)}) %collective-permute-start.16) | collective-permute-done | bytes 393248 | tf_op jit(solution)/shard_map/ppermute | solution.py:122
  68.4 1.5 %shard_map.103 = (bf16[256,384]{1,0:T(8,128)(2,1)}, bf16[256,768]{1,0:T(8,128)(2,1)S(1)}) custom-call(s32[4]{0:T(128)S(1)} %broadcast_xor_fusion.order_ref, f32[256,768]{1,0:T(8,128)S(1)} %fusion.9.pre_ref, bf16[256,1]{1,0:T(8,128)(2,1)S(1)} %pad_maximum_fusion.17.prob_ref, bf16[256,384]{1,0:T(8,128)(2,1)S(1)} %copy-done, ...), custom_call_target="tpu_custom_call" | custom-call | flops 1966080 | bytes 2949120 | tf_op jit(solution)/shard_map/pallas_call | solution.py:61
  70.9 1.8 %collective-permute-start.19 = (bf16[256,768]{1,0:T(8,128)(2,1)S(1)}, bf16[256,768]{1,0:T(8,128)(2,1)S(1)}, u32[]{:S(2)}, u32[]{:S(2)}) collective-permute-start(bf16[256,768]{1,0:T(8,128)(2,1)S(1)} %get-tuple-element.38), channel_id=1, source_target_pairs={{0,16},{4,20},{16,24},{20,28},{24,8},{28,12},{8,0},{12,4},{1,17},{... | collective-permute-start | bytes 1179656 | tf_op jit(solution)/shard_map/ppermute | solution.py:122
  72.7 1.3 collective-permute-start.20
  75.0 1.5 %collective-permute-start.18 = (bf16[64,1280]{1,0:T(8,128)(2,1)S(1)}, bf16[64,1280]{1,0:T(8,128)(2,1)S(1)}, u32[]{:S(2)}, u32[]{:S(2)}) collective-permute-start(bf16[64,1280]{1,0:T(8,128)(2,1)S(1)} %slice.260), channel_id=1, source_target_pairs={{0,2},{1,3},{2,0},{3,1},{4,6},{5,7},{6,4},{7,5},{8,10},{9,11},{10,... | collective-permute-start | bytes 491528 | tf_op jit(solution)/shard_map/ppermute | solution.py:89
  76.5 6.1 %collective-permute-done.19 = bf16[256,768]{1,0:T(8,128)(2,1)S(1)} collective-permute-done((bf16[256,768]{1,0:T(8,128)(2,1)S(1)}, bf16[256,768]{1,0:T(8,128)(2,1)S(1)}, u32[]{:S(2)}, u32[]{:S(2)}) %collective-permute-start.19) | collective-permute-done | bytes 393248 | tf_op jit(solution)/shard_map/ppermute | solution.py:122
  82.6 2.7 %collective-permute-start.22 = (bf16[256,768]{1,0:T(8,128)(2,1)S(1)}, bf16[256,768]{1,0:T(8,128)(2,1)S(1)}, u32[]{:S(2)}, u32[]{:S(2)}) collective-permute-start(bf16[256,768]{1,0:T(8,128)(2,1)S(1)} %broadcast_select_fusion.2), channel_id=1, source_target_pairs={{0,8},{4,12},{8,0},{12,4},{16,24},{20,28},{24,16},{28,20},{1,9},{5... | collective-permute-start | bytes 1179656 | tf_op jit(solution)/shard_map/ppermute | solution.py:122
  85.3 7.8 %collective-permute-done.20 = bf16[256,768]{1,0:T(8,128)(2,1)S(1)} collective-permute-done((bf16[256,768]{1,0:T(8,128)(2,1)S(1)}, bf16[256,768]{1,0:T(8,128)(2,1)S(1)}, u32[]{:S(2)}, u32[]{:S(2)}) %collective-permute-start.20) | collective-permute-done | bytes 393248 | tf_op jit(solution)/shard_map/ppermute | solution.py:122
  94.8 6.5 %collective-permute-done.22 = bf16[256,768]{1,0:T(8,128)(2,1)S(1)} collective-permute-done((bf16[256,768]{1,0:T(8,128)(2,1)S(1)}, bf16[256,768]{1,0:T(8,128)(2,1)S(1)}, u32[]{:S(2)}, u32[]{:S(2)}) %collective-permute-start.22) | collective-permute-done | bytes 393248 | tf_op jit(solution)/shard_map/ppermute | solution.py:122
  103.9 1.5 %collective-permute-start.27 = (bf16[64,1280]{1,0:T(8,128)(2,1)S(1)}, bf16[64,1280]{1,0:T(8,128)(2,1)S(1)}, u32[]{:S(2)}, u32[]{:S(2)}) collective-permute-start(bf16[64,1280]{1,0:T(8,128)(2,1)S(1)} %slice.257), channel_id=1, source_target_pairs={{0,2},{1,3},{2,0},{3,1},{4,6},{5,7},{6,4},{7,5},{8,10},{9,11},{10,... | collective-permute-start | bytes 491528 | tf_op jit(solution)/shard_map/ppermute | solution.py:89
  105.4 1.5 %collective-permute-start.30 = (bf16[640,768]{1,0:T(8,128)(2,1)S(1)}, bf16[640,768]{1,0:T(8,128)(2,1)S(1)}, u32[]{:S(2)}, u32[]{:S(2)}) collective-permute-start(bf16[640,768]{1,0:T(8,128)(2,1)S(1)} %add_convert_fusion), channel_id=1, source_target_pairs={{0,4},{4,0},{8,12},{12,8},{16,20},{20,16},{24,28},{28,24},{1,5},{5... | collective-permute-start | bytes 2949128 | tf_op jit(solution)/shard_map/ppermute | solution.py:85
  107.0 1.2 fusion
  109.1 1.5 %collective-permute-done.27 = bf16[64,1280]{1,0:T(8,128)(2,1)S(1)} collective-permute-done((bf16[64,1280]{1,0:T(8,128)(2,1)S(1)}, bf16[64,1280]{1,0:T(8,128)(2,1)S(1)}, u32[]{:S(2)}, u32[]{:S(2)}) %collective-permute-start.27) | collective-permute-done | bytes 163872 | tf_op jit(solution)/shard_map/ppermute | solution.py:89
  111.4 6.7 %collective-permute-done.24 = bf16[128,1280]{1,0:T(8,128)(2,1)S(1)} collective-permute-done((bf16[128,1280]{1,0:T(8,128)(2,1)S(1)}, bf16[128,1280]{1,0:T(8,128)(2,1)S(1)}, u32[]{:S(2)}, u32[]{:S(2)}) %collective-permute-start.24) | collective-permute-done | bytes 327712 | tf_op jit(solution)/shard_map/ppermute | solution.py:89
  119.0 1.9 %collective-permute-done.28 = bf16[64,1280]{1,0:T(8,128)(2,1)S(1)} collective-permute-done((bf16[64,1280]{1,0:T(8,128)(2,1)S(1)}, bf16[64,1280]{1,0:T(8,128)(2,1)S(1)}, u32[]{:S(2)}, u32[]{:S(2)}) %collective-permute-start.28) | collective-permute-done | bytes 163872 | tf_op jit(solution)/shard_map/ppermute | solution.py:81
  121.0 1.5 %collective-permute-start.29 = (bf16[64,1280]{1,0:T(8,128)(2,1)S(1)}, bf16[64,1280]{1,0:T(8,128)(2,1)S(1)}, u32[]{:S(2)}, u32[]{:S(2)}) collective-permute-start(bf16[64,1280]{1,0:T(8,128)(2,1)S(1)} %get-tuple-element.52), channel_id=1, source_target_pairs={{0,24},{4,28},{8,16},{12,20},{16,8},{20,12},{24,0},{28,4},{1,25},{... | collective-permute-start | bytes 491528 | tf_op jit(solution)/shard_map/ppermute | solution.py:81
  122.6 6.7 %collective-permute-done.30 = bf16[640,768]{1,0:T(8,128)(2,1)S(1)} collective-permute-done((bf16[640,768]{1,0:T(8,128)(2,1)S(1)}, bf16[640,768]{1,0:T(8,128)(2,1)S(1)}, u32[]{:S(2)}, u32[]{:S(2)}) %collective-permute-start.30) | collective-permute-done | bytes 983072 | tf_op jit(solution)/shard_map/ppermute | solution.py:85
  129.3 1.5 %slice_add_fusion = (f32[640,384]{1,0:T(8,128)}, f32[640,384]{1,0:T(8,128)}) fusion(f32[640,768]{1,0:T(8,128)S(1)} %fusion, bf16[640,768]{1,0:T(8,128)(2,1)S(1)} %collective-permute-done.30), kind=kLoop, calls=%fused_computation.18 | loop fusion | flops 983040 | bytes 4915200 | tf_op jit(solution)/shard_map/add | solution.py:256
  131.0 4.0 %convolution_convert_fusion = bf16[512,5120]{1,0:T(8,128)(2,1)} fusion(bf16[64,5120]{1,0:T(8,128)(2,1)S(1)} %slice_dynamic-update-slice_fusion.2, s32[64]{0:T(128)S(1)} %copy-done.6), kind=kOutput, calls=%fused_computation | convolution fusion | flops 338198528 | bytes 5898496 | tf_op jit(solution)/shard_map/dot_general | solution.py:269
  (120 shorter events, 21.5 us)
Async XLA Ops:
  4.3 15.6 %copy-start.8 = (s32[4]{0:T(128)S(1)}, s32[4]{0:T(128)}, u32[]{:S(2)}) copy-start(s32[4]{0:T(128)} %constant.49.clone) | copy-start | bytes 52
  4.5 10.2 %collective-permute-start.1 = (bf16[64,1280]{1,0:T(8,128)(2,1)S(1)}, bf16[64,1280]{1,0:T(8,128)(2,1)S(1)}, u32[]{:S(2)}, u32[]{:S(2)}) collective-permute-start(bf16[64,1280]{1,0:T(8,128)(2,1)S(1)} %pad_maximum_fusion.15), channel_id=1, source_target_pairs={{0,24},{4,28},{8,16},{12,20},{16,8},{20,12},{24,0},{28,4},{1,25},{... | collective-permute-start | bytes 491528 | tf_op jit(solution)/shard_map/ppermute | solution.py:81
  9.6 8.8 %collective-permute-start = (bf16[64,1280]{1,0:T(8,128)(2,1)S(1)}, bf16[64,1280]{1,0:T(8,128)(2,1)S(1)}, u32[]{:S(2)}, u32[]{:S(2)}) collective-permute-start(bf16[64,1280]{1,0:T(8,128)(2,1)S(1)} %pad_maximum_fusion.14), channel_id=1, source_target_pairs={{0,8},{4,12},{8,0},{12,4},{16,24},{20,28},{24,16},{28,20},{1,9},{5... | collective-permute-start | bytes 491528 | tf_op jit(solution)/shard_map/ppermute | solution.py:81
  9.7 22.9 %collective-permute-start.9 = (bf16[640,384]{1,0:T(8,128)(2,1)S(1)}, bf16[640,384]{1,0:T(8,128)(2,1)S(1)}, u32[]{:S(2)}, u32[]{:S(2)}) collective-permute-start(bf16[640,384]{1,0:T(8,128)(2,1)S(1)} %copy-done.4), channel_id=1, source_target_pairs={{0,4},{4,0},{8,12},{12,8},{16,20},{20,16},{24,28},{28,24},{1,5},{5... | collective-permute-start | bytes 1474568 | tf_op jit(solution)/shard_map/ppermute | solution.py:85
  11.3 21.7 %collective-permute-start.8 = (bf16[640,384]{1,0:T(8,128)(2,1)S(1)}, bf16[640,384]{1,0:T(8,128)(2,1)S(1)}, u32[]{:S(2)}, u32[]{:S(2)}) collective-permute-start(bf16[640,384]{1,0:T(8,128)(2,1)S(1)} %copy-done.5), channel_id=1, source_target_pairs={{0,4},{4,0},{8,12},{12,8},{16,20},{20,16},{24,28},{28,24},{1,5},{5... | collective-permute-start | bytes 1474568 | tf_op jit(solution)/shard_map/ppermute | solution.py:85
  11.8 11.7 %collective-permute-start.10 = (bf16[64,1280]{1,0:T(8,128)(2,1)S(1)}, bf16[64,1280]{1,0:T(8,128)(2,1)S(1)}, u32[]{:S(2)}, u32[]{:S(2)}) collective-permute-start(bf16[64,1280]{1,0:T(8,128)(2,1)S(1)} %pad_maximum_fusion.16), channel_id=1, source_target_pairs={{0,16},{4,20},{8,24},{12,28},{16,0},{20,4},{24,8},{28,12},{1,17},{... | collective-permute-start | bytes 491528 | tf_op jit(solution)/shard_map/ppermute | solution.py:81
  18.4 7.1 %collective-permute-start.2 = (bf16[64,1280]{1,0:T(8,128)(2,1)S(1)}, bf16[64,1280]{1,0:T(8,128)(2,1)S(1)}, u32[]{:S(2)}, u32[]{:S(2)}) collective-permute-start(bf16[64,1280]{1,0:T(8,128)(2,1)S(1)} %get-tuple-element.75), channel_id=1, source_target_pairs={{0,2},{1,3},{2,0},{3,1},{4,6},{5,7},{6,4},{7,5},{8,10},{9,11},{10,... | collective-permute-start | bytes 491528 | tf_op jit(solution)/shard_map/ppermute | solution.py:89
  20.0 9.1 %collective-permute-start.6 = (bf16[64,1280]{1,0:T(8,128)(2,1)S(1)}, bf16[64,1280]{1,0:T(8,128)(2,1)S(1)}, u32[]{:S(2)}, u32[]{:S(2)}) collective-permute-start(bf16[64,1280]{1,0:T(8,128)(2,1)S(1)} %get-tuple-element.74), channel_id=1, source_target_pairs={{0,2},{1,3},{2,0},{3,1},{4,6},{5,7},{6,4},{7,5},{8,10},{9,11},{10,... | collective-permute-start | bytes 491528 | tf_op jit(solution)/shard_map/ppermute | solution.py:89
  23.5 9.1 %collective-permute-start.11 = (bf16[64,1280]{1,0:T(8,128)(2,1)S(1)}, bf16[64,1280]{1,0:T(8,128)(2,1)S(1)}, u32[]{:S(2)}, u32[]{:S(2)}) collective-permute-start(bf16[64,1280]{1,0:T(8,128)(2,1)S(1)} %collective-permute-done.10), channel_id=1, source_target_pairs={{0,2},{1,3},{2,0},{3,1},{4,6},{5,7},{6,4},{7,5},{8,10},{9,11},{10,... | collective-permute-start | bytes 491528 | tf_op jit(solution)/shard_map/ppermute | solution.py:89
  26.2 9.9 %collective-permute-start.3 = (bf16[64,1408]{1,0:T(8,128)(2,1)}, bf16[64,1408]{1,0:T(8,128)(2,1)S(1)}, u32[]{:S(2)}, u32[]{:S(2)}) collective-permute-start(bf16[64,1408]{1,0:T(8,128)(2,1)} %shard_map.102), channel_id=1, source_target_pairs={{0,2},{1,3},{2,0},{3,1},{4,6},{5,7},{6,4},{7,5},{8,10},{9,11},{10,... | collective-permute-start | bytes 540680 | tf_op jit(solution)/shard_map/ppermute | solution.py:89
  29.1 5.9 %collective-permute-start.5 = (bf16[128,1280]{1,0:T(8,128)(2,1)S(1)}, bf16[128,1280]{1,0:T(8,128)(2,1)S(1)}, u32[]{:S(2)}, u32[]{:S(2)}) collective-permute-start(bf16[128,1280]{1,0:T(8,128)(2,1)S(1)} %pad_maximum_fusion.9), channel_id=1, source_target_pairs={{0,1},{1,0},{2,3},{3,2},{4,5},{5,4},{6,7},{7,6},{8,9},{9,8},{10,11... | collective-permute-start | bytes 983048 | tf_op jit(solution)/shard_map/ppermute | solution.py:89
  32.6 1.6 %collective-permute-start.7 = (bf16[128,1280]{1,0:T(8,128)(2,1)S(1)}, bf16[128,1280]{1,0:T(8,128)(2,1)S(1)}, u32[]{:S(2)}, u32[]{:S(2)}) collective-permute-start(bf16[128,1280]{1,0:T(8,128)(2,1)S(1)} %pad_maximum_fusion.10), channel_id=1, source_target_pairs={{0,1},{1,0},{2,3},{3,2},{4,5},{5,4},{6,7},{7,6},{8,9},{9,8},{10,11... | collective-permute-start | bytes 983048 | tf_op jit(solution)/shard_map/ppermute | solution.py:89
  35.9 2.1 %collective-permute-start.12 = (bf16[128,1280]{1,0:T(8,128)(2,1)S(1)}, bf16[128,1280]{1,0:T(8,128)(2,1)S(1)}, u32[]{:S(2)}, u32[]{:S(2)}) collective-permute-start(bf16[128,1280]{1,0:T(8,128)(2,1)S(1)} %pad_maximum_fusion.11), channel_id=1, source_target_pairs={{0,1},{1,0},{2,3},{3,2},{4,5},{5,4},{6,7},{7,6},{8,9},{9,8},{10,11... | collective-permute-start | bytes 983048 | tf_op jit(solution)/shard_map/ppermute | solution.py:89
  36.2 8.6 %collective-permute-start.4 = (bf16[128,1408]{1,0:T(8,128)(2,1)S(1)}, bf16[128,1408]{1,0:T(8,128)(2,1)S(1)}, u32[]{:S(2)}, u32[]{:S(2)}) collective-permute-start(bf16[128,1408]{1,0:T(8,128)(2,1)S(1)} %pad_maximum_fusion.8), channel_id=1, source_target_pairs={{0,1},{1,0},{2,3},{3,2},{4,5},{5,4},{6,7},{7,6},{8,9},{9,8},{10,11... | collective-permute-start | bytes 1081352 | tf_op jit(solution)/shard_map/ppermute | solution.py:89
  36.6 11.2 %collective-permute-start.13 = (bf16[256,768]{1,0:T(8,128)(2,1)S(1)}, bf16[256,768]{1,0:T(8,128)(2,1)S(1)}, u32[]{:S(2)}, u32[]{:S(2)}) collective-permute-start(bf16[256,768]{1,0:T(8,128)(2,1)S(1)} %convolution_convert_fusion.3), channel_id=1, source_target_pairs={{0,8},{4,12},{8,0},{12,4},{16,24},{20,28},{24,16},{28,20},{1,9},{5... | collective-permute-start | bytes 1179656 | tf_op jit(solution)/shard_map/ppermute | solution.py:122
  37.3 10.5 %collective-permute-start.14 = (bf16[256,768]{1,0:T(8,128)(2,1)S(1)}, bf16[256,768]{1,0:T(8,128)(2,1)S(1)}, u32[]{:S(2)}, u32[]{:S(2)}) collective-permute-start(bf16[256,768]{1,0:T(8,128)(2,1)S(1)} %convolution_convert_fusion.2), channel_id=1, source_target_pairs={{8,16},{12,20},{16,8},{20,12},{9,17},{13,21},{17,9},{21,13},{10,18... | collective-permute-start | bytes 1179656 | tf_op jit(solution)/shard_map/ppermute | solution.py:122
  38.8 21.2 %collective-permute-start.15 = (bf16[256,768]{1,0:T(8,128)(2,1)S(1)}, bf16[256,768]{1,0:T(8,128)(2,1)S(1)}, u32[]{:S(2)}, u32[]{:S(2)}) collective-permute-start(bf16[256,768]{1,0:T(8,128)(2,1)S(1)} %convert_element_type.88), channel_id=1, source_target_pairs={{0,16},{4,20},{24,8},{28,12},{1,17},{5,21},{25,9},{29,13},{2,18},{... | collective-permute-start | bytes 1179656 | tf_op jit(solution)/shard_map/ppermute | solution.py:122
  47.9 20.4 %collective-permute-start.16 = (bf16[256,768]{1,0:T(8,128)(2,1)S(1)}, bf16[256,768]{1,0:T(8,128)(2,1)S(1)}, u32[]{:S(2)}, u32[]{:S(2)}) collective-permute-start(bf16[256,768]{1,0:T(8,128)(2,1)S(1)} %fusion.18), channel_id=1, source_target_pairs={{16,0},{20,4},{24,16},{28,20},{8,24},{12,28},{0,8},{4,12},{17,1},{... | collective-permute-start | bytes 1179656 | tf_op jit(solution)/shard_map/ppermute | solution.py:122
  70.6 4.2 %collective-permute-start.17 = (bf16[128,1280]{1,0:T(8,128)(2,1)S(1)}, bf16[128,1280]{1,0:T(8,128)(2,1)S(1)}, u32[]{:S(2)}, u32[]{:S(2)}) collective-permute-start(bf16[128,1280]{1,0:T(8,128)(2,1)S(1)} %slice.256), channel_id=1, source_target_pairs={{0,1},{1,0},{2,3},{3,2},{4,5},{5,4},{6,7},{7,6},{8,9},{9,8},{10,11... | collective-permute-start | bytes 983048 | tf_op jit(solution)/shard_map/ppermute | solution.py:89
  70.9 11.7 %collective-permute-start.19 = (bf16[256,768]{1,0:T(8,128)(2,1)S(1)}, bf16[256,768]{1,0:T(8,128)(2,1)S(1)}, u32[]{:S(2)}, u32[]{:S(2)}) collective-permute-start(bf16[256,768]{1,0:T(8,128)(2,1)S(1)} %get-tuple-element.38), channel_id=1, source_target_pairs={{0,16},{4,20},{16,24},{20,28},{24,8},{28,12},{8,0},{12,4},{1,17},{... | collective-permute-start | bytes 1179656 | tf_op jit(solution)/shard_map/ppermute | solution.py:122
  72.7 20.3 %collective-permute-start.20 = (bf16[256,768]{1,0:T(8,128)(2,1)S(1)}, bf16[256,768]{1,0:T(8,128)(2,1)S(1)}, u32[]{:S(2)}, u32[]{:S(2)}) collective-permute-start(bf16[256,768]{1,0:T(8,128)(2,1)S(1)} %get-tuple-element.38), channel_id=1, source_target_pairs={{16,0},{20,4},{8,24},{12,28},{17,1},{21,5},{9,25},{13,29},{18,2},{... | collective-permute-start | bytes 1179656 | tf_op jit(solution)/shard_map/ppermute | solution.py:122
  74.0 20.7 %collective-permute-start.21 = (bf16[256,768]{1,0:T(8,128)(2,1)S(1)}, bf16[256,768]{1,0:T(8,128)(2,1)S(1)}, u32[]{:S(2)}, u32[]{:S(2)}) collective-permute-start(bf16[256,768]{1,0:T(8,128)(2,1)S(1)} %get-tuple-element.38), channel_id=1, source_target_pairs={{8,16},{12,20},{16,8},{20,12},{9,17},{13,21},{17,9},{21,13},{10,18... | collective-permute-start | bytes 1179656 | tf_op jit(solution)/shard_map/ppermute | solution.py:122
  75.0 19.8 %collective-permute-start.18 = (bf16[64,1280]{1,0:T(8,128)(2,1)S(1)}, bf16[64,1280]{1,0:T(8,128)(2,1)S(1)}, u32[]{:S(2)}, u32[]{:S(2)}) collective-permute-start(bf16[64,1280]{1,0:T(8,128)(2,1)S(1)} %slice.260), channel_id=1, source_target_pairs={{0,2},{1,3},{2,0},{3,1},{4,6},{5,7},{6,4},{7,5},{8,10},{9,11},{10,... | collective-permute-start | bytes 491528 | tf_op jit(solution)/shard_map/ppermute | solution.py:89
  82.6 18.7 %collective-permute-start.22 = (bf16[256,768]{1,0:T(8,128)(2,1)S(1)}, bf16[256,768]{1,0:T(8,128)(2,1)S(1)}, u32[]{:S(2)}, u32[]{:S(2)}) collective-permute-start(bf16[256,768]{1,0:T(8,128)(2,1)S(1)} %broadcast_select_fusion.2), channel_id=1, source_target_pairs={{0,8},{4,12},{8,0},{12,4},{16,24},{20,28},{24,16},{28,20},{1,9},{5... | collective-permute-start | bytes 1179656 | tf_op jit(solution)/shard_map/ppermute | solution.py:122
  94.6 9.2 %collective-permute-start.26 = (bf16[128,1280]{1,0:T(8,128)(2,1)S(1)}, bf16[128,1280]{1,0:T(8,128)(2,1)S(1)}, u32[]{:S(2)}, u32[]{:S(2)}) collective-permute-start(bf16[128,1280]{1,0:T(8,128)(2,1)S(1)} %slice.253), channel_id=1, source_target_pairs={{0,1},{1,0},{2,3},{3,2},{4,5},{5,4},{6,7},{7,6},{8,9},{9,8},{10,11... | collective-permute-start | bytes 983048 | tf_op jit(solution)/shard_map/ppermute | solution.py:89
  103.7 4.5 %collective-permute-start.23 = (bf16[256,1280]{1,0:T(8,128)(2,1)S(1)}, bf16[256,1280]{1,0:T(8,128)(2,1)S(1)}, u32[]{:S(2)}, u32[]{:S(2)}) collective-permute-start(bf16[256,1280]{1,0:T(8,128)(2,1)S(1)} %pad_maximum_fusion.7), channel_id=1, source_target_pairs={{0,1},{1,0},{2,3},{3,2},{4,5},{5,4},{6,7},{7,6},{8,9},{9,8},{10,11... | collective-permute-start | bytes 1966088 | tf_op jit(solution)/shard_map/ppermute | solution.py:89
  103.9 6.7 %collective-permute-start.27 = (bf16[64,1280]{1,0:T(8,128)(2,1)S(1)}, bf16[64,1280]{1,0:T(8,128)(2,1)S(1)}, u32[]{:S(2)}, u32[]{:S(2)}) collective-permute-start(bf16[64,1280]{1,0:T(8,128)(2,1)S(1)} %slice.257), channel_id=1, source_target_pairs={{0,2},{1,3},{2,0},{3,1},{4,6},{5,7},{6,4},{7,5},{8,10},{9,11},{10,... | collective-permute-start | bytes 491528 | tf_op jit(solution)/shard_map/ppermute | solution.py:89
  105.4 23.9 %collective-permute-start.30 = (bf16[640,768]{1,0:T(8,128)(2,1)S(1)}, bf16[640,768]{1,0:T(8,128)(2,1)S(1)}, u32[]{:S(2)}, u32[]{:S(2)}) collective-permute-start(bf16[640,768]{1,0:T(8,128)(2,1)S(1)} %add_convert_fusion), channel_id=1, source_target_pairs={{0,4},{4,0},{8,12},{12,8},{16,20},{20,16},{24,28},{28,24},{1,5},{5... | collective-permute-start | bytes 2949128 | tf_op jit(solution)/shard_map/ppermute | solution.py:85
  108.5 9.6 %collective-permute-start.24 = (bf16[128,1280]{1,0:T(8,128)(2,1)S(1)}, bf16[128,1280]{1,0:T(8,128)(2,1)S(1)}, u32[]{:S(2)}, u32[]{:S(2)}) collective-permute-start(bf16[128,1280]{1,0:T(8,128)(2,1)S(1)} %pad_maximum_fusion.12), channel_id=1, source_target_pairs={{0,2},{1,3},{2,0},{3,1},{4,6},{5,7},{6,4},{7,5},{8,10},{9,11},{10,... | collective-permute-start | bytes 983048 | tf_op jit(solution)/shard_map/ppermute | solution.py:89
  110.6 10.4 %collective-permute-start.28 = (bf16[64,1280]{1,0:T(8,128)(2,1)S(1)}, bf16[64,1280]{1,0:T(8,128)(2,1)S(1)}, u32[]{:S(2)}, u32[]{:S(2)}) collective-permute-start(bf16[64,1280]{1,0:T(8,128)(2,1)S(1)} %fusion.19), channel_id=1, source_target_pairs={{0,16},{4,20},{8,24},{12,28},{16,0},{20,4},{24,8},{28,12},{1,17},{... | collective-permute-start | bytes 491528 | tf_op jit(solution)/shard_map/ppermute | solution.py:81
  118.2 12.5 %collective-permute-start.25 = (bf16[64,1280]{1,0:T(8,128)(2,1)S(1)}, bf16[64,1280]{1,0:T(8,128)(2,1)S(1)}, u32[]{:S(2)}, u32[]{:S(2)}) collective-permute-start(bf16[64,1280]{1,0:T(8,128)(2,1)S(1)} %broadcast_select_fusion.4), channel_id=1, source_target_pairs={{0,8},{4,12},{8,0},{12,4},{16,24},{20,28},{24,16},{28,20},{1,9},{5... | collective-permute-start | bytes 491528 | tf_op jit(solution)/shard_map/ppermute | solution.py:81
  121.0 9.9 %collective-permute-start.29 = (bf16[64,1280]{1,0:T(8,128)(2,1)S(1)}, bf16[64,1280]{1,0:T(8,128)(2,1)S(1)}, u32[]{:S(2)}, u32[]{:S(2)}) collective-permute-start(bf16[64,1280]{1,0:T(8,128)(2,1)S(1)} %get-tuple-element.52), channel_id=1, source_target_pairs={{0,24},{4,28},{8,16},{12,20},{16,8},{20,12},{24,0},{28,4},{1,25},{... | collective-permute-start | bytes 491528 | tf_op jit(solution)/shard_map/ppermute | solution.py:81
  (8 other events, 39.7 us)

commit v18 on v17

--- a/solution.py
+++ b/solution.py
@@ -181,7 +181,7 @@
             x_chunks[0], probs = joined[:, :span], joined[:, span : span + 1]
             two = after(multiply(2, near), near)
             inwards = outer_pairs(two.astype(BF16), inward)
-            relayed = pick(near, (after(two, swapped, crossed) + swapped.astype(F32)).astype(BF16))
+            relayed = pick(near, (after(two, swapped) + swapped.astype(F32)).astype(BF16))
             cycled = outer_pairs(relayed, back)
             own = multiply(0, relayed) + crossed.astype(F32) + inwards.astype(F32)
             own = own + jnp.where(at_end, swapped.astype(F32), 0.0)

time: 135 us -> 135 us (level)
  starting transfers between devices: 48 us -> 30.7 us
  waiting for transfers between devices: 61.8 us -> 78.8 us
    ppermute x8, starting transfers between devices: 26 us -> 11.1 us  [outer_pairs(): return lax.ppermute(value, 'dp', pairs)]
    ppermute x8, waiting for transfers between devices: 30.8 us -> 45.4 us  [outer_pairs(): return lax.ppermute(value, 'dp', pairs)]
    ppermute x6, starting transfers between devices: 8.9 us -> 6.5 us  [over_outer(): return lax.ppermute(value, 'dp', pairs)]
    ppermute x3, waiting for transfers between devices: 7.07 us -> 8.57 us  [over_inner(): return lax.ppermute(value, 'dp', pairs)]
where the time goes in v18:
time: 135 us
  waiting for transfers between devices  78.8 us (58%)
  starting transfers between devices  30.7 us (23%)
  matrix products  15.8 us (12%)
  other arithmetic  4.64 us (3%)
  local copies, waits for them, and re-layouts  1.82 us (1%)
  Pallas kernels  1.51 us (1%)
  between operations  1.39 us (1%)
    ppermute x8, waiting for transfers between devices, outer_pairs(): return lax.ppermute(value, 'dp', pairs)  45.4 us
    ppermute x14, waiting for transfers between devices, over_etp(): return lax.ppermute(value, 'etp', pairs)  14.5 us
    ppermute x8, starting transfers between devices, outer_pairs(): return lax.ppermute(value, 'dp', pairs)  11.1 us
    ppermute x6, waiting for transfers between devices, over_outer(): return lax.ppermute(value, 'dp', pairs)  10.3 us
    ppermute x14, starting transfers between devices, over_etp(): return lax.ppermute(value, 'etp', pairs)  9.51 us
    ppermute x3, waiting for transfers between devices, over_inner(): return lax.ppermute(value, 'dp', pairs)  8.57 us
    ppermute x6, starting transfers between devices, over_outer(): return lax.ppermute(value, 'dp', pairs)  6.5 us
    dot_general x1, matrix products, shards(): lax.dot_general(onehot, dx, (((0,), (0,)), ((), ())), preferred_element_t...  3.99 us
  transfers between devices with their start and end apart: 31, of which 17 were waited for; matrix products, arithmetic and copies ran while one was open for 10% of the time, Pallas kernels for 0%

profile of v18, /device:TPU:0, one launch (start us, length us, event | category | flops | bytes accessed | tf_op | source)
XLA Modules:
  0.0 134.7 jit_solution(17700469014132575049)
XLA Ops:
  0.7 3.6 %convolution_convert_fusion.1 = bf16[64,5120]{1,0:T(8,128)(2,1)S(1)} fusion(bf16[512,5120]{1,0:T(8,128)(2,1)} %param.7, s32[64]{0:T(128)} %param.8), kind=kOutput, calls=%fused_computation.1 | convolution fusion | flops 335904768 | bytes 5898496 | tf_op jit(solution)/shard_map/dot_general | solution.py:150
  4.5 5.1 %collective-permute-start.1 = (bf16[64,1280]{1,0:T(8,128)(2,1)S(1)}, bf16[64,1280]{1,0:T(8,128)(2,1)S(1)}, u32[]{:S(2)}, u32[]{:S(2)}) collective-permute-start(bf16[64,1280]{1,0:T(8,128)(2,1)S(1)} %pad_maximum_fusion.15), channel_id=1, source_target_pairs={{0,24},{4,28},{8,16},{12,20},{16,8},{20,12},{24,0},{28,4},{1,25},{... | collective-permute-start | bytes 491528 | tf_op jit(solution)/shard_map/ppermute | solution.py:81
  9.7 1.6 %collective-permute-start.9 = (bf16[640,384]{1,0:T(8,128)(2,1)S(1)}, bf16[640,384]{1,0:T(8,128)(2,1)S(1)}, u32[]{:S(2)}, u32[]{:S(2)}) collective-permute-start(bf16[640,384]{1,0:T(8,128)(2,1)S(1)} %copy-done.4), channel_id=1, source_target_pairs={{0,4},{4,0},{8,12},{12,8},{16,20},{20,16},{24,28},{28,24},{1,5},{5... | collective-permute-start | bytes 1474568 | tf_op jit(solution)/shard_map/ppermute | solution.py:85
  13.2 1.5 %collective-permute-done.1 = bf16[64,1280]{1,0:T(8,128)(2,1)S(1)} collective-permute-done((bf16[64,1280]{1,0:T(8,128)(2,1)S(1)}, bf16[64,1280]{1,0:T(8,128)(2,1)S(1)}, u32[]{:S(2)}, u32[]{:S(2)}) %collective-permute-start.1) | collective-permute-done | bytes 163872 | tf_op jit(solution)/shard_map/ppermute | solution.py:81
  14.7 3.7 %collective-permute-done = bf16[64,1280]{1,0:T(8,128)(2,1)S(1)} collective-permute-done((bf16[64,1280]{1,0:T(8,128)(2,1)S(1)}, bf16[64,1280]{1,0:T(8,128)(2,1)S(1)}, u32[]{:S(2)}, u32[]{:S(2)}) %collective-permute-start) | collective-permute-done | bytes 163872 | tf_op jit(solution)/shard_map/ppermute | solution.py:81
  18.4 1.5 %collective-permute-start.2 = (bf16[64,1280]{1,0:T(8,128)(2,1)S(1)}, bf16[64,1280]{1,0:T(8,128)(2,1)S(1)}, u32[]{:S(2)}, u32[]{:S(2)}) collective-permute-start(bf16[64,1280]{1,0:T(8,128)(2,1)S(1)} %get-tuple-element.75), channel_id=1, source_target_pairs={{0,2},{1,3},{2,0},{3,1},{4,6},{5,7},{6,4},{7,5},{8,10},{9,11},{10,... | collective-permute-start | bytes 491528 | tf_op jit(solution)/shard_map/ppermute | solution.py:89
  20.5 3.0 %collective-permute-done.10 = bf16[64,1280]{1,0:T(8,128)(2,1)S(1)} collective-permute-done((bf16[64,1280]{1,0:T(8,128)(2,1)S(1)}, bf16[64,1280]{1,0:T(8,128)(2,1)S(1)}, u32[]{:S(2)}, u32[]{:S(2)}) %collective-permute-start.10) | collective-permute-done | bytes 163872 | tf_op jit(solution)/shard_map/ppermute | solution.py:81
  23.5 1.5 %collective-permute-start.11 = (bf16[64,1280]{1,0:T(8,128)(2,1)S(1)}, bf16[64,1280]{1,0:T(8,128)(2,1)S(1)}, u32[]{:S(2)}, u32[]{:S(2)}) collective-permute-start(bf16[64,1280]{1,0:T(8,128)(2,1)S(1)} %collective-permute-done.10), channel_id=1, source_target_pairs={{0,2},{1,3},{2,0},{3,1},{4,6},{5,7},{6,4},{7,5},{8,10},{9,11},{10,... | collective-permute-start | bytes 491528 | tf_op jit(solution)/shard_map/ppermute | solution.py:89
  26.2 1.4 %collective-permute-start.3 = (bf16[64,1408]{1,0:T(8,128)(2,1)}, bf16[64,1408]{1,0:T(8,128)(2,1)S(1)}, u32[]{:S(2)}, u32[]{:S(2)}) collective-permute-start(bf16[64,1408]{1,0:T(8,128)(2,1)} %shard_map.102), channel_id=1, source_target_pairs={{0,2},{1,3},{2,0},{3,1},{4,6},{5,7},{6,4},{7,5},{8,10},{9,11},{10,... | collective-permute-start | bytes 540680 | tf_op jit(solution)/shard_map/ppermute | solution.py:89
  27.7 0.9 pad_maximum_fusion.9
  29.1 3.5 %collective-permute-done.11 = bf16[64,1280]{1,0:T(8,128)(2,1)S(1)} collective-permute-done((bf16[64,1280]{1,0:T(8,128)(2,1)S(1)}, bf16[64,1280]{1,0:T(8,128)(2,1)S(1)}, u32[]{:S(2)}, u32[]{:S(2)}) %collective-permute-start.11) | collective-permute-done | bytes 163872 | tf_op jit(solution)/shard_map/ppermute | solution.py:89
  33.2 1.1 collective-permute-done.7
  38.8 6.0 %collective-permute-start.15 = (bf16[256,768]{1,0:T(8,128)(2,1)S(1)}, bf16[256,768]{1,0:T(8,128)(2,1)S(1)}, u32[]{:S(2)}, u32[]{:S(2)}) collective-permute-start(bf16[256,768]{1,0:T(8,128)(2,1)S(1)} %convert_element_type.88), channel_id=1, source_target_pairs={{0,16},{4,20},{24,8},{28,12},{1,17},{5,21},{25,9},{29,13},{2,18},{... | collective-permute-start | bytes 1179656 | tf_op jit(solution)/shard_map/ppermute | solution.py:122
  44.9 2.9 %collective-permute-done.13 = bf16[256,768]{1,0:T(8,128)(2,1)S(1)} collective-permute-done((bf16[256,768]{1,0:T(8,128)(2,1)S(1)}, bf16[256,768]{1,0:T(8,128)(2,1)S(1)}, u32[]{:S(2)}, u32[]{:S(2)}) %collective-permute-start.13) | collective-permute-done | bytes 393248 | tf_op jit(solution)/shard_map/ppermute | solution.py:122
  47.9 1.5 %collective-permute-start.16 = (bf16[256,768]{1,0:T(8,128)(2,1)S(1)}, bf16[256,768]{1,0:T(8,128)(2,1)S(1)}, u32[]{:S(2)}, u32[]{:S(2)}) collective-permute-start(bf16[256,768]{1,0:T(8,128)(2,1)S(1)} %fusion.18), channel_id=1, source_target_pairs={{16,0},{20,4},{24,16},{28,20},{8,24},{12,28},{0,8},{4,12},{17,1},{... | collective-permute-start | bytes 1179656 | tf_op jit(solution)/shard_map/ppermute | solution.py:122
  49.5 5.7 %collective-permute-done.15 = bf16[256,768]{1,0:T(8,128)(2,1)S(1)} collective-permute-done((bf16[256,768]{1,0:T(8,128)(2,1)S(1)}, bf16[256,768]{1,0:T(8,128)(2,1)S(1)}, u32[]{:S(2)}, u32[]{:S(2)}) %collective-permute-start.15) | collective-permute-done | bytes 393248 | tf_op jit(solution)/shard_map/ppermute | solution.py:122
  56.0 11.8 %collective-permute-done.16.refs_0_ = bf16[256,768]{1,0:T(8,128)(2,1)S(1)} collective-permute-done((bf16[256,768]{1,0:T(8,128)(2,1)S(1)}, bf16[256,768]{1,0:T(8,128)(2,1)S(1)}, u32[]{:S(2)}, u32[]{:S(2)}) %collective-permute-start.16) | collective-permute-done | bytes 393248 | tf_op jit(solution)/shard_map/ppermute | solution.py:122
  67.7 1.5 %shard_map.103 = (bf16[256,384]{1,0:T(8,128)(2,1)}, bf16[256,768]{1,0:T(8,128)(2,1)S(1)}) custom-call(s32[4]{0:T(128)S(1)} %broadcast_xor_fusion.order_ref, f32[256,768]{1,0:T(8,128)S(1)} %fusion.9.pre_ref, bf16[256,1]{1,0:T(8,128)(2,1)S(1)} %pad_maximum_fusion.17.prob_ref, bf16[256,384]{1,0:T(8,128)(2,1)S(1)} %copy-done, ...), custom_call_target="tpu_custom_call" | custom-call | flops 1966080 | bytes 2949120 | tf_op jit(solution)/shard_map/pallas_call | solution.py:61
  70.3 1.3 collective-permute-start.20
  71.6 0.9 collective-permute-start.21
  72.6 1.5 %collective-permute-start.18 = (bf16[64,1280]{1,0:T(8,128)(2,1)S(1)}, bf16[64,1280]{1,0:T(8,128)(2,1)S(1)}, u32[]{:S(2)}, u32[]{:S(2)}) collective-permute-start(bf16[64,1280]{1,0:T(8,128)(2,1)S(1)} %slice.260), channel_id=1, source_target_pairs={{0,2},{1,3},{2,0},{3,1},{4,6},{5,7},{6,4},{7,5},{8,10},{9,11},{10,... | collective-permute-start | bytes 491528 | tf_op jit(solution)/shard_map/ppermute | solution.py:89
  74.1 16.1 %collective-permute-done.19 = bf16[256,768]{1,0:T(8,128)(2,1)S(1)} collective-permute-done((bf16[256,768]{1,0:T(8,128)(2,1)S(1)}, bf16[256,768]{1,0:T(8,128)(2,1)S(1)}, u32[]{:S(2)}, u32[]{:S(2)}) %collective-permute-start.19) | collective-permute-done | bytes 393248 | tf_op jit(solution)/shard_map/ppermute | solution.py:122
  92.2 8.9 %collective-permute-done.22 = bf16[256,768]{1,0:T(8,128)(2,1)S(1)} collective-permute-done((bf16[256,768]{1,0:T(8,128)(2,1)S(1)}, bf16[256,768]{1,0:T(8,128)(2,1)S(1)}, u32[]{:S(2)}, u32[]{:S(2)}) %collective-permute-start.22) | collective-permute-done | bytes 393248 | tf_op jit(solution)/shard_map/ppermute | solution.py:122
  103.6 1.5 %collective-permute-start.27 = (bf16[64,1280]{1,0:T(8,128)(2,1)S(1)}, bf16[64,1280]{1,0:T(8,128)(2,1)S(1)}, u32[]{:S(2)}, u32[]{:S(2)}) collective-permute-start(bf16[64,1280]{1,0:T(8,128)(2,1)S(1)} %slice.257), channel_id=1, source_target_pairs={{0,2},{1,3},{2,0},{3,1},{4,6},{5,7},{6,4},{7,5},{8,10},{9,11},{10,... | collective-permute-start | bytes 491528 | tf_op jit(solution)/shard_map/ppermute | solution.py:89
  105.2 1.5 %collective-permute-start.30 = (bf16[640,768]{1,0:T(8,128)(2,1)S(1)}, bf16[640,768]{1,0:T(8,128)(2,1)S(1)}, u32[]{:S(2)}, u32[]{:S(2)}) collective-permute-start(bf16[640,768]{1,0:T(8,128)(2,1)S(1)} %add_convert_fusion), channel_id=1, source_target_pairs={{0,4},{4,0},{8,12},{12,8},{16,20},{20,16},{24,28},{28,24},{1,5},{5... | collective-permute-start | bytes 2949128 | tf_op jit(solution)/shard_map/ppermute | solution.py:85
  106.8 1.2 fusion
  108.8 1.5 %collective-permute-done.27 = bf16[64,1280]{1,0:T(8,128)(2,1)S(1)} collective-permute-done((bf16[64,1280]{1,0:T(8,128)(2,1)S(1)}, bf16[64,1280]{1,0:T(8,128)(2,1)S(1)}, u32[]{:S(2)}, u32[]{:S(2)}) %collective-permute-start.27) | collective-permute-done | bytes 163872 | tf_op jit(solution)/shard_map/ppermute | solution.py:89
  110.4 7.4 %collective-permute-done.24 = bf16[128,1280]{1,0:T(8,128)(2,1)S(1)} collective-permute-done((bf16[128,1280]{1,0:T(8,128)(2,1)S(1)}, bf16[128,1280]{1,0:T(8,128)(2,1)S(1)}, u32[]{:S(2)}, u32[]{:S(2)}) %collective-permute-start.24) | collective-permute-done | bytes 327712 | tf_op jit(solution)/shard_map/ppermute | solution.py:89
  118.3 2.1 %collective-permute-done.28 = bf16[64,1280]{1,0:T(8,128)(2,1)S(1)} collective-permute-done((bf16[64,1280]{1,0:T(8,128)(2,1)S(1)}, bf16[64,1280]{1,0:T(8,128)(2,1)S(1)}, u32[]{:S(2)}, u32[]{:S(2)}) %collective-permute-start.28) | collective-permute-done | bytes 163872 | tf_op jit(solution)/shard_map/ppermute | solution.py:81
  120.8 8.2 %collective-permute-done.30 = bf16[640,768]{1,0:T(8,128)(2,1)S(1)} collective-permute-done((bf16[640,768]{1,0:T(8,128)(2,1)S(1)}, bf16[640,768]{1,0:T(8,128)(2,1)S(1)}, u32[]{:S(2)}, u32[]{:S(2)}) %collective-permute-start.30) | collective-permute-done | bytes 983072 | tf_op jit(solution)/shard_map/ppermute | solution.py:85
  129.0 1.5 %slice_add_fusion = (f32[640,384]{1,0:T(8,128)}, f32[640,384]{1,0:T(8,128)}) fusion(f32[640,768]{1,0:T(8,128)S(1)} %fusion, bf16[640,768]{1,0:T(8,128)(2,1)S(1)} %collective-permute-done.30), kind=kLoop, calls=%fused_computation.18 | loop fusion | flops 983040 | bytes 4915200 | tf_op jit(solution)/shard_map/add | solution.py:256
  130.7 4.0 %convolution_convert_fusion = bf16[512,5120]{1,0:T(8,128)(2,1)} fusion(bf16[64,5120]{1,0:T(8,128)(2,1)S(1)} %slice_dynamic-update-slice_fusion.2, s32[64]{0:T(128)S(1)} %copy-done.6), kind=kOutput, calls=%fused_computation | convolution fusion | flops 338198528 | bytes 5898496 | tf_op jit(solution)/shard_map/dot_general | solution.py:269
  (120 shorter events, 17.9 us)
Async XLA Ops:
  4.5 10.2 %collective-permute-start.1 = (bf16[64,1280]{1,0:T(8,128)(2,1)S(1)}, bf16[64,1280]{1,0:T(8,128)(2,1)S(1)}, u32[]{:S(2)}, u32[]{:S(2)}) collective-permute-start(bf16[64,1280]{1,0:T(8,128)(2,1)S(1)} %pad_maximum_fusion.15), channel_id=1, source_target_pairs={{0,24},{4,28},{8,16},{12,20},{16,8},{20,12},{24,0},{28,4},{1,25},{... | collective-permute-start | bytes 491528 | tf_op jit(solution)/shard_map/ppermute | solution.py:81
  9.6 8.8 %collective-permute-start = (bf16[64,1280]{1,0:T(8,128)(2,1)S(1)}, bf16[64,1280]{1,0:T(8,128)(2,1)S(1)}, u32[]{:S(2)}, u32[]{:S(2)}) collective-permute-start(bf16[64,1280]{1,0:T(8,128)(2,1)S(1)} %pad_maximum_fusion.14), channel_id=1, source_target_pairs={{0,8},{4,12},{8,0},{12,4},{16,24},{20,28},{24,16},{28,20},{1,9},{5... | collective-permute-start | bytes 491528 | tf_op jit(solution)/shard_map/ppermute | solution.py:81
  9.7 22.9 %collective-permute-start.9 = (bf16[640,384]{1,0:T(8,128)(2,1)S(1)}, bf16[640,384]{1,0:T(8,128)(2,1)S(1)}, u32[]{:S(2)}, u32[]{:S(2)}) collective-permute-start(bf16[640,384]{1,0:T(8,128)(2,1)S(1)} %copy-done.4), channel_id=1, source_target_pairs={{0,4},{4,0},{8,12},{12,8},{16,20},{20,16},{24,28},{28,24},{1,5},{5... | collective-permute-start | bytes 1474568 | tf_op jit(solution)/shard_map/ppermute | solution.py:85
  11.3 21.7 %collective-permute-start.8 = (bf16[640,384]{1,0:T(8,128)(2,1)S(1)}, bf16[640,384]{1,0:T(8,128)(2,1)S(1)}, u32[]{:S(2)}, u32[]{:S(2)}) collective-permute-start(bf16[640,384]{1,0:T(8,128)(2,1)S(1)} %copy-done.5), channel_id=1, source_target_pairs={{0,4},{4,0},{8,12},{12,8},{16,20},{20,16},{24,28},{28,24},{1,5},{5... | collective-permute-start | bytes 1474568 | tf_op jit(solution)/shard_map/ppermute | solution.py:85
  11.8 11.7 %collective-permute-start.10 = (bf16[64,1280]{1,0:T(8,128)(2,1)S(1)}, bf16[64,1280]{1,0:T(8,128)(2,1)S(1)}, u32[]{:S(2)}, u32[]{:S(2)}) collective-permute-start(bf16[64,1280]{1,0:T(8,128)(2,1)S(1)} %pad_maximum_fusion.16), channel_id=1, source_target_pairs={{0,16},{4,20},{8,24},{12,28},{16,0},{20,4},{24,8},{28,12},{1,17},{... | collective-permute-start | bytes 491528 | tf_op jit(solution)/shard_map/ppermute | solution.py:81
  18.4 7.1 %collective-permute-start.2 = (bf16[64,1280]{1,0:T(8,128)(2,1)S(1)}, bf16[64,1280]{1,0:T(8,128)(2,1)S(1)}, u32[]{:S(2)}, u32[]{:S(2)}) collective-permute-start(bf16[64,1280]{1,0:T(8,128)(2,1)S(1)} %get-tuple-element.75), channel_id=1, source_target_pairs={{0,2},{1,3},{2,0},{3,1},{4,6},{5,7},{6,4},{7,5},{8,10},{9,11},{10,... | collective-permute-start | bytes 491528 | tf_op jit(solution)/shard_map/ppermute | solution.py:89
  20.0 9.1 %collective-permute-start.6 = (bf16[64,1280]{1,0:T(8,128)(2,1)S(1)}, bf16[64,1280]{1,0:T(8,128)(2,1)S(1)}, u32[]{:S(2)}, u32[]{:S(2)}) collective-permute-start(bf16[64,1280]{1,0:T(8,128)(2,1)S(1)} %get-tuple-element.74), channel_id=1, source_target_pairs={{0,2},{1,3},{2,0},{3,1},{4,6},{5,7},{6,4},{7,5},{8,10},{9,11},{10,... | collective-permute-start | bytes 491528 | tf_op jit(solution)/shard_map/ppermute | solution.py:89
  23.5 9.1 %collective-permute-start.11 = (bf16[64,1280]{1,0:T(8,128)(2,1)S(1)}, bf16[64,1280]{1,0:T(8,128)(2,1)S(1)}, u32[]{:S(2)}, u32[]{:S(2)}) collective-permute-start(bf16[64,1280]{1,0:T(8,128)(2,1)S(1)} %collective-permute-done.10), channel_id=1, source_target_pairs={{0,2},{1,3},{2,0},{3,1},{4,6},{5,7},{6,4},{7,5},{8,10},{9,11},{10,... | collective-permute-start | bytes 491528 | tf_op jit(solution)/shard_map/ppermute | solution.py:89
  26.2 9.9 %collective-permute-start.3 = (bf16[64,1408]{1,0:T(8,128)(2,1)}, bf16[64,1408]{1,0:T(8,128)(2,1)S(1)}, u32[]{:S(2)}, u32[]{:S(2)}) collective-permute-start(bf16[64,1408]{1,0:T(8,128)(2,1)} %shard_map.102), channel_id=1, source_target_pairs={{0,2},{1,3},{2,0},{3,1},{4,6},{5,7},{6,4},{7,5},{8,10},{9,11},{10,... | collective-permute-start | bytes 540680 | tf_op jit(solution)/shard_map/ppermute | solution.py:89
  29.1 5.9 %collective-permute-start.5 = (bf16[128,1280]{1,0:T(8,128)(2,1)S(1)}, bf16[128,1280]{1,0:T(8,128)(2,1)S(1)}, u32[]{:S(2)}, u32[]{:S(2)}) collective-permute-start(bf16[128,1280]{1,0:T(8,128)(2,1)S(1)} %pad_maximum_fusion.9), channel_id=1, source_target_pairs={{0,1},{1,0},{2,3},{3,2},{4,5},{5,4},{6,7},{7,6},{8,9},{9,8},{10,11... | collective-permute-start | bytes 983048 | tf_op jit(solution)/shard_map/ppermute | solution.py:89
  32.6 1.6 %collective-permute-start.7 = (bf16[128,1280]{1,0:T(8,128)(2,1)S(1)}, bf16[128,1280]{1,0:T(8,128)(2,1)S(1)}, u32[]{:S(2)}, u32[]{:S(2)}) collective-permute-start(bf16[128,1280]{1,0:T(8,128)(2,1)S(1)} %pad_maximum_fusion.10), channel_id=1, source_target_pairs={{0,1},{1,0},{2,3},{3,2},{4,5},{5,4},{6,7},{7,6},{8,9},{9,8},{10,11... | collective-permute-start | bytes 983048 | tf_op jit(solution)/shard_map/ppermute | solution.py:89
  35.9 2.1 %collective-permute-start.12 = (bf16[128,1280]{1,0:T(8,128)(2,1)S(1)}, bf16[128,1280]{1,0:T(8,128)(2,1)S(1)}, u32[]{:S(2)}, u32[]{:S(2)}) collective-permute-start(bf16[128,1280]{1,0:T(8,128)(2,1)S(1)} %pad_maximum_fusion.11), channel_id=1, source_target_pairs={{0,1},{1,0},{2,3},{3,2},{4,5},{5,4},{6,7},{7,6},{8,9},{9,8},{10,11... | collective-permute-start | bytes 983048 | tf_op jit(solution)/shard_map/ppermute | solution.py:89
  36.2 8.6 %collective-permute-start.4 = (bf16[128,1408]{1,0:T(8,128)(2,1)S(1)}, bf16[128,1408]{1,0:T(8,128)(2,1)S(1)}, u32[]{:S(2)}, u32[]{:S(2)}) collective-permute-start(bf16[128,1408]{1,0:T(8,128)(2,1)S(1)} %pad_maximum_fusion.8), channel_id=1, source_target_pairs={{0,1},{1,0},{2,3},{3,2},{4,5},{5,4},{6,7},{7,6},{8,9},{9,8},{10,11... | collective-permute-start | bytes 1081352 | tf_op jit(solution)/shard_map/ppermute | solution.py:89
  36.6 11.2 %collective-permute-start.13 = (bf16[256,768]{1,0:T(8,128)(2,1)S(1)}, bf16[256,768]{1,0:T(8,128)(2,1)S(1)}, u32[]{:S(2)}, u32[]{:S(2)}) collective-permute-start(bf16[256,768]{1,0:T(8,128)(2,1)S(1)} %convolution_convert_fusion.3), channel_id=1, source_target_pairs={{0,8},{4,12},{8,0},{12,4},{16,24},{20,28},{24,16},{28,20},{1,9},{5... | collective-permute-start | bytes 1179656 | tf_op jit(solution)/shard_map/ppermute | solution.py:122
  37.3 12.2 %collective-permute-start.14 = (bf16[256,768]{1,0:T(8,128)(2,1)S(1)}, bf16[256,768]{1,0:T(8,128)(2,1)S(1)}, u32[]{:S(2)}, u32[]{:S(2)}) collective-permute-start(bf16[256,768]{1,0:T(8,128)(2,1)S(1)} %convolution_convert_fusion.2), channel_id=1, source_target_pairs={{8,16},{12,20},{16,8},{20,12},{9,17},{13,21},{17,9},{21,13},{10,18... | collective-permute-start | bytes 1179656 | tf_op jit(solution)/shard_map/ppermute | solution.py:122
  38.8 16.4 %collective-permute-start.15 = (bf16[256,768]{1,0:T(8,128)(2,1)S(1)}, bf16[256,768]{1,0:T(8,128)(2,1)S(1)}, u32[]{:S(2)}, u32[]{:S(2)}) collective-permute-start(bf16[256,768]{1,0:T(8,128)(2,1)S(1)} %convert_element_type.88), channel_id=1, source_target_pairs={{0,16},{4,20},{24,8},{28,12},{1,17},{5,21},{25,9},{29,13},{2,18},{... | collective-permute-start | bytes 1179656 | tf_op jit(solution)/shard_map/ppermute | solution.py:122
  47.9 19.8 %collective-permute-start.16 = (bf16[256,768]{1,0:T(8,128)(2,1)S(1)}, bf16[256,768]{1,0:T(8,128)(2,1)S(1)}, u32[]{:S(2)}, u32[]{:S(2)}) collective-permute-start(bf16[256,768]{1,0:T(8,128)(2,1)S(1)} %fusion.18), channel_id=1, source_target_pairs={{16,0},{20,4},{24,16},{28,20},{8,24},{12,28},{0,8},{4,12},{17,1},{... | collective-permute-start | bytes 1179656 | tf_op jit(solution)/shard_map/ppermute | solution.py:122
  49.5 18.2 %copy-start = (bf16[256,384]{1,0:T(8,128)(2,1)S(1)}, bf16[256,384]{1,0:T(8,128)(2,1)}, u32[]{:S(2)}) copy-start(bf16[256,384]{1,0:T(8,128)(2,1)} %cot_ref.1) | copy-start | bytes 589828
  70.0 2.5 %collective-permute-start.17 = (bf16[128,1280]{1,0:T(8,128)(2,1)S(1)}, bf16[128,1280]{1,0:T(8,128)(2,1)S(1)}, u32[]{:S(2)}, u32[]{:S(2)}) collective-permute-start(bf16[128,1280]{1,0:T(8,128)(2,1)S(1)} %slice.256), channel_id=1, source_target_pairs={{0,1},{1,0},{2,3},{3,2},{4,5},{5,4},{6,7},{7,6},{8,9},{9,8},{10,11... | collective-permute-start | bytes 983048 | tf_op jit(solution)/shard_map/ppermute | solution.py:89
  70.2 20.0 %collective-permute-start.19 = (bf16[256,768]{1,0:T(8,128)(2,1)S(1)}, bf16[256,768]{1,0:T(8,128)(2,1)S(1)}, u32[]{:S(2)}, u32[]{:S(2)}) collective-permute-start(bf16[256,768]{1,0:T(8,128)(2,1)S(1)} %get-tuple-element.38), channel_id=1, source_target_pairs={{0,16},{4,20},{16,24},{20,28},{24,8},{28,12},{8,0},{12,4},{1,17},{... | collective-permute-start | bytes 1179656 | tf_op jit(solution)/shard_map/ppermute | solution.py:122
  70.3 20.1 %collective-permute-start.20 = (bf16[256,768]{1,0:T(8,128)(2,1)S(1)}, bf16[256,768]{1,0:T(8,128)(2,1)S(1)}, u32[]{:S(2)}, u32[]{:S(2)}) collective-permute-start(bf16[256,768]{1,0:T(8,128)(2,1)S(1)} %get-tuple-element.38), channel_id=1, source_target_pairs={{16,0},{20,4},{8,24},{12,28},{17,1},{21,5},{9,25},{13,29},{18,2},{... | collective-permute-start | bytes 1179656 | tf_op jit(solution)/shard_map/ppermute | solution.py:122
  71.6 20.4 %collective-permute-start.21 = (bf16[256,768]{1,0:T(8,128)(2,1)S(1)}, bf16[256,768]{1,0:T(8,128)(2,1)S(1)}, u32[]{:S(2)}, u32[]{:S(2)}) collective-permute-start(bf16[256,768]{1,0:T(8,128)(2,1)S(1)} %get-tuple-element.38), channel_id=1, source_target_pairs={{8,16},{12,20},{16,8},{20,12},{9,17},{13,21},{17,9},{21,13},{10,18... | collective-permute-start | bytes 1179656 | tf_op jit(solution)/shard_map/ppermute | solution.py:122
  72.6 19.5 %collective-permute-start.18 = (bf16[64,1280]{1,0:T(8,128)(2,1)S(1)}, bf16[64,1280]{1,0:T(8,128)(2,1)S(1)}, u32[]{:S(2)}, u32[]{:S(2)}) collective-permute-start(bf16[64,1280]{1,0:T(8,128)(2,1)S(1)} %slice.260), channel_id=1, source_target_pairs={{0,2},{1,3},{2,0},{3,1},{4,6},{5,7},{6,4},{7,5},{8,10},{9,11},{10,... | collective-permute-start | bytes 491528 | tf_op jit(solution)/shard_map/ppermute | solution.py:89
  90.3 10.8 %collective-permute-start.22 = (bf16[256,768]{1,0:T(8,128)(2,1)S(1)}, bf16[256,768]{1,0:T(8,128)(2,1)S(1)}, u32[]{:S(2)}, u32[]{:S(2)}) collective-permute-start(bf16[256,768]{1,0:T(8,128)(2,1)S(1)} %broadcast_select_fusion.2), channel_id=1, source_target_pairs={{0,8},{4,12},{8,0},{12,4},{16,24},{20,28},{24,16},{28,20},{1,9},{5... | collective-permute-start | bytes 1179656 | tf_op jit(solution)/shard_map/ppermute | solution.py:122
  92.0 11.6 %collective-permute-start.26 = (bf16[128,1280]{1,0:T(8,128)(2,1)S(1)}, bf16[128,1280]{1,0:T(8,128)(2,1)S(1)}, u32[]{:S(2)}, u32[]{:S(2)}) collective-permute-start(bf16[128,1280]{1,0:T(8,128)(2,1)S(1)} %slice.253), channel_id=1, source_target_pairs={{0,1},{1,0},{2,3},{3,2},{4,5},{5,4},{6,7},{7,6},{8,9},{9,8},{10,11... | collective-permute-start | bytes 983048 | tf_op jit(solution)/shard_map/ppermute | solution.py:89
  103.5 4.5 %collective-permute-start.23 = (bf16[256,1280]{1,0:T(8,128)(2,1)S(1)}, bf16[256,1280]{1,0:T(8,128)(2,1)S(1)}, u32[]{:S(2)}, u32[]{:S(2)}) collective-permute-start(bf16[256,1280]{1,0:T(8,128)(2,1)S(1)} %pad_maximum_fusion.7), channel_id=1, source_target_pairs={{0,1},{1,0},{2,3},{3,2},{4,5},{5,4},{6,7},{7,6},{8,9},{9,8},{10,11... | collective-permute-start | bytes 1966088 | tf_op jit(solution)/shard_map/ppermute | solution.py:89
  103.6 6.7 %collective-permute-start.27 = (bf16[64,1280]{1,0:T(8,128)(2,1)S(1)}, bf16[64,1280]{1,0:T(8,128)(2,1)S(1)}, u32[]{:S(2)}, u32[]{:S(2)}) collective-permute-start(bf16[64,1280]{1,0:T(8,128)(2,1)S(1)} %slice.257), channel_id=1, source_target_pairs={{0,2},{1,3},{2,0},{3,1},{4,6},{5,7},{6,4},{7,5},{8,10},{9,11},{10,... | collective-permute-start | bytes 491528 | tf_op jit(solution)/shard_map/ppermute | solution.py:89
  105.2 23.9 %collective-permute-start.30 = (bf16[640,768]{1,0:T(8,128)(2,1)S(1)}, bf16[640,768]{1,0:T(8,128)(2,1)S(1)}, u32[]{:S(2)}, u32[]{:S(2)}) collective-permute-start(bf16[640,768]{1,0:T(8,128)(2,1)S(1)} %add_convert_fusion), channel_id=1, source_target_pairs={{0,4},{4,0},{8,12},{12,8},{16,20},{20,16},{24,28},{28,24},{1,5},{5... | collective-permute-start | bytes 2949128 | tf_op jit(solution)/shard_map/ppermute | solution.py:85
  108.2 9.6 %collective-permute-start.24 = (bf16[128,1280]{1,0:T(8,128)(2,1)S(1)}, bf16[128,1280]{1,0:T(8,128)(2,1)S(1)}, u32[]{:S(2)}, u32[]{:S(2)}) collective-permute-start(bf16[128,1280]{1,0:T(8,128)(2,1)S(1)} %pad_maximum_fusion.12), channel_id=1, source_target_pairs={{0,2},{1,3},{2,0},{3,1},{4,6},{5,7},{6,4},{7,5},{8,10},{9,11},{10,... | collective-permute-start | bytes 983048 | tf_op jit(solution)/shard_map/ppermute | solution.py:89
  110.3 10.1 %collective-permute-start.28 = (bf16[64,1280]{1,0:T(8,128)(2,1)S(1)}, bf16[64,1280]{1,0:T(8,128)(2,1)S(1)}, u32[]{:S(2)}, u32[]{:S(2)}) collective-permute-start(bf16[64,1280]{1,0:T(8,128)(2,1)S(1)} %fusion.19), channel_id=1, source_target_pairs={{0,16},{4,20},{8,24},{12,28},{16,0},{20,4},{24,8},{28,12},{1,17},{... | collective-permute-start | bytes 491528 | tf_op jit(solution)/shard_map/ppermute | solution.py:81
  118.0 12.5 %collective-permute-start.25 = (bf16[64,1280]{1,0:T(8,128)(2,1)S(1)}, bf16[64,1280]{1,0:T(8,128)(2,1)S(1)}, u32[]{:S(2)}, u32[]{:S(2)}) collective-permute-start(bf16[64,1280]{1,0:T(8,128)(2,1)S(1)} %broadcast_select_fusion.4), channel_id=1, source_target_pairs={{0,8},{4,12},{8,0},{12,4},{16,24},{20,28},{24,16},{28,20},{1,9},{5... | collective-permute-start | bytes 491528 | tf_op jit(solution)/shard_map/ppermute | solution.py:81
  120.4 10.2 %collective-permute-start.29 = (bf16[64,1280]{1,0:T(8,128)(2,1)S(1)}, bf16[64,1280]{1,0:T(8,128)(2,1)S(1)}, u32[]{:S(2)}, u32[]{:S(2)}) collective-permute-start(bf16[64,1280]{1,0:T(8,128)(2,1)S(1)} %get-tuple-element.52), channel_id=1, source_target_pairs={{0,24},{4,28},{8,16},{12,20},{16,8},{20,12},{24,0},{28,4},{1,25},{... | collective-permute-start | bytes 491528 | tf_op jit(solution)/shard_map/ppermute | solution.py:81
  (8 other events, 48.6 us)

commit v19 on v15

--- a/solution.py
+++ b/solution.py
@@ -161,7 +161,7 @@
             crossed = outer_pairs(near, middle)
             x_chunks[2] = gather_etp(got[2], [[], [near]])
             x_chunks[0] = gather_etp(after(got[0], near))
-            two = after(multiply(2, swapped, crossed), swapped)
+            two = after(multiply(2, swapped), swapped)
             inwards = outer_pairs(two.astype(BF16), inward)
             relayed = pick(near, (after(two, swapped) + swapped.astype(F32)).astype(BF16))
             cycled = outer_pairs(relayed, back)

time: 133 us -> 133 us (level)
  starting transfers between devices: 36.4 us -> 33.8 us
  waiting for transfers between devices: 74.1 us -> 76.6 us
    ppermute x8, starting transfers between devices: 12.7 us -> 11.4 us  [outer_pairs(): return lax.ppermute(value, 'dp', pairs)]
where the time goes in v19:
time: 133 us
  waiting for transfers between devices  76.6 us (58%)
  starting transfers between devices  33.8 us (25%)
  matrix products  15.8 us (12%)
  other arithmetic  3.17 us (2%)
  Pallas kernels  1.51 us (1%)
  between operations  1.38 us (1%)
    ppermute x8, waiting for transfers between devices, outer_pairs(): return lax.ppermute(value, 'dp', pairs)  40.2 us
    ppermute x16, waiting for transfers between devices, over_etp(): return lax.ppermute(value, 'etp', pairs)  20.5 us
    ppermute x8, starting transfers between devices, outer_pairs(): return lax.ppermute(value, 'dp', pairs)  11.4 us
    ppermute x16, starting transfers between devices, over_etp(): return lax.ppermute(value, 'etp', pairs)  11 us
    ppermute x3, waiting for transfers between devices, over_inner(): return lax.ppermute(value, 'dp', pairs)  8.29 us
    ppermute x6, starting transfers between devices, over_outer(): return lax.ppermute(value, 'dp', pairs)  7.89 us
    ppermute x6, waiting for transfers between devices, over_outer(): return lax.ppermute(value, 'dp', pairs)  7.57 us
    dot_general x1, matrix products, shards(): lax.dot_general(onehot, dx, (((0,), (0,)), ((), ())), preferred_element_t...  3.99 us
  transfers between devices with their start and end apart: 33, of which 18 were waited for; matrix products, arithmetic and copies ran while one was open for 9% of the time, Pallas kernels for 0%

profile of v19, /device:TPU:0, one launch (start us, length us, event | category | flops | bytes accessed | tf_op | source)
XLA Modules:
  0.0 133.3 jit_solution(11020361918164519652)
XLA Ops:
  0.7 3.6 %convolution_convert_fusion.1 = bf16[64,5120]{1,0:T(8,128)(2,1)S(1)} fusion(bf16[512,5120]{1,0:T(8,128)(2,1)} %param.7, s32[64]{0:T(128)} %param.8), kind=kOutput, calls=%fused_computation.1 | convolution fusion | flops 335904768 | bytes 5898496 | tf_op jit(solution)/shard_map/dot_general | solution.py:136
  4.5 5.1 %collective-permute-start.1 = (bf16[64,1280]{1,0:T(8,128)(2,1)S(1)}, bf16[64,1280]{1,0:T(8,128)(2,1)S(1)}, u32[]{:S(2)}, u32[]{:S(2)}) collective-permute-start(bf16[64,1280]{1,0:T(8,128)(2,1)S(1)} %pad_maximum_fusion.15), channel_id=1, source_target_pairs={{0,24},{4,28},{8,16},{12,20},{16,8},{20,12},{24,0},{28,4},{1,25},{... | collective-permute-start | bytes 491528 | tf_op jit(solution)/shard_map/ppermute | solution.py:69
  9.7 1.6 %collective-permute-start.7 = (bf16[640,384]{1,0:T(8,128)(2,1)S(1)}, bf16[640,384]{1,0:T(8,128)(2,1)S(1)}, u32[]{:S(2)}, u32[]{:S(2)}) collective-permute-start(bf16[640,384]{1,0:T(8,128)(2,1)S(1)} %copy-done.1), channel_id=1, source_target_pairs={{0,4},{4,0},{8,12},{12,8},{16,20},{20,16},{24,28},{28,24},{1,5},{5... | collective-permute-start | bytes 1474568 | tf_op jit(solution)/shard_map/ppermute | solution.py:73
  11.8 1.5 %collective-permute-start.16 = (bf16[64]{0:T(256)(128)(2,1)S(1)}, bf16[64]{0:T(256)(128)(2,1)S(1)}, u32[]{:S(2)}, u32[]{:S(2)}) collective-permute-start(bf16[64]{0:T(256)(128)(2,1)S(1)} %copy-done.4), channel_id=1, source_target_pairs={{0,2},{1,3},{2,0},{3,1},{4,6},{5,7},{6,4},{7,5},{8,10},{9,11},{10,... | collective-permute-start | bytes 392 | tf_op jit(solution)/shard_map/ppermute | solution.py:77
  13.4 2.0 %collective-permute-done.16 = bf16[64]{0:T(256)(128)(2,1)S(1)} collective-permute-done((bf16[64]{0:T(256)(128)(2,1)S(1)}, bf16[64]{0:T(256)(128)(2,1)S(1)}, u32[]{:S(2)}, u32[]{:S(2)}) %collective-permute-start.16) | collective-permute-done | bytes 160 | tf_op jit(solution)/shard_map/ppermute | solution.py:77
  16.0 2.6 %collective-permute-done = bf16[64,1280]{1,0:T(8,128)(2,1)S(1)} collective-permute-done((bf16[64,1280]{1,0:T(8,128)(2,1)S(1)}, bf16[64,1280]{1,0:T(8,128)(2,1)S(1)}, u32[]{:S(2)}, u32[]{:S(2)}) %collective-permute-start) | collective-permute-done | bytes 163872 | tf_op jit(solution)/shard_map/ppermute | solution.py:69
  18.6 1.6 %collective-permute-start.2 = (bf16[64,1280]{1,0:T(8,128)(2,1)S(1)}, bf16[64,1280]{1,0:T(8,128)(2,1)S(1)}, u32[]{:S(2)}, u32[]{:S(2)}) collective-permute-start(bf16[64,1280]{1,0:T(8,128)(2,1)S(1)} %get-tuple-element.79), channel_id=1, source_target_pairs={{0,2},{1,3},{2,0},{3,1},{4,6},{5,7},{6,4},{7,5},{8,10},{9,11},{10,... | collective-permute-start | bytes 491528 | tf_op jit(solution)/shard_map/ppermute | solution.py:77
  21.0 3.1 %collective-permute-done.10 = bf16[64,1280]{1,0:T(8,128)(2,1)S(1)} collective-permute-done((bf16[64,1280]{1,0:T(8,128)(2,1)S(1)}, bf16[64,1280]{1,0:T(8,128)(2,1)S(1)}, u32[]{:S(2)}, u32[]{:S(2)}) %collective-permute-start.10) | collective-permute-done | bytes 163872 | tf_op jit(solution)/shard_map/ppermute | solution.py:69
  24.1 1.5 %collective-permute-start.11 = (bf16[64,1280]{1,0:T(8,128)(2,1)S(1)}, bf16[64,1280]{1,0:T(8,128)(2,1)S(1)}, u32[]{:S(2)}, u32[]{:S(2)}) collective-permute-start(bf16[64,1280]{1,0:T(8,128)(2,1)S(1)} %collective-permute-done.10), channel_id=1, source_target_pairs={{0,2},{1,3},{2,0},{3,1},{4,6},{5,7},{6,4},{7,5},{8,10},{9,11},{10,... | collective-permute-start | bytes 491528 | tf_op jit(solution)/shard_map/ppermute | solution.py:77
  25.8 3.4 %collective-permute-done.4 = bf16[64,1280]{1,0:T(8,128)(2,1)S(1)} collective-permute-done((bf16[64,1280]{1,0:T(8,128)(2,1)S(1)}, bf16[64,1280]{1,0:T(8,128)(2,1)S(1)}, u32[]{:S(2)}, u32[]{:S(2)}) %collective-permute-start.4) | collective-permute-done | bytes 163872 | tf_op jit(solution)/shard_map/ppermute | solution.py:77
  29.3 2.5 %collective-permute-done.11 = bf16[64,1280]{1,0:T(8,128)(2,1)S(1)} collective-permute-done((bf16[64,1280]{1,0:T(8,128)(2,1)S(1)}, bf16[64,1280]{1,0:T(8,128)(2,1)S(1)}, u32[]{:S(2)}, u32[]{:S(2)}) %collective-permute-start.11) | collective-permute-done | bytes 163872 | tf_op jit(solution)/shard_map/ppermute | solution.py:77
  33.9 1.7 %collective-permute-start.13 = (bf16[256,768]{1,0:T(8,128)(2,1)S(1)}, bf16[256,768]{1,0:T(8,128)(2,1)S(1)}, u32[]{:S(2)}, u32[]{:S(2)}) collective-permute-start(bf16[256,768]{1,0:T(8,128)(2,1)S(1)} %convolution_convert_fusion.3), channel_id=1, source_target_pairs={{0,8},{4,12},{8,0},{12,4},{16,24},{20,28},{24,16},{28,20},{1,9},{5... | collective-permute-start | bytes 1179656 | tf_op jit(solution)/shard_map/ppermute | solution.py:108
  37.1 1.6 %collective-permute-start.8 = (bf16[64,1280]{1,0:T(8,128)(2,1)S(1)}, bf16[64,1280]{1,0:T(8,128)(2,1)S(1)}, u32[]{:S(2)}, u32[]{:S(2)}) collective-permute-start(bf16[64,1280]{1,0:T(8,128)(2,1)S(1)} %pad_maximum_fusion.13), channel_id=1, source_target_pairs={{0,2},{1,3},{2,0},{3,1},{4,6},{5,7},{6,4},{7,5},{8,10},{9,11},{10,... | collective-permute-start | bytes 491528 | tf_op jit(solution)/shard_map/ppermute | solution.py:77
  38.7 3.7 %collective-permute-done.8 = bf16[64,1280]{1,0:T(8,128)(2,1)S(1)} collective-permute-done((bf16[64,1280]{1,0:T(8,128)(2,1)S(1)}, bf16[64,1280]{1,0:T(8,128)(2,1)S(1)}, u32[]{:S(2)}, u32[]{:S(2)}) %collective-permute-start.8) | collective-permute-done | bytes 163872 | tf_op jit(solution)/shard_map/ppermute | solution.py:77
  44.4 4.0 %collective-permute-start.15 = (bf16[256,768]{1,0:T(8,128)(2,1)S(1)}, bf16[256,768]{1,0:T(8,128)(2,1)S(1)}, u32[]{:S(2)}, u32[]{:S(2)}) collective-permute-start(bf16[256,768]{1,0:T(8,128)(2,1)S(1)} %convert_element_type.88), channel_id=1, source_target_pairs={{0,16},{4,20},{24,8},{28,12},{1,17},{5,21},{25,9},{29,13},{2,18},{... | collective-permute-start | bytes 1179656 | tf_op jit(solution)/shard_map/ppermute | solution.py:108
  48.6 9.2 %collective-permute-done.15 = bf16[256,768]{1,0:T(8,128)(2,1)S(1)} collective-permute-done((bf16[256,768]{1,0:T(8,128)(2,1)S(1)}, bf16[256,768]{1,0:T(8,128)(2,1)S(1)}, u32[]{:S(2)}, u32[]{:S(2)}) %collective-permute-start.15) | collective-permute-done | bytes 393248 | tf_op jit(solution)/shard_map/ppermute | solution.py:108
  58.5 8.6 %collective-permute-done.18.refs_0_ = bf16[256,768]{1,0:T(8,128)(2,1)S(1)} collective-permute-done((bf16[256,768]{1,0:T(8,128)(2,1)S(1)}, bf16[256,768]{1,0:T(8,128)(2,1)S(1)}, u32[]{:S(2)}, u32[]{:S(2)}) %collective-permute-start.18) | collective-permute-done | bytes 393248 | tf_op jit(solution)/shard_map/ppermute | solution.py:108
  67.1 1.5 %shard_map.102 = (bf16[256,384]{1,0:T(8,128)(2,1)}, bf16[256,768]{1,0:T(8,128)(2,1)S(1)}) custom-call(s32[4]{0:T(128)S(1)} %broadcast_xor_fusion.order_ref, f32[256,768]{1,0:T(8,128)S(1)} %fusion.9.pre_ref, bf16[256,1]{1,0:T(8,128)(2,1)S(1)} %broadcast_in_dim.15.prob_ref, bf16[256,384]{1,0:T(8,128)(2,1)S(1)} %copy-done, ...), custom_call_target="tpu_custom_call" | custom-call | flops 1966080 | bytes 2949120 | tf_op jit(solution)/shard_map/pallas_call | solution.py:49
  70.3 1.3 collective-permute-start.22
  72.6 1.6 %collective-permute-start.20 = (bf16[64,1280]{1,0:T(8,128)(2,1)S(1)}, bf16[64,1280]{1,0:T(8,128)(2,1)S(1)}, u32[]{:S(2)}, u32[]{:S(2)}) collective-permute-start(bf16[64,1280]{1,0:T(8,128)(2,1)S(1)} %slice.251), channel_id=1, source_target_pairs={{0,2},{1,3},{2,0},{3,1},{4,6},{5,7},{6,4},{7,5},{8,10},{9,11},{10,... | collective-permute-start | bytes 491528 | tf_op jit(solution)/shard_map/ppermute | solution.py:77
  74.2 7.1 %collective-permute-done.21 = bf16[256,768]{1,0:T(8,128)(2,1)S(1)} collective-permute-done((bf16[256,768]{1,0:T(8,128)(2,1)S(1)}, bf16[256,768]{1,0:T(8,128)(2,1)S(1)}, u32[]{:S(2)}, u32[]{:S(2)}) %collective-permute-start.21) | collective-permute-done | bytes 393248 | tf_op jit(solution)/shard_map/ppermute | solution.py:108
  81.4 2.1 %collective-permute-start.24 = (bf16[256,768]{1,0:T(8,128)(2,1)S(1)}, bf16[256,768]{1,0:T(8,128)(2,1)S(1)}, u32[]{:S(2)}, u32[]{:S(2)}) collective-permute-start(bf16[256,768]{1,0:T(8,128)(2,1)S(1)} %broadcast_select_fusion.2), channel_id=1, source_target_pairs={{0,8},{4,12},{8,0},{12,4},{16,24},{20,28},{24,16},{28,20},{1,9},{5... | collective-permute-start | bytes 1179656 | tf_op jit(solution)/shard_map/ppermute | solution.py:108
  83.5 7.8 %collective-permute-done.22 = bf16[256,768]{1,0:T(8,128)(2,1)S(1)} collective-permute-done((bf16[256,768]{1,0:T(8,128)(2,1)S(1)}, bf16[256,768]{1,0:T(8,128)(2,1)S(1)}, u32[]{:S(2)}, u32[]{:S(2)}) %collective-permute-start.22) | collective-permute-done | bytes 393248 | tf_op jit(solution)/shard_map/ppermute | solution.py:108
  93.0 6.5 %collective-permute-done.24 = bf16[256,768]{1,0:T(8,128)(2,1)S(1)} collective-permute-done((bf16[256,768]{1,0:T(8,128)(2,1)S(1)}, bf16[256,768]{1,0:T(8,128)(2,1)S(1)}, u32[]{:S(2)}, u32[]{:S(2)}) %collective-permute-start.24) | collective-permute-done | bytes 393248 | tf_op jit(solution)/shard_map/ppermute | solution.py:108
  102.1 1.6 %collective-permute-start.29 = (bf16[64,1280]{1,0:T(8,128)(2,1)S(1)}, bf16[64,1280]{1,0:T(8,128)(2,1)S(1)}, u32[]{:S(2)}, u32[]{:S(2)}) collective-permute-start(bf16[64,1280]{1,0:T(8,128)(2,1)S(1)} %slice.248), channel_id=1, source_target_pairs={{0,2},{1,3},{2,0},{3,1},{4,6},{5,7},{6,4},{7,5},{8,10},{9,11},{10,... | collective-permute-start | bytes 491528 | tf_op jit(solution)/shard_map/ppermute | solution.py:77
  103.7 1.5 %collective-permute-start.32 = (bf16[640,768]{1,0:T(8,128)(2,1)S(1)}, bf16[640,768]{1,0:T(8,128)(2,1)S(1)}, u32[]{:S(2)}, u32[]{:S(2)}) collective-permute-start(bf16[640,768]{1,0:T(8,128)(2,1)S(1)} %add_convert_fusion), channel_id=1, source_target_pairs={{0,4},{4,0},{8,12},{12,8},{16,20},{20,16},{24,28},{28,24},{1,5},{5... | collective-permute-start | bytes 2949128 | tf_op jit(solution)/shard_map/ppermute | solution.py:73
  107.4 1.4 %collective-permute-done.29 = bf16[64,1280]{1,0:T(8,128)(2,1)S(1)} collective-permute-done((bf16[64,1280]{1,0:T(8,128)(2,1)S(1)}, bf16[64,1280]{1,0:T(8,128)(2,1)S(1)}, u32[]{:S(2)}, u32[]{:S(2)}) %collective-permute-start.29) | collective-permute-done | bytes 163872 | tf_op jit(solution)/shard_map/ppermute | solution.py:77
  109.1 7.3 %collective-permute-done.26 = bf16[128,1280]{1,0:T(8,128)(2,1)S(1)} collective-permute-done((bf16[128,1280]{1,0:T(8,128)(2,1)S(1)}, bf16[128,1280]{1,0:T(8,128)(2,1)S(1)}, u32[]{:S(2)}, u32[]{:S(2)}) %collective-permute-start.26) | collective-permute-done | bytes 327712 | tf_op jit(solution)/shard_map/ppermute | solution.py:77
  117.3 1.8 %collective-permute-done.30 = bf16[64,1280]{1,0:T(8,128)(2,1)S(1)} collective-permute-done((bf16[64,1280]{1,0:T(8,128)(2,1)S(1)}, bf16[64,1280]{1,0:T(8,128)(2,1)S(1)}, u32[]{:S(2)}, u32[]{:S(2)}) %collective-permute-start.30) | collective-permute-done | bytes 163872 | tf_op jit(solution)/shard_map/ppermute | solution.py:69
  120.4 7.1 %collective-permute-done.32 = bf16[640,768]{1,0:T(8,128)(2,1)S(1)} collective-permute-done((bf16[640,768]{1,0:T(8,128)(2,1)S(1)}, bf16[640,768]{1,0:T(8,128)(2,1)S(1)}, u32[]{:S(2)}, u32[]{:S(2)}) %collective-permute-start.32) | collective-permute-done | bytes 983072 | tf_op jit(solution)/shard_map/ppermute | solution.py:73
  127.6 1.5 %slice_add_fusion = (f32[640,384]{1,0:T(8,128)}, f32[640,384]{1,0:T(8,128)}) fusion(f32[640,768]{1,0:T(8,128)S(1)} %fusion, bf16[640,768]{1,0:T(8,128)(2,1)S(1)} %collective-permute-done.32), kind=kLoop, calls=%fused_computation.18 | loop fusion | flops 983040 | bytes 4915200 | tf_op jit(solution)/shard_map/add | solution.py:238
  129.3 4.0 %convolution_convert_fusion = bf16[512,5120]{1,0:T(8,128)(2,1)} fusion(bf16[64,5120]{1,0:T(8,128)(2,1)S(1)} %slice_dynamic-update-slice_fusion.2, s32[64]{0:T(128)S(1)} %copy-done.3), kind=kOutput, calls=%fused_computation | convolution fusion | flops 338198528 | bytes 5898496 | tf_op jit(solution)/shard_map/dot_general | solution.py:251
  (117 shorter events, 20.4 us)
Async XLA Ops:
  4.5 11.4 %collective-permute-start.1 = (bf16[64,1280]{1,0:T(8,128)(2,1)S(1)}, bf16[64,1280]{1,0:T(8,128)(2,1)S(1)}, u32[]{:S(2)}, u32[]{:S(2)}) collective-permute-start(bf16[64,1280]{1,0:T(8,128)(2,1)S(1)} %pad_maximum_fusion.15), channel_id=1, source_target_pairs={{0,24},{4,28},{8,16},{12,20},{16,8},{20,12},{24,0},{28,4},{1,25},{... | collective-permute-start | bytes 491528 | tf_op jit(solution)/shard_map/ppermute | solution.py:69
  9.6 8.9 %collective-permute-start = (bf16[64,1280]{1,0:T(8,128)(2,1)S(1)}, bf16[64,1280]{1,0:T(8,128)(2,1)S(1)}, u32[]{:S(2)}, u32[]{:S(2)}) collective-permute-start(bf16[64,1280]{1,0:T(8,128)(2,1)S(1)} %pad_maximum_fusion.14), channel_id=1, source_target_pairs={{0,8},{4,12},{8,0},{12,4},{16,24},{20,28},{24,16},{28,20},{1,9},{5... | collective-permute-start | bytes 491528 | tf_op jit(solution)/shard_map/ppermute | solution.py:69
  9.7 22.1 %collective-permute-start.7 = (bf16[640,384]{1,0:T(8,128)(2,1)S(1)}, bf16[640,384]{1,0:T(8,128)(2,1)S(1)}, u32[]{:S(2)}, u32[]{:S(2)}) collective-permute-start(bf16[640,384]{1,0:T(8,128)(2,1)S(1)} %copy-done.1), channel_id=1, source_target_pairs={{0,4},{4,0},{8,12},{12,8},{16,20},{20,16},{24,28},{28,24},{1,5},{5... | collective-permute-start | bytes 1474568 | tf_op jit(solution)/shard_map/ppermute | solution.py:73
  11.3 21.7 %collective-permute-start.6 = (bf16[640,384]{1,0:T(8,128)(2,1)S(1)}, bf16[640,384]{1,0:T(8,128)(2,1)S(1)}, u32[]{:S(2)}, u32[]{:S(2)}) collective-permute-start(bf16[640,384]{1,0:T(8,128)(2,1)S(1)} %copy-done.2), channel_id=1, source_target_pairs={{0,4},{4,0},{8,12},{12,8},{16,20},{20,16},{24,28},{28,24},{1,5},{5... | collective-permute-start | bytes 1474568 | tf_op jit(solution)/shard_map/ppermute | solution.py:73
  11.8 3.5 %collective-permute-start.16 = (bf16[64]{0:T(256)(128)(2,1)S(1)}, bf16[64]{0:T(256)(128)(2,1)S(1)}, u32[]{:S(2)}, u32[]{:S(2)}) collective-permute-start(bf16[64]{0:T(256)(128)(2,1)S(1)} %copy-done.4), channel_id=1, source_target_pairs={{0,2},{1,3},{2,0},{3,1},{4,6},{5,7},{6,4},{7,5},{8,10},{9,11},{10,... | collective-permute-start | bytes 392 | tf_op jit(solution)/shard_map/ppermute | solution.py:77
  15.4 8.7 %collective-permute-start.10 = (bf16[64,1280]{1,0:T(8,128)(2,1)S(1)}, bf16[64,1280]{1,0:T(8,128)(2,1)S(1)}, u32[]{:S(2)}, u32[]{:S(2)}) collective-permute-start(bf16[64,1280]{1,0:T(8,128)(2,1)S(1)} %pad_maximum_fusion.16), channel_id=1, source_target_pairs={{0,16},{4,20},{8,24},{12,28},{16,0},{20,4},{24,8},{28,12},{1,17},{... | collective-permute-start | bytes 491528 | tf_op jit(solution)/shard_map/ppermute | solution.py:69
  15.9 4.3 %collective-permute-start.17 = (bf16[128]{0:T(256)(128)(2,1)S(1)}, bf16[128]{0:T(256)(128)(2,1)S(1)}, u32[]{:S(2)}, u32[]{:S(2)}) collective-permute-start(bf16[128]{0:T(256)(128)(2,1)S(1)} %pad_maximum_fusion.17), channel_id=1, source_target_pairs={{0,1},{1,0},{2,3},{3,2},{4,5},{5,4},{6,7},{7,6},{8,9},{9,8},{10,11... | collective-permute-start | bytes 776 | tf_op jit(solution)/shard_map/ppermute | solution.py:77
  18.6 7.1 %collective-permute-start.2 = (bf16[64,1280]{1,0:T(8,128)(2,1)S(1)}, bf16[64,1280]{1,0:T(8,128)(2,1)S(1)}, u32[]{:S(2)}, u32[]{:S(2)}) collective-permute-start(bf16[64,1280]{1,0:T(8,128)(2,1)S(1)} %get-tuple-element.79), channel_id=1, source_target_pairs={{0,2},{1,3},{2,0},{3,1},{4,6},{5,7},{6,4},{7,5},{8,10},{9,11},{10,... | collective-permute-start | bytes 491528 | tf_op jit(solution)/shard_map/ppermute | solution.py:77
  20.4 8.9 %collective-permute-start.4 = (bf16[64,1280]{1,0:T(8,128)(2,1)S(1)}, bf16[64,1280]{1,0:T(8,128)(2,1)S(1)}, u32[]{:S(2)}, u32[]{:S(2)}) collective-permute-start(bf16[64,1280]{1,0:T(8,128)(2,1)S(1)} %get-tuple-element.78), channel_id=1, source_target_pairs={{0,2},{1,3},{2,0},{3,1},{4,6},{5,7},{6,4},{7,5},{8,10},{9,11},{10,... | collective-permute-start | bytes 491528 | tf_op jit(solution)/shard_map/ppermute | solution.py:77
  24.1 7.8 %collective-permute-start.11 = (bf16[64,1280]{1,0:T(8,128)(2,1)S(1)}, bf16[64,1280]{1,0:T(8,128)(2,1)S(1)}, u32[]{:S(2)}, u32[]{:S(2)}) collective-permute-start(bf16[64,1280]{1,0:T(8,128)(2,1)S(1)} %collective-permute-done.10), channel_id=1, source_target_pairs={{0,2},{1,3},{2,0},{3,1},{4,6},{5,7},{6,4},{7,5},{8,10},{9,11},{10,... | collective-permute-start | bytes 491528 | tf_op jit(solution)/shard_map/ppermute | solution.py:77
  25.8 9.9 %collective-permute-start.3 = (bf16[128,1280]{1,0:T(8,128)(2,1)S(1)}, bf16[128,1280]{1,0:T(8,128)(2,1)S(1)}, u32[]{:S(2)}, u32[]{:S(2)}) collective-permute-start(bf16[128,1280]{1,0:T(8,128)(2,1)S(1)} %pad_maximum_fusion.8), channel_id=1, source_target_pairs={{0,1},{1,0},{2,3},{3,2},{4,5},{5,4},{6,7},{7,6},{8,9},{9,8},{10,11... | collective-permute-start | bytes 983048 | tf_op jit(solution)/shard_map/ppermute | solution.py:77
  29.3 3.9 %collective-permute-start.5 = (bf16[128,1280]{1,0:T(8,128)(2,1)S(1)}, bf16[128,1280]{1,0:T(8,128)(2,1)S(1)}, u32[]{:S(2)}, u32[]{:S(2)}) collective-permute-start(bf16[128,1280]{1,0:T(8,128)(2,1)S(1)} %pad_maximum_fusion.9), channel_id=1, source_target_pairs={{0,1},{1,0},{2,3},{3,2},{4,5},{5,4},{6,7},{7,6},{8,9},{9,8},{10,11... | collective-permute-start | bytes 983048 | tf_op jit(solution)/shard_map/ppermute | solution.py:77
  33.9 9.7 %collective-permute-start.13 = (bf16[256,768]{1,0:T(8,128)(2,1)S(1)}, bf16[256,768]{1,0:T(8,128)(2,1)S(1)}, u32[]{:S(2)}, u32[]{:S(2)}) collective-permute-start(bf16[256,768]{1,0:T(8,128)(2,1)S(1)} %convolution_convert_fusion.3), channel_id=1, source_target_pairs={{0,8},{4,12},{8,0},{12,4},{16,24},{20,28},{24,16},{28,20},{1,9},{5... | collective-permute-start | bytes 1179656 | tf_op jit(solution)/shard_map/ppermute | solution.py:108
  36.4 12.3 %collective-permute-start.14 = (bf16[256,768]{1,0:T(8,128)(2,1)S(1)}, bf16[256,768]{1,0:T(8,128)(2,1)S(1)}, u32[]{:S(2)}, u32[]{:S(2)}) collective-permute-start(bf16[256,768]{1,0:T(8,128)(2,1)S(1)} %convolution_convert_fusion.2), channel_id=1, source_target_pairs={{8,16},{12,20},{16,8},{20,12},{9,17},{13,21},{17,9},{21,13},{10,18... | collective-permute-start | bytes 1179656 | tf_op jit(solution)/shard_map/ppermute | solution.py:108
  37.1 5.4 %collective-permute-start.8 = (bf16[64,1280]{1,0:T(8,128)(2,1)S(1)}, bf16[64,1280]{1,0:T(8,128)(2,1)S(1)}, u32[]{:S(2)}, u32[]{:S(2)}) collective-permute-start(bf16[64,1280]{1,0:T(8,128)(2,1)S(1)} %pad_maximum_fusion.13), channel_id=1, source_target_pairs={{0,2},{1,3},{2,0},{3,1},{4,6},{5,7},{6,4},{7,5},{8,10},{9,11},{10,... | collective-permute-start | bytes 491528 | tf_op jit(solution)/shard_map/ppermute | solution.py:77
  38.6 3.9 %collective-permute-start.12 = (bf16[128,1280]{1,0:T(8,128)(2,1)S(1)}, bf16[128,1280]{1,0:T(8,128)(2,1)S(1)}, u32[]{:S(2)}, u32[]{:S(2)}) collective-permute-start(bf16[128,1280]{1,0:T(8,128)(2,1)S(1)} %pad_maximum_fusion.11), channel_id=1, source_target_pairs={{0,1},{1,0},{2,3},{3,2},{4,5},{5,4},{6,7},{7,6},{8,9},{9,8},{10,11... | collective-permute-start | bytes 983048 | tf_op jit(solution)/shard_map/ppermute | solution.py:77
  42.5 6.1 %collective-permute-start.9 = (bf16[128,1280]{1,0:T(8,128)(2,1)S(1)}, bf16[128,1280]{1,0:T(8,128)(2,1)S(1)}, u32[]{:S(2)}, u32[]{:S(2)}) collective-permute-start(bf16[128,1280]{1,0:T(8,128)(2,1)S(1)} %pad_maximum_fusion.10), channel_id=1, source_target_pairs={{0,1},{1,0},{2,3},{3,2},{4,5},{5,4},{6,7},{7,6},{8,9},{9,8},{10,11... | collective-permute-start | bytes 983048 | tf_op jit(solution)/shard_map/ppermute | solution.py:77
  44.4 13.4 %collective-permute-start.15 = (bf16[256,768]{1,0:T(8,128)(2,1)S(1)}, bf16[256,768]{1,0:T(8,128)(2,1)S(1)}, u32[]{:S(2)}, u32[]{:S(2)}) collective-permute-start(bf16[256,768]{1,0:T(8,128)(2,1)S(1)} %convert_element_type.88), channel_id=1, source_target_pairs={{0,16},{4,20},{24,8},{28,12},{1,17},{5,21},{25,9},{29,13},{2,18},{... | collective-permute-start | bytes 1179656 | tf_op jit(solution)/shard_map/ppermute | solution.py:108
  48.5 18.6 %collective-permute-start.18 = (bf16[256,768]{1,0:T(8,128)(2,1)S(1)}, bf16[256,768]{1,0:T(8,128)(2,1)S(1)}, u32[]{:S(2)}, u32[]{:S(2)}) collective-permute-start(bf16[256,768]{1,0:T(8,128)(2,1)S(1)} %fusion.18), channel_id=1, source_target_pairs={{16,0},{20,4},{24,16},{28,20},{8,24},{12,28},{0,8},{4,12},{17,1},{... | collective-permute-start | bytes 1179656 | tf_op jit(solution)/shard_map/ppermute | solution.py:108
  69.7 11.6 %collective-permute-start.21 = (bf16[256,768]{1,0:T(8,128)(2,1)S(1)}, bf16[256,768]{1,0:T(8,128)(2,1)S(1)}, u32[]{:S(2)}, u32[]{:S(2)}) collective-permute-start(bf16[256,768]{1,0:T(8,128)(2,1)S(1)} %get-tuple-element.42), channel_id=1, source_target_pairs={{0,16},{4,20},{16,24},{20,28},{24,8},{28,12},{8,0},{12,4},{1,17},{... | collective-permute-start | bytes 1179656 | tf_op jit(solution)/shard_map/ppermute | solution.py:108
  70.3 20.9 %collective-permute-start.22 = (bf16[256,768]{1,0:T(8,128)(2,1)S(1)}, bf16[256,768]{1,0:T(8,128)(2,1)S(1)}, u32[]{:S(2)}, u32[]{:S(2)}) collective-permute-start(bf16[256,768]{1,0:T(8,128)(2,1)S(1)} %get-tuple-element.42), channel_id=1, source_target_pairs={{16,0},{20,4},{8,24},{12,28},{17,1},{21,5},{9,25},{13,29},{18,2},{... | collective-permute-start | bytes 1179656 | tf_op jit(solution)/shard_map/ppermute | solution.py:108
  71.6 21.3 %collective-permute-start.23 = (bf16[256,768]{1,0:T(8,128)(2,1)S(1)}, bf16[256,768]{1,0:T(8,128)(2,1)S(1)}, u32[]{:S(2)}, u32[]{:S(2)}) collective-permute-start(bf16[256,768]{1,0:T(8,128)(2,1)S(1)} %get-tuple-element.42), channel_id=1, source_target_pairs={{8,16},{12,20},{16,8},{20,12},{9,17},{13,21},{17,9},{21,13},{10,18... | collective-permute-start | bytes 1179656 | tf_op jit(solution)/shard_map/ppermute | solution.py:108
  72.6 20.4 %collective-permute-start.20 = (bf16[64,1280]{1,0:T(8,128)(2,1)S(1)}, bf16[64,1280]{1,0:T(8,128)(2,1)S(1)}, u32[]{:S(2)}, u32[]{:S(2)}) collective-permute-start(bf16[64,1280]{1,0:T(8,128)(2,1)S(1)} %slice.251), channel_id=1, source_target_pairs={{0,2},{1,3},{2,0},{3,1},{4,6},{5,7},{6,4},{7,5},{8,10},{9,11},{10,... | collective-permute-start | bytes 491528 | tf_op jit(solution)/shard_map/ppermute | solution.py:77
  81.4 18.2 %collective-permute-start.24 = (bf16[256,768]{1,0:T(8,128)(2,1)S(1)}, bf16[256,768]{1,0:T(8,128)(2,1)S(1)}, u32[]{:S(2)}, u32[]{:S(2)}) collective-permute-start(bf16[256,768]{1,0:T(8,128)(2,1)S(1)} %broadcast_select_fusion.2), channel_id=1, source_target_pairs={{0,8},{4,12},{8,0},{12,4},{16,24},{20,28},{24,16},{28,20},{1,9},{5... | collective-permute-start | bytes 1179656 | tf_op jit(solution)/shard_map/ppermute | solution.py:108
  92.8 9.2 %collective-permute-start.28 = (bf16[128,1280]{1,0:T(8,128)(2,1)S(1)}, bf16[128,1280]{1,0:T(8,128)(2,1)S(1)}, u32[]{:S(2)}, u32[]{:S(2)}) collective-permute-start(bf16[128,1280]{1,0:T(8,128)(2,1)S(1)} %slice.244), channel_id=1, source_target_pairs={{0,1},{1,0},{2,3},{3,2},{4,5},{5,4},{6,7},{7,6},{8,9},{9,8},{10,11... | collective-permute-start | bytes 983048 | tf_op jit(solution)/shard_map/ppermute | solution.py:77
  101.9 4.6 %collective-permute-start.25 = (bf16[256,1280]{1,0:T(8,128)(2,1)S(1)}, bf16[256,1280]{1,0:T(8,128)(2,1)S(1)}, u32[]{:S(2)}, u32[]{:S(2)}) collective-permute-start(bf16[256,1280]{1,0:T(8,128)(2,1)S(1)} %pad_maximum_fusion.7), channel_id=1, source_target_pairs={{0,1},{1,0},{2,3},{3,2},{4,5},{5,4},{6,7},{7,6},{8,9},{9,8},{10,11... | collective-permute-start | bytes 1966088 | tf_op jit(solution)/shard_map/ppermute | solution.py:77
  102.1 6.7 %collective-permute-start.29 = (bf16[64,1280]{1,0:T(8,128)(2,1)S(1)}, bf16[64,1280]{1,0:T(8,128)(2,1)S(1)}, u32[]{:S(2)}, u32[]{:S(2)}) collective-permute-start(bf16[64,1280]{1,0:T(8,128)(2,1)S(1)} %slice.248), channel_id=1, source_target_pairs={{0,2},{1,3},{2,0},{3,1},{4,6},{5,7},{6,4},{7,5},{8,10},{9,11},{10,... | collective-permute-start | bytes 491528 | tf_op jit(solution)/shard_map/ppermute | solution.py:77
  103.7 23.9 %collective-permute-start.32 = (bf16[640,768]{1,0:T(8,128)(2,1)S(1)}, bf16[640,768]{1,0:T(8,128)(2,1)S(1)}, u32[]{:S(2)}, u32[]{:S(2)}) collective-permute-start(bf16[640,768]{1,0:T(8,128)(2,1)S(1)} %add_convert_fusion), channel_id=1, source_target_pairs={{0,4},{4,0},{8,12},{12,8},{16,20},{20,16},{24,28},{28,24},{1,5},{5... | collective-permute-start | bytes 2949128 | tf_op jit(solution)/shard_map/ppermute | solution.py:73
  106.8 9.6 %collective-permute-start.26 = (bf16[128,1280]{1,0:T(8,128)(2,1)S(1)}, bf16[128,1280]{1,0:T(8,128)(2,1)S(1)}, u32[]{:S(2)}, u32[]{:S(2)}) collective-permute-start(bf16[128,1280]{1,0:T(8,128)(2,1)S(1)} %pad_maximum_fusion.12), channel_id=1, source_target_pairs={{0,2},{1,3},{2,0},{3,1},{4,6},{5,7},{6,4},{7,5},{8,10},{9,11},{10,... | collective-permute-start | bytes 983048 | tf_op jit(solution)/shard_map/ppermute | solution.py:77
  108.8 10.4 %collective-permute-start.30 = (bf16[64,1280]{1,0:T(8,128)(2,1)S(1)}, bf16[64,1280]{1,0:T(8,128)(2,1)S(1)}, u32[]{:S(2)}, u32[]{:S(2)}) collective-permute-start(bf16[64,1280]{1,0:T(8,128)(2,1)S(1)} %fusion.19), channel_id=1, source_target_pairs={{0,16},{4,20},{8,24},{12,28},{16,0},{20,4},{24,8},{28,12},{1,17},{... | collective-permute-start | bytes 491528 | tf_op jit(solution)/shard_map/ppermute | solution.py:69
  116.5 12.5 %collective-permute-start.27 = (bf16[64,1280]{1,0:T(8,128)(2,1)S(1)}, bf16[64,1280]{1,0:T(8,128)(2,1)S(1)}, u32[]{:S(2)}, u32[]{:S(2)}) collective-permute-start(bf16[64,1280]{1,0:T(8,128)(2,1)S(1)} %broadcast_select_fusion.4), channel_id=1, source_target_pairs={{0,8},{4,12},{8,0},{12,4},{16,24},{20,28},{24,16},{28,20},{1,9},{5... | collective-permute-start | bytes 491528 | tf_op jit(solution)/shard_map/ppermute | solution.py:69
  119.2 10.0 %collective-permute-start.31 = (bf16[64,1280]{1,0:T(8,128)(2,1)S(1)}, bf16[64,1280]{1,0:T(8,128)(2,1)S(1)}, u32[]{:S(2)}, u32[]{:S(2)}) collective-permute-start(bf16[64,1280]{1,0:T(8,128)(2,1)S(1)} %get-tuple-element.56), channel_id=1, source_target_pairs={{0,24},{4,28},{8,16},{12,20},{16,8},{20,12},{24,0},{28,4},{1,25},{... | collective-permute-start | bytes 491528 | tf_op jit(solution)/shard_map/ppermute | solution.py:69
  (7 other events, 66.3 us)

commit v20 on v19

--- a/solution.py
+++ b/solution.py
@@ -230,19 +230,17 @@
         arriving = [over_inner(leaving[j - 1], j) for j in range(1, inner)]
         last = leaving[0] if inner > 1 else last
         if late:
-            last = advance(late, last)
+            last = advance(late, after(last, *[sums[k] for k in early]))
         total = weight_grad(sequence, 0, last)
-        gate_total, up_total = total[:, :width], total[:, width:]
-        for part in arriving:
-            gate_total = gate_total + part[:, :width].astype(F32)
-            up_total = up_total + part[:, width:].astype(F32)
-
         last = sums[sequence[-1]]
-        if relay:
+        returned = {0: sums[0]}
+        if relay:
+            returned[2] = over_outer(sums[2], 2)
             sums[3], sums[1] = pick(sums[3], sums[1]), pick(sums[1], sums[3])
+            sums[3], sums[1] = after(sums[3], returned[2]), after(sums[1], returned[2])
         dx = jnp.zeros((cap, outer * span), BF16)
         for k in keys:
-            own = over_outer(sums[k], k) if k else sums[k]
+            own = returned[k] if k in returned else over_outer(sums[k], k)
             if k != sequence[-1]:
                 own = after(own, last)
             for j in range(inner):
@@ -251,6 +249,11 @@
         grad_tokens = lax.dot_general(
             onehot, dx, (((0,), (0,)), ((), ())), preferred_element_type=F32
         ).astype(BF16)
+        gate_total, up_total = total[:, :width], total[:, width:]
+        for part in arriving:
+            part = after(part, grad_tokens)
+            gate_total = gate_total + part[:, :width].astype(F32)
+            up_total = up_total + part[:, width:].astype(F32)
         return (hidden, grad_tokens, gate_total, up_total)
 
     return shards

time: 133 us -> 135 us (1.015)
  starting transfers between devices: 33.8 us -> 40.9 us
  waiting for transfers between devices: 76.6 us -> 71.3 us
    ppermute x3, waiting for transfers between devices: 8.29 us -> 1.15 us  [over_inner(): return lax.ppermute(value, 'dp', pairs)]
    ppermute x6, starting transfers between devices: 7.89 us -> 13.9 us  [over_outer(): return lax.ppermute(value, 'dp', pairs)]
    ppermute x6, waiting for transfers between devices: 7.57 us -> 12.5 us  [over_outer(): return lax.ppermute(value, 'dp', pairs)]
    ppermute x8, waiting for transfers between devices: 40.2 us -> 37.1 us  [outer_pairs(): return lax.ppermute(value, 'dp', pairs)]
where the time goes in v20:
time: 135 us
  waiting for transfers between devices  71.3 us (53%)
  starting transfers between devices  40.9 us (30%)
  matrix products  15.8 us (12%)
  other arithmetic  3.14 us (2%)
  Pallas kernels  1.51 us (1%)
  between operations  1.36 us (1%)
    ppermute x8, waiting for transfers between devices, outer_pairs(): return lax.ppermute(value, 'dp', pairs)  37.1 us
    ppermute x16, waiting for transfers between devices, over_etp(): return lax.ppermute(value, 'etp', pairs)  20.5 us
    ppermute x6, starting transfers between devices, over_outer(): return lax.ppermute(value, 'dp', pairs)  13.9 us
    ppermute x6, waiting for transfers between devices, over_outer(): return lax.ppermute(value, 'dp', pairs)  12.5 us
    ppermute x16, starting transfers between devices, over_etp(): return lax.ppermute(value, 'etp', pairs)  12 us
    ppermute x8, starting transfers between devices, outer_pairs(): return lax.ppermute(value, 'dp', pairs)  11.4 us
    dot_general x1, matrix products, shards(): lax.dot_general(onehot, dx, (((0,), (0,)), ((), ())), preferred_element_t...  3.99 us
    ppermute x3, starting transfers between devices, over_inner(): return lax.ppermute(value, 'dp', pairs)  3.64 us
  transfers between devices with their start and end apart: 33, of which 18 were waited for; matrix products, arithmetic and copies ran while one was open for 9% of the time, Pallas kernels for 0%

profile of v20, /device:TPU:0, one launch (start us, length us, event | category | flops | bytes accessed | tf_op | source)
XLA Modules:
  0.0 135.0 jit_solution(9020118045508599035)
XLA Ops:
  0.7 3.6 %convolution_convert_fusion.1 = bf16[64,5120]{1,0:T(8,128)(2,1)S(1)} fusion(bf16[512,5120]{1,0:T(8,128)(2,1)} %param.7, s32[64]{0:T(128)} %param.8), kind=kOutput, calls=%fused_computation.1 | convolution fusion | flops 335904768 | bytes 5898496 | tf_op jit(solution)/shard_map/dot_general | solution.py:136
  4.5 5.1 %collective-permute-start.1 = (bf16[64,1280]{1,0:T(8,128)(2,1)S(1)}, bf16[64,1280]{1,0:T(8,128)(2,1)S(1)}, u32[]{:S(2)}, u32[]{:S(2)}) collective-permute-start(bf16[64,1280]{1,0:T(8,128)(2,1)S(1)} %pad_maximum_fusion.15), channel_id=1, source_target_pairs={{0,24},{4,28},{8,16},{12,20},{16,8},{20,12},{24,0},{28,4},{1,25},{... | collective-permute-start | bytes 491528 | tf_op jit(solution)/shard_map/ppermute | solution.py:69
  9.7 1.6 %collective-permute-start.7 = (bf16[640,384]{1,0:T(8,128)(2,1)S(1)}, bf16[640,384]{1,0:T(8,128)(2,1)S(1)}, u32[]{:S(2)}, u32[]{:S(2)}) collective-permute-start(bf16[640,384]{1,0:T(8,128)(2,1)S(1)} %copy-done.1), channel_id=1, source_target_pairs={{0,4},{4,0},{8,12},{12,8},{16,20},{20,16},{24,28},{28,24},{1,5},{5... | collective-permute-start | bytes 1474568 | tf_op jit(solution)/shard_map/ppermute | solution.py:73
  11.8 1.5 %collective-permute-start.16 = (bf16[64]{0:T(256)(128)(2,1)S(1)}, bf16[64]{0:T(256)(128)(2,1)S(1)}, u32[]{:S(2)}, u32[]{:S(2)}) collective-permute-start(bf16[64]{0:T(256)(128)(2,1)S(1)} %copy-done.4), channel_id=1, source_target_pairs={{0,2},{1,3},{2,0},{3,1},{4,6},{5,7},{6,4},{7,5},{8,10},{9,11},{10,... | collective-permute-start | bytes 392 | tf_op jit(solution)/shard_map/ppermute | solution.py:77
  13.4 2.0 %collective-permute-done.16 = bf16[64]{0:T(256)(128)(2,1)S(1)} collective-permute-done((bf16[64]{0:T(256)(128)(2,1)S(1)}, bf16[64]{0:T(256)(128)(2,1)S(1)}, u32[]{:S(2)}, u32[]{:S(2)}) %collective-permute-start.16) | collective-permute-done | bytes 160 | tf_op jit(solution)/shard_map/ppermute | solution.py:77
  16.0 2.6 %collective-permute-done = bf16[64,1280]{1,0:T(8,128)(2,1)S(1)} collective-permute-done((bf16[64,1280]{1,0:T(8,128)(2,1)S(1)}, bf16[64,1280]{1,0:T(8,128)(2,1)S(1)}, u32[]{:S(2)}, u32[]{:S(2)}) %collective-permute-start) | collective-permute-done | bytes 163872 | tf_op jit(solution)/shard_map/ppermute | solution.py:69
  18.6 1.6 %collective-permute-start.2 = (bf16[64,1280]{1,0:T(8,128)(2,1)S(1)}, bf16[64,1280]{1,0:T(8,128)(2,1)S(1)}, u32[]{:S(2)}, u32[]{:S(2)}) collective-permute-start(bf16[64,1280]{1,0:T(8,128)(2,1)S(1)} %get-tuple-element.87), channel_id=1, source_target_pairs={{0,2},{1,3},{2,0},{3,1},{4,6},{5,7},{6,4},{7,5},{8,10},{9,11},{10,... | collective-permute-start | bytes 491528 | tf_op jit(solution)/shard_map/ppermute | solution.py:77
  21.0 3.1 %collective-permute-done.10 = bf16[64,1280]{1,0:T(8,128)(2,1)S(1)} collective-permute-done((bf16[64,1280]{1,0:T(8,128)(2,1)S(1)}, bf16[64,1280]{1,0:T(8,128)(2,1)S(1)}, u32[]{:S(2)}, u32[]{:S(2)}) %collective-permute-start.10) | collective-permute-done | bytes 163872 | tf_op jit(solution)/shard_map/ppermute | solution.py:69
  24.1 1.5 %collective-permute-start.11 = (bf16[64,1280]{1,0:T(8,128)(2,1)S(1)}, bf16[64,1280]{1,0:T(8,128)(2,1)S(1)}, u32[]{:S(2)}, u32[]{:S(2)}) collective-permute-start(bf16[64,1280]{1,0:T(8,128)(2,1)S(1)} %collective-permute-done.10), channel_id=1, source_target_pairs={{0,2},{1,3},{2,0},{3,1},{4,6},{5,7},{6,4},{7,5},{8,10},{9,11},{10,... | collective-permute-start | bytes 491528 | tf_op jit(solution)/shard_map/ppermute | solution.py:77
  25.8 3.4 %collective-permute-done.4 = bf16[64,1280]{1,0:T(8,128)(2,1)S(1)} collective-permute-done((bf16[64,1280]{1,0:T(8,128)(2,1)S(1)}, bf16[64,1280]{1,0:T(8,128)(2,1)S(1)}, u32[]{:S(2)}, u32[]{:S(2)}) %collective-permute-start.4) | collective-permute-done | bytes 163872 | tf_op jit(solution)/shard_map/ppermute | solution.py:77
  29.3 2.5 %collective-permute-done.11 = bf16[64,1280]{1,0:T(8,128)(2,1)S(1)} collective-permute-done((bf16[64,1280]{1,0:T(8,128)(2,1)S(1)}, bf16[64,1280]{1,0:T(8,128)(2,1)S(1)}, u32[]{:S(2)}, u32[]{:S(2)}) %collective-permute-start.11) | collective-permute-done | bytes 163872 | tf_op jit(solution)/shard_map/ppermute | solution.py:77
  33.9 1.7 %collective-permute-start.13 = (bf16[256,768]{1,0:T(8,128)(2,1)S(1)}, bf16[256,768]{1,0:T(8,128)(2,1)S(1)}, u32[]{:S(2)}, u32[]{:S(2)}) collective-permute-start(bf16[256,768]{1,0:T(8,128)(2,1)S(1)} %convolution_convert_fusion.3), channel_id=1, source_target_pairs={{0,8},{4,12},{8,0},{12,4},{16,24},{20,28},{24,16},{28,20},{1,9},{5... | collective-permute-start | bytes 1179656 | tf_op jit(solution)/shard_map/ppermute | solution.py:108
  37.1 1.6 %collective-permute-start.8 = (bf16[64,1280]{1,0:T(8,128)(2,1)S(1)}, bf16[64,1280]{1,0:T(8,128)(2,1)S(1)}, u32[]{:S(2)}, u32[]{:S(2)}) collective-permute-start(bf16[64,1280]{1,0:T(8,128)(2,1)S(1)} %pad_maximum_fusion.13), channel_id=1, source_target_pairs={{0,2},{1,3},{2,0},{3,1},{4,6},{5,7},{6,4},{7,5},{8,10},{9,11},{10,... | collective-permute-start | bytes 491528 | tf_op jit(solution)/shard_map/ppermute | solution.py:77
  38.7 3.7 %collective-permute-done.8 = bf16[64,1280]{1,0:T(8,128)(2,1)S(1)} collective-permute-done((bf16[64,1280]{1,0:T(8,128)(2,1)S(1)}, bf16[64,1280]{1,0:T(8,128)(2,1)S(1)}, u32[]{:S(2)}, u32[]{:S(2)}) %collective-permute-start.8) | collective-permute-done | bytes 163872 | tf_op jit(solution)/shard_map/ppermute | solution.py:77
  44.4 4.0 %collective-permute-start.15 = (bf16[256,768]{1,0:T(8,128)(2,1)S(1)}, bf16[256,768]{1,0:T(8,128)(2,1)S(1)}, u32[]{:S(2)}, u32[]{:S(2)}) collective-permute-start(bf16[256,768]{1,0:T(8,128)(2,1)S(1)} %convert_element_type.88), channel_id=1, source_target_pairs={{0,16},{4,20},{24,8},{28,12},{1,17},{5,21},{25,9},{29,13},{2,18},{... | collective-permute-start | bytes 1179656 | tf_op jit(solution)/shard_map/ppermute | solution.py:108
  48.6 9.2 %collective-permute-done.15 = bf16[256,768]{1,0:T(8,128)(2,1)S(1)} collective-permute-done((bf16[256,768]{1,0:T(8,128)(2,1)S(1)}, bf16[256,768]{1,0:T(8,128)(2,1)S(1)}, u32[]{:S(2)}, u32[]{:S(2)}) %collective-permute-start.15) | collective-permute-done | bytes 393248 | tf_op jit(solution)/shard_map/ppermute | solution.py:108
  58.5 8.6 %collective-permute-done.18.refs_0_ = bf16[256,768]{1,0:T(8,128)(2,1)S(1)} collective-permute-done((bf16[256,768]{1,0:T(8,128)(2,1)S(1)}, bf16[256,768]{1,0:T(8,128)(2,1)S(1)}, u32[]{:S(2)}, u32[]{:S(2)}) %collective-permute-start.18) | collective-permute-done | bytes 393248 | tf_op jit(solution)/shard_map/ppermute | solution.py:108
  67.1 1.5 %shard_map.102 = (bf16[256,384]{1,0:T(8,128)(2,1)}, bf16[256,768]{1,0:T(8,128)(2,1)S(1)}) custom-call(s32[4]{0:T(128)S(1)} %broadcast_xor_fusion.order_ref, f32[256,768]{1,0:T(8,128)S(1)} %fusion.9.pre_ref, bf16[256,1]{1,0:T(8,128)(2,1)S(1)} %broadcast_in_dim.15.prob_ref, bf16[256,384]{1,0:T(8,128)(2,1)S(1)} %copy-done, ...), custom_call_target="tpu_custom_call" | custom-call | flops 1966080 | bytes 2949120 | tf_op jit(solution)/shard_map/pallas_call | solution.py:49
  72.6 1.6 %collective-permute-start.20 = (bf16[64,1280]{1,0:T(8,128)(2,1)S(1)}, bf16[64,1280]{1,0:T(8,128)(2,1)S(1)}, u32[]{:S(2)}, u32[]{:S(2)}) collective-permute-start(bf16[64,1280]{1,0:T(8,128)(2,1)S(1)} %slice.249), channel_id=1, source_target_pairs={{0,2},{1,3},{2,0},{3,1},{4,6},{5,7},{6,4},{7,5},{8,10},{9,11},{10,... | collective-permute-start | bytes 491528 | tf_op jit(solution)/shard_map/ppermute | solution.py:77
  74.2 7.1 %collective-permute-done.21 = bf16[256,768]{1,0:T(8,128)(2,1)S(1)} collective-permute-done((bf16[256,768]{1,0:T(8,128)(2,1)S(1)}, bf16[256,768]{1,0:T(8,128)(2,1)S(1)}, u32[]{:S(2)}, u32[]{:S(2)}) %collective-permute-start.21) | collective-permute-done | bytes 393248 | tf_op jit(solution)/shard_map/ppermute | solution.py:108
  81.4 2.1 %collective-permute-start.24 = (bf16[256,768]{1,0:T(8,128)(2,1)S(1)}, bf16[256,768]{1,0:T(8,128)(2,1)S(1)}, u32[]{:S(2)}, u32[]{:S(2)}) collective-permute-start(bf16[256,768]{1,0:T(8,128)(2,1)S(1)} %broadcast_select_fusion.2), channel_id=1, source_target_pairs={{0,8},{4,12},{8,0},{12,4},{16,24},{20,28},{24,16},{28,20},{1,9},{5... | collective-permute-start | bytes 1179656 | tf_op jit(solution)/shard_map/ppermute | solution.py:108
  83.5 7.8 %collective-permute-done.22 = bf16[256,768]{1,0:T(8,128)(2,1)S(1)} collective-permute-done((bf16[256,768]{1,0:T(8,128)(2,1)S(1)}, bf16[256,768]{1,0:T(8,128)(2,1)S(1)}, u32[]{:S(2)}, u32[]{:S(2)}) %collective-permute-start.22) | collective-permute-done | bytes 393248 | tf_op jit(solution)/shard_map/ppermute | solution.py:108
  93.0 1.5 %collective-permute-done.25 = bf16[128,1280]{1,0:T(8,128)(2,1)S(1)} collective-permute-done((bf16[128,1280]{1,0:T(8,128)(2,1)S(1)}, bf16[128,1280]{1,0:T(8,128)(2,1)S(1)}, u32[]{:S(2)}, u32[]{:S(2)}) %collective-permute-start.25) | collective-permute-done | bytes 327712 | tf_op jit(solution)/shard_map/ppermute | solution.py:77
  94.6 1.6 %collective-permute-start.26 = (bf16[64,1280]{1,0:T(8,128)(2,1)S(1)}, bf16[64,1280]{1,0:T(8,128)(2,1)S(1)}, u32[]{:S(2)}, u32[]{:S(2)}) collective-permute-start(bf16[64,1280]{1,0:T(8,128)(2,1)S(1)} %slice.248), channel_id=1, source_target_pairs={{0,2},{1,3},{2,0},{3,1},{4,6},{5,7},{6,4},{7,5},{8,10},{9,11},{10,... | collective-permute-start | bytes 491528 | tf_op jit(solution)/shard_map/ppermute | solution.py:77
  96.2 3.4 %collective-permute-done.24 = bf16[256,768]{1,0:T(8,128)(2,1)S(1)} collective-permute-done((bf16[256,768]{1,0:T(8,128)(2,1)S(1)}, bf16[256,768]{1,0:T(8,128)(2,1)S(1)}, u32[]{:S(2)}, u32[]{:S(2)}) %collective-permute-start.24) | collective-permute-done | bytes 393248 | tf_op jit(solution)/shard_map/ppermute | solution.py:108
  102.6 1.5 %collective-permute-start.32 = (bf16[640,768]{1,0:T(8,128)(2,1)S(1)}, bf16[640,768]{1,0:T(8,128)(2,1)S(1)}, u32[]{:S(2)}, u32[]{:S(2)}) collective-permute-start(bf16[640,768]{1,0:T(8,128)(2,1)S(1)} %add_convert_fusion), channel_id=1, source_target_pairs={{0,4},{4,0},{8,12},{12,8},{16,20},{20,16},{24,28},{28,24},{1,5},{5... | collective-permute-start | bytes 2949128 | tf_op jit(solution)/shard_map/ppermute | solution.py:73
  104.3 5.2 %collective-permute-start.29 = (bf16[64,1280]{1,0:T(8,128)(2,1)S(1)}, bf16[64,1280]{1,0:T(8,128)(2,1)S(1)}, u32[]{:S(2)}, u32[]{:S(2)}) collective-permute-start(bf16[64,1280]{1,0:T(8,128)(2,1)S(1)} %fusion.21), channel_id=1, source_target_pairs={{0,16},{4,20},{8,24},{12,28},{16,0},{20,4},{24,8},{28,12},{1,17},{... | collective-permute-start | bytes 491528 | tf_op jit(solution)/shard_map/ppermute | solution.py:69
  109.7 1.6 %collective-permute-start.28 = (bf16[128,1280]{1,0:T(8,128)(2,1)S(1)}, bf16[128,1280]{1,0:T(8,128)(2,1)S(1)}, u32[]{:S(2)}, u32[]{:S(2)}) collective-permute-start(bf16[128,1280]{1,0:T(8,128)(2,1)S(1)} %pad_maximum_fusion.12), channel_id=1, source_target_pairs={{0,2},{1,3},{2,0},{3,1},{4,6},{5,7},{6,4},{7,5},{8,10},{9,11},{10,... | collective-permute-start | bytes 983048 | tf_op jit(solution)/shard_map/ppermute | solution.py:77
  112.5 6.7 %collective-permute-done.28 = bf16[128,1280]{1,0:T(8,128)(2,1)S(1)} collective-permute-done((bf16[128,1280]{1,0:T(8,128)(2,1)S(1)}, bf16[128,1280]{1,0:T(8,128)(2,1)S(1)}, u32[]{:S(2)}, u32[]{:S(2)}) %collective-permute-start.28) | collective-permute-done | bytes 327712 | tf_op jit(solution)/shard_map/ppermute | solution.py:77
  120.6 1.8 %collective-permute-start.31 = (bf16[64,1280]{1,0:T(8,128)(2,1)S(1)}, bf16[64,1280]{1,0:T(8,128)(2,1)S(1)}, u32[]{:S(2)}, u32[]{:S(2)}) collective-permute-start(bf16[64,1280]{1,0:T(8,128)(2,1)S(1)} %get-tuple-element.60), channel_id=1, source_target_pairs={{0,24},{4,28},{8,16},{12,20},{16,8},{20,12},{24,0},{28,4},{1,25},{... | collective-permute-start | bytes 491528 | tf_op jit(solution)/shard_map/ppermute | solution.py:69
  122.6 6.8 %collective-permute-done.31 = bf16[64,1280]{1,0:T(8,128)(2,1)S(1)} collective-permute-done((bf16[64,1280]{1,0:T(8,128)(2,1)S(1)}, bf16[64,1280]{1,0:T(8,128)(2,1)S(1)}, u32[]{:S(2)}, u32[]{:S(2)}) %collective-permute-start.31) | collective-permute-done | bytes 163872 | tf_op jit(solution)/shard_map/ppermute | solution.py:69
  129.5 4.0 %convolution_convert_fusion = bf16[512,5120]{1,0:T(8,128)(2,1)} fusion(bf16[64,5120]{1,0:T(8,128)(2,1)S(1)} %slice_dynamic-update-slice_fusion.2, s32[64]{0:T(128)S(1)} %copy-done.3), kind=kOutput, calls=%fused_computation | convolution fusion | flops 338198528 | bytes 5898496 | tf_op jit(solution)/shard_map/dot_general | solution.py:249
  (117 shorter events, 22.1 us)
Async XLA Ops:
  4.5 11.4 %collective-permute-start.1 = (bf16[64,1280]{1,0:T(8,128)(2,1)S(1)}, bf16[64,1280]{1,0:T(8,128)(2,1)S(1)}, u32[]{:S(2)}, u32[]{:S(2)}) collective-permute-start(bf16[64,1280]{1,0:T(8,128)(2,1)S(1)} %pad_maximum_fusion.15), channel_id=1, source_target_pairs={{0,24},{4,28},{8,16},{12,20},{16,8},{20,12},{24,0},{28,4},{1,25},{... | collective-permute-start | bytes 491528 | tf_op jit(solution)/shard_map/ppermute | solution.py:69
  9.6 8.9 %collective-permute-start = (bf16[64,1280]{1,0:T(8,128)(2,1)S(1)}, bf16[64,1280]{1,0:T(8,128)(2,1)S(1)}, u32[]{:S(2)}, u32[]{:S(2)}) collective-permute-start(bf16[64,1280]{1,0:T(8,128)(2,1)S(1)} %pad_maximum_fusion.14), channel_id=1, source_target_pairs={{0,8},{4,12},{8,0},{12,4},{16,24},{20,28},{24,16},{28,20},{1,9},{5... | collective-permute-start | bytes 491528 | tf_op jit(solution)/shard_map/ppermute | solution.py:69
  9.7 22.1 %collective-permute-start.7 = (bf16[640,384]{1,0:T(8,128)(2,1)S(1)}, bf16[640,384]{1,0:T(8,128)(2,1)S(1)}, u32[]{:S(2)}, u32[]{:S(2)}) collective-permute-start(bf16[640,384]{1,0:T(8,128)(2,1)S(1)} %copy-done.1), channel_id=1, source_target_pairs={{0,4},{4,0},{8,12},{12,8},{16,20},{20,16},{24,28},{28,24},{1,5},{5... | collective-permute-start | bytes 1474568 | tf_op jit(solution)/shard_map/ppermute | solution.py:73
  11.3 21.7 %collective-permute-start.6 = (bf16[640,384]{1,0:T(8,128)(2,1)S(1)}, bf16[640,384]{1,0:T(8,128)(2,1)S(1)}, u32[]{:S(2)}, u32[]{:S(2)}) collective-permute-start(bf16[640,384]{1,0:T(8,128)(2,1)S(1)} %copy-done.2), channel_id=1, source_target_pairs={{0,4},{4,0},{8,12},{12,8},{16,20},{20,16},{24,28},{28,24},{1,5},{5... | collective-permute-start | bytes 1474568 | tf_op jit(solution)/shard_map/ppermute | solution.py:73
  11.8 3.5 %collective-permute-start.16 = (bf16[64]{0:T(256)(128)(2,1)S(1)}, bf16[64]{0:T(256)(128)(2,1)S(1)}, u32[]{:S(2)}, u32[]{:S(2)}) collective-permute-start(bf16[64]{0:T(256)(128)(2,1)S(1)} %copy-done.4), channel_id=1, source_target_pairs={{0,2},{1,3},{2,0},{3,1},{4,6},{5,7},{6,4},{7,5},{8,10},{9,11},{10,... | collective-permute-start | bytes 392 | tf_op jit(solution)/shard_map/ppermute | solution.py:77
  15.4 8.7 %collective-permute-start.10 = (bf16[64,1280]{1,0:T(8,128)(2,1)S(1)}, bf16[64,1280]{1,0:T(8,128)(2,1)S(1)}, u32[]{:S(2)}, u32[]{:S(2)}) collective-permute-start(bf16[64,1280]{1,0:T(8,128)(2,1)S(1)} %pad_maximum_fusion.16), channel_id=1, source_target_pairs={{0,16},{4,20},{8,24},{12,28},{16,0},{20,4},{24,8},{28,12},{1,17},{... | collective-permute-start | bytes 491528 | tf_op jit(solution)/shard_map/ppermute | solution.py:69
  15.9 4.3 %collective-permute-start.17 = (bf16[128]{0:T(256)(128)(2,1)S(1)}, bf16[128]{0:T(256)(128)(2,1)S(1)}, u32[]{:S(2)}, u32[]{:S(2)}) collective-permute-start(bf16[128]{0:T(256)(128)(2,1)S(1)} %pad_maximum_fusion.17), channel_id=1, source_target_pairs={{0,1},{1,0},{2,3},{3,2},{4,5},{5,4},{6,7},{7,6},{8,9},{9,8},{10,11... | collective-permute-start | bytes 776 | tf_op jit(solution)/shard_map/ppermute | solution.py:77
  18.6 7.1 %collective-permute-start.2 = (bf16[64,1280]{1,0:T(8,128)(2,1)S(1)}, bf16[64,1280]{1,0:T(8,128)(2,1)S(1)}, u32[]{:S(2)}, u32[]{:S(2)}) collective-permute-start(bf16[64,1280]{1,0:T(8,128)(2,1)S(1)} %get-tuple-element.87), channel_id=1, source_target_pairs={{0,2},{1,3},{2,0},{3,1},{4,6},{5,7},{6,4},{7,5},{8,10},{9,11},{10,... | collective-permute-start | bytes 491528 | tf_op jit(solution)/shard_map/ppermute | solution.py:77
  20.4 8.9 %collective-permute-start.4 = (bf16[64,1280]{1,0:T(8,128)(2,1)S(1)}, bf16[64,1280]{1,0:T(8,128)(2,1)S(1)}, u32[]{:S(2)}, u32[]{:S(2)}) collective-permute-start(bf16[64,1280]{1,0:T(8,128)(2,1)S(1)} %get-tuple-element.86), channel_id=1, source_target_pairs={{0,2},{1,3},{2,0},{3,1},{4,6},{5,7},{6,4},{7,5},{8,10},{9,11},{10,... | collective-permute-start | bytes 491528 | tf_op jit(solution)/shard_map/ppermute | solution.py:77
  24.1 7.8 %collective-permute-start.11 = (bf16[64,1280]{1,0:T(8,128)(2,1)S(1)}, bf16[64,1280]{1,0:T(8,128)(2,1)S(1)}, u32[]{:S(2)}, u32[]{:S(2)}) collective-permute-start(bf16[64,1280]{1,0:T(8,128)(2,1)S(1)} %collective-permute-done.10), channel_id=1, source_target_pairs={{0,2},{1,3},{2,0},{3,1},{4,6},{5,7},{6,4},{7,5},{8,10},{9,11},{10,... | collective-permute-start | bytes 491528 | tf_op jit(solution)/shard_map/ppermute | solution.py:77
  25.8 9.9 %collective-permute-start.3 = (bf16[128,1280]{1,0:T(8,128)(2,1)S(1)}, bf16[128,1280]{1,0:T(8,128)(2,1)S(1)}, u32[]{:S(2)}, u32[]{:S(2)}) collective-permute-start(bf16[128,1280]{1,0:T(8,128)(2,1)S(1)} %pad_maximum_fusion.8), channel_id=1, source_target_pairs={{0,1},{1,0},{2,3},{3,2},{4,5},{5,4},{6,7},{7,6},{8,9},{9,8},{10,11... | collective-permute-start | bytes 983048 | tf_op jit(solution)/shard_map/ppermute | solution.py:77
  29.3 3.9 %collective-permute-start.5 = (bf16[128,1280]{1,0:T(8,128)(2,1)S(1)}, bf16[128,1280]{1,0:T(8,128)(2,1)S(1)}, u32[]{:S(2)}, u32[]{:S(2)}) collective-permute-start(bf16[128,1280]{1,0:T(8,128)(2,1)S(1)} %pad_maximum_fusion.9), channel_id=1, source_target_pairs={{0,1},{1,0},{2,3},{3,2},{4,5},{5,4},{6,7},{7,6},{8,9},{9,8},{10,11... | collective-permute-start | bytes 983048 | tf_op jit(solution)/shard_map/ppermute | solution.py:77
  33.9 9.7 %collective-permute-start.13 = (bf16[256,768]{1,0:T(8,128)(2,1)S(1)}, bf16[256,768]{1,0:T(8,128)(2,1)S(1)}, u32[]{:S(2)}, u32[]{:S(2)}) collective-permute-start(bf16[256,768]{1,0:T(8,128)(2,1)S(1)} %convolution_convert_fusion.3), channel_id=1, source_target_pairs={{0,8},{4,12},{8,0},{12,4},{16,24},{20,28},{24,16},{28,20},{1,9},{5... | collective-permute-start | bytes 1179656 | tf_op jit(solution)/shard_map/ppermute | solution.py:108
  36.4 12.3 %collective-permute-start.14 = (bf16[256,768]{1,0:T(8,128)(2,1)S(1)}, bf16[256,768]{1,0:T(8,128)(2,1)S(1)}, u32[]{:S(2)}, u32[]{:S(2)}) collective-permute-start(bf16[256,768]{1,0:T(8,128)(2,1)S(1)} %convolution_convert_fusion.2), channel_id=1, source_target_pairs={{8,16},{12,20},{16,8},{20,12},{9,17},{13,21},{17,9},{21,13},{10,18... | collective-permute-start | bytes 1179656 | tf_op jit(solution)/shard_map/ppermute | solution.py:108
  37.1 5.4 %collective-permute-start.8 = (bf16[64,1280]{1,0:T(8,128)(2,1)S(1)}, bf16[64,1280]{1,0:T(8,128)(2,1)S(1)}, u32[]{:S(2)}, u32[]{:S(2)}) collective-permute-start(bf16[64,1280]{1,0:T(8,128)(2,1)S(1)} %pad_maximum_fusion.13), channel_id=1, source_target_pairs={{0,2},{1,3},{2,0},{3,1},{4,6},{5,7},{6,4},{7,5},{8,10},{9,11},{10,... | collective-permute-start | bytes 491528 | tf_op jit(solution)/shard_map/ppermute | solution.py:77
  38.6 3.9 %collective-permute-start.12 = (bf16[128,1280]{1,0:T(8,128)(2,1)S(1)}, bf16[128,1280]{1,0:T(8,128)(2,1)S(1)}, u32[]{:S(2)}, u32[]{:S(2)}) collective-permute-start(bf16[128,1280]{1,0:T(8,128)(2,1)S(1)} %pad_maximum_fusion.11), channel_id=1, source_target_pairs={{0,1},{1,0},{2,3},{3,2},{4,5},{5,4},{6,7},{7,6},{8,9},{9,8},{10,11... | collective-permute-start | bytes 983048 | tf_op jit(solution)/shard_map/ppermute | solution.py:77
  42.5 6.1 %collective-permute-start.9 = (bf16[128,1280]{1,0:T(8,128)(2,1)S(1)}, bf16[128,1280]{1,0:T(8,128)(2,1)S(1)}, u32[]{:S(2)}, u32[]{:S(2)}) collective-permute-start(bf16[128,1280]{1,0:T(8,128)(2,1)S(1)} %pad_maximum_fusion.10), channel_id=1, source_target_pairs={{0,1},{1,0},{2,3},{3,2},{4,5},{5,4},{6,7},{7,6},{8,9},{9,8},{10,11... | collective-permute-start | bytes 983048 | tf_op jit(solution)/shard_map/ppermute | solution.py:77
  44.4 13.4 %collective-permute-start.15 = (bf16[256,768]{1,0:T(8,128)(2,1)S(1)}, bf16[256,768]{1,0:T(8,128)(2,1)S(1)}, u32[]{:S(2)}, u32[]{:S(2)}) collective-permute-start(bf16[256,768]{1,0:T(8,128)(2,1)S(1)} %convert_element_type.88), channel_id=1, source_target_pairs={{0,16},{4,20},{24,8},{28,12},{1,17},{5,21},{25,9},{29,13},{2,18},{... | collective-permute-start | bytes 1179656 | tf_op jit(solution)/shard_map/ppermute | solution.py:108
  48.5 18.6 %collective-permute-start.18 = (bf16[256,768]{1,0:T(8,128)(2,1)S(1)}, bf16[256,768]{1,0:T(8,128)(2,1)S(1)}, u32[]{:S(2)}, u32[]{:S(2)}) collective-permute-start(bf16[256,768]{1,0:T(8,128)(2,1)S(1)} %fusion.18), channel_id=1, source_target_pairs={{16,0},{20,4},{24,16},{28,20},{8,24},{12,28},{0,8},{4,12},{17,1},{... | collective-permute-start | bytes 1179656 | tf_op jit(solution)/shard_map/ppermute | solution.py:108
  69.4 3.1 %collective-permute-start.19 = (bf16[128,1280]{1,0:T(8,128)(2,1)S(1)}, bf16[128,1280]{1,0:T(8,128)(2,1)S(1)}, u32[]{:S(2)}, u32[]{:S(2)}) collective-permute-start(bf16[128,1280]{1,0:T(8,128)(2,1)S(1)} %slice.245), channel_id=1, source_target_pairs={{0,1},{1,0},{2,3},{3,2},{4,5},{5,4},{6,7},{7,6},{8,9},{9,8},{10,11... | collective-permute-start | bytes 983048 | tf_op jit(solution)/shard_map/ppermute | solution.py:77
  69.7 11.6 %collective-permute-start.21 = (bf16[256,768]{1,0:T(8,128)(2,1)S(1)}, bf16[256,768]{1,0:T(8,128)(2,1)S(1)}, u32[]{:S(2)}, u32[]{:S(2)}) collective-permute-start(bf16[256,768]{1,0:T(8,128)(2,1)S(1)} %get-tuple-element.46), channel_id=1, source_target_pairs={{0,16},{4,20},{16,24},{20,28},{24,8},{28,12},{8,0},{12,4},{1,17},{... | collective-permute-start | bytes 1179656 | tf_op jit(solution)/shard_map/ppermute | solution.py:108
  70.3 20.9 %collective-permute-start.22 = (bf16[256,768]{1,0:T(8,128)(2,1)S(1)}, bf16[256,768]{1,0:T(8,128)(2,1)S(1)}, u32[]{:S(2)}, u32[]{:S(2)}) collective-permute-start(bf16[256,768]{1,0:T(8,128)(2,1)S(1)} %get-tuple-element.46), channel_id=1, source_target_pairs={{16,0},{20,4},{8,24},{12,28},{17,1},{21,5},{9,25},{13,29},{18,2},{... | collective-permute-start | bytes 1179656 | tf_op jit(solution)/shard_map/ppermute | solution.py:108
  71.6 21.3 %collective-permute-start.23 = (bf16[256,768]{1,0:T(8,128)(2,1)S(1)}, bf16[256,768]{1,0:T(8,128)(2,1)S(1)}, u32[]{:S(2)}, u32[]{:S(2)}) collective-permute-start(bf16[256,768]{1,0:T(8,128)(2,1)S(1)} %get-tuple-element.46), channel_id=1, source_target_pairs={{8,16},{12,20},{16,8},{20,12},{9,17},{13,21},{17,9},{21,13},{10,18... | collective-permute-start | bytes 1179656 | tf_op jit(solution)/shard_map/ppermute | solution.py:108
  72.6 20.4 %collective-permute-start.20 = (bf16[64,1280]{1,0:T(8,128)(2,1)S(1)}, bf16[64,1280]{1,0:T(8,128)(2,1)S(1)}, u32[]{:S(2)}, u32[]{:S(2)}) collective-permute-start(bf16[64,1280]{1,0:T(8,128)(2,1)S(1)} %slice.249), channel_id=1, source_target_pairs={{0,2},{1,3},{2,0},{3,1},{4,6},{5,7},{6,4},{7,5},{8,10},{9,11},{10,... | collective-permute-start | bytes 491528 | tf_op jit(solution)/shard_map/ppermute | solution.py:77
  81.4 18.2 %collective-permute-start.24 = (bf16[256,768]{1,0:T(8,128)(2,1)S(1)}, bf16[256,768]{1,0:T(8,128)(2,1)S(1)}, u32[]{:S(2)}, u32[]{:S(2)}) collective-permute-start(bf16[256,768]{1,0:T(8,128)(2,1)S(1)} %broadcast_select_fusion.2), channel_id=1, source_target_pairs={{0,8},{4,12},{8,0},{12,4},{16,24},{20,28},{24,16},{28,20},{1,9},{5... | collective-permute-start | bytes 1179656 | tf_op jit(solution)/shard_map/ppermute | solution.py:108
  94.6 6.3 %collective-permute-start.26 = (bf16[64,1280]{1,0:T(8,128)(2,1)S(1)}, bf16[64,1280]{1,0:T(8,128)(2,1)S(1)}, u32[]{:S(2)}, u32[]{:S(2)}) collective-permute-start(bf16[64,1280]{1,0:T(8,128)(2,1)S(1)} %slice.248), channel_id=1, source_target_pairs={{0,2},{1,3},{2,0},{3,1},{4,6},{5,7},{6,4},{7,5},{8,10},{9,11},{10,... | collective-permute-start | bytes 491528 | tf_op jit(solution)/shard_map/ppermute | solution.py:77
  102.6 6.9 %collective-permute-start.27 = (bf16[256,1280]{1,0:T(8,128)(2,1)S(1)}, bf16[256,1280]{1,0:T(8,128)(2,1)S(1)}, u32[]{:S(2)}, u32[]{:S(2)}) collective-permute-start(bf16[256,1280]{1,0:T(8,128)(2,1)S(1)} %pad_maximum_fusion.7), channel_id=1, source_target_pairs={{0,1},{1,0},{2,3},{3,2},{4,5},{5,4},{6,7},{7,6},{8,9},{9,8},{10,11... | collective-permute-start | bytes 1966088 | tf_op jit(solution)/shard_map/ppermute | solution.py:77
  102.6 30.9 %collective-permute-start.32 = (bf16[640,768]{1,0:T(8,128)(2,1)S(1)}, bf16[640,768]{1,0:T(8,128)(2,1)S(1)}, u32[]{:S(2)}, u32[]{:S(2)}) collective-permute-start(bf16[640,768]{1,0:T(8,128)(2,1)S(1)} %add_convert_fusion), channel_id=1, source_target_pairs={{0,4},{4,0},{8,12},{12,8},{16,20},{20,16},{24,28},{28,24},{1,5},{5... | collective-permute-start | bytes 2949128 | tf_op jit(solution)/shard_map/ppermute | solution.py:73
  104.3 15.1 %collective-permute-start.29 = (bf16[64,1280]{1,0:T(8,128)(2,1)S(1)}, bf16[64,1280]{1,0:T(8,128)(2,1)S(1)}, u32[]{:S(2)}, u32[]{:S(2)}) collective-permute-start(bf16[64,1280]{1,0:T(8,128)(2,1)S(1)} %fusion.21), channel_id=1, source_target_pairs={{0,16},{4,20},{8,24},{12,28},{16,0},{20,4},{24,8},{28,12},{1,17},{... | collective-permute-start | bytes 491528 | tf_op jit(solution)/shard_map/ppermute | solution.py:69
  109.7 9.6 %collective-permute-start.28 = (bf16[128,1280]{1,0:T(8,128)(2,1)S(1)}, bf16[128,1280]{1,0:T(8,128)(2,1)S(1)}, u32[]{:S(2)}, u32[]{:S(2)}) collective-permute-start(bf16[128,1280]{1,0:T(8,128)(2,1)S(1)} %pad_maximum_fusion.12), channel_id=1, source_target_pairs={{0,2},{1,3},{2,0},{3,1},{4,6},{5,7},{6,4},{7,5},{8,10},{9,11},{10,... | collective-permute-start | bytes 983048 | tf_op jit(solution)/shard_map/ppermute | solution.py:77
  119.4 10.0 %collective-permute-start.30 = (bf16[64,1280]{1,0:T(8,128)(2,1)S(1)}, bf16[64,1280]{1,0:T(8,128)(2,1)S(1)}, u32[]{:S(2)}, u32[]{:S(2)}) collective-permute-start(bf16[64,1280]{1,0:T(8,128)(2,1)S(1)} %broadcast_select_fusion.4), channel_id=1, source_target_pairs={{0,8},{4,12},{8,0},{12,4},{16,24},{20,28},{24,16},{28,20},{1,9},{5... | collective-permute-start | bytes 491528 | tf_op jit(solution)/shard_map/ppermute | solution.py:69
  120.6 8.8 %collective-permute-start.31 = (bf16[64,1280]{1,0:T(8,128)(2,1)S(1)}, bf16[64,1280]{1,0:T(8,128)(2,1)S(1)}, u32[]{:S(2)}, u32[]{:S(2)}) collective-permute-start(bf16[64,1280]{1,0:T(8,128)(2,1)S(1)} %get-tuple-element.60), channel_id=1, source_target_pairs={{0,24},{4,28},{8,16},{12,20},{16,8},{20,12},{24,0},{28,4},{1,25},{... | collective-permute-start | bytes 491528 | tf_op jit(solution)/shard_map/ppermute | solution.py:69
  (7 other events, 73.1 us)

commit v21 on v20

--- a/solution.py
+++ b/solution.py
@@ -230,7 +230,7 @@
         arriving = [over_inner(leaving[j - 1], j) for j in range(1, inner)]
         last = leaving[0] if inner > 1 else last
         if late:
-            last = advance(late, after(last, *[sums[k] for k in early]))
+            last = advance(late, last)
         total = weight_grad(sequence, 0, last)
         last = sums[sequence[-1]]
         returned = {0: sums[0]}

time: 135 us -> 134 us (level)
  starting transfers between devices: 40.9 us -> 33.1 us
  waiting for transfers between devices: 71.3 us -> 78.4 us
    ppermute x6, starting transfers between devices: 13.9 us -> 7.13 us  [over_outer(): return lax.ppermute(value, 'dp', pairs)]
    ppermute x6, waiting for transfers between devices: 12.5 us -> 16.5 us  [over_outer(): return lax.ppermute(value, 'dp', pairs)]
    ppermute x8, waiting for transfers between devices: 37.1 us -> 40.2 us  [outer_pairs(): return lax.ppermute(value, 'dp', pairs)]
  transfers between devices with their start and end apart: 33 -> 33, of which waited for: 18 -> 19; matrix products, arithmetic and copies ran while one was open for 9% -> 10% of each run, Pallas kernels for 0% -> 0%
where the time goes in v21:
time: 134 us
  waiting for transfers between devices  78.4 us (59%)
  starting transfers between devices  33.1 us (25%)
  matrix products  15.8 us (12%)
  other arithmetic  3.15 us (2%)
  Pallas kernels  1.51 us (1%)
  between operations  1.36 us (1%)
    ppermute x8, waiting for transfers between devices, outer_pairs(): return lax.ppermute(value, 'dp', pairs)  40.2 us
    ppermute x16, waiting for transfers between devices, over_etp(): return lax.ppermute(value, 'etp', pairs)  20.5 us
    ppermute x6, waiting for transfers between devices, over_outer(): return lax.ppermute(value, 'dp', pairs)  16.5 us
    ppermute x8, starting transfers between devices, outer_pairs(): return lax.ppermute(value, 'dp', pairs)  11.4 us
    ppermute x16, starting transfers between devices, over_etp(): return lax.ppermute(value, 'etp', pairs)  11 us
    ppermute x6, starting transfers between devices, over_outer(): return lax.ppermute(value, 'dp', pairs)  7.13 us
    dot_general x1, matrix products, shards(): lax.dot_general(onehot, dx, (((0,), (0,)), ((), ())), preferred_element_t...  4 us
    ppermute x3, starting transfers between devices, over_inner(): return lax.ppermute(value, 'dp', pairs)  3.59 us
  transfers between devices with their start and end apart: 33, of which 19 were waited for; matrix products, arithmetic and copies ran while one was open for 10% of the time, Pallas kernels for 0%

profile of v21, /device:TPU:0, one launch (start us, length us, event | category | flops | bytes accessed | tf_op | source)
XLA Modules:
  0.0 134.2 jit_solution(6180923774937167642)
XLA Ops:
  0.7 3.6 %convolution_convert_fusion.1 = bf16[64,5120]{1,0:T(8,128)(2,1)S(1)} fusion(bf16[512,5120]{1,0:T(8,128)(2,1)} %param.7, s32[64]{0:T(128)} %param.8), kind=kOutput, calls=%fused_computation.1 | convolution fusion | flops 335904768 | bytes 5898496 | tf_op jit(solution)/shard_map/dot_general | solution.py:136
  4.5 5.1 %collective-permute-start.1 = (bf16[64,1280]{1,0:T(8,128)(2,1)S(1)}, bf16[64,1280]{1,0:T(8,128)(2,1)S(1)}, u32[]{:S(2)}, u32[]{:S(2)}) collective-permute-start(bf16[64,1280]{1,0:T(8,128)(2,1)S(1)} %pad_maximum_fusion.15), channel_id=1, source_target_pairs={{0,24},{4,28},{8,16},{12,20},{16,8},{20,12},{24,0},{28,4},{1,25},{... | collective-permute-start | bytes 491528 | tf_op jit(solution)/shard_map/ppermute | solution.py:69
  9.7 1.6 %collective-permute-start.7 = (bf16[640,384]{1,0:T(8,128)(2,1)S(1)}, bf16[640,384]{1,0:T(8,128)(2,1)S(1)}, u32[]{:S(2)}, u32[]{:S(2)}) collective-permute-start(bf16[640,384]{1,0:T(8,128)(2,1)S(1)} %copy-done.1), channel_id=1, source_target_pairs={{0,4},{4,0},{8,12},{12,8},{16,20},{20,16},{24,28},{28,24},{1,5},{5... | collective-permute-start | bytes 1474568 | tf_op jit(solution)/shard_map/ppermute | solution.py:73
  11.8 1.5 %collective-permute-start.16 = (bf16[64]{0:T(256)(128)(2,1)S(1)}, bf16[64]{0:T(256)(128)(2,1)S(1)}, u32[]{:S(2)}, u32[]{:S(2)}) collective-permute-start(bf16[64]{0:T(256)(128)(2,1)S(1)} %copy-done.4), channel_id=1, source_target_pairs={{0,2},{1,3},{2,0},{3,1},{4,6},{5,7},{6,4},{7,5},{8,10},{9,11},{10,... | collective-permute-start | bytes 392 | tf_op jit(solution)/shard_map/ppermute | solution.py:77
  13.4 2.0 %collective-permute-done.16 = bf16[64]{0:T(256)(128)(2,1)S(1)} collective-permute-done((bf16[64]{0:T(256)(128)(2,1)S(1)}, bf16[64]{0:T(256)(128)(2,1)S(1)}, u32[]{:S(2)}, u32[]{:S(2)}) %collective-permute-start.16) | collective-permute-done | bytes 160 | tf_op jit(solution)/shard_map/ppermute | solution.py:77
  16.0 2.6 %collective-permute-done = bf16[64,1280]{1,0:T(8,128)(2,1)S(1)} collective-permute-done((bf16[64,1280]{1,0:T(8,128)(2,1)S(1)}, bf16[64,1280]{1,0:T(8,128)(2,1)S(1)}, u32[]{:S(2)}, u32[]{:S(2)}) %collective-permute-start) | collective-permute-done | bytes 163872 | tf_op jit(solution)/shard_map/ppermute | solution.py:69
  18.6 1.6 %collective-permute-start.2 = (bf16[64,1280]{1,0:T(8,128)(2,1)S(1)}, bf16[64,1280]{1,0:T(8,128)(2,1)S(1)}, u32[]{:S(2)}, u32[]{:S(2)}) collective-permute-start(bf16[64,1280]{1,0:T(8,128)(2,1)S(1)} %get-tuple-element.85), channel_id=1, source_target_pairs={{0,2},{1,3},{2,0},{3,1},{4,6},{5,7},{6,4},{7,5},{8,10},{9,11},{10,... | collective-permute-start | bytes 491528 | tf_op jit(solution)/shard_map/ppermute | solution.py:77
  21.0 3.1 %collective-permute-done.10 = bf16[64,1280]{1,0:T(8,128)(2,1)S(1)} collective-permute-done((bf16[64,1280]{1,0:T(8,128)(2,1)S(1)}, bf16[64,1280]{1,0:T(8,128)(2,1)S(1)}, u32[]{:S(2)}, u32[]{:S(2)}) %collective-permute-start.10) | collective-permute-done | bytes 163872 | tf_op jit(solution)/shard_map/ppermute | solution.py:69
  24.1 1.5 %collective-permute-start.11 = (bf16[64,1280]{1,0:T(8,128)(2,1)S(1)}, bf16[64,1280]{1,0:T(8,128)(2,1)S(1)}, u32[]{:S(2)}, u32[]{:S(2)}) collective-permute-start(bf16[64,1280]{1,0:T(8,128)(2,1)S(1)} %collective-permute-done.10), channel_id=1, source_target_pairs={{0,2},{1,3},{2,0},{3,1},{4,6},{5,7},{6,4},{7,5},{8,10},{9,11},{10,... | collective-permute-start | bytes 491528 | tf_op jit(solution)/shard_map/ppermute | solution.py:77
  25.8 3.4 %collective-permute-done.4 = bf16[64,1280]{1,0:T(8,128)(2,1)S(1)} collective-permute-done((bf16[64,1280]{1,0:T(8,128)(2,1)S(1)}, bf16[64,1280]{1,0:T(8,128)(2,1)S(1)}, u32[]{:S(2)}, u32[]{:S(2)}) %collective-permute-start.4) | collective-permute-done | bytes 163872 | tf_op jit(solution)/shard_map/ppermute | solution.py:77
  29.3 2.5 %collective-permute-done.11 = bf16[64,1280]{1,0:T(8,128)(2,1)S(1)} collective-permute-done((bf16[64,1280]{1,0:T(8,128)(2,1)S(1)}, bf16[64,1280]{1,0:T(8,128)(2,1)S(1)}, u32[]{:S(2)}, u32[]{:S(2)}) %collective-permute-start.11) | collective-permute-done | bytes 163872 | tf_op jit(solution)/shard_map/ppermute | solution.py:77
  33.9 1.7 %collective-permute-start.13 = (bf16[256,768]{1,0:T(8,128)(2,1)S(1)}, bf16[256,768]{1,0:T(8,128)(2,1)S(1)}, u32[]{:S(2)}, u32[]{:S(2)}) collective-permute-start(bf16[256,768]{1,0:T(8,128)(2,1)S(1)} %convolution_convert_fusion.3), channel_id=1, source_target_pairs={{0,8},{4,12},{8,0},{12,4},{16,24},{20,28},{24,16},{28,20},{1,9},{5... | collective-permute-start | bytes 1179656 | tf_op jit(solution)/shard_map/ppermute | solution.py:108
  37.1 1.6 %collective-permute-start.8 = (bf16[64,1280]{1,0:T(8,128)(2,1)S(1)}, bf16[64,1280]{1,0:T(8,128)(2,1)S(1)}, u32[]{:S(2)}, u32[]{:S(2)}) collective-permute-start(bf16[64,1280]{1,0:T(8,128)(2,1)S(1)} %pad_maximum_fusion.13), channel_id=1, source_target_pairs={{0,2},{1,3},{2,0},{3,1},{4,6},{5,7},{6,4},{7,5},{8,10},{9,11},{10,... | collective-permute-start | bytes 491528 | tf_op jit(solution)/shard_map/ppermute | solution.py:77
  38.7 3.7 %collective-permute-done.8 = bf16[64,1280]{1,0:T(8,128)(2,1)S(1)} collective-permute-done((bf16[64,1280]{1,0:T(8,128)(2,1)S(1)}, bf16[64,1280]{1,0:T(8,128)(2,1)S(1)}, u32[]{:S(2)}, u32[]{:S(2)}) %collective-permute-start.8) | collective-permute-done | bytes 163872 | tf_op jit(solution)/shard_map/ppermute | solution.py:77
  44.4 4.0 %collective-permute-start.15 = (bf16[256,768]{1,0:T(8,128)(2,1)S(1)}, bf16[256,768]{1,0:T(8,128)(2,1)S(1)}, u32[]{:S(2)}, u32[]{:S(2)}) collective-permute-start(bf16[256,768]{1,0:T(8,128)(2,1)S(1)} %convert_element_type.88), channel_id=1, source_target_pairs={{0,16},{4,20},{24,8},{28,12},{1,17},{5,21},{25,9},{29,13},{2,18},{... | collective-permute-start | bytes 1179656 | tf_op jit(solution)/shard_map/ppermute | solution.py:108
  48.6 9.2 %collective-permute-done.15 = bf16[256,768]{1,0:T(8,128)(2,1)S(1)} collective-permute-done((bf16[256,768]{1,0:T(8,128)(2,1)S(1)}, bf16[256,768]{1,0:T(8,128)(2,1)S(1)}, u32[]{:S(2)}, u32[]{:S(2)}) %collective-permute-start.15) | collective-permute-done | bytes 393248 | tf_op jit(solution)/shard_map/ppermute | solution.py:108
  58.5 8.6 %collective-permute-done.18.refs_0_ = bf16[256,768]{1,0:T(8,128)(2,1)S(1)} collective-permute-done((bf16[256,768]{1,0:T(8,128)(2,1)S(1)}, bf16[256,768]{1,0:T(8,128)(2,1)S(1)}, u32[]{:S(2)}, u32[]{:S(2)}) %collective-permute-start.18) | collective-permute-done | bytes 393248 | tf_op jit(solution)/shard_map/ppermute | solution.py:108
  67.1 1.5 %shard_map.102 = (bf16[256,384]{1,0:T(8,128)(2,1)}, bf16[256,768]{1,0:T(8,128)(2,1)S(1)}) custom-call(s32[4]{0:T(128)S(1)} %broadcast_xor_fusion.order_ref, f32[256,768]{1,0:T(8,128)S(1)} %fusion.9.pre_ref, bf16[256,1]{1,0:T(8,128)(2,1)S(1)} %broadcast_in_dim.15.prob_ref, bf16[256,384]{1,0:T(8,128)(2,1)S(1)} %copy-done, ...), custom_call_target="tpu_custom_call" | custom-call | flops 1966080 | bytes 2949120 | tf_op jit(solution)/shard_map/pallas_call | solution.py:49
  70.3 1.3 collective-permute-start.22
  72.6 1.6 %collective-permute-start.20 = (bf16[64,1280]{1,0:T(8,128)(2,1)S(1)}, bf16[64,1280]{1,0:T(8,128)(2,1)S(1)}, u32[]{:S(2)}, u32[]{:S(2)}) collective-permute-start(bf16[64,1280]{1,0:T(8,128)(2,1)S(1)} %slice.249), channel_id=1, source_target_pairs={{0,2},{1,3},{2,0},{3,1},{4,6},{5,7},{6,4},{7,5},{8,10},{9,11},{10,... | collective-permute-start | bytes 491528 | tf_op jit(solution)/shard_map/ppermute | solution.py:77
  74.2 7.1 %collective-permute-done.21 = bf16[256,768]{1,0:T(8,128)(2,1)S(1)} collective-permute-done((bf16[256,768]{1,0:T(8,128)(2,1)S(1)}, bf16[256,768]{1,0:T(8,128)(2,1)S(1)}, u32[]{:S(2)}, u32[]{:S(2)}) %collective-permute-start.21) | collective-permute-done | bytes 393248 | tf_op jit(solution)/shard_map/ppermute | solution.py:108
  81.4 2.1 %collective-permute-start.24 = (bf16[256,768]{1,0:T(8,128)(2,1)S(1)}, bf16[256,768]{1,0:T(8,128)(2,1)S(1)}, u32[]{:S(2)}, u32[]{:S(2)}) collective-permute-start(bf16[256,768]{1,0:T(8,128)(2,1)S(1)} %broadcast_select_fusion.2), channel_id=1, source_target_pairs={{0,8},{4,12},{8,0},{12,4},{16,24},{20,28},{24,16},{28,20},{1,9},{5... | collective-permute-start | bytes 1179656 | tf_op jit(solution)/shard_map/ppermute | solution.py:108
  83.5 7.8 %collective-permute-done.22 = bf16[256,768]{1,0:T(8,128)(2,1)S(1)} collective-permute-done((bf16[256,768]{1,0:T(8,128)(2,1)S(1)}, bf16[256,768]{1,0:T(8,128)(2,1)S(1)}, u32[]{:S(2)}, u32[]{:S(2)}) %collective-permute-start.22) | collective-permute-done | bytes 393248 | tf_op jit(solution)/shard_map/ppermute | solution.py:108
  93.0 6.5 %collective-permute-done.24 = bf16[256,768]{1,0:T(8,128)(2,1)S(1)} collective-permute-done((bf16[256,768]{1,0:T(8,128)(2,1)S(1)}, bf16[256,768]{1,0:T(8,128)(2,1)S(1)}, u32[]{:S(2)}, u32[]{:S(2)}) %collective-permute-start.24) | collective-permute-done | bytes 393248 | tf_op jit(solution)/shard_map/ppermute | solution.py:108
  102.1 1.6 %collective-permute-start.28 = (bf16[64,1280]{1,0:T(8,128)(2,1)S(1)}, bf16[64,1280]{1,0:T(8,128)(2,1)S(1)}, u32[]{:S(2)}, u32[]{:S(2)}) collective-permute-start(bf16[64,1280]{1,0:T(8,128)(2,1)S(1)} %slice.246), channel_id=1, source_target_pairs={{0,2},{1,3},{2,0},{3,1},{4,6},{5,7},{6,4},{7,5},{8,10},{9,11},{10,... | collective-permute-start | bytes 491528 | tf_op jit(solution)/shard_map/ppermute | solution.py:77
  103.7 1.5 %collective-permute-start.32 = (bf16[640,768]{1,0:T(8,128)(2,1)S(1)}, bf16[640,768]{1,0:T(8,128)(2,1)S(1)}, u32[]{:S(2)}, u32[]{:S(2)}) collective-permute-start(bf16[640,768]{1,0:T(8,128)(2,1)S(1)} %add_convert_fusion), channel_id=1, source_target_pairs={{0,4},{4,0},{8,12},{12,8},{16,20},{20,16},{24,28},{28,24},{1,5},{5... | collective-permute-start | bytes 2949128 | tf_op jit(solution)/shard_map/ppermute | solution.py:73
  107.4 1.4 %collective-permute-done.28 = bf16[64,1280]{1,0:T(8,128)(2,1)S(1)} collective-permute-done((bf16[64,1280]{1,0:T(8,128)(2,1)S(1)}, bf16[64,1280]{1,0:T(8,128)(2,1)S(1)}, u32[]{:S(2)}, u32[]{:S(2)}) %collective-permute-start.28) | collective-permute-done | bytes 163872 | tf_op jit(solution)/shard_map/ppermute | solution.py:77
  109.1 7.3 %collective-permute-done.26 = bf16[128,1280]{1,0:T(8,128)(2,1)S(1)} collective-permute-done((bf16[128,1280]{1,0:T(8,128)(2,1)S(1)}, bf16[128,1280]{1,0:T(8,128)(2,1)S(1)}, u32[]{:S(2)}, u32[]{:S(2)}) %collective-permute-start.26) | collective-permute-done | bytes 327712 | tf_op jit(solution)/shard_map/ppermute | solution.py:77
  116.5 2.6 %collective-permute-done.29 = bf16[64,1280]{1,0:T(8,128)(2,1)S(1)} collective-permute-done((bf16[64,1280]{1,0:T(8,128)(2,1)S(1)}, bf16[64,1280]{1,0:T(8,128)(2,1)S(1)}, u32[]{:S(2)}, u32[]{:S(2)}) %collective-permute-start.29) | collective-permute-done | bytes 163872 | tf_op jit(solution)/shard_map/ppermute | solution.py:69
  120.4 7.9 %collective-permute-done.31 = bf16[64,1280]{1,0:T(8,128)(2,1)S(1)} collective-permute-done((bf16[64,1280]{1,0:T(8,128)(2,1)S(1)}, bf16[64,1280]{1,0:T(8,128)(2,1)S(1)}, u32[]{:S(2)}, u32[]{:S(2)}) %collective-permute-start.31) | collective-permute-done | bytes 163872 | tf_op jit(solution)/shard_map/ppermute | solution.py:69
  128.8 4.0 %convolution_convert_fusion = bf16[512,5120]{1,0:T(8,128)(2,1)} fusion(bf16[64,5120]{1,0:T(8,128)(2,1)S(1)} %slice_dynamic-update-slice_fusion.2, s32[64]{0:T(128)S(1)} %copy-done.3), kind=kOutput, calls=%fused_computation | convolution fusion | flops 338198528 | bytes 5898496 | tf_op jit(solution)/shard_map/dot_general | solution.py:249
  132.8 1.4 %slice_add_fusion = (f32[640,384]{1,0:T(8,128)}, f32[640,384]{1,0:T(8,128)}) fusion(f32[640,768]{1,0:T(8,128)S(1)} %fusion, bf16[640,768]{1,0:T(8,128)(2,1)S(1)} %collective-permute-done.32), kind=kLoop, calls=%fused_computation.18 | loop fusion | flops 983040 | bytes 4915200 | tf_op jit(solution)/shard_map/add | solution.py:256
  (117 shorter events, 19.9 us)
Async XLA Ops:
  4.5 11.4 %collective-permute-start.1 = (bf16[64,1280]{1,0:T(8,128)(2,1)S(1)}, bf16[64,1280]{1,0:T(8,128)(2,1)S(1)}, u32[]{:S(2)}, u32[]{:S(2)}) collective-permute-start(bf16[64,1280]{1,0:T(8,128)(2,1)S(1)} %pad_maximum_fusion.15), channel_id=1, source_target_pairs={{0,24},{4,28},{8,16},{12,20},{16,8},{20,12},{24,0},{28,4},{1,25},{... | collective-permute-start | bytes 491528 | tf_op jit(solution)/shard_map/ppermute | solution.py:69
  9.6 8.9 %collective-permute-start = (bf16[64,1280]{1,0:T(8,128)(2,1)S(1)}, bf16[64,1280]{1,0:T(8,128)(2,1)S(1)}, u32[]{:S(2)}, u32[]{:S(2)}) collective-permute-start(bf16[64,1280]{1,0:T(8,128)(2,1)S(1)} %pad_maximum_fusion.14), channel_id=1, source_target_pairs={{0,8},{4,12},{8,0},{12,4},{16,24},{20,28},{24,16},{28,20},{1,9},{5... | collective-permute-start | bytes 491528 | tf_op jit(solution)/shard_map/ppermute | solution.py:69
  9.7 22.1 %collective-permute-start.7 = (bf16[640,384]{1,0:T(8,128)(2,1)S(1)}, bf16[640,384]{1,0:T(8,128)(2,1)S(1)}, u32[]{:S(2)}, u32[]{:S(2)}) collective-permute-start(bf16[640,384]{1,0:T(8,128)(2,1)S(1)} %copy-done.1), channel_id=1, source_target_pairs={{0,4},{4,0},{8,12},{12,8},{16,20},{20,16},{24,28},{28,24},{1,5},{5... | collective-permute-start | bytes 1474568 | tf_op jit(solution)/shard_map/ppermute | solution.py:73
  11.3 21.7 %collective-permute-start.6 = (bf16[640,384]{1,0:T(8,128)(2,1)S(1)}, bf16[640,384]{1,0:T(8,128)(2,1)S(1)}, u32[]{:S(2)}, u32[]{:S(2)}) collective-permute-start(bf16[640,384]{1,0:T(8,128)(2,1)S(1)} %copy-done.2), channel_id=1, source_target_pairs={{0,4},{4,0},{8,12},{12,8},{16,20},{20,16},{24,28},{28,24},{1,5},{5... | collective-permute-start | bytes 1474568 | tf_op jit(solution)/shard_map/ppermute | solution.py:73
  11.8 3.5 %collective-permute-start.16 = (bf16[64]{0:T(256)(128)(2,1)S(1)}, bf16[64]{0:T(256)(128)(2,1)S(1)}, u32[]{:S(2)}, u32[]{:S(2)}) collective-permute-start(bf16[64]{0:T(256)(128)(2,1)S(1)} %copy-done.4), channel_id=1, source_target_pairs={{0,2},{1,3},{2,0},{3,1},{4,6},{5,7},{6,4},{7,5},{8,10},{9,11},{10,... | collective-permute-start | bytes 392 | tf_op jit(solution)/shard_map/ppermute | solution.py:77
  15.4 8.7 %collective-permute-start.10 = (bf16[64,1280]{1,0:T(8,128)(2,1)S(1)}, bf16[64,1280]{1,0:T(8,128)(2,1)S(1)}, u32[]{:S(2)}, u32[]{:S(2)}) collective-permute-start(bf16[64,1280]{1,0:T(8,128)(2,1)S(1)} %pad_maximum_fusion.16), channel_id=1, source_target_pairs={{0,16},{4,20},{8,24},{12,28},{16,0},{20,4},{24,8},{28,12},{1,17},{... | collective-permute-start | bytes 491528 | tf_op jit(solution)/shard_map/ppermute | solution.py:69
  15.9 4.3 %collective-permute-start.17 = (bf16[128]{0:T(256)(128)(2,1)S(1)}, bf16[128]{0:T(256)(128)(2,1)S(1)}, u32[]{:S(2)}, u32[]{:S(2)}) collective-permute-start(bf16[128]{0:T(256)(128)(2,1)S(1)} %pad_maximum_fusion.17), channel_id=1, source_target_pairs={{0,1},{1,0},{2,3},{3,2},{4,5},{5,4},{6,7},{7,6},{8,9},{9,8},{10,11... | collective-permute-start | bytes 776 | tf_op jit(solution)/shard_map/ppermute | solution.py:77
  18.6 7.1 %collective-permute-start.2 = (bf16[64,1280]{1,0:T(8,128)(2,1)S(1)}, bf16[64,1280]{1,0:T(8,128)(2,1)S(1)}, u32[]{:S(2)}, u32[]{:S(2)}) collective-permute-start(bf16[64,1280]{1,0:T(8,128)(2,1)S(1)} %get-tuple-element.85), channel_id=1, source_target_pairs={{0,2},{1,3},{2,0},{3,1},{4,6},{5,7},{6,4},{7,5},{8,10},{9,11},{10,... | collective-permute-start | bytes 491528 | tf_op jit(solution)/shard_map/ppermute | solution.py:77
  20.4 8.9 %collective-permute-start.4 = (bf16[64,1280]{1,0:T(8,128)(2,1)S(1)}, bf16[64,1280]{1,0:T(8,128)(2,1)S(1)}, u32[]{:S(2)}, u32[]{:S(2)}) collective-permute-start(bf16[64,1280]{1,0:T(8,128)(2,1)S(1)} %get-tuple-element.84), channel_id=1, source_target_pairs={{0,2},{1,3},{2,0},{3,1},{4,6},{5,7},{6,4},{7,5},{8,10},{9,11},{10,... | collective-permute-start | bytes 491528 | tf_op jit(solution)/shard_map/ppermute | solution.py:77
  24.1 7.8 %collective-permute-start.11 = (bf16[64,1280]{1,0:T(8,128)(2,1)S(1)}, bf16[64,1280]{1,0:T(8,128)(2,1)S(1)}, u32[]{:S(2)}, u32[]{:S(2)}) collective-permute-start(bf16[64,1280]{1,0:T(8,128)(2,1)S(1)} %collective-permute-done.10), channel_id=1, source_target_pairs={{0,2},{1,3},{2,0},{3,1},{4,6},{5,7},{6,4},{7,5},{8,10},{9,11},{10,... | collective-permute-start | bytes 491528 | tf_op jit(solution)/shard_map/ppermute | solution.py:77
  25.8 9.9 %collective-permute-start.3 = (bf16[128,1280]{1,0:T(8,128)(2,1)S(1)}, bf16[128,1280]{1,0:T(8,128)(2,1)S(1)}, u32[]{:S(2)}, u32[]{:S(2)}) collective-permute-start(bf16[128,1280]{1,0:T(8,128)(2,1)S(1)} %pad_maximum_fusion.8), channel_id=1, source_target_pairs={{0,1},{1,0},{2,3},{3,2},{4,5},{5,4},{6,7},{7,6},{8,9},{9,8},{10,11... | collective-permute-start | bytes 983048 | tf_op jit(solution)/shard_map/ppermute | solution.py:77
  29.3 3.9 %collective-permute-start.5 = (bf16[128,1280]{1,0:T(8,128)(2,1)S(1)}, bf16[128,1280]{1,0:T(8,128)(2,1)S(1)}, u32[]{:S(2)}, u32[]{:S(2)}) collective-permute-start(bf16[128,1280]{1,0:T(8,128)(2,1)S(1)} %pad_maximum_fusion.9), channel_id=1, source_target_pairs={{0,1},{1,0},{2,3},{3,2},{4,5},{5,4},{6,7},{7,6},{8,9},{9,8},{10,11... | collective-permute-start | bytes 983048 | tf_op jit(solution)/shard_map/ppermute | solution.py:77
  33.9 9.7 %collective-permute-start.13 = (bf16[256,768]{1,0:T(8,128)(2,1)S(1)}, bf16[256,768]{1,0:T(8,128)(2,1)S(1)}, u32[]{:S(2)}, u32[]{:S(2)}) collective-permute-start(bf16[256,768]{1,0:T(8,128)(2,1)S(1)} %convolution_convert_fusion.3), channel_id=1, source_target_pairs={{0,8},{4,12},{8,0},{12,4},{16,24},{20,28},{24,16},{28,20},{1,9},{5... | collective-permute-start | bytes 1179656 | tf_op jit(solution)/shard_map/ppermute | solution.py:108
  36.4 12.3 %collective-permute-start.14 = (bf16[256,768]{1,0:T(8,128)(2,1)S(1)}, bf16[256,768]{1,0:T(8,128)(2,1)S(1)}, u32[]{:S(2)}, u32[]{:S(2)}) collective-permute-start(bf16[256,768]{1,0:T(8,128)(2,1)S(1)} %convolution_convert_fusion.2), channel_id=1, source_target_pairs={{8,16},{12,20},{16,8},{20,12},{9,17},{13,21},{17,9},{21,13},{10,18... | collective-permute-start | bytes 1179656 | tf_op jit(solution)/shard_map/ppermute | solution.py:108
  37.1 5.4 %collective-permute-start.8 = (bf16[64,1280]{1,0:T(8,128)(2,1)S(1)}, bf16[64,1280]{1,0:T(8,128)(2,1)S(1)}, u32[]{:S(2)}, u32[]{:S(2)}) collective-permute-start(bf16[64,1280]{1,0:T(8,128)(2,1)S(1)} %pad_maximum_fusion.13), channel_id=1, source_target_pairs={{0,2},{1,3},{2,0},{3,1},{4,6},{5,7},{6,4},{7,5},{8,10},{9,11},{10,... | collective-permute-start | bytes 491528 | tf_op jit(solution)/shard_map/ppermute | solution.py:77
  38.6 3.9 %collective-permute-start.12 = (bf16[128,1280]{1,0:T(8,128)(2,1)S(1)}, bf16[128,1280]{1,0:T(8,128)(2,1)S(1)}, u32[]{:S(2)}, u32[]{:S(2)}) collective-permute-start(bf16[128,1280]{1,0:T(8,128)(2,1)S(1)} %pad_maximum_fusion.11), channel_id=1, source_target_pairs={{0,1},{1,0},{2,3},{3,2},{4,5},{5,4},{6,7},{7,6},{8,9},{9,8},{10,11... | collective-permute-start | bytes 983048 | tf_op jit(solution)/shard_map/ppermute | solution.py:77
  42.5 6.1 %collective-permute-start.9 = (bf16[128,1280]{1,0:T(8,128)(2,1)S(1)}, bf16[128,1280]{1,0:T(8,128)(2,1)S(1)}, u32[]{:S(2)}, u32[]{:S(2)}) collective-permute-start(bf16[128,1280]{1,0:T(8,128)(2,1)S(1)} %pad_maximum_fusion.10), channel_id=1, source_target_pairs={{0,1},{1,0},{2,3},{3,2},{4,5},{5,4},{6,7},{7,6},{8,9},{9,8},{10,11... | collective-permute-start | bytes 983048 | tf_op jit(solution)/shard_map/ppermute | solution.py:77
  44.4 13.4 %collective-permute-start.15 = (bf16[256,768]{1,0:T(8,128)(2,1)S(1)}, bf16[256,768]{1,0:T(8,128)(2,1)S(1)}, u32[]{:S(2)}, u32[]{:S(2)}) collective-permute-start(bf16[256,768]{1,0:T(8,128)(2,1)S(1)} %convert_element_type.88), channel_id=1, source_target_pairs={{0,16},{4,20},{24,8},{28,12},{1,17},{5,21},{25,9},{29,13},{2,18},{... | collective-permute-start | bytes 1179656 | tf_op jit(solution)/shard_map/ppermute | solution.py:108
  48.5 18.6 %collective-permute-start.18 = (bf16[256,768]{1,0:T(8,128)(2,1)S(1)}, bf16[256,768]{1,0:T(8,128)(2,1)S(1)}, u32[]{:S(2)}, u32[]{:S(2)}) collective-permute-start(bf16[256,768]{1,0:T(8,128)(2,1)S(1)} %fusion.18), channel_id=1, source_target_pairs={{16,0},{20,4},{24,16},{28,20},{8,24},{12,28},{0,8},{4,12},{17,1},{... | collective-permute-start | bytes 1179656 | tf_op jit(solution)/shard_map/ppermute | solution.py:108
  69.7 11.6 %collective-permute-start.21 = (bf16[256,768]{1,0:T(8,128)(2,1)S(1)}, bf16[256,768]{1,0:T(8,128)(2,1)S(1)}, u32[]{:S(2)}, u32[]{:S(2)}) collective-permute-start(bf16[256,768]{1,0:T(8,128)(2,1)S(1)} %get-tuple-element.45), channel_id=1, source_target_pairs={{0,16},{4,20},{16,24},{20,28},{24,8},{28,12},{8,0},{12,4},{1,17},{... | collective-permute-start | bytes 1179656 | tf_op jit(solution)/shard_map/ppermute | solution.py:108
  70.3 20.9 %collective-permute-start.22 = (bf16[256,768]{1,0:T(8,128)(2,1)S(1)}, bf16[256,768]{1,0:T(8,128)(2,1)S(1)}, u32[]{:S(2)}, u32[]{:S(2)}) collective-permute-start(bf16[256,768]{1,0:T(8,128)(2,1)S(1)} %get-tuple-element.45), channel_id=1, source_target_pairs={{16,0},{20,4},{8,24},{12,28},{17,1},{21,5},{9,25},{13,29},{18,2},{... | collective-permute-start | bytes 1179656 | tf_op jit(solution)/shard_map/ppermute | solution.py:108
  71.6 21.3 %collective-permute-start.23 = (bf16[256,768]{1,0:T(8,128)(2,1)S(1)}, bf16[256,768]{1,0:T(8,128)(2,1)S(1)}, u32[]{:S(2)}, u32[]{:S(2)}) collective-permute-start(bf16[256,768]{1,0:T(8,128)(2,1)S(1)} %get-tuple-element.45), channel_id=1, source_target_pairs={{8,16},{12,20},{16,8},{20,12},{9,17},{13,21},{17,9},{21,13},{10,18... | collective-permute-start | bytes 1179656 | tf_op jit(solution)/shard_map/ppermute | solution.py:108
  72.6 20.4 %collective-permute-start.20 = (bf16[64,1280]{1,0:T(8,128)(2,1)S(1)}, bf16[64,1280]{1,0:T(8,128)(2,1)S(1)}, u32[]{:S(2)}, u32[]{:S(2)}) collective-permute-start(bf16[64,1280]{1,0:T(8,128)(2,1)S(1)} %slice.249), channel_id=1, source_target_pairs={{0,2},{1,3},{2,0},{3,1},{4,6},{5,7},{6,4},{7,5},{8,10},{9,11},{10,... | collective-permute-start | bytes 491528 | tf_op jit(solution)/shard_map/ppermute | solution.py:77
  81.4 18.2 %collective-permute-start.24 = (bf16[256,768]{1,0:T(8,128)(2,1)S(1)}, bf16[256,768]{1,0:T(8,128)(2,1)S(1)}, u32[]{:S(2)}, u32[]{:S(2)}) collective-permute-start(bf16[256,768]{1,0:T(8,128)(2,1)S(1)} %broadcast_select_fusion.2), channel_id=1, source_target_pairs={{0,8},{4,12},{8,0},{12,4},{16,24},{20,28},{24,16},{28,20},{1,9},{5... | collective-permute-start | bytes 1179656 | tf_op jit(solution)/shard_map/ppermute | solution.py:108
  92.8 9.2 %collective-permute-start.27 = (bf16[128,1280]{1,0:T(8,128)(2,1)S(1)}, bf16[128,1280]{1,0:T(8,128)(2,1)S(1)}, u32[]{:S(2)}, u32[]{:S(2)}) collective-permute-start(bf16[128,1280]{1,0:T(8,128)(2,1)S(1)} %slice.242), channel_id=1, source_target_pairs={{0,1},{1,0},{2,3},{3,2},{4,5},{5,4},{6,7},{7,6},{8,9},{9,8},{10,11... | collective-permute-start | bytes 983048 | tf_op jit(solution)/shard_map/ppermute | solution.py:77
  101.9 4.6 %collective-permute-start.25 = (bf16[256,1280]{1,0:T(8,128)(2,1)S(1)}, bf16[256,1280]{1,0:T(8,128)(2,1)S(1)}, u32[]{:S(2)}, u32[]{:S(2)}) collective-permute-start(bf16[256,1280]{1,0:T(8,128)(2,1)S(1)} %pad_maximum_fusion.7), channel_id=1, source_target_pairs={{0,1},{1,0},{2,3},{3,2},{4,5},{5,4},{6,7},{7,6},{8,9},{9,8},{10,11... | collective-permute-start | bytes 1966088 | tf_op jit(solution)/shard_map/ppermute | solution.py:77
  102.1 6.7 %collective-permute-start.28 = (bf16[64,1280]{1,0:T(8,128)(2,1)S(1)}, bf16[64,1280]{1,0:T(8,128)(2,1)S(1)}, u32[]{:S(2)}, u32[]{:S(2)}) collective-permute-start(bf16[64,1280]{1,0:T(8,128)(2,1)S(1)} %slice.246), channel_id=1, source_target_pairs={{0,2},{1,3},{2,0},{3,1},{4,6},{5,7},{6,4},{7,5},{8,10},{9,11},{10,... | collective-permute-start | bytes 491528 | tf_op jit(solution)/shard_map/ppermute | solution.py:77
  103.7 29.0 %collective-permute-start.32 = (bf16[640,768]{1,0:T(8,128)(2,1)S(1)}, bf16[640,768]{1,0:T(8,128)(2,1)S(1)}, u32[]{:S(2)}, u32[]{:S(2)}) collective-permute-start(bf16[640,768]{1,0:T(8,128)(2,1)S(1)} %add_convert_fusion), channel_id=1, source_target_pairs={{0,4},{4,0},{8,12},{12,8},{16,20},{20,16},{24,28},{28,24},{1,5},{5... | collective-permute-start | bytes 2949128 | tf_op jit(solution)/shard_map/ppermute | solution.py:73
  106.8 9.6 %collective-permute-start.26 = (bf16[128,1280]{1,0:T(8,128)(2,1)S(1)}, bf16[128,1280]{1,0:T(8,128)(2,1)S(1)}, u32[]{:S(2)}, u32[]{:S(2)}) collective-permute-start(bf16[128,1280]{1,0:T(8,128)(2,1)S(1)} %pad_maximum_fusion.12), channel_id=1, source_target_pairs={{0,2},{1,3},{2,0},{3,1},{4,6},{5,7},{6,4},{7,5},{8,10},{9,11},{10,... | collective-permute-start | bytes 983048 | tf_op jit(solution)/shard_map/ppermute | solution.py:77
  108.8 10.3 %collective-permute-start.29 = (bf16[64,1280]{1,0:T(8,128)(2,1)S(1)}, bf16[64,1280]{1,0:T(8,128)(2,1)S(1)}, u32[]{:S(2)}, u32[]{:S(2)}) collective-permute-start(bf16[64,1280]{1,0:T(8,128)(2,1)S(1)} %fusion.19), channel_id=1, source_target_pairs={{0,16},{4,20},{8,24},{12,28},{16,0},{20,4},{24,8},{28,12},{1,17},{... | collective-permute-start | bytes 491528 | tf_op jit(solution)/shard_map/ppermute | solution.py:69
  119.1 9.5 %collective-permute-start.30 = (bf16[64,1280]{1,0:T(8,128)(2,1)S(1)}, bf16[64,1280]{1,0:T(8,128)(2,1)S(1)}, u32[]{:S(2)}, u32[]{:S(2)}) collective-permute-start(bf16[64,1280]{1,0:T(8,128)(2,1)S(1)} %broadcast_select_fusion.4), channel_id=1, source_target_pairs={{0,8},{4,12},{8,0},{12,4},{16,24},{20,28},{24,16},{28,20},{1,9},{5... | collective-permute-start | bytes 491528 | tf_op jit(solution)/shard_map/ppermute | solution.py:69
  119.1 9.2 %collective-permute-start.31 = (bf16[64,1280]{1,0:T(8,128)(2,1)S(1)}, bf16[64,1280]{1,0:T(8,128)(2,1)S(1)}, u32[]{:S(2)}, u32[]{:S(2)}) collective-permute-start(bf16[64,1280]{1,0:T(8,128)(2,1)S(1)} %get-tuple-element.58), channel_id=1, source_target_pairs={{0,24},{4,28},{8,16},{12,20},{16,8},{20,12},{24,0},{28,4},{1,25},{... | collective-permute-start | bytes 491528 | tf_op jit(solution)/shard_map/ppermute | solution.py:69
  (7 other events, 77.4 us)

commit v22 on v19

--- a/solution.py
+++ b/solution.py
@@ -144,7 +144,9 @@
         got = {k: over_outer(pieces[k], k) for k in far_first}
         if relay:
             got[3], got[1] = pick(got[3], got[1]), pick(got[1], got[3])
-        got[0] = pieces[0]
+        got[0] = jnp.concatenate(
+            [pieces[0], jnp.broadcast_to(gate_probs[:, None], (cap, 128))], axis=1
+        )
 
         x_chunks = {}
 
@@ -160,7 +162,8 @@
             near = after(multiply(1, far).astype(BF16), far)
             crossed = outer_pairs(near, middle)
             x_chunks[2] = gather_etp(got[2], [[], [near]])
-            x_chunks[0] = gather_etp(after(got[0], near))
+            joined = gather_etp(after(got[0], near))
+            x_chunks[0], probs = joined[:, :span], joined[:, span : span + 1]
             two = after(multiply(2, swapped), swapped)
             inwards = outer_pairs(two.astype(BF16), inward)
             relayed = pick(near, (after(two, swapped) + swapped.astype(F32)).astype(BF16))
@@ -171,15 +174,15 @@
             last = relayed
         else:
             last, parts = rows, []
-            x_chunks[0] = gather_etp(got[0])
+            joined = gather_etp(got[0])
+            x_chunks[0], probs = joined[:, :span], joined[:, span : span + 1]
             for k in far_first:
                 x_chunks[k] = gather_etp(got[k], [[last]])
                 last = multiply(k).astype(BF16)
                 parts.append(over_outer(last, k))
             own = multiply(0, last)
-        probs = gather_etp(after(gate_probs, rows))
         order = etp ^ jnp.array(chunk_order, jnp.int32)
-        hidden, paired = gate_call(order, own, probs[:, None], d_hidden, parts)
+        hidden, paired = gate_call(order, own, probs, d_hidden, parts)
 
         grads, sums = {0: paired}, {}
 

time: 133 us -> 134 us (level)
  waiting for transfers between devices: 76.6 us -> 78.2 us
    ppermute x6, waiting for transfers between devices: 7.57 us -> 10.7 us  [over_outer(): return lax.ppermute(value, 'dp', pairs)]
    ppermute x16 -> x14, starting transfers between devices: 11 us -> 9.42 us  [over_etp(): return lax.ppermute(value, 'etp', pairs)]
    ppermute x16 -> x14, waiting for transfers between devices: 20.5 us -> 19.1 us  [over_etp(): return lax.ppermute(value, 'etp', pairs)]
  transfers between devices with their start and end apart: 33 -> 31, of which waited for: 18 -> 18; matrix products, arithmetic and copies ran while one was open for 9% -> 8% of each run, Pallas kernels for 0% -> 0%
where the time goes in v22:
time: 134 us
  waiting for transfers between devices  78.2 us (58%)
  starting transfers between devices  32.6 us (24%)
  matrix products  15.8 us (12%)
  other arithmetic  2.99 us (2%)
  Pallas kernels  1.51 us (1%)
  between operations  1.38 us (1%)
    ppermute x8, waiting for transfers between devices, outer_pairs(): return lax.ppermute(value, 'dp', pairs)  39.9 us
    ppermute x14, waiting for transfers between devices, over_etp(): return lax.ppermute(value, 'etp', pairs)  19.1 us
    ppermute x8, starting transfers between devices, outer_pairs(): return lax.ppermute(value, 'dp', pairs)  11.6 us
    ppermute x6, waiting for transfers between devices, over_outer(): return lax.ppermute(value, 'dp', pairs)  10.7 us
    ppermute x14, starting transfers between devices, over_etp(): return lax.ppermute(value, 'etp', pairs)  9.42 us
    ppermute x3, waiting for transfers between devices, over_inner(): return lax.ppermute(value, 'dp', pairs)  8.47 us
    ppermute x6, starting transfers between devices, over_outer(): return lax.ppermute(value, 'dp', pairs)  7.96 us
    dot_general x1, matrix products, shards(): lax.dot_general(onehot, dx, (((0,), (0,)), ((), ())), preferred_element_t...  3.99 us
  transfers between devices with their start and end apart: 31, of which 18 were waited for; matrix products, arithmetic and copies ran while one was open for 8% of the time, Pallas kernels for 0%

profile of v22, /device:TPU:0, one launch (start us, length us, event | category | flops | bytes accessed | tf_op | source)
XLA Modules:
  0.0 133.5 jit_solution(15495035826605518978)
XLA Ops:
  0.7 3.6 %convolution_convert_fusion.1 = bf16[64,5120]{1,0:T(8,128)(2,1)S(1)} fusion(bf16[512,5120]{1,0:T(8,128)(2,1)} %param.7, s32[64]{0:T(128)} %param.8), kind=kOutput, calls=%fused_computation.1 | convolution fusion | flops 335904768 | bytes 5898496 | tf_op jit(solution)/shard_map/dot_general | solution.py:136
  4.5 5.1 %collective-permute-start.1 = (bf16[64,1280]{1,0:T(8,128)(2,1)S(1)}, bf16[64,1280]{1,0:T(8,128)(2,1)S(1)}, u32[]{:S(2)}, u32[]{:S(2)}) collective-permute-start(bf16[64,1280]{1,0:T(8,128)(2,1)S(1)} %pad_maximum_fusion.14), channel_id=1, source_target_pairs={{0,24},{4,28},{8,16},{12,20},{16,8},{20,12},{24,0},{28,4},{1,25},{... | collective-permute-start | bytes 491528 | tf_op jit(solution)/shard_map/ppermute | solution.py:69
  9.7 1.6 %collective-permute-start.7 = (bf16[640,384]{1,0:T(8,128)(2,1)S(1)}, bf16[640,384]{1,0:T(8,128)(2,1)S(1)}, u32[]{:S(2)}, u32[]{:S(2)}) collective-permute-start(bf16[640,384]{1,0:T(8,128)(2,1)S(1)} %copy-done.1), channel_id=1, source_target_pairs={{0,4},{4,0},{8,12},{12,8},{16,20},{20,16},{24,28},{28,24},{1,5},{5... | collective-permute-start | bytes 1474568 | tf_op jit(solution)/shard_map/ppermute | solution.py:73
  12.5 2.2 %collective-permute-done.1 = bf16[64,1280]{1,0:T(8,128)(2,1)S(1)} collective-permute-done((bf16[64,1280]{1,0:T(8,128)(2,1)S(1)}, bf16[64,1280]{1,0:T(8,128)(2,1)S(1)}, u32[]{:S(2)}, u32[]{:S(2)}) %collective-permute-start.1) | collective-permute-done | bytes 163872 | tf_op jit(solution)/shard_map/ppermute | solution.py:69
  14.7 3.7 %collective-permute-done = bf16[64,1280]{1,0:T(8,128)(2,1)S(1)} collective-permute-done((bf16[64,1280]{1,0:T(8,128)(2,1)S(1)}, bf16[64,1280]{1,0:T(8,128)(2,1)S(1)}, u32[]{:S(2)}, u32[]{:S(2)}) %collective-permute-start) | collective-permute-done | bytes 163872 | tf_op jit(solution)/shard_map/ppermute | solution.py:69
  18.4 1.5 %collective-permute-start.2 = (bf16[64,1280]{1,0:T(8,128)(2,1)S(1)}, bf16[64,1280]{1,0:T(8,128)(2,1)S(1)}, u32[]{:S(2)}, u32[]{:S(2)}) collective-permute-start(bf16[64,1280]{1,0:T(8,128)(2,1)S(1)} %get-tuple-element.77), channel_id=1, source_target_pairs={{0,2},{1,3},{2,0},{3,1},{4,6},{5,7},{6,4},{7,5},{8,10},{9,11},{10,... | collective-permute-start | bytes 491528 | tf_op jit(solution)/shard_map/ppermute | solution.py:77
  20.5 3.0 %collective-permute-done.10 = bf16[64,1280]{1,0:T(8,128)(2,1)S(1)} collective-permute-done((bf16[64,1280]{1,0:T(8,128)(2,1)S(1)}, bf16[64,1280]{1,0:T(8,128)(2,1)S(1)}, u32[]{:S(2)}, u32[]{:S(2)}) %collective-permute-start.10) | collective-permute-done | bytes 163872 | tf_op jit(solution)/shard_map/ppermute | solution.py:69
  23.5 1.5 %collective-permute-start.11 = (bf16[64,1280]{1,0:T(8,128)(2,1)S(1)}, bf16[64,1280]{1,0:T(8,128)(2,1)S(1)}, u32[]{:S(2)}, u32[]{:S(2)}) collective-permute-start(bf16[64,1280]{1,0:T(8,128)(2,1)S(1)} %collective-permute-done.10), channel_id=1, source_target_pairs={{0,2},{1,3},{2,0},{3,1},{4,6},{5,7},{6,4},{7,5},{8,10},{9,11},{10,... | collective-permute-start | bytes 491528 | tf_op jit(solution)/shard_map/ppermute | solution.py:77
  25.7 3.4 %collective-permute-done.4 = bf16[64,1280]{1,0:T(8,128)(2,1)S(1)} collective-permute-done((bf16[64,1280]{1,0:T(8,128)(2,1)S(1)}, bf16[64,1280]{1,0:T(8,128)(2,1)S(1)}, u32[]{:S(2)}, u32[]{:S(2)}) %collective-permute-start.4) | collective-permute-done | bytes 163872 | tf_op jit(solution)/shard_map/ppermute | solution.py:77
  29.2 2.4 %collective-permute-done.11 = bf16[64,1280]{1,0:T(8,128)(2,1)S(1)} collective-permute-done((bf16[64,1280]{1,0:T(8,128)(2,1)S(1)}, bf16[64,1280]{1,0:T(8,128)(2,1)S(1)}, u32[]{:S(2)}, u32[]{:S(2)}) %collective-permute-start.11) | collective-permute-done | bytes 163872 | tf_op jit(solution)/shard_map/ppermute | solution.py:77
  31.7 1.3 collective-permute-done.6
  33.9 1.7 %collective-permute-start.13 = (bf16[256,768]{1,0:T(8,128)(2,1)S(1)}, bf16[256,768]{1,0:T(8,128)(2,1)S(1)}, u32[]{:S(2)}, u32[]{:S(2)}) collective-permute-start(bf16[256,768]{1,0:T(8,128)(2,1)S(1)} %convolution_convert_fusion.3), channel_id=1, source_target_pairs={{0,8},{4,12},{8,0},{12,4},{16,24},{20,28},{24,16},{28,20},{1,9},{5... | collective-permute-start | bytes 1179656 | tf_op jit(solution)/shard_map/ppermute | solution.py:108
  37.1 1.6 %collective-permute-start.8 = (bf16[64,1408]{1,0:T(8,128)(2,1)S(1)}, bf16[64,1408]{1,0:T(8,128)(2,1)S(1)}, u32[]{:S(2)}, u32[]{:S(2)}) collective-permute-start(bf16[64,1408]{1,0:T(8,128)(2,1)S(1)} %pad_maximum_fusion.12), channel_id=1, source_target_pairs={{0,2},{1,3},{2,0},{3,1},{4,6},{5,7},{6,4},{7,5},{8,10},{9,11},{10,... | collective-permute-start | bytes 540680 | tf_op jit(solution)/shard_map/ppermute | solution.py:77
  38.7 4.0 %collective-permute-done.8 = bf16[64,1408]{1,0:T(8,128)(2,1)S(1)} collective-permute-done((bf16[64,1408]{1,0:T(8,128)(2,1)S(1)}, bf16[64,1408]{1,0:T(8,128)(2,1)S(1)}, u32[]{:S(2)}, u32[]{:S(2)}) %collective-permute-start.8) | collective-permute-done | bytes 180256 | tf_op jit(solution)/shard_map/ppermute | solution.py:77
  44.4 4.2 %collective-permute-start.15 = (bf16[256,768]{1,0:T(8,128)(2,1)S(1)}, bf16[256,768]{1,0:T(8,128)(2,1)S(1)}, u32[]{:S(2)}, u32[]{:S(2)}) collective-permute-start(bf16[256,768]{1,0:T(8,128)(2,1)S(1)} %convert_element_type.88), channel_id=1, source_target_pairs={{0,16},{4,20},{24,8},{28,12},{1,17},{5,21},{25,9},{29,13},{2,18},{... | collective-permute-start | bytes 1179656 | tf_op jit(solution)/shard_map/ppermute | solution.py:108
  48.9 9.1 %collective-permute-done.15 = bf16[256,768]{1,0:T(8,128)(2,1)S(1)} collective-permute-done((bf16[256,768]{1,0:T(8,128)(2,1)S(1)}, bf16[256,768]{1,0:T(8,128)(2,1)S(1)}, u32[]{:S(2)}, u32[]{:S(2)}) %collective-permute-start.15) | collective-permute-done | bytes 393248 | tf_op jit(solution)/shard_map/ppermute | solution.py:108
  58.8 8.6 %collective-permute-done.16.refs_0_ = bf16[256,768]{1,0:T(8,128)(2,1)S(1)} collective-permute-done((bf16[256,768]{1,0:T(8,128)(2,1)S(1)}, bf16[256,768]{1,0:T(8,128)(2,1)S(1)}, u32[]{:S(2)}, u32[]{:S(2)}) %collective-permute-start.16) | collective-permute-done | bytes 393248 | tf_op jit(solution)/shard_map/ppermute | solution.py:108
  67.4 1.5 %shard_map.102 = (bf16[256,384]{1,0:T(8,128)(2,1)}, bf16[256,768]{1,0:T(8,128)(2,1)S(1)}) custom-call(s32[4]{0:T(128)S(1)} %broadcast_xor_fusion.order_ref, f32[256,768]{1,0:T(8,128)S(1)} %fusion.9.pre_ref, bf16[256,1]{1,0:T(8,128)(2,1)S(1)} %slice.177.prob_ref, bf16[256,384]{1,0:T(8,128)(2,1)S(1)} %copy-done, ...), custom_call_target="tpu_custom_call" | custom-call | flops 1966080 | bytes 2949120 | tf_op jit(solution)/shard_map/pallas_call | solution.py:49
  70.6 1.3 collective-permute-start.20
  72.9 1.6 %collective-permute-start.18 = (bf16[64,1280]{1,0:T(8,128)(2,1)S(1)}, bf16[64,1280]{1,0:T(8,128)(2,1)S(1)}, u32[]{:S(2)}, u32[]{:S(2)}) collective-permute-start(bf16[64,1280]{1,0:T(8,128)(2,1)S(1)} %slice.261), channel_id=1, source_target_pairs={{0,2},{1,3},{2,0},{3,1},{4,6},{5,7},{6,4},{7,5},{8,10},{9,11},{10,... | collective-permute-start | bytes 491528 | tf_op jit(solution)/shard_map/ppermute | solution.py:77
  74.5 7.1 %collective-permute-done.19 = bf16[256,768]{1,0:T(8,128)(2,1)S(1)} collective-permute-done((bf16[256,768]{1,0:T(8,128)(2,1)S(1)}, bf16[256,768]{1,0:T(8,128)(2,1)S(1)}, u32[]{:S(2)}, u32[]{:S(2)}) %collective-permute-start.19) | collective-permute-done | bytes 393248 | tf_op jit(solution)/shard_map/ppermute | solution.py:108
  81.6 2.1 %collective-permute-start.22 = (bf16[256,768]{1,0:T(8,128)(2,1)S(1)}, bf16[256,768]{1,0:T(8,128)(2,1)S(1)}, u32[]{:S(2)}, u32[]{:S(2)}) collective-permute-start(bf16[256,768]{1,0:T(8,128)(2,1)S(1)} %broadcast_select_fusion.2), channel_id=1, source_target_pairs={{0,8},{4,12},{8,0},{12,4},{16,24},{20,28},{24,16},{28,20},{1,9},{5... | collective-permute-start | bytes 1179656 | tf_op jit(solution)/shard_map/ppermute | solution.py:108
  83.8 7.8 %collective-permute-done.20 = bf16[256,768]{1,0:T(8,128)(2,1)S(1)} collective-permute-done((bf16[256,768]{1,0:T(8,128)(2,1)S(1)}, bf16[256,768]{1,0:T(8,128)(2,1)S(1)}, u32[]{:S(2)}, u32[]{:S(2)}) %collective-permute-start.20) | collective-permute-done | bytes 393248 | tf_op jit(solution)/shard_map/ppermute | solution.py:108
  93.3 6.5 %collective-permute-done.22 = bf16[256,768]{1,0:T(8,128)(2,1)S(1)} collective-permute-done((bf16[256,768]{1,0:T(8,128)(2,1)S(1)}, bf16[256,768]{1,0:T(8,128)(2,1)S(1)}, u32[]{:S(2)}, u32[]{:S(2)}) %collective-permute-start.22) | collective-permute-done | bytes 393248 | tf_op jit(solution)/shard_map/ppermute | solution.py:108
  102.4 1.6 %collective-permute-start.27 = (bf16[64,1280]{1,0:T(8,128)(2,1)S(1)}, bf16[64,1280]{1,0:T(8,128)(2,1)S(1)}, u32[]{:S(2)}, u32[]{:S(2)}) collective-permute-start(bf16[64,1280]{1,0:T(8,128)(2,1)S(1)} %slice.258), channel_id=1, source_target_pairs={{0,2},{1,3},{2,0},{3,1},{4,6},{5,7},{6,4},{7,5},{8,10},{9,11},{10,... | collective-permute-start | bytes 491528 | tf_op jit(solution)/shard_map/ppermute | solution.py:77
  104.0 1.5 %collective-permute-start.30 = (bf16[640,768]{1,0:T(8,128)(2,1)S(1)}, bf16[640,768]{1,0:T(8,128)(2,1)S(1)}, u32[]{:S(2)}, u32[]{:S(2)}) collective-permute-start(bf16[640,768]{1,0:T(8,128)(2,1)S(1)} %add_convert_fusion), channel_id=1, source_target_pairs={{0,4},{4,0},{8,12},{12,8},{16,20},{20,16},{24,28},{28,24},{1,5},{5... | collective-permute-start | bytes 2949128 | tf_op jit(solution)/shard_map/ppermute | solution.py:73
  107.6 1.4 %collective-permute-done.27 = bf16[64,1280]{1,0:T(8,128)(2,1)S(1)} collective-permute-done((bf16[64,1280]{1,0:T(8,128)(2,1)S(1)}, bf16[64,1280]{1,0:T(8,128)(2,1)S(1)}, u32[]{:S(2)}, u32[]{:S(2)}) %collective-permute-start.27) | collective-permute-done | bytes 163872 | tf_op jit(solution)/shard_map/ppermute | solution.py:77
  109.3 7.3 %collective-permute-done.24 = bf16[128,1280]{1,0:T(8,128)(2,1)S(1)} collective-permute-done((bf16[128,1280]{1,0:T(8,128)(2,1)S(1)}, bf16[128,1280]{1,0:T(8,128)(2,1)S(1)}, u32[]{:S(2)}, u32[]{:S(2)}) %collective-permute-start.24) | collective-permute-done | bytes 327712 | tf_op jit(solution)/shard_map/ppermute | solution.py:77
  117.6 1.9 %collective-permute-done.28 = bf16[64,1280]{1,0:T(8,128)(2,1)S(1)} collective-permute-done((bf16[64,1280]{1,0:T(8,128)(2,1)S(1)}, bf16[64,1280]{1,0:T(8,128)(2,1)S(1)}, u32[]{:S(2)}, u32[]{:S(2)}) %collective-permute-start.28) | collective-permute-done | bytes 163872 | tf_op jit(solution)/shard_map/ppermute | solution.py:69
  120.7 7.1 %collective-permute-done.30 = bf16[640,768]{1,0:T(8,128)(2,1)S(1)} collective-permute-done((bf16[640,768]{1,0:T(8,128)(2,1)S(1)}, bf16[640,768]{1,0:T(8,128)(2,1)S(1)}, u32[]{:S(2)}, u32[]{:S(2)}) %collective-permute-start.30) | collective-permute-done | bytes 983072 | tf_op jit(solution)/shard_map/ppermute | solution.py:73
  127.9 1.5 %slice_add_fusion = (f32[640,384]{1,0:T(8,128)}, f32[640,384]{1,0:T(8,128)}) fusion(f32[640,768]{1,0:T(8,128)S(1)} %fusion, bf16[640,768]{1,0:T(8,128)(2,1)S(1)} %collective-permute-done.30), kind=kLoop, calls=%fused_computation.18 | loop fusion | flops 983040 | bytes 4915200 | tf_op jit(solution)/shard_map/add | solution.py:241
  129.5 4.0 %convolution_convert_fusion = bf16[512,5120]{1,0:T(8,128)(2,1)} fusion(bf16[64,5120]{1,0:T(8,128)(2,1)S(1)} %slice_dynamic-update-slice_fusion.2, s32[64]{0:T(128)S(1)} %copy-done.3), kind=kOutput, calls=%fused_computation | convolution fusion | flops 338198528 | bytes 5898496 | tf_op jit(solution)/shard_map/dot_general | solution.py:254
  (115 shorter events, 19.4 us)
Async XLA Ops:
  4.5 10.2 %collective-permute-start.1 = (bf16[64,1280]{1,0:T(8,128)(2,1)S(1)}, bf16[64,1280]{1,0:T(8,128)(2,1)S(1)}, u32[]{:S(2)}, u32[]{:S(2)}) collective-permute-start(bf16[64,1280]{1,0:T(8,128)(2,1)S(1)} %pad_maximum_fusion.14), channel_id=1, source_target_pairs={{0,24},{4,28},{8,16},{12,20},{16,8},{20,12},{24,0},{28,4},{1,25},{... | collective-permute-start | bytes 491528 | tf_op jit(solution)/shard_map/ppermute | solution.py:69
  9.6 8.8 %collective-permute-start = (bf16[64,1280]{1,0:T(8,128)(2,1)S(1)}, bf16[64,1280]{1,0:T(8,128)(2,1)S(1)}, u32[]{:S(2)}, u32[]{:S(2)}) collective-permute-start(bf16[64,1280]{1,0:T(8,128)(2,1)S(1)} %pad_maximum_fusion.13), channel_id=1, source_target_pairs={{0,8},{4,12},{8,0},{12,4},{16,24},{20,28},{24,16},{28,20},{1,9},{5... | collective-permute-start | bytes 491528 | tf_op jit(solution)/shard_map/ppermute | solution.py:69
  9.7 21.9 %collective-permute-start.7 = (bf16[640,384]{1,0:T(8,128)(2,1)S(1)}, bf16[640,384]{1,0:T(8,128)(2,1)S(1)}, u32[]{:S(2)}, u32[]{:S(2)}) collective-permute-start(bf16[640,384]{1,0:T(8,128)(2,1)S(1)} %copy-done.1), channel_id=1, source_target_pairs={{0,4},{4,0},{8,12},{12,8},{16,20},{20,16},{24,28},{28,24},{1,5},{5... | collective-permute-start | bytes 1474568 | tf_op jit(solution)/shard_map/ppermute | solution.py:73
  11.3 21.7 %collective-permute-start.6 = (bf16[640,384]{1,0:T(8,128)(2,1)S(1)}, bf16[640,384]{1,0:T(8,128)(2,1)S(1)}, u32[]{:S(2)}, u32[]{:S(2)}) collective-permute-start(bf16[640,384]{1,0:T(8,128)(2,1)S(1)} %copy-done.2), channel_id=1, source_target_pairs={{0,4},{4,0},{8,12},{12,8},{16,20},{20,16},{24,28},{28,24},{1,5},{5... | collective-permute-start | bytes 1474568 | tf_op jit(solution)/shard_map/ppermute | solution.py:73
  11.8 11.7 %collective-permute-start.10 = (bf16[64,1280]{1,0:T(8,128)(2,1)S(1)}, bf16[64,1280]{1,0:T(8,128)(2,1)S(1)}, u32[]{:S(2)}, u32[]{:S(2)}) collective-permute-start(bf16[64,1280]{1,0:T(8,128)(2,1)S(1)} %pad_maximum_fusion.15), channel_id=1, source_target_pairs={{0,16},{4,20},{8,24},{12,28},{16,0},{20,4},{24,8},{28,12},{1,17},{... | collective-permute-start | bytes 491528 | tf_op jit(solution)/shard_map/ppermute | solution.py:69
  18.4 7.1 %collective-permute-start.2 = (bf16[64,1280]{1,0:T(8,128)(2,1)S(1)}, bf16[64,1280]{1,0:T(8,128)(2,1)S(1)}, u32[]{:S(2)}, u32[]{:S(2)}) collective-permute-start(bf16[64,1280]{1,0:T(8,128)(2,1)S(1)} %get-tuple-element.77), channel_id=1, source_target_pairs={{0,2},{1,3},{2,0},{3,1},{4,6},{5,7},{6,4},{7,5},{8,10},{9,11},{10,... | collective-permute-start | bytes 491528 | tf_op jit(solution)/shard_map/ppermute | solution.py:77
  20.0 9.1 %collective-permute-start.4 = (bf16[64,1280]{1,0:T(8,128)(2,1)S(1)}, bf16[64,1280]{1,0:T(8,128)(2,1)S(1)}, u32[]{:S(2)}, u32[]{:S(2)}) collective-permute-start(bf16[64,1280]{1,0:T(8,128)(2,1)S(1)} %get-tuple-element.76), channel_id=1, source_target_pairs={{0,2},{1,3},{2,0},{3,1},{4,6},{5,7},{6,4},{7,5},{8,10},{9,11},{10,... | collective-permute-start | bytes 491528 | tf_op jit(solution)/shard_map/ppermute | solution.py:77
  23.5 8.1 %collective-permute-start.11 = (bf16[64,1280]{1,0:T(8,128)(2,1)S(1)}, bf16[64,1280]{1,0:T(8,128)(2,1)S(1)}, u32[]{:S(2)}, u32[]{:S(2)}) collective-permute-start(bf16[64,1280]{1,0:T(8,128)(2,1)S(1)} %collective-permute-done.10), channel_id=1, source_target_pairs={{0,2},{1,3},{2,0},{3,1},{4,6},{5,7},{6,4},{7,5},{8,10},{9,11},{10,... | collective-permute-start | bytes 491528 | tf_op jit(solution)/shard_map/ppermute | solution.py:77
  25.6 10.0 %collective-permute-start.3 = (bf16[128,1280]{1,0:T(8,128)(2,1)S(1)}, bf16[128,1280]{1,0:T(8,128)(2,1)S(1)}, u32[]{:S(2)}, u32[]{:S(2)}) collective-permute-start(bf16[128,1280]{1,0:T(8,128)(2,1)S(1)} %pad_maximum_fusion.8), channel_id=1, source_target_pairs={{0,1},{1,0},{2,3},{3,2},{4,5},{5,4},{6,7},{7,6},{8,9},{9,8},{10,11... | collective-permute-start | bytes 983048 | tf_op jit(solution)/shard_map/ppermute | solution.py:77
  29.1 4.0 %collective-permute-start.5 = (bf16[128,1280]{1,0:T(8,128)(2,1)S(1)}, bf16[128,1280]{1,0:T(8,128)(2,1)S(1)}, u32[]{:S(2)}, u32[]{:S(2)}) collective-permute-start(bf16[128,1280]{1,0:T(8,128)(2,1)S(1)} %pad_maximum_fusion.9), channel_id=1, source_target_pairs={{0,1},{1,0},{2,3},{3,2},{4,5},{5,4},{6,7},{7,6},{8,9},{9,8},{10,11... | collective-permute-start | bytes 983048 | tf_op jit(solution)/shard_map/ppermute | solution.py:77
  33.9 9.7 %collective-permute-start.13 = (bf16[256,768]{1,0:T(8,128)(2,1)S(1)}, bf16[256,768]{1,0:T(8,128)(2,1)S(1)}, u32[]{:S(2)}, u32[]{:S(2)}) collective-permute-start(bf16[256,768]{1,0:T(8,128)(2,1)S(1)} %convolution_convert_fusion.3), channel_id=1, source_target_pairs={{0,8},{4,12},{8,0},{12,4},{16,24},{20,28},{24,16},{28,20},{1,9},{5... | collective-permute-start | bytes 1179656 | tf_op jit(solution)/shard_map/ppermute | solution.py:108
  36.4 12.5 %collective-permute-start.14 = (bf16[256,768]{1,0:T(8,128)(2,1)S(1)}, bf16[256,768]{1,0:T(8,128)(2,1)S(1)}, u32[]{:S(2)}, u32[]{:S(2)}) collective-permute-start(bf16[256,768]{1,0:T(8,128)(2,1)S(1)} %convolution_convert_fusion.2), channel_id=1, source_target_pairs={{8,16},{12,20},{16,8},{20,12},{9,17},{13,21},{17,9},{21,13},{10,18... | collective-permute-start | bytes 1179656 | tf_op jit(solution)/shard_map/ppermute | solution.py:108
  37.1 5.6 %collective-permute-start.8 = (bf16[64,1408]{1,0:T(8,128)(2,1)S(1)}, bf16[64,1408]{1,0:T(8,128)(2,1)S(1)}, u32[]{:S(2)}, u32[]{:S(2)}) collective-permute-start(bf16[64,1408]{1,0:T(8,128)(2,1)S(1)} %pad_maximum_fusion.12), channel_id=1, source_target_pairs={{0,2},{1,3},{2,0},{3,1},{4,6},{5,7},{6,4},{7,5},{8,10},{9,11},{10,... | collective-permute-start | bytes 540680 | tf_op jit(solution)/shard_map/ppermute | solution.py:77
  38.7 4.1 %collective-permute-start.12 = (bf16[128,1280]{1,0:T(8,128)(2,1)S(1)}, bf16[128,1280]{1,0:T(8,128)(2,1)S(1)}, u32[]{:S(2)}, u32[]{:S(2)}) collective-permute-start(bf16[128,1280]{1,0:T(8,128)(2,1)S(1)} %pad_maximum_fusion.10), channel_id=1, source_target_pairs={{0,1},{1,0},{2,3},{3,2},{4,5},{5,4},{6,7},{7,6},{8,9},{9,8},{10,11... | collective-permute-start | bytes 983048 | tf_op jit(solution)/shard_map/ppermute | solution.py:77
  42.7 6.1 %collective-permute-start.9 = (bf16[128,1408]{1,0:T(8,128)(2,1)S(1)}, bf16[128,1408]{1,0:T(8,128)(2,1)S(1)}, u32[]{:S(2)}, u32[]{:S(2)}) collective-permute-start(bf16[128,1408]{1,0:T(8,128)(2,1)S(1)} %pad_maximum_fusion.7), channel_id=1, source_target_pairs={{0,1},{1,0},{2,3},{3,2},{4,5},{5,4},{6,7},{7,6},{8,9},{9,8},{10,11... | collective-permute-start | bytes 1081352 | tf_op jit(solution)/shard_map/ppermute | solution.py:77
  44.4 13.7 %collective-permute-start.15 = (bf16[256,768]{1,0:T(8,128)(2,1)S(1)}, bf16[256,768]{1,0:T(8,128)(2,1)S(1)}, u32[]{:S(2)}, u32[]{:S(2)}) collective-permute-start(bf16[256,768]{1,0:T(8,128)(2,1)S(1)} %convert_element_type.88), channel_id=1, source_target_pairs={{0,16},{4,20},{24,8},{28,12},{1,17},{5,21},{25,9},{29,13},{2,18},{... | collective-permute-start | bytes 1179656 | tf_op jit(solution)/shard_map/ppermute | solution.py:108
  48.7 18.7 %collective-permute-start.16 = (bf16[256,768]{1,0:T(8,128)(2,1)S(1)}, bf16[256,768]{1,0:T(8,128)(2,1)S(1)}, u32[]{:S(2)}, u32[]{:S(2)}) collective-permute-start(bf16[256,768]{1,0:T(8,128)(2,1)S(1)} %fusion.18), channel_id=1, source_target_pairs={{16,0},{20,4},{24,16},{28,20},{8,24},{12,28},{0,8},{4,12},{17,1},{... | collective-permute-start | bytes 1179656 | tf_op jit(solution)/shard_map/ppermute | solution.py:108
  48.9 18.5 %copy-start = (bf16[256,384]{1,0:T(8,128)(2,1)S(1)}, bf16[256,384]{1,0:T(8,128)(2,1)}, u32[]{:S(2)}) copy-start(bf16[256,384]{1,0:T(8,128)(2,1)} %cot_ref.1) | copy-start | bytes 589828
  69.7 3.1 %collective-permute-start.17 = (bf16[128,1280]{1,0:T(8,128)(2,1)S(1)}, bf16[128,1280]{1,0:T(8,128)(2,1)S(1)}, u32[]{:S(2)}, u32[]{:S(2)}) collective-permute-start(bf16[128,1280]{1,0:T(8,128)(2,1)S(1)} %slice.257), channel_id=1, source_target_pairs={{0,1},{1,0},{2,3},{3,2},{4,5},{5,4},{6,7},{7,6},{8,9},{9,8},{10,11... | collective-permute-start | bytes 983048 | tf_op jit(solution)/shard_map/ppermute | solution.py:77
  70.0 11.6 %collective-permute-start.19 = (bf16[256,768]{1,0:T(8,128)(2,1)S(1)}, bf16[256,768]{1,0:T(8,128)(2,1)S(1)}, u32[]{:S(2)}, u32[]{:S(2)}) collective-permute-start(bf16[256,768]{1,0:T(8,128)(2,1)S(1)} %get-tuple-element.40), channel_id=1, source_target_pairs={{0,16},{4,20},{16,24},{20,28},{24,8},{28,12},{8,0},{12,4},{1,17},{... | collective-permute-start | bytes 1179656 | tf_op jit(solution)/shard_map/ppermute | solution.py:108
  70.6 20.9 %collective-permute-start.20 = (bf16[256,768]{1,0:T(8,128)(2,1)S(1)}, bf16[256,768]{1,0:T(8,128)(2,1)S(1)}, u32[]{:S(2)}, u32[]{:S(2)}) collective-permute-start(bf16[256,768]{1,0:T(8,128)(2,1)S(1)} %get-tuple-element.40), channel_id=1, source_target_pairs={{16,0},{20,4},{8,24},{12,28},{17,1},{21,5},{9,25},{13,29},{18,2},{... | collective-permute-start | bytes 1179656 | tf_op jit(solution)/shard_map/ppermute | solution.py:108
  71.9 21.3 %collective-permute-start.21 = (bf16[256,768]{1,0:T(8,128)(2,1)S(1)}, bf16[256,768]{1,0:T(8,128)(2,1)S(1)}, u32[]{:S(2)}, u32[]{:S(2)}) collective-permute-start(bf16[256,768]{1,0:T(8,128)(2,1)S(1)} %get-tuple-element.40), channel_id=1, source_target_pairs={{8,16},{12,20},{16,8},{20,12},{9,17},{13,21},{17,9},{21,13},{10,18... | collective-permute-start | bytes 1179656 | tf_op jit(solution)/shard_map/ppermute | solution.py:108
  72.9 20.4 %collective-permute-start.18 = (bf16[64,1280]{1,0:T(8,128)(2,1)S(1)}, bf16[64,1280]{1,0:T(8,128)(2,1)S(1)}, u32[]{:S(2)}, u32[]{:S(2)}) collective-permute-start(bf16[64,1280]{1,0:T(8,128)(2,1)S(1)} %slice.261), channel_id=1, source_target_pairs={{0,2},{1,3},{2,0},{3,1},{4,6},{5,7},{6,4},{7,5},{8,10},{9,11},{10,... | collective-permute-start | bytes 491528 | tf_op jit(solution)/shard_map/ppermute | solution.py:77
  81.6 18.2 %collective-permute-start.22 = (bf16[256,768]{1,0:T(8,128)(2,1)S(1)}, bf16[256,768]{1,0:T(8,128)(2,1)S(1)}, u32[]{:S(2)}, u32[]{:S(2)}) collective-permute-start(bf16[256,768]{1,0:T(8,128)(2,1)S(1)} %broadcast_select_fusion.2), channel_id=1, source_target_pairs={{0,8},{4,12},{8,0},{12,4},{16,24},{20,28},{24,16},{28,20},{1,9},{5... | collective-permute-start | bytes 1179656 | tf_op jit(solution)/shard_map/ppermute | solution.py:108
  93.1 9.2 %collective-permute-start.26 = (bf16[128,1280]{1,0:T(8,128)(2,1)S(1)}, bf16[128,1280]{1,0:T(8,128)(2,1)S(1)}, u32[]{:S(2)}, u32[]{:S(2)}) collective-permute-start(bf16[128,1280]{1,0:T(8,128)(2,1)S(1)} %slice.254), channel_id=1, source_target_pairs={{0,1},{1,0},{2,3},{3,2},{4,5},{5,4},{6,7},{7,6},{8,9},{9,8},{10,11... | collective-permute-start | bytes 983048 | tf_op jit(solution)/shard_map/ppermute | solution.py:77
  102.2 4.6 %collective-permute-start.23 = (bf16[256,1280]{1,0:T(8,128)(2,1)S(1)}, bf16[256,1280]{1,0:T(8,128)(2,1)S(1)}, u32[]{:S(2)}, u32[]{:S(2)}) collective-permute-start(bf16[256,1280]{1,0:T(8,128)(2,1)S(1)} %pad_maximum_fusion.6), channel_id=1, source_target_pairs={{0,1},{1,0},{2,3},{3,2},{4,5},{5,4},{6,7},{7,6},{8,9},{9,8},{10,11... | collective-permute-start | bytes 1966088 | tf_op jit(solution)/shard_map/ppermute | solution.py:77
  102.4 6.7 %collective-permute-start.27 = (bf16[64,1280]{1,0:T(8,128)(2,1)S(1)}, bf16[64,1280]{1,0:T(8,128)(2,1)S(1)}, u32[]{:S(2)}, u32[]{:S(2)}) collective-permute-start(bf16[64,1280]{1,0:T(8,128)(2,1)S(1)} %slice.258), channel_id=1, source_target_pairs={{0,2},{1,3},{2,0},{3,1},{4,6},{5,7},{6,4},{7,5},{8,10},{9,11},{10,... | collective-permute-start | bytes 491528 | tf_op jit(solution)/shard_map/ppermute | solution.py:77
  104.0 23.9 %collective-permute-start.30 = (bf16[640,768]{1,0:T(8,128)(2,1)S(1)}, bf16[640,768]{1,0:T(8,128)(2,1)S(1)}, u32[]{:S(2)}, u32[]{:S(2)}) collective-permute-start(bf16[640,768]{1,0:T(8,128)(2,1)S(1)} %add_convert_fusion), channel_id=1, source_target_pairs={{0,4},{4,0},{8,12},{12,8},{16,20},{20,16},{24,28},{28,24},{1,5},{5... | collective-permute-start | bytes 2949128 | tf_op jit(solution)/shard_map/ppermute | solution.py:73
  107.1 9.6 %collective-permute-start.24 = (bf16[128,1280]{1,0:T(8,128)(2,1)S(1)}, bf16[128,1280]{1,0:T(8,128)(2,1)S(1)}, u32[]{:S(2)}, u32[]{:S(2)}) collective-permute-start(bf16[128,1280]{1,0:T(8,128)(2,1)S(1)} %pad_maximum_fusion.11), channel_id=1, source_target_pairs={{0,2},{1,3},{2,0},{3,1},{4,6},{5,7},{6,4},{7,5},{8,10},{9,11},{10,... | collective-permute-start | bytes 983048 | tf_op jit(solution)/shard_map/ppermute | solution.py:77
  109.1 10.4 %collective-permute-start.28 = (bf16[64,1280]{1,0:T(8,128)(2,1)S(1)}, bf16[64,1280]{1,0:T(8,128)(2,1)S(1)}, u32[]{:S(2)}, u32[]{:S(2)}) collective-permute-start(bf16[64,1280]{1,0:T(8,128)(2,1)S(1)} %fusion.19), channel_id=1, source_target_pairs={{0,16},{4,20},{8,24},{12,28},{16,0},{20,4},{24,8},{28,12},{1,17},{... | collective-permute-start | bytes 491528 | tf_op jit(solution)/shard_map/ppermute | solution.py:69
  116.8 12.5 %collective-permute-start.25 = (bf16[64,1280]{1,0:T(8,128)(2,1)S(1)}, bf16[64,1280]{1,0:T(8,128)(2,1)S(1)}, u32[]{:S(2)}, u32[]{:S(2)}) collective-permute-start(bf16[64,1280]{1,0:T(8,128)(2,1)S(1)} %broadcast_select_fusion.4), channel_id=1, source_target_pairs={{0,8},{4,12},{8,0},{12,4},{16,24},{20,28},{24,16},{28,20},{1,9},{5... | collective-permute-start | bytes 491528 | tf_op jit(solution)/shard_map/ppermute | solution.py:69
  119.5 10.0 %collective-permute-start.29 = (bf16[64,1280]{1,0:T(8,128)(2,1)S(1)}, bf16[64,1280]{1,0:T(8,128)(2,1)S(1)}, u32[]{:S(2)}, u32[]{:S(2)}) collective-permute-start(bf16[64,1280]{1,0:T(8,128)(2,1)S(1)} %get-tuple-element.54), channel_id=1, source_target_pairs={{0,24},{4,28},{8,16},{12,20},{16,8},{20,12},{24,0},{28,4},{1,25},{... | collective-permute-start | bytes 491528 | tf_op jit(solution)/shard_map/ppermute | solution.py:69
  (5 other events, 45.0 us)
